TPU v7x, 32 devices: a whole 2x2x4 slice. The times are simulated.
32 devices in a mesh: island: 4 (over z), fsdp: 4 (over y, core), tp: 2 (over x).
Axes of the slice: x: 2, y: 2, z: 4, core: 2. Of those that a mesh axis runs over, the one named last changes fastest.
Arguments:
- context: bfloat16 [4096, 3072], P(('island', 'fsdp'), 'tp'), may hold values from -6 to 6
- residual: bfloat16 [4096, 6144], P(('island', 'fsdp'), 'tp'), may hold values from -32 to 32
- cotangent: bfloat16 [4096, 6144], P(('island', 'fsdp'), 'tp'), may hold values from -8 to 8
- gain: bfloat16 [6144], replicated, may hold values from 0.5 to 1.5
- weight: bfloat16 [3072, 6144], P('tp', 'fsdp'), may hold values from -1 to 1
- first_moment: bfloat16 [4, 3072, 6144], P('island', 'tp', 'fsdp'), may hold values from -0.011962891 to 0.011962891
- second_moment: bfloat16 [4, 3072, 6144], P('island', 'tp', 'fsdp'), may hold values from 9.9651515e-08 to 9.983778e-07
- momentum: float32 [3072, 6144], P('tp', 'fsdp'), may hold values from -3 to 3
Outputs:
- new_momentum: float32 [3072, 6144], P('tp', 'fsdp')
- outer_step: bfloat16 [3072, 6144], P('tp', 'fsdp')
All inputs are finite; a program needn't handle non-finite values.
Results may differ from a plain program's by a relative error of at most 0.014.
Values may be sent and summed in bfloat16 or wider, within the bound.
No kernel may reach another device: no remote copies, remote signals or barrier semaphores. Data moves between devices by JAX's collectives and lax.ppermute only.
A program may use at most 192 MiB of HBM per device.

v0:
```python
import jax
import jax.numpy as jnp
from jax import lax
from jax.sharding import PartitionSpec as P

norm_eps = 1e-06
adam_eps = 1e-08
beta_one = 0.9
beta_two = 0.999
bias_one = 1.0 - 0.9**10
bias_two = 1.0 - 0.999**10
decay_rate = 0.1
outer_mu = 0.9


def outer_update(delta, momentum):
    new_momentum = outer_mu * momentum + delta
    outer_step = (delta + outer_mu * new_momentum).astype(jnp.bfloat16)
    return (new_momentum, outer_step)


def body(context, residual, cotangent, gain, weight, first_moment, second_moment, momentum):
    tok_rows = context.shape[0]
    width = gain.shape[0]
    tp_count = lax.axis_size("tp")
    half = width // tp_count
    fsdp_count = lax.axis_size("fsdp")
    partial_out = jnp.dot(
        context,
        lax.all_gather(weight, "fsdp", axis=1, tiled=True),
        preferred_element_type=jnp.float32,
    )
    head_part = lax.psum_scatter(
        partial_out.astype(jnp.bfloat16), "tp", scatter_dimension=1, tiled=True
    ).astype(jnp.float32)
    hidden = residual.astype(jnp.float32) + head_part
    gain_part = lax.dynamic_slice_in_dim(gain, lax.axis_index("tp") * half, half).astype(
        jnp.float32
    )
    weighted = gain_part[None, :] * cotangent.astype(jnp.float32)
    square_sum, row_dot = lax.psum(
        (jnp.sum(hidden * hidden, axis=-1), jnp.sum(hidden * weighted, axis=-1)), "tp"
    )
    inv_rms = lax.rsqrt(square_sum / width + norm_eps)
    d_local = (
        weighted * inv_rms[:, None] - hidden * (inv_rms**3 * row_dot / width)[:, None]
    ).astype(jnp.bfloat16)
    d_hidden = lax.all_gather(d_local, "tp", axis=1, tiled=True)
    grad_sum = (
        lax.psum_scatter(
            lax.dot_general(
                d_hidden, context, (((0,), (0,)), ((), ())), preferred_element_type=jnp.float32
            ).astype(jnp.bfloat16),
            "fsdp",
            scatter_dimension=0,
            tiled=True,
        )
        .astype(jnp.float32)
        .T
    )
    grad = grad_sum / (tok_rows * fsdp_count)
    m_new = beta_one * first_moment[0].astype(jnp.float32) + (1.0 - beta_one) * grad
    v_new = beta_two * second_moment[0].astype(jnp.float32) + (1.0 - beta_two) * grad * grad
    update = m_new / bias_one / (
        jnp.sqrt(v_new / bias_two) + adam_eps
    ) + decay_rate * weight.astype(jnp.float32)
    pseudo = lax.optimization_barrier(update.astype(jnp.bfloat16)).astype(jnp.float32)
    island_count = lax.axis_size("island")
    delta = lax.psum(pseudo.astype(jnp.bfloat16), "island").astype(jnp.float32) / island_count
    new_momentum, outer_step = outer_update(delta, momentum)
    return (new_momentum, outer_step)


def solution(mesh):
    in_specs = (
        P(("island", "fsdp"), "tp"),
        P(("island", "fsdp"), "tp"),
        P(("island", "fsdp"), "tp"),
        P(),
        P("tp", "fsdp"),
        P("island", "tp", "fsdp"),
        P("island", "tp", "fsdp"),
        P("tp", "fsdp"),
    )
    out_specs = (P("tp", "fsdp"), P("tp", "fsdp"))
    return jax.shard_map(body, mesh=mesh, in_specs=in_specs, out_specs=out_specs, check_vma=False)
```

profile of v0, /device:TPU:2, one launch (start us, length us, event | category | flops | bytes accessed | tf_op | source)
XLA Modules:
  0.0 615.4 jit_solution(587240720519905741)
XLA Ops:
  7.2 0.0 copy-start
  7.2 0.0 all-gather.3.cloned.1.call-start
  7.2 0.7 all-gather.3.cloned.1.call-update
  7.9 0.0 copy-start.3
  7.9 0.0 copy-start.2
  7.9 0.0 reduce-scatter.3.cloned.1.call-start
  8.0 122.9 %all-gather.3.cloned.1.call-done = bf16[1536,6144]{1,0:T(8,128)(2,1)} async-done(((bf16[1536,1536]{1,0:T(8,128)(2,1)}), bf16[1536,6144]{1,0:T(8,128)(2,1)}) %all-gather.3.cloned.1.call-update) | async-done | bytes 18874384 | tf_op jit(solution)/shard_map/all_gather | solution.py:30
  130.8 0.0 copy-done
  130.9 12.8 %convolution_convert_fusion.1 = bf16[256,6144]{1,0:T(8,128)(2,1)} fusion(bf16[256,1536]{1,0:T(8,128)(2,1)S(1)} %copy-done, bf16[1536,6144]{1,0:T(8,128)(2,1)} %all-gather.3.cloned.1.call-done), kind=kOutput, calls=%fused_computation.19 | convolution fusion | flops 4833411072 | bytes 22806528 | tf_op jit(solution)/shard_map/dot_general | solution.py:28
  143.6 0.0 reduce-scatter.3.cloned.1.call-update
  143.6 0.0 all-gather.5.cloned.1.call-start
  143.7 0.0 copy-done.3
  143.7 42.3 %reduce-scatter.3.cloned.1.call-done = bf16[256,3072]{1,0:T(8,128)(2,1)} async-done(((bf16[256,6144]{1,0:T(8,128)(2,1)}), bf16[256,3072]{1,0:T(8,128)(2,1)}) %reduce-scatter.3.cloned.1.call-update) | async-done | bytes 1572880 | tf_op jit(solution)/shard_map/reduce_scatter | solution.py:33
  186.0 0.0 copy-done.2
  186.0 2.9 multiply_reduce_fusion.1
  188.9 4.9 all-reduce
  193.8 4.2 subtract_convert_fusion
  198.0 0.0 all-gather.5.cloned.1.call-update
  198.0 0.0 reduce-scatter.5.cloned.1.call-start
  198.1 45.0 %all-gather.5.cloned.1.call-done = bf16[256,6144]{1,0:T(8,128)(2,1)} async-done(((bf16[256,3072]{1,0:T(8,128)(2,1)}), bf16[256,6144]{1,0:T(8,128)(2,1)}) %all-gather.5.cloned.1.call-update) | async-done | bytes 3145744 | tf_op jit(solution)/shard_map/all_gather | solution.py:48
  243.1 11.2 %convolution_convert_fusion = bf16[6144,1536]{1,0:T(8,128)(2,1)} fusion(bf16[256,6144]{1,0:T(8,128)(2,1)} %all-gather.5.cloned.1.call-done, bf16[256,1536]{1,0:T(8,128)(2,1)S(1)} %copy-done), kind=kOutput, calls=%fused_computation | convolution fusion | flops 4841275392 | bytes 22806528 | tf_op jit(solution)/shard_map/dot_general | solution.py:51
  254.3 0.0 reduce-scatter.5.cloned.1.call-update
  254.3 0.2 all-reduce.3.cloned.1.call-start
  254.5 6.6 %copy.13 = bf16[1536,1536]{0,1:T(8,128)(2,1)} copy(bf16[1536,1536]{1,0:T(8,128)(2,1)} %param.12) | data formatting | bytes 9437184 | tf_op args[4]
  261.2 7.1 %copy.11 = bf16[1,1536,1536]{1,2,0:T(8,128)(2,1)} copy(bf16[1,1536,1536]{2,1,0:T(8,128)(2,1)} %param.13) | data formatting | bytes 9437184 | tf_op args[5]
  268.3 7.3 %copy.12 = bf16[1,1536,1536]{1,2,0:T(8,128)(2,1)} copy(bf16[1,1536,1536]{2,1,0:T(8,128)(2,1)} %param.14) | data formatting | bytes 9437184 | tf_op args[6]
  275.6 119.5 %reduce-scatter.5.cloned.1.call-done = bf16[1536,1536]{1,0:T(8,128)(2,1)} async-done(((bf16[6144,1536]{1,0:T(8,128)(2,1)}), bf16[1536,1536]{1,0:T(8,128)(2,1)}) %reduce-scatter.5.cloned.1.call-update) | async-done | bytes 4718608 | tf_op jit(solution)/shard_map/reduce_scatter | solution.py:50
  395.1 13.0 %fusion.12 = bf16[1536,1536]{0,1:T(8,128)(2,1)} fusion(bf16[1536,1536]{0,1:T(8,128)(2,1)} %copy.13, bf16[1,1536,1536]{1,2,0:T(8,128)(2,1)} %copy.12, bf16[1536,1536]{1,0:T(8,128)(2,1)} %reduce-scatter.5.cloned.1.call-done, bf16[1,1536,1536]{1,2,0:T(8,128)(2,1)} %copy.11), kind=kLoop, calls=%fused_computation.18 | loop fusion | flops 44826624 | bytes 23592960 | tf_op jit(solution)/shard_map/convert_element_type | solution.py:67
  408.1 0.0 all-reduce.3.cloned.1.call-update
  408.2 9.7 %copy.10 = f32[1536,1536]{0,1:T(8,128)} copy(f32[1536,1536]{1,0:T(8,128)} %param.15) | data formatting | bytes 18874368 | tf_op args[7]
  417.9 162.4 %all-reduce.3.cloned.1.call-done = bf16[1536,1536]{0,1:T(8,128)(2,1)} async-done(((bf16[1536,1536]{0,1:T(8,128)(2,1)}), bf16[1536,1536]{0,1:T(8,128)(2,1)}) %all-reduce.3.cloned.1.call-update) | async-done | bytes 4718608 | tf_op jit(solution)/shard_map/psum | solution.py:69
  580.3 12.3 %add_convert_fusion = (bf16[1536,1536]{0,1:T(8,128)(2,1)}, f32[1536,1536]{0,1:T(8,128)}) fusion(bf16[1536,1536]{0,1:T(8,128)(2,1)} %all-reduce.3.cloned.1.call-done, f32[1536,1536]{0,1:T(8,128)} %copy.10), kind=kLoop, calls=%fused_computation.15 | loop fusion | flops 16515072 | bytes 28311552 | tf_op jit(solution)/shard_map/convert_element_type | solution.py:18
  592.6 9.6 %copy.14 = f32[1536,1536]{1,0:T(8,128)} copy(f32[1536,1536]{0,1:T(8,128)} %get-tuple-element.9) | data formatting | bytes 18874368
  602.2 0.0 copy-start.1
  602.2 6.7 %copy.15 = bf16[1536,1536]{1,0:T(8,128)(2,1)} copy(bf16[1536,1536]{0,1:T(8,128)(2,1)} %get-tuple-element.8) | data formatting | bytes 9437184
  608.9 0.0 copy-done.1
  (2 shorter events, 0.0 us)
Async XLA Ops:
  7.2 123.7 %copy-start = (bf16[256,1536]{1,0:T(8,128)(2,1)S(1)}, bf16[256,1536]{1,0:T(8,128)(2,1)}, u32[]{:S(2)}) copy-start(bf16[256,1536]{1,0:T(8,128)(2,1)} %param.8) | copy-start | bytes 2359300
  7.2 123.7 %all-gather.3.cloned.1.call-start = ((), (), s32[]{:S(2)}) async-start(), calls=%async_computation.2 | async-start | bytes 23592960 | tf_op jit(solution)/shard_map/all_gather | solution.py:30
  7.9 135.8 %copy-start.3 = (bf16[6144]{0:T(1024)(128)(2,1)S(1)}, bf16[6144]{0:T(1024)(128)(2,1)}, u32[]{:S(2)}) copy-start(bf16[6144]{0:T(1024)(128)(2,1)} %param.11) | copy-start | bytes 36868
  7.9 178.1 %copy-start.2 = (bf16[256,3072]{1,0:T(8,128)(2,1)S(1)}, bf16[256,3072]{1,0:T(8,128)(2,1)}, u32[]{:S(2)}) copy-start(bf16[256,3072]{1,0:T(8,128)(2,1)} %param.10) | copy-start | bytes 4718596
  7.9 178.1 %reduce-scatter.3.cloned.1.call-start = ((), (), s32[]{:S(2)}) async-start(), calls=%async_computation.3 | async-start | bytes 4718592 | tf_op jit(solution)/shard_map/reduce_scatter | solution.py:33
  143.6 99.5 %all-gather.5.cloned.1.call-start = ((), (), s32[]{:S(2)}) async-start(), calls=%async_computation.4 | async-start | bytes 4718592 | tf_op jit(solution)/shard_map/all_gather | solution.py:48
  198.0 197.1 %reduce-scatter.5.cloned.1.call-start = ((), (), s32[]{:S(2)}) async-start(), calls=%async_computation.5 | async-start | bytes 23592960 | tf_op jit(solution)/shard_map/reduce_scatter | solution.py:50
  254.3 326.0 %all-reduce.3.cloned.1.call-start = ((), (), s32[]{:S(2)}) async-start(), calls=%async_computation.6 | async-start | bytes 9437184 | tf_op jit(solution)/shard_map/psum | solution.py:69
  602.2 6.7 %copy-start.1 = (bf16[256,1536]{1,0:T(8,128)(2,1)S(1)}, bf16[256,1536]{1,0:T(8,128)(2,1)}, u32[]{:S(2)}) copy-start(bf16[256,1536]{1,0:T(8,128)(2,1)} %param.8) | copy-start | bytes 2359300
Sparse Core Ops, SparseCore 0:
  9.6 121.2 all-gather.2
  143.8 42.1 reduce-scatter.2
  198.1 44.9 all-gather.4
  254.4 140.6 reduce-scatter.4
  408.3 171.9 all-reduce.2
where the time goes:
time: 618 us; the launch traced here: 615 us
  waiting for transfers between devices  493 us (80%)
  local copies, waits for them, and re-layouts  47 us (8%)
  other arithmetic  32.4 us (5%)
  matrix products  23.9 us (4%)
  between operations  13.8 us (2%)
    psum x1, waiting for transfers between devices, body(): lax.psum(pseudo.astype(jnp.bfloat16), 'island').astype(jnp.float32)  162 us
    all_gather x1, waiting for transfers between devices, body(): lax.all_gather(weight, 'fsdp', axis=1, tiled=True)  123 us
    reduce_scatter x1, waiting for transfers between devices, body(): lax.psum_scatter(lax.dot_general(d_hidden, context, (((0,), (0,)), ((), (...  120 us
    unnamed x14, local copies, waits for them, and re-layouts  47 us
    all_gather x1, waiting for transfers between devices, body(): d_hidden = lax.all_gather(d_local, 'tp', axis=1, tiled=True)  45 us
    reduce_scatter x1, waiting for transfers between devices, body(): lax.psum_scatter(partial_out.astype(jnp.bfloat16), 'tp', scatter_dimensio...  42.3 us
    convert_element_type x1, other arithmetic, body(): update.astype(jnp.bfloat16)  13 us
    dot_general x1, matrix products, body(): jnp.dot(context, lax.all_gather(weight, 'fsdp', axis=1, tiled=True), pref...  12.8 us
  transfers between devices with their start and end apart: 5, of which 5 were waited for; matrix products, arithmetic and copies ran while one was open for 5% of the time, Pallas kernels for 0%

commit v1 on v0

v1 whole, which is shorter than its diff:
```python
import jax
import jax.numpy as jnp
from jax import lax
from jax.sharding import PartitionSpec as P

norm_eps = 1e-06
adam_eps = 1e-08
beta_one = 0.9
beta_two = 0.999
bias_one = 1.0 - 0.9**10
bias_two = 1.0 - 0.999**10
decay_rate = 0.1
outer_mu = 0.9

f32 = jnp.float32
bf16 = jnp.bfloat16


def outer_update(delta, momentum):
    new_momentum = outer_mu * momentum + delta
    outer_step = (delta + outer_mu * new_momentum).astype(bf16)
    return (new_momentum, outer_step)


def swap(value, axis, bit):
    count = lax.axis_size(axis)
    return lax.ppermute(value, axis, [(i, i ^ bit) for i in range(count)])


def island_sum(value):
    count = lax.axis_size("island")
    half = count // 2
    me = lax.axis_index("island")
    held = value
    for hop in range(half - 1):
        pairs = [(hop, hop + 1), (count - 1 - hop, count - 2 - hop)]
        came = lax.ppermute(held, "island", pairs)
        held = (came.astype(f32) + value.astype(f32)).astype(bf16)
    came = lax.ppermute(held, "island", [(half - 1, half), (half, half - 1)])
    total = (held.astype(f32) + came.astype(f32)).astype(bf16)
    for hop in range(half - 1):
        inner, outer = half - 1 - hop, half - 2 - hop
        pairs = [(inner, outer), (count - 1 - inner, count - 1 - outer)]
        came = lax.ppermute(total, "island", pairs)
        total = jnp.where((me == outer) | (me == count - 1 - outer), came, total)
    return total


def body(context, residual, cotangent, gain, weight, first_moment, second_moment, momentum):
    tok_rows = context.shape[0]
    width = gain.shape[0]
    fsdp_count = lax.axis_size("fsdp")
    group = fsdp_count // 2
    cols = weight.shape[1]
    t = lax.axis_index("tp")
    f = lax.axis_index("fsdp")
    high = f // group
    low = f % group
    near = t == high

    blocks = {0: context}
    bit = group
    while bit:
        for delta in sorted(blocks):
            blocks[delta ^ bit] = swap(blocks[delta], "fsdp", bit)
        bit //= 2

    def regroup(array):
        parts = []
        for r in range(group):
            part = lax.dynamic_slice_in_dim(array, (low ^ r) * cols, cols, axis=1)
            parts.append(swap(part, "fsdp", r) if r else part)
        return parts

    residual_parts = regroup(residual)
    cotangent_parts = regroup(cotangent)
    gain_part = lax.dynamic_slice_in_dim(gain, t * (width // 2) + low * cols, cols).astype(f32)

    def project(block):
        return jnp.dot(block, weight, preferred_element_type=f32).astype(bf16)

    hidden, weighted, sums = [], [], []
    for r in range(group):
        far_out = swap(project(blocks[group ^ r]), "fsdp", group)
        own_out = project(blocks[r])
        keep = jnp.where(near, own_out, far_out)
        came = swap(jnp.where(near, far_out, own_out), "tp", 1)
        h = residual_parts[r].astype(f32) + keep.astype(f32) + came.astype(f32)
        w = gain_part[None, :] * cotangent_parts[r].astype(f32)
        hidden.append(h)
        weighted.append(w)
        sums.append(jnp.stack([jnp.sum(h * h, axis=-1), jnp.sum(h * w, axis=-1)]))
    own_sums = jnp.concatenate(sums, axis=1)
    totals = own_sums
    for r in range(1, group):
        came = swap(own_sums, "fsdp", r)
        order = [r ^ k for k in range(group)]
        came = jnp.concatenate(
            [came[:, k * tok_rows : (k + 1) * tok_rows] for k in order], axis=1
        )
        totals = totals + came
    totals = totals + swap(totals, "tp", 1)
    inv_rms = lax.rsqrt(totals[0] / width + norm_eps)
    pull = inv_rms**3 * totals[1] / width

    tokens = [blocks[r] for r in range(group)] + [blocks[group ^ r] for r in range(group)]
    context_all = jnp.concatenate(tokens, axis=0)
    chunks = 6
    step = cols // chunks
    momentum_out, step_out = [], []
    for c in range(chunks):
        lo = c * step
        d_local = jnp.concatenate(
            [
                weighted[r][:, lo : lo + step] * inv_rms[r * tok_rows : (r + 1) * tok_rows, None]
                - hidden[r][:, lo : lo + step] * pull[r * tok_rows : (r + 1) * tok_rows, None]
                for r in range(group)
            ],
            axis=0,
        ).astype(bf16)
        came = swap(d_local, "tp", 1)
        d_own = jnp.where(near, d_local, came)
        d_far = swap(jnp.where(near, came, d_local), "fsdp", group)
        d_all = jnp.concatenate([d_own, d_far], axis=0)
        grad = lax.dot_general(
            context_all, d_all, (((0,), (0,)), ((), ())), preferred_element_type=f32
        ) / (tok_rows * fsdp_count)
        first = first_moment[0, :, lo : lo + step].astype(f32)
        second = second_moment[0, :, lo : lo + step].astype(f32)
        m_new = beta_one * first + (1.0 - beta_one) * grad
        v_new = beta_two * second + (1.0 - beta_two) * grad * grad
        update = m_new / bias_one / (
            jnp.sqrt(v_new / bias_two) + adam_eps
        ) + decay_rate * weight[:, lo : lo + step].astype(f32)
        pseudo = update.astype(bf16)
        half = pseudo.shape[0] // 2
        total = jnp.concatenate([island_sum(pseudo[:half]), island_sum(pseudo[half:])], axis=0)
        delta = total.astype(f32) / lax.axis_size("island")
        new_momentum, outer_step = outer_update(delta, momentum[:, lo : lo + step])
        momentum_out.append(new_momentum)
        step_out.append(outer_step)
    return (jnp.concatenate(momentum_out, axis=1), jnp.concatenate(step_out, axis=1))


def solution(mesh):
    in_specs = (
        P(("island", "fsdp"), "tp"),
        P(("island", "fsdp"), "tp"),
        P(("island", "fsdp"), "tp"),
        P(),
        P("tp", "fsdp"),
        P("island", "tp", "fsdp"),
        P("island", "tp", "fsdp"),
        P("tp", "fsdp"),
    )
    out_specs = (P("tp", "fsdp"), P("tp", "fsdp"))
    return jax.shard_map(body, mesh=mesh, in_specs=in_specs, out_specs=out_specs, check_vma=False)
```

time: 618 us -> 390 us (0.63)
  waiting for transfers between devices: 493 us -> 254 us
  starting transfers between devices: 0.38 us -> 77.9 us
  local copies, waits for them, and re-layouts: 47 us -> 11.4 us
  other arithmetic: 32.4 us -> 12.8 us
  between operations: 13.8 us -> 1.72 us
  matrix products: 23.9 us -> 30.4 us
    ppermute x0 -> x59, waiting for transfers between devices: none -> 254 us  [the longest x12 117 us: island_sum(): came = lax.ppermute(total, 'island', pairs)]
    all_gather x2 -> x0, waiting for transfers between devices: 168 us -> none  [the longest x1 123 us: body(): lax.all_gather(weight, 'fsdp', axis=1, tiled=True)]
    psum x1 -> x0, waiting for transfers between devices: 162 us -> none  [body(): lax.psum(pseudo.astype(jnp.bfloat16), 'island').astype(jnp.float32)]
    reduce_scatter x2 -> x0, waiting for transfers between devices: 162 us -> none  [the longest x1 120 us: body(): lax.psum_scatter(lax.dot_general(d_hidden, context, (((0,), (0,)), ((), (...]
    ppermute x0 -> x59, starting transfers between devices: none -> 77.9 us  [the longest x12 36.7 us: island_sum(): came = lax.ppermute(held, 'island', pairs)]
    unnamed x14 -> x43, local copies, waits for them, and re-layouts: 47 us -> 9.08 us
    convert_element_type x4 -> x19, other arithmetic: 29.5 us -> 3.29 us  [the longest x6 1.28 us: island_sum(): held = (came.astype(f32) + value.astype(f32)).astype(bf16)]
    dot_general x2 -> x10, matrix products: 23.9 us -> 30.4 us  [the longest x4 17.3 us: project(): return jnp.dot(block, weight, preferred_element_type=f32).astype(bf16)]
  transfers between devices with their start and end apart: 5 -> 59, of which waited for: 5 -> 34; matrix products, arithmetic and copies ran while one was open for 5% -> 11% of each run, Pallas kernels for 0% -> 0%
where the time goes in v1:
time: 390 us; the launch traced here: 388 us
  waiting for transfers between devices  254 us (65%)
  starting transfers between devices  77.9 us (20%)
  matrix products  30.4 us (8%)
  other arithmetic  12.8 us (3%)
  local copies, waits for them, and re-layouts  11.4 us (3%)
    ppermute x12, waiting for transfers between devices, island_sum(): came = lax.ppermute(total, 'island', pairs)  117 us
    ppermute x23, waiting for transfers between devices, swap(): return lax.ppermute(value, axis, [(i, i ^ bit) for i in range(count)])  86.5 us
    ppermute x12, waiting for transfers between devices, island_sum(): came = lax.ppermute(held, 'island', pairs)  50.3 us
    ppermute x12, starting transfers between devices, island_sum(): came = lax.ppermute(held, 'island', pairs)  36.7 us
    dot_general x4, matrix products, project(): return jnp.dot(block, weight, preferred_element_type=f32).astype(bf16)  17.3 us
    ppermute x23, starting transfers between devices, swap(): return lax.ppermute(value, axis, [(i, i ^ bit) for i in range(count)])  17.2 us
    ppermute x12, starting transfers between devices, island_sum(): came = lax.ppermute(total, 'island', pairs)  15.6 us
    dot_general x6, matrix products, body(): lax.dot_general(context_all, d_all, (((0,), (0,)), ((), ())), preferred_e...  13.1 us
  transfers between devices with their start and end apart: 59, of which 34 were waited for; matrix products, arithmetic and copies ran while one was open for 11% of the time, Pallas kernels for 0%

profile of v1, /device:TPU:2, one launch (start us, length us, event | category | flops | bytes accessed | tf_op | source)
XLA Modules:
  0.0 388.3 jit_solution(8736914021933925217)
XLA Ops:
  2.2 18.0 %collective-permute-done.1 = bf16[256,1536]{1,0:T(8,128)(2,1)S(1)} collective-permute-done((bf16[256,1536]{1,0:T(8,128)(2,1)}, bf16[256,1536]{1,0:T(8,128)(2,1)S(1)}, u32[]{:S(2)}, u32[]{:S(2)}) %collective-permute-start.1) | collective-permute-done | bytes 786464 | tf_op jit(solution)/shard_map/ppermute | solution.py:27
  20.7 4.8 %convolution_convert_fusion.2 = bf16[256,1536]{1,0:T(8,128)(2,1)} fusion(bf16[256,1536]{1,0:T(8,128)(2,1)S(1)} %collective-permute-done.1, bf16[1536,1536]{1,0:T(8,128)(2,1)} %param.12), kind=kOutput, calls=%fused_computation.2 | convolution fusion | flops 1208352768 | bytes 6291456 | tf_op jit(solution)/shard_map/dot_general | solution.py:80
  27.9 2.3 convolution_convert_fusion
  33.1 13.0 %collective-permute-done.3 = bf16[256,1536]{1,0:T(8,128)(2,1)} collective-permute-done((bf16[256,1536]{1,0:T(8,128)(2,1)}, bf16[256,1536]{1,0:T(8,128)(2,1)}, u32[]{:S(2)}, u32[]{:S(2)}) %collective-permute-start.3) | collective-permute-done | bytes 786464 | tf_op jit(solution)/shard_map/ppermute | solution.py:27
  46.2 5.2 %broadcast_select_fusion.1 = (bf16[256,1536]{1,0:T(8,128)(2,1)}, bf16[256,1536]{1,0:T(8,128)(2,1)}) fusion(bf16[256,1536]{1,0:T(8,128)(2,1)} %collective-permute-done.3, pred[]{:T(512)S(6)} %eq.10, bf16[256,1536]{1,0:T(8,128)(2,1)} %param.8, bf16[1536,1536]{1,0:T(8,128)(2,1)} %param.12), kind=kOutput, calls=%fused_computation.127 | convolution fusion | flops 1208745984 | bytes 7864321 | tf_op jit(solution)/shard_map/dot_general | solution.py:80
  51.9 10.2 %collective-permute-done.6 = bf16[256,1536]{1,0:T(8,128)(2,1)} collective-permute-done((bf16[256,1536]{1,0:T(8,128)(2,1)}, bf16[256,1536]{1,0:T(8,128)(2,1)}, u32[]{:S(2)}, u32[]{:S(2)}) %collective-permute-start.6) | collective-permute-done | bytes 786464 | tf_op jit(solution)/shard_map/ppermute | solution.py:27
  62.1 5.1 %broadcast_select_fusion = (bf16[256,1536]{1,0:T(8,128)(2,1)}, bf16[256,1536]{1,0:T(8,128)(2,1)}) fusion(bf16[256,1536]{1,0:T(8,128)(2,1)} %collective-permute-done.6, pred[]{:T(512)S(6)} %eq.10, bf16[256,1536]{1,0:T(8,128)(2,1)} %collective-permute-done, bf16[1536,1536]{1,0:T(8,128)(2,1)} %param.12), kind=kOutput, calls=%fused_computation.126 | convolution fusion | flops 1208745984 | bytes 7864321 | tf_op jit(solution)/shard_map/dot_general | solution.py:80
  71.0 15.2 %collective-permute-done.7 = bf16[256,1536]{1,0:T(8,128)(2,1)} collective-permute-done((bf16[256,1536]{1,0:T(8,128)(2,1)}, bf16[256,1536]{1,0:T(8,128)(2,1)}, u32[]{:S(2)}, u32[]{:S(2)}) %collective-permute-start.7) | collective-permute-done | bytes 786464 | tf_op jit(solution)/shard_map/ppermute | solution.py:27
  86.2 3.8 multiply_reduce_fusion.3
  91.4 3.5 collective-permute-done.10
  100.1 4.8 %collective-permute-done.11 = bf16[512,256]{1,0:T(8,128)(2,1)S(1)} collective-permute-done((bf16[512,256]{1,0:T(8,128)(2,1)S(1)}, bf16[512,256]{1,0:T(8,128)(2,1)S(1)}, u32[]{:S(2)}, u32[]{:S(2)}) %collective-permute-start.11) | collective-permute-done | bytes 262176 | tf_op jit(solution)/shard_map/ppermute | solution.py:27
  105.0 5.5 %collective-permute-done.19 = bf16[512,256]{1,0:T(8,128)(2,1)S(1)} collective-permute-done((bf16[512,256]{1,0:T(8,128)(2,1)S(1)}, bf16[512,256]{1,0:T(8,128)(2,1)S(1)}, u32[]{:S(2)}, u32[]{:S(2)}) %collective-permute-start.19) | collective-permute-done | bytes 262176 | tf_op jit(solution)/shard_map/ppermute | solution.py:27
  111.8 4.3 %collective-permute-done.27 = bf16[512,256]{1,0:T(8,128)(2,1)S(1)} collective-permute-done((bf16[512,256]{1,0:T(8,128)(2,1)S(1)}, bf16[512,256]{1,0:T(8,128)(2,1)S(1)}, u32[]{:S(2)}, u32[]{:S(2)}) %collective-permute-start.27) | collective-permute-done | bytes 262176 | tf_op jit(solution)/shard_map/ppermute | solution.py:27
  117.5 4.3 %collective-permute-done.35 = bf16[512,256]{1,0:T(8,128)(2,1)S(1)} collective-permute-done((bf16[512,256]{1,0:T(8,128)(2,1)S(1)}, bf16[512,256]{1,0:T(8,128)(2,1)S(1)}, u32[]{:S(2)}, u32[]{:S(2)}) %collective-permute-start.35) | collective-permute-done | bytes 262176 | tf_op jit(solution)/shard_map/ppermute | solution.py:27
  123.1 4.3 %collective-permute-done.43 = bf16[512,256]{1,0:T(8,128)(2,1)S(1)} collective-permute-done((bf16[512,256]{1,0:T(8,128)(2,1)S(1)}, bf16[512,256]{1,0:T(8,128)(2,1)S(1)}, u32[]{:S(2)}, u32[]{:S(2)}) %collective-permute-start.43) | collective-permute-done | bytes 262176 | tf_op jit(solution)/shard_map/ppermute | solution.py:27
  128.7 2.3 collective-permute-done.51
  133.2 2.2 fusion.42
  135.5 3.7 collective-permute-start.13
  153.4 2.2 fusion.47
  157.1 4.5 %collective-permute-start.37 = (bf16[768,256]{1,0:T(8,128)(2,1)S(1)}, bf16[768,256]{1,0:T(8,128)(2,1)S(1)}, u32[]{:S(2)}, u32[]{:S(2)}) collective-permute-start(bf16[768,256]{1,0:T(8,128)(2,1)S(1)} %get-tuple-element.32), channel_id=1, source_target_pairs={{0,8},{24,16},{1,9},{25,17},{2,10},{26,18},{3,11},{27,19},{4,12},{... | collective-permute-start | bytes 1179656 | tf_op jit(solution)/shard_map/ppermute | solution.py:37
  161.8 3.6 collective-permute-done.21
  165.4 4.4 %collective-permute-start.40 = (bf16[768,256]{1,0:T(8,128)(2,1)S(1)}, bf16[768,256]{1,0:T(8,128)(2,1)S(1)}, u32[]{:S(2)}, u32[]{:S(2)}) collective-permute-start(bf16[768,256]{1,0:T(8,128)(2,1)S(1)} %get-tuple-element.33), channel_id=1, source_target_pairs={{0,8},{24,16},{1,9},{25,17},{2,10},{26,18},{3,11},{27,19},{4,12},{... | collective-permute-start | bytes 1179656 | tf_op jit(solution)/shard_map/ppermute | solution.py:37
  169.8 4.0 %collective-permute-done.24 = bf16[768,256]{1,0:T(8,128)(2,1)S(1)} collective-permute-done((bf16[768,256]{1,0:T(8,128)(2,1)S(1)}, bf16[768,256]{1,0:T(8,128)(2,1)S(1)}, u32[]{:S(2)}, u32[]{:S(2)}) %collective-permute-start.24) | collective-permute-done | bytes 393248 | tf_op jit(solution)/shard_map/ppermute | solution.py:37
  173.8 4.4 %collective-permute-start.45 = (bf16[768,256]{1,0:T(8,128)(2,1)S(1)}, bf16[768,256]{1,0:T(8,128)(2,1)S(1)}, u32[]{:S(2)}, u32[]{:S(2)}) collective-permute-start(bf16[768,256]{1,0:T(8,128)(2,1)S(1)} %get-tuple-element.28), channel_id=1, source_target_pairs={{0,8},{24,16},{1,9},{25,17},{2,10},{26,18},{3,11},{27,19},{4,12},{... | collective-permute-start | bytes 1179656 | tf_op jit(solution)/shard_map/ppermute | solution.py:37
  178.4 3.8 collective-permute-done.29
  182.2 4.4 %collective-permute-start.48 = (bf16[768,256]{1,0:T(8,128)(2,1)S(1)}, bf16[768,256]{1,0:T(8,128)(2,1)S(1)}, u32[]{:S(2)}, u32[]{:S(2)}) collective-permute-start(bf16[768,256]{1,0:T(8,128)(2,1)S(1)} %get-tuple-element.29), channel_id=1, source_target_pairs={{0,8},{24,16},{1,9},{25,17},{2,10},{26,18},{3,11},{27,19},{4,12},{... | collective-permute-start | bytes 1179656 | tf_op jit(solution)/shard_map/ppermute | solution.py:37
  186.6 4.0 %collective-permute-done.32 = bf16[768,256]{1,0:T(8,128)(2,1)S(1)} collective-permute-done((bf16[768,256]{1,0:T(8,128)(2,1)S(1)}, bf16[768,256]{1,0:T(8,128)(2,1)S(1)}, u32[]{:S(2)}, u32[]{:S(2)}) %collective-permute-start.32) | collective-permute-done | bytes 393248 | tf_op jit(solution)/shard_map/ppermute | solution.py:37
  190.7 4.4 %collective-permute-start.53 = (bf16[768,256]{1,0:T(8,128)(2,1)S(1)}, bf16[768,256]{1,0:T(8,128)(2,1)S(1)}, u32[]{:S(2)}, u32[]{:S(2)}) collective-permute-start(bf16[768,256]{1,0:T(8,128)(2,1)S(1)} %get-tuple-element.24), channel_id=1, source_target_pairs={{0,8},{24,16},{1,9},{25,17},{2,10},{26,18},{3,11},{27,19},{4,12},{... | collective-permute-start | bytes 1179656 | tf_op jit(solution)/shard_map/ppermute | solution.py:37
  195.3 3.8 collective-permute-done.37
  199.1 4.4 %collective-permute-start.56 = (bf16[768,256]{1,0:T(8,128)(2,1)S(1)}, bf16[768,256]{1,0:T(8,128)(2,1)S(1)}, u32[]{:S(2)}, u32[]{:S(2)}) collective-permute-start(bf16[768,256]{1,0:T(8,128)(2,1)S(1)} %get-tuple-element.25), channel_id=1, source_target_pairs={{0,8},{24,16},{1,9},{25,17},{2,10},{26,18},{3,11},{27,19},{4,12},{... | collective-permute-start | bytes 1179656 | tf_op jit(solution)/shard_map/ppermute | solution.py:37
  203.5 4.0 %collective-permute-done.40 = bf16[768,256]{1,0:T(8,128)(2,1)S(1)} collective-permute-done((bf16[768,256]{1,0:T(8,128)(2,1)S(1)}, bf16[768,256]{1,0:T(8,128)(2,1)S(1)}, u32[]{:S(2)}, u32[]{:S(2)}) %collective-permute-start.40) | collective-permute-done | bytes 393248 | tf_op jit(solution)/shard_map/ppermute | solution.py:37
  208.4 7.5 %collective-permute-done.45 = bf16[768,256]{1,0:T(8,128)(2,1)S(1)} collective-permute-done((bf16[768,256]{1,0:T(8,128)(2,1)S(1)}, bf16[768,256]{1,0:T(8,128)(2,1)S(1)}, u32[]{:S(2)}, u32[]{:S(2)}) %collective-permute-start.45) | collective-permute-done | bytes 393248 | tf_op jit(solution)/shard_map/ppermute | solution.py:37
  216.6 7.7 %collective-permute-done.48 = bf16[768,256]{1,0:T(8,128)(2,1)S(1)} collective-permute-done((bf16[768,256]{1,0:T(8,128)(2,1)S(1)}, bf16[768,256]{1,0:T(8,128)(2,1)S(1)}, u32[]{:S(2)}, u32[]{:S(2)}) %collective-permute-start.48) | collective-permute-done | bytes 393248 | tf_op jit(solution)/shard_map/ppermute | solution.py:37
  225.3 7.5 %collective-permute-done.53 = bf16[768,256]{1,0:T(8,128)(2,1)S(1)} collective-permute-done((bf16[768,256]{1,0:T(8,128)(2,1)S(1)}, bf16[768,256]{1,0:T(8,128)(2,1)S(1)}, u32[]{:S(2)}, u32[]{:S(2)}) %collective-permute-start.53) | collective-permute-done | bytes 393248 | tf_op jit(solution)/shard_map/ppermute | solution.py:37
  233.5 4.2 %collective-permute-done.56 = bf16[768,256]{1,0:T(8,128)(2,1)S(1)} collective-permute-done((bf16[768,256]{1,0:T(8,128)(2,1)S(1)}, bf16[768,256]{1,0:T(8,128)(2,1)S(1)}, u32[]{:S(2)}, u32[]{:S(2)}) %collective-permute-start.56) | collective-permute-done | bytes 393248 | tf_op jit(solution)/shard_map/ppermute | solution.py:37
  251.8 41.3 %collective-permute-done.18 = bf16[768,256]{1,0:T(8,128)(2,1)S(1)} collective-permute-done((bf16[768,256]{1,0:T(8,128)(2,1)S(1)}, bf16[768,256]{1,0:T(8,128)(2,1)S(1)}, u32[]{:S(2)}, u32[]{:S(2)}) %collective-permute-start.18) | collective-permute-done | bytes 393248 | tf_op jit(solution)/shard_map/ppermute | solution.py:44
  294.5 7.1 %collective-permute-done.15 = bf16[768,256]{1,0:T(8,128)(2,1)S(1)} collective-permute-done((bf16[768,256]{1,0:T(8,128)(2,1)S(1)}, bf16[768,256]{1,0:T(8,128)(2,1)S(1)}, u32[]{:S(2)}, u32[]{:S(2)}) %collective-permute-start.15) | collective-permute-done | bytes 393248 | tf_op jit(solution)/shard_map/ppermute | solution.py:44
  303.3 6.7 %collective-permute-done.26 = bf16[768,256]{1,0:T(8,128)(2,1)S(1)} collective-permute-done((bf16[768,256]{1,0:T(8,128)(2,1)S(1)}, bf16[768,256]{1,0:T(8,128)(2,1)S(1)}, u32[]{:S(2)}, u32[]{:S(2)}) %collective-permute-start.26) | collective-permute-done | bytes 393248 | tf_op jit(solution)/shard_map/ppermute | solution.py:44
  311.4 7.1 %collective-permute-done.23 = bf16[768,256]{1,0:T(8,128)(2,1)S(1)} collective-permute-done((bf16[768,256]{1,0:T(8,128)(2,1)S(1)}, bf16[768,256]{1,0:T(8,128)(2,1)S(1)}, u32[]{:S(2)}, u32[]{:S(2)}) %collective-permute-start.23) | collective-permute-done | bytes 393248 | tf_op jit(solution)/shard_map/ppermute | solution.py:44
  320.1 6.8 %collective-permute-done.34 = bf16[768,256]{1,0:T(8,128)(2,1)S(1)} collective-permute-done((bf16[768,256]{1,0:T(8,128)(2,1)S(1)}, bf16[768,256]{1,0:T(8,128)(2,1)S(1)}, u32[]{:S(2)}, u32[]{:S(2)}) %collective-permute-start.34) | collective-permute-done | bytes 393248 | tf_op jit(solution)/shard_map/ppermute | solution.py:44
  328.2 7.1 %collective-permute-done.31 = bf16[768,256]{1,0:T(8,128)(2,1)S(1)} collective-permute-done((bf16[768,256]{1,0:T(8,128)(2,1)S(1)}, bf16[768,256]{1,0:T(8,128)(2,1)S(1)}, u32[]{:S(2)}, u32[]{:S(2)}) %collective-permute-start.31) | collective-permute-done | bytes 393248 | tf_op jit(solution)/shard_map/ppermute | solution.py:44
  337.0 6.8 %collective-permute-done.42 = bf16[768,256]{1,0:T(8,128)(2,1)S(1)} collective-permute-done((bf16[768,256]{1,0:T(8,128)(2,1)S(1)}, bf16[768,256]{1,0:T(8,128)(2,1)S(1)}, u32[]{:S(2)}, u32[]{:S(2)}) %collective-permute-start.42) | collective-permute-done | bytes 393248 | tf_op jit(solution)/shard_map/ppermute | solution.py:44
  345.4 6.7 %collective-permute-done.39 = bf16[768,256]{1,0:T(8,128)(2,1)S(1)} collective-permute-done((bf16[768,256]{1,0:T(8,128)(2,1)S(1)}, bf16[768,256]{1,0:T(8,128)(2,1)S(1)}, u32[]{:S(2)}, u32[]{:S(2)}) %collective-permute-start.39) | collective-permute-done | bytes 393248 | tf_op jit(solution)/shard_map/ppermute | solution.py:44
  352.9 7.7 %collective-permute-done.50 = bf16[768,256]{1,0:T(8,128)(2,1)S(1)} collective-permute-done((bf16[768,256]{1,0:T(8,128)(2,1)S(1)}, bf16[768,256]{1,0:T(8,128)(2,1)S(1)}, u32[]{:S(2)}, u32[]{:S(2)}) %collective-permute-start.50) | collective-permute-done | bytes 393248 | tf_op jit(solution)/shard_map/ppermute | solution.py:44
  361.0 8.0 %collective-permute-done.47 = bf16[768,256]{1,0:T(8,128)(2,1)S(1)} collective-permute-done((bf16[768,256]{1,0:T(8,128)(2,1)S(1)}, bf16[768,256]{1,0:T(8,128)(2,1)S(1)}, u32[]{:S(2)}, u32[]{:S(2)}) %collective-permute-start.47) | collective-permute-done | bytes 393248 | tf_op jit(solution)/shard_map/ppermute | solution.py:44
  369.7 7.7 %collective-permute-done.58 = bf16[768,256]{1,0:T(8,128)(2,1)S(1)} collective-permute-done((bf16[768,256]{1,0:T(8,128)(2,1)S(1)}, bf16[768,256]{1,0:T(8,128)(2,1)S(1)}, u32[]{:S(2)}, u32[]{:S(2)}) %collective-permute-start.58) | collective-permute-done | bytes 393248 | tf_op jit(solution)/shard_map/ppermute | solution.py:44
  377.8 4.2 %collective-permute-done.55 = bf16[768,256]{1,0:T(8,128)(2,1)S(1)} collective-permute-done((bf16[768,256]{1,0:T(8,128)(2,1)S(1)}, bf16[768,256]{1,0:T(8,128)(2,1)S(1)}, u32[]{:S(2)}, u32[]{:S(2)}) %collective-permute-start.55) | collective-permute-done | bytes 393248 | tf_op jit(solution)/shard_map/ppermute | solution.py:44
  382.8 3.4 copy-done.8
  (202 shorter events, 74.6 us)
Async XLA Ops:
  0.6 19.6 %collective-permute-start.1 = (bf16[256,1536]{1,0:T(8,128)(2,1)}, bf16[256,1536]{1,0:T(8,128)(2,1)S(1)}, u32[]{:S(2)}, u32[]{:S(2)}) collective-permute-start(bf16[256,1536]{1,0:T(8,128)(2,1)} %param.8), channel_id=1, source_target_pairs={{0,4},{2,6},{4,0},{6,2},{1,5},{3,7},{5,1},{7,3},{8,12},{10,14},{12... | collective-permute-start | bytes 2359304 | tf_op jit(solution)/shard_map/ppermute | solution.py:27
  20.2 31.7 %collective-permute-start = (bf16[256,1536]{1,0:T(8,128)(2,1)}, bf16[256,1536]{1,0:T(8,128)(2,1)}, u32[]{:S(2)}, u32[]{:S(2)}) collective-permute-start(bf16[256,1536]{1,0:T(8,128)(2,1)} %param.8), channel_id=1, source_target_pairs={{0,2},{2,0},{4,6},{6,4},{1,3},{3,1},{5,7},{7,5},{8,10},{10,8},{12,... | collective-permute-start | bytes 2359304 | tf_op jit(solution)/shard_map/ppermute | solution.py:27
  25.5 20.7 %collective-permute-start.3 = (bf16[256,1536]{1,0:T(8,128)(2,1)}, bf16[256,1536]{1,0:T(8,128)(2,1)}, u32[]{:S(2)}, u32[]{:S(2)}) collective-permute-start(bf16[256,1536]{1,0:T(8,128)(2,1)} %convolution_convert_fusion.2), channel_id=1, source_target_pairs={{0,4},{2,6},{4,0},{6,2},{1,5},{3,7},{5,1},{7,3},{8,12},{10,14},{12... | collective-permute-start | bytes 2359304 | tf_op jit(solution)/shard_map/ppermute | solution.py:27
  30.2 31.9 %collective-permute-start.6 = (bf16[256,1536]{1,0:T(8,128)(2,1)}, bf16[256,1536]{1,0:T(8,128)(2,1)}, u32[]{:S(2)}, u32[]{:S(2)}) collective-permute-start(bf16[256,1536]{1,0:T(8,128)(2,1)} %convolution_convert_fusion), channel_id=1, source_target_pairs={{0,4},{2,6},{4,0},{6,2},{1,5},{3,7},{5,1},{7,3},{8,12},{10,14},{12... | collective-permute-start | bytes 2359304 | tf_op jit(solution)/shard_map/ppermute | solution.py:27
  31.6 39.4 %collective-permute-start.8 = (bf16[256,1536]{1,0:T(8,128)(2,1)}, bf16[256,1536]{1,0:T(8,128)(2,1)}, u32[]{:S(2)}, u32[]{:S(2)}) collective-permute-start(bf16[256,1536]{1,0:T(8,128)(2,1)} %constant_dynamic-slice_fusion), channel_id=1, source_target_pairs={{0,2},{2,0},{4,6},{6,4},{1,3},{3,1},{5,7},{7,5},{8,10},{10,8},{12,... | collective-permute-start | bytes 2359304 | tf_op jit(solution)/shard_map/ppermute | solution.py:27
  32.6 38.3 %collective-permute-start.5 = (bf16[256,1536]{1,0:T(8,128)(2,1)}, bf16[256,1536]{1,0:T(8,128)(2,1)}, u32[]{:S(2)}, u32[]{:S(2)}) collective-permute-start(bf16[256,1536]{1,0:T(8,128)(2,1)} %constant_dynamic-slice_fusion.1), channel_id=1, source_target_pairs={{0,2},{2,0},{4,6},{6,4},{1,3},{3,1},{5,7},{7,5},{8,10},{10,8},{12,... | collective-permute-start | bytes 2359304 | tf_op jit(solution)/shard_map/ppermute | solution.py:27
  51.4 19.6 %collective-permute-start.4 = (bf16[256,1536]{1,0:T(8,128)(2,1)}, bf16[256,1536]{1,0:T(8,128)(2,1)}, u32[]{:S(2)}, u32[]{:S(2)}) collective-permute-start(bf16[256,1536]{1,0:T(8,128)(2,1)} %get-tuple-element.70), channel_id=1, source_target_pairs={{0,1},{1,0},{2,3},{3,2},{4,5},{5,4},{6,7},{7,6},{8,9},{9,8},{10,11... | collective-permute-start | bytes 2359304 | tf_op jit(solution)/shard_map/ppermute | solution.py:27
  67.2 19.0 %collective-permute-start.7 = (bf16[256,1536]{1,0:T(8,128)(2,1)}, bf16[256,1536]{1,0:T(8,128)(2,1)}, u32[]{:S(2)}, u32[]{:S(2)}) collective-permute-start(bf16[256,1536]{1,0:T(8,128)(2,1)} %get-tuple-element.72), channel_id=1, source_target_pairs={{0,1},{1,0},{2,3},{3,2},{4,5},{5,4},{6,7},{7,6},{8,9},{9,8},{10,11... | collective-permute-start | bytes 2359304 | tf_op jit(solution)/shard_map/ppermute | solution.py:27
  95.6 9.3 %collective-permute-start.11 = (bf16[512,256]{1,0:T(8,128)(2,1)S(1)}, bf16[512,256]{1,0:T(8,128)(2,1)S(1)}, u32[]{:S(2)}, u32[]{:S(2)}) collective-permute-start(bf16[512,256]{1,0:T(8,128)(2,1)S(1)} %pad_maximum_fusion.6), channel_id=1, source_target_pairs={{0,1},{1,0},{2,3},{3,2},{4,5},{5,4},{6,7},{7,6},{8,9},{9,8},{10,11... | collective-permute-start | bytes 786440 | tf_op jit(solution)/shard_map/ppermute | solution.py:27
  95.7 14.8 %collective-permute-start.19 = (bf16[512,256]{1,0:T(8,128)(2,1)S(1)}, bf16[512,256]{1,0:T(8,128)(2,1)S(1)}, u32[]{:S(2)}, u32[]{:S(2)}) collective-permute-start(bf16[512,256]{1,0:T(8,128)(2,1)S(1)} %pad_maximum_fusion.7), channel_id=1, source_target_pairs={{0,1},{1,0},{2,3},{3,2},{4,5},{5,4},{6,7},{7,6},{8,9},{9,8},{10,11... | collective-permute-start | bytes 786440 | tf_op jit(solution)/shard_map/ppermute | solution.py:27
  97.8 18.3 %collective-permute-start.27 = (bf16[512,256]{1,0:T(8,128)(2,1)S(1)}, bf16[512,256]{1,0:T(8,128)(2,1)S(1)}, u32[]{:S(2)}, u32[]{:S(2)}) collective-permute-start(bf16[512,256]{1,0:T(8,128)(2,1)S(1)} %pad_maximum_fusion.8), channel_id=1, source_target_pairs={{0,1},{1,0},{2,3},{3,2},{4,5},{5,4},{6,7},{7,6},{8,9},{9,8},{10,11... | collective-permute-start | bytes 786440 | tf_op jit(solution)/shard_map/ppermute | solution.py:27
  97.9 23.8 %collective-permute-start.35 = (bf16[512,256]{1,0:T(8,128)(2,1)S(1)}, bf16[512,256]{1,0:T(8,128)(2,1)S(1)}, u32[]{:S(2)}, u32[]{:S(2)}) collective-permute-start(bf16[512,256]{1,0:T(8,128)(2,1)S(1)} %pad_maximum_fusion.9), channel_id=1, source_target_pairs={{0,1},{1,0},{2,3},{3,2},{4,5},{5,4},{6,7},{7,6},{8,9},{9,8},{10,11... | collective-permute-start | bytes 786440 | tf_op jit(solution)/shard_map/ppermute | solution.py:27
  100.0 27.4 %collective-permute-start.43 = (bf16[512,256]{1,0:T(8,128)(2,1)S(1)}, bf16[512,256]{1,0:T(8,128)(2,1)S(1)}, u32[]{:S(2)}, u32[]{:S(2)}) collective-permute-start(bf16[512,256]{1,0:T(8,128)(2,1)S(1)} %pad_maximum_fusion.10), channel_id=1, source_target_pairs={{0,1},{1,0},{2,3},{3,2},{4,5},{5,4},{6,7},{7,6},{8,9},{9,8},{10,11... | collective-permute-start | bytes 786440 | tf_op jit(solution)/shard_map/ppermute | solution.py:27
  104.9 26.1 %collective-permute-start.51 = (bf16[512,256]{1,0:T(8,128)(2,1)S(1)}, bf16[512,256]{1,0:T(8,128)(2,1)S(1)}, u32[]{:S(2)}, u32[]{:S(2)}) collective-permute-start(bf16[512,256]{1,0:T(8,128)(2,1)S(1)} %pad_maximum_fusion.11), channel_id=1, source_target_pairs={{0,1},{1,0},{2,3},{3,2},{4,5},{5,4},{6,7},{7,6},{8,9},{9,8},{10,11... | collective-permute-start | bytes 786440 | tf_op jit(solution)/shard_map/ppermute | solution.py:27
  110.5 21.8 %collective-permute-start.12 = (bf16[512,256]{1,0:T(8,128)(2,1)S(1)}, bf16[512,256]{1,0:T(8,128)(2,1)S(1)}, u32[]{:S(2)}, u32[]{:S(2)}) collective-permute-start(bf16[512,256]{1,0:T(8,128)(2,1)S(1)} %get-tuple-element.57), channel_id=1, source_target_pairs={{0,4},{2,6},{4,0},{6,2},{1,5},{3,7},{5,1},{7,3},{8,12},{10,14},{12... | collective-permute-start | bytes 786440 | tf_op jit(solution)/shard_map/ppermute | solution.py:27
  116.1 19.4 %collective-permute-start.20 = (bf16[512,256]{1,0:T(8,128)(2,1)S(1)}, bf16[512,256]{1,0:T(8,128)(2,1)S(1)}, u32[]{:S(2)}, u32[]{:S(2)}) collective-permute-start(bf16[512,256]{1,0:T(8,128)(2,1)S(1)} %get-tuple-element.55), channel_id=1, source_target_pairs={{0,4},{2,6},{4,0},{6,2},{1,5},{3,7},{5,1},{7,3},{8,12},{10,14},{12... | collective-permute-start | bytes 786440 | tf_op jit(solution)/shard_map/ppermute | solution.py:27
  121.7 19.6 %collective-permute-start.28 = (bf16[512,256]{1,0:T(8,128)(2,1)S(1)}, bf16[512,256]{1,0:T(8,128)(2,1)S(1)}, u32[]{:S(2)}, u32[]{:S(2)}) collective-permute-start(bf16[512,256]{1,0:T(8,128)(2,1)S(1)} %get-tuple-element.53), channel_id=1, source_target_pairs={{0,4},{2,6},{4,0},{6,2},{1,5},{3,7},{5,1},{7,3},{8,12},{10,14},{12... | collective-permute-start | bytes 786440 | tf_op jit(solution)/shard_map/ppermute | solution.py:27
  127.4 17.6 %collective-permute-start.36 = (bf16[512,256]{1,0:T(8,128)(2,1)S(1)}, bf16[512,256]{1,0:T(8,128)(2,1)S(1)}, u32[]{:S(2)}, u32[]{:S(2)}) collective-permute-start(bf16[512,256]{1,0:T(8,128)(2,1)S(1)} %get-tuple-element.51), channel_id=1, source_target_pairs={{0,4},{2,6},{4,0},{6,2},{1,5},{3,7},{5,1},{7,3},{8,12},{10,14},{12... | collective-permute-start | bytes 786440 | tf_op jit(solution)/shard_map/ppermute | solution.py:27
  131.0 17.5 %collective-permute-start.44 = (bf16[512,256]{1,0:T(8,128)(2,1)S(1)}, bf16[512,256]{1,0:T(8,128)(2,1)S(1)}, u32[]{:S(2)}, u32[]{:S(2)}) collective-permute-start(bf16[512,256]{1,0:T(8,128)(2,1)S(1)} %get-tuple-element.49), channel_id=1, source_target_pairs={{0,4},{2,6},{4,0},{6,2},{1,5},{3,7},{5,1},{7,3},{8,12},{10,14},{12... | collective-permute-start | bytes 786440 | tf_op jit(solution)/shard_map/ppermute | solution.py:27
  132.3 19.8 %collective-permute-start.52 = (bf16[512,256]{1,0:T(8,128)(2,1)S(1)}, bf16[512,256]{1,0:T(8,128)(2,1)S(1)}, u32[]{:S(2)}, u32[]{:S(2)}) collective-permute-start(bf16[512,256]{1,0:T(8,128)(2,1)S(1)} %get-tuple-element.47), channel_id=1, source_target_pairs={{0,4},{2,6},{4,0},{6,2},{1,5},{3,7},{5,1},{7,3},{8,12},{10,14},{12... | collective-permute-start | bytes 786440 | tf_op jit(solution)/shard_map/ppermute | solution.py:27
  135.5 20.3 %collective-permute-start.13 = (bf16[768,256]{1,0:T(8,128)(2,1)S(1)}, bf16[768,256]{1,0:T(8,128)(2,1)S(1)}, u32[]{:S(2)}, u32[]{:S(2)}) collective-permute-start(bf16[768,256]{1,0:T(8,128)(2,1)S(1)} %get-tuple-element.44), channel_id=1, source_target_pairs={{0,8},{24,16},{1,9},{25,17},{2,10},{26,18},{3,11},{27,19},{4,12},{... | collective-permute-start | bytes 1179656 | tf_op jit(solution)/shard_map/ppermute | solution.py:37
  141.4 15.7 %collective-permute-start.16 = (bf16[768,256]{1,0:T(8,128)(2,1)S(1)}, bf16[768,256]{1,0:T(8,128)(2,1)S(1)}, u32[]{:S(2)}, u32[]{:S(2)}) collective-permute-start(bf16[768,256]{1,0:T(8,128)(2,1)S(1)} %get-tuple-element.45), channel_id=1, source_target_pairs={{0,8},{24,16},{1,9},{25,17},{2,10},{26,18},{3,11},{27,19},{4,12},{... | collective-permute-start | bytes 1179656 | tf_op jit(solution)/shard_map/ppermute | solution.py:37
  145.0 20.4 %collective-permute-start.21 = (bf16[768,256]{1,0:T(8,128)(2,1)S(1)}, bf16[768,256]{1,0:T(8,128)(2,1)S(1)}, u32[]{:S(2)}, u32[]{:S(2)}) collective-permute-start(bf16[768,256]{1,0:T(8,128)(2,1)S(1)} %get-tuple-element.40), channel_id=1, source_target_pairs={{0,8},{24,16},{1,9},{25,17},{2,10},{26,18},{3,11},{27,19},{4,12},{... | collective-permute-start | bytes 1179656 | tf_op jit(solution)/shard_map/ppermute | solution.py:37
  148.5 25.3 %collective-permute-start.24 = (bf16[768,256]{1,0:T(8,128)(2,1)S(1)}, bf16[768,256]{1,0:T(8,128)(2,1)S(1)}, u32[]{:S(2)}, u32[]{:S(2)}) collective-permute-start(bf16[768,256]{1,0:T(8,128)(2,1)S(1)} %get-tuple-element.41), channel_id=1, source_target_pairs={{0,8},{24,16},{1,9},{25,17},{2,10},{26,18},{3,11},{27,19},{4,12},{... | collective-permute-start | bytes 1179656 | tf_op jit(solution)/shard_map/ppermute | solution.py:37
  152.1 30.1 %collective-permute-start.29 = (bf16[768,256]{1,0:T(8,128)(2,1)S(1)}, bf16[768,256]{1,0:T(8,128)(2,1)S(1)}, u32[]{:S(2)}, u32[]{:S(2)}) collective-permute-start(bf16[768,256]{1,0:T(8,128)(2,1)S(1)} %get-tuple-element.36), channel_id=1, source_target_pairs={{0,8},{24,16},{1,9},{25,17},{2,10},{26,18},{3,11},{27,19},{4,12},{... | collective-permute-start | bytes 1179656 | tf_op jit(solution)/shard_map/ppermute | solution.py:37
  155.8 34.9 %collective-permute-start.32 = (bf16[768,256]{1,0:T(8,128)(2,1)S(1)}, bf16[768,256]{1,0:T(8,128)(2,1)S(1)}, u32[]{:S(2)}, u32[]{:S(2)}) collective-permute-start(bf16[768,256]{1,0:T(8,128)(2,1)S(1)} %get-tuple-element.37), channel_id=1, source_target_pairs={{0,8},{24,16},{1,9},{25,17},{2,10},{26,18},{3,11},{27,19},{4,12},{... | collective-permute-start | bytes 1179656 | tf_op jit(solution)/shard_map/ppermute | solution.py:37
  157.1 42.0 %collective-permute-start.37 = (bf16[768,256]{1,0:T(8,128)(2,1)S(1)}, bf16[768,256]{1,0:T(8,128)(2,1)S(1)}, u32[]{:S(2)}, u32[]{:S(2)}) collective-permute-start(bf16[768,256]{1,0:T(8,128)(2,1)S(1)} %get-tuple-element.32), channel_id=1, source_target_pairs={{0,8},{24,16},{1,9},{25,17},{2,10},{26,18},{3,11},{27,19},{4,12},{... | collective-permute-start | bytes 1179656 | tf_op jit(solution)/shard_map/ppermute | solution.py:37
  165.4 42.1 %collective-permute-start.40 = (bf16[768,256]{1,0:T(8,128)(2,1)S(1)}, bf16[768,256]{1,0:T(8,128)(2,1)S(1)}, u32[]{:S(2)}, u32[]{:S(2)}) collective-permute-start(bf16[768,256]{1,0:T(8,128)(2,1)S(1)} %get-tuple-element.33), channel_id=1, source_target_pairs={{0,8},{24,16},{1,9},{25,17},{2,10},{26,18},{3,11},{27,19},{4,12},{... | collective-permute-start | bytes 1179656 | tf_op jit(solution)/shard_map/ppermute | solution.py:37
  173.8 42.1 %collective-permute-start.45 = (bf16[768,256]{1,0:T(8,128)(2,1)S(1)}, bf16[768,256]{1,0:T(8,128)(2,1)S(1)}, u32[]{:S(2)}, u32[]{:S(2)}) collective-permute-start(bf16[768,256]{1,0:T(8,128)(2,1)S(1)} %get-tuple-element.28), channel_id=1, source_target_pairs={{0,8},{24,16},{1,9},{25,17},{2,10},{26,18},{3,11},{27,19},{4,12},{... | collective-permute-start | bytes 1179656 | tf_op jit(solution)/shard_map/ppermute | solution.py:37
  182.2 42.1 %collective-permute-start.48 = (bf16[768,256]{1,0:T(8,128)(2,1)S(1)}, bf16[768,256]{1,0:T(8,128)(2,1)S(1)}, u32[]{:S(2)}, u32[]{:S(2)}) collective-permute-start(bf16[768,256]{1,0:T(8,128)(2,1)S(1)} %get-tuple-element.29), channel_id=1, source_target_pairs={{0,8},{24,16},{1,9},{25,17},{2,10},{26,18},{3,11},{27,19},{4,12},{... | collective-permute-start | bytes 1179656 | tf_op jit(solution)/shard_map/ppermute | solution.py:37
  190.7 42.1 %collective-permute-start.53 = (bf16[768,256]{1,0:T(8,128)(2,1)S(1)}, bf16[768,256]{1,0:T(8,128)(2,1)S(1)}, u32[]{:S(2)}, u32[]{:S(2)}) collective-permute-start(bf16[768,256]{1,0:T(8,128)(2,1)S(1)} %get-tuple-element.24), channel_id=1, source_target_pairs={{0,8},{24,16},{1,9},{25,17},{2,10},{26,18},{3,11},{27,19},{4,12},{... | collective-permute-start | bytes 1179656 | tf_op jit(solution)/shard_map/ppermute | solution.py:37
  199.1 38.6 %collective-permute-start.56 = (bf16[768,256]{1,0:T(8,128)(2,1)S(1)}, bf16[768,256]{1,0:T(8,128)(2,1)S(1)}, u32[]{:S(2)}, u32[]{:S(2)}) collective-permute-start(bf16[768,256]{1,0:T(8,128)(2,1)S(1)} %get-tuple-element.25), channel_id=1, source_target_pairs={{0,8},{24,16},{1,9},{25,17},{2,10},{26,18},{3,11},{27,19},{4,12},{... | collective-permute-start | bytes 1179656 | tf_op jit(solution)/shard_map/ppermute | solution.py:37
  207.5 31.1 %collective-permute-start.17 = (bf16[768,256]{1,0:T(8,128)(2,1)S(1)}, bf16[768,256]{1,0:T(8,128)(2,1)S(1)}, u32[]{:S(2)}, u32[]{:S(2)}) collective-permute-start(bf16[768,256]{1,0:T(8,128)(2,1)S(1)} %get-tuple-element.43), channel_id=1, source_target_pairs={{8,16},{16,8},{9,17},{17,9},{10,18},{18,10},{11,19},{19,11},{12,20... | collective-permute-start | bytes 1179656 | tf_op jit(solution)/shard_map/ppermute | solution.py:39
  215.9 23.6 %collective-permute-start.14 = (bf16[768,256]{1,0:T(8,128)(2,1)S(1)}, bf16[768,256]{1,0:T(8,128)(2,1)S(1)}, u32[]{:S(2)}, u32[]{:S(2)}) collective-permute-start(bf16[768,256]{1,0:T(8,128)(2,1)S(1)} %get-tuple-element.42), channel_id=1, source_target_pairs={{8,16},{16,8},{9,17},{17,9},{10,18},{18,10},{11,19},{19,11},{12,20... | collective-permute-start | bytes 1179656 | tf_op jit(solution)/shard_map/ppermute | solution.py:39
  224.4 16.2 %collective-permute-start.25 = (bf16[768,256]{1,0:T(8,128)(2,1)S(1)}, bf16[768,256]{1,0:T(8,128)(2,1)S(1)}, u32[]{:S(2)}, u32[]{:S(2)}) collective-permute-start(bf16[768,256]{1,0:T(8,128)(2,1)S(1)} %get-tuple-element.39), channel_id=1, source_target_pairs={{8,16},{16,8},{9,17},{17,9},{10,18},{18,10},{11,19},{19,11},{12,20... | collective-permute-start | bytes 1179656 | tf_op jit(solution)/shard_map/ppermute | solution.py:39
  232.8 8.5 %collective-permute-start.22 = (bf16[768,256]{1,0:T(8,128)(2,1)S(1)}, bf16[768,256]{1,0:T(8,128)(2,1)S(1)}, u32[]{:S(2)}, u32[]{:S(2)}) collective-permute-start(bf16[768,256]{1,0:T(8,128)(2,1)S(1)} %get-tuple-element.38), channel_id=1, source_target_pairs={{8,16},{16,8},{9,17},{17,9},{10,18},{18,10},{11,19},{19,11},{12,20... | collective-permute-start | bytes 1179656 | tf_op jit(solution)/shard_map/ppermute | solution.py:39
  244.6 48.6 %collective-permute-start.18 = (bf16[768,256]{1,0:T(8,128)(2,1)S(1)}, bf16[768,256]{1,0:T(8,128)(2,1)S(1)}, u32[]{:S(2)}, u32[]{:S(2)}) collective-permute-start(bf16[768,256]{1,0:T(8,128)(2,1)S(1)} %add_convert_fusion.26), channel_id=1, source_target_pairs={{8,0},{16,24},{9,1},{17,25},{10,2},{18,26},{11,3},{19,27},{12,4},{... | collective-permute-start | bytes 1179656 | tf_op jit(solution)/shard_map/ppermute | solution.py:44
  246.2 55.4 %collective-permute-start.15 = (bf16[768,256]{1,0:T(8,128)(2,1)S(1)}, bf16[768,256]{1,0:T(8,128)(2,1)S(1)}, u32[]{:S(2)}, u32[]{:S(2)}) collective-permute-start(bf16[768,256]{1,0:T(8,128)(2,1)S(1)} %add_convert_fusion.28), channel_id=1, source_target_pairs={{8,0},{16,24},{9,1},{17,25},{10,2},{18,26},{11,3},{19,27},{12,4},{... | collective-permute-start | bytes 1179656 | tf_op jit(solution)/shard_map/ppermute | solution.py:44
  247.6 62.5 %collective-permute-start.26 = (bf16[768,256]{1,0:T(8,128)(2,1)S(1)}, bf16[768,256]{1,0:T(8,128)(2,1)S(1)}, u32[]{:S(2)}, u32[]{:S(2)}) collective-permute-start(bf16[768,256]{1,0:T(8,128)(2,1)S(1)} %add_convert_fusion.22), channel_id=1, source_target_pairs={{8,0},{16,24},{9,1},{17,25},{10,2},{18,26},{11,3},{19,27},{12,4},{... | collective-permute-start | bytes 1179656 | tf_op jit(solution)/shard_map/ppermute | solution.py:44
  249.0 69.5 %collective-permute-start.23 = (bf16[768,256]{1,0:T(8,128)(2,1)S(1)}, bf16[768,256]{1,0:T(8,128)(2,1)S(1)}, u32[]{:S(2)}, u32[]{:S(2)}) collective-permute-start(bf16[768,256]{1,0:T(8,128)(2,1)S(1)} %add_convert_fusion.24), channel_id=1, source_target_pairs={{8,0},{16,24},{9,1},{17,25},{10,2},{18,26},{11,3},{19,27},{12,4},{... | collective-permute-start | bytes 1179656 | tf_op jit(solution)/shard_map/ppermute | solution.py:44
  250.4 76.5 %collective-permute-start.34 = (bf16[768,256]{1,0:T(8,128)(2,1)S(1)}, bf16[768,256]{1,0:T(8,128)(2,1)S(1)}, u32[]{:S(2)}, u32[]{:S(2)}) collective-permute-start(bf16[768,256]{1,0:T(8,128)(2,1)S(1)} %add_convert_fusion.18), channel_id=1, source_target_pairs={{8,0},{16,24},{9,1},{17,25},{10,2},{18,26},{11,3},{19,27},{12,4},{... | collective-permute-start | bytes 1179656 | tf_op jit(solution)/shard_map/ppermute | solution.py:44
  293.2 42.1 %collective-permute-start.31 = (bf16[768,256]{1,0:T(8,128)(2,1)S(1)}, bf16[768,256]{1,0:T(8,128)(2,1)S(1)}, u32[]{:S(2)}, u32[]{:S(2)}) collective-permute-start(bf16[768,256]{1,0:T(8,128)(2,1)S(1)} %add_convert_fusion.20), channel_id=1, source_target_pairs={{8,0},{16,24},{9,1},{17,25},{10,2},{18,26},{11,3},{19,27},{12,4},{... | collective-permute-start | bytes 1179656 | tf_op jit(solution)/shard_map/ppermute | solution.py:44
  301.6 42.1 %collective-permute-start.42 = (bf16[768,256]{1,0:T(8,128)(2,1)S(1)}, bf16[768,256]{1,0:T(8,128)(2,1)S(1)}, u32[]{:S(2)}, u32[]{:S(2)}) collective-permute-start(bf16[768,256]{1,0:T(8,128)(2,1)S(1)} %add_convert_fusion.14), channel_id=1, source_target_pairs={{8,0},{16,24},{9,1},{17,25},{10,2},{18,26},{11,3},{19,27},{12,4},{... | collective-permute-start | bytes 1179656 | tf_op jit(solution)/shard_map/ppermute | solution.py:44
  310.0 42.1 %collective-permute-start.39 = (bf16[768,256]{1,0:T(8,128)(2,1)S(1)}, bf16[768,256]{1,0:T(8,128)(2,1)S(1)}, u32[]{:S(2)}, u32[]{:S(2)}) collective-permute-start(bf16[768,256]{1,0:T(8,128)(2,1)S(1)} %add_convert_fusion.16), channel_id=1, source_target_pairs={{8,0},{16,24},{9,1},{17,25},{10,2},{18,26},{11,3},{19,27},{12,4},{... | collective-permute-start | bytes 1179656 | tf_op jit(solution)/shard_map/ppermute | solution.py:44
  318.5 42.1 %collective-permute-start.50 = (bf16[768,256]{1,0:T(8,128)(2,1)S(1)}, bf16[768,256]{1,0:T(8,128)(2,1)S(1)}, u32[]{:S(2)}, u32[]{:S(2)}) collective-permute-start(bf16[768,256]{1,0:T(8,128)(2,1)S(1)} %add_convert_fusion.10), channel_id=1, source_target_pairs={{8,0},{16,24},{9,1},{17,25},{10,2},{18,26},{11,3},{19,27},{12,4},{... | collective-permute-start | bytes 1179656 | tf_op jit(solution)/shard_map/ppermute | solution.py:44
  326.9 42.1 %collective-permute-start.47 = (bf16[768,256]{1,0:T(8,128)(2,1)S(1)}, bf16[768,256]{1,0:T(8,128)(2,1)S(1)}, u32[]{:S(2)}, u32[]{:S(2)}) collective-permute-start(bf16[768,256]{1,0:T(8,128)(2,1)S(1)} %add_convert_fusion.12), channel_id=1, source_target_pairs={{8,0},{16,24},{9,1},{17,25},{10,2},{18,26},{11,3},{19,27},{12,4},{... | collective-permute-start | bytes 1179656 | tf_op jit(solution)/shard_map/ppermute | solution.py:44
  335.3 42.1 %collective-permute-start.58 = (bf16[768,256]{1,0:T(8,128)(2,1)S(1)}, bf16[768,256]{1,0:T(8,128)(2,1)S(1)}, u32[]{:S(2)}, u32[]{:S(2)}) collective-permute-start(bf16[768,256]{1,0:T(8,128)(2,1)S(1)} %add_convert_fusion.6), channel_id=1, source_target_pairs={{8,0},{16,24},{9,1},{17,25},{10,2},{18,26},{11,3},{19,27},{12,4},{... | collective-permute-start | bytes 1179656 | tf_op jit(solution)/shard_map/ppermute | solution.py:44
  343.7 38.3 %collective-permute-start.55 = (bf16[768,256]{1,0:T(8,128)(2,1)S(1)}, bf16[768,256]{1,0:T(8,128)(2,1)S(1)}, u32[]{:S(2)}, u32[]{:S(2)}) collective-permute-start(bf16[768,256]{1,0:T(8,128)(2,1)S(1)} %add_convert_fusion.8), channel_id=1, source_target_pairs={{8,0},{16,24},{9,1},{17,25},{10,2},{18,26},{11,3},{19,27},{12,4},{... | collective-permute-start | bytes 1179656 | tf_op jit(solution)/shard_map/ppermute | solution.py:44
  (31 other events, 566.8 us)

commit v2 on v1

v2 whole, which is shorter than its diff:
```python
import jax
import jax.numpy as jnp
from jax import lax
from jax.sharding import PartitionSpec as P

norm_eps = 1e-06
adam_eps = 1e-08
beta_one = 0.9
beta_two = 0.999
bias_one = 1.0 - 0.9**10
bias_two = 1.0 - 0.999**10
decay_rate = 0.1
outer_mu = 0.9

f32 = jnp.float32
bf16 = jnp.bfloat16


def outer_update(delta, momentum):
    new_momentum = outer_mu * momentum + delta
    outer_step = (delta + outer_mu * new_momentum).astype(bf16)
    return (new_momentum, outer_step)


def swap(value, axis, bit):
    count = lax.axis_size(axis)
    return lax.ppermute(value, axis, [(i, i ^ bit) for i in range(count)])


def tie(value, *others):
    for other in others:
        mark = other[(0,) * other.ndim]
        value = jnp.where(mark == mark, value, jnp.zeros_like(value))
    return value


def island_sums(values):
    count = lax.axis_size("island")
    half = count // 2
    me = lax.axis_index("island")
    passed = {}
    totals = []
    for j, value in enumerate(values):

        def send(payload, hop, pairs):
            passed[j, hop - 1] = payload
            if (j - 2, hop) in passed:
                payload = tie(payload, passed[j - 2, hop])
            return lax.ppermute(lax.optimization_barrier(payload), "island", pairs)

        held = value
        for hop in range(half - 1):
            came = send(held, hop, [(hop, hop + 1), (count - 1 - hop, count - 2 - hop)])
            held = (came.astype(f32) + value.astype(f32)).astype(bf16)
        came = send(held, half - 1, [(half - 1, half), (half, half - 1)])
        total = (held.astype(f32) + came.astype(f32)).astype(bf16)
        for step in range(half - 1):
            inner, outer = half - 1 - step, half - 2 - step
            pairs = [(inner, outer), (count - 1 - inner, count - 1 - outer)]
            came = send(total, half + step, pairs)
            total = jnp.where((me == outer) | (me == count - 1 - outer), came, total)
        total = lax.optimization_barrier(total)
        passed[j, 2 * half - 2] = total
        totals.append(total)
    return totals


def body(context, residual, cotangent, gain, weight, first_moment, second_moment, momentum):
    tok_rows = context.shape[0]
    width = gain.shape[0]
    fsdp_count = lax.axis_size("fsdp")
    group = fsdp_count // 2
    cols = weight.shape[1]
    t = lax.axis_index("tp")
    f = lax.axis_index("fsdp")
    high = f // group
    low = f % group
    near = t == high

    pieces = 2
    rows = tok_rows // pieces

    def regroup(array):
        parts = []
        for r in range(group):
            part = lax.dynamic_slice_in_dim(array, (low ^ r) * cols, cols, axis=1)
            parts.append(swap(part, "fsdp", r) if r else part)
        return parts

    def project(block):
        return lax.optimization_barrier(
            jnp.dot(block, weight, preferred_element_type=f32).astype(bf16)
        )

    residual_parts = regroup(residual)
    cotangent_parts = regroup(cotangent)

    near_blocks = [context] + [swap(context, "fsdp", r) for r in range(1, group)]
    far_pieces = [[swap(context[p * rows : (p + 1) * rows], "fsdp", group) for p in range(pieces)]]
    for r in range(1, group):
        far_pieces.append([swap(piece, "fsdp", r) for piece in far_pieces[0]])
    near_out = [project(block) for block in near_blocks]
    far_outs = []
    for r in range(group):
        for p in range(pieces):
            out = jnp.dot(far_pieces[r][p], weight, preferred_element_type=f32).astype(bf16)
            if r:
                out = tie(out, residual_parts[r], cotangent_parts[r], near_out[r])
            far_outs.append(swap(lax.optimization_barrier(out), "fsdp", group))

    gain_part = lax.dynamic_slice_in_dim(gain, t * (width // 2) + low * cols, cols).astype(f32)

    hidden, weighted, sums = [], [], []
    before = None
    for r in range(group):
        for p in range(pieces):
            span = slice(p * rows, (p + 1) * rows)
            far_out, own_out = lax.optimization_barrier((far_outs[r * pieces + p], near_out[r]))
            own_out = own_out[span]
            keep = jnp.where(near, own_out, far_out)
            sent = jnp.where(near, far_out, own_out)
            if before is not None:
                sent = tie(sent, before)
            before = sent
            came = swap(sent, "tp", 1)
            keep, came, res, cot = lax.optimization_barrier(
                (keep, came, residual_parts[r], cotangent_parts[r])
            )
            h = res[span].astype(f32) + keep.astype(f32) + came.astype(f32)
            w = gain_part[None, :] * cot[span].astype(f32)
            hidden.append(h)
            weighted.append(w)
            sums.append(jnp.stack([jnp.sum(h * h, axis=-1), jnp.sum(h * w, axis=-1)]))
    own_sums = jnp.concatenate(sums, axis=1)
    totals = own_sums
    for r in range(1, group):
        came = swap(own_sums, "fsdp", r)
        order = [r ^ k for k in range(group)]
        came = jnp.concatenate(
            [came[:, k * tok_rows : (k + 1) * tok_rows] for k in order], axis=1
        )
        totals = totals + came
    totals = totals + swap(totals, "tp", 1)
    inv_rms = lax.rsqrt(totals[0] / width + norm_eps)
    pull = inv_rms**3 * totals[1] / width

    tokens = near_blocks + [piece for block in far_pieces for piece in block]
    context_all = jnp.concatenate(tokens, axis=0)
    narrow = 128
    units = cols // narrow
    widths = [1, 1, 2]
    while sum(widths) < units:
        widths.append(min(4, units - sum(widths)))
    def at(h, q, x):
        return (h * group + q) * 2 + x

    ring_pairs, cross_pairs = [], []
    for q in range(group):
        ring_pairs += [(at(x, q, x), at(x, q, 1 - x)) for x in (0, 1)]
        ring_pairs += [(at(1 - x, q, x), at(x, q, x)) for x in (0, 1)]
        cross_pairs += [(at(1 - x, q, x), at(x, q, 1 - x)) for x in (0, 1)]

    parts = []
    pseudos, arrivals = [], []
    k = 0
    for c, wide in enumerate(widths):
        cols_at = slice(k * narrow, (k + wide) * narrow)
        d_local = jnp.concatenate(
            [
                weighted[j][:, cols_at] * inv_rms[j * rows : (j + 1) * rows, None]
                - hidden[j][:, cols_at] * pull[j * rows : (j + 1) * rows, None]
                for j in range(group * pieces)
            ],
            axis=0,
        ).astype(bf16)
        if c > 1:
            d_local = tie(d_local, arrivals[0 if c == 2 else c - 1])
        d_local = lax.optimization_barrier(d_local)
        ring = lax.ppermute(d_local, ("fsdp", "tp"), ring_pairs)
        cross = lax.ppermute(d_local, ("fsdp", "tp"), cross_pairs)
        arrivals.append(ring)
        d_near = jnp.where(near, d_local, ring)
        d_far = jnp.where(near, ring, cross)
        d_all = jnp.concatenate([d_near, d_far], axis=0)
        grad = lax.dot_general(
            context_all, d_all, (((0,), (0,)), ((), ())), preferred_element_type=f32
        ) / (tok_rows * fsdp_count)
        first = first_moment[0, :, cols_at].astype(f32)
        second = second_moment[0, :, cols_at].astype(f32)
        m_new = beta_one * first + (1.0 - beta_one) * grad
        v_new = beta_two * second + (1.0 - beta_two) * grad * grad
        update = m_new / bias_one / (
            jnp.sqrt(v_new / bias_two) + adam_eps
        ) + decay_rate * weight[:, cols_at].astype(f32)
        pseudos.append(lax.optimization_barrier(update.astype(bf16)))
        parts += [pseudos[c][:, u * narrow : (u + 1) * narrow] for u in range(wide)]
        k += wide
    momentum_out, step_out = [], []
    for k, total in enumerate(island_sums(parts)):
        cols_at = slice(k * narrow, (k + 1) * narrow)
        delta = total.astype(f32) / lax.axis_size("island")
        new_momentum, outer_step = outer_update(delta, momentum[:, cols_at])
        momentum_out.append(new_momentum)
        step_out.append(outer_step)
    return (jnp.concatenate(momentum_out, axis=1), jnp.concatenate(step_out, axis=1))


def solution(mesh):
    in_specs = (
        P(("island", "fsdp"), "tp"),
        P(("island", "fsdp"), "tp"),
        P(("island", "fsdp"), "tp"),
        P(),
        P("tp", "fsdp"),
        P("island", "tp", "fsdp"),
        P("island", "tp", "fsdp"),
        P("tp", "fsdp"),
    )
    out_specs = (P("tp", "fsdp"), P("tp", "fsdp"))
    return jax.shard_map(body, mesh=mesh, in_specs=in_specs, out_specs=out_specs, check_vma=False)
```

time: 390 us -> 360 us (0.923)
  waiting for transfers between devices: 254 us -> 106 us
  between operations: 1.72 us -> 52.8 us
  starting transfers between devices: 77.9 us -> 114 us
  local copies, waits for them, and re-layouts: 11.4 us -> 34.5 us
  other arithmetic: 12.8 us -> 17 us
    ppermute x36 -> x46, waiting for transfers between devices: 168 us -> 58.5 us  [the longest x36 56.5 us: send(): return lax.ppermute(lax.optimization_barrier(payload), 'island', pairs)]
    ppermute x36 -> x46, starting transfers between devices: 60.7 us -> 102 us  [the longest x36 84.7 us: send(): return lax.ppermute(lax.optimization_barrier(payload), 'island', pairs)]
    ppermute x23 -> x17, waiting for transfers between devices: 86.5 us -> 47.1 us  [swap(): return lax.ppermute(value, axis, [(i, i ^ bit) for i in range(count)])]
    slice x8 -> x42, local copies, waits for them, and re-layouts: 0.33 us -> 22.8 us  [the longest x39 20.7 us: tie(): mark = other[(0,) * other.ndim]]
    dot_general x6 -> x5, matrix products: 13.1 us -> 20.4 us  [body(): lax.dot_general(context_all, d_all, (((0,), (0,)), ((), ())), preferred_e...]
    select_n x18 -> x45, other arithmetic: 1.11 us -> 7.58 us  [the longest x27 3.88 us: tie(): value = jnp.where(mark == mark, value, jnp.zeros_like(value))]
    ppermute x23 -> x17, starting transfers between devices: 17.2 us -> 11.7 us  [swap(): return lax.ppermute(value, axis, [(i, i ^ bit) for i in range(count)])]
    dot_general x4 -> x6, matrix products: 17.3 us -> 11.9 us  [the longest x2 6.25 us: project(): jnp.dot(block, weight, preferred_element_type=f32).astype(bf16)]
  transfers between devices with their start and end apart: 59 -> 63, of which waited for: 34 -> 22; matrix products, arithmetic and copies ran while one was open for 11% -> 20% of each run, Pallas kernels for 0% -> 0%
where the time goes in v2:
time: 360 us; the launch traced here: 356 us
  starting transfers between devices  114 us (32%)
  waiting for transfers between devices  106 us (29%)
  between operations  52.8 us (15%)
  local copies, waits for them, and re-layouts  34.5 us (10%)
  matrix products  32.3 us (9%)
  other arithmetic  17 us (5%)
    ppermute x36, starting transfers between devices, send(): return lax.ppermute(lax.optimization_barrier(payload), 'island', pairs)  84.7 us
    ppermute x36, waiting for transfers between devices, send(): return lax.ppermute(lax.optimization_barrier(payload), 'island', pairs)  56.5 us
    ppermute x17, waiting for transfers between devices, swap(): return lax.ppermute(value, axis, [(i, i ^ bit) for i in range(count)])  47.1 us
    slice x39, local copies, waits for them, and re-layouts, tie(): mark = other[(0,) * other.ndim]  20.7 us
    dot_general x5, matrix products, body(): lax.dot_general(context_all, d_all, (((0,), (0,)), ((), ())), preferred_e...  20.4 us
    ppermute x5, starting transfers between devices, body(): cross = lax.ppermute(d_local, ('fsdp', 'tp'), cross_pairs)  16.7 us
    ppermute x17, starting transfers between devices, swap(): return lax.ppermute(value, axis, [(i, i ^ bit) for i in range(count)])  11.7 us
    unnamed x27, local copies, waits for them, and re-layouts  8.15 us
  transfers between devices with their start and end apart: 63, of which 22 were waited for; matrix products, arithmetic and copies ran while one was open for 20% of the time, Pallas kernels for 0%

profile of v2, /device:TPU:2, one launch (start us, length us, event | category | flops | bytes accessed | tf_op | source)
XLA Modules:
  0.0 355.8 jit_solution(17015284663545308334)
XLA Ops:
  0.7 2.2 fusion.156
  4.9 2.5 constant_dynamic-slice_fusion.3
  8.9 6.1 %collective-permute-done.2 = bf16[128,1536]{1,0:T(8,128)(2,1)S(1)} collective-permute-done((bf16[128,1536]{1,0:T(8,128)(2,1)}, bf16[128,1536]{1,0:T(8,128)(2,1)S(1)}, u32[]{:S(2)}, u32[]{:S(2)}) %collective-permute-start.2) | collective-permute-done | bytes 393248 | tf_op jit(solution)/shard_map/ppermute | solution.py:27
  18.1 5.4 %collective-permute-done.1 = bf16[128,1536]{1,0:T(8,128)(2,1)} collective-permute-done((bf16[128,1536]{1,0:T(8,128)(2,1)}, bf16[128,1536]{1,0:T(8,128)(2,1)}, u32[]{:S(2)}, u32[]{:S(2)}) %collective-permute-start.1) | collective-permute-done | bytes 393248 | tf_op jit(solution)/shard_map/ppermute | solution.py:27
  23.6 2.5 convolution_convert_fusion.5
  27.6 2.3 convolution_convert_fusion.1
  32.0 7.9 %collective-permute-done.5 = bf16[128,1536]{1,0:T(8,128)(2,1)} collective-permute-done((bf16[128,1536]{1,0:T(8,128)(2,1)}, bf16[128,1536]{1,0:T(8,128)(2,1)}, u32[]{:S(2)}, u32[]{:S(2)}) %collective-permute-start.5) | collective-permute-done | bytes 393248 | tf_op jit(solution)/shard_map/ppermute | solution.py:27
  44.3 4.0 %convolution_convert_fusion = bf16[256,1536]{1,0:T(8,128)(2,1)S(1)} fusion(bf16[256,1536]{1,0:T(8,128)(2,1)} %collective-permute-done, bf16[1536,1536]{1,0:T(8,128)(2,1)} %param.12), kind=kOutput, calls=%fused_computation.18 | convolution fusion | flops 1208352768 | bytes 6291456 | tf_op jit(solution)/shard_map/dot_general | solution.py:92
  51.9 1.8 collective-permute-start.6
  59.7 1.6 collective-permute-start.11
  64.0 7.7 %collective-permute-done.11 = bf16[128,1536]{1,0:T(8,128)(2,1)S(1)} collective-permute-done((bf16[128,1536]{1,0:T(8,128)(2,1)S(1)}, bf16[128,1536]{1,0:T(8,128)(2,1)S(1)}, u32[]{:S(2)}, u32[]{:S(2)}) %collective-permute-start.11) | collective-permute-done | bytes 393248 | tf_op jit(solution)/shard_map/ppermute | solution.py:27
  73.9 5.2 %collective-permute-done.13 = bf16[128,1536]{1,0:T(8,128)(2,1)S(1)} collective-permute-done((bf16[128,1536]{1,0:T(8,128)(2,1)S(1)}, bf16[128,1536]{1,0:T(8,128)(2,1)S(1)}, u32[]{:S(2)}, u32[]{:S(2)}) %collective-permute-start.13) | collective-permute-done | bytes 393248 | tf_op jit(solution)/shard_map/ppermute | solution.py:27
  81.7 8.0 %collective-permute-done.14 = bf16[128,1536]{1,0:T(8,128)(2,1)S(1)} collective-permute-done((bf16[128,1536]{1,0:T(8,128)(2,1)S(1)}, bf16[128,1536]{1,0:T(8,128)(2,1)S(1)}, u32[]{:S(2)}, u32[]{:S(2)}) %collective-permute-start.14) | collective-permute-done | bytes 393248 | tf_op jit(solution)/shard_map/ppermute | solution.py:27
  89.8 2.0 multiply_reduce_fusion.7
  94.0 2.8 collective-permute-done.16
  98.2 3.4 collective-permute-start.18
  101.7 3.3 collective-permute-start.23
  105.2 2.0 collective-permute-done.17
  109.0 3.2 collective-permute-start.28
  112.6 2.6 fusion.64
  115.1 2.6 fusion.63
  117.7 3.6 %collective-permute-start.19 = (bf16[1536,128]{1,0:T(8,128)(2,1)S(1)}, bf16[1536,128]{1,0:T(8,128)(2,1)S(1)}, u32[]{:S(2)}, u32[]{:S(2)}) collective-permute-start(bf16[1536,128]{1,0:T(8,128)(2,1)S(1)} %fusion.63), channel_id=1, source_target_pairs={{0,8},{24,16},{1,9},{25,17},{2,10},{26,18},{3,11},{27,19},{4,12},{... | collective-permute-start | bytes 1179656 | tf_op jit(solution)/shard_map/ppermute | solution.py:49
  124.5 3.4 collective-permute-start.36
  128.1 3.7 %fusion.26 = bf16[1536,256]{1,0:T(8,128)(2,1)S(1)} fusion(bf16[1536,1536]{1,0:T(8,128)(2,1)S(1)} %bitcast.187, bf16[1,1536,1536]{2,1,0:T(8,128)(2,1)} %param.14, bf16[1,1536,1536]{2,1,0:T(8,128)(2,1)} %param.13, bf16[1024,1536]{1,0:T(8,128)(2,1)S(1)} %constant_dynamic-update-slice_fusion, bf16[512,256]{1,0:T(8,128)(2,1)S(1)} %get-tuple-element.146, ...), kind=kOutput, calls=%fused_computation.38 | convolution fusion | flops 813432832 | bytes 6815744 | tf_op jit(solution)/shard_map/dot_general | solution.py:185
  132.5 2.6 collective-permute-done.24
  139.8 8.9 %collective-permute-start.29 = (bf16[1536,128]{1,0:T(8,128)(2,1)S(1)}, bf16[1536,128]{1,0:T(8,128)(2,1)S(1)}, u32[]{:S(2)}, u32[]{:S(2)}) collective-permute-start(bf16[1536,128]{1,0:T(8,128)(2,1)S(1)} %get-tuple-element.138), channel_id=1, source_target_pairs={{0,8},{24,16},{1,9},{25,17},{2,10},{26,18},{3,11},{27,19},{4,12},{... | collective-permute-start | bytes 1179656 | tf_op jit(solution)/shard_map/ppermute | solution.py:49
  148.7 6.1 %collective-permute-start.32 = (bf16[1536,128]{1,0:T(8,128)(2,1)S(1)}, bf16[1536,128]{1,0:T(8,128)(2,1)S(1)}, u32[]{:S(2)}, u32[]{:S(2)}) collective-permute-start(bf16[1536,128]{1,0:T(8,128)(2,1)S(1)} %get-tuple-element.137), channel_id=1, source_target_pairs={{0,8},{24,16},{1,9},{25,17},{2,10},{26,18},{3,11},{27,19},{4,12},{... | collective-permute-start | bytes 1179656 | tf_op jit(solution)/shard_map/ppermute | solution.py:49
  157.3 3.4 collective-permute-start.50
  170.6 3.1 collective-permute-done.21
  176.2 4.6 %collective-permute-done.26 = bf16[1536,128]{1,0:T(8,128)(2,1)S(1)} collective-permute-done((bf16[1536,128]{1,0:T(8,128)(2,1)S(1)}, bf16[1536,128]{1,0:T(8,128)(2,1)S(1)}, u32[]{:S(2)}, u32[]{:S(2)}) %collective-permute-start.26) | collective-permute-done | bytes 393248 | tf_op jit(solution)/shard_map/ppermute | solution.py:49
  191.1 5.8 %fusion.13 = bf16[1536,512]{1,0:T(8,128)(2,1)S(1)} fusion(bf16[1536,1536]{1,0:T(8,128)(2,1)S(1)} %bitcast.187, bf16[1,1536,1536]{2,1,0:T(8,128)(2,1)} %param.14, bf16[1,1536,1536]{2,1,0:T(8,128)(2,1)} %param.13, bf16[1024,1536]{1,0:T(8,128)(2,1)S(1)} %constant_dynamic-update-slice_fusion, bf16[512,512]{1,0:T(8,128)(2,1)S(1)} %get-tuple-element.142, ...), kind=kOutput, calls=%fused_computation.17 | convolution fusion | flops 1626865664 | bytes 10485760 | tf_op jit(solution)/shard_map/dot_general | solution.py:185
  196.9 5.8 %fusion.12 = bf16[1536,512]{1,0:T(8,128)(2,1)S(1)} fusion(bf16[1536,1536]{1,0:T(8,128)(2,1)S(1)} %bitcast.187, bf16[1,1536,1536]{2,1,0:T(8,128)(2,1)} %param.14, bf16[1,1536,1536]{2,1,0:T(8,128)(2,1)} %param.13, bf16[1024,1536]{1,0:T(8,128)(2,1)S(1)} %constant_dynamic-update-slice_fusion, bf16[512,512]{1,0:T(8,128)(2,1)S(1)} %get-tuple-element.171, ...), kind=kOutput, calls=%fused_computation.16 | convolution fusion | flops 1626865664 | bytes 10485760 | tf_op jit(solution)/shard_map/dot_general | solution.py:185
  202.8 6.7 %collective-permute-start.40 = (bf16[1536,128]{1,0:T(8,128)(2,1)S(1)}, bf16[1536,128]{1,0:T(8,128)(2,1)S(1)}, u32[]{:S(2)}, u32[]{:S(2)}) collective-permute-start(bf16[1536,128]{1,0:T(8,128)(2,1)S(1)} %broadcast_select_fusion.23), channel_id=1, source_target_pairs={{0,8},{24,16},{1,9},{25,17},{2,10},{26,18},{3,11},{27,19},{4,12},{... | collective-permute-start | bytes 1179656 | tf_op jit(solution)/shard_map/ppermute | solution.py:49
  214.0 4.9 %collective-permute-done.40 = bf16[1536,128]{1,0:T(8,128)(2,1)S(1)} collective-permute-done((bf16[1536,128]{1,0:T(8,128)(2,1)S(1)}, bf16[1536,128]{1,0:T(8,128)(2,1)S(1)}, u32[]{:S(2)}, u32[]{:S(2)}) %collective-permute-start.40) | collective-permute-done | bytes 393248 | tf_op jit(solution)/shard_map/ppermute | solution.py:49
  221.7 6.5 %collective-permute-start.37 = (bf16[1536,128]{1,0:T(8,128)(2,1)S(1)}, bf16[1536,128]{1,0:T(8,128)(2,1)S(1)}, u32[]{:S(2)}, u32[]{:S(2)}) collective-permute-start(bf16[1536,128]{1,0:T(8,128)(2,1)S(1)} %get-tuple-element.118), channel_id=1, source_target_pairs={{0,8},{24,16},{1,9},{25,17},{2,10},{26,18},{3,11},{27,19},{4,12},{... | collective-permute-start | bytes 1179656 | tf_op jit(solution)/shard_map/ppermute | solution.py:49
  232.9 3.5 collective-permute-done.37
  236.4 8.4 %collective-permute-done.46 = bf16[1536,128]{1,0:T(8,128)(2,1)S(1)} collective-permute-done((bf16[1536,128]{1,0:T(8,128)(2,1)S(1)}, bf16[1536,128]{1,0:T(8,128)(2,1)S(1)}, u32[]{:S(2)}, u32[]{:S(2)}) %collective-permute-start.46) | collective-permute-done | bytes 393248 | tf_op jit(solution)/shard_map/ppermute | solution.py:49
  248.9 4.4 %collective-permute-start.43 = (bf16[1536,128]{1,0:T(8,128)(2,1)S(1)}, bf16[1536,128]{1,0:T(8,128)(2,1)S(1)}, u32[]{:S(2)}, u32[]{:S(2)}) collective-permute-start(bf16[1536,128]{1,0:T(8,128)(2,1)S(1)} %broadcast_select_fusion.20), channel_id=1, source_target_pairs={{0,8},{24,16},{1,9},{25,17},{2,10},{26,18},{3,11},{27,19},{4,12},{... | collective-permute-start | bytes 1179656 | tf_op jit(solution)/shard_map/ppermute | solution.py:49
  259.9 2.8 collective-permute-done.43
  270.8 9.6 %collective-permute-start.60 = (bf16[1536,128]{1,0:T(8,128)(2,1)S(1)}, bf16[1536,128]{1,0:T(8,128)(2,1)S(1)}, u32[]{:S(2)}, u32[]{:S(2)}) collective-permute-start(bf16[1536,128]{1,0:T(8,128)(2,1)S(1)} %broadcast_select_fusion.5), channel_id=1, source_target_pairs={{0,8},{24,16},{1,9},{25,17},{2,10},{26,18},{3,11},{27,19},{4,12},{... | collective-permute-start | bytes 1179656 | tf_op jit(solution)/shard_map/ppermute | solution.py:49
  287.6 3.2 collective-permute-done.48
  296.2 4.6 %collective-permute-start.51 = (bf16[1536,128]{1,0:T(8,128)(2,1)S(1)}, bf16[1536,128]{1,0:T(8,128)(2,1)S(1)}, u32[]{:S(2)}, u32[]{:S(2)}) collective-permute-start(bf16[1536,128]{1,0:T(8,128)(2,1)S(1)} %get-tuple-element.114), channel_id=1, source_target_pairs={{0,8},{24,16},{1,9},{25,17},{2,10},{26,18},{3,11},{27,19},{4,12},{... | collective-permute-start | bytes 1179656 | tf_op jit(solution)/shard_map/ppermute | solution.py:49
  308.5 6.1 %collective-permute-start.57 = (bf16[1536,128]{1,0:T(8,128)(2,1)S(1)}, bf16[1536,128]{1,0:T(8,128)(2,1)S(1)}, u32[]{:S(2)}, u32[]{:S(2)}) collective-permute-start(bf16[1536,128]{1,0:T(8,128)(2,1)S(1)} %broadcast_select_fusion.8), channel_id=1, source_target_pairs={{0,8},{24,16},{1,9},{25,17},{2,10},{26,18},{3,11},{27,19},{4,12},{... | collective-permute-start | bytes 1179656 | tf_op jit(solution)/shard_map/ppermute | solution.py:49
  320.7 3.9 %collective-permute-done.62 = bf16[1536,128]{1,0:T(8,128)(2,1)S(1)} collective-permute-done((bf16[1536,128]{1,0:T(8,128)(2,1)S(1)}, bf16[1536,128]{1,0:T(8,128)(2,1)S(1)}, u32[]{:S(2)}, u32[]{:S(2)}) %collective-permute-start.62) | collective-permute-done | bytes 393248 | tf_op jit(solution)/shard_map/ppermute | solution.py:49
  325.6 11.7 %collective-permute-done.53 = bf16[1536,128]{1,0:T(8,128)(2,1)S(1)} collective-permute-done((bf16[1536,128]{1,0:T(8,128)(2,1)S(1)}, bf16[1536,128]{1,0:T(8,128)(2,1)S(1)}, u32[]{:S(2)}, u32[]{:S(2)}) %collective-permute-start.53) | collective-permute-done | bytes 393248 | tf_op jit(solution)/shard_map/ppermute | solution.py:49
  341.4 7.6 %collective-permute-done.59 = bf16[1536,128]{1,0:T(8,128)(2,1)S(1)} collective-permute-done((bf16[1536,128]{1,0:T(8,128)(2,1)S(1)}, bf16[1536,128]{1,0:T(8,128)(2,1)S(1)}, u32[]{:S(2)}, u32[]{:S(2)}) %collective-permute-start.59) | collective-permute-done | bytes 393248 | tf_op jit(solution)/shard_map/ppermute | solution.py:49
  350.0 2.0 copy-done.5
  352.0 3.7 %copy-done.4 = f32[1536,1536]{1,0:T(8,128)} copy-done((f32[1536,1536]{1,0:T(8,128)}, f32[1536,1536]{1,0:T(8,128)S(1)}, u32[]{:S(2)}) %copy-start.4) | copy-done | bytes 9437208
  (259 shorter events, 83.1 us)
Async XLA Ops:
  0.6 43.3 %collective-permute-start = (bf16[256,1536]{1,0:T(8,128)(2,1)}, bf16[256,1536]{1,0:T(8,128)(2,1)}, u32[]{:S(2)}, u32[]{:S(2)}) collective-permute-start(bf16[256,1536]{1,0:T(8,128)(2,1)} %param.8), channel_id=1, source_target_pairs={{0,2},{2,0},{4,6},{6,4},{1,3},{3,1},{5,7},{7,5},{8,10},{10,8},{12,... | collective-permute-start | bytes 2359304 | tf_op jit(solution)/shard_map/ppermute | solution.py:27
  2.9 12.2 %collective-permute-start.2 = (bf16[128,1536]{1,0:T(8,128)(2,1)}, bf16[128,1536]{1,0:T(8,128)(2,1)S(1)}, u32[]{:S(2)}, u32[]{:S(2)}) collective-permute-start(bf16[128,1536]{1,0:T(8,128)(2,1)} %get-tuple-element.139), channel_id=1, source_target_pairs={{0,4},{2,6},{4,0},{6,2},{1,5},{3,7},{5,1},{7,3},{8,12},{10,14},{12... | collective-permute-start | bytes 1179656 | tf_op jit(solution)/shard_map/ppermute | solution.py:27
  4.4 19.2 %collective-permute-start.1 = (bf16[128,1536]{1,0:T(8,128)(2,1)}, bf16[128,1536]{1,0:T(8,128)(2,1)}, u32[]{:S(2)}, u32[]{:S(2)}) collective-permute-start(bf16[128,1536]{1,0:T(8,128)(2,1)} %get-tuple-element.140), channel_id=1, source_target_pairs={{0,4},{2,6},{4,0},{6,2},{1,5},{3,7},{5,1},{7,3},{8,12},{10,14},{12... | collective-permute-start | bytes 1179656 | tf_op jit(solution)/shard_map/ppermute | solution.py:27
  7.4 44.5 %collective-permute-start.10 = (bf16[256,1536]{1,0:T(8,128)(2,1)}, bf16[256,1536]{1,0:T(8,128)(2,1)}, u32[]{:S(2)}, u32[]{:S(2)}) collective-permute-start(bf16[256,1536]{1,0:T(8,128)(2,1)} %get-tuple-element.122), channel_id=1, source_target_pairs={{0,2},{2,0},{4,6},{6,4},{1,3},{3,1},{5,7},{7,5},{8,10},{10,8},{12,... | collective-permute-start | bytes 2359304 | tf_op jit(solution)/shard_map/ppermute | solution.py:27
  8.4 47.8 %collective-permute-start.9 = (bf16[256,1536]{1,0:T(8,128)(2,1)}, bf16[256,1536]{1,0:T(8,128)(2,1)S(1)}, u32[]{:S(2)}, u32[]{:S(2)}) collective-permute-start(bf16[256,1536]{1,0:T(8,128)(2,1)} %get-tuple-element.120), channel_id=1, source_target_pairs={{0,2},{2,0},{4,6},{6,4},{1,3},{3,1},{5,7},{7,5},{8,10},{10,8},{12,... | collective-permute-start | bytes 2359304 | tf_op jit(solution)/shard_map/ppermute | solution.py:27
  16.6 15.4 %collective-permute-start.7 = (bf16[128,1536]{1,0:T(8,128)(2,1)}, bf16[128,1536]{1,0:T(8,128)(2,1)}, u32[]{:S(2)}, u32[]{:S(2)}) collective-permute-start(bf16[128,1536]{1,0:T(8,128)(2,1)} %convolution_convert_fusion.4), channel_id=1, source_target_pairs={{0,4},{2,6},{4,0},{6,2},{1,5},{3,7},{5,1},{7,3},{8,12},{10,14},{12... | collective-permute-start | bytes 1179656 | tf_op jit(solution)/shard_map/ppermute | solution.py:27
  26.1 13.8 %collective-permute-start.5 = (bf16[128,1536]{1,0:T(8,128)(2,1)}, bf16[128,1536]{1,0:T(8,128)(2,1)}, u32[]{:S(2)}, u32[]{:S(2)}) collective-permute-start(bf16[128,1536]{1,0:T(8,128)(2,1)} %convolution_convert_fusion.5), channel_id=1, source_target_pairs={{0,4},{2,6},{4,0},{6,2},{1,5},{3,7},{5,1},{7,3},{8,12},{10,14},{12... | collective-permute-start | bytes 1179656 | tf_op jit(solution)/shard_map/ppermute | solution.py:27
  32.0 26.0 %collective-permute-start.4 = (bf16[128,1536]{1,0:T(8,128)(2,1)S(1)}, bf16[128,1536]{1,0:T(8,128)(2,1)S(1)}, u32[]{:S(2)}, u32[]{:S(2)}) collective-permute-start(bf16[128,1536]{1,0:T(8,128)(2,1)S(1)} %collective-permute-done.2), channel_id=1, source_target_pairs={{0,2},{2,0},{4,6},{6,4},{1,3},{3,1},{5,7},{7,5},{8,10},{10,8},{12,... | collective-permute-start | bytes 1179656 | tf_op jit(solution)/shard_map/ppermute | solution.py:27
  39.9 19.0 %collective-permute-start.3 = (bf16[128,1536]{1,0:T(8,128)(2,1)}, bf16[128,1536]{1,0:T(8,128)(2,1)S(1)}, u32[]{:S(2)}, u32[]{:S(2)}) collective-permute-start(bf16[128,1536]{1,0:T(8,128)(2,1)} %collective-permute-done.1), channel_id=1, source_target_pairs={{0,2},{2,0},{4,6},{6,4},{1,3},{3,1},{5,7},{7,5},{8,10},{10,8},{12,... | collective-permute-start | bytes 1179656 | tf_op jit(solution)/shard_map/ppermute | solution.py:27
  43.9 35.9 %collective-permute-start.8 = (bf16[128,1536]{1,0:T(8,128)(2,1)S(1)}, bf16[128,1536]{1,0:T(8,128)(2,1)S(1)}, u32[]{:S(2)}, u32[]{:S(2)}) collective-permute-start(bf16[128,1536]{1,0:T(8,128)(2,1)S(1)} %get-tuple-element.126), channel_id=1, source_target_pairs={{0,1},{1,0},{2,3},{3,2},{4,5},{5,4},{6,7},{7,6},{8,9},{9,8},{10,11... | collective-permute-start | bytes 1179656 | tf_op jit(solution)/shard_map/ppermute | solution.py:27
  51.9 27.9 %collective-permute-start.6 = (bf16[128,1536]{1,0:T(8,128)(2,1)S(1)}, bf16[128,1536]{1,0:T(8,128)(2,1)S(1)}, u32[]{:S(2)}, u32[]{:S(2)}) collective-permute-start(bf16[128,1536]{1,0:T(8,128)(2,1)S(1)} %get-tuple-element.124), channel_id=1, source_target_pairs={{0,1},{1,0},{2,3},{3,2},{4,5},{5,4},{6,7},{7,6},{8,9},{9,8},{10,11... | collective-permute-start | bytes 1179656 | tf_op jit(solution)/shard_map/ppermute | solution.py:27
  59.7 12.1 %collective-permute-start.11 = (bf16[128,1536]{1,0:T(8,128)(2,1)S(1)}, bf16[128,1536]{1,0:T(8,128)(2,1)S(1)}, u32[]{:S(2)}, u32[]{:S(2)}) collective-permute-start(bf16[128,1536]{1,0:T(8,128)(2,1)S(1)} %fusion.16), channel_id=1, source_target_pairs={{0,4},{2,6},{4,0},{6,2},{1,5},{3,7},{5,1},{7,3},{8,12},{10,14},{12... | collective-permute-start | bytes 1179656 | tf_op jit(solution)/shard_map/ppermute | solution.py:27
  61.3 17.9 %collective-permute-start.13 = (bf16[128,1536]{1,0:T(8,128)(2,1)S(1)}, bf16[128,1536]{1,0:T(8,128)(2,1)S(1)}, u32[]{:S(2)}, u32[]{:S(2)}) collective-permute-start(bf16[128,1536]{1,0:T(8,128)(2,1)S(1)} %fusion.19), channel_id=1, source_target_pairs={{0,4},{2,6},{4,0},{6,2},{1,5},{3,7},{5,1},{7,3},{8,12},{10,14},{12... | collective-permute-start | bytes 1179656 | tf_op jit(solution)/shard_map/ppermute | solution.py:27
  79.2 10.6 %collective-permute-start.14 = (bf16[128,1536]{1,0:T(8,128)(2,1)S(1)}, bf16[128,1536]{1,0:T(8,128)(2,1)S(1)}, u32[]{:S(2)}, u32[]{:S(2)}) collective-permute-start(bf16[128,1536]{1,0:T(8,128)(2,1)S(1)} %get-tuple-element.129), channel_id=1, source_target_pairs={{0,1},{1,0},{2,3},{3,2},{4,5},{5,4},{6,7},{7,6},{8,9},{9,8},{10,11... | collective-permute-start | bytes 1179656 | tf_op jit(solution)/shard_map/ppermute | solution.py:27
  98.2 14.3 %collective-permute-start.18 = (bf16[512,128]{1,0:T(8,128)(2,1)S(1)}, bf16[512,128]{1,0:T(8,128)(2,1)S(1)}, u32[]{:S(2)}, u32[]{:S(2)}) collective-permute-start(bf16[512,128]{1,0:T(8,128)(2,1)S(1)} %pad_maximum_fusion), channel_id=1, source_target_pairs={{4,1},{1,4},{6,3},{3,6},{12,9},{9,12},{14,11},{11,14},{20,17},{17,... | collective-permute-start | bytes 393224 | tf_op jit(solution)/shard_map/ppermute | solution.py:180
  101.7 10.8 %collective-permute-start.23 = (bf16[512,128]{1,0:T(8,128)(2,1)S(1)}, bf16[512,128]{1,0:T(8,128)(2,1)S(1)}, u32[]{:S(2)}, u32[]{:S(2)}) collective-permute-start(bf16[512,128]{1,0:T(8,128)(2,1)S(1)} %pad_maximum_fusion.1), channel_id=1, source_target_pairs={{4,1},{1,4},{6,3},{3,6},{12,9},{9,12},{14,11},{11,14},{20,17},{17,... | collective-permute-start | bytes 393224 | tf_op jit(solution)/shard_map/ppermute | solution.py:180
  109.0 19.0 %collective-permute-start.28 = (bf16[512,256]{1,0:T(8,128)(2,1)S(1)}, bf16[512,256]{1,0:T(8,128)(2,1)S(1)}, u32[]{:S(2)}, u32[]{:S(2)}) collective-permute-start(bf16[512,256]{1,0:T(8,128)(2,1)S(1)} %maximum_select_fusion.2), channel_id=1, source_target_pairs={{4,1},{1,4},{6,3},{3,6},{12,9},{9,12},{14,11},{11,14},{20,17},{17,... | collective-permute-start | bytes 786440 | tf_op jit(solution)/shard_map/ppermute | solution.py:180
  112.2 10.4 %collective-permute-start.27 = (bf16[512,256]{1,0:T(8,128)(2,1)S(1)}, bf16[512,256]{1,0:T(8,128)(2,1)S(1)}, u32[]{:S(2)}, u32[]{:S(2)}) collective-permute-start(bf16[512,256]{1,0:T(8,128)(2,1)S(1)} %maximum_select_fusion.2), channel_id=1, source_target_pairs={{0,1},{5,4},{4,0},{1,5},{2,3},{7,6},{6,2},{3,7},{8,9},{13,12},{12,... | collective-permute-start | bytes 786440 | tf_op jit(solution)/shard_map/ppermute | solution.py:179
  117.7 14.2 %collective-permute-start.19 = (bf16[1536,128]{1,0:T(8,128)(2,1)S(1)}, bf16[1536,128]{1,0:T(8,128)(2,1)S(1)}, u32[]{:S(2)}, u32[]{:S(2)}) collective-permute-start(bf16[1536,128]{1,0:T(8,128)(2,1)S(1)} %fusion.63), channel_id=1, source_target_pairs={{0,8},{24,16},{1,9},{25,17},{2,10},{26,18},{3,11},{27,19},{4,12},{... | collective-permute-start | bytes 1179656 | tf_op jit(solution)/shard_map/ppermute | solution.py:49
  121.3 13.8 %collective-permute-start.24 = (bf16[1536,128]{1,0:T(8,128)(2,1)S(1)}, bf16[1536,128]{1,0:T(8,128)(2,1)S(1)}, u32[]{:S(2)}, u32[]{:S(2)}) collective-permute-start(bf16[1536,128]{1,0:T(8,128)(2,1)S(1)} %fusion.64), channel_id=1, source_target_pairs={{0,8},{24,16},{1,9},{25,17},{2,10},{26,18},{3,11},{27,19},{4,12},{... | collective-permute-start | bytes 1179656 | tf_op jit(solution)/shard_map/ppermute | solution.py:49
  124.5 66.4 %collective-permute-start.36 = (bf16[512,512]{1,0:T(8,128)(2,1)S(1)}, bf16[512,512]{1,0:T(8,128)(2,1)S(1)}, u32[]{:S(2)}, u32[]{:S(2)}) collective-permute-start(bf16[512,512]{1,0:T(8,128)(2,1)S(1)} %maximum_select_fusion), channel_id=1, source_target_pairs={{4,1},{1,4},{6,3},{3,6},{12,9},{9,12},{14,11},{11,14},{20,17},{17,... | collective-permute-start | bytes 1572872 | tf_op jit(solution)/shard_map/ppermute | solution.py:180
  128.0 27.4 %collective-permute-start.35 = (bf16[512,512]{1,0:T(8,128)(2,1)S(1)}, bf16[512,512]{1,0:T(8,128)(2,1)S(1)}, u32[]{:S(2)}, u32[]{:S(2)}) collective-permute-start(bf16[512,512]{1,0:T(8,128)(2,1)S(1)} %maximum_select_fusion), channel_id=1, source_target_pairs={{0,1},{5,4},{4,0},{1,5},{2,3},{7,6},{6,2},{3,7},{8,9},{13,12},{12,... | collective-permute-start | bytes 1572872 | tf_op jit(solution)/shard_map/ppermute | solution.py:179
  137.0 11.7 %collective-permute-start.20 = (bf16[1536,128]{1,0:T(8,128)(2,1)S(1)}, bf16[1536,128]{1,0:T(8,128)(2,1)S(1)}, u32[]{:S(2)}, u32[]{:S(2)}) collective-permute-start(bf16[1536,128]{1,0:T(8,128)(2,1)S(1)} %add_convert_fusion.35), channel_id=1, source_target_pairs={{8,16},{16,8},{9,17},{17,9},{10,18},{18,10},{11,19},{19,11},{12,20... | collective-permute-start | bytes 1179656 | tf_op jit(solution)/shard_map/ppermute | solution.py:49
  139.0 21.7 %collective-permute-start.25 = (bf16[1536,128]{1,0:T(8,128)(2,1)S(1)}, bf16[1536,128]{1,0:T(8,128)(2,1)S(1)}, u32[]{:S(2)}, u32[]{:S(2)}) collective-permute-start(bf16[1536,128]{1,0:T(8,128)(2,1)S(1)} %add_convert_fusion.33), channel_id=1, source_target_pairs={{8,16},{16,8},{9,17},{17,9},{10,18},{18,10},{11,19},{19,11},{12,20... | collective-permute-start | bytes 1179656 | tf_op jit(solution)/shard_map/ppermute | solution.py:49
  139.8 24.2 %collective-permute-start.29 = (bf16[1536,128]{1,0:T(8,128)(2,1)S(1)}, bf16[1536,128]{1,0:T(8,128)(2,1)S(1)}, u32[]{:S(2)}, u32[]{:S(2)}) collective-permute-start(bf16[1536,128]{1,0:T(8,128)(2,1)S(1)} %get-tuple-element.138), channel_id=1, source_target_pairs={{0,8},{24,16},{1,9},{25,17},{2,10},{26,18},{3,11},{27,19},{4,12},{... | collective-permute-start | bytes 1179656 | tf_op jit(solution)/shard_map/ppermute | solution.py:49
  148.7 16.6 %collective-permute-start.32 = (bf16[1536,128]{1,0:T(8,128)(2,1)S(1)}, bf16[1536,128]{1,0:T(8,128)(2,1)S(1)}, u32[]{:S(2)}, u32[]{:S(2)}) collective-permute-start(bf16[1536,128]{1,0:T(8,128)(2,1)S(1)} %get-tuple-element.137), channel_id=1, source_target_pairs={{0,8},{24,16},{1,9},{25,17},{2,10},{26,18},{3,11},{27,19},{4,12},{... | collective-permute-start | bytes 1179656 | tf_op jit(solution)/shard_map/ppermute | solution.py:49
  157.3 33.6 %collective-permute-start.50 = (bf16[512,512]{1,0:T(8,128)(2,1)S(1)}, bf16[512,512]{1,0:T(8,128)(2,1)S(1)}, u32[]{:S(2)}, u32[]{:S(2)}) collective-permute-start(bf16[512,512]{1,0:T(8,128)(2,1)S(1)} %maximum_select_fusion.1), channel_id=1, source_target_pairs={{4,1},{1,4},{6,3},{3,6},{12,9},{9,12},{14,11},{11,14},{20,17},{17,... | collective-permute-start | bytes 1572872 | tf_op jit(solution)/shard_map/ppermute | solution.py:180
  160.7 30.3 %collective-permute-start.49 = (bf16[512,512]{1,0:T(8,128)(2,1)S(1)}, bf16[512,512]{1,0:T(8,128)(2,1)S(1)}, u32[]{:S(2)}, u32[]{:S(2)}) collective-permute-start(bf16[512,512]{1,0:T(8,128)(2,1)S(1)} %maximum_select_fusion.1), channel_id=1, source_target_pairs={{0,1},{5,4},{4,0},{1,5},{2,3},{7,6},{6,2},{3,7},{8,9},{13,12},{12,... | collective-permute-start | bytes 1572872 | tf_op jit(solution)/shard_map/ppermute | solution.py:179
  165.3 15.5 %collective-permute-start.26 = (bf16[1536,128]{1,0:T(8,128)(2,1)S(1)}, bf16[1536,128]{1,0:T(8,128)(2,1)S(1)}, u32[]{:S(2)}, u32[]{:S(2)}) collective-permute-start(bf16[1536,128]{1,0:T(8,128)(2,1)S(1)} %add_convert_fusion.32), channel_id=1, source_target_pairs={{8,0},{16,24},{9,1},{17,25},{10,2},{18,26},{11,3},{19,27},{12,4},{... | collective-permute-start | bytes 1179656 | tf_op jit(solution)/shard_map/ppermute | solution.py:49
  183.6 26.0 %collective-permute-start.31 = (bf16[1536,128]{1,0:T(8,128)(2,1)S(1)}, bf16[1536,128]{1,0:T(8,128)(2,1)S(1)}, u32[]{:S(2)}, u32[]{:S(2)}) collective-permute-start(bf16[1536,128]{1,0:T(8,128)(2,1)S(1)} %get-tuple-element.86), channel_id=1, source_target_pairs={{8,0},{16,24},{9,1},{17,25},{10,2},{18,26},{11,3},{19,27},{12,4},{... | collective-permute-start | bytes 1179656 | tf_op jit(solution)/shard_map/ppermute | solution.py:49
  185.4 26.0 %collective-permute-start.34 = (bf16[1536,128]{1,0:T(8,128)(2,1)S(1)}, bf16[1536,128]{1,0:T(8,128)(2,1)S(1)}, u32[]{:S(2)}, u32[]{:S(2)}) collective-permute-start(bf16[1536,128]{1,0:T(8,128)(2,1)S(1)} %get-tuple-element.82), channel_id=1, source_target_pairs={{8,0},{16,24},{9,1},{17,25},{10,2},{18,26},{11,3},{19,27},{12,4},{... | collective-permute-start | bytes 1179656 | tf_op jit(solution)/shard_map/ppermute | solution.py:49
  202.8 16.2 %collective-permute-start.40 = (bf16[1536,128]{1,0:T(8,128)(2,1)S(1)}, bf16[1536,128]{1,0:T(8,128)(2,1)S(1)}, u32[]{:S(2)}, u32[]{:S(2)}) collective-permute-start(bf16[1536,128]{1,0:T(8,128)(2,1)S(1)} %broadcast_select_fusion.23), channel_id=1, source_target_pairs={{0,8},{24,16},{1,9},{25,17},{2,10},{26,18},{3,11},{27,19},{4,12},{... | collective-permute-start | bytes 1179656 | tf_op jit(solution)/shard_map/ppermute | solution.py:49
  221.7 14.7 %collective-permute-start.37 = (bf16[1536,128]{1,0:T(8,128)(2,1)S(1)}, bf16[1536,128]{1,0:T(8,128)(2,1)S(1)}, u32[]{:S(2)}, u32[]{:S(2)}) collective-permute-start(bf16[1536,128]{1,0:T(8,128)(2,1)S(1)} %get-tuple-element.118), channel_id=1, source_target_pairs={{0,8},{24,16},{1,9},{25,17},{2,10},{26,18},{3,11},{27,19},{4,12},{... | collective-permute-start | bytes 1179656 | tf_op jit(solution)/shard_map/ppermute | solution.py:49
  228.3 16.6 %collective-permute-start.46 = (bf16[1536,128]{1,0:T(8,128)(2,1)S(1)}, bf16[1536,128]{1,0:T(8,128)(2,1)S(1)}, u32[]{:S(2)}, u32[]{:S(2)}) collective-permute-start(bf16[1536,128]{1,0:T(8,128)(2,1)S(1)} %get-tuple-element.117), channel_id=1, source_target_pairs={{0,8},{24,16},{1,9},{25,17},{2,10},{26,18},{3,11},{27,19},{4,12},{... | collective-permute-start | bytes 1179656 | tf_op jit(solution)/shard_map/ppermute | solution.py:49
  231.6 24.5 %collective-permute-start.42 = (bf16[1536,128]{1,0:T(8,128)(2,1)S(1)}, bf16[1536,128]{1,0:T(8,128)(2,1)S(1)}, u32[]{:S(2)}, u32[]{:S(2)}) collective-permute-start(bf16[1536,128]{1,0:T(8,128)(2,1)S(1)} %get-tuple-element.74), channel_id=1, source_target_pairs={{8,0},{16,24},{9,1},{17,25},{10,2},{18,26},{11,3},{19,27},{12,4},{... | collective-permute-start | bytes 1179656 | tf_op jit(solution)/shard_map/ppermute | solution.py:49
  248.9 13.8 %collective-permute-start.43 = (bf16[1536,128]{1,0:T(8,128)(2,1)S(1)}, bf16[1536,128]{1,0:T(8,128)(2,1)S(1)}, u32[]{:S(2)}, u32[]{:S(2)}) collective-permute-start(bf16[1536,128]{1,0:T(8,128)(2,1)S(1)} %broadcast_select_fusion.20), channel_id=1, source_target_pairs={{0,8},{24,16},{1,9},{25,17},{2,10},{26,18},{3,11},{27,19},{4,12},{... | collective-permute-start | bytes 1179656 | tf_op jit(solution)/shard_map/ppermute | solution.py:49
  253.3 15.4 %collective-permute-start.54 = (bf16[1536,128]{1,0:T(8,128)(2,1)S(1)}, bf16[1536,128]{1,0:T(8,128)(2,1)S(1)}, u32[]{:S(2)}, u32[]{:S(2)}) collective-permute-start(bf16[1536,128]{1,0:T(8,128)(2,1)S(1)} %broadcast_select_fusion.11), channel_id=1, source_target_pairs={{0,8},{24,16},{1,9},{25,17},{2,10},{26,18},{3,11},{27,19},{4,12},{... | collective-permute-start | bytes 1179656 | tf_op jit(solution)/shard_map/ppermute | solution.py:49
  255.4 11.3 %collective-permute-start.47 = (bf16[1536,128]{1,0:T(8,128)(2,1)S(1)}, bf16[1536,128]{1,0:T(8,128)(2,1)S(1)}, u32[]{:S(2)}, u32[]{:S(2)}) collective-permute-start(bf16[1536,128]{1,0:T(8,128)(2,1)S(1)} %get-tuple-element.68), channel_id=1, source_target_pairs={{8,16},{16,8},{9,17},{17,9},{10,18},{18,10},{11,19},{19,11},{12,20... | collective-permute-start | bytes 1179656 | tf_op jit(solution)/shard_map/ppermute | solution.py:49
  264.7 17.7 %collective-permute-start.39 = (bf16[1536,128]{1,0:T(8,128)(2,1)S(1)}, bf16[1536,128]{1,0:T(8,128)(2,1)S(1)}, u32[]{:S(2)}, u32[]{:S(2)}) collective-permute-start(bf16[1536,128]{1,0:T(8,128)(2,1)S(1)} %get-tuple-element.78), channel_id=1, source_target_pairs={{8,0},{16,24},{9,1},{17,25},{10,2},{18,26},{11,3},{19,27},{12,4},{... | collective-permute-start | bytes 1179656 | tf_op jit(solution)/shard_map/ppermute | solution.py:49
  266.0 18.3 %collective-permute-start.44 = (bf16[1536,128]{1,0:T(8,128)(2,1)S(1)}, bf16[1536,128]{1,0:T(8,128)(2,1)S(1)}, u32[]{:S(2)}, u32[]{:S(2)}) collective-permute-start(bf16[1536,128]{1,0:T(8,128)(2,1)S(1)} %get-tuple-element.72), channel_id=1, source_target_pairs={{8,16},{16,8},{9,17},{17,9},{10,18},{18,10},{11,19},{19,11},{12,20... | collective-permute-start | bytes 1179656 | tf_op jit(solution)/shard_map/ppermute | solution.py:49
  270.8 25.2 %collective-permute-start.60 = (bf16[1536,128]{1,0:T(8,128)(2,1)S(1)}, bf16[1536,128]{1,0:T(8,128)(2,1)S(1)}, u32[]{:S(2)}, u32[]{:S(2)}) collective-permute-start(bf16[1536,128]{1,0:T(8,128)(2,1)S(1)} %broadcast_select_fusion.5), channel_id=1, source_target_pairs={{0,8},{24,16},{1,9},{25,17},{2,10},{26,18},{3,11},{27,19},{4,12},{... | collective-permute-start | bytes 1179656 | tf_op jit(solution)/shard_map/ppermute | solution.py:49
  280.4 12.2 %collective-permute-start.55 = (bf16[1536,128]{1,0:T(8,128)(2,1)S(1)}, bf16[1536,128]{1,0:T(8,128)(2,1)S(1)}, u32[]{:S(2)}, u32[]{:S(2)}) collective-permute-start(bf16[1536,128]{1,0:T(8,128)(2,1)S(1)} %get-tuple-element.60), channel_id=1, source_target_pairs={{8,16},{16,8},{9,17},{17,9},{10,18},{18,10},{11,19},{19,11},{12,20... | collective-permute-start | bytes 1179656 | tf_op jit(solution)/shard_map/ppermute | solution.py:49
  286.3 16.2 %collective-permute-start.45 = (bf16[1536,128]{1,0:T(8,128)(2,1)S(1)}, bf16[1536,128]{1,0:T(8,128)(2,1)S(1)}, u32[]{:S(2)}, u32[]{:S(2)}) collective-permute-start(bf16[1536,128]{1,0:T(8,128)(2,1)S(1)} %get-tuple-element.70), channel_id=1, source_target_pairs={{8,0},{16,24},{9,1},{17,25},{10,2},{18,26},{11,3},{19,27},{12,4},{... | collective-permute-start | bytes 1179656 | tf_op jit(solution)/shard_map/ppermute | solution.py:49
  296.2 10.1 %collective-permute-start.51 = (bf16[1536,128]{1,0:T(8,128)(2,1)S(1)}, bf16[1536,128]{1,0:T(8,128)(2,1)S(1)}, u32[]{:S(2)}, u32[]{:S(2)}) collective-permute-start(bf16[1536,128]{1,0:T(8,128)(2,1)S(1)} %get-tuple-element.114), channel_id=1, source_target_pairs={{0,8},{24,16},{1,9},{25,17},{2,10},{26,18},{3,11},{27,19},{4,12},{... | collective-permute-start | bytes 1179656 | tf_op jit(solution)/shard_map/ppermute | solution.py:49
  308.5 12.2 %collective-permute-start.57 = (bf16[1536,128]{1,0:T(8,128)(2,1)S(1)}, bf16[1536,128]{1,0:T(8,128)(2,1)S(1)}, u32[]{:S(2)}, u32[]{:S(2)}) collective-permute-start(bf16[1536,128]{1,0:T(8,128)(2,1)S(1)} %broadcast_select_fusion.8), channel_id=1, source_target_pairs={{0,8},{24,16},{1,9},{25,17},{2,10},{26,18},{3,11},{27,19},{4,12},{... | collective-permute-start | bytes 1179656 | tf_op jit(solution)/shard_map/ppermute | solution.py:49
  314.6 9.9 %collective-permute-start.62 = (bf16[1536,128]{1,0:T(8,128)(2,1)S(1)}, bf16[1536,128]{1,0:T(8,128)(2,1)S(1)}, u32[]{:S(2)}, u32[]{:S(2)}) collective-permute-start(bf16[1536,128]{1,0:T(8,128)(2,1)S(1)} %get-tuple-element.112), channel_id=1, source_target_pairs={{8,0},{16,24},{9,1},{17,25},{10,2},{18,26},{11,3},{19,27},{12,4},{... | collective-permute-start | bytes 1179656 | tf_op jit(solution)/shard_map/ppermute | solution.py:49
  319.4 17.9 %collective-permute-start.53 = (bf16[1536,128]{1,0:T(8,128)(2,1)S(1)}, bf16[1536,128]{1,0:T(8,128)(2,1)S(1)}, u32[]{:S(2)}, u32[]{:S(2)}) collective-permute-start(bf16[1536,128]{1,0:T(8,128)(2,1)S(1)} %get-tuple-element.62), channel_id=1, source_target_pairs={{8,0},{16,24},{9,1},{17,25},{10,2},{18,26},{11,3},{19,27},{12,4},{... | collective-permute-start | bytes 1179656 | tf_op jit(solution)/shard_map/ppermute | solution.py:49
  324.9 14.2 %collective-permute-start.58 = (bf16[1536,128]{1,0:T(8,128)(2,1)S(1)}, bf16[1536,128]{1,0:T(8,128)(2,1)S(1)}, u32[]{:S(2)}, u32[]{:S(2)}) collective-permute-start(bf16[1536,128]{1,0:T(8,128)(2,1)S(1)} %get-tuple-element.111), channel_id=1, source_target_pairs={{8,16},{16,8},{9,17},{17,9},{10,18},{18,10},{11,19},{19,11},{12,20... | collective-permute-start | bytes 1179656 | tf_op jit(solution)/shard_map/ppermute | solution.py:49
  (26 other events, 341.8 us)

commit v3 on v2

v3 whole, which is shorter than its diff:
```python
import jax
import jax.numpy as jnp
from jax import lax
from jax.sharding import PartitionSpec as P

norm_eps = 1e-06
adam_eps = 1e-08
beta_one = 0.9
beta_two = 0.999
bias_one = 1.0 - 0.9**10
bias_two = 1.0 - 0.999**10
decay_rate = 0.1
outer_mu = 0.9

f32 = jnp.float32
bf16 = jnp.bfloat16


def outer_update(delta, momentum):
    new_momentum = outer_mu * momentum + delta
    outer_step = (delta + outer_mu * new_momentum).astype(bf16)
    return (new_momentum, outer_step)


def swap(value, axis, bit):
    count = lax.axis_size(axis)
    return lax.ppermute(value, axis, [(i, i ^ bit) for i in range(count)])


def together(*values):
    return lax.optimization_barrier(values)


class IslandLine:
    def __init__(self):
        self.count = lax.axis_size("island")
        self.hops = self.count - 1
        self.me = lax.axis_index("island")
        self.value, self.held, self.came, self.totals = {}, {}, {}, {}

    def pairs(self, hop):
        n, half = self.count, self.count // 2
        if hop < half - 1:
            ways = [(hop, hop + 1)]
        elif hop == half - 1:
            return [(half - 1, half), (half, half - 1)]
        else:
            ways = [(self.hops - hop, self.hops - 1 - hop)]
        return ways + [(n - 1 - i, n - 1 - j) for i, j in ways]

    def send(self, j, hop, payload):
        self.came[j] = lax.ppermute(payload, "island", self.pairs(hop))

    def enter(self, j, value, after):
        if after in self.held:
            value, self.held[after] = together(value, self.held[after])
        self.value[j] = value
        self.send(j, 0, value)

    def step(self, j, hop, after):
        half = self.count // 2
        came = self.came[j]
        if after in self.held:
            came, self.held[after] = together(came, self.held[after])
        if hop < half - 1:
            fresh = (came.astype(f32) + self.value[j].astype(f32)).astype(bf16)
        elif hop == half - 1:
            base = self.held[j] if hop else self.value[j]
            fresh = (came.astype(f32) + base.astype(f32)).astype(bf16)
        else:
            outer = self.hops - 1 - hop
            far = (self.me == outer) | (self.me == self.hops - outer)
            fresh = jnp.where(far, came, self.held[j])
        if hop + 1 < self.hops:
            self.held[j] = fresh
            self.send(j, hop + 1, fresh)
        else:
            del self.held[j]
            self.totals[j] = fresh


def body(context, residual, cotangent, gain, weight, first_moment, second_moment, momentum):
    tok_rows = context.shape[0]
    width = gain.shape[0]
    fsdp_count = lax.axis_size("fsdp")
    group = fsdp_count // 2
    cols = weight.shape[1]
    t = lax.axis_index("tp")
    f = lax.axis_index("fsdp")
    high = f // group
    low = f % group
    near = t == high

    pieces = 2
    rows = tok_rows // pieces

    def project(block):
        return lax.optimization_barrier(
            jnp.dot(block, weight, preferred_element_type=f32).astype(bf16)
        )

    near_blocks = [context] + [swap(context, "fsdp", r) for r in range(1, group)]
    slices = [
        [lax.dynamic_slice_in_dim(array, (low ^ r) * cols, cols, axis=1) for r in range(group)]
        for array in (residual, cotangent)
    ]
    held = together(context, *slices[0], *slices[1])
    later, slices = held[0], [held[1 : 1 + group], held[1 + group :]]
    moved = [[swap(parts[r], "fsdp", r) if r else parts[r] for r in range(group)] for parts in slices]
    far_pieces = [
        swap((later if p else context)[p * rows : (p + 1) * rows], "fsdp", group) for p in range(pieces)
    ]
    near_out = [project(context)]
    held = together(far_pieces[0], *near_blocks[1:], *moved[0], *moved[1])
    far_pieces[0] = held[0]
    near_blocks = [context] + list(held[1:group])
    residual_parts, cotangent_parts = held[group : 2 * group], held[2 * group :]
    far_pieces = [far_pieces] + [
        [swap(piece, "fsdp", r) for piece in far_pieces] for r in range(1, group)
    ]
    far_outs = []
    for r in range(group):
        far_outs += [swap(project(piece), "fsdp", group) for piece in far_pieces[r]]
    near_out += [project(block) for block in near_blocks[1:]]

    gain_part = lax.dynamic_slice_in_dim(gain, t * (width // 2) + low * cols, cols).astype(f32)

    keeps, arrivals = [], []
    for r in range(group):
        for p in range(pieces):
            far_out, own_out = far_outs[r * pieces + p], near_out[r]
            if keeps:
                far_out, own_out, keeps[-1] = together(far_out, own_out, keeps[-1])
            else:
                far_out, own_out = together(far_out, own_out)
            own_out = own_out[p * rows : (p + 1) * rows]
            keeps.append(jnp.where(near, own_out, far_out))
            arrivals.append(swap(jnp.where(near, far_out, own_out), "tp", 1))
    hidden, weighted, sums = [], [], []
    for k, (keep, came) in enumerate(zip(keeps, arrivals)):
        span = slice(k % pieces * rows, (k % pieces + 1) * rows)
        res, cot = residual_parts[k // pieces], cotangent_parts[k // pieces]
        if sums:
            came, sums[-1] = together(came, sums[-1])
        h = res[span].astype(f32) + keep.astype(f32) + came.astype(f32)
        w = gain_part[None, :] * cot[span].astype(f32)
        hidden.append(h)
        weighted.append(w)
        sums.append(jnp.stack([jnp.sum(h * h, axis=-1), jnp.sum(h * w, axis=-1)]))
    own_sums = jnp.concatenate(sums, axis=1)
    totals = own_sums
    for r in range(1, group):
        came = swap(own_sums, "fsdp", r)
        order = [r ^ k for k in range(group)]
        came = jnp.concatenate(
            [came[:, k * tok_rows : (k + 1) * tok_rows] for k in order], axis=1
        )
        totals = totals + came
    totals = totals + swap(totals, "tp", 1)
    inv_rms = lax.rsqrt(totals[0] / width + norm_eps)
    pull = inv_rms**3 * totals[1] / width

    tokens = near_blocks + [piece for block in far_pieces for piece in block]
    context_all = jnp.concatenate(tokens, axis=0)
    narrow = 128
    units = cols // narrow
    widths = [1, 3]
    while sum(widths) < units:
        widths.append(min(4, units - sum(widths)))
    def at(h, q, x):
        return (h * group + q) * 2 + x

    ring_pairs, cross_pairs = [], []
    for q in range(group):
        ring_pairs += [(at(x, q, x), at(x, q, 1 - x)) for x in (0, 1)]
        ring_pairs += [(at(1 - x, q, x), at(x, q, x)) for x in (0, 1)]
        cross_pairs += [(at(1 - x, q, x), at(x, q, 1 - x)) for x in (0, 1)]

    line = IslandLine()
    parts, rings = [], []

    def add_parts(c, after):
        cols_at = slice(sum(widths[:c]) * narrow, sum(widths[: c + 1]) * narrow)
        d_local = jnp.concatenate(
            [
                weighted[j][:, cols_at] * inv_rms[j * rows : (j + 1) * rows, None]
                - hidden[j][:, cols_at] * pull[j * rows : (j + 1) * rows, None]
                for j in range(group * pieces)
            ],
            axis=0,
        ).astype(bf16)
        if c < 3:
            if c == 2:
                d_local, rings[0] = together(d_local, rings[0])
            rings.append(lax.ppermute(d_local, ("fsdp", "tp"), ring_pairs))
            cross = lax.ppermute(d_local, ("fsdp", "tp"), cross_pairs)
            blocks = (d_local, cross)
        else:
            if after in line.held:
                d_local, line.held[after] = together(d_local, line.held[after])
            came = swap(d_local, "tp", 1)
            far = swap(jnp.where(near, came, d_local), "fsdp", group)
            rings.append(None)
            blocks = (jnp.where(near, d_local, came), far)
        return cols_at, blocks

    def add_pseudo(c, cols_at, blocks):
        if rings[c] is None:
            d_near, d_far = blocks
        else:
            d_near = jnp.where(near, blocks[0], rings[c])
            d_far = jnp.where(near, rings[c], blocks[1])
        d_all = jnp.concatenate([d_near, d_far], axis=0)
        grad = lax.dot_general(
            context_all, d_all, (((0,), (0,)), ((), ())), preferred_element_type=f32
        ) / (tok_rows * fsdp_count)
        first = first_moment[0, :, cols_at].astype(f32)
        second = second_moment[0, :, cols_at].astype(f32)
        m_new = beta_one * first + (1.0 - beta_one) * grad
        v_new = beta_two * second + (1.0 - beta_two) * grad * grad
        update = m_new / bias_one / (
            jnp.sqrt(v_new / bias_two) + adam_eps
        ) + decay_rate * weight[:, cols_at].astype(f32)
        pseudo = lax.optimization_barrier(update.astype(bf16))
        parts.extend(pseudo[:, u * narrow : (u + 1) * narrow] for u in range(widths[c]))

    first_three = [add_parts(c, None) for c in range(min(3, len(widths)))]
    for c, found in enumerate(first_three):
        add_pseudo(c, *found)
    next_chunk = len(first_three)
    for time in range(-2, units + line.hops - 1):
        for hop in range(line.hops):
            j = time - hop
            if 0 <= j < units:
                line.step(j, hop, j + 1 if hop else time - line.hops + 1)
        if next_chunk < len(widths) and time >= sum(widths[:next_chunk]) - 6:
            add_pseudo(next_chunk, *add_parts(next_chunk, time - line.hops + 2))
            next_chunk += 1
        if time + 2 < units:
            line.enter(time + 2, parts[time + 2], time - line.hops + 2)
    momentum_out, step_out = [], []
    for k in range(units):
        cols_at = slice(k * narrow, (k + 1) * narrow)
        total = lax.optimization_barrier(line.totals[k])
        delta = total.astype(f32) / lax.axis_size("island")
        new_momentum, outer_step = outer_update(delta, momentum[:, cols_at])
        momentum_out.append(new_momentum)
        step_out.append(outer_step)
    return (jnp.concatenate(momentum_out, axis=1), jnp.concatenate(step_out, axis=1))


def solution(mesh):
    in_specs = (
        P(("island", "fsdp"), "tp"),
        P(("island", "fsdp"), "tp"),
        P(("island", "fsdp"), "tp"),
        P(),
        P("tp", "fsdp"),
        P("island", "tp", "fsdp"),
        P("island", "tp", "fsdp"),
        P("tp", "fsdp"),
    )
    out_specs = (P("tp", "fsdp"), P("tp", "fsdp"))
    return jax.shard_map(body, mesh=mesh, in_specs=in_specs, out_specs=out_specs, check_vma=False)
```

time: 360 us -> 271 us (0.75)
  between operations: 52.8 us -> 2.18 us
  local copies, waits for them, and re-layouts: 34.5 us -> 15.8 us
  starting transfers between devices: 114 us -> 106 us
  matrix products: 32.3 us -> 27.1 us
  waiting for transfers between devices: 106 us -> 102 us
    slice x42 -> x7, local copies, waits for them, and re-layouts: 22.8 us -> 3.31 us  [the longest x2 2.55 us: body(): (later if p else context)[p * rows:(p + 1) * rows]]
    ppermute x46 -> x42, waiting for transfers between devices: 58.5 us -> 43 us  [the longest x36 40.3 us: send(): self.came[j] = lax.ppermute(payload, 'island', self.pairs(hop))]
    ppermute x17 -> x19, waiting for transfers between devices: 47.1 us -> 59 us  [swap(): return lax.ppermute(value, axis, [(i, i ^ bit) for i in range(count)])]
    dot_general x9 -> x4, matrix products: 26.1 us -> 15.1 us  [add_pseudo(): lax.dot_general(context_all, d_all, (((0,), (0,)), ((), ())), preferred_e...]
    ppermute x46 -> x42, starting transfers between devices: 102 us -> 92.2 us  [the longest x36 81.4 us: send(): self.came[j] = lax.ppermute(payload, 'island', self.pairs(hop))]
    select_n x45 -> x20, other arithmetic: 7.58 us -> 1.19 us  [the longest x12 0.52 us: step(): fresh = jnp.where(far, came, self.held[j])]
    dot_general x2 -> x6, matrix products: 6.25 us -> 12 us  [project(): jnp.dot(block, weight, preferred_element_type=f32).astype(bf16)]
    ppermute x17 -> x19, starting transfers between devices: 11.7 us -> 13.9 us  [swap(): return lax.ppermute(value, axis, [(i, i ^ bit) for i in range(count)])]
  transfers between devices with their start and end apart: 63 -> 61, of which waited for: 22 -> 21; matrix products, arithmetic and copies ran while one was open for 20% -> 18% of each run, Pallas kernels for 0% -> 0%
where the time goes in v3:
time: 271 us; the launch traced here: 267 us
  starting transfers between devices  106 us (39%)
  waiting for transfers between devices  102 us (38%)
  matrix products  27.1 us (10%)
  local copies, waits for them, and re-layouts  15.8 us (6%)
  other arithmetic  14.1 us (5%)
    ppermute x36, starting transfers between devices, send(): self.came[j] = lax.ppermute(payload, 'island', self.pairs(hop))  81.4 us
    ppermute x19, waiting for transfers between devices, swap(): return lax.ppermute(value, axis, [(i, i ^ bit) for i in range(count)])  59 us
    ppermute x36, waiting for transfers between devices, send(): self.came[j] = lax.ppermute(payload, 'island', self.pairs(hop))  40.3 us
    dot_general x4, matrix products, add_pseudo(): lax.dot_general(context_all, d_all, (((0,), (0,)), ((), ())), preferred_e...  15.1 us
    ppermute x19, starting transfers between devices, swap(): return lax.ppermute(value, axis, [(i, i ^ bit) for i in range(count)])  13.9 us
    dot_general x6, matrix products, project(): jnp.dot(block, weight, preferred_element_type=f32).astype(bf16)  12 us
    ppermute x3, starting transfers between devices, add_parts(): cross = lax.ppermute(d_local, ('fsdp', 'tp'), cross_pairs)  9.55 us
    unnamed x35, local copies, waits for them, and re-layouts  9.02 us
  transfers between devices with their start and end apart: 61, of which 21 were waited for; matrix products, arithmetic and copies ran while one was open for 18% of the time, Pallas kernels for 0%

profile of v3, /device:TPU:2, one launch (start us, length us, event | category | flops | bytes accessed | tf_op | source)
XLA Modules:
  0.0 267.3 jit_solution(4235173870376798813)
XLA Ops:
  0.7 1.8 slice.317
  2.5 1.5 collective-permute-start
  4.0 3.4 %constant_dynamic-slice_fusion = (bf16[256,1536]{1,0:T(8,128)(2,1)}, bf16[256,1536]{1,0:T(8,128)(2,1)S(1)}, bf16[256,1536]{1,0:T(8,128)(2,1)S(1)}, bf16[256,1536]{1,0:T(8,128)(2,1)}) fusion(bf16[256,3072]{1,0:T(8,128)(2,1)} %param.10, s32[]{:T(128)S(6)} %select_n.157, s32[]{:T(128)S(6)} %select_n.156, bf16[256,3072]{1,0:T(8,128)(2,1)} %param.9), kind=kLoop, calls=%fused_computation.271 | loop fusion | bytes 6291464 | tf_op jit(solution)/shard_map/dynamic_slice | solution.py:104
  9.2 2.3 convolution_convert_fusion.1
  13.2 9.5 %collective-permute-done.4 = bf16[128,1536]{1,0:T(8,128)(2,1)} collective-permute-done((bf16[128,1536]{1,0:T(8,128)(2,1)}, bf16[128,1536]{1,0:T(8,128)(2,1)}, u32[]{:S(2)}, u32[]{:S(2)}) %collective-permute-start.4) | collective-permute-done | bytes 393248 | tf_op jit(solution)/shard_map/ppermute | solution.py:27
  22.7 3.4 %convolution_convert_fusion.5 = bf16[128,1536]{1,0:T(8,128)(2,1)S(1)} fusion(bf16[128,1536]{1,0:T(8,128)(2,1)} %collective-permute-done.4, bf16[1536,1536]{1,0:T(8,128)(2,1)} %param.12), kind=kOutput, calls=%fused_computation.23 | convolution fusion | flops 604176384 | bytes 5505024 | tf_op jit(solution)/shard_map/dot_general | solution.py:99
  26.2 1.6 collective-permute-start.7
  27.8 4.0 %convolution_convert_fusion = bf16[256,1536]{1,0:T(8,128)(2,1)S(1)} fusion(bf16[256,1536]{1,0:T(8,128)(2,1)} %collective-permute-done.1, bf16[1536,1536]{1,0:T(8,128)(2,1)} %param.12), kind=kOutput, calls=%fused_computation.18 | convolution fusion | flops 1208352768 | bytes 6291456 | tf_op jit(solution)/shard_map/dot_general | solution.py:99
  35.7 1.5 collective-permute-start.8
  39.7 15.9 %collective-permute-done.8 = bf16[128,1536]{1,0:T(8,128)(2,1)S(1)} collective-permute-done((bf16[128,1536]{1,0:T(8,128)(2,1)S(1)}, bf16[128,1536]{1,0:T(8,128)(2,1)S(1)}, u32[]{:S(2)}, u32[]{:S(2)}) %collective-permute-start.8) | collective-permute-done | bytes 393248 | tf_op jit(solution)/shard_map/ppermute | solution.py:27
  56.3 1.5 collective-permute-start.10
  57.8 5.3 %collective-permute-done.11 = bf16[128,1536]{1,0:T(8,128)(2,1)S(1)} collective-permute-done((bf16[128,1536]{1,0:T(8,128)(2,1)S(1)}, bf16[128,1536]{1,0:T(8,128)(2,1)S(1)}, u32[]{:S(2)}, u32[]{:S(2)}) %collective-permute-start.11) | collective-permute-done | bytes 393248 | tf_op jit(solution)/shard_map/ppermute | solution.py:27
  63.8 1.5 collective-permute-start.12
  65.3 11.0 %collective-permute-done.10 = bf16[128,1536]{1,0:T(8,128)(2,1)S(1)} collective-permute-done((bf16[128,1536]{1,0:T(8,128)(2,1)S(1)}, bf16[128,1536]{1,0:T(8,128)(2,1)S(1)}, u32[]{:S(2)}, u32[]{:S(2)}) %collective-permute-start.10) | collective-permute-done | bytes 393248 | tf_op jit(solution)/shard_map/ppermute | solution.py:27
  77.1 13.2 %collective-permute-done.12 = bf16[128,1536]{1,0:T(8,128)(2,1)S(1)} collective-permute-done((bf16[128,1536]{1,0:T(8,128)(2,1)S(1)}, bf16[128,1536]{1,0:T(8,128)(2,1)S(1)}, u32[]{:S(2)}, u32[]{:S(2)}) %collective-permute-start.12) | collective-permute-done | bytes 393248 | tf_op jit(solution)/shard_map/ppermute | solution.py:27
  91.8 1.6 multiply_reduce_fusion.1
  95.3 3.0 %collective-permute-done.16 = f32[2,512]{1,0:T(2,128)S(1)} collective-permute-done((f32[2,512]{1,0:T(2,128)S(1)}, f32[2,512]{1,0:T(2,128)S(1)}, u32[]{:S(2)}, u32[]{:S(2)}) %collective-permute-start.16) | collective-permute-done | bytes 4128 | tf_op jit(solution)/shard_map/ppermute | solution.py:27
  100.5 2.8 %collective-permute-start.18 = (bf16[512,128]{1,0:T(8,128)(2,1)S(1)}, bf16[512,128]{1,0:T(8,128)(2,1)S(1)}, u32[]{:S(2)}, u32[]{:S(2)}) collective-permute-start(bf16[512,128]{1,0:T(8,128)(2,1)S(1)} %pad_maximum_fusion.3), channel_id=1, source_target_pairs={{4,1},{1,4},{6,3},{3,6},{12,9},{9,12},{14,11},{11,14},{20,17},{17,... | collective-permute-start | bytes 393224 | tf_op jit(solution)/shard_map/ppermute | solution.py:196
  103.9 3.9 %collective-permute-start.22 = (bf16[512,384]{1,0:T(8,128)(2,1)S(1)}, bf16[512,384]{1,0:T(8,128)(2,1)S(1)}, u32[]{:S(2)}, u32[]{:S(2)}) collective-permute-start(bf16[512,384]{1,0:T(8,128)(2,1)S(1)} %pad_maximum_fusion.2), channel_id=1, source_target_pairs={{4,1},{1,4},{6,3},{3,6},{12,9},{9,12},{14,11},{11,14},{20,17},{17,... | collective-permute-start | bytes 1179656 | tf_op jit(solution)/shard_map/ppermute | solution.py:196
  108.0 2.8 %collective-permute-start.31 = (bf16[512,512]{1,0:T(8,128)(2,1)S(1)}, bf16[512,512]{1,0:T(8,128)(2,1)S(1)}, u32[]{:S(2)}, u32[]{:S(2)}) collective-permute-start(bf16[512,512]{1,0:T(8,128)(2,1)S(1)} %pad_maximum_fusion), channel_id=1, source_target_pairs={{4,1},{1,4},{6,3},{3,6},{12,9},{9,12},{14,11},{11,14},{20,17},{17,... | collective-permute-start | bytes 1572872 | tf_op jit(solution)/shard_map/ppermute | solution.py:196
  112.4 3.7 %collective-permute-start.19 = (bf16[1536,128]{1,0:T(8,128)(2,1)S(1)}, bf16[1536,128]{1,0:T(8,128)(2,1)S(1)}, u32[]{:S(2)}, u32[]{:S(2)}) collective-permute-start(bf16[1536,128]{1,0:T(8,128)(2,1)S(1)} %fusion.57), channel_id=1, source_target_pairs={{0,8},{24,16},{1,9},{25,17},{2,10},{26,18},{3,11},{27,19},{4,12},{... | collective-permute-start | bytes 1179656 | tf_op jit(solution)/shard_map/ppermute | solution.py:52
  116.1 2.6 collective-permute-done.22
  118.9 3.5 %fusion.20 = bf16[1536,384]{1,0:T(8,128)(2,1)S(1)} fusion(bf16[1536,1536]{1,0:T(8,128)(2,1)S(1)} %bitcast.123, bf16[1,1536,1536]{2,1,0:T(8,128)(2,1)S(1)} %bitcast.139, bf16[1,1536,1536]{2,1,0:T(8,128)(2,1)S(1)} %bitcast.141, bf16[1024,1536]{1,0:T(8,128)(2,1)S(1)} %constant_dynamic-update-slice_fusion, bf16[512,384]{1,0:T(8,128)(2,1)S(1)} %get-tuple-element.280, ...), kind=kOutput, calls=%fused_computation.32 | convolution fusion | flops 1220149248 | bytes 8650752 | tf_op jit(solution)/shard_map/dot_general | solution.py:214
  122.6 3.5 %collective-permute-start.23 = (bf16[1536,128]{1,0:T(8,128)(2,1)S(1)}, bf16[1536,128]{1,0:T(8,128)(2,1)S(1)}, u32[]{:S(2)}, u32[]{:S(2)}) collective-permute-start(bf16[1536,128]{1,0:T(8,128)(2,1)S(1)} %get-tuple-element.264), channel_id=1, source_target_pairs={{0,8},{24,16},{1,9},{25,17},{2,10},{26,18},{3,11},{27,19},{4,12},{... | collective-permute-start | bytes 1179656 | tf_op jit(solution)/shard_map/ppermute | solution.py:52
  128.5 4.4 %fusion.12 = bf16[1536,512]{1,0:T(8,128)(2,1)S(1)} fusion(bf16[1536,1536]{1,0:T(8,128)(2,1)S(1)} %bitcast.123, bf16[1,1536,1536]{2,1,0:T(8,128)(2,1)S(1)} %bitcast.139, bf16[1,1536,1536]{2,1,0:T(8,128)(2,1)S(1)} %bitcast.141, bf16[1024,1536]{1,0:T(8,128)(2,1)S(1)} %constant_dynamic-update-slice_fusion, bf16[512,512]{1,0:T(8,128)(2,1)S(1)} %get-tuple-element.278, ...), kind=kOutput, calls=%fused_computation.16 | convolution fusion | flops 1626865664 | bytes 10485760 | tf_op jit(solution)/shard_map/dot_general | solution.py:214
  133.1 1.8 collective-permute-done.23
  137.2 2.0 collective-permute-done.26
  139.9 7.2 %collective-permute-start.29 = (bf16[1536,128]{1,0:T(8,128)(2,1)S(1)}, bf16[1536,128]{1,0:T(8,128)(2,1)S(1)}, u32[]{:S(2)}, u32[]{:S(2)}) collective-permute-start(bf16[1536,128]{1,0:T(8,128)(2,1)S(1)} %get-tuple-element.152), channel_id=1, source_target_pairs={{0,8},{24,16},{1,9},{25,17},{2,10},{26,18},{3,11},{27,19},{4,12},{... | collective-permute-start | bytes 1179656 | tf_op jit(solution)/shard_map/ppermute | solution.py:52
  149.9 2.5 collective-permute-done.29
  154.7 7.0 %collective-permute-start.34 = (bf16[1536,128]{1,0:T(8,128)(2,1)S(1)}, bf16[1536,128]{1,0:T(8,128)(2,1)S(1)}, u32[]{:S(2)}, u32[]{:S(2)}) collective-permute-start(bf16[1536,128]{1,0:T(8,128)(2,1)S(1)} %get-tuple-element.162), channel_id=1, source_target_pairs={{0,8},{24,16},{1,9},{25,17},{2,10},{26,18},{3,11},{27,19},{4,12},{... | collective-permute-start | bytes 1179656 | tf_op jit(solution)/shard_map/ppermute | solution.py:52
  163.8 3.8 %collective-permute-done.34 = bf16[1536,128]{1,0:T(8,128)(2,1)S(1)} collective-permute-done((bf16[1536,128]{1,0:T(8,128)(2,1)S(1)}, bf16[1536,128]{1,0:T(8,128)(2,1)S(1)}, u32[]{:S(2)}, u32[]{:S(2)}) %collective-permute-start.34) | collective-permute-done | bytes 393248 | tf_op jit(solution)/shard_map/ppermute | solution.py:52
  169.9 6.8 %collective-permute-start.40 = (bf16[1536,128]{1,0:T(8,128)(2,1)S(1)}, bf16[1536,128]{1,0:T(8,128)(2,1)S(1)}, u32[]{:S(2)}, u32[]{:S(2)}) collective-permute-start(bf16[1536,128]{1,0:T(8,128)(2,1)S(1)} %get-tuple-element.178), channel_id=1, source_target_pairs={{0,8},{24,16},{1,9},{25,17},{2,10},{26,18},{3,11},{27,19},{4,12},{... | collective-permute-start | bytes 1179656 | tf_op jit(solution)/shard_map/ppermute | solution.py:52
  177.2 1.5 collective-permute-start.45
  181.0 2.4 collective-permute-done.35
  184.3 5.3 %collective-permute-start.43 = (bf16[1536,128]{1,0:T(8,128)(2,1)S(1)}, bf16[1536,128]{1,0:T(8,128)(2,1)S(1)}, u32[]{:S(2)}, u32[]{:S(2)}) collective-permute-start(bf16[1536,128]{1,0:T(8,128)(2,1)S(1)} %get-tuple-element.186), channel_id=1, source_target_pairs={{0,8},{24,16},{1,9},{25,17},{2,10},{26,18},{3,11},{27,19},{4,12},{... | collective-permute-start | bytes 1179656 | tf_op jit(solution)/shard_map/ppermute | solution.py:52
  189.9 5.8 %fusion.13 = bf16[1536,512]{1,0:T(8,128)(2,1)S(1)} fusion(bf16[1536,1536]{1,0:T(8,128)(2,1)S(1)} %bitcast.123, bf16[1,1536,1536]{2,1,0:T(8,128)(2,1)} %param.14, bf16[1,1536,1536]{2,1,0:T(8,128)(2,1)} %param.13, bf16[1024,1536]{1,0:T(8,128)(2,1)S(1)} %constant_dynamic-update-slice_fusion, bf16[512,512]{1,0:T(8,128)(2,1)S(1)} %collective-permute-done.45, ...), kind=kOutput, calls=%fused_computation.17 | convolution fusion | flops 1626865664 | bytes 10485760 | tf_op jit(solution)/shard_map/dot_general | solution.py:214
  199.7 7.0 %collective-permute-start.48 = (bf16[1536,128]{1,0:T(8,128)(2,1)S(1)}, bf16[1536,128]{1,0:T(8,128)(2,1)S(1)}, u32[]{:S(2)}, u32[]{:S(2)}) collective-permute-start(bf16[1536,128]{1,0:T(8,128)(2,1)S(1)} %get-tuple-element.195), channel_id=1, source_target_pairs={{0,8},{24,16},{1,9},{25,17},{2,10},{26,18},{3,11},{27,19},{4,12},{... | collective-permute-start | bytes 1179656 | tf_op jit(solution)/shard_map/ppermute | solution.py:52
  207.2 1.5 collective-permute-start.51
  209.1 3.4 %collective-permute-done.48 = bf16[1536,128]{1,0:T(8,128)(2,1)S(1)} collective-permute-done((bf16[1536,128]{1,0:T(8,128)(2,1)S(1)}, bf16[1536,128]{1,0:T(8,128)(2,1)S(1)}, u32[]{:S(2)}, u32[]{:S(2)}) %collective-permute-start.48) | collective-permute-done | bytes 393248 | tf_op jit(solution)/shard_map/ppermute | solution.py:52
  214.8 6.8 %collective-permute-start.54 = (bf16[1536,128]{1,0:T(8,128)(2,1)S(1)}, bf16[1536,128]{1,0:T(8,128)(2,1)S(1)}, u32[]{:S(2)}, u32[]{:S(2)}) collective-permute-start(bf16[1536,128]{1,0:T(8,128)(2,1)S(1)} %get-tuple-element.211), channel_id=1, source_target_pairs={{0,8},{24,16},{1,9},{25,17},{2,10},{26,18},{3,11},{27,19},{4,12},{... | collective-permute-start | bytes 1179656 | tf_op jit(solution)/shard_map/ppermute | solution.py:52
  224.2 2.7 %collective-permute-done.49 = bf16[1536,128]{1,0:T(8,128)(2,1)S(1)} collective-permute-done((bf16[1536,128]{1,0:T(8,128)(2,1)S(1)}, bf16[1536,128]{1,0:T(8,128)(2,1)S(1)}, u32[]{:S(2)}, u32[]{:S(2)}) %collective-permute-start.49) | collective-permute-done | bytes 393248 | tf_op jit(solution)/shard_map/ppermute | solution.py:52
  227.8 6.3 %collective-permute-start.57 = (bf16[1536,128]{1,0:T(8,128)(2,1)S(1)}, bf16[1536,128]{1,0:T(8,128)(2,1)S(1)}, u32[]{:S(2)}, u32[]{:S(2)}) collective-permute-start(bf16[1536,128]{1,0:T(8,128)(2,1)S(1)} %get-tuple-element.219), channel_id=1, source_target_pairs={{0,8},{24,16},{1,9},{25,17},{2,10},{26,18},{3,11},{27,19},{4,12},{... | collective-permute-start | bytes 1179656 | tf_op jit(solution)/shard_map/ppermute | solution.py:52
  236.0 3.4 %collective-permute-done.57 = bf16[1536,128]{1,0:T(8,128)(2,1)S(1)} collective-permute-done((bf16[1536,128]{1,0:T(8,128)(2,1)S(1)}, bf16[1536,128]{1,0:T(8,128)(2,1)S(1)}, u32[]{:S(2)}, u32[]{:S(2)}) %collective-permute-start.57) | collective-permute-done | bytes 393248 | tf_op jit(solution)/shard_map/ppermute | solution.py:52
  242.0 6.5 %collective-permute-done.55 = bf16[1536,128]{1,0:T(8,128)(2,1)S(1)} collective-permute-done((bf16[1536,128]{1,0:T(8,128)(2,1)S(1)}, bf16[1536,128]{1,0:T(8,128)(2,1)S(1)}, u32[]{:S(2)}, u32[]{:S(2)}) %collective-permute-start.55) | collective-permute-done | bytes 393248 | tf_op jit(solution)/shard_map/ppermute | solution.py:52
  250.4 6.6 %collective-permute-done.58 = bf16[1536,128]{1,0:T(8,128)(2,1)S(1)} collective-permute-done((bf16[1536,128]{1,0:T(8,128)(2,1)S(1)}, bf16[1536,128]{1,0:T(8,128)(2,1)S(1)}, u32[]{:S(2)}, u32[]{:S(2)}) %collective-permute-start.58) | collective-permute-done | bytes 393248 | tf_op jit(solution)/shard_map/ppermute | solution.py:52
  257.4 3.8 %collective-permute-done.60 = bf16[1536,128]{1,0:T(8,128)(2,1)S(1)} collective-permute-done((bf16[1536,128]{1,0:T(8,128)(2,1)S(1)}, bf16[1536,128]{1,0:T(8,128)(2,1)S(1)}, u32[]{:S(2)}, u32[]{:S(2)}) %collective-permute-start.60) | collective-permute-done | bytes 393248 | tf_op jit(solution)/shard_map/ppermute | solution.py:52
  261.6 3.5 %copy-done.4 = f32[1536,1536]{1,0:T(8,128)} copy-done((f32[1536,1536]{1,0:T(8,128)}, f32[1536,1536]{1,0:T(8,128)S(1)}, u32[]{:S(2)}) %copy-start.4) | copy-done | bytes 9437208
  265.1 2.2 copy-done.5
  (230 shorter events, 56.2 us)
Async XLA Ops:
  0.6 27.1 %collective-permute-start.1 = (bf16[256,1536]{1,0:T(8,128)(2,1)}, bf16[256,1536]{1,0:T(8,128)(2,1)}, u32[]{:S(2)}, u32[]{:S(2)}) collective-permute-start(bf16[256,1536]{1,0:T(8,128)(2,1)} %param.8), channel_id=1, source_target_pairs={{0,2},{2,0},{4,6},{6,4},{1,3},{3,1},{5,7},{7,5},{8,10},{10,8},{12,... | collective-permute-start | bytes 2359304 | tf_op jit(solution)/shard_map/ppermute | solution.py:27
  2.5 25.3 %collective-permute-start = (bf16[128,1536]{1,0:T(8,128)(2,1)}, bf16[128,1536]{1,0:T(8,128)(2,1)S(1)}, u32[]{:S(2)}, u32[]{:S(2)}) collective-permute-start(bf16[128,1536]{1,0:T(8,128)(2,1)} %slice.317), channel_id=1, source_target_pairs={{0,4},{2,6},{4,0},{6,2},{1,5},{3,7},{5,1},{7,3},{8,12},{10,14},{12... | collective-permute-start | bytes 1179656 | tf_op jit(solution)/shard_map/ppermute | solution.py:27
  7.4 20.3 %collective-permute-start.2 = (bf16[256,1536]{1,0:T(8,128)(2,1)}, bf16[256,1536]{1,0:T(8,128)(2,1)}, u32[]{:S(2)}, u32[]{:S(2)}) collective-permute-start(bf16[256,1536]{1,0:T(8,128)(2,1)} %get-tuple-element.117), channel_id=1, source_target_pairs={{0,2},{2,0},{4,6},{6,4},{1,3},{3,1},{5,7},{7,5},{8,10},{10,8},{12,... | collective-permute-start | bytes 2359304 | tf_op jit(solution)/shard_map/ppermute | solution.py:27
  7.6 20.1 %collective-permute-start.3 = (bf16[256,1536]{1,0:T(8,128)(2,1)}, bf16[256,1536]{1,0:T(8,128)(2,1)S(1)}, u32[]{:S(2)}, u32[]{:S(2)}) collective-permute-start(bf16[256,1536]{1,0:T(8,128)(2,1)} %get-tuple-element.119), channel_id=1, source_target_pairs={{0,2},{2,0},{4,6},{6,4},{1,3},{3,1},{5,7},{7,5},{8,10},{10,8},{12,... | collective-permute-start | bytes 2359304 | tf_op jit(solution)/shard_map/ppermute | solution.py:27
  8.7 14.0 %collective-permute-start.4 = (bf16[128,1536]{1,0:T(8,128)(2,1)}, bf16[128,1536]{1,0:T(8,128)(2,1)}, u32[]{:S(2)}, u32[]{:S(2)}) collective-permute-start(bf16[128,1536]{1,0:T(8,128)(2,1)} %slice.318), channel_id=1, source_target_pairs={{0,4},{2,6},{4,0},{6,2},{1,5},{3,7},{5,1},{7,3},{8,12},{10,14},{12... | collective-permute-start | bytes 1179656 | tf_op jit(solution)/shard_map/ppermute | solution.py:27
  26.2 29.5 %collective-permute-start.7 = (bf16[128,1536]{1,0:T(8,128)(2,1)S(1)}, bf16[128,1536]{1,0:T(8,128)(2,1)S(1)}, u32[]{:S(2)}, u32[]{:S(2)}) collective-permute-start(bf16[128,1536]{1,0:T(8,128)(2,1)S(1)} %convolution_convert_fusion.5), channel_id=1, source_target_pairs={{0,4},{2,6},{4,0},{6,2},{1,5},{3,7},{5,1},{7,3},{8,12},{10,14},{12... | collective-permute-start | bytes 1179656 | tf_op jit(solution)/shard_map/ppermute | solution.py:27
  35.1 28.0 %collective-permute-start.13 = (bf16[128,1536]{1,0:T(8,128)(2,1)S(1)}, bf16[128,1536]{1,0:T(8,128)(2,1)S(1)}, u32[]{:S(2)}, u32[]{:S(2)}) collective-permute-start(bf16[128,1536]{1,0:T(8,128)(2,1)S(1)} %convolution_convert_fusion.2), channel_id=1, source_target_pairs={{0,4},{2,6},{4,0},{6,2},{1,5},{3,7},{5,1},{7,3},{8,12},{10,14},{12... | collective-permute-start | bytes 1179656 | tf_op jit(solution)/shard_map/ppermute | solution.py:27
  35.7 19.9 %collective-permute-start.8 = (bf16[128,1536]{1,0:T(8,128)(2,1)S(1)}, bf16[128,1536]{1,0:T(8,128)(2,1)S(1)}, u32[]{:S(2)}, u32[]{:S(2)}) collective-permute-start(bf16[128,1536]{1,0:T(8,128)(2,1)S(1)} %convolution_convert_fusion.4), channel_id=1, source_target_pairs={{0,4},{2,6},{4,0},{6,2},{1,5},{3,7},{5,1},{7,3},{8,12},{10,14},{12... | collective-permute-start | bytes 1179656 | tf_op jit(solution)/shard_map/ppermute | solution.py:27
  39.1 23.9 %collective-permute-start.11 = (bf16[128,1536]{1,0:T(8,128)(2,1)S(1)}, bf16[128,1536]{1,0:T(8,128)(2,1)S(1)}, u32[]{:S(2)}, u32[]{:S(2)}) collective-permute-start(bf16[128,1536]{1,0:T(8,128)(2,1)S(1)} %convolution_convert_fusion.3), channel_id=1, source_target_pairs={{0,4},{2,6},{4,0},{6,2},{1,5},{3,7},{5,1},{7,3},{8,12},{10,14},{12... | collective-permute-start | bytes 1179656 | tf_op jit(solution)/shard_map/ppermute | solution.py:27
  55.7 20.9 %collective-permute-start.9 = (bf16[128,1536]{1,0:T(8,128)(2,1)S(1)}, bf16[128,1536]{1,0:T(8,128)(2,1)S(1)}, u32[]{:S(2)}, u32[]{:S(2)}) collective-permute-start(bf16[128,1536]{1,0:T(8,128)(2,1)S(1)} %get-tuple-element.267), channel_id=1, source_target_pairs={{0,1},{1,0},{2,3},{3,2},{4,5},{5,4},{6,7},{7,6},{8,9},{9,8},{10,11... | collective-permute-start | bytes 1179656 | tf_op jit(solution)/shard_map/ppermute | solution.py:27
  56.3 19.9 %collective-permute-start.10 = (bf16[128,1536]{1,0:T(8,128)(2,1)S(1)}, bf16[128,1536]{1,0:T(8,128)(2,1)S(1)}, u32[]{:S(2)}, u32[]{:S(2)}) collective-permute-start(bf16[128,1536]{1,0:T(8,128)(2,1)S(1)} %get-tuple-element.265), channel_id=1, source_target_pairs={{0,1},{1,0},{2,3},{3,2},{4,5},{5,4},{6,7},{7,6},{8,9},{9,8},{10,11... | collective-permute-start | bytes 1179656 | tf_op jit(solution)/shard_map/ppermute | solution.py:27
  63.2 28.5 %collective-permute-start.14 = (bf16[128,1536]{1,0:T(8,128)(2,1)S(1)}, bf16[128,1536]{1,0:T(8,128)(2,1)S(1)}, u32[]{:S(2)}, u32[]{:S(2)}) collective-permute-start(bf16[128,1536]{1,0:T(8,128)(2,1)S(1)} %broadcast_select_fusion.6), channel_id=1, source_target_pairs={{0,1},{1,0},{2,3},{3,2},{4,5},{5,4},{6,7},{7,6},{8,9},{9,8},{10,11... | collective-permute-start | bytes 1179656 | tf_op jit(solution)/shard_map/ppermute | solution.py:27
  63.8 26.5 %collective-permute-start.12 = (bf16[128,1536]{1,0:T(8,128)(2,1)S(1)}, bf16[128,1536]{1,0:T(8,128)(2,1)S(1)}, u32[]{:S(2)}, u32[]{:S(2)}) collective-permute-start(bf16[128,1536]{1,0:T(8,128)(2,1)S(1)} %get-tuple-element.269), channel_id=1, source_target_pairs={{0,1},{1,0},{2,3},{3,2},{4,5},{5,4},{6,7},{7,6},{8,9},{9,8},{10,11... | collective-permute-start | bytes 1179656 | tf_op jit(solution)/shard_map/ppermute | solution.py:27
  103.8 12.3 %collective-permute-start.21 = (bf16[512,384]{1,0:T(8,128)(2,1)S(1)}, bf16[512,384]{1,0:T(8,128)(2,1)S(1)}, u32[]{:S(2)}, u32[]{:S(2)}) collective-permute-start(bf16[512,384]{1,0:T(8,128)(2,1)S(1)} %pad_maximum_fusion.2), channel_id=1, source_target_pairs={{0,1},{5,4},{4,0},{1,5},{2,3},{7,6},{6,2},{3,7},{8,9},{13,12},{12,... | collective-permute-start | bytes 1179656 | tf_op jit(solution)/shard_map/ppermute | solution.py:195
  103.9 14.8 %collective-permute-start.22 = (bf16[512,384]{1,0:T(8,128)(2,1)S(1)}, bf16[512,384]{1,0:T(8,128)(2,1)S(1)}, u32[]{:S(2)}, u32[]{:S(2)}) collective-permute-start(bf16[512,384]{1,0:T(8,128)(2,1)S(1)} %pad_maximum_fusion.2), channel_id=1, source_target_pairs={{4,1},{1,4},{6,3},{3,6},{12,9},{9,12},{14,11},{11,14},{20,17},{17,... | collective-permute-start | bytes 1179656 | tf_op jit(solution)/shard_map/ppermute | solution.py:196
  107.9 20.4 %collective-permute-start.30 = (bf16[512,512]{1,0:T(8,128)(2,1)S(1)}, bf16[512,512]{1,0:T(8,128)(2,1)S(1)}, u32[]{:S(2)}, u32[]{:S(2)}) collective-permute-start(bf16[512,512]{1,0:T(8,128)(2,1)S(1)} %pad_maximum_fusion), channel_id=1, source_target_pairs={{0,1},{5,4},{4,0},{1,5},{2,3},{7,6},{6,2},{3,7},{8,9},{13,12},{12,... | collective-permute-start | bytes 1572872 | tf_op jit(solution)/shard_map/ppermute | solution.py:195
  108.0 20.3 %collective-permute-start.31 = (bf16[512,512]{1,0:T(8,128)(2,1)S(1)}, bf16[512,512]{1,0:T(8,128)(2,1)S(1)}, u32[]{:S(2)}, u32[]{:S(2)}) collective-permute-start(bf16[512,512]{1,0:T(8,128)(2,1)S(1)} %pad_maximum_fusion), channel_id=1, source_target_pairs={{4,1},{1,4},{6,3},{3,6},{12,9},{9,12},{14,11},{11,14},{20,17},{17,... | collective-permute-start | bytes 1572872 | tf_op jit(solution)/shard_map/ppermute | solution.py:196
  112.4 15.1 %collective-permute-start.19 = (bf16[1536,128]{1,0:T(8,128)(2,1)S(1)}, bf16[1536,128]{1,0:T(8,128)(2,1)S(1)}, u32[]{:S(2)}, u32[]{:S(2)}) collective-permute-start(bf16[1536,128]{1,0:T(8,128)(2,1)S(1)} %fusion.57), channel_id=1, source_target_pairs={{0,8},{24,16},{1,9},{25,17},{2,10},{26,18},{3,11},{27,19},{4,12},{... | collective-permute-start | bytes 1179656 | tf_op jit(solution)/shard_map/ppermute | solution.py:52
  122.6 12.3 %collective-permute-start.23 = (bf16[1536,128]{1,0:T(8,128)(2,1)S(1)}, bf16[1536,128]{1,0:T(8,128)(2,1)S(1)}, u32[]{:S(2)}, u32[]{:S(2)}) collective-permute-start(bf16[1536,128]{1,0:T(8,128)(2,1)S(1)} %get-tuple-element.264), channel_id=1, source_target_pairs={{0,8},{24,16},{1,9},{25,17},{2,10},{26,18},{3,11},{27,19},{4,12},{... | collective-permute-start | bytes 1179656 | tf_op jit(solution)/shard_map/ppermute | solution.py:52
  126.1 13.0 %collective-permute-start.26 = (bf16[1536,128]{1,0:T(8,128)(2,1)S(1)}, bf16[1536,128]{1,0:T(8,128)(2,1)S(1)}, u32[]{:S(2)}, u32[]{:S(2)}) collective-permute-start(bf16[1536,128]{1,0:T(8,128)(2,1)S(1)} %get-tuple-element.263), channel_id=1, source_target_pairs={{0,8},{24,16},{1,9},{25,17},{2,10},{26,18},{3,11},{27,19},{4,12},{... | collective-permute-start | bytes 1179656 | tf_op jit(solution)/shard_map/ppermute | solution.py:52
  135.0 12.1 %collective-permute-start.25 = (bf16[1536,128]{1,0:T(8,128)(2,1)S(1)}, bf16[1536,128]{1,0:T(8,128)(2,1)S(1)}, u32[]{:S(2)}, u32[]{:S(2)}) collective-permute-start(bf16[1536,128]{1,0:T(8,128)(2,1)S(1)} %add_convert_fusion.34), channel_id=1, source_target_pairs={{8,16},{16,8},{9,17},{17,9},{10,18},{18,10},{11,19},{19,11},{12,20... | collective-permute-start | bytes 1179656 | tf_op jit(solution)/shard_map/ppermute | solution.py:52
  135.9 14.0 %collective-permute-start.24 = (bf16[1536,128]{1,0:T(8,128)(2,1)S(1)}, bf16[1536,128]{1,0:T(8,128)(2,1)S(1)}, u32[]{:S(2)}, u32[]{:S(2)}) collective-permute-start(bf16[1536,128]{1,0:T(8,128)(2,1)S(1)} %add_convert_fusion.33), channel_id=1, source_target_pairs={{8,0},{16,24},{9,1},{17,25},{10,2},{18,26},{11,3},{19,27},{12,4},{... | collective-permute-start | bytes 1179656 | tf_op jit(solution)/shard_map/ppermute | solution.py:52
  139.3 14.0 %collective-permute-start.28 = (bf16[1536,128]{1,0:T(8,128)(2,1)S(1)}, bf16[1536,128]{1,0:T(8,128)(2,1)S(1)}, u32[]{:S(2)}, u32[]{:S(2)}) collective-permute-start(bf16[1536,128]{1,0:T(8,128)(2,1)S(1)} %add_convert_fusion.32), channel_id=1, source_target_pairs={{8,16},{16,8},{9,17},{17,9},{10,18},{18,10},{11,19},{19,11},{12,20... | collective-permute-start | bytes 1179656 | tf_op jit(solution)/shard_map/ppermute | solution.py:52
  139.9 12.5 %collective-permute-start.29 = (bf16[1536,128]{1,0:T(8,128)(2,1)S(1)}, bf16[1536,128]{1,0:T(8,128)(2,1)S(1)}, u32[]{:S(2)}, u32[]{:S(2)}) collective-permute-start(bf16[1536,128]{1,0:T(8,128)(2,1)S(1)} %get-tuple-element.152), channel_id=1, source_target_pairs={{0,8},{24,16},{1,9},{25,17},{2,10},{26,18},{3,11},{27,19},{4,12},{... | collective-permute-start | bytes 1179656 | tf_op jit(solution)/shard_map/ppermute | solution.py:52
  147.3 14.8 %collective-permute-start.27 = (bf16[1536,128]{1,0:T(8,128)(2,1)S(1)}, bf16[1536,128]{1,0:T(8,128)(2,1)S(1)}, u32[]{:S(2)}, u32[]{:S(2)}) collective-permute-start(bf16[1536,128]{1,0:T(8,128)(2,1)S(1)} %add_convert_fusion.31), channel_id=1, source_target_pairs={{8,0},{16,24},{9,1},{17,25},{10,2},{18,26},{11,3},{19,27},{12,4},{... | collective-permute-start | bytes 1179656 | tf_op jit(solution)/shard_map/ppermute | solution.py:52
  152.5 15.9 %collective-permute-start.33 = (bf16[1536,128]{1,0:T(8,128)(2,1)S(1)}, bf16[1536,128]{1,0:T(8,128)(2,1)S(1)}, u32[]{:S(2)}, u32[]{:S(2)}) collective-permute-start(bf16[1536,128]{1,0:T(8,128)(2,1)S(1)} %add_convert_fusion.30), channel_id=1, source_target_pairs={{8,16},{16,8},{9,17},{17,9},{10,18},{18,10},{11,19},{19,11},{12,20... | collective-permute-start | bytes 1179656 | tf_op jit(solution)/shard_map/ppermute | solution.py:52
  153.4 16.5 %collective-permute-start.32 = (bf16[1536,128]{1,0:T(8,128)(2,1)S(1)}, bf16[1536,128]{1,0:T(8,128)(2,1)S(1)}, u32[]{:S(2)}, u32[]{:S(2)}) collective-permute-start(bf16[1536,128]{1,0:T(8,128)(2,1)S(1)} %add_convert_fusion.29), channel_id=1, source_target_pairs={{8,0},{16,24},{9,1},{17,25},{10,2},{18,26},{11,3},{19,27},{12,4},{... | collective-permute-start | bytes 1179656 | tf_op jit(solution)/shard_map/ppermute | solution.py:52
  154.7 13.0 %collective-permute-start.34 = (bf16[1536,128]{1,0:T(8,128)(2,1)S(1)}, bf16[1536,128]{1,0:T(8,128)(2,1)S(1)}, u32[]{:S(2)}, u32[]{:S(2)}) collective-permute-start(bf16[1536,128]{1,0:T(8,128)(2,1)S(1)} %get-tuple-element.162), channel_id=1, source_target_pairs={{0,8},{24,16},{1,9},{25,17},{2,10},{26,18},{3,11},{27,19},{4,12},{... | collective-permute-start | bytes 1179656 | tf_op jit(solution)/shard_map/ppermute | solution.py:52
  161.6 15.5 %collective-permute-start.44 = (bf16[512,512]{1,0:T(8,128)(2,1)S(1)}, bf16[512,512]{1,0:T(8,128)(2,1)S(1)}, u32[]{:S(2)}, u32[]{:S(2)}) collective-permute-start(bf16[512,512]{1,0:T(8,128)(2,1)S(1)} %pad_maximum_fusion.1), channel_id=1, source_target_pairs={{0,1},{1,0},{2,3},{3,2},{4,5},{5,4},{6,7},{7,6},{8,9},{9,8},{10,11... | collective-permute-start | bytes 1572872 | tf_op jit(solution)/shard_map/ppermute | solution.py:27
  162.1 16.7 %collective-permute-start.37 = (bf16[1536,128]{1,0:T(8,128)(2,1)S(1)}, bf16[1536,128]{1,0:T(8,128)(2,1)S(1)}, u32[]{:S(2)}, u32[]{:S(2)}) collective-permute-start(bf16[1536,128]{1,0:T(8,128)(2,1)S(1)} %get-tuple-element.170), channel_id=1, source_target_pairs={{0,8},{24,16},{1,9},{25,17},{2,10},{26,18},{3,11},{27,19},{4,12},{... | collective-permute-start | bytes 1179656 | tf_op jit(solution)/shard_map/ppermute | solution.py:52
  168.6 14.8 %collective-permute-start.35 = (bf16[1536,128]{1,0:T(8,128)(2,1)S(1)}, bf16[1536,128]{1,0:T(8,128)(2,1)S(1)}, u32[]{:S(2)}, u32[]{:S(2)}) collective-permute-start(bf16[1536,128]{1,0:T(8,128)(2,1)S(1)} %add_convert_fusion.27), channel_id=1, source_target_pairs={{8,0},{16,24},{9,1},{17,25},{10,2},{18,26},{11,3},{19,27},{12,4},{... | collective-permute-start | bytes 1179656 | tf_op jit(solution)/shard_map/ppermute | solution.py:52
  169.9 13.5 %collective-permute-start.40 = (bf16[1536,128]{1,0:T(8,128)(2,1)S(1)}, bf16[1536,128]{1,0:T(8,128)(2,1)S(1)}, u32[]{:S(2)}, u32[]{:S(2)}) collective-permute-start(bf16[1536,128]{1,0:T(8,128)(2,1)S(1)} %get-tuple-element.178), channel_id=1, source_target_pairs={{0,8},{24,16},{1,9},{25,17},{2,10},{26,18},{3,11},{27,19},{4,12},{... | collective-permute-start | bytes 1179656 | tf_op jit(solution)/shard_map/ppermute | solution.py:52
  177.2 12.7 %collective-permute-start.45 = (bf16[512,512]{1,0:T(8,128)(2,1)S(1)}, bf16[512,512]{1,0:T(8,128)(2,1)S(1)}, u32[]{:S(2)}, u32[]{:S(2)}) collective-permute-start(bf16[512,512]{1,0:T(8,128)(2,1)S(1)} %get-tuple-element.272), channel_id=1, source_target_pairs={{0,4},{2,6},{4,0},{6,2},{1,5},{3,7},{5,1},{7,3},{8,12},{10,14},{12... | collective-permute-start | bytes 1572872 | tf_op jit(solution)/shard_map/ppermute | solution.py:27
  178.9 17.1 %collective-permute-start.39 = (bf16[1536,128]{1,0:T(8,128)(2,1)S(1)}, bf16[1536,128]{1,0:T(8,128)(2,1)S(1)}, u32[]{:S(2)}, u32[]{:S(2)}) collective-permute-start(bf16[1536,128]{1,0:T(8,128)(2,1)S(1)} %add_convert_fusion.26), channel_id=1, source_target_pairs={{8,16},{16,8},{9,17},{17,9},{10,18},{18,10},{11,19},{19,11},{12,20... | collective-permute-start | bytes 1179656 | tf_op jit(solution)/shard_map/ppermute | solution.py:52
  179.7 17.7 %collective-permute-start.38 = (bf16[1536,128]{1,0:T(8,128)(2,1)S(1)}, bf16[1536,128]{1,0:T(8,128)(2,1)S(1)}, u32[]{:S(2)}, u32[]{:S(2)}) collective-permute-start(bf16[1536,128]{1,0:T(8,128)(2,1)S(1)} %add_convert_fusion.25), channel_id=1, source_target_pairs={{8,0},{16,24},{9,1},{17,25},{10,2},{18,26},{11,3},{19,27},{12,4},{... | collective-permute-start | bytes 1179656 | tf_op jit(solution)/shard_map/ppermute | solution.py:52
  183.6 14.7 %collective-permute-start.42 = (bf16[1536,128]{1,0:T(8,128)(2,1)S(1)}, bf16[1536,128]{1,0:T(8,128)(2,1)S(1)}, u32[]{:S(2)}, u32[]{:S(2)}) collective-permute-start(bf16[1536,128]{1,0:T(8,128)(2,1)S(1)} %add_convert_fusion.24), channel_id=1, source_target_pairs={{8,16},{16,8},{9,17},{17,9},{10,18},{18,10},{11,19},{19,11},{12,20... | collective-permute-start | bytes 1179656 | tf_op jit(solution)/shard_map/ppermute | solution.py:52
  184.3 13.2 %collective-permute-start.43 = (bf16[1536,128]{1,0:T(8,128)(2,1)S(1)}, bf16[1536,128]{1,0:T(8,128)(2,1)S(1)}, u32[]{:S(2)}, u32[]{:S(2)}) collective-permute-start(bf16[1536,128]{1,0:T(8,128)(2,1)S(1)} %get-tuple-element.186), channel_id=1, source_target_pairs={{0,8},{24,16},{1,9},{25,17},{2,10},{26,18},{3,11},{27,19},{4,12},{... | collective-permute-start | bytes 1179656 | tf_op jit(solution)/shard_map/ppermute | solution.py:52
  197.6 15.7 %collective-permute-start.47 = (bf16[1536,128]{1,0:T(8,128)(2,1)S(1)}, bf16[1536,128]{1,0:T(8,128)(2,1)S(1)}, u32[]{:S(2)}, u32[]{:S(2)}) collective-permute-start(bf16[1536,128]{1,0:T(8,128)(2,1)S(1)} %add_convert_fusion.22), channel_id=1, source_target_pairs={{8,16},{16,8},{9,17},{17,9},{10,18},{18,10},{11,19},{19,11},{12,20... | collective-permute-start | bytes 1179656 | tf_op jit(solution)/shard_map/ppermute | solution.py:52
  198.4 16.3 %collective-permute-start.46 = (bf16[1536,128]{1,0:T(8,128)(2,1)S(1)}, bf16[1536,128]{1,0:T(8,128)(2,1)S(1)}, u32[]{:S(2)}, u32[]{:S(2)}) collective-permute-start(bf16[1536,128]{1,0:T(8,128)(2,1)S(1)} %add_convert_fusion.21), channel_id=1, source_target_pairs={{8,0},{16,24},{9,1},{17,25},{10,2},{18,26},{11,3},{19,27},{12,4},{... | collective-permute-start | bytes 1179656 | tf_op jit(solution)/shard_map/ppermute | solution.py:52
  199.7 12.8 %collective-permute-start.48 = (bf16[1536,128]{1,0:T(8,128)(2,1)S(1)}, bf16[1536,128]{1,0:T(8,128)(2,1)S(1)}, u32[]{:S(2)}, u32[]{:S(2)}) collective-permute-start(bf16[1536,128]{1,0:T(8,128)(2,1)S(1)} %get-tuple-element.195), channel_id=1, source_target_pairs={{0,8},{24,16},{1,9},{25,17},{2,10},{26,18},{3,11},{27,19},{4,12},{... | collective-permute-start | bytes 1179656 | tf_op jit(solution)/shard_map/ppermute | solution.py:52
  207.2 14.8 %collective-permute-start.51 = (bf16[1536,128]{1,0:T(8,128)(2,1)S(1)}, bf16[1536,128]{1,0:T(8,128)(2,1)S(1)}, u32[]{:S(2)}, u32[]{:S(2)}) collective-permute-start(bf16[1536,128]{1,0:T(8,128)(2,1)S(1)} %get-tuple-element.203), channel_id=1, source_target_pairs={{0,8},{24,16},{1,9},{25,17},{2,10},{26,18},{3,11},{27,19},{4,12},{... | collective-permute-start | bytes 1179656 | tf_op jit(solution)/shard_map/ppermute | solution.py:52
  213.4 13.5 %collective-permute-start.49 = (bf16[1536,128]{1,0:T(8,128)(2,1)S(1)}, bf16[1536,128]{1,0:T(8,128)(2,1)S(1)}, u32[]{:S(2)}, u32[]{:S(2)}) collective-permute-start(bf16[1536,128]{1,0:T(8,128)(2,1)S(1)} %add_convert_fusion.19), channel_id=1, source_target_pairs={{8,0},{16,24},{9,1},{17,25},{10,2},{18,26},{11,3},{19,27},{12,4},{... | collective-permute-start | bytes 1179656 | tf_op jit(solution)/shard_map/ppermute | solution.py:52
  214.8 12.2 %collective-permute-start.54 = (bf16[1536,128]{1,0:T(8,128)(2,1)S(1)}, bf16[1536,128]{1,0:T(8,128)(2,1)S(1)}, u32[]{:S(2)}, u32[]{:S(2)}) collective-permute-start(bf16[1536,128]{1,0:T(8,128)(2,1)S(1)} %get-tuple-element.211), channel_id=1, source_target_pairs={{0,8},{24,16},{1,9},{25,17},{2,10},{26,18},{3,11},{27,19},{4,12},{... | collective-permute-start | bytes 1179656 | tf_op jit(solution)/shard_map/ppermute | solution.py:52
  222.1 12.4 %collective-permute-start.53 = (bf16[1536,128]{1,0:T(8,128)(2,1)S(1)}, bf16[1536,128]{1,0:T(8,128)(2,1)S(1)}, u32[]{:S(2)}, u32[]{:S(2)}) collective-permute-start(bf16[1536,128]{1,0:T(8,128)(2,1)S(1)} %add_convert_fusion.18), channel_id=1, source_target_pairs={{8,16},{16,8},{9,17},{17,9},{10,18},{18,10},{11,19},{19,11},{12,20... | collective-permute-start | bytes 1179656 | tf_op jit(solution)/shard_map/ppermute | solution.py:52
  222.9 13.0 %collective-permute-start.52 = (bf16[1536,128]{1,0:T(8,128)(2,1)S(1)}, bf16[1536,128]{1,0:T(8,128)(2,1)S(1)}, u32[]{:S(2)}, u32[]{:S(2)}) collective-permute-start(bf16[1536,128]{1,0:T(8,128)(2,1)S(1)} %add_convert_fusion.17), channel_id=1, source_target_pairs={{8,0},{16,24},{9,1},{17,25},{10,2},{18,26},{11,3},{19,27},{12,4},{... | collective-permute-start | bytes 1179656 | tf_op jit(solution)/shard_map/ppermute | solution.py:52
  227.1 13.1 %collective-permute-start.56 = (bf16[1536,128]{1,0:T(8,128)(2,1)S(1)}, bf16[1536,128]{1,0:T(8,128)(2,1)S(1)}, u32[]{:S(2)}, u32[]{:S(2)}) collective-permute-start(bf16[1536,128]{1,0:T(8,128)(2,1)S(1)} %add_convert_fusion.16), channel_id=1, source_target_pairs={{8,16},{16,8},{9,17},{17,9},{10,18},{18,10},{11,19},{19,11},{12,20... | collective-permute-start | bytes 1179656 | tf_op jit(solution)/shard_map/ppermute | solution.py:52
  234.7 13.9 %collective-permute-start.55 = (bf16[1536,128]{1,0:T(8,128)(2,1)S(1)}, bf16[1536,128]{1,0:T(8,128)(2,1)S(1)}, u32[]{:S(2)}, u32[]{:S(2)}) collective-permute-start(bf16[1536,128]{1,0:T(8,128)(2,1)S(1)} %add_convert_fusion.15), channel_id=1, source_target_pairs={{8,0},{16,24},{9,1},{17,25},{10,2},{18,26},{11,3},{19,27},{12,4},{... | collective-permute-start | bytes 1179656 | tf_op jit(solution)/shard_map/ppermute | solution.py:52
  240.3 16.6 %collective-permute-start.58 = (bf16[1536,128]{1,0:T(8,128)(2,1)S(1)}, bf16[1536,128]{1,0:T(8,128)(2,1)S(1)}, u32[]{:S(2)}, u32[]{:S(2)}) collective-permute-start(bf16[1536,128]{1,0:T(8,128)(2,1)S(1)} %add_convert_fusion.13), channel_id=1, source_target_pairs={{8,0},{16,24},{9,1},{17,25},{10,2},{18,26},{11,3},{19,27},{12,4},{... | collective-permute-start | bytes 1179656 | tf_op jit(solution)/shard_map/ppermute | solution.py:52
  (28 other events, 329.9 us)

commit v4 on v3

--- a/solution.py
+++ b/solution.py
@@ -32,51 +32,41 @@
 
 
 class IslandLine:
-    def __init__(self):
-        self.count = lax.axis_size("island")
-        self.hops = self.count - 1
-        self.me = lax.axis_index("island")
-        self.value, self.held, self.came, self.totals = {}, {}, {}, {}
-
-    def pairs(self, hop):
-        n, half = self.count, self.count // 2
-        if hop < half - 1:
-            ways = [(hop, hop + 1)]
-        elif hop == half - 1:
-            return [(half - 1, half), (half, half - 1)]
+    def __init__(self, chunks):
+        self.chunks = chunks
+        me = lax.axis_index("island")
+        self.outer = (me == 0) | (me == 3)
+        self.part, self.paid, self.edge, self.mid, self.sums, self.totals = {}, {}, {}, {}, {}, {}
+
+    def send_outer(self, s):
+        if s >= self.chunks + 3:
+            return
+        pairs = [(0, 1), (3, 2)] if s < self.chunks else []
+        if s >= 3:
+            pairs = pairs + [(1, 0), (2, 3)]
+            total = (self.sums[s - 3].astype(f32) + self.mid[s - 3].astype(f32)).astype(bf16)
+            payload = jnp.where(self.outer, self.part[s], total) if s < self.chunks else total
         else:
-            ways = [(self.hops - hop, self.hops - 1 - hop)]
-        return ways + [(n - 1 - i, n - 1 - j) for i, j in ways]
-
-    def send(self, j, hop, payload):
-        self.came[j] = lax.ppermute(payload, "island", self.pairs(hop))
-
-    def enter(self, j, value, after):
-        if after in self.held:
-            value, self.held[after] = together(value, self.held[after])
-        self.value[j] = value
-        self.send(j, 0, value)
-
-    def step(self, j, hop, after):
-        half = self.count // 2
-        came = self.came[j]
-        if after in self.held:
-            came, self.held[after] = together(came, self.held[after])
-        if hop < half - 1:
-            fresh = (came.astype(f32) + self.value[j].astype(f32)).astype(bf16)
-        elif hop == half - 1:
-            base = self.held[j] if hop else self.value[j]
-            fresh = (came.astype(f32) + base.astype(f32)).astype(bf16)
-        else:
-            outer = self.hops - 1 - hop
-            far = (self.me == outer) | (self.me == self.hops - outer)
-            fresh = jnp.where(far, came, self.held[j])
-        if hop + 1 < self.hops:
-            self.held[j] = fresh
-            self.send(j, hop + 1, fresh)
-        else:
-            del self.held[j]
-            self.totals[j] = fresh
+            payload = self.part[s]
+        self.paid[s] = payload
+        self.edge[s] = lax.ppermute(payload, "island", pairs)
+
+    def step(self, s):
+        edge = self.edge[s]
+        if s + 1 in self.paid:
+            edge, self.paid[s + 1] = together(edge, self.paid[s + 1])
+        if s < self.chunks:
+            self.sums[s] = (edge.astype(f32) + self.part[s].astype(f32)).astype(bf16)
+            self.mid[s] = lax.ppermute(self.sums[s], "island", [(1, 2), (2, 1)])
+            if s >= 1:
+                self.mid[s - 1], self.sums[s] = together(self.mid[s - 1], self.sums[s])
+        self.send_outer(s + 2)
+        if s >= 3:
+            if s + 2 in self.paid:
+                edge, self.paid[s], self.paid[s + 2] = together(edge, self.paid[s], self.paid[s + 2])
+            else:
+                edge, self.paid[s] = together(edge, self.paid[s])
+            self.totals[s - 3] = jnp.where(self.outer, edge, self.paid[s])
 
 
 def body(context, residual, cotangent, gain, weight, first_moment, second_moment, momentum):
@@ -110,7 +100,6 @@
     far_pieces = [
         swap((later if p else context)[p * rows : (p + 1) * rows], "fsdp", group) for p in range(pieces)
     ]
-    near_out = [project(context)]
     held = together(far_pieces[0], *near_blocks[1:], *moved[0], *moved[1])
     far_pieces[0] = held[0]
     near_blocks = [context] + list(held[1:group])
@@ -118,22 +107,31 @@
     far_pieces = [far_pieces] + [
         [swap(piece, "fsdp", r) for piece in far_pieces] for r in range(1, group)
     ]
-    far_outs = []
+    far_outs, near_out = [], [[None] * pieces for r in range(group)]
+    last = None
     for r in range(group):
-        far_outs += [swap(project(piece), "fsdp", group) for piece in far_pieces[r]]
-    near_out += [project(block) for block in near_blocks[1:]]
+        for p in range(pieces):
+            beside = (r + 1) % group
+            far = far_pieces[r][p]
+            if last:
+                far, near_out[last[0]][last[1]] = together(far, near_out[last[0]][last[1]])
+            both = project(
+                jnp.concatenate([far, near_blocks[beside][p * rows : (p + 1) * rows]], axis=0)
+            )
+            far_outs.append(swap(both[:rows], "fsdp", group))
+            near_out[beside][p] = both[rows:]
+            last = (beside, p)
 
     gain_part = lax.dynamic_slice_in_dim(gain, t * (width // 2) + low * cols, cols).astype(f32)
 
     keeps, arrivals = [], []
     for r in range(group):
         for p in range(pieces):
-            far_out, own_out = far_outs[r * pieces + p], near_out[r]
+            far_out, own_out = far_outs[r * pieces + p], near_out[r][p]
             if keeps:
                 far_out, own_out, keeps[-1] = together(far_out, own_out, keeps[-1])
             else:
                 far_out, own_out = together(far_out, own_out)
-            own_out = own_out[p * rows : (p + 1) * rows]
             keeps.append(jnp.where(near, own_out, far_out))
             arrivals.append(swap(jnp.where(near, far_out, own_out), "tp", 1))
     hidden, weighted, sums = [], [], []
@@ -164,9 +162,9 @@
     context_all = jnp.concatenate(tokens, axis=0)
     narrow = 128
     units = cols // narrow
-    widths = [1, 3]
+    widths = [1, 2]
     while sum(widths) < units:
-        widths.append(min(4, units - sum(widths)))
+        widths.append(min(2 + len(widths), units - sum(widths)))
     def at(h, q, x):
         return (h * group + q) * 2 + x
 
@@ -176,8 +174,9 @@
         ring_pairs += [(at(1 - x, q, x), at(x, q, x)) for x in (0, 1)]
         cross_pairs += [(at(1 - x, q, x), at(x, q, 1 - x)) for x in (0, 1)]
 
-    line = IslandLine()
-    parts, rings = [], []
+    islands = lax.axis_size("island")
+    line = IslandLine(units)
+    parts, rings, pseudos = [], [], []
 
     def add_parts(c, after):
         cols_at = slice(sum(widths[:c]) * narrow, sum(widths[: c + 1]) * narrow)
@@ -190,14 +189,16 @@
             axis=0,
         ).astype(bf16)
         if c < 3:
-            if c == 2:
+            if c == 1:
                 d_local, rings[0] = together(d_local, rings[0])
+            elif c == 2:
+                d_local, pseudos[0] = together(d_local, pseudos[0])
             rings.append(lax.ppermute(d_local, ("fsdp", "tp"), ring_pairs))
             cross = lax.ppermute(d_local, ("fsdp", "tp"), cross_pairs)
             blocks = (d_local, cross)
         else:
-            if after in line.held:
-                d_local, line.held[after] = together(d_local, line.held[after])
+            if after in line.sums:
+                d_local, line.sums[after] = together(d_local, line.sums[after])
             came = swap(d_local, "tp", 1)
             far = swap(jnp.where(near, came, d_local), "fsdp", group)
             rings.append(None)
@@ -221,28 +222,37 @@
         update = m_new / bias_one / (
             jnp.sqrt(v_new / bias_two) + adam_eps
         ) + decay_rate * weight[:, cols_at].astype(f32)
-        pseudo = lax.optimization_barrier(update.astype(bf16))
-        parts.extend(pseudo[:, u * narrow : (u + 1) * narrow] for u in range(widths[c]))
-
-    first_three = [add_parts(c, None) for c in range(min(3, len(widths)))]
-    for c, found in enumerate(first_three):
-        add_pseudo(c, *found)
-    next_chunk = len(first_three)
-    for time in range(-2, units + line.hops - 1):
-        for hop in range(line.hops):
-            j = time - hop
-            if 0 <= j < units:
-                line.step(j, hop, j + 1 if hop else time - line.hops + 1)
-        if next_chunk < len(widths) and time >= sum(widths[:next_chunk]) - 6:
-            add_pseudo(next_chunk, *add_parts(next_chunk, time - line.hops + 2))
-            next_chunk += 1
-        if time + 2 < units:
-            line.enter(time + 2, parts[time + 2], time - line.hops + 2)
+        pseudos.append(lax.optimization_barrier(update.astype(bf16)))
+
+    def slice_pseudo(c):
+        parts.extend(pseudos[c][:, u * narrow : (u + 1) * narrow] for u in range(widths[c]))
+
+    early = min(3, len(widths))
+    first, second = add_parts(0, None), add_parts(1, None)
+    add_pseudo(0, *first)
+    third = add_parts(2, None)
+    add_pseudo(1, *second)
+    add_pseudo(2, *third)
+    for c in range(early):
+        slice_pseudo(c)
+    if islands == 4:
+        line.part.update(enumerate(parts))
+        for s in range(2):
+            line.send_outer(s)
+        for s in range(units + 3):
+            if early < len(widths) and s == 2:
+                for c in range(early, len(widths)):
+                    add_pseudo(c, *add_parts(c, 1))
+                    slice_pseudo(c)
+                line.part.update(enumerate(parts))
+            line.step(s)
+        sums = [line.totals[k] for k in range(units)]
+    else:
+        sums = [lax.psum(part, "island") for part in parts]
     momentum_out, step_out = [], []
-    for k in range(units):
+    for k, total in enumerate(sums):
         cols_at = slice(k * narrow, (k + 1) * narrow)
-        total = lax.optimization_barrier(line.totals[k])
-        delta = total.astype(f32) / lax.axis_size("island")
+        delta = total.astype(f32) / islands
         new_momentum, outer_step = outer_update(delta, momentum[:, cols_at])
         momentum_out.append(new_momentum)
         step_out.append(outer_step)

time: 271 us -> 253 us (0.934); the launches traced: 267 us -> 252 us
  starting transfers between devices: 106 us -> 92.2 us
  waiting for transfers between devices: 102 us -> 106 us
  local copies, waits for them, and re-layouts: 15.8 us -> 12.3 us
    ppermute x36 -> x27, starting transfers between devices: 81.4 us -> 68.7 us  [the longest x15 60.3 us: send_outer(): self.edge[s] = lax.ppermute(payload, 'island', pairs)]
    ppermute x19, waiting for transfers between devices: 59 us -> 64.2 us  [swap(): return lax.ppermute(value, axis, [(i, i ^ bit) for i in range(count)])]
    dot_general x6 -> x4, matrix products: 12 us -> 9.16 us  [project(): jnp.dot(block, weight, preferred_element_type=f32).astype(bf16)]
    unnamed x35 -> x31, local copies, waits for them, and re-layouts: 9.02 us -> 6.89 us
    ppermute x36 -> x27, waiting for transfers between devices: 40.3 us -> 40.4 us  [the longest x15 40.4 us: send_outer(): self.edge[s] = lax.ppermute(payload, 'island', pairs)]
  transfers between devices with their start and end apart: 61 -> 52, of which waited for: 21 -> 25; matrix products, arithmetic and copies ran while one was open for 18% -> 17% of each run, Pallas kernels for 0% -> 0%
where the time goes in v4:
time: 253 us; the launch traced here: 252 us
  waiting for transfers between devices  106 us (42%)
  starting transfers between devices  92.2 us (36%)
  matrix products  24.6 us (10%)
  other arithmetic  15.6 us (6%)
  local copies, waits for them, and re-layouts  12.3 us (5%)
    ppermute x19, waiting for transfers between devices, swap(): return lax.ppermute(value, axis, [(i, i ^ bit) for i in range(count)])  64.2 us
    ppermute x15, starting transfers between devices, send_outer(): self.edge[s] = lax.ppermute(payload, 'island', pairs)  60.3 us
    ppermute x15, waiting for transfers between devices, send_outer(): self.edge[s] = lax.ppermute(payload, 'island', pairs)  40.4 us
    dot_general x4, matrix products, add_pseudo(): lax.dot_general(context_all, d_all, (((0,), (0,)), ((), ())), preferred_e...  15.4 us
    ppermute x19, starting transfers between devices, swap(): return lax.ppermute(value, axis, [(i, i ^ bit) for i in range(count)])  11.7 us
    dot_general x4, matrix products, project(): jnp.dot(block, weight, preferred_element_type=f32).astype(bf16)  9.16 us
    ppermute x3, starting transfers between devices, add_parts(): cross = lax.ppermute(d_local, ('fsdp', 'tp'), cross_pairs)  8.63 us
    ppermute x12, starting transfers between devices, step(): self.mid[s] = lax.ppermute(self.sums[s], 'island', [(1, 2), (2, 1)])  8.45 us
  transfers between devices with their start and end apart: 52, of which 25 were waited for; matrix products, arithmetic and copies ran while one was open for 17% of the time, Pallas kernels for 0%

profile of v4, /device:TPU:2, one launch (start us, length us, event | category | flops | bytes accessed | tf_op | source)
XLA Modules:
  0.0 252.1 jit_solution(694160794046342164)
XLA Ops:
  0.7 3.3 %constant_dynamic-slice_fusion = (bf16[256,1536]{1,0:T(8,128)(2,1)}, bf16[256,1536]{1,0:T(8,128)(2,1)S(1)}, bf16[256,1536]{1,0:T(8,128)(2,1)S(1)}, bf16[256,1536]{1,0:T(8,128)(2,1)}) fusion(bf16[256,3072]{1,0:T(8,128)(2,1)} %param.10, s32[]{:T(128)S(6)} %select_n.197, s32[]{:T(128)S(6)} %select_n.196, bf16[256,3072]{1,0:T(8,128)(2,1)} %param.9), kind=kLoop, calls=%fused_computation.290 | loop fusion | bytes 6291464 | tf_op jit(solution)/shard_map/dynamic_slice | solution.py:94
  5.4 1.5 collective-permute-start.4
  9.2 8.3 %collective-permute-done.4 = bf16[128,1536]{1,0:T(8,128)(2,1)S(1)} collective-permute-done((bf16[128,1536]{1,0:T(8,128)(2,1)}, bf16[128,1536]{1,0:T(8,128)(2,1)S(1)}, u32[]{:S(2)}, u32[]{:S(2)}) %collective-permute-start.4) | collective-permute-done | bytes 393248 | tf_op jit(solution)/shard_map/ppermute | solution.py:27
  17.5 8.1 %collective-permute-done = bf16[128,1536]{1,0:T(8,128)(2,1)} collective-permute-done((bf16[128,1536]{1,0:T(8,128)(2,1)}, bf16[128,1536]{1,0:T(8,128)(2,1)}, u32[]{:S(2)}, u32[]{:S(2)}) %collective-permute-start) | collective-permute-done | bytes 393248 | tf_op jit(solution)/shard_map/ppermute | solution.py:27
  25.7 4.0 %convolution_convert_fusion.3 = bf16[256,1536]{1,0:T(8,128)(2,1)S(1)} fusion(bf16[1536,1536]{1,0:T(8,128)(2,1)} %param.12, bf16[128,1536]{1,0:T(8,128)(2,1)S(1)} %get-tuple-element.284, bf16[128,1536]{1,0:T(8,128)(2,1)} %collective-permute-done), kind=kOutput, calls=%fused_computation.21 | convolution fusion | flops 1209925632 | bytes 6291456 | tf_op jit(solution)/shard_map/dot_general | solution.py:89
  31.3 1.6 collective-permute-start.7
  34.5 2.4 convolution_convert_fusion.1
  38.4 1.6 collective-permute-start.13
  40.5 11.1 %collective-permute-done.8 = bf16[128,1536]{1,0:T(8,128)(2,1)S(1)} collective-permute-done((bf16[128,1536]{1,0:T(8,128)(2,1)S(1)}, bf16[128,1536]{1,0:T(8,128)(2,1)S(1)}, u32[]{:S(2)}, u32[]{:S(2)}) %collective-permute-start.8) | collective-permute-done | bytes 393248 | tf_op jit(solution)/shard_map/ppermute | solution.py:27
  52.1 1.8 collective-permute-start.10
  53.9 14.2 %collective-permute-done.11 = bf16[128,1536]{1,0:T(8,128)(2,1)S(1)} collective-permute-done((bf16[128,1536]{1,0:T(8,128)(2,1)S(1)}, bf16[128,1536]{1,0:T(8,128)(2,1)S(1)}, u32[]{:S(2)}, u32[]{:S(2)}) %collective-permute-start.11) | collective-permute-done | bytes 393248 | tf_op jit(solution)/shard_map/ppermute | solution.py:27
  68.6 1.7 collective-permute-start.12
  71.5 16.0 %collective-permute-done.12 = bf16[128,1536]{1,0:T(8,128)(2,1)S(1)} collective-permute-done((bf16[128,1536]{1,0:T(8,128)(2,1)S(1)}, bf16[128,1536]{1,0:T(8,128)(2,1)S(1)}, u32[]{:S(2)}, u32[]{:S(2)}) %collective-permute-start.12) | collective-permute-done | bytes 393248 | tf_op jit(solution)/shard_map/ppermute | solution.py:27
  87.4 1.5 multiply_reduce_fusion.3
  89.0 1.8 multiply_reduce_fusion.1
  92.5 3.2 %collective-permute-done.16 = f32[2,512]{1,0:T(2,128)S(1)} collective-permute-done((f32[2,512]{1,0:T(2,128)S(1)}, f32[2,512]{1,0:T(2,128)S(1)}, u32[]{:S(2)}, u32[]{:S(2)}) %collective-permute-start.16) | collective-permute-done | bytes 4128 | tf_op jit(solution)/shard_map/ppermute | solution.py:27
  97.1 1.6 collective-permute-start.17
  98.7 2.2 collective-permute-start.18
  102.2 1.5 collective-permute-start.22
  103.7 2.5 collective-permute-start.23
  106.6 1.4 fusion.63
  108.1 4.0 %collective-permute-start.20 = (bf16[512,512]{1,0:T(8,128)(2,1)S(1)}, bf16[512,512]{1,0:T(8,128)(2,1)S(1)}, u32[]{:S(2)}, u32[]{:S(2)}) collective-permute-start(bf16[512,512]{1,0:T(8,128)(2,1)S(1)} %pad_maximum_fusion.1), channel_id=1, source_target_pairs={{4,1},{1,4},{6,3},{3,6},{12,9},{9,12},{14,11},{11,14},{20,17},{17,... | collective-permute-start | bytes 1572872 | tf_op jit(solution)/shard_map/ppermute | solution.py:197
  112.1 3.7 %collective-permute-start.21 = (bf16[1536,128]{1,0:T(8,128)(2,1)S(1)}, bf16[1536,128]{1,0:T(8,128)(2,1)S(1)}, u32[]{:S(2)}, u32[]{:S(2)}) collective-permute-start(bf16[1536,128]{1,0:T(8,128)(2,1)S(1)} %fusion.63), channel_id=1, source_target_pairs={{0,8},{24,16},{1,9},{25,17},{2,10},{26,18},{3,11},{27,19},{4,12},{... | collective-permute-start | bytes 1179656 | tf_op jit(solution)/shard_map/ppermute | solution.py:52
  115.8 2.2 fusion.20
  118.1 2.0 collective-permute-start.25
  121.4 3.7 %collective-permute-done.21 = bf16[1536,128]{1,0:T(8,128)(2,1)S(1)} collective-permute-done((bf16[1536,128]{1,0:T(8,128)(2,1)S(1)}, bf16[1536,128]{1,0:T(8,128)(2,1)S(1)}, u32[]{:S(2)}, u32[]{:S(2)}) %collective-permute-start.21) | collective-permute-done | bytes 393248 | tf_op jit(solution)/shard_map/ppermute | solution.py:52
  126.1 4.4 %fusion.13 = bf16[1536,512]{1,0:T(8,128)(2,1)S(1)} fusion(bf16[1536,1536]{1,0:T(8,128)(2,1)S(1)} %bitcast.129, bf16[1,1536,1536]{2,1,0:T(8,128)(2,1)S(1)} %bitcast.131, bf16[1,1536,1536]{2,1,0:T(8,128)(2,1)S(1)} %bitcast.133, bf16[1024,1536]{1,0:T(8,128)(2,1)S(1)} %constant_dynamic-update-slice_fusion, bf16[512,512]{1,0:T(8,128)(2,1)S(1)} %get-tuple-element.289, ...), kind=kOutput, calls=%fused_computation.17 | convolution fusion | flops 1626865664 | bytes 10485760 | tf_op jit(solution)/shard_map/dot_general | solution.py:215
  130.5 3.0 %collective-permute-done.25 = bf16[1536,128]{1,0:T(8,128)(2,1)S(1)} collective-permute-done((bf16[1536,128]{1,0:T(8,128)(2,1)S(1)}, bf16[1536,128]{1,0:T(8,128)(2,1)S(1)}, u32[]{:S(2)}, u32[]{:S(2)}) %collective-permute-start.25) | collective-permute-done | bytes 393248 | tf_op jit(solution)/shard_map/ppermute | solution.py:52
  134.5 7.2 %collective-permute-start.26 = (bf16[1536,128]{1,0:T(8,128)(2,1)S(1)}, bf16[1536,128]{1,0:T(8,128)(2,1)S(1)}, u32[]{:S(2)}, u32[]{:S(2)}) collective-permute-start(bf16[1536,128]{1,0:T(8,128)(2,1)S(1)} %fusion.82), channel_id=1, source_target_pairs={{0,8},{24,16},{8,0},{16,24},{1,9},{25,17},{9,1},{17,25},{2,10},{26... | collective-permute-start | bytes 1179656 | tf_op jit(solution)/shard_map/ppermute | solution.py:52
  143.0 7.3 %collective-permute-start.30 = (bf16[1536,128]{1,0:T(8,128)(2,1)S(1)}, bf16[1536,128]{1,0:T(8,128)(2,1)S(1)}, u32[]{:S(2)}, u32[]{:S(2)}) collective-permute-start(bf16[1536,128]{1,0:T(8,128)(2,1)S(1)} %fusion.83), channel_id=1, source_target_pairs={{0,8},{24,16},{8,0},{16,24},{1,9},{25,17},{9,1},{17,25},{2,10},{26... | collective-permute-start | bytes 1179656 | tf_op jit(solution)/shard_map/ppermute | solution.py:52
  152.2 6.5 %collective-permute-start.32 = (bf16[1536,128]{1,0:T(8,128)(2,1)S(1)}, bf16[1536,128]{1,0:T(8,128)(2,1)S(1)}, u32[]{:S(2)}, u32[]{:S(2)}) collective-permute-start(bf16[1536,128]{1,0:T(8,128)(2,1)S(1)} %fusion.84), channel_id=1, source_target_pairs={{0,8},{24,16},{8,0},{16,24},{1,9},{25,17},{9,1},{17,25},{2,10},{26... | collective-permute-start | bytes 1179656 | tf_op jit(solution)/shard_map/ppermute | solution.py:52
  160.8 6.7 %collective-permute-start.36 = (bf16[1536,128]{1,0:T(8,128)(2,1)S(1)}, bf16[1536,128]{1,0:T(8,128)(2,1)S(1)}, u32[]{:S(2)}, u32[]{:S(2)}) collective-permute-start(bf16[1536,128]{1,0:T(8,128)(2,1)S(1)} %fusion.85), channel_id=1, source_target_pairs={{0,8},{24,16},{8,0},{16,24},{1,9},{25,17},{9,1},{17,25},{2,10},{26... | collective-permute-start | bytes 1179656 | tf_op jit(solution)/shard_map/ppermute | solution.py:52
  169.3 1.9 collective-permute-done.34
  171.2 7.4 %fusion.6 = bf16[1536,640]{1,0:T(8,128)(2,1)S(1)} fusion(bf16[1536,1536]{1,0:T(8,128)(2,1)} %param.12, bf16[1,1536,1536]{2,1,0:T(8,128)(2,1)} %param.14, bf16[1,1536,1536]{2,1,0:T(8,128)(2,1)} %param.13, bf16[1024,1536]{1,0:T(8,128)(2,1)S(1)} %constant_dynamic-update-slice_fusion, bf16[512,640]{1,0:T(8,128)(2,1)S(1)} %collective-permute-done.34, ...), kind=kOutput, calls=%fused_computation.8 | convolution fusion | flops 2033582080 | bytes 12320768 | tf_op jit(solution)/shard_map/dot_general | solution.py:215
  178.8 4.9 %collective-permute-start.38 = (bf16[1536,128]{1,0:T(8,128)(2,1)S(1)}, bf16[1536,128]{1,0:T(8,128)(2,1)S(1)}, u32[]{:S(2)}, u32[]{:S(2)}) collective-permute-start(bf16[1536,128]{1,0:T(8,128)(2,1)S(1)} %fusion.86), channel_id=1, source_target_pairs={{0,8},{24,16},{8,0},{16,24},{1,9},{25,17},{9,1},{17,25},{2,10},{26... | collective-permute-start | bytes 1179656 | tf_op jit(solution)/shard_map/ppermute | solution.py:52
  184.9 2.1 collective-permute-start.40
  188.0 5.7 %collective-permute-done.38 = bf16[1536,128]{1,0:T(8,128)(2,1)S(1)} collective-permute-done((bf16[1536,128]{1,0:T(8,128)(2,1)S(1)}, bf16[1536,128]{1,0:T(8,128)(2,1)S(1)}, u32[]{:S(2)}, u32[]{:S(2)}) %collective-permute-start.38) | collective-permute-done | bytes 393248 | tf_op jit(solution)/shard_map/ppermute | solution.py:52
  194.6 4.1 %collective-permute-start.42 = (bf16[1536,128]{1,0:T(8,128)(2,1)S(1)}, bf16[1536,128]{1,0:T(8,128)(2,1)S(1)}, u32[]{:S(2)}, u32[]{:S(2)}) collective-permute-start(bf16[1536,128]{1,0:T(8,128)(2,1)S(1)} %fusion.88), channel_id=1, source_target_pairs={{0,8},{24,16},{8,0},{16,24},{1,9},{25,17},{9,1},{17,25},{2,10},{26... | collective-permute-start | bytes 1179656 | tf_op jit(solution)/shard_map/ppermute | solution.py:52
  198.7 3.3 %collective-permute-done.40 = bf16[1536,128]{1,0:T(8,128)(2,1)S(1)} collective-permute-done((bf16[1536,128]{1,0:T(8,128)(2,1)S(1)}, bf16[1536,128]{1,0:T(8,128)(2,1)S(1)}, u32[]{:S(2)}, u32[]{:S(2)}) %collective-permute-start.40) | collective-permute-done | bytes 393248 | tf_op jit(solution)/shard_map/ppermute | solution.py:52
  203.5 5.1 %collective-permute-start.44 = (bf16[1536,128]{1,0:T(8,128)(2,1)S(1)}, bf16[1536,128]{1,0:T(8,128)(2,1)S(1)}, u32[]{:S(2)}, u32[]{:S(2)}) collective-permute-start(bf16[1536,128]{1,0:T(8,128)(2,1)S(1)} %fusion.89), channel_id=1, source_target_pairs={{0,8},{24,16},{8,0},{16,24},{1,9},{25,17},{9,1},{17,25},{2,10},{26... | collective-permute-start | bytes 1179656 | tf_op jit(solution)/shard_map/ppermute | solution.py:52
  208.6 1.9 collective-permute-done.42
  211.5 5.5 %collective-permute-start.46 = (bf16[1536,128]{1,0:T(8,128)(2,1)S(1)}, bf16[1536,128]{1,0:T(8,128)(2,1)S(1)}, u32[]{:S(2)}, u32[]{:S(2)}) collective-permute-start(bf16[1536,128]{1,0:T(8,128)(2,1)S(1)} %fusion.90), channel_id=1, source_target_pairs={{0,8},{24,16},{8,0},{16,24},{1,9},{25,17},{9,1},{17,25},{2,10},{26... | collective-permute-start | bytes 1179656 | tf_op jit(solution)/shard_map/ppermute | solution.py:52
  221.1 6.2 %collective-permute-done.46 = bf16[1536,128]{1,0:T(8,128)(2,1)S(1)} collective-permute-done((bf16[1536,128]{1,0:T(8,128)(2,1)S(1)}, bf16[1536,128]{1,0:T(8,128)(2,1)S(1)}, u32[]{:S(2)}, u32[]{:S(2)}) %collective-permute-start.46) | collective-permute-done | bytes 393248 | tf_op jit(solution)/shard_map/ppermute | solution.py:52
  230.0 5.8 %collective-permute-done.48 = bf16[1536,128]{1,0:T(8,128)(2,1)S(1)} collective-permute-done((bf16[1536,128]{1,0:T(8,128)(2,1)S(1)}, bf16[1536,128]{1,0:T(8,128)(2,1)S(1)}, u32[]{:S(2)}, u32[]{:S(2)}) %collective-permute-start.48) | collective-permute-done | bytes 393248 | tf_op jit(solution)/shard_map/ppermute | solution.py:52
  238.1 1.9 collective-permute-done.50
  240.0 5.6 %collective-permute-done.51 = bf16[1536,128]{1,0:T(8,128)(2,1)S(1)} collective-permute-done((bf16[1536,128]{1,0:T(8,128)(2,1)S(1)}, bf16[1536,128]{1,0:T(8,128)(2,1)S(1)}, u32[]{:S(2)}, u32[]{:S(2)}) %collective-permute-start.51) | collective-permute-done | bytes 393248 | tf_op jit(solution)/shard_map/ppermute | solution.py:52
  246.5 3.4 %copy-done.2 = f32[1536,1536]{1,0:T(8,128)} copy-done((f32[1536,1536]{1,0:T(8,128)}, f32[1536,1536]{1,0:T(8,128)S(1)}, u32[]{:S(2)}) %copy-start.2) | copy-done | bytes 9437208
  250.0 2.2 copy-done.3
  (201 shorter events, 41.3 us)
Async XLA Ops:
  0.6 24.9 %collective-permute-start.1 = (bf16[256,1536]{1,0:T(8,128)(2,1)}, bf16[256,1536]{1,0:T(8,128)(2,1)S(1)}, u32[]{:S(2)}, u32[]{:S(2)}) collective-permute-start(bf16[256,1536]{1,0:T(8,128)(2,1)} %param.8), channel_id=1, source_target_pairs={{0,2},{2,0},{4,6},{6,4},{1,3},{3,1},{5,7},{7,5},{8,10},{10,8},{12,... | collective-permute-start | bytes 2359304 | tf_op jit(solution)/shard_map/ppermute | solution.py:27
  4.1 21.5 %collective-permute-start.2 = (bf16[256,1536]{1,0:T(8,128)(2,1)}, bf16[256,1536]{1,0:T(8,128)(2,1)}, u32[]{:S(2)}, u32[]{:S(2)}) collective-permute-start(bf16[256,1536]{1,0:T(8,128)(2,1)} %get-tuple-element.125), channel_id=1, source_target_pairs={{0,2},{2,0},{4,6},{6,4},{1,3},{3,1},{5,7},{7,5},{8,10},{10,8},{12,... | collective-permute-start | bytes 2359304 | tf_op jit(solution)/shard_map/ppermute | solution.py:27
  4.5 21.1 %collective-permute-start.3 = (bf16[256,1536]{1,0:T(8,128)(2,1)}, bf16[256,1536]{1,0:T(8,128)(2,1)}, u32[]{:S(2)}, u32[]{:S(2)}) collective-permute-start(bf16[256,1536]{1,0:T(8,128)(2,1)} %get-tuple-element.127), channel_id=1, source_target_pairs={{0,2},{2,0},{4,6},{6,4},{1,3},{3,1},{5,7},{7,5},{8,10},{10,8},{12,... | collective-permute-start | bytes 2359304 | tf_op jit(solution)/shard_map/ppermute | solution.py:27
  5.4 12.1 %collective-permute-start.4 = (bf16[128,1536]{1,0:T(8,128)(2,1)}, bf16[128,1536]{1,0:T(8,128)(2,1)S(1)}, u32[]{:S(2)}, u32[]{:S(2)}) collective-permute-start(bf16[128,1536]{1,0:T(8,128)(2,1)} %slice.340), channel_id=1, source_target_pairs={{0,4},{2,6},{4,0},{6,2},{1,5},{3,7},{5,1},{7,3},{8,12},{10,14},{12... | collective-permute-start | bytes 1179656 | tf_op jit(solution)/shard_map/ppermute | solution.py:27
  7.8 17.7 %collective-permute-start = (bf16[128,1536]{1,0:T(8,128)(2,1)}, bf16[128,1536]{1,0:T(8,128)(2,1)}, u32[]{:S(2)}, u32[]{:S(2)}) collective-permute-start(bf16[128,1536]{1,0:T(8,128)(2,1)} %get-tuple-element.287), channel_id=1, source_target_pairs={{0,4},{2,6},{4,0},{6,2},{1,5},{3,7},{5,1},{7,3},{8,12},{10,14},{12... | collective-permute-start | bytes 1179656 | tf_op jit(solution)/shard_map/ppermute | solution.py:27
  17.5 19.5 %collective-permute-start.6 = (bf16[128,1536]{1,0:T(8,128)(2,1)S(1)}, bf16[128,1536]{1,0:T(8,128)(2,1)S(1)}, u32[]{:S(2)}, u32[]{:S(2)}) collective-permute-start(bf16[128,1536]{1,0:T(8,128)(2,1)S(1)} %collective-permute-done.4), channel_id=1, source_target_pairs={{0,2},{2,0},{4,6},{6,4},{1,3},{3,1},{5,7},{7,5},{8,10},{10,8},{12,... | collective-permute-start | bytes 1179656 | tf_op jit(solution)/shard_map/ppermute | solution.py:27
  25.6 8.9 %collective-permute-start.5 = (bf16[128,1536]{1,0:T(8,128)(2,1)}, bf16[128,1536]{1,0:T(8,128)(2,1)S(1)}, u32[]{:S(2)}, u32[]{:S(2)}) collective-permute-start(bf16[128,1536]{1,0:T(8,128)(2,1)} %collective-permute-done), channel_id=1, source_target_pairs={{0,2},{2,0},{4,6},{6,4},{1,3},{3,1},{5,7},{7,5},{8,10},{10,8},{12,... | collective-permute-start | bytes 1179656 | tf_op jit(solution)/shard_map/ppermute | solution.py:27
  31.3 20.5 %collective-permute-start.7 = (bf16[128,1536]{1,0:T(8,128)(2,1)S(1)}, bf16[128,1536]{1,0:T(8,128)(2,1)S(1)}, u32[]{:S(2)}, u32[]{:S(2)}) collective-permute-start(bf16[128,1536]{1,0:T(8,128)(2,1)S(1)} %get-tuple-element.280), channel_id=1, source_target_pairs={{0,4},{2,6},{4,0},{6,2},{1,5},{3,7},{5,1},{7,3},{8,12},{10,14},{12... | collective-permute-start | bytes 1179656 | tf_op jit(solution)/shard_map/ppermute | solution.py:27
  32.8 18.8 %collective-permute-start.8 = (bf16[128,1536]{1,0:T(8,128)(2,1)S(1)}, bf16[128,1536]{1,0:T(8,128)(2,1)S(1)}, u32[]{:S(2)}, u32[]{:S(2)}) collective-permute-start(bf16[128,1536]{1,0:T(8,128)(2,1)S(1)} %get-tuple-element.276), channel_id=1, source_target_pairs={{0,4},{2,6},{4,0},{6,2},{1,5},{3,7},{5,1},{7,3},{8,12},{10,14},{12... | collective-permute-start | bytes 1179656 | tf_op jit(solution)/shard_map/ppermute | solution.py:27
  38.4 29.7 %collective-permute-start.13 = (bf16[128,1536]{1,0:T(8,128)(2,1)S(1)}, bf16[128,1536]{1,0:T(8,128)(2,1)S(1)}, u32[]{:S(2)}, u32[]{:S(2)}) collective-permute-start(bf16[128,1536]{1,0:T(8,128)(2,1)S(1)} %get-tuple-element.279), channel_id=1, source_target_pairs={{0,4},{2,6},{4,0},{6,2},{1,5},{3,7},{5,1},{7,3},{8,12},{10,14},{12... | collective-permute-start | bytes 1179656 | tf_op jit(solution)/shard_map/ppermute | solution.py:27
  40.0 28.1 %collective-permute-start.11 = (bf16[128,1536]{1,0:T(8,128)(2,1)S(1)}, bf16[128,1536]{1,0:T(8,128)(2,1)S(1)}, u32[]{:S(2)}, u32[]{:S(2)}) collective-permute-start(bf16[128,1536]{1,0:T(8,128)(2,1)S(1)} %get-tuple-element.282), channel_id=1, source_target_pairs={{0,4},{2,6},{4,0},{6,2},{1,5},{3,7},{5,1},{7,3},{8,12},{10,14},{12... | collective-permute-start | bytes 1179656 | tf_op jit(solution)/shard_map/ppermute | solution.py:27
  51.8 19.2 %collective-permute-start.9 = (bf16[128,1536]{1,0:T(8,128)(2,1)S(1)}, bf16[128,1536]{1,0:T(8,128)(2,1)S(1)}, u32[]{:S(2)}, u32[]{:S(2)}) collective-permute-start(bf16[128,1536]{1,0:T(8,128)(2,1)S(1)} %get-tuple-element.272), channel_id=1, source_target_pairs={{0,1},{1,0},{2,3},{3,2},{4,5},{5,4},{6,7},{7,6},{8,9},{9,8},{10,11... | collective-permute-start | bytes 1179656 | tf_op jit(solution)/shard_map/ppermute | solution.py:27
  52.1 18.5 %collective-permute-start.10 = (bf16[128,1536]{1,0:T(8,128)(2,1)S(1)}, bf16[128,1536]{1,0:T(8,128)(2,1)S(1)}, u32[]{:S(2)}, u32[]{:S(2)}) collective-permute-start(bf16[128,1536]{1,0:T(8,128)(2,1)S(1)} %get-tuple-element.270), channel_id=1, source_target_pairs={{0,1},{1,0},{2,3},{3,2},{4,5},{5,4},{6,7},{7,6},{8,9},{9,8},{10,11... | collective-permute-start | bytes 1179656 | tf_op jit(solution)/shard_map/ppermute | solution.py:27
  68.2 20.7 %collective-permute-start.14 = (bf16[128,1536]{1,0:T(8,128)(2,1)S(1)}, bf16[128,1536]{1,0:T(8,128)(2,1)S(1)}, u32[]{:S(2)}, u32[]{:S(2)}) collective-permute-start(bf16[128,1536]{1,0:T(8,128)(2,1)S(1)} %broadcast_select_fusion.4), channel_id=1, source_target_pairs={{0,1},{1,0},{2,3},{3,2},{4,5},{5,4},{6,7},{7,6},{8,9},{9,8},{10,11... | collective-permute-start | bytes 1179656 | tf_op jit(solution)/shard_map/ppermute | solution.py:27
  68.6 18.8 %collective-permute-start.12 = (bf16[128,1536]{1,0:T(8,128)(2,1)S(1)}, bf16[128,1536]{1,0:T(8,128)(2,1)S(1)}, u32[]{:S(2)}, u32[]{:S(2)}) collective-permute-start(bf16[128,1536]{1,0:T(8,128)(2,1)S(1)} %get-tuple-element.274), channel_id=1, source_target_pairs={{0,1},{1,0},{2,3},{3,2},{4,5},{5,4},{6,7},{7,6},{8,9},{9,8},{10,11... | collective-permute-start | bytes 1179656 | tf_op jit(solution)/shard_map/ppermute | solution.py:27
  102.2 13.6 %collective-permute-start.22 = (bf16[512,256]{1,0:T(8,128)(2,1)S(1)}, bf16[512,256]{1,0:T(8,128)(2,1)S(1)}, u32[]{:S(2)}, u32[]{:S(2)}) collective-permute-start(bf16[512,256]{1,0:T(8,128)(2,1)S(1)} %pad_maximum_fusion.2), channel_id=1, source_target_pairs={{0,1},{5,4},{4,0},{1,5},{2,3},{7,6},{6,2},{3,7},{8,9},{13,12},{12,... | collective-permute-start | bytes 786440 | tf_op jit(solution)/shard_map/ppermute | solution.py:196
  103.7 12.1 %collective-permute-start.23 = (bf16[512,256]{1,0:T(8,128)(2,1)S(1)}, bf16[512,256]{1,0:T(8,128)(2,1)S(1)}, u32[]{:S(2)}, u32[]{:S(2)}) collective-permute-start(bf16[512,256]{1,0:T(8,128)(2,1)S(1)} %pad_maximum_fusion.2), channel_id=1, source_target_pairs={{4,1},{1,4},{6,3},{3,6},{12,9},{9,12},{14,11},{11,14},{20,17},{17,... | collective-permute-start | bytes 786440 | tf_op jit(solution)/shard_map/ppermute | solution.py:197
  108.0 17.9 %collective-permute-start.19 = (bf16[512,512]{1,0:T(8,128)(2,1)S(1)}, bf16[512,512]{1,0:T(8,128)(2,1)S(1)}, u32[]{:S(2)}, u32[]{:S(2)}) collective-permute-start(bf16[512,512]{1,0:T(8,128)(2,1)S(1)} %pad_maximum_fusion.1), channel_id=1, source_target_pairs={{0,1},{5,4},{4,0},{1,5},{2,3},{7,6},{6,2},{3,7},{8,9},{13,12},{12,... | collective-permute-start | bytes 1572872 | tf_op jit(solution)/shard_map/ppermute | solution.py:196
  108.1 17.8 %collective-permute-start.20 = (bf16[512,512]{1,0:T(8,128)(2,1)S(1)}, bf16[512,512]{1,0:T(8,128)(2,1)S(1)}, u32[]{:S(2)}, u32[]{:S(2)}) collective-permute-start(bf16[512,512]{1,0:T(8,128)(2,1)S(1)} %pad_maximum_fusion.1), channel_id=1, source_target_pairs={{4,1},{1,4},{6,3},{3,6},{12,9},{9,12},{14,11},{11,14},{20,17},{17,... | collective-permute-start | bytes 1572872 | tf_op jit(solution)/shard_map/ppermute | solution.py:197
  112.1 13.0 %collective-permute-start.21 = (bf16[1536,128]{1,0:T(8,128)(2,1)S(1)}, bf16[1536,128]{1,0:T(8,128)(2,1)S(1)}, u32[]{:S(2)}, u32[]{:S(2)}) collective-permute-start(bf16[1536,128]{1,0:T(8,128)(2,1)S(1)} %fusion.63), channel_id=1, source_target_pairs={{0,8},{24,16},{1,9},{25,17},{2,10},{26,18},{3,11},{27,19},{4,12},{... | collective-permute-start | bytes 1179656 | tf_op jit(solution)/shard_map/ppermute | solution.py:52
  118.1 15.5 %collective-permute-start.25 = (bf16[1536,128]{1,0:T(8,128)(2,1)S(1)}, bf16[1536,128]{1,0:T(8,128)(2,1)S(1)}, u32[]{:S(2)}, u32[]{:S(2)}) collective-permute-start(bf16[1536,128]{1,0:T(8,128)(2,1)S(1)} %get-tuple-element.269), channel_id=1, source_target_pairs={{0,8},{24,16},{1,9},{25,17},{2,10},{26,18},{3,11},{27,19},{4,12},{... | collective-permute-start | bytes 1179656 | tf_op jit(solution)/shard_map/ppermute | solution.py:52
  120.1 21.9 %collective-permute-start.28 = (bf16[1536,128]{1,0:T(8,128)(2,1)S(1)}, bf16[1536,128]{1,0:T(8,128)(2,1)S(1)}, u32[]{:S(2)}, u32[]{:S(2)}) collective-permute-start(bf16[1536,128]{1,0:T(8,128)(2,1)S(1)} %get-tuple-element.268), channel_id=1, source_target_pairs={{0,8},{24,16},{1,9},{25,17},{2,10},{26,18},{3,11},{27,19},{4,12},{... | collective-permute-start | bytes 1179656 | tf_op jit(solution)/shard_map/ppermute | solution.py:52
  125.2 9.1 %collective-permute-start.24 = (bf16[1536,128]{1,0:T(8,128)(2,1)S(1)}, bf16[1536,128]{1,0:T(8,128)(2,1)S(1)}, u32[]{:S(2)}, u32[]{:S(2)}) collective-permute-start(bf16[1536,128]{1,0:T(8,128)(2,1)S(1)} %add_convert_fusion.35), channel_id=1, source_target_pairs={{8,16},{16,8},{9,17},{17,9},{10,18},{18,10},{11,19},{19,11},{12,20... | collective-permute-start | bytes 1179656 | tf_op jit(solution)/shard_map/ppermute | solution.py:60
  133.7 9.2 %collective-permute-start.27 = (bf16[1536,128]{1,0:T(8,128)(2,1)S(1)}, bf16[1536,128]{1,0:T(8,128)(2,1)S(1)}, u32[]{:S(2)}, u32[]{:S(2)}) collective-permute-start(bf16[1536,128]{1,0:T(8,128)(2,1)S(1)} %add_convert_fusion.34), channel_id=1, source_target_pairs={{8,16},{16,8},{9,17},{17,9},{10,18},{18,10},{11,19},{19,11},{12,20... | collective-permute-start | bytes 1179656 | tf_op jit(solution)/shard_map/ppermute | solution.py:60
  134.5 16.7 %collective-permute-start.26 = (bf16[1536,128]{1,0:T(8,128)(2,1)S(1)}, bf16[1536,128]{1,0:T(8,128)(2,1)S(1)}, u32[]{:S(2)}, u32[]{:S(2)}) collective-permute-start(bf16[1536,128]{1,0:T(8,128)(2,1)S(1)} %fusion.82), channel_id=1, source_target_pairs={{0,8},{24,16},{8,0},{16,24},{1,9},{25,17},{9,1},{17,25},{2,10},{26... | collective-permute-start | bytes 1179656 | tf_op jit(solution)/shard_map/ppermute | solution.py:52
  142.1 9.9 %collective-permute-start.29 = (bf16[1536,128]{1,0:T(8,128)(2,1)S(1)}, bf16[1536,128]{1,0:T(8,128)(2,1)S(1)}, u32[]{:S(2)}, u32[]{:S(2)}) collective-permute-start(bf16[1536,128]{1,0:T(8,128)(2,1)S(1)} %add_convert_fusion.32), channel_id=1, source_target_pairs={{8,16},{16,8},{9,17},{17,9},{10,18},{18,10},{11,19},{19,11},{12,20... | collective-permute-start | bytes 1179656 | tf_op jit(solution)/shard_map/ppermute | solution.py:60
  142.8 17.7 %collective-permute-start.33 = (bf16[512,640]{1,0:T(8,128)(2,1)S(1)}, bf16[512,640]{1,0:T(8,128)(2,1)S(1)}, u32[]{:S(2)}, u32[]{:S(2)}) collective-permute-start(bf16[512,640]{1,0:T(8,128)(2,1)S(1)} %pad_maximum_fusion), channel_id=1, source_target_pairs={{0,1},{1,0},{2,3},{3,2},{4,5},{5,4},{6,7},{7,6},{8,9},{9,8},{10,11... | collective-permute-start | bytes 1966088 | tf_op jit(solution)/shard_map/ppermute | solution.py:27
  143.0 16.6 %collective-permute-start.30 = (bf16[1536,128]{1,0:T(8,128)(2,1)S(1)}, bf16[1536,128]{1,0:T(8,128)(2,1)S(1)}, u32[]{:S(2)}, u32[]{:S(2)}) collective-permute-start(bf16[1536,128]{1,0:T(8,128)(2,1)S(1)} %fusion.83), channel_id=1, source_target_pairs={{0,8},{24,16},{8,0},{16,24},{1,9},{25,17},{9,1},{17,25},{2,10},{26... | collective-permute-start | bytes 1179656 | tf_op jit(solution)/shard_map/ppermute | solution.py:52
  151.3 9.3 %collective-permute-start.31 = (bf16[1536,128]{1,0:T(8,128)(2,1)S(1)}, bf16[1536,128]{1,0:T(8,128)(2,1)S(1)}, u32[]{:S(2)}, u32[]{:S(2)}) collective-permute-start(bf16[1536,128]{1,0:T(8,128)(2,1)S(1)} %add_convert_fusion.30), channel_id=1, source_target_pairs={{8,16},{16,8},{9,17},{17,9},{10,18},{18,10},{11,19},{19,11},{12,20... | collective-permute-start | bytes 1179656 | tf_op jit(solution)/shard_map/ppermute | solution.py:60
  152.2 15.9 %collective-permute-start.32 = (bf16[1536,128]{1,0:T(8,128)(2,1)S(1)}, bf16[1536,128]{1,0:T(8,128)(2,1)S(1)}, u32[]{:S(2)}, u32[]{:S(2)}) collective-permute-start(bf16[1536,128]{1,0:T(8,128)(2,1)S(1)} %fusion.84), channel_id=1, source_target_pairs={{0,8},{24,16},{8,0},{16,24},{1,9},{25,17},{9,1},{17,25},{2,10},{26... | collective-permute-start | bytes 1179656 | tf_op jit(solution)/shard_map/ppermute | solution.py:52
  159.7 9.6 %collective-permute-start.35 = (bf16[1536,128]{1,0:T(8,128)(2,1)S(1)}, bf16[1536,128]{1,0:T(8,128)(2,1)S(1)}, u32[]{:S(2)}, u32[]{:S(2)}) collective-permute-start(bf16[1536,128]{1,0:T(8,128)(2,1)S(1)} %add_convert_fusion.28), channel_id=1, source_target_pairs={{8,16},{16,8},{9,17},{17,9},{10,18},{18,10},{11,19},{19,11},{12,20... | collective-permute-start | bytes 1179656 | tf_op jit(solution)/shard_map/ppermute | solution.py:60
  160.6 10.7 %collective-permute-start.34 = (bf16[512,640]{1,0:T(8,128)(2,1)S(1)}, bf16[512,640]{1,0:T(8,128)(2,1)S(1)}, u32[]{:S(2)}, u32[]{:S(2)}) collective-permute-start(bf16[512,640]{1,0:T(8,128)(2,1)S(1)} %get-tuple-element.263), channel_id=1, source_target_pairs={{0,4},{2,6},{4,0},{6,2},{1,5},{3,7},{5,1},{7,3},{8,12},{10,14},{12... | collective-permute-start | bytes 1966088 | tf_op jit(solution)/shard_map/ppermute | solution.py:27
  160.8 22.9 %collective-permute-start.36 = (bf16[1536,128]{1,0:T(8,128)(2,1)S(1)}, bf16[1536,128]{1,0:T(8,128)(2,1)S(1)}, u32[]{:S(2)}, u32[]{:S(2)}) collective-permute-start(bf16[1536,128]{1,0:T(8,128)(2,1)S(1)} %fusion.85), channel_id=1, source_target_pairs={{0,8},{24,16},{8,0},{16,24},{1,9},{25,17},{9,1},{17,25},{2,10},{26... | collective-permute-start | bytes 1179656 | tf_op jit(solution)/shard_map/ppermute | solution.py:52
  168.2 16.6 %collective-permute-start.37 = (bf16[1536,128]{1,0:T(8,128)(2,1)S(1)}, bf16[1536,128]{1,0:T(8,128)(2,1)S(1)}, u32[]{:S(2)}, u32[]{:S(2)}) collective-permute-start(bf16[1536,128]{1,0:T(8,128)(2,1)S(1)} %add_convert_fusion.26), channel_id=1, source_target_pairs={{8,16},{16,8},{9,17},{17,9},{10,18},{18,10},{11,19},{19,11},{12,20... | collective-permute-start | bytes 1179656 | tf_op jit(solution)/shard_map/ppermute | solution.py:60
  178.8 14.8 %collective-permute-start.38 = (bf16[1536,128]{1,0:T(8,128)(2,1)S(1)}, bf16[1536,128]{1,0:T(8,128)(2,1)S(1)}, u32[]{:S(2)}, u32[]{:S(2)}) collective-permute-start(bf16[1536,128]{1,0:T(8,128)(2,1)S(1)} %fusion.86), channel_id=1, source_target_pairs={{0,8},{24,16},{8,0},{16,24},{1,9},{25,17},{9,1},{17,25},{2,10},{26... | collective-permute-start | bytes 1179656 | tf_op jit(solution)/shard_map/ppermute | solution.py:52
  183.8 10.6 %collective-permute-start.39 = (bf16[1536,128]{1,0:T(8,128)(2,1)S(1)}, bf16[1536,128]{1,0:T(8,128)(2,1)S(1)}, u32[]{:S(2)}, u32[]{:S(2)}) collective-permute-start(bf16[1536,128]{1,0:T(8,128)(2,1)S(1)} %add_convert_fusion.24), channel_id=1, source_target_pairs={{8,16},{16,8},{9,17},{17,9},{10,18},{18,10},{11,19},{19,11},{12,20... | collective-permute-start | bytes 1179656 | tf_op jit(solution)/shard_map/ppermute | solution.py:60
  184.9 17.2 %collective-permute-start.40 = (bf16[1536,128]{1,0:T(8,128)(2,1)S(1)}, bf16[1536,128]{1,0:T(8,128)(2,1)S(1)}, u32[]{:S(2)}, u32[]{:S(2)}) collective-permute-start(bf16[1536,128]{1,0:T(8,128)(2,1)S(1)} %fusion.87), channel_id=1, source_target_pairs={{0,8},{24,16},{8,0},{16,24},{1,9},{25,17},{9,1},{17,25},{2,10},{26... | collective-permute-start | bytes 1179656 | tf_op jit(solution)/shard_map/ppermute | solution.py:52
  193.7 9.6 %collective-permute-start.41 = (bf16[1536,128]{1,0:T(8,128)(2,1)S(1)}, bf16[1536,128]{1,0:T(8,128)(2,1)S(1)}, u32[]{:S(2)}, u32[]{:S(2)}) collective-permute-start(bf16[1536,128]{1,0:T(8,128)(2,1)S(1)} %add_convert_fusion.22), channel_id=1, source_target_pairs={{8,16},{16,8},{9,17},{17,9},{10,18},{18,10},{11,19},{19,11},{12,20... | collective-permute-start | bytes 1179656 | tf_op jit(solution)/shard_map/ppermute | solution.py:60
  194.6 15.9 %collective-permute-start.42 = (bf16[1536,128]{1,0:T(8,128)(2,1)S(1)}, bf16[1536,128]{1,0:T(8,128)(2,1)S(1)}, u32[]{:S(2)}, u32[]{:S(2)}) collective-permute-start(bf16[1536,128]{1,0:T(8,128)(2,1)S(1)} %fusion.88), channel_id=1, source_target_pairs={{0,8},{24,16},{8,0},{16,24},{1,9},{25,17},{9,1},{17,25},{2,10},{26... | collective-permute-start | bytes 1179656 | tf_op jit(solution)/shard_map/ppermute | solution.py:52
  202.2 9.1 %collective-permute-start.43 = (bf16[1536,128]{1,0:T(8,128)(2,1)S(1)}, bf16[1536,128]{1,0:T(8,128)(2,1)S(1)}, u32[]{:S(2)}, u32[]{:S(2)}) collective-permute-start(bf16[1536,128]{1,0:T(8,128)(2,1)S(1)} %add_convert_fusion.20), channel_id=1, source_target_pairs={{8,16},{16,8},{9,17},{17,9},{10,18},{18,10},{11,19},{19,11},{12,20... | collective-permute-start | bytes 1179656 | tf_op jit(solution)/shard_map/ppermute | solution.py:60
  203.5 15.4 %collective-permute-start.44 = (bf16[1536,128]{1,0:T(8,128)(2,1)S(1)}, bf16[1536,128]{1,0:T(8,128)(2,1)S(1)}, u32[]{:S(2)}, u32[]{:S(2)}) collective-permute-start(bf16[1536,128]{1,0:T(8,128)(2,1)S(1)} %fusion.89), channel_id=1, source_target_pairs={{0,8},{24,16},{8,0},{16,24},{1,9},{25,17},{9,1},{17,25},{2,10},{26... | collective-permute-start | bytes 1179656 | tf_op jit(solution)/shard_map/ppermute | solution.py:52
  210.6 9.1 %collective-permute-start.45 = (bf16[1536,128]{1,0:T(8,128)(2,1)S(1)}, bf16[1536,128]{1,0:T(8,128)(2,1)S(1)}, u32[]{:S(2)}, u32[]{:S(2)}) collective-permute-start(bf16[1536,128]{1,0:T(8,128)(2,1)S(1)} %add_convert_fusion.18), channel_id=1, source_target_pairs={{8,16},{16,8},{9,17},{17,9},{10,18},{18,10},{11,19},{19,11},{12,20... | collective-permute-start | bytes 1179656 | tf_op jit(solution)/shard_map/ppermute | solution.py:60
  211.5 15.9 %collective-permute-start.46 = (bf16[1536,128]{1,0:T(8,128)(2,1)S(1)}, bf16[1536,128]{1,0:T(8,128)(2,1)S(1)}, u32[]{:S(2)}, u32[]{:S(2)}) collective-permute-start(bf16[1536,128]{1,0:T(8,128)(2,1)S(1)} %fusion.90), channel_id=1, source_target_pairs={{0,8},{24,16},{8,0},{16,24},{1,9},{25,17},{9,1},{17,25},{2,10},{26... | collective-permute-start | bytes 1179656 | tf_op jit(solution)/shard_map/ppermute | solution.py:52
  219.0 9.6 %collective-permute-start.47 = (bf16[1536,128]{1,0:T(8,128)(2,1)S(1)}, bf16[1536,128]{1,0:T(8,128)(2,1)S(1)}, u32[]{:S(2)}, u32[]{:S(2)}) collective-permute-start(bf16[1536,128]{1,0:T(8,128)(2,1)S(1)} %add_convert_fusion.16), channel_id=1, source_target_pairs={{8,16},{16,8},{9,17},{17,9},{10,18},{18,10},{11,19},{19,11},{12,20... | collective-permute-start | bytes 1179656 | tf_op jit(solution)/shard_map/ppermute | solution.py:60
  219.8 16.0 %collective-permute-start.48 = (bf16[1536,128]{1,0:T(8,128)(2,1)S(1)}, bf16[1536,128]{1,0:T(8,128)(2,1)S(1)}, u32[]{:S(2)}, u32[]{:S(2)}) collective-permute-start(bf16[1536,128]{1,0:T(8,128)(2,1)S(1)} %add_convert_fusion.15), channel_id=1, source_target_pairs={{8,0},{16,24},{9,1},{17,25},{10,2},{18,26},{11,3},{19,27},{12,4},{... | collective-permute-start | bytes 1179656 | tf_op jit(solution)/shard_map/ppermute | solution.py:52
  227.5 8.4 %collective-permute-start.49 = (bf16[1536,128]{1,0:T(8,128)(2,1)S(1)}, bf16[1536,128]{1,0:T(8,128)(2,1)S(1)}, u32[]{:S(2)}, u32[]{:S(2)}) collective-permute-start(bf16[1536,128]{1,0:T(8,128)(2,1)S(1)} %add_convert_fusion.14), channel_id=1, source_target_pairs={{8,16},{16,8},{9,17},{17,9},{10,18},{18,10},{11,19},{19,11},{12,20... | collective-permute-start | bytes 1179656 | tf_op jit(solution)/shard_map/ppermute | solution.py:60
  228.7 11.3 %collective-permute-start.50 = (bf16[1536,128]{1,0:T(8,128)(2,1)S(1)}, bf16[1536,128]{1,0:T(8,128)(2,1)S(1)}, u32[]{:S(2)}, u32[]{:S(2)}) collective-permute-start(bf16[1536,128]{1,0:T(8,128)(2,1)S(1)} %add_convert_fusion.13), channel_id=1, source_target_pairs={{8,0},{16,24},{9,1},{17,25},{10,2},{18,26},{11,3},{19,27},{12,4},{... | collective-permute-start | bytes 1179656 | tf_op jit(solution)/shard_map/ppermute | solution.py:52
  235.9 9.7 %collective-permute-start.51 = (bf16[1536,128]{1,0:T(8,128)(2,1)S(1)}, bf16[1536,128]{1,0:T(8,128)(2,1)S(1)}, u32[]{:S(2)}, u32[]{:S(2)}) collective-permute-start(bf16[1536,128]{1,0:T(8,128)(2,1)S(1)} %add_convert_fusion.12), channel_id=1, source_target_pairs={{8,0},{16,24},{9,1},{17,25},{10,2},{18,26},{11,3},{19,27},{12,4},{... | collective-permute-start | bytes 1179656 | tf_op jit(solution)/shard_map/ppermute | solution.py:52
  (17 other events, 191.9 us)

commit v5 on v4

--- a/solution.py
+++ b/solution.py
@@ -89,6 +89,17 @@
             jnp.dot(block, weight, preferred_element_type=f32).astype(bf16)
         )
 
+    def at(h, q, x):
+        return (h * group + q) * 2 + x
+
+    ring_pairs, cross_pairs = [], []
+    for q in range(group):
+        ring_pairs += [(at(x, q, x), at(x, q, 1 - x)) for x in (0, 1)]
+        ring_pairs += [(at(1 - x, q, x), at(x, q, x)) for x in (0, 1)]
+        cross_pairs += [(at(1 - x, q, x), at(x, q, 1 - x)) for x in (0, 1)]
+    inward_pairs = [(at(1 - x, q, x), at(1 - x, q, 1 - x)) for q in range(group) for x in (0, 1)]
+    outward_pairs = [(at(x, q, x), at(x, q, 1 - x)) for q in range(group) for x in (0, 1)]
+
     near_blocks = [context] + [swap(context, "fsdp", r) for r in range(1, group)]
     slices = [
         [lax.dynamic_slice_in_dim(array, (low ^ r) * cols, cols, axis=1) for r in range(group)]
@@ -102,12 +113,13 @@
     ]
     held = together(far_pieces[0], *near_blocks[1:], *moved[0], *moved[1])
     far_pieces[0] = held[0]
-    near_blocks = [context] + list(held[1:group])
+    near_blocks = [later] + list(held[1:group])
     residual_parts, cotangent_parts = held[group : 2 * group], held[2 * group :]
     far_pieces = [far_pieces] + [
         [swap(piece, "fsdp", r) for piece in far_pieces] for r in range(1, group)
     ]
     far_outs, near_out = [], [[None] * pieces for r in range(group)]
+    near_came = {}
     last = None
     for r in range(group):
         for p in range(pieces):
@@ -121,25 +133,21 @@
             far_outs.append(swap(both[:rows], "fsdp", group))
             near_out[beside][p] = both[rows:]
             last = (beside, p)
+        whole = jnp.concatenate(near_out[beside], axis=0)
+        near_came[beside] = lax.ppermute(whole, ("fsdp", "tp"), inward_pairs)
+    passed = [lax.ppermute(out, ("fsdp", "tp"), outward_pairs) for out in far_outs]
 
     gain_part = lax.dynamic_slice_in_dim(gain, t * (width // 2) + low * cols, cols).astype(f32)
 
-    keeps, arrivals = [], []
-    for r in range(group):
-        for p in range(pieces):
-            far_out, own_out = far_outs[r * pieces + p], near_out[r][p]
-            if keeps:
-                far_out, own_out, keeps[-1] = together(far_out, own_out, keeps[-1])
-            else:
-                far_out, own_out = together(far_out, own_out)
-            keeps.append(jnp.where(near, own_out, far_out))
-            arrivals.append(swap(jnp.where(near, far_out, own_out), "tp", 1))
     hidden, weighted, sums = [], [], []
-    for k, (keep, came) in enumerate(zip(keeps, arrivals)):
-        span = slice(k % pieces * rows, (k % pieces + 1) * rows)
-        res, cot = residual_parts[k // pieces], cotangent_parts[k // pieces]
+    for k in range(group * pieces):
+        r, p = k // pieces, k % pieces
+        span = slice(p * rows, (p + 1) * rows)
+        res, cot, came = residual_parts[r], cotangent_parts[r], passed[k]
         if sums:
             came, sums[-1] = together(came, sums[-1])
+        keep = jnp.where(near, near_out[r][p], far_outs[k])
+        came = jnp.where(near, near_came[r][span], came)
         h = res[span].astype(f32) + keep.astype(f32) + came.astype(f32)
         w = gain_part[None, :] * cot[span].astype(f32)
         hidden.append(h)
@@ -162,21 +170,12 @@
     context_all = jnp.concatenate(tokens, axis=0)
     narrow = 128
     units = cols // narrow
-    widths = [1, 2]
+    widths = [1, 3]
     while sum(widths) < units:
-        widths.append(min(2 + len(widths), units - sum(widths)))
-    def at(h, q, x):
-        return (h * group + q) * 2 + x
-
-    ring_pairs, cross_pairs = [], []
-    for q in range(group):
-        ring_pairs += [(at(x, q, x), at(x, q, 1 - x)) for x in (0, 1)]
-        ring_pairs += [(at(1 - x, q, x), at(x, q, x)) for x in (0, 1)]
-        cross_pairs += [(at(1 - x, q, x), at(x, q, 1 - x)) for x in (0, 1)]
-
+        widths.append(min(4, units - sum(widths)))
     islands = lax.axis_size("island")
     line = IslandLine(units)
-    parts, rings, pseudos = [], [], []
+    parts, rings = [], []
 
     def add_parts(c, after):
         cols_at = slice(sum(widths[:c]) * narrow, sum(widths[: c + 1]) * narrow)
@@ -191,8 +190,8 @@
         if c < 3:
             if c == 1:
                 d_local, rings[0] = together(d_local, rings[0])
-            elif c == 2:
-                d_local, pseudos[0] = together(d_local, pseudos[0])
+            elif c == 2 and after in line.edge:
+                d_local, line.edge[after] = together(d_local, line.edge[after])
             rings.append(lax.ppermute(d_local, ("fsdp", "tp"), ring_pairs))
             cross = lax.ppermute(d_local, ("fsdp", "tp"), cross_pairs)
             blocks = (d_local, cross)
@@ -212,42 +211,41 @@
             d_near = jnp.where(near, blocks[0], rings[c])
             d_far = jnp.where(near, rings[c], blocks[1])
         d_all = jnp.concatenate([d_near, d_far], axis=0)
-        grad = lax.dot_general(
-            context_all, d_all, (((0,), (0,)), ((), ())), preferred_element_type=f32
-        ) / (tok_rows * fsdp_count)
-        first = first_moment[0, :, cols_at].astype(f32)
-        second = second_moment[0, :, cols_at].astype(f32)
-        m_new = beta_one * first + (1.0 - beta_one) * grad
-        v_new = beta_two * second + (1.0 - beta_two) * grad * grad
-        update = m_new / bias_one / (
-            jnp.sqrt(v_new / bias_two) + adam_eps
-        ) + decay_rate * weight[:, cols_at].astype(f32)
-        pseudos.append(lax.optimization_barrier(update.astype(bf16)))
-
-    def slice_pseudo(c):
-        parts.extend(pseudos[c][:, u * narrow : (u + 1) * narrow] for u in range(widths[c]))
-
-    early = min(3, len(widths))
+        cuts = list(range(0, widths[c], 2)) if widths[c] % 2 == 0 else [0] + list(range(1, widths[c], 2))
+        for lo, hi in zip(cuts, cuts[1:] + [widths[c]]):
+            at_cols = slice(cols_at.start + lo * narrow, cols_at.start + hi * narrow)
+            grad = lax.dot_general(
+                context_all,
+                lax.optimization_barrier(d_all[:, lo * narrow : hi * narrow]),
+                (((0,), (0,)), ((), ())),
+                preferred_element_type=f32,
+            ) / (tok_rows * fsdp_count)
+            first = first_moment[0, :, at_cols].astype(f32)
+            second = second_moment[0, :, at_cols].astype(f32)
+            m_new = beta_one * first + (1.0 - beta_one) * grad
+            v_new = beta_two * second + (1.0 - beta_two) * grad * grad
+            update = m_new / bias_one / (
+                jnp.sqrt(v_new / bias_two) + adam_eps
+            ) + decay_rate * weight[:, at_cols].astype(f32)
+            pseudo = lax.optimization_barrier(update.astype(bf16))
+            parts.extend(pseudo[:, u * narrow : (u + 1) * narrow] for u in range(hi - lo))
+
     first, second = add_parts(0, None), add_parts(1, None)
     add_pseudo(0, *first)
-    third = add_parts(2, None)
     add_pseudo(1, *second)
-    add_pseudo(2, *third)
-    for c in range(early):
-        slice_pseudo(c)
     if islands == 4:
         line.part.update(enumerate(parts))
         for s in range(2):
             line.send_outer(s)
         for s in range(units + 3):
-            if early < len(widths) and s == 2:
-                for c in range(early, len(widths)):
-                    add_pseudo(c, *add_parts(c, 1))
-                    slice_pseudo(c)
-                line.part.update(enumerate(parts))
+            for c in {0: [2], 3: range(3, len(widths))}.get(s, []):
+                add_pseudo(c, *add_parts(c, max(s - 1, 0)))
+            line.part.update(enumerate(parts))
             line.step(s)
         sums = [line.totals[k] for k in range(units)]
     else:
+        for c in range(2, len(widths)):
+            add_pseudo(c, *add_parts(c, None))
         sums = [lax.psum(part, "island") for part in parts]
     momentum_out, step_out = [], []
     for k, total in enumerate(sums):

time: 253 us -> 277 us (1.095)
  waiting for transfers between devices: 106 us -> 119 us
  starting transfers between devices: 92.2 us -> 97.6 us
  matrix products: 24.6 us -> 28.3 us
    ppermute x19 -> x15, waiting for transfers between devices: 64.2 us -> 44.6 us  [swap(): return lax.ppermute(value, axis, [(i, i ^ bit) for i in range(count)])]
    ppermute x0 -> x6, waiting for transfers between devices: none -> 17.3 us  [the longest x4 17.3 us: body(): lax.ppermute(out, ('fsdp', 'tp'), outward_pairs)]
    ppermute x0 -> x6, starting transfers between devices: none -> 9.87 us  [the longest x4 5.13 us: body(): lax.ppermute(out, ('fsdp', 'tp'), outward_pairs)]
    ppermute x15, waiting for transfers between devices: 40.4 us -> 48.8 us  [send_outer(): self.edge[s] = lax.ppermute(payload, 'island', pairs)]
    ppermute x3, waiting for transfers between devices: 0.63 us -> 4.95 us  [add_parts(): rings.append(lax.ppermute(d_local, ('fsdp', 'tp'), ring_pairs))]
    dot_general x4 -> x7, matrix products: 15.4 us -> 19.2 us  [add_pseudo(): lax.dot_general(context_all, lax.optimization_barrier(d_all[:, lo * narro...]
    ppermute x3, starting transfers between devices: 3.15 us -> 0.12 us  [add_parts(): rings.append(lax.ppermute(d_local, ('fsdp', 'tp'), ring_pairs))]
    ppermute x19 -> x15, starting transfers between devices: 11.7 us -> 8.91 us  [swap(): return lax.ppermute(value, axis, [(i, i ^ bit) for i in range(count)])]
  transfers between devices with their start and end apart: 52 -> 54, of which waited for: 25 -> 28; matrix products, arithmetic and copies ran while one was open for 17% -> 16% of each run, Pallas kernels for 0% -> 0%
where the time goes in v5:
time: 277 us; the launch traced here: 275 us
  waiting for transfers between devices  119 us (43%)
  starting transfers between devices  97.6 us (35%)
  matrix products  28.3 us (10%)
  other arithmetic  15.9 us (6%)
  local copies, waits for them, and re-layouts  12.2 us (4%)
    ppermute x15, starting transfers between devices, send_outer(): self.edge[s] = lax.ppermute(payload, 'island', pairs)  59.6 us
    ppermute x15, waiting for transfers between devices, send_outer(): self.edge[s] = lax.ppermute(payload, 'island', pairs)  48.8 us
    ppermute x15, waiting for transfers between devices, swap(): return lax.ppermute(value, axis, [(i, i ^ bit) for i in range(count)])  44.6 us
    dot_general x7, matrix products, add_pseudo(): lax.dot_general(context_all, lax.optimization_barrier(d_all[:, lo * narro...  19.2 us
    ppermute x4, waiting for transfers between devices, body(): lax.ppermute(out, ('fsdp', 'tp'), outward_pairs)  17.3 us
    ppermute x3, starting transfers between devices, add_parts(): cross = lax.ppermute(d_local, ('fsdp', 'tp'), cross_pairs)  10.4 us
    dot_general x4, matrix products, project(): jnp.dot(block, weight, preferred_element_type=f32).astype(bf16)  9.11 us
    ppermute x15, starting transfers between devices, swap(): return lax.ppermute(value, axis, [(i, i ^ bit) for i in range(count)])  8.91 us
  transfers between devices with their start and end apart: 54, of which 28 were waited for; matrix products, arithmetic and copies ran while one was open for 16% of the time, Pallas kernels for 0%

profile of v5, /device:TPU:2, one launch (start us, length us, event | category | flops | bytes accessed | tf_op | source)
XLA Modules:
  0.0 274.6 jit_solution(15344588551225593465)
XLA Ops:
  0.7 3.3 %constant_dynamic-slice_fusion = (bf16[256,1536]{1,0:T(8,128)(2,1)}, bf16[256,1536]{1,0:T(8,128)(2,1)S(1)}, bf16[256,1536]{1,0:T(8,128)(2,1)S(1)}, bf16[256,1536]{1,0:T(8,128)(2,1)}) fusion(bf16[256,3072]{1,0:T(8,128)(2,1)} %param.10, s32[]{:T(128)S(6)} %select_n.193, s32[]{:T(128)S(6)} %select_n.192, bf16[256,3072]{1,0:T(8,128)(2,1)} %param.9), kind=kLoop, calls=%fused_computation.313 | loop fusion | bytes 6291464 | tf_op jit(solution)/shard_map/dynamic_slice | solution.py:105
  9.1 8.5 %collective-permute-done.4 = bf16[128,1536]{1,0:T(8,128)(2,1)S(1)} collective-permute-done((bf16[128,1536]{1,0:T(8,128)(2,1)}, bf16[128,1536]{1,0:T(8,128)(2,1)S(1)}, u32[]{:S(2)}, u32[]{:S(2)}) %collective-permute-start.4) | collective-permute-done | bytes 393248 | tf_op jit(solution)/shard_map/ppermute | solution.py:27
  17.7 8.1 %collective-permute-done = bf16[128,1536]{1,0:T(8,128)(2,1)} collective-permute-done((bf16[128,1536]{1,0:T(8,128)(2,1)}, bf16[128,1536]{1,0:T(8,128)(2,1)}, u32[]{:S(2)}, u32[]{:S(2)}) %collective-permute-start) | collective-permute-done | bytes 393248 | tf_op jit(solution)/shard_map/ppermute | solution.py:27
  25.9 4.0 %convolution_convert_fusion.3 = bf16[256,1536]{1,0:T(8,128)(2,1)S(1)} fusion(bf16[1536,1536]{1,0:T(8,128)(2,1)} %param.12, bf16[128,1536]{1,0:T(8,128)(2,1)S(1)} %get-tuple-element.272, bf16[128,1536]{1,0:T(8,128)(2,1)} %collective-permute-done), kind=kOutput, calls=%fused_computation.3 | convolution fusion | flops 1209925632 | bytes 6291456 | tf_op jit(solution)/shard_map/dot_general | solution.py:89
  34.5 2.4 convolution_convert_fusion
  37.0 2.5 collective-permute-start.10
  44.8 7.0 %collective-permute-done.7 = bf16[128,1536]{1,0:T(8,128)(2,1)S(1)} collective-permute-done((bf16[128,1536]{1,0:T(8,128)(2,1)S(1)}, bf16[128,1536]{1,0:T(8,128)(2,1)S(1)}, u32[]{:S(2)}, u32[]{:S(2)}) %collective-permute-start.7) | collective-permute-done | bytes 393248 | tf_op jit(solution)/shard_map/ppermute | solution.py:27
  51.8 2.2 collective-permute-start.16
  54.1 6.2 %collective-permute-done.14 = bf16[128,1536]{1,0:T(8,128)(2,1)S(1)} collective-permute-done((bf16[128,1536]{1,0:T(8,128)(2,1)S(1)}, bf16[128,1536]{1,0:T(8,128)(2,1)S(1)}, u32[]{:S(2)}, u32[]{:S(2)}) %collective-permute-start.14) | collective-permute-done | bytes 393248 | tf_op jit(solution)/shard_map/ppermute | solution.py:27
  61.5 6.7 %collective-permute-done.12 = bf16[128,1536]{1,0:T(8,128)(2,1)S(1)} collective-permute-done((bf16[128,1536]{1,0:T(8,128)(2,1)S(1)}, bf16[128,1536]{1,0:T(8,128)(2,1)S(1)}, u32[]{:S(2)}, u32[]{:S(2)}) %collective-permute-start.12) | collective-permute-done | bytes 393248 | tf_op jit(solution)/shard_map/ppermute | solution.py:27
  73.0 16.3 %collective-permute-done.13 = bf16[128,1536]{1,0:T(8,128)(2,1)S(1)} collective-permute-done((bf16[128,1536]{1,0:T(8,128)(2,1)S(1)}, bf16[128,1536]{1,0:T(8,128)(2,1)S(1)}, u32[]{:S(2)}, u32[]{:S(2)}) %collective-permute-start.13) | collective-permute-done | bytes 393248 | tf_op jit(solution)/shard_map/ppermute | solution.py:138
  94.1 3.6 %collective-permute-done.18 = f32[2,512]{1,0:T(2,128)S(1)} collective-permute-done((f32[2,512]{1,0:T(2,128)S(1)}, f32[2,512]{1,0:T(2,128)S(1)}, u32[]{:S(2)}, u32[]{:S(2)}) %collective-permute-start.18) | collective-permute-done | bytes 4128 | tf_op jit(solution)/shard_map/ppermute | solution.py:27
  98.7 3.4 %collective-permute-start.22 = (bf16[512,128]{1,0:T(8,128)(2,1)S(1)}, bf16[512,128]{1,0:T(8,128)(2,1)S(1)}, u32[]{:S(2)}, u32[]{:S(2)}) collective-permute-start(bf16[512,128]{1,0:T(8,128)(2,1)S(1)} %pad_maximum_fusion.9), channel_id=1, source_target_pairs={{4,1},{1,4},{6,3},{3,6},{12,9},{9,12},{14,11},{11,14},{20,17},{17,... | collective-permute-start | bytes 393224 | tf_op jit(solution)/shard_map/ppermute | solution.py:196
  103.7 3.7 %collective-permute-start.21 = (bf16[512,384]{1,0:T(8,128)(2,1)S(1)}, bf16[512,384]{1,0:T(8,128)(2,1)S(1)}, u32[]{:S(2)}, u32[]{:S(2)}) collective-permute-start(bf16[512,384]{1,0:T(8,128)(2,1)S(1)} %pad_maximum_fusion.6), channel_id=1, source_target_pairs={{4,1},{1,4},{6,3},{3,6},{12,9},{9,12},{14,11},{11,14},{20,17},{17,... | collective-permute-start | bytes 1179656 | tf_op jit(solution)/shard_map/ppermute | solution.py:196
  108.5 4.1 %collective-permute-done.20 = bf16[512,384]{1,0:T(8,128)(2,1)S(1)} collective-permute-done((bf16[512,384]{1,0:T(8,128)(2,1)S(1)}, bf16[512,384]{1,0:T(8,128)(2,1)S(1)}, u32[]{:S(2)}, u32[]{:S(2)}) %collective-permute-start.20) | collective-permute-done | bytes 393248 | tf_op jit(solution)/shard_map/ppermute | solution.py:195
  112.6 3.1 %collective-permute-done.21 = bf16[512,384]{1,0:T(8,128)(2,1)S(1)} collective-permute-done((bf16[512,384]{1,0:T(8,128)(2,1)S(1)}, bf16[512,384]{1,0:T(8,128)(2,1)S(1)}, u32[]{:S(2)}, u32[]{:S(2)}) %collective-permute-start.21) | collective-permute-done | bytes 393248 | tf_op jit(solution)/shard_map/ppermute | solution.py:196
  118.0 3.5 %collective-permute-start.23 = (bf16[1536,128]{1,0:T(8,128)(2,1)S(1)}, bf16[1536,128]{1,0:T(8,128)(2,1)S(1)}, u32[]{:S(2)}, u32[]{:S(2)}) collective-permute-start(bf16[1536,128]{1,0:T(8,128)(2,1)S(1)} %get-tuple-element.241), channel_id=1, source_target_pairs={{0,8},{24,16},{1,9},{25,17},{2,10},{26,18},{3,11},{27,19},{4,12},{... | collective-permute-start | bytes 1179656 | tf_op jit(solution)/shard_map/ppermute | solution.py:52
  122.8 2.2 fusion.30
  126.3 4.7 %collective-permute-done.23 = bf16[1536,128]{1,0:T(8,128)(2,1)S(1)} collective-permute-done((bf16[1536,128]{1,0:T(8,128)(2,1)S(1)}, bf16[1536,128]{1,0:T(8,128)(2,1)S(1)}, u32[]{:S(2)}, u32[]{:S(2)}) %collective-permute-start.23) | collective-permute-done | bytes 393248 | tf_op jit(solution)/shard_map/ppermute | solution.py:52
  131.0 3.3 %collective-permute-start.28 = (bf16[512,512]{1,0:T(8,128)(2,1)S(1)}, bf16[512,512]{1,0:T(8,128)(2,1)S(1)}, u32[]{:S(2)}, u32[]{:S(2)}) collective-permute-start(bf16[512,512]{1,0:T(8,128)(2,1)S(1)} %pad_maximum_fusion.4), channel_id=1, source_target_pairs={{4,1},{1,4},{6,3},{3,6},{12,9},{9,12},{14,11},{11,14},{20,17},{17,... | collective-permute-start | bytes 1572872 | tf_op jit(solution)/shard_map/ppermute | solution.py:196
  135.2 4.3 %collective-permute-done.25 = bf16[1536,128]{1,0:T(8,128)(2,1)S(1)} collective-permute-done((bf16[1536,128]{1,0:T(8,128)(2,1)S(1)}, bf16[1536,128]{1,0:T(8,128)(2,1)S(1)}, u32[]{:S(2)}, u32[]{:S(2)}) %collective-permute-start.25) | collective-permute-done | bytes 393248 | tf_op jit(solution)/shard_map/ppermute | solution.py:52
  140.4 3.6 %collective-permute-done.30 = bf16[1536,128]{1,0:T(8,128)(2,1)S(1)} collective-permute-done((bf16[1536,128]{1,0:T(8,128)(2,1)S(1)}, bf16[1536,128]{1,0:T(8,128)(2,1)S(1)}, u32[]{:S(2)}, u32[]{:S(2)}) %collective-permute-start.30) | collective-permute-done | bytes 393248 | tf_op jit(solution)/shard_map/ppermute | solution.py:52
  144.2 10.9 %collective-permute-start.26 = (bf16[1536,128]{1,0:T(8,128)(2,1)S(1)}, bf16[1536,128]{1,0:T(8,128)(2,1)S(1)}, u32[]{:S(2)}, u32[]{:S(2)}) collective-permute-start(bf16[1536,128]{1,0:T(8,128)(2,1)S(1)} %fusion.88), channel_id=1, source_target_pairs={{0,8},{24,16},{8,0},{16,24},{1,9},{25,17},{9,1},{17,25},{2,10},{26... | collective-permute-start | bytes 1179656 | tf_op jit(solution)/shard_map/ppermute | solution.py:52
  156.3 2.2 collective-permute-start.38
  158.5 2.2 fusion.159
  160.7 2.2 fusion.158
  162.8 2.8 %collective-permute-done.38 = bf16[512,512]{1,0:T(8,128)(2,1)S(1)} collective-permute-done((bf16[512,512]{1,0:T(8,128)(2,1)S(1)}, bf16[512,512]{1,0:T(8,128)(2,1)S(1)}, u32[]{:S(2)}, u32[]{:S(2)}) %collective-permute-start.38) | collective-permute-done | bytes 524320 | tf_op jit(solution)/shard_map/ppermute | solution.py:27
  165.7 2.2 fusion.160
  167.9 7.5 %fusion.34 = (bf16[1536,256]{1,0:T(8,128)(2,1)S(1)}, bf16[1536,256]{1,0:T(8,128)(2,1)S(1)}, bf16[1536,256]{1,0:T(8,128)(2,1)S(1)}, bf16[1536,256]{1,0:T(8,128)(2,1)S(1)}) fusion(bf16[1536,1536]{1,0:T(8,128)(2,1)S(1)} %bitcast.205, bf16[1,1536,1536]{2,1,0:T(8,128)(2,1)S(1)} %bitcast.207, bf16[1,1536,1536]{2,1,0:T(8,128)(2,1)S(1)} %bitcast.209, ...), kind=kOutput, calls=%fused_computation.48 | convolution fusion | flops 833617920 | bytes 20971520 | tf_op jit(solution)/shard_map/dot_general | solution.py:217
  175.5 8.0 %collective-permute-start.32 = (bf16[1536,128]{1,0:T(8,128)(2,1)S(1)}, bf16[1536,128]{1,0:T(8,128)(2,1)S(1)}, u32[]{:S(2)}, u32[]{:S(2)}) collective-permute-start(bf16[1536,128]{1,0:T(8,128)(2,1)S(1)} %fusion.89), channel_id=1, source_target_pairs={{0,8},{24,16},{8,0},{16,24},{1,9},{25,17},{9,1},{17,25},{2,10},{26... | collective-permute-start | bytes 1179656 | tf_op jit(solution)/shard_map/ppermute | solution.py:52
  184.5 2.9 %collective-permute-start.34 = (bf16[1536,128]{1,0:T(8,128)(2,1)S(1)}, bf16[1536,128]{1,0:T(8,128)(2,1)S(1)}, u32[]{:S(2)}, u32[]{:S(2)}) collective-permute-start(bf16[1536,128]{1,0:T(8,128)(2,1)S(1)} %fusion.90), channel_id=1, source_target_pairs={{0,8},{24,16},{8,0},{16,24},{1,9},{25,17},{9,1},{17,25},{2,10},{26... | collective-permute-start | bytes 1179656 | tf_op jit(solution)/shard_map/ppermute | solution.py:52
  187.8 5.3 %collective-permute-done.32 = bf16[1536,128]{1,0:T(8,128)(2,1)S(1)} collective-permute-done((bf16[1536,128]{1,0:T(8,128)(2,1)S(1)}, bf16[1536,128]{1,0:T(8,128)(2,1)S(1)}, u32[]{:S(2)}, u32[]{:S(2)}) %collective-permute-start.32) | collective-permute-done | bytes 393248 | tf_op jit(solution)/shard_map/ppermute | solution.py:52
  194.1 3.7 %collective-permute-start.36 = (bf16[1536,128]{1,0:T(8,128)(2,1)S(1)}, bf16[1536,128]{1,0:T(8,128)(2,1)S(1)}, u32[]{:S(2)}, u32[]{:S(2)}) collective-permute-start(bf16[1536,128]{1,0:T(8,128)(2,1)S(1)} %fusion.91), channel_id=1, source_target_pairs={{0,8},{24,16},{8,0},{16,24},{1,9},{25,17},{9,1},{17,25},{2,10},{26... | collective-permute-start | bytes 1179656 | tf_op jit(solution)/shard_map/ppermute | solution.py:52
  197.8 3.8 %collective-permute-done.34 = bf16[1536,128]{1,0:T(8,128)(2,1)S(1)} collective-permute-done((bf16[1536,128]{1,0:T(8,128)(2,1)S(1)}, bf16[1536,128]{1,0:T(8,128)(2,1)S(1)}, u32[]{:S(2)}, u32[]{:S(2)}) %collective-permute-start.34) | collective-permute-done | bytes 393248 | tf_op jit(solution)/shard_map/ppermute | solution.py:52
  203.0 4.6 %collective-permute-start.40 = (bf16[1536,128]{1,0:T(8,128)(2,1)S(1)}, bf16[1536,128]{1,0:T(8,128)(2,1)S(1)}, u32[]{:S(2)}, u32[]{:S(2)}) collective-permute-start(bf16[1536,128]{1,0:T(8,128)(2,1)S(1)} %fusion.92), channel_id=1, source_target_pairs={{0,8},{24,16},{8,0},{16,24},{1,9},{25,17},{9,1},{17,25},{2,10},{26... | collective-permute-start | bytes 1179656 | tf_op jit(solution)/shard_map/ppermute | solution.py:52
  207.6 2.4 collective-permute-done.36
  210.9 5.1 %collective-permute-start.42 = (bf16[1536,128]{1,0:T(8,128)(2,1)S(1)}, bf16[1536,128]{1,0:T(8,128)(2,1)S(1)}, u32[]{:S(2)}, u32[]{:S(2)}) collective-permute-start(bf16[1536,128]{1,0:T(8,128)(2,1)S(1)} %fusion.93), channel_id=1, source_target_pairs={{0,8},{24,16},{8,0},{16,24},{1,9},{25,17},{9,1},{17,25},{2,10},{26... | collective-permute-start | bytes 1179656 | tf_op jit(solution)/shard_map/ppermute | solution.py:52
  219.4 5.1 %collective-permute-start.44 = (bf16[1536,128]{1,0:T(8,128)(2,1)S(1)}, bf16[1536,128]{1,0:T(8,128)(2,1)S(1)}, u32[]{:S(2)}, u32[]{:S(2)}) collective-permute-start(bf16[1536,128]{1,0:T(8,128)(2,1)S(1)} %fusion.94), channel_id=1, source_target_pairs={{0,8},{24,16},{8,0},{16,24},{1,9},{25,17},{9,1},{17,25},{2,10},{26... | collective-permute-start | bytes 1179656 | tf_op jit(solution)/shard_map/ppermute | solution.py:52
  224.4 2.4 collective-permute-done.42
  228.3 4.6 %collective-permute-start.46 = (bf16[1536,128]{1,0:T(8,128)(2,1)S(1)}, bf16[1536,128]{1,0:T(8,128)(2,1)S(1)}, u32[]{:S(2)}, u32[]{:S(2)}) collective-permute-start(bf16[1536,128]{1,0:T(8,128)(2,1)S(1)} %fusion.95), channel_id=1, source_target_pairs={{0,8},{24,16},{8,0},{16,24},{1,9},{25,17},{9,1},{17,25},{2,10},{26... | collective-permute-start | bytes 1179656 | tf_op jit(solution)/shard_map/ppermute | solution.py:52
  232.9 2.4 collective-permute-done.44
  236.5 4.8 %collective-permute-start.48 = (bf16[1536,128]{1,0:T(8,128)(2,1)S(1)}, bf16[1536,128]{1,0:T(8,128)(2,1)S(1)}, u32[]{:S(2)}, u32[]{:S(2)}) collective-permute-start(bf16[1536,128]{1,0:T(8,128)(2,1)S(1)} %fusion.96), channel_id=1, source_target_pairs={{0,8},{24,16},{8,0},{16,24},{1,9},{25,17},{9,1},{17,25},{2,10},{26... | collective-permute-start | bytes 1179656 | tf_op jit(solution)/shard_map/ppermute | solution.py:52
  245.9 5.7 %collective-permute-done.48 = bf16[1536,128]{1,0:T(8,128)(2,1)S(1)} collective-permute-done((bf16[1536,128]{1,0:T(8,128)(2,1)S(1)}, bf16[1536,128]{1,0:T(8,128)(2,1)S(1)}, u32[]{:S(2)}, u32[]{:S(2)}) %collective-permute-start.48) | collective-permute-done | bytes 393248 | tf_op jit(solution)/shard_map/ppermute | solution.py:52
  254.3 3.2 %collective-permute-done.50 = bf16[1536,128]{1,0:T(8,128)(2,1)S(1)} collective-permute-done((bf16[1536,128]{1,0:T(8,128)(2,1)S(1)}, bf16[1536,128]{1,0:T(8,128)(2,1)S(1)}, u32[]{:S(2)}, u32[]{:S(2)}) %collective-permute-start.50) | collective-permute-done | bytes 393248 | tf_op jit(solution)/shard_map/ppermute | solution.py:52
  259.8 2.9 %collective-permute-done.52 = bf16[1536,128]{1,0:T(8,128)(2,1)S(1)} collective-permute-done((bf16[1536,128]{1,0:T(8,128)(2,1)S(1)}, bf16[1536,128]{1,0:T(8,128)(2,1)S(1)}, u32[]{:S(2)}, u32[]{:S(2)}) %collective-permute-start.52) | collective-permute-done | bytes 393248 | tf_op jit(solution)/shard_map/ppermute | solution.py:52
  262.7 5.4 %collective-permute-done.53 = bf16[1536,128]{1,0:T(8,128)(2,1)S(1)} collective-permute-done((bf16[1536,128]{1,0:T(8,128)(2,1)S(1)}, bf16[1536,128]{1,0:T(8,128)(2,1)S(1)}, u32[]{:S(2)}, u32[]{:S(2)}) %collective-permute-start.53) | collective-permute-done | bytes 393248 | tf_op jit(solution)/shard_map/ppermute | solution.py:52
  269.0 3.4 %copy-done.2 = f32[1536,1536]{1,0:T(8,128)} copy-done((f32[1536,1536]{1,0:T(8,128)}, f32[1536,1536]{1,0:T(8,128)S(1)}, u32[]{:S(2)}) %copy-start.2) | copy-done | bytes 9437208
  272.4 2.2 copy-done.3
  (207 shorter events, 58.7 us)
Async XLA Ops:
  0.6 25.1 %collective-permute-start.1 = (bf16[256,1536]{1,0:T(8,128)(2,1)}, bf16[256,1536]{1,0:T(8,128)(2,1)S(1)}, u32[]{:S(2)}, u32[]{:S(2)}) collective-permute-start(bf16[256,1536]{1,0:T(8,128)(2,1)} %param.8), channel_id=1, source_target_pairs={{0,2},{2,0},{4,6},{6,4},{1,3},{3,1},{5,7},{7,5},{8,10},{10,8},{12,... | collective-permute-start | bytes 2359304 | tf_op jit(solution)/shard_map/ppermute | solution.py:27
  4.1 21.7 %collective-permute-start.2 = (bf16[256,1536]{1,0:T(8,128)(2,1)}, bf16[256,1536]{1,0:T(8,128)(2,1)}, u32[]{:S(2)}, u32[]{:S(2)}) collective-permute-start(bf16[256,1536]{1,0:T(8,128)(2,1)} %get-tuple-element.115), channel_id=1, source_target_pairs={{0,2},{2,0},{4,6},{6,4},{1,3},{3,1},{5,7},{7,5},{8,10},{10,8},{12,... | collective-permute-start | bytes 2359304 | tf_op jit(solution)/shard_map/ppermute | solution.py:27
  4.5 21.2 %collective-permute-start.3 = (bf16[256,1536]{1,0:T(8,128)(2,1)}, bf16[256,1536]{1,0:T(8,128)(2,1)}, u32[]{:S(2)}, u32[]{:S(2)}) collective-permute-start(bf16[256,1536]{1,0:T(8,128)(2,1)} %get-tuple-element.117), channel_id=1, source_target_pairs={{0,2},{2,0},{4,6},{6,4},{1,3},{3,1},{5,7},{7,5},{8,10},{10,8},{12,... | collective-permute-start | bytes 2359304 | tf_op jit(solution)/shard_map/ppermute | solution.py:27
  5.5 12.1 %collective-permute-start.4 = (bf16[128,1536]{1,0:T(8,128)(2,1)}, bf16[128,1536]{1,0:T(8,128)(2,1)S(1)}, u32[]{:S(2)}, u32[]{:S(2)}) collective-permute-start(bf16[128,1536]{1,0:T(8,128)(2,1)} %get-tuple-element.275), channel_id=1, source_target_pairs={{0,4},{2,6},{4,0},{6,2},{1,5},{3,7},{5,1},{7,3},{8,12},{10,14},{12... | collective-permute-start | bytes 1179656 | tf_op jit(solution)/shard_map/ppermute | solution.py:27
  7.8 17.9 %collective-permute-start = (bf16[128,1536]{1,0:T(8,128)(2,1)}, bf16[128,1536]{1,0:T(8,128)(2,1)}, u32[]{:S(2)}, u32[]{:S(2)}) collective-permute-start(bf16[128,1536]{1,0:T(8,128)(2,1)} %slice.393), channel_id=1, source_target_pairs={{0,4},{2,6},{4,0},{6,2},{1,5},{3,7},{5,1},{7,3},{8,12},{10,14},{12... | collective-permute-start | bytes 1179656 | tf_op jit(solution)/shard_map/ppermute | solution.py:27
  17.7 16.9 %collective-permute-start.6 = (bf16[128,1536]{1,0:T(8,128)(2,1)S(1)}, bf16[128,1536]{1,0:T(8,128)(2,1)S(1)}, u32[]{:S(2)}, u32[]{:S(2)}) collective-permute-start(bf16[128,1536]{1,0:T(8,128)(2,1)S(1)} %collective-permute-done.4), channel_id=1, source_target_pairs={{0,2},{2,0},{4,6},{6,4},{1,3},{3,1},{5,7},{7,5},{8,10},{10,8},{12,... | collective-permute-start | bytes 1179656 | tf_op jit(solution)/shard_map/ppermute | solution.py:27
  25.8 7.3 %collective-permute-start.5 = (bf16[128,1536]{1,0:T(8,128)(2,1)}, bf16[128,1536]{1,0:T(8,128)(2,1)S(1)}, u32[]{:S(2)}, u32[]{:S(2)}) collective-permute-start(bf16[128,1536]{1,0:T(8,128)(2,1)} %collective-permute-done), channel_id=1, source_target_pairs={{0,2},{2,0},{4,6},{6,4},{1,3},{3,1},{5,7},{7,5},{8,10},{10,8},{12,... | collective-permute-start | bytes 1179656 | tf_op jit(solution)/shard_map/ppermute | solution.py:27
  31.4 12.0 %collective-permute-start.9 = (bf16[128,1536]{1,0:T(8,128)(2,1)S(1)}, bf16[128,1536]{1,0:T(8,128)(2,1)S(1)}, u32[]{:S(2)}, u32[]{:S(2)}) collective-permute-start(bf16[128,1536]{1,0:T(8,128)(2,1)S(1)} %get-tuple-element.266), channel_id=1, source_target_pairs={{0,4},{2,6},{4,0},{6,2},{1,5},{3,7},{5,1},{7,3},{8,12},{10,14},{12... | collective-permute-start | bytes 1179656 | tf_op jit(solution)/shard_map/ppermute | solution.py:27
  37.0 33.8 %collective-permute-start.10 = (bf16[256,1536]{1,0:T(8,128)(2,1)S(1)}, bf16[256,1536]{1,0:T(8,128)(2,1)S(1)}, u32[]{:S(2)}, u32[]{:S(2)}) collective-permute-start(bf16[256,1536]{1,0:T(8,128)(2,1)S(1)} %pad_maximum_fusion), channel_id=1, source_target_pairs={{4,5},{1,0},{6,7},{3,2},{12,13},{9,8},{14,15},{11,10},{20,21},{17,... | collective-permute-start | bytes 2359304 | tf_op jit(solution)/shard_map/ppermute | solution.py:137
  39.6 12.2 %collective-permute-start.7 = (bf16[128,1536]{1,0:T(8,128)(2,1)S(1)}, bf16[128,1536]{1,0:T(8,128)(2,1)S(1)}, u32[]{:S(2)}, u32[]{:S(2)}) collective-permute-start(bf16[128,1536]{1,0:T(8,128)(2,1)S(1)} %get-tuple-element.268), channel_id=1, source_target_pairs={{0,4},{2,6},{4,0},{6,2},{1,5},{3,7},{5,1},{7,3},{8,12},{10,14},{12... | collective-permute-start | bytes 1179656 | tf_op jit(solution)/shard_map/ppermute | solution.py:27
  40.7 19.6 %collective-permute-start.14 = (bf16[128,1536]{1,0:T(8,128)(2,1)S(1)}, bf16[128,1536]{1,0:T(8,128)(2,1)S(1)}, u32[]{:S(2)}, u32[]{:S(2)}) collective-permute-start(bf16[128,1536]{1,0:T(8,128)(2,1)S(1)} %get-tuple-element.265), channel_id=1, source_target_pairs={{0,4},{2,6},{4,0},{6,2},{1,5},{3,7},{5,1},{7,3},{8,12},{10,14},{12... | collective-permute-start | bytes 1179656 | tf_op jit(solution)/shard_map/ppermute | solution.py:27
  42.8 25.5 %collective-permute-start.12 = (bf16[128,1536]{1,0:T(8,128)(2,1)S(1)}, bf16[128,1536]{1,0:T(8,128)(2,1)S(1)}, u32[]{:S(2)}, u32[]{:S(2)}) collective-permute-start(bf16[128,1536]{1,0:T(8,128)(2,1)S(1)} %get-tuple-element.270), channel_id=1, source_target_pairs={{0,4},{2,6},{4,0},{6,2},{1,5},{3,7},{5,1},{7,3},{8,12},{10,14},{12... | collective-permute-start | bytes 1179656 | tf_op jit(solution)/shard_map/ppermute | solution.py:27
  43.4 26.2 %collective-permute-start.11 = (bf16[128,1536]{1,0:T(8,128)(2,1)S(1)}, bf16[128,1536]{1,0:T(8,128)(2,1)S(1)}, u32[]{:S(2)}, u32[]{:S(2)}) collective-permute-start(bf16[128,1536]{1,0:T(8,128)(2,1)S(1)} %collective-permute-done.9), channel_id=1, source_target_pairs={{0,1},{5,4},{2,3},{7,6},{8,9},{13,12},{10,11},{15,14},{16,17},{21,... | collective-permute-start | bytes 1179656 | tf_op jit(solution)/shard_map/ppermute | solution.py:138
  51.8 37.5 %collective-permute-start.16 = (bf16[256,1536]{1,0:T(8,128)(2,1)S(1)}, bf16[256,1536]{1,0:T(8,128)(2,1)S(1)}, u32[]{:S(2)}, u32[]{:S(2)}) collective-permute-start(bf16[256,1536]{1,0:T(8,128)(2,1)S(1)} %pad_maximum_fusion.1), channel_id=1, source_target_pairs={{4,5},{1,0},{6,7},{3,2},{12,13},{9,8},{14,15},{11,10},{20,21},{17,... | collective-permute-start | bytes 2359304 | tf_op jit(solution)/shard_map/ppermute | solution.py:137
  60.2 12.2 %collective-permute-start.8 = (bf16[128,1536]{1,0:T(8,128)(2,1)S(1)}, bf16[128,1536]{1,0:T(8,128)(2,1)S(1)}, u32[]{:S(2)}, u32[]{:S(2)}) collective-permute-start(bf16[128,1536]{1,0:T(8,128)(2,1)S(1)} %collective-permute-done.7), channel_id=1, source_target_pairs={{0,1},{5,4},{2,3},{7,6},{8,9},{13,12},{10,11},{15,14},{16,17},{21,... | collective-permute-start | bytes 1179656 | tf_op jit(solution)/shard_map/ppermute | solution.py:138
  68.3 22.7 %collective-permute-start.15 = (bf16[128,1536]{1,0:T(8,128)(2,1)S(1)}, bf16[128,1536]{1,0:T(8,128)(2,1)S(1)}, u32[]{:S(2)}, u32[]{:S(2)}) collective-permute-start(bf16[128,1536]{1,0:T(8,128)(2,1)S(1)} %collective-permute-done.14), channel_id=1, source_target_pairs={{0,1},{5,4},{2,3},{7,6},{8,9},{13,12},{10,11},{15,14},{16,17},{21,... | collective-permute-start | bytes 1179656 | tf_op jit(solution)/shard_map/ppermute | solution.py:138
  69.5 19.7 %collective-permute-start.13 = (bf16[128,1536]{1,0:T(8,128)(2,1)S(1)}, bf16[128,1536]{1,0:T(8,128)(2,1)S(1)}, u32[]{:S(2)}, u32[]{:S(2)}) collective-permute-start(bf16[128,1536]{1,0:T(8,128)(2,1)S(1)} %collective-permute-done.12), channel_id=1, source_target_pairs={{0,1},{5,4},{2,3},{7,6},{8,9},{13,12},{10,11},{15,14},{16,17},{21,... | collective-permute-start | bytes 1179656 | tf_op jit(solution)/shard_map/ppermute | solution.py:138
  98.7 8.7 %collective-permute-start.22 = (bf16[512,128]{1,0:T(8,128)(2,1)S(1)}, bf16[512,128]{1,0:T(8,128)(2,1)S(1)}, u32[]{:S(2)}, u32[]{:S(2)}) collective-permute-start(bf16[512,128]{1,0:T(8,128)(2,1)S(1)} %pad_maximum_fusion.9), channel_id=1, source_target_pairs={{4,1},{1,4},{6,3},{3,6},{12,9},{9,12},{14,11},{11,14},{20,17},{17,... | collective-permute-start | bytes 393224 | tf_op jit(solution)/shard_map/ppermute | solution.py:196
  103.7 9.0 %collective-permute-start.20 = (bf16[512,384]{1,0:T(8,128)(2,1)S(1)}, bf16[512,384]{1,0:T(8,128)(2,1)S(1)}, u32[]{:S(2)}, u32[]{:S(2)}) collective-permute-start(bf16[512,384]{1,0:T(8,128)(2,1)S(1)} %pad_maximum_fusion.6), channel_id=1, source_target_pairs={{0,1},{5,4},{4,0},{1,5},{2,3},{7,6},{6,2},{3,7},{8,9},{13,12},{12,... | collective-permute-start | bytes 1179656 | tf_op jit(solution)/shard_map/ppermute | solution.py:195
  103.7 12.0 %collective-permute-start.21 = (bf16[512,384]{1,0:T(8,128)(2,1)S(1)}, bf16[512,384]{1,0:T(8,128)(2,1)S(1)}, u32[]{:S(2)}, u32[]{:S(2)}) collective-permute-start(bf16[512,384]{1,0:T(8,128)(2,1)S(1)} %pad_maximum_fusion.6), channel_id=1, source_target_pairs={{4,1},{1,4},{6,3},{3,6},{12,9},{9,12},{14,11},{11,14},{20,17},{17,... | collective-permute-start | bytes 1179656 | tf_op jit(solution)/shard_map/ppermute | solution.py:196
  118.0 13.0 %collective-permute-start.23 = (bf16[1536,128]{1,0:T(8,128)(2,1)S(1)}, bf16[1536,128]{1,0:T(8,128)(2,1)S(1)}, u32[]{:S(2)}, u32[]{:S(2)}) collective-permute-start(bf16[1536,128]{1,0:T(8,128)(2,1)S(1)} %get-tuple-element.241), channel_id=1, source_target_pairs={{0,8},{24,16},{1,9},{25,17},{2,10},{26,18},{3,11},{27,19},{4,12},{... | collective-permute-start | bytes 1179656 | tf_op jit(solution)/shard_map/ppermute | solution.py:52
  121.5 18.0 %collective-permute-start.25 = (bf16[1536,128]{1,0:T(8,128)(2,1)S(1)}, bf16[1536,128]{1,0:T(8,128)(2,1)S(1)}, u32[]{:S(2)}, u32[]{:S(2)}) collective-permute-start(bf16[1536,128]{1,0:T(8,128)(2,1)S(1)} %get-tuple-element.240), channel_id=1, source_target_pairs={{0,8},{24,16},{1,9},{25,17},{2,10},{26,18},{3,11},{27,19},{4,12},{... | collective-permute-start | bytes 1179656 | tf_op jit(solution)/shard_map/ppermute | solution.py:52
  125.0 19.0 %collective-permute-start.30 = (bf16[1536,128]{1,0:T(8,128)(2,1)S(1)}, bf16[1536,128]{1,0:T(8,128)(2,1)S(1)}, u32[]{:S(2)}, u32[]{:S(2)}) collective-permute-start(bf16[1536,128]{1,0:T(8,128)(2,1)S(1)} %slice.560), channel_id=1, source_target_pairs={{0,8},{24,16},{1,9},{25,17},{2,10},{26,18},{3,11},{27,19},{4,12},{... | collective-permute-start | bytes 1179656 | tf_op jit(solution)/shard_map/ppermute | solution.py:52
  131.0 25.0 %collective-permute-start.27 = (bf16[512,512]{1,0:T(8,128)(2,1)S(1)}, bf16[512,512]{1,0:T(8,128)(2,1)S(1)}, u32[]{:S(2)}, u32[]{:S(2)}) collective-permute-start(bf16[512,512]{1,0:T(8,128)(2,1)S(1)} %pad_maximum_fusion.4), channel_id=1, source_target_pairs={{0,1},{5,4},{4,0},{1,5},{2,3},{7,6},{6,2},{3,7},{8,9},{13,12},{12,... | collective-permute-start | bytes 1572872 | tf_op jit(solution)/shard_map/ppermute | solution.py:195
  131.0 25.0 %collective-permute-start.28 = (bf16[512,512]{1,0:T(8,128)(2,1)S(1)}, bf16[512,512]{1,0:T(8,128)(2,1)S(1)}, u32[]{:S(2)}, u32[]{:S(2)}) collective-permute-start(bf16[512,512]{1,0:T(8,128)(2,1)S(1)} %pad_maximum_fusion.4), channel_id=1, source_target_pairs={{4,1},{1,4},{6,3},{3,6},{12,9},{9,12},{14,11},{11,14},{20,17},{17,... | collective-permute-start | bytes 1572872 | tf_op jit(solution)/shard_map/ppermute | solution.py:196
  144.1 12.1 %collective-permute-start.37 = (bf16[512,512]{1,0:T(8,128)(2,1)S(1)}, bf16[512,512]{1,0:T(8,128)(2,1)S(1)}, u32[]{:S(2)}, u32[]{:S(2)}) collective-permute-start(bf16[512,512]{1,0:T(8,128)(2,1)S(1)} %pad_maximum_fusion.5), channel_id=1, source_target_pairs={{0,1},{1,0},{2,3},{3,2},{4,5},{5,4},{6,7},{7,6},{8,9},{9,8},{10,11... | collective-permute-start | bytes 1572872 | tf_op jit(solution)/shard_map/ppermute | solution.py:27
  144.2 39.4 %collective-permute-start.26 = (bf16[1536,128]{1,0:T(8,128)(2,1)S(1)}, bf16[1536,128]{1,0:T(8,128)(2,1)S(1)}, u32[]{:S(2)}, u32[]{:S(2)}) collective-permute-start(bf16[1536,128]{1,0:T(8,128)(2,1)S(1)} %fusion.88), channel_id=1, source_target_pairs={{0,8},{24,16},{8,0},{16,24},{1,9},{25,17},{9,1},{17,25},{2,10},{26... | collective-permute-start | bytes 1179656 | tf_op jit(solution)/shard_map/ppermute | solution.py:52
  155.1 29.3 %collective-permute-start.31 = (bf16[1536,128]{1,0:T(8,128)(2,1)S(1)}, bf16[1536,128]{1,0:T(8,128)(2,1)S(1)}, u32[]{:S(2)}, u32[]{:S(2)}) collective-permute-start(bf16[1536,128]{1,0:T(8,128)(2,1)S(1)} %add_convert_fusion.32), channel_id=1, source_target_pairs={{8,16},{16,8},{9,17},{17,9},{10,18},{18,10},{11,19},{19,11},{12,20... | collective-permute-start | bytes 1179656 | tf_op jit(solution)/shard_map/ppermute | solution.py:60
  156.3 9.4 %collective-permute-start.38 = (bf16[512,512]{1,0:T(8,128)(2,1)S(1)}, bf16[512,512]{1,0:T(8,128)(2,1)S(1)}, u32[]{:S(2)}, u32[]{:S(2)}) collective-permute-start(bf16[512,512]{1,0:T(8,128)(2,1)S(1)} %get-tuple-element.256), channel_id=1, source_target_pairs={{0,4},{2,6},{4,0},{6,2},{1,5},{3,7},{5,1},{7,3},{8,12},{10,14},{12... | collective-permute-start | bytes 1572872 | tf_op jit(solution)/shard_map/ppermute | solution.py:27
  175.5 17.6 %collective-permute-start.32 = (bf16[1536,128]{1,0:T(8,128)(2,1)S(1)}, bf16[1536,128]{1,0:T(8,128)(2,1)S(1)}, u32[]{:S(2)}, u32[]{:S(2)}) collective-permute-start(bf16[1536,128]{1,0:T(8,128)(2,1)S(1)} %fusion.89), channel_id=1, source_target_pairs={{0,8},{24,16},{8,0},{16,24},{1,9},{25,17},{9,1},{17,25},{2,10},{26... | collective-permute-start | bytes 1179656 | tf_op jit(solution)/shard_map/ppermute | solution.py:52
  183.7 10.3 %collective-permute-start.33 = (bf16[1536,128]{1,0:T(8,128)(2,1)S(1)}, bf16[1536,128]{1,0:T(8,128)(2,1)S(1)}, u32[]{:S(2)}, u32[]{:S(2)}) collective-permute-start(bf16[1536,128]{1,0:T(8,128)(2,1)S(1)} %add_convert_fusion.30), channel_id=1, source_target_pairs={{8,16},{16,8},{9,17},{17,9},{10,18},{18,10},{11,19},{19,11},{12,20... | collective-permute-start | bytes 1179656 | tf_op jit(solution)/shard_map/ppermute | solution.py:60
  184.5 17.0 %collective-permute-start.34 = (bf16[1536,128]{1,0:T(8,128)(2,1)S(1)}, bf16[1536,128]{1,0:T(8,128)(2,1)S(1)}, u32[]{:S(2)}, u32[]{:S(2)}) collective-permute-start(bf16[1536,128]{1,0:T(8,128)(2,1)S(1)} %fusion.90), channel_id=1, source_target_pairs={{0,8},{24,16},{8,0},{16,24},{1,9},{25,17},{9,1},{17,25},{2,10},{26... | collective-permute-start | bytes 1179656 | tf_op jit(solution)/shard_map/ppermute | solution.py:52
  193.2 9.6 %collective-permute-start.35 = (bf16[1536,128]{1,0:T(8,128)(2,1)S(1)}, bf16[1536,128]{1,0:T(8,128)(2,1)S(1)}, u32[]{:S(2)}, u32[]{:S(2)}) collective-permute-start(bf16[1536,128]{1,0:T(8,128)(2,1)S(1)} %add_convert_fusion.28), channel_id=1, source_target_pairs={{8,16},{16,8},{9,17},{17,9},{10,18},{18,10},{11,19},{19,11},{12,20... | collective-permute-start | bytes 1179656 | tf_op jit(solution)/shard_map/ppermute | solution.py:60
  194.1 15.9 %collective-permute-start.36 = (bf16[1536,128]{1,0:T(8,128)(2,1)S(1)}, bf16[1536,128]{1,0:T(8,128)(2,1)S(1)}, u32[]{:S(2)}, u32[]{:S(2)}) collective-permute-start(bf16[1536,128]{1,0:T(8,128)(2,1)S(1)} %fusion.91), channel_id=1, source_target_pairs={{0,8},{24,16},{8,0},{16,24},{1,9},{25,17},{9,1},{17,25},{2,10},{26... | collective-permute-start | bytes 1179656 | tf_op jit(solution)/shard_map/ppermute | solution.py:52
  201.7 9.1 %collective-permute-start.39 = (bf16[1536,128]{1,0:T(8,128)(2,1)S(1)}, bf16[1536,128]{1,0:T(8,128)(2,1)S(1)}, u32[]{:S(2)}, u32[]{:S(2)}) collective-permute-start(bf16[1536,128]{1,0:T(8,128)(2,1)S(1)} %add_convert_fusion.26), channel_id=1, source_target_pairs={{8,16},{16,8},{9,17},{17,9},{10,18},{18,10},{11,19},{19,11},{12,20... | collective-permute-start | bytes 1179656 | tf_op jit(solution)/shard_map/ppermute | solution.py:60
  203.0 15.4 %collective-permute-start.40 = (bf16[1536,128]{1,0:T(8,128)(2,1)S(1)}, bf16[1536,128]{1,0:T(8,128)(2,1)S(1)}, u32[]{:S(2)}, u32[]{:S(2)}) collective-permute-start(bf16[1536,128]{1,0:T(8,128)(2,1)S(1)} %fusion.92), channel_id=1, source_target_pairs={{0,8},{24,16},{8,0},{16,24},{1,9},{25,17},{9,1},{17,25},{2,10},{26... | collective-permute-start | bytes 1179656 | tf_op jit(solution)/shard_map/ppermute | solution.py:52
  210.1 9.1 %collective-permute-start.41 = (bf16[1536,128]{1,0:T(8,128)(2,1)S(1)}, bf16[1536,128]{1,0:T(8,128)(2,1)S(1)}, u32[]{:S(2)}, u32[]{:S(2)}) collective-permute-start(bf16[1536,128]{1,0:T(8,128)(2,1)S(1)} %add_convert_fusion.24), channel_id=1, source_target_pairs={{8,16},{16,8},{9,17},{17,9},{10,18},{18,10},{11,19},{19,11},{12,20... | collective-permute-start | bytes 1179656 | tf_op jit(solution)/shard_map/ppermute | solution.py:60
  210.9 15.9 %collective-permute-start.42 = (bf16[1536,128]{1,0:T(8,128)(2,1)S(1)}, bf16[1536,128]{1,0:T(8,128)(2,1)S(1)}, u32[]{:S(2)}, u32[]{:S(2)}) collective-permute-start(bf16[1536,128]{1,0:T(8,128)(2,1)S(1)} %fusion.93), channel_id=1, source_target_pairs={{0,8},{24,16},{8,0},{16,24},{1,9},{25,17},{9,1},{17,25},{2,10},{26... | collective-permute-start | bytes 1179656 | tf_op jit(solution)/shard_map/ppermute | solution.py:52
  218.5 9.6 %collective-permute-start.43 = (bf16[1536,128]{1,0:T(8,128)(2,1)S(1)}, bf16[1536,128]{1,0:T(8,128)(2,1)S(1)}, u32[]{:S(2)}, u32[]{:S(2)}) collective-permute-start(bf16[1536,128]{1,0:T(8,128)(2,1)S(1)} %add_convert_fusion.22), channel_id=1, source_target_pairs={{8,16},{16,8},{9,17},{17,9},{10,18},{18,10},{11,19},{19,11},{12,20... | collective-permute-start | bytes 1179656 | tf_op jit(solution)/shard_map/ppermute | solution.py:60
  219.4 15.9 %collective-permute-start.44 = (bf16[1536,128]{1,0:T(8,128)(2,1)S(1)}, bf16[1536,128]{1,0:T(8,128)(2,1)S(1)}, u32[]{:S(2)}, u32[]{:S(2)}) collective-permute-start(bf16[1536,128]{1,0:T(8,128)(2,1)S(1)} %fusion.94), channel_id=1, source_target_pairs={{0,8},{24,16},{8,0},{16,24},{1,9},{25,17},{9,1},{17,25},{2,10},{26... | collective-permute-start | bytes 1179656 | tf_op jit(solution)/shard_map/ppermute | solution.py:52
  226.9 9.4 %collective-permute-start.45 = (bf16[1536,128]{1,0:T(8,128)(2,1)S(1)}, bf16[1536,128]{1,0:T(8,128)(2,1)S(1)}, u32[]{:S(2)}, u32[]{:S(2)}) collective-permute-start(bf16[1536,128]{1,0:T(8,128)(2,1)S(1)} %add_convert_fusion.20), channel_id=1, source_target_pairs={{8,16},{16,8},{9,17},{17,9},{10,18},{18,10},{11,19},{19,11},{12,20... | collective-permute-start | bytes 1179656 | tf_op jit(solution)/shard_map/ppermute | solution.py:60
  228.3 15.4 %collective-permute-start.46 = (bf16[1536,128]{1,0:T(8,128)(2,1)S(1)}, bf16[1536,128]{1,0:T(8,128)(2,1)S(1)}, u32[]{:S(2)}, u32[]{:S(2)}) collective-permute-start(bf16[1536,128]{1,0:T(8,128)(2,1)S(1)} %fusion.95), channel_id=1, source_target_pairs={{0,8},{24,16},{8,0},{16,24},{1,9},{25,17},{9,1},{17,25},{2,10},{26... | collective-permute-start | bytes 1179656 | tf_op jit(solution)/shard_map/ppermute | solution.py:52
  235.4 9.1 %collective-permute-start.47 = (bf16[1536,128]{1,0:T(8,128)(2,1)S(1)}, bf16[1536,128]{1,0:T(8,128)(2,1)S(1)}, u32[]{:S(2)}, u32[]{:S(2)}) collective-permute-start(bf16[1536,128]{1,0:T(8,128)(2,1)S(1)} %add_convert_fusion.18), channel_id=1, source_target_pairs={{8,16},{16,8},{9,17},{17,9},{10,18},{18,10},{11,19},{19,11},{12,20... | collective-permute-start | bytes 1179656 | tf_op jit(solution)/shard_map/ppermute | solution.py:60
  236.5 15.1 %collective-permute-start.48 = (bf16[1536,128]{1,0:T(8,128)(2,1)S(1)}, bf16[1536,128]{1,0:T(8,128)(2,1)S(1)}, u32[]{:S(2)}, u32[]{:S(2)}) collective-permute-start(bf16[1536,128]{1,0:T(8,128)(2,1)S(1)} %fusion.96), channel_id=1, source_target_pairs={{0,8},{24,16},{8,0},{16,24},{1,9},{25,17},{9,1},{17,25},{2,10},{26... | collective-permute-start | bytes 1179656 | tf_op jit(solution)/shard_map/ppermute | solution.py:52
  243.8 9.1 %collective-permute-start.49 = (bf16[1536,128]{1,0:T(8,128)(2,1)S(1)}, bf16[1536,128]{1,0:T(8,128)(2,1)S(1)}, u32[]{:S(2)}, u32[]{:S(2)}) collective-permute-start(bf16[1536,128]{1,0:T(8,128)(2,1)S(1)} %add_convert_fusion.16), channel_id=1, source_target_pairs={{8,16},{16,8},{9,17},{17,9},{10,18},{18,10},{11,19},{19,11},{12,20... | collective-permute-start | bytes 1179656 | tf_op jit(solution)/shard_map/ppermute | solution.py:60
  244.6 12.9 %collective-permute-start.50 = (bf16[1536,128]{1,0:T(8,128)(2,1)S(1)}, bf16[1536,128]{1,0:T(8,128)(2,1)S(1)}, u32[]{:S(2)}, u32[]{:S(2)}) collective-permute-start(bf16[1536,128]{1,0:T(8,128)(2,1)S(1)} %add_convert_fusion.15), channel_id=1, source_target_pairs={{8,0},{16,24},{9,1},{17,25},{10,2},{18,26},{11,3},{19,27},{12,4},{... | collective-permute-start | bytes 1179656 | tf_op jit(solution)/shard_map/ppermute | solution.py:52
  253.0 9.7 %collective-permute-start.52 = (bf16[1536,128]{1,0:T(8,128)(2,1)S(1)}, bf16[1536,128]{1,0:T(8,128)(2,1)S(1)}, u32[]{:S(2)}, u32[]{:S(2)}) collective-permute-start(bf16[1536,128]{1,0:T(8,128)(2,1)S(1)} %add_convert_fusion.13), channel_id=1, source_target_pairs={{8,0},{16,24},{9,1},{17,25},{10,2},{18,26},{11,3},{19,27},{12,4},{... | collective-permute-start | bytes 1179656 | tf_op jit(solution)/shard_map/ppermute | solution.py:52
  257.6 10.5 %collective-permute-start.53 = (bf16[1536,128]{1,0:T(8,128)(2,1)S(1)}, bf16[1536,128]{1,0:T(8,128)(2,1)S(1)}, u32[]{:S(2)}, u32[]{:S(2)}) collective-permute-start(bf16[1536,128]{1,0:T(8,128)(2,1)S(1)} %add_convert_fusion.12), channel_id=1, source_target_pairs={{8,0},{16,24},{9,1},{17,25},{10,2},{18,26},{11,3},{19,27},{12,4},{... | collective-permute-start | bytes 1179656 | tf_op jit(solution)/shard_map/ppermute | solution.py:52
  (19 other events, 160.7 us)

commit v6 on v5

--- a/solution.py
+++ b/solution.py
@@ -89,65 +89,49 @@
             jnp.dot(block, weight, preferred_element_type=f32).astype(bf16)
         )
 
-    def at(h, q, x):
-        return (h * group + q) * 2 + x
-
-    ring_pairs, cross_pairs = [], []
-    for q in range(group):
-        ring_pairs += [(at(x, q, x), at(x, q, 1 - x)) for x in (0, 1)]
-        ring_pairs += [(at(1 - x, q, x), at(x, q, x)) for x in (0, 1)]
-        cross_pairs += [(at(1 - x, q, x), at(x, q, 1 - x)) for x in (0, 1)]
-    inward_pairs = [(at(1 - x, q, x), at(1 - x, q, 1 - x)) for q in range(group) for x in (0, 1)]
-    outward_pairs = [(at(x, q, x), at(x, q, 1 - x)) for q in range(group) for x in (0, 1)]
-
     near_blocks = [context] + [swap(context, "fsdp", r) for r in range(1, group)]
     slices = [
         [lax.dynamic_slice_in_dim(array, (low ^ r) * cols, cols, axis=1) for r in range(group)]
         for array in (residual, cotangent)
     ]
-    held = together(context, *slices[0], *slices[1])
-    later, slices = held[0], [held[1 : 1 + group], held[1 + group :]]
     moved = [[swap(parts[r], "fsdp", r) if r else parts[r] for r in range(group)] for parts in slices]
-    far_pieces = [
-        swap((later if p else context)[p * rows : (p + 1) * rows], "fsdp", group) for p in range(pieces)
-    ]
-    held = together(far_pieces[0], *near_blocks[1:], *moved[0], *moved[1])
-    far_pieces[0] = held[0]
-    near_blocks = [later] + list(held[1:group])
+    held = together(swap(context, "fsdp", group), *near_blocks[1:], *moved[0], *moved[1])
+    near_blocks = [context] + list(held[1:group])
     residual_parts, cotangent_parts = held[group : 2 * group], held[2 * group :]
-    far_pieces = [far_pieces] + [
-        [swap(piece, "fsdp", r) for piece in far_pieces] for r in range(1, group)
-    ]
+    far_blocks = [held[0]] + [swap(held[0], "fsdp", r) for r in range(1, group)]
     far_outs, near_out = [], [[None] * pieces for r in range(group)]
-    near_came = {}
     last = None
     for r in range(group):
         for p in range(pieces):
             beside = (r + 1) % group
-            far = far_pieces[r][p]
+            far = far_blocks[r]
             if last:
                 far, near_out[last[0]][last[1]] = together(far, near_out[last[0]][last[1]])
             both = project(
-                jnp.concatenate([far, near_blocks[beside][p * rows : (p + 1) * rows]], axis=0)
+                jnp.concatenate([block[p * rows : (p + 1) * rows] for block in (far, near_blocks[beside])], axis=0)
             )
             far_outs.append(swap(both[:rows], "fsdp", group))
             near_out[beside][p] = both[rows:]
             last = (beside, p)
-        whole = jnp.concatenate(near_out[beside], axis=0)
-        near_came[beside] = lax.ppermute(whole, ("fsdp", "tp"), inward_pairs)
-    passed = [lax.ppermute(out, ("fsdp", "tp"), outward_pairs) for out in far_outs]
 
     gain_part = lax.dynamic_slice_in_dim(gain, t * (width // 2) + low * cols, cols).astype(f32)
 
+    keeps, arrivals = [], []
+    for r in range(group):
+        for p in range(pieces):
+            far_out, own_out = far_outs[r * pieces + p], near_out[r][p]
+            if keeps:
+                far_out, own_out, keeps[-1] = together(far_out, own_out, keeps[-1])
+            else:
+                far_out, own_out = together(far_out, own_out)
+            keeps.append(jnp.where(near, own_out, far_out))
+            arrivals.append(swap(jnp.where(near, far_out, own_out), "tp", 1))
     hidden, weighted, sums = [], [], []
-    for k in range(group * pieces):
-        r, p = k // pieces, k % pieces
-        span = slice(p * rows, (p + 1) * rows)
-        res, cot, came = residual_parts[r], cotangent_parts[r], passed[k]
+    for k, (keep, came) in enumerate(zip(keeps, arrivals)):
+        span = slice(k % pieces * rows, (k % pieces + 1) * rows)
+        res, cot = residual_parts[k // pieces], cotangent_parts[k // pieces]
         if sums:
             came, sums[-1] = together(came, sums[-1])
-        keep = jnp.where(near, near_out[r][p], far_outs[k])
-        came = jnp.where(near, near_came[r][span], came)
         h = res[span].astype(f32) + keep.astype(f32) + came.astype(f32)
         w = gain_part[None, :] * cot[span].astype(f32)
         hidden.append(h)
@@ -166,13 +150,21 @@
     inv_rms = lax.rsqrt(totals[0] / width + norm_eps)
     pull = inv_rms**3 * totals[1] / width
 
-    tokens = near_blocks + [piece for block in far_pieces for piece in block]
-    context_all = jnp.concatenate(tokens, axis=0)
+    context_all = jnp.concatenate(near_blocks + far_blocks, axis=0)
     narrow = 128
     units = cols // narrow
     widths = [1, 3]
     while sum(widths) < units:
         widths.append(min(4, units - sum(widths)))
+    def at(h, q, x):
+        return (h * group + q) * 2 + x
+
+    ring_pairs, cross_pairs = [], []
+    for q in range(group):
+        ring_pairs += [(at(x, q, x), at(x, q, 1 - x)) for x in (0, 1)]
+        ring_pairs += [(at(1 - x, q, x), at(x, q, x)) for x in (0, 1)]
+        cross_pairs += [(at(1 - x, q, x), at(x, q, 1 - x)) for x in (0, 1)]
+
     islands = lax.axis_size("island")
     line = IslandLine(units)
     parts, rings = [], []
@@ -220,13 +212,14 @@
                 (((0,), (0,)), ((), ())),
                 preferred_element_type=f32,
             ) / (tok_rows * fsdp_count)
-            first = first_moment[0, :, at_cols].astype(f32)
-            second = second_moment[0, :, at_cols].astype(f32)
+            first, second, outer = together(first_moment, second_moment, weight)
+            first = first[0, :, at_cols].astype(f32)
+            second = second[0, :, at_cols].astype(f32)
             m_new = beta_one * first + (1.0 - beta_one) * grad
             v_new = beta_two * second + (1.0 - beta_two) * grad * grad
             update = m_new / bias_one / (
                 jnp.sqrt(v_new / bias_two) + adam_eps
-            ) + decay_rate * weight[:, at_cols].astype(f32)
+            ) + decay_rate * outer[:, at_cols].astype(f32)
             pseudo = lax.optimization_barrier(update.astype(bf16))
             parts.extend(pseudo[:, u * narrow : (u + 1) * narrow] for u in range(hi - lo))
 

time: 277 us -> 270 us (0.975)
    ppermute x15 -> x17, waiting for transfers between devices: 44.6 us -> 62.9 us  [swap(): return lax.ppermute(value, axis, [(i, i ^ bit) for i in range(count)])]
    ppermute x6 -> x0, waiting for transfers between devices: 17.3 us -> none  [the longest x4 17.3 us: body(): lax.ppermute(out, ('fsdp', 'tp'), outward_pairs)]
    ppermute x6 -> x0, starting transfers between devices: 9.87 us -> none  [the longest x4 5.13 us: body(): lax.ppermute(out, ('fsdp', 'tp'), outward_pairs)]
    ppermute x15 -> x17, starting transfers between devices: 8.91 us -> 12.3 us  [swap(): return lax.ppermute(value, axis, [(i, i ^ bit) for i in range(count)])]
    ppermute x3, starting transfers between devices: 0.12 us -> 3.09 us  [add_parts(): rings.append(lax.ppermute(d_local, ('fsdp', 'tp'), ring_pairs))]
  transfers between devices with their start and end apart: 54 -> 50, of which waited for: 28 -> 26; matrix products, arithmetic and copies ran while one was open for 16% -> 16% of each run, Pallas kernels for 0% -> 0%
where the time goes in v6:
time: 270 us; the launch traced here: 267 us
  waiting for transfers between devices  117 us (43%)
  starting transfers between devices  95.1 us (35%)
  matrix products  27.2 us (10%)
  other arithmetic  15.6 us (6%)
  local copies, waits for them, and re-layouts  10.1 us (4%)
    ppermute x17, waiting for transfers between devices, swap(): return lax.ppermute(value, axis, [(i, i ^ bit) for i in range(count)])  62.9 us
    ppermute x15, starting transfers between devices, send_outer(): self.edge[s] = lax.ppermute(payload, 'island', pairs)  62.3 us
    ppermute x15, waiting for transfers between devices, send_outer(): self.edge[s] = lax.ppermute(payload, 'island', pairs)  46.3 us
    dot_general x7, matrix products, add_pseudo(): lax.dot_general(context_all, lax.optimization_barrier(d_all[:, lo * narro...  19.2 us
    ppermute x17, starting transfers between devices, swap(): return lax.ppermute(value, axis, [(i, i ^ bit) for i in range(count)])  12.3 us
    ppermute x12, starting transfers between devices, step(): self.mid[s] = lax.ppermute(self.sums[s], 'island', [(1, 2), (2, 1)])  8.7 us
    ppermute x3, starting transfers between devices, add_parts(): cross = lax.ppermute(d_local, ('fsdp', 'tp'), cross_pairs)  8.69 us
    dot_general x4, matrix products, project(): jnp.dot(block, weight, preferred_element_type=f32).astype(bf16)  8 us
  transfers between devices with their start and end apart: 50, of which 26 were waited for; matrix products, arithmetic and copies ran while one was open for 16% of the time, Pallas kernels for 0%

profile of v6, /device:TPU:2, one launch (start us, length us, event | category | flops | bytes accessed | tf_op | source)
XLA Modules:
  0.0 266.8 jit_solution(613250266506387704)
XLA Ops:
  0.6 1.6 collective-permute-start
  2.2 2.8 %constant_dynamic-slice_fusion.2 = (bf16[256,1536]{1,0:T(8,128)(2,1)}, bf16[256,1536]{1,0:T(8,128)(2,1)}) fusion(bf16[256,3072]{1,0:T(8,128)(2,1)} %param.9, s32[]{:T(128)S(6)} %select_n.193, s32[]{:T(128)S(6)} %select_n.192), kind=kLoop, calls=%fused_computation.314 | loop fusion | bytes 3145736 | tf_op jit(solution)/shard_map/dynamic_slice | solution.py:94
  7.4 12.8 %collective-permute-done = bf16[256,1536]{1,0:T(8,128)(2,1)S(1)} collective-permute-done((bf16[256,1536]{1,0:T(8,128)(2,1)}, bf16[256,1536]{1,0:T(8,128)(2,1)S(1)}, u32[]{:S(2)}, u32[]{:S(2)}) %collective-permute-start) | collective-permute-done | bytes 786464 | tf_op jit(solution)/shard_map/ppermute | solution.py:27
  20.4 3.9 %convolution_convert_fusion.3 = bf16[256,1536]{1,0:T(8,128)(2,1)S(1)} fusion(bf16[1536,1536]{1,0:T(8,128)(2,1)} %param.12, bf16[128,1536]{1,0:T(8,128)(2,1)S(1)} %get-tuple-element.296, bf16[128,1536]{1,0:T(8,128)(2,1)S(1)} %slice.391), kind=kOutput, calls=%fused_computation.3 | convolution fusion | flops 1209925632 | bytes 6291456 | tf_op jit(solution)/shard_map/dot_general | solution.py:89
  29.5 6.8 %collective-permute-done.6 = bf16[128,1536]{1,0:T(8,128)(2,1)S(1)} collective-permute-done((bf16[128,1536]{1,0:T(8,128)(2,1)S(1)}, bf16[128,1536]{1,0:T(8,128)(2,1)S(1)}, u32[]{:S(2)}, u32[]{:S(2)}) %collective-permute-start.6) | collective-permute-done | bytes 393248 | tf_op jit(solution)/shard_map/ppermute | solution.py:27
  39.9 4.8 %collective-permute-done.5 = bf16[128,1536]{1,0:T(8,128)(2,1)S(1)} collective-permute-done((bf16[128,1536]{1,0:T(8,128)(2,1)S(1)}, bf16[128,1536]{1,0:T(8,128)(2,1)S(1)}, u32[]{:S(2)}, u32[]{:S(2)}) %collective-permute-start.5) | collective-permute-done | bytes 393248 | tf_op jit(solution)/shard_map/ppermute | solution.py:27
  45.2 1.7 collective-permute-start.8
  46.9 14.3 %collective-permute-done.9 = bf16[128,1536]{1,0:T(8,128)(2,1)S(1)} collective-permute-done((bf16[128,1536]{1,0:T(8,128)(2,1)S(1)}, bf16[128,1536]{1,0:T(8,128)(2,1)S(1)}, u32[]{:S(2)}, u32[]{:S(2)}) %collective-permute-start.9) | collective-permute-done | bytes 393248 | tf_op jit(solution)/shard_map/ppermute | solution.py:27
  61.7 1.7 collective-permute-start.10
  64.6 16.0 %collective-permute-done.10 = bf16[128,1536]{1,0:T(8,128)(2,1)S(1)} collective-permute-done((bf16[128,1536]{1,0:T(8,128)(2,1)S(1)}, bf16[128,1536]{1,0:T(8,128)(2,1)S(1)}, u32[]{:S(2)}, u32[]{:S(2)}) %collective-permute-start.10) | collective-permute-done | bytes 393248 | tf_op jit(solution)/shard_map/ppermute | solution.py:27
  82.1 1.7 multiply_reduce_fusion.1
  85.5 3.2 %collective-permute-done.14 = f32[2,512]{1,0:T(2,128)S(1)} collective-permute-done((f32[2,512]{1,0:T(2,128)S(1)}, f32[2,512]{1,0:T(2,128)S(1)}, u32[]{:S(2)}, u32[]{:S(2)}) %collective-permute-start.14) | collective-permute-done | bytes 4128 | tf_op jit(solution)/shard_map/ppermute | solution.py:27
  91.2 2.2 collective-permute-start.18
  96.2 3.0 %collective-permute-start.17 = (bf16[512,384]{1,0:T(8,128)(2,1)S(1)}, bf16[512,384]{1,0:T(8,128)(2,1)S(1)}, u32[]{:S(2)}, u32[]{:S(2)}) collective-permute-start(bf16[512,384]{1,0:T(8,128)(2,1)S(1)} %pad_maximum_fusion.4), channel_id=1, source_target_pairs={{4,1},{1,4},{6,3},{3,6},{12,9},{9,12},{14,11},{11,14},{20,17},{17,... | collective-permute-start | bytes 1179656 | tf_op jit(solution)/shard_map/ppermute | solution.py:188
  100.4 3.3 %collective-permute-done.16 = bf16[512,384]{1,0:T(8,128)(2,1)S(1)} collective-permute-done((bf16[512,384]{1,0:T(8,128)(2,1)S(1)}, bf16[512,384]{1,0:T(8,128)(2,1)S(1)}, u32[]{:S(2)}, u32[]{:S(2)}) %collective-permute-start.16) | collective-permute-done | bytes 393248 | tf_op jit(solution)/shard_map/ppermute | solution.py:187
  103.7 3.9 %collective-permute-done.17 = bf16[512,384]{1,0:T(8,128)(2,1)S(1)} collective-permute-done((bf16[512,384]{1,0:T(8,128)(2,1)S(1)}, bf16[512,384]{1,0:T(8,128)(2,1)S(1)}, u32[]{:S(2)}, u32[]{:S(2)}) %collective-permute-start.17) | collective-permute-done | bytes 393248 | tf_op jit(solution)/shard_map/ppermute | solution.py:188
  107.8 2.0 fusion.72
  109.8 3.6 %collective-permute-start.19 = (bf16[1536,128]{1,0:T(8,128)(2,1)S(1)}, bf16[1536,128]{1,0:T(8,128)(2,1)S(1)}, u32[]{:S(2)}, u32[]{:S(2)}) collective-permute-start(bf16[1536,128]{1,0:T(8,128)(2,1)S(1)} %get-tuple-element.259), channel_id=1, source_target_pairs={{0,8},{24,16},{1,9},{25,17},{2,10},{26,18},{3,11},{27,19},{4,12},{... | collective-permute-start | bytes 1179656 | tf_op jit(solution)/shard_map/ppermute | solution.py:52
  114.8 2.2 fusion.30
  118.4 4.7 %collective-permute-done.19 = bf16[1536,128]{1,0:T(8,128)(2,1)S(1)} collective-permute-done((bf16[1536,128]{1,0:T(8,128)(2,1)S(1)}, bf16[1536,128]{1,0:T(8,128)(2,1)S(1)}, u32[]{:S(2)}, u32[]{:S(2)}) %collective-permute-start.19) | collective-permute-done | bytes 393248 | tf_op jit(solution)/shard_map/ppermute | solution.py:52
  123.0 3.5 %collective-permute-start.24 = (bf16[512,512]{1,0:T(8,128)(2,1)S(1)}, bf16[512,512]{1,0:T(8,128)(2,1)S(1)}, u32[]{:S(2)}, u32[]{:S(2)}) collective-permute-start(bf16[512,512]{1,0:T(8,128)(2,1)S(1)} %pad_maximum_fusion.2), channel_id=1, source_target_pairs={{4,1},{1,4},{6,3},{3,6},{12,9},{9,12},{14,11},{11,14},{20,17},{17,... | collective-permute-start | bytes 1572872 | tf_op jit(solution)/shard_map/ppermute | solution.py:188
  127.4 4.1 %collective-permute-done.21 = bf16[1536,128]{1,0:T(8,128)(2,1)S(1)} collective-permute-done((bf16[1536,128]{1,0:T(8,128)(2,1)S(1)}, bf16[1536,128]{1,0:T(8,128)(2,1)S(1)}, u32[]{:S(2)}, u32[]{:S(2)}) %collective-permute-start.21) | collective-permute-done | bytes 393248 | tf_op jit(solution)/shard_map/ppermute | solution.py:52
  132.4 3.4 %collective-permute-done.26 = bf16[1536,128]{1,0:T(8,128)(2,1)S(1)} collective-permute-done((bf16[1536,128]{1,0:T(8,128)(2,1)S(1)}, bf16[1536,128]{1,0:T(8,128)(2,1)S(1)}, u32[]{:S(2)}, u32[]{:S(2)}) %collective-permute-start.26) | collective-permute-done | bytes 393248 | tf_op jit(solution)/shard_map/ppermute | solution.py:52
  136.0 11.6 %collective-permute-start.22 = (bf16[1536,128]{1,0:T(8,128)(2,1)S(1)}, bf16[1536,128]{1,0:T(8,128)(2,1)S(1)}, u32[]{:S(2)}, u32[]{:S(2)}) collective-permute-start(bf16[1536,128]{1,0:T(8,128)(2,1)S(1)} %fusion.88), channel_id=1, source_target_pairs={{0,8},{24,16},{8,0},{16,24},{1,9},{25,17},{9,1},{17,25},{2,10},{26... | collective-permute-start | bytes 1179656 | tf_op jit(solution)/shard_map/ppermute | solution.py:52
  150.0 2.2 fusion.159
  152.1 2.2 fusion.158
  154.3 3.8 %collective-permute-done.34 = bf16[512,512]{1,0:T(8,128)(2,1)S(1)} collective-permute-done((bf16[512,512]{1,0:T(8,128)(2,1)S(1)}, bf16[512,512]{1,0:T(8,128)(2,1)S(1)}, u32[]{:S(2)}, u32[]{:S(2)}) %collective-permute-start.34) | collective-permute-done | bytes 524320 | tf_op jit(solution)/shard_map/ppermute | solution.py:27
  158.1 2.2 fusion.160
  160.3 7.5 %fusion.34 = (bf16[1536,256]{1,0:T(8,128)(2,1)S(1)}, bf16[1536,256]{1,0:T(8,128)(2,1)S(1)}, bf16[1536,256]{1,0:T(8,128)(2,1)S(1)}, bf16[1536,256]{1,0:T(8,128)(2,1)S(1)}) fusion(bf16[1536,1536]{1,0:T(8,128)(2,1)S(1)} %bitcast.205, bf16[1,1536,1536]{2,1,0:T(8,128)(2,1)S(1)} %bitcast.207, bf16[1,1536,1536]{2,1,0:T(8,128)(2,1)S(1)} %bitcast.209, ...), kind=kOutput, calls=%fused_computation.48 | convolution fusion | flops 833617920 | bytes 20971520 | tf_op jit(solution)/shard_map/dot_general | solution.py:209
  167.9 8.1 %collective-permute-start.28 = (bf16[1536,128]{1,0:T(8,128)(2,1)S(1)}, bf16[1536,128]{1,0:T(8,128)(2,1)S(1)}, u32[]{:S(2)}, u32[]{:S(2)}) collective-permute-start(bf16[1536,128]{1,0:T(8,128)(2,1)S(1)} %fusion.89), channel_id=1, source_target_pairs={{0,8},{24,16},{8,0},{16,24},{1,9},{25,17},{9,1},{17,25},{2,10},{26... | collective-permute-start | bytes 1179656 | tf_op jit(solution)/shard_map/ppermute | solution.py:52
  177.0 2.9 %collective-permute-start.30 = (bf16[1536,128]{1,0:T(8,128)(2,1)S(1)}, bf16[1536,128]{1,0:T(8,128)(2,1)S(1)}, u32[]{:S(2)}, u32[]{:S(2)}) collective-permute-start(bf16[1536,128]{1,0:T(8,128)(2,1)S(1)} %fusion.90), channel_id=1, source_target_pairs={{0,8},{24,16},{8,0},{16,24},{1,9},{25,17},{9,1},{17,25},{2,10},{26... | collective-permute-start | bytes 1179656 | tf_op jit(solution)/shard_map/ppermute | solution.py:52
  180.4 4.8 %collective-permute-done.28 = bf16[1536,128]{1,0:T(8,128)(2,1)S(1)} collective-permute-done((bf16[1536,128]{1,0:T(8,128)(2,1)S(1)}, bf16[1536,128]{1,0:T(8,128)(2,1)S(1)}, u32[]{:S(2)}, u32[]{:S(2)}) %collective-permute-start.28) | collective-permute-done | bytes 393248 | tf_op jit(solution)/shard_map/ppermute | solution.py:52
  186.2 4.6 %collective-permute-start.32 = (bf16[1536,128]{1,0:T(8,128)(2,1)S(1)}, bf16[1536,128]{1,0:T(8,128)(2,1)S(1)}, u32[]{:S(2)}, u32[]{:S(2)}) collective-permute-start(bf16[1536,128]{1,0:T(8,128)(2,1)S(1)} %fusion.91), channel_id=1, source_target_pairs={{0,8},{24,16},{8,0},{16,24},{1,9},{25,17},{9,1},{17,25},{2,10},{26... | collective-permute-start | bytes 1179656 | tf_op jit(solution)/shard_map/ppermute | solution.py:52
  190.8 2.8 %collective-permute-done.30 = bf16[1536,128]{1,0:T(8,128)(2,1)S(1)} collective-permute-done((bf16[1536,128]{1,0:T(8,128)(2,1)S(1)}, bf16[1536,128]{1,0:T(8,128)(2,1)S(1)}, u32[]{:S(2)}, u32[]{:S(2)}) %collective-permute-start.30) | collective-permute-done | bytes 393248 | tf_op jit(solution)/shard_map/ppermute | solution.py:52
  195.1 4.8 %collective-permute-start.36 = (bf16[1536,128]{1,0:T(8,128)(2,1)S(1)}, bf16[1536,128]{1,0:T(8,128)(2,1)S(1)}, u32[]{:S(2)}, u32[]{:S(2)}) collective-permute-start(bf16[1536,128]{1,0:T(8,128)(2,1)S(1)} %fusion.92), channel_id=1, source_target_pairs={{0,8},{24,16},{8,0},{16,24},{1,9},{25,17},{9,1},{17,25},{2,10},{26... | collective-permute-start | bytes 1179656 | tf_op jit(solution)/shard_map/ppermute | solution.py:52
  199.8 2.2 collective-permute-done.32
  203.0 5.2 %collective-permute-start.38 = (bf16[1536,128]{1,0:T(8,128)(2,1)S(1)}, bf16[1536,128]{1,0:T(8,128)(2,1)S(1)}, u32[]{:S(2)}, u32[]{:S(2)}) collective-permute-start(bf16[1536,128]{1,0:T(8,128)(2,1)S(1)} %fusion.93), channel_id=1, source_target_pairs={{0,8},{24,16},{8,0},{16,24},{1,9},{25,17},{9,1},{17,25},{2,10},{26... | collective-permute-start | bytes 1179656 | tf_op jit(solution)/shard_map/ppermute | solution.py:52
  211.5 5.2 %collective-permute-start.40 = (bf16[1536,128]{1,0:T(8,128)(2,1)S(1)}, bf16[1536,128]{1,0:T(8,128)(2,1)S(1)}, u32[]{:S(2)}, u32[]{:S(2)}) collective-permute-start(bf16[1536,128]{1,0:T(8,128)(2,1)S(1)} %fusion.94), channel_id=1, source_target_pairs={{0,8},{24,16},{8,0},{16,24},{1,9},{25,17},{9,1},{17,25},{2,10},{26... | collective-permute-start | bytes 1179656 | tf_op jit(solution)/shard_map/ppermute | solution.py:52
  216.7 2.2 collective-permute-done.38
  220.3 4.8 %collective-permute-start.42 = (bf16[1536,128]{1,0:T(8,128)(2,1)S(1)}, bf16[1536,128]{1,0:T(8,128)(2,1)S(1)}, u32[]{:S(2)}, u32[]{:S(2)}) collective-permute-start(bf16[1536,128]{1,0:T(8,128)(2,1)S(1)} %fusion.95), channel_id=1, source_target_pairs={{0,8},{24,16},{8,0},{16,24},{1,9},{25,17},{9,1},{17,25},{2,10},{26... | collective-permute-start | bytes 1179656 | tf_op jit(solution)/shard_map/ppermute | solution.py:52
  225.1 2.2 collective-permute-done.40
  228.6 5.0 %collective-permute-start.44 = (bf16[1536,128]{1,0:T(8,128)(2,1)S(1)}, bf16[1536,128]{1,0:T(8,128)(2,1)S(1)}, u32[]{:S(2)}, u32[]{:S(2)}) collective-permute-start(bf16[1536,128]{1,0:T(8,128)(2,1)S(1)} %fusion.96), channel_id=1, source_target_pairs={{0,8},{24,16},{8,0},{16,24},{1,9},{25,17},{9,1},{17,25},{2,10},{26... | collective-permute-start | bytes 1179656 | tf_op jit(solution)/shard_map/ppermute | solution.py:52
  238.0 5.8 %collective-permute-done.44 = bf16[1536,128]{1,0:T(8,128)(2,1)S(1)} collective-permute-done((bf16[1536,128]{1,0:T(8,128)(2,1)S(1)}, bf16[1536,128]{1,0:T(8,128)(2,1)S(1)}, u32[]{:S(2)}, u32[]{:S(2)}) %collective-permute-start.44) | collective-permute-done | bytes 393248 | tf_op jit(solution)/shard_map/ppermute | solution.py:52
  246.4 3.1 %collective-permute-done.46 = bf16[1536,128]{1,0:T(8,128)(2,1)S(1)} collective-permute-done((bf16[1536,128]{1,0:T(8,128)(2,1)S(1)}, bf16[1536,128]{1,0:T(8,128)(2,1)S(1)}, u32[]{:S(2)}, u32[]{:S(2)}) %collective-permute-start.46) | collective-permute-done | bytes 393248 | tf_op jit(solution)/shard_map/ppermute | solution.py:52
  251.9 2.9 %collective-permute-done.48 = bf16[1536,128]{1,0:T(8,128)(2,1)S(1)} collective-permute-done((bf16[1536,128]{1,0:T(8,128)(2,1)S(1)}, bf16[1536,128]{1,0:T(8,128)(2,1)S(1)}, u32[]{:S(2)}, u32[]{:S(2)}) %collective-permute-start.48) | collective-permute-done | bytes 393248 | tf_op jit(solution)/shard_map/ppermute | solution.py:52
  254.8 5.4 %collective-permute-done.49 = bf16[1536,128]{1,0:T(8,128)(2,1)S(1)} collective-permute-done((bf16[1536,128]{1,0:T(8,128)(2,1)S(1)}, bf16[1536,128]{1,0:T(8,128)(2,1)S(1)}, u32[]{:S(2)}, u32[]{:S(2)}) %collective-permute-start.49) | collective-permute-done | bytes 393248 | tf_op jit(solution)/shard_map/ppermute | solution.py:52
  261.2 3.4 %copy-done.3 = f32[1536,1536]{1,0:T(8,128)} copy-done((f32[1536,1536]{1,0:T(8,128)}, f32[1536,1536]{1,0:T(8,128)S(1)}, u32[]{:S(2)}) %copy-start.3) | copy-done | bytes 9437208
  264.6 2.2 copy-done.4
  (204 shorter events, 50.9 us)
Async XLA Ops:
  0.6 19.6 %collective-permute-start = (bf16[256,1536]{1,0:T(8,128)(2,1)}, bf16[256,1536]{1,0:T(8,128)(2,1)S(1)}, u32[]{:S(2)}, u32[]{:S(2)}) collective-permute-start(bf16[256,1536]{1,0:T(8,128)(2,1)} %param.8), channel_id=1, source_target_pairs={{0,4},{2,6},{4,0},{6,2},{1,5},{3,7},{5,1},{7,3},{8,12},{10,14},{12... | collective-permute-start | bytes 2359304 | tf_op jit(solution)/shard_map/ppermute | solution.py:27
  2.2 18.0 %collective-permute-start.1 = (bf16[256,1536]{1,0:T(8,128)(2,1)}, bf16[256,1536]{1,0:T(8,128)(2,1)S(1)}, u32[]{:S(2)}, u32[]{:S(2)}) collective-permute-start(bf16[256,1536]{1,0:T(8,128)(2,1)} %param.8), channel_id=1, source_target_pairs={{0,2},{2,0},{4,6},{6,4},{1,3},{3,1},{5,7},{7,5},{8,10},{10,8},{12,... | collective-permute-start | bytes 2359304 | tf_op jit(solution)/shard_map/ppermute | solution.py:27
  5.0 15.2 %collective-permute-start.2 = (bf16[256,1536]{1,0:T(8,128)(2,1)}, bf16[256,1536]{1,0:T(8,128)(2,1)}, u32[]{:S(2)}, u32[]{:S(2)}) collective-permute-start(bf16[256,1536]{1,0:T(8,128)(2,1)} %get-tuple-element.270), channel_id=1, source_target_pairs={{0,2},{2,0},{4,6},{6,4},{1,3},{3,1},{5,7},{7,5},{8,10},{10,8},{12,... | collective-permute-start | bytes 2359304 | tf_op jit(solution)/shard_map/ppermute | solution.py:27
  6.5 13.7 %collective-permute-start.3 = (bf16[256,1536]{1,0:T(8,128)(2,1)}, bf16[256,1536]{1,0:T(8,128)(2,1)}, u32[]{:S(2)}, u32[]{:S(2)}) collective-permute-start(bf16[256,1536]{1,0:T(8,128)(2,1)} %get-tuple-element.268), channel_id=1, source_target_pairs={{0,2},{2,0},{4,6},{6,4},{1,3},{3,1},{5,7},{7,5},{8,10},{10,8},{12,... | collective-permute-start | bytes 2359304 | tf_op jit(solution)/shard_map/ppermute | solution.py:27
  20.2 7.9 %collective-permute-start.4 = (bf16[256,1536]{1,0:T(8,128)(2,1)S(1)}, bf16[256,1536]{1,0:T(8,128)(2,1)S(1)}, u32[]{:S(2)}, u32[]{:S(2)}) collective-permute-start(bf16[256,1536]{1,0:T(8,128)(2,1)S(1)} %collective-permute-done), channel_id=1, source_target_pairs={{0,2},{2,0},{4,6},{6,4},{1,3},{3,1},{5,7},{7,5},{8,10},{10,8},{12,... | collective-permute-start | bytes 2359304 | tf_op jit(solution)/shard_map/ppermute | solution.py:27
  24.3 12.0 %collective-permute-start.6 = (bf16[128,1536]{1,0:T(8,128)(2,1)S(1)}, bf16[128,1536]{1,0:T(8,128)(2,1)S(1)}, u32[]{:S(2)}, u32[]{:S(2)}) collective-permute-start(bf16[128,1536]{1,0:T(8,128)(2,1)S(1)} %get-tuple-element.288), channel_id=1, source_target_pairs={{0,4},{2,6},{4,0},{6,2},{1,5},{3,7},{5,1},{7,3},{8,12},{10,14},{12... | collective-permute-start | bytes 1179656 | tf_op jit(solution)/shard_map/ppermute | solution.py:27
  27.4 17.3 %collective-permute-start.5 = (bf16[128,1536]{1,0:T(8,128)(2,1)S(1)}, bf16[128,1536]{1,0:T(8,128)(2,1)S(1)}, u32[]{:S(2)}, u32[]{:S(2)}) collective-permute-start(bf16[128,1536]{1,0:T(8,128)(2,1)S(1)} %get-tuple-element.292), channel_id=1, source_target_pairs={{0,4},{2,6},{4,0},{6,2},{1,5},{3,7},{5,1},{7,3},{8,12},{10,14},{12... | collective-permute-start | bytes 1179656 | tf_op jit(solution)/shard_map/ppermute | solution.py:27
  37.9 23.4 %collective-permute-start.11 = (bf16[128,1536]{1,0:T(8,128)(2,1)S(1)}, bf16[128,1536]{1,0:T(8,128)(2,1)S(1)}, u32[]{:S(2)}, u32[]{:S(2)}) collective-permute-start(bf16[128,1536]{1,0:T(8,128)(2,1)S(1)} %get-tuple-element.318), channel_id=1, source_target_pairs={{0,4},{2,6},{4,0},{6,2},{1,5},{3,7},{5,1},{7,3},{8,12},{10,14},{12... | collective-permute-start | bytes 1179656 | tf_op jit(solution)/shard_map/ppermute | solution.py:27
  39.4 21.8 %collective-permute-start.9 = (bf16[128,1536]{1,0:T(8,128)(2,1)S(1)}, bf16[128,1536]{1,0:T(8,128)(2,1)S(1)}, u32[]{:S(2)}, u32[]{:S(2)}) collective-permute-start(bf16[128,1536]{1,0:T(8,128)(2,1)S(1)} %get-tuple-element.294), channel_id=1, source_target_pairs={{0,4},{2,6},{4,0},{6,2},{1,5},{3,7},{5,1},{7,3},{8,12},{10,14},{12... | collective-permute-start | bytes 1179656 | tf_op jit(solution)/shard_map/ppermute | solution.py:27
  44.8 19.2 %collective-permute-start.7 = (bf16[128,1536]{1,0:T(8,128)(2,1)S(1)}, bf16[128,1536]{1,0:T(8,128)(2,1)S(1)}, u32[]{:S(2)}, u32[]{:S(2)}) collective-permute-start(bf16[128,1536]{1,0:T(8,128)(2,1)S(1)} %get-tuple-element.284), channel_id=1, source_target_pairs={{0,1},{1,0},{2,3},{3,2},{4,5},{5,4},{6,7},{7,6},{8,9},{9,8},{10,11... | collective-permute-start | bytes 1179656 | tf_op jit(solution)/shard_map/ppermute | solution.py:27
  45.2 18.4 %collective-permute-start.8 = (bf16[128,1536]{1,0:T(8,128)(2,1)S(1)}, bf16[128,1536]{1,0:T(8,128)(2,1)S(1)}, u32[]{:S(2)}, u32[]{:S(2)}) collective-permute-start(bf16[128,1536]{1,0:T(8,128)(2,1)S(1)} %get-tuple-element.282), channel_id=1, source_target_pairs={{0,1},{1,0},{2,3},{3,2},{4,5},{5,4},{6,7},{7,6},{8,9},{9,8},{10,11... | collective-permute-start | bytes 1179656 | tf_op jit(solution)/shard_map/ppermute | solution.py:27
  61.3 20.8 %collective-permute-start.12 = (bf16[128,1536]{1,0:T(8,128)(2,1)S(1)}, bf16[128,1536]{1,0:T(8,128)(2,1)S(1)}, u32[]{:S(2)}, u32[]{:S(2)}) collective-permute-start(bf16[128,1536]{1,0:T(8,128)(2,1)S(1)} %broadcast_select_fusion.4), channel_id=1, source_target_pairs={{0,1},{1,0},{2,3},{3,2},{4,5},{5,4},{6,7},{7,6},{8,9},{9,8},{10,11... | collective-permute-start | bytes 1179656 | tf_op jit(solution)/shard_map/ppermute | solution.py:27
  61.7 18.8 %collective-permute-start.10 = (bf16[128,1536]{1,0:T(8,128)(2,1)S(1)}, bf16[128,1536]{1,0:T(8,128)(2,1)S(1)}, u32[]{:S(2)}, u32[]{:S(2)}) collective-permute-start(bf16[128,1536]{1,0:T(8,128)(2,1)S(1)} %get-tuple-element.286), channel_id=1, source_target_pairs={{0,1},{1,0},{2,3},{3,2},{4,5},{5,4},{6,7},{7,6},{8,9},{9,8},{10,11... | collective-permute-start | bytes 1179656 | tf_op jit(solution)/shard_map/ppermute | solution.py:27
  89.7 5.0 %collective-permute-start.15 = (bf16[512,128]{1,0:T(8,128)(2,1)S(1)}, bf16[512,128]{1,0:T(8,128)(2,1)S(1)}, u32[]{:S(2)}, u32[]{:S(2)}) collective-permute-start(bf16[512,128]{1,0:T(8,128)(2,1)S(1)} %pad_maximum_fusion.7), channel_id=1, source_target_pairs={{0,1},{5,4},{4,0},{1,5},{2,3},{7,6},{6,2},{3,7},{8,9},{13,12},{12,... | collective-permute-start | bytes 393224 | tf_op jit(solution)/shard_map/ppermute | solution.py:187
  91.2 8.0 %collective-permute-start.18 = (bf16[512,128]{1,0:T(8,128)(2,1)S(1)}, bf16[512,128]{1,0:T(8,128)(2,1)S(1)}, u32[]{:S(2)}, u32[]{:S(2)}) collective-permute-start(bf16[512,128]{1,0:T(8,128)(2,1)S(1)} %pad_maximum_fusion.7), channel_id=1, source_target_pairs={{4,1},{1,4},{6,3},{3,6},{12,9},{9,12},{14,11},{11,14},{20,17},{17,... | collective-permute-start | bytes 393224 | tf_op jit(solution)/shard_map/ppermute | solution.py:188
  94.7 9.0 %collective-permute-start.16 = (bf16[512,384]{1,0:T(8,128)(2,1)S(1)}, bf16[512,384]{1,0:T(8,128)(2,1)S(1)}, u32[]{:S(2)}, u32[]{:S(2)}) collective-permute-start(bf16[512,384]{1,0:T(8,128)(2,1)S(1)} %pad_maximum_fusion.4), channel_id=1, source_target_pairs={{0,1},{5,4},{4,0},{1,5},{2,3},{7,6},{6,2},{3,7},{8,9},{13,12},{12,... | collective-permute-start | bytes 1179656 | tf_op jit(solution)/shard_map/ppermute | solution.py:187
  96.2 11.4 %collective-permute-start.17 = (bf16[512,384]{1,0:T(8,128)(2,1)S(1)}, bf16[512,384]{1,0:T(8,128)(2,1)S(1)}, u32[]{:S(2)}, u32[]{:S(2)}) collective-permute-start(bf16[512,384]{1,0:T(8,128)(2,1)S(1)} %pad_maximum_fusion.4), channel_id=1, source_target_pairs={{4,1},{1,4},{6,3},{3,6},{12,9},{9,12},{14,11},{11,14},{20,17},{17,... | collective-permute-start | bytes 1179656 | tf_op jit(solution)/shard_map/ppermute | solution.py:188
  109.8 13.2 %collective-permute-start.19 = (bf16[1536,128]{1,0:T(8,128)(2,1)S(1)}, bf16[1536,128]{1,0:T(8,128)(2,1)S(1)}, u32[]{:S(2)}, u32[]{:S(2)}) collective-permute-start(bf16[1536,128]{1,0:T(8,128)(2,1)S(1)} %get-tuple-element.259), channel_id=1, source_target_pairs={{0,8},{24,16},{1,9},{25,17},{2,10},{26,18},{3,11},{27,19},{4,12},{... | collective-permute-start | bytes 1179656 | tf_op jit(solution)/shard_map/ppermute | solution.py:52
  113.5 18.0 %collective-permute-start.21 = (bf16[1536,128]{1,0:T(8,128)(2,1)S(1)}, bf16[1536,128]{1,0:T(8,128)(2,1)S(1)}, u32[]{:S(2)}, u32[]{:S(2)}) collective-permute-start(bf16[1536,128]{1,0:T(8,128)(2,1)S(1)} %get-tuple-element.258), channel_id=1, source_target_pairs={{0,8},{24,16},{1,9},{25,17},{2,10},{26,18},{3,11},{27,19},{4,12},{... | collective-permute-start | bytes 1179656 | tf_op jit(solution)/shard_map/ppermute | solution.py:52
  117.0 18.8 %collective-permute-start.26 = (bf16[1536,128]{1,0:T(8,128)(2,1)S(1)}, bf16[1536,128]{1,0:T(8,128)(2,1)S(1)}, u32[]{:S(2)}, u32[]{:S(2)}) collective-permute-start(bf16[1536,128]{1,0:T(8,128)(2,1)S(1)} %slice.551), channel_id=1, source_target_pairs={{0,8},{24,16},{1,9},{25,17},{2,10},{26,18},{3,11},{27,19},{4,12},{... | collective-permute-start | bytes 1179656 | tf_op jit(solution)/shard_map/ppermute | solution.py:52
  123.0 25.5 %collective-permute-start.23 = (bf16[512,512]{1,0:T(8,128)(2,1)S(1)}, bf16[512,512]{1,0:T(8,128)(2,1)S(1)}, u32[]{:S(2)}, u32[]{:S(2)}) collective-permute-start(bf16[512,512]{1,0:T(8,128)(2,1)S(1)} %pad_maximum_fusion.2), channel_id=1, source_target_pairs={{0,1},{5,4},{4,0},{1,5},{2,3},{7,6},{6,2},{3,7},{8,9},{13,12},{12,... | collective-permute-start | bytes 1572872 | tf_op jit(solution)/shard_map/ppermute | solution.py:187
  123.0 25.5 %collective-permute-start.24 = (bf16[512,512]{1,0:T(8,128)(2,1)S(1)}, bf16[512,512]{1,0:T(8,128)(2,1)S(1)}, u32[]{:S(2)}, u32[]{:S(2)}) collective-permute-start(bf16[512,512]{1,0:T(8,128)(2,1)S(1)} %pad_maximum_fusion.2), channel_id=1, source_target_pairs={{4,1},{1,4},{6,3},{3,6},{12,9},{9,12},{14,11},{11,14},{20,17},{17,... | collective-permute-start | bytes 1572872 | tf_op jit(solution)/shard_map/ppermute | solution.py:188
  126.7 5.6 %collective-permute-start.20 = (bf16[1536,128]{1,0:T(8,128)(2,1)S(1)}, bf16[1536,128]{1,0:T(8,128)(2,1)S(1)}, u32[]{:S(2)}, u32[]{:S(2)}) collective-permute-start(bf16[1536,128]{1,0:T(8,128)(2,1)S(1)} %add_convert_fusion.35), channel_id=1, source_target_pairs={{8,16},{16,8},{9,17},{17,9},{10,18},{18,10},{11,19},{19,11},{12,20... | collective-permute-start | bytes 1179656 | tf_op jit(solution)/shard_map/ppermute | solution.py:60
  131.5 4.4 %collective-permute-start.25 = (bf16[1536,128]{1,0:T(8,128)(2,1)S(1)}, bf16[1536,128]{1,0:T(8,128)(2,1)S(1)}, u32[]{:S(2)}, u32[]{:S(2)}) collective-permute-start(bf16[1536,128]{1,0:T(8,128)(2,1)S(1)} %add_convert_fusion.34), channel_id=1, source_target_pairs={{8,16},{16,8},{9,17},{17,9},{10,18},{18,10},{11,19},{19,11},{12,20... | collective-permute-start | bytes 1179656 | tf_op jit(solution)/shard_map/ppermute | solution.py:60
  135.9 12.8 %collective-permute-start.33 = (bf16[512,512]{1,0:T(8,128)(2,1)S(1)}, bf16[512,512]{1,0:T(8,128)(2,1)S(1)}, u32[]{:S(2)}, u32[]{:S(2)}) collective-permute-start(bf16[512,512]{1,0:T(8,128)(2,1)S(1)} %pad_maximum_fusion.3), channel_id=1, source_target_pairs={{0,1},{1,0},{2,3},{3,2},{4,5},{5,4},{6,7},{7,6},{8,9},{9,8},{10,11... | collective-permute-start | bytes 1572872 | tf_op jit(solution)/shard_map/ppermute | solution.py:27
  136.0 40.0 %collective-permute-start.22 = (bf16[1536,128]{1,0:T(8,128)(2,1)S(1)}, bf16[1536,128]{1,0:T(8,128)(2,1)S(1)}, u32[]{:S(2)}, u32[]{:S(2)}) collective-permute-start(bf16[1536,128]{1,0:T(8,128)(2,1)S(1)} %fusion.88), channel_id=1, source_target_pairs={{0,8},{24,16},{8,0},{16,24},{1,9},{25,17},{9,1},{17,25},{2,10},{26... | collective-permute-start | bytes 1179656 | tf_op jit(solution)/shard_map/ppermute | solution.py:52
  147.6 29.2 %collective-permute-start.27 = (bf16[1536,128]{1,0:T(8,128)(2,1)S(1)}, bf16[1536,128]{1,0:T(8,128)(2,1)S(1)}, u32[]{:S(2)}, u32[]{:S(2)}) collective-permute-start(bf16[1536,128]{1,0:T(8,128)(2,1)S(1)} %add_convert_fusion.32), channel_id=1, source_target_pairs={{8,16},{16,8},{9,17},{17,9},{10,18},{18,10},{11,19},{19,11},{12,20... | collective-permute-start | bytes 1179656 | tf_op jit(solution)/shard_map/ppermute | solution.py:60
  148.8 9.2 %collective-permute-start.34 = (bf16[512,512]{1,0:T(8,128)(2,1)S(1)}, bf16[512,512]{1,0:T(8,128)(2,1)S(1)}, u32[]{:S(2)}, u32[]{:S(2)}) collective-permute-start(bf16[512,512]{1,0:T(8,128)(2,1)S(1)} %get-tuple-element.274), channel_id=1, source_target_pairs={{0,4},{2,6},{4,0},{6,2},{1,5},{3,7},{5,1},{7,3},{8,12},{10,14},{12... | collective-permute-start | bytes 1572872 | tf_op jit(solution)/shard_map/ppermute | solution.py:27
  167.9 17.3 %collective-permute-start.28 = (bf16[1536,128]{1,0:T(8,128)(2,1)S(1)}, bf16[1536,128]{1,0:T(8,128)(2,1)S(1)}, u32[]{:S(2)}, u32[]{:S(2)}) collective-permute-start(bf16[1536,128]{1,0:T(8,128)(2,1)S(1)} %fusion.89), channel_id=1, source_target_pairs={{0,8},{24,16},{8,0},{16,24},{1,9},{25,17},{9,1},{17,25},{2,10},{26... | collective-permute-start | bytes 1179656 | tf_op jit(solution)/shard_map/ppermute | solution.py:52
  176.2 9.8 %collective-permute-start.29 = (bf16[1536,128]{1,0:T(8,128)(2,1)S(1)}, bf16[1536,128]{1,0:T(8,128)(2,1)S(1)}, u32[]{:S(2)}, u32[]{:S(2)}) collective-permute-start(bf16[1536,128]{1,0:T(8,128)(2,1)S(1)} %add_convert_fusion.30), channel_id=1, source_target_pairs={{8,16},{16,8},{9,17},{17,9},{10,18},{18,10},{11,19},{19,11},{12,20... | collective-permute-start | bytes 1179656 | tf_op jit(solution)/shard_map/ppermute | solution.py:60
  177.0 16.6 %collective-permute-start.30 = (bf16[1536,128]{1,0:T(8,128)(2,1)S(1)}, bf16[1536,128]{1,0:T(8,128)(2,1)S(1)}, u32[]{:S(2)}, u32[]{:S(2)}) collective-permute-start(bf16[1536,128]{1,0:T(8,128)(2,1)S(1)} %fusion.90), channel_id=1, source_target_pairs={{0,8},{24,16},{8,0},{16,24},{1,9},{25,17},{9,1},{17,25},{2,10},{26... | collective-permute-start | bytes 1179656 | tf_op jit(solution)/shard_map/ppermute | solution.py:52
  185.3 9.6 %collective-permute-start.31 = (bf16[1536,128]{1,0:T(8,128)(2,1)S(1)}, bf16[1536,128]{1,0:T(8,128)(2,1)S(1)}, u32[]{:S(2)}, u32[]{:S(2)}) collective-permute-start(bf16[1536,128]{1,0:T(8,128)(2,1)S(1)} %add_convert_fusion.28), channel_id=1, source_target_pairs={{8,16},{16,8},{9,17},{17,9},{10,18},{18,10},{11,19},{19,11},{12,20... | collective-permute-start | bytes 1179656 | tf_op jit(solution)/shard_map/ppermute | solution.py:60
  186.2 15.9 %collective-permute-start.32 = (bf16[1536,128]{1,0:T(8,128)(2,1)S(1)}, bf16[1536,128]{1,0:T(8,128)(2,1)S(1)}, u32[]{:S(2)}, u32[]{:S(2)}) collective-permute-start(bf16[1536,128]{1,0:T(8,128)(2,1)S(1)} %fusion.91), channel_id=1, source_target_pairs={{0,8},{24,16},{8,0},{16,24},{1,9},{25,17},{9,1},{17,25},{2,10},{26... | collective-permute-start | bytes 1179656 | tf_op jit(solution)/shard_map/ppermute | solution.py:52
  193.7 9.1 %collective-permute-start.35 = (bf16[1536,128]{1,0:T(8,128)(2,1)S(1)}, bf16[1536,128]{1,0:T(8,128)(2,1)S(1)}, u32[]{:S(2)}, u32[]{:S(2)}) collective-permute-start(bf16[1536,128]{1,0:T(8,128)(2,1)S(1)} %add_convert_fusion.26), channel_id=1, source_target_pairs={{8,16},{16,8},{9,17},{17,9},{10,18},{18,10},{11,19},{19,11},{12,20... | collective-permute-start | bytes 1179656 | tf_op jit(solution)/shard_map/ppermute | solution.py:60
  195.1 15.4 %collective-permute-start.36 = (bf16[1536,128]{1,0:T(8,128)(2,1)S(1)}, bf16[1536,128]{1,0:T(8,128)(2,1)S(1)}, u32[]{:S(2)}, u32[]{:S(2)}) collective-permute-start(bf16[1536,128]{1,0:T(8,128)(2,1)S(1)} %fusion.92), channel_id=1, source_target_pairs={{0,8},{24,16},{8,0},{16,24},{1,9},{25,17},{9,1},{17,25},{2,10},{26... | collective-permute-start | bytes 1179656 | tf_op jit(solution)/shard_map/ppermute | solution.py:52
  202.2 9.1 %collective-permute-start.37 = (bf16[1536,128]{1,0:T(8,128)(2,1)S(1)}, bf16[1536,128]{1,0:T(8,128)(2,1)S(1)}, u32[]{:S(2)}, u32[]{:S(2)}) collective-permute-start(bf16[1536,128]{1,0:T(8,128)(2,1)S(1)} %add_convert_fusion.24), channel_id=1, source_target_pairs={{8,16},{16,8},{9,17},{17,9},{10,18},{18,10},{11,19},{19,11},{12,20... | collective-permute-start | bytes 1179656 | tf_op jit(solution)/shard_map/ppermute | solution.py:60
  203.0 15.9 %collective-permute-start.38 = (bf16[1536,128]{1,0:T(8,128)(2,1)S(1)}, bf16[1536,128]{1,0:T(8,128)(2,1)S(1)}, u32[]{:S(2)}, u32[]{:S(2)}) collective-permute-start(bf16[1536,128]{1,0:T(8,128)(2,1)S(1)} %fusion.93), channel_id=1, source_target_pairs={{0,8},{24,16},{8,0},{16,24},{1,9},{25,17},{9,1},{17,25},{2,10},{26... | collective-permute-start | bytes 1179656 | tf_op jit(solution)/shard_map/ppermute | solution.py:52
  210.6 9.6 %collective-permute-start.39 = (bf16[1536,128]{1,0:T(8,128)(2,1)S(1)}, bf16[1536,128]{1,0:T(8,128)(2,1)S(1)}, u32[]{:S(2)}, u32[]{:S(2)}) collective-permute-start(bf16[1536,128]{1,0:T(8,128)(2,1)S(1)} %add_convert_fusion.22), channel_id=1, source_target_pairs={{8,16},{16,8},{9,17},{17,9},{10,18},{18,10},{11,19},{19,11},{12,20... | collective-permute-start | bytes 1179656 | tf_op jit(solution)/shard_map/ppermute | solution.py:60
  211.5 15.9 %collective-permute-start.40 = (bf16[1536,128]{1,0:T(8,128)(2,1)S(1)}, bf16[1536,128]{1,0:T(8,128)(2,1)S(1)}, u32[]{:S(2)}, u32[]{:S(2)}) collective-permute-start(bf16[1536,128]{1,0:T(8,128)(2,1)S(1)} %fusion.94), channel_id=1, source_target_pairs={{0,8},{24,16},{8,0},{16,24},{1,9},{25,17},{9,1},{17,25},{2,10},{26... | collective-permute-start | bytes 1179656 | tf_op jit(solution)/shard_map/ppermute | solution.py:52
  219.0 9.4 %collective-permute-start.41 = (bf16[1536,128]{1,0:T(8,128)(2,1)S(1)}, bf16[1536,128]{1,0:T(8,128)(2,1)S(1)}, u32[]{:S(2)}, u32[]{:S(2)}) collective-permute-start(bf16[1536,128]{1,0:T(8,128)(2,1)S(1)} %add_convert_fusion.20), channel_id=1, source_target_pairs={{8,16},{16,8},{9,17},{17,9},{10,18},{18,10},{11,19},{19,11},{12,20... | collective-permute-start | bytes 1179656 | tf_op jit(solution)/shard_map/ppermute | solution.py:60
  220.3 15.4 %collective-permute-start.42 = (bf16[1536,128]{1,0:T(8,128)(2,1)S(1)}, bf16[1536,128]{1,0:T(8,128)(2,1)S(1)}, u32[]{:S(2)}, u32[]{:S(2)}) collective-permute-start(bf16[1536,128]{1,0:T(8,128)(2,1)S(1)} %fusion.95), channel_id=1, source_target_pairs={{0,8},{24,16},{8,0},{16,24},{1,9},{25,17},{9,1},{17,25},{2,10},{26... | collective-permute-start | bytes 1179656 | tf_op jit(solution)/shard_map/ppermute | solution.py:52
  227.4 9.1 %collective-permute-start.43 = (bf16[1536,128]{1,0:T(8,128)(2,1)S(1)}, bf16[1536,128]{1,0:T(8,128)(2,1)S(1)}, u32[]{:S(2)}, u32[]{:S(2)}) collective-permute-start(bf16[1536,128]{1,0:T(8,128)(2,1)S(1)} %add_convert_fusion.18), channel_id=1, source_target_pairs={{8,16},{16,8},{9,17},{17,9},{10,18},{18,10},{11,19},{19,11},{12,20... | collective-permute-start | bytes 1179656 | tf_op jit(solution)/shard_map/ppermute | solution.py:60
  228.6 15.2 %collective-permute-start.44 = (bf16[1536,128]{1,0:T(8,128)(2,1)S(1)}, bf16[1536,128]{1,0:T(8,128)(2,1)S(1)}, u32[]{:S(2)}, u32[]{:S(2)}) collective-permute-start(bf16[1536,128]{1,0:T(8,128)(2,1)S(1)} %fusion.96), channel_id=1, source_target_pairs={{0,8},{24,16},{8,0},{16,24},{1,9},{25,17},{9,1},{17,25},{2,10},{26... | collective-permute-start | bytes 1179656 | tf_op jit(solution)/shard_map/ppermute | solution.py:52
  235.9 9.1 %collective-permute-start.45 = (bf16[1536,128]{1,0:T(8,128)(2,1)S(1)}, bf16[1536,128]{1,0:T(8,128)(2,1)S(1)}, u32[]{:S(2)}, u32[]{:S(2)}) collective-permute-start(bf16[1536,128]{1,0:T(8,128)(2,1)S(1)} %add_convert_fusion.16), channel_id=1, source_target_pairs={{8,16},{16,8},{9,17},{17,9},{10,18},{18,10},{11,19},{19,11},{12,20... | collective-permute-start | bytes 1179656 | tf_op jit(solution)/shard_map/ppermute | solution.py:60
  236.7 12.8 %collective-permute-start.46 = (bf16[1536,128]{1,0:T(8,128)(2,1)S(1)}, bf16[1536,128]{1,0:T(8,128)(2,1)S(1)}, u32[]{:S(2)}, u32[]{:S(2)}) collective-permute-start(bf16[1536,128]{1,0:T(8,128)(2,1)S(1)} %add_convert_fusion.15), channel_id=1, source_target_pairs={{8,0},{16,24},{9,1},{17,25},{10,2},{18,26},{11,3},{19,27},{12,4},{... | collective-permute-start | bytes 1179656 | tf_op jit(solution)/shard_map/ppermute | solution.py:52
  243.9 5.7 %collective-permute-start.47 = (bf16[1536,128]{1,0:T(8,128)(2,1)S(1)}, bf16[1536,128]{1,0:T(8,128)(2,1)S(1)}, u32[]{:S(2)}, u32[]{:S(2)}) collective-permute-start(bf16[1536,128]{1,0:T(8,128)(2,1)S(1)} %add_convert_fusion.14), channel_id=1, source_target_pairs={{8,16},{16,8},{9,17},{17,9},{10,18},{18,10},{11,19},{19,11},{12,20... | collective-permute-start | bytes 1179656 | tf_op jit(solution)/shard_map/ppermute | solution.py:60
  245.1 9.7 %collective-permute-start.48 = (bf16[1536,128]{1,0:T(8,128)(2,1)S(1)}, bf16[1536,128]{1,0:T(8,128)(2,1)S(1)}, u32[]{:S(2)}, u32[]{:S(2)}) collective-permute-start(bf16[1536,128]{1,0:T(8,128)(2,1)S(1)} %add_convert_fusion.13), channel_id=1, source_target_pairs={{8,0},{16,24},{9,1},{17,25},{10,2},{18,26},{11,3},{19,27},{12,4},{... | collective-permute-start | bytes 1179656 | tf_op jit(solution)/shard_map/ppermute | solution.py:52
  249.6 10.6 %collective-permute-start.49 = (bf16[1536,128]{1,0:T(8,128)(2,1)S(1)}, bf16[1536,128]{1,0:T(8,128)(2,1)S(1)}, u32[]{:S(2)}, u32[]{:S(2)}) collective-permute-start(bf16[1536,128]{1,0:T(8,128)(2,1)S(1)} %add_convert_fusion.12), channel_id=1, source_target_pairs={{8,0},{16,24},{9,1},{17,25},{10,2},{18,26},{11,3},{19,27},{12,4},{... | collective-permute-start | bytes 1179656 | tf_op jit(solution)/shard_map/ppermute | solution.py:52
  (16 other events, 169.8 us)

commit v7 on v6

--- a/solution.py
+++ b/solution.py
@@ -99,31 +99,23 @@
     near_blocks = [context] + list(held[1:group])
     residual_parts, cotangent_parts = held[group : 2 * group], held[2 * group :]
     far_blocks = [held[0]] + [swap(held[0], "fsdp", r) for r in range(1, group)]
-    far_outs, near_out = [], [[None] * pieces for r in range(group)]
-    last = None
+    far_outs, near_first = [], None
     for r in range(group):
-        for p in range(pieces):
-            beside = (r + 1) % group
-            far = far_blocks[r]
-            if last:
-                far, near_out[last[0]][last[1]] = together(far, near_out[last[0]][last[1]])
-            both = project(
-                jnp.concatenate([block[p * rows : (p + 1) * rows] for block in (far, near_blocks[beside])], axis=0)
-            )
-            far_outs.append(swap(both[:rows], "fsdp", group))
-            near_out[beside][p] = both[rows:]
-            last = (beside, p)
+        blocks = [far_blocks[r]] + ([context[:rows]] if r == group - 1 else [])
+        out = project(jnp.concatenate(blocks, axis=0))
+        far_outs += [swap(out[p * rows : (p + 1) * rows], "fsdp", group) for p in range(pieces)]
+        near_first = out[tok_rows:]
 
     gain_part = lax.dynamic_slice_in_dim(gain, t * (width // 2) + low * cols, cols).astype(f32)
 
     keeps, arrivals = [], []
     for r in range(group):
         for p in range(pieces):
-            far_out, own_out = far_outs[r * pieces + p], near_out[r][p]
+            far_out, own_out = far_outs[r * pieces + p], near_first
             if keeps:
-                far_out, own_out, keeps[-1] = together(far_out, own_out, keeps[-1])
-            else:
-                far_out, own_out = together(far_out, own_out)
+                block, keeps[-1] = together(near_blocks[r], keeps[-1])
+                own_out = project(block[p * rows : (p + 1) * rows])
+            far_out, own_out = together(far_out, own_out)
             keeps.append(jnp.where(near, own_out, far_out))
             arrivals.append(swap(jnp.where(near, far_out, own_out), "tp", 1))
     hidden, weighted, sums = [], [], []
@@ -153,9 +145,7 @@
     context_all = jnp.concatenate(near_blocks + far_blocks, axis=0)
     narrow = 128
     units = cols // narrow
-    widths = [1, 3]
-    while sum(widths) < units:
-        widths.append(min(4, units - sum(widths)))
+    widths = [1, 3, units - 4]
     def at(h, q, x):
         return (h * group + q) * 2 + x
 
@@ -167,9 +157,9 @@
 
     islands = lax.axis_size("island")
     line = IslandLine(units)
-    parts, rings = [], []
-
-    def add_parts(c, after):
+    parts, locals_, rings, crosses = [], [], [], []
+
+    def move(c):
         cols_at = slice(sum(widths[:c]) * narrow, sum(widths[: c + 1]) * narrow)
         d_local = jnp.concatenate(
             [
@@ -179,40 +169,28 @@
             ],
             axis=0,
         ).astype(bf16)
-        if c < 3:
-            if c == 1:
-                d_local, rings[0] = together(d_local, rings[0])
-            elif c == 2 and after in line.edge:
-                d_local, line.edge[after] = together(d_local, line.edge[after])
-            rings.append(lax.ppermute(d_local, ("fsdp", "tp"), ring_pairs))
-            cross = lax.ppermute(d_local, ("fsdp", "tp"), cross_pairs)
-            blocks = (d_local, cross)
-        else:
-            if after in line.sums:
-                d_local, line.sums[after] = together(d_local, line.sums[after])
-            came = swap(d_local, "tp", 1)
-            far = swap(jnp.where(near, came, d_local), "fsdp", group)
-            rings.append(None)
-            blocks = (jnp.where(near, d_local, came), far)
-        return cols_at, blocks
-
-    def add_pseudo(c, cols_at, blocks):
-        if rings[c] is None:
-            d_near, d_far = blocks
-        else:
-            d_near = jnp.where(near, blocks[0], rings[c])
-            d_far = jnp.where(near, rings[c], blocks[1])
+        if c == 1:
+            d_local, rings[0] = together(d_local, rings[0])
+        elif c == 2:
+            d_local, crosses[0] = together(d_local, crosses[0])
+        locals_.append(d_local)
+        rings.append(lax.ppermute(d_local, ("fsdp", "tp"), ring_pairs))
+        crosses.append(lax.ppermute(d_local, ("fsdp", "tp"), cross_pairs))
+
+    def add_pseudo(c):
+        start = sum(widths[:c]) * narrow
+        d_near = jnp.where(near, locals_[c], rings[c])
+        d_far = jnp.where(near, rings[c], crosses[c])
         d_all = jnp.concatenate([d_near, d_far], axis=0)
         cuts = list(range(0, widths[c], 2)) if widths[c] % 2 == 0 else [0] + list(range(1, widths[c], 2))
         for lo, hi in zip(cuts, cuts[1:] + [widths[c]]):
-            at_cols = slice(cols_at.start + lo * narrow, cols_at.start + hi * narrow)
+            at_cols = slice(start + lo * narrow, start + hi * narrow)
+            piece, first, second, outer = together(
+                d_all[:, lo * narrow : hi * narrow], first_moment, second_moment, weight
+            )
             grad = lax.dot_general(
-                context_all,
-                lax.optimization_barrier(d_all[:, lo * narrow : hi * narrow]),
-                (((0,), (0,)), ((), ())),
-                preferred_element_type=f32,
+                context_all, piece, (((0,), (0,)), ((), ())), preferred_element_type=f32
             ) / (tok_rows * fsdp_count)
-            first, second, outer = together(first_moment, second_moment, weight)
             first = first[0, :, at_cols].astype(f32)
             second = second[0, :, at_cols].astype(f32)
             m_new = beta_one * first + (1.0 - beta_one) * grad
@@ -223,22 +201,18 @@
             pseudo = lax.optimization_barrier(update.astype(bf16))
             parts.extend(pseudo[:, u * narrow : (u + 1) * narrow] for u in range(hi - lo))
 
-    first, second = add_parts(0, None), add_parts(1, None)
-    add_pseudo(0, *first)
-    add_pseudo(1, *second)
+    for c in range(len(widths)):
+        move(c)
+    for c in range(len(widths)):
+        add_pseudo(c)
     if islands == 4:
         line.part.update(enumerate(parts))
         for s in range(2):
             line.send_outer(s)
         for s in range(units + 3):
-            for c in {0: [2], 3: range(3, len(widths))}.get(s, []):
-                add_pseudo(c, *add_parts(c, max(s - 1, 0)))
-            line.part.update(enumerate(parts))
             line.step(s)
         sums = [line.totals[k] for k in range(units)]
     else:
-        for c in range(2, len(widths)):
-            add_pseudo(c, *add_parts(c, None))
         sums = [lax.psum(part, "island") for part in parts]
     momentum_out, step_out = [], []
     for k, total in enumerate(sums):

time: 270 us -> 247 us (0.915)
  waiting for transfers between devices: 117 us -> 101 us
  matrix products: 27.2 us -> 22.2 us
    ppermute x15, waiting for transfers between devices: 46.3 us -> 36.2 us  [send_outer(): self.edge[s] = lax.ppermute(payload, 'island', pairs)]
    dot_general x7, matrix products: 19.2 us -> 13.8 us  [add_pseudo(): lax.dot_general(context_all, piece, (((0,), (0,)), ((), ())), preferred_e...]
    ppermute x6, waiting for transfers between devices: 7.82 us -> 4.49 us  [the longest x3 3.33 us: move(): crosses.append(lax.ppermute(d_local, ('fsdp', 'tp'), cross_pairs))]
    ppermute x17 -> x15, waiting for transfers between devices: 62.9 us -> 60.1 us  [swap(): return lax.ppermute(value, axis, [(i, i ^ bit) for i in range(count)])]
    ppermute x17 -> x15, starting transfers between devices: 12.3 us -> 11 us  [swap(): return lax.ppermute(value, axis, [(i, i ^ bit) for i in range(count)])]
    unnamed x31 -> x29, local copies, waits for them, and re-layouts: 5.84 us -> 7.12 us
    dot_general x4 -> x5, matrix products: 8 us -> 8.34 us  [project(): jnp.dot(block, weight, preferred_element_type=f32).astype(bf16)]
  transfers between devices with their start and end apart: 50 -> 48, of which waited for: 26 -> 22; matrix products, arithmetic and copies ran while one was open for 16% -> 16% of each run, Pallas kernels for 0% -> 0%
where the time goes in v7:
time: 247 us; the launch traced here: 246 us
  waiting for transfers between devices  101 us (41%)
  starting transfers between devices  95.4 us (39%)
  matrix products  22.2 us (9%)
  other arithmetic  15.5 us (6%)
  local copies, waits for them, and re-layouts  10.9 us (4%)
    ppermute x15, starting transfers between devices, send_outer(): self.edge[s] = lax.ppermute(payload, 'island', pairs)  64.5 us
    ppermute x15, waiting for transfers between devices, swap(): return lax.ppermute(value, axis, [(i, i ^ bit) for i in range(count)])  60.1 us
    ppermute x15, waiting for transfers between devices, send_outer(): self.edge[s] = lax.ppermute(payload, 'island', pairs)  36.2 us
    dot_general x7, matrix products, add_pseudo(): lax.dot_general(context_all, piece, (((0,), (0,)), ((), ())), preferred_e...  13.8 us
    ppermute x15, starting transfers between devices, swap(): return lax.ppermute(value, axis, [(i, i ^ bit) for i in range(count)])  11 us
    ppermute x12, starting transfers between devices, step(): self.mid[s] = lax.ppermute(self.sums[s], 'island', [(1, 2), (2, 1)])  8.45 us
    dot_general x5, matrix products, project(): jnp.dot(block, weight, preferred_element_type=f32).astype(bf16)  8.34 us
    ppermute x3, starting transfers between devices, move(): crosses.append(lax.ppermute(d_local, ('fsdp', 'tp'), cross_pairs))  8.34 us
  transfers between devices with their start and end apart: 48, of which 22 were waited for; matrix products, arithmetic and copies ran while one was open for 16% of the time, Pallas kernels for 0%

profile of v7, /device:TPU:2, one launch (start us, length us, event | category | flops | bytes accessed | tf_op | source)
XLA Modules:
  0.0 246.3 jit_solution(11553536242867478941)
XLA Ops:
  0.6 1.6 collective-permute-start
  2.2 2.5 %constant_dynamic-slice_fusion.2 = (bf16[256,1536]{1,0:T(8,128)(2,1)}, bf16[256,1536]{1,0:T(8,128)(2,1)S(1)}) fusion(bf16[256,3072]{1,0:T(8,128)(2,1)} %param.9, s32[]{:T(128)S(6)} %select_n.188, s32[]{:T(128)S(6)} %select_n.187), kind=kLoop, calls=%fused_computation.292 | loop fusion | bytes 3145736 | tf_op jit(solution)/shard_map/dynamic_slice | solution.py:94
  7.1 13.2 %collective-permute-done = bf16[256,1536]{1,0:T(8,128)(2,1)} collective-permute-done((bf16[256,1536]{1,0:T(8,128)(2,1)}, bf16[256,1536]{1,0:T(8,128)(2,1)}, u32[]{:S(2)}, u32[]{:S(2)}) %collective-permute-start) | collective-permute-done | bytes 786464 | tf_op jit(solution)/shard_map/ppermute | solution.py:27
  20.4 4.0 %convolution_convert_fusion.1 = bf16[256,1536]{1,0:T(8,128)(2,1)S(1)} fusion(bf16[256,1536]{1,0:T(8,128)(2,1)} %collective-permute-done, bf16[1536,1536]{1,0:T(8,128)(2,1)} %param.12), kind=kOutput, calls=%fused_computation.7 | convolution fusion | flops 1208352768 | bytes 6291456 | tf_op jit(solution)/shard_map/dot_general | solution.py:89
  24.5 1.6 collective-permute-start.4
  26.7 2.0 convolution_convert_fusion
  28.7 1.6 collective-permute-start.11
  30.8 14.1 %collective-permute-done.5 = bf16[128,1536]{1,0:T(8,128)(2,1)S(1)} collective-permute-done((bf16[128,1536]{1,0:T(8,128)(2,1)S(1)}, bf16[128,1536]{1,0:T(8,128)(2,1)S(1)}, u32[]{:S(2)}, u32[]{:S(2)}) %collective-permute-start.5) | collective-permute-done | bytes 393248 | tf_op jit(solution)/shard_map/ppermute | solution.py:27
  47.0 1.7 collective-permute-start.8
  48.7 12.6 %collective-permute-done.9 = bf16[128,1536]{1,0:T(8,128)(2,1)S(1)} collective-permute-done((bf16[128,1536]{1,0:T(8,128)(2,1)S(1)}, bf16[128,1536]{1,0:T(8,128)(2,1)S(1)}, u32[]{:S(2)}, u32[]{:S(2)}) %collective-permute-start.9) | collective-permute-done | bytes 393248 | tf_op jit(solution)/shard_map/ppermute | solution.py:27
  62.6 1.7 collective-permute-start.10
  64.3 1.8 collective-permute-done.8
  67.0 15.2 %collective-permute-done.10 = bf16[128,1536]{1,0:T(8,128)(2,1)S(1)} collective-permute-done((bf16[128,1536]{1,0:T(8,128)(2,1)S(1)}, bf16[128,1536]{1,0:T(8,128)(2,1)S(1)}, u32[]{:S(2)}, u32[]{:S(2)}) %collective-permute-start.10) | collective-permute-done | bytes 393248 | tf_op jit(solution)/shard_map/ppermute | solution.py:27
  82.2 1.5 multiply_reduce_fusion.3
  83.7 1.7 multiply_reduce_fusion.1
  87.4 3.2 %collective-permute-done.14 = f32[2,512]{1,0:T(2,128)S(1)} collective-permute-done((f32[2,512]{1,0:T(2,128)S(1)}, f32[2,512]{1,0:T(2,128)S(1)}, u32[]{:S(2)}, u32[]{:S(2)}) %collective-permute-start.14) | collective-permute-done | bytes 4128 | tf_op jit(solution)/shard_map/ppermute | solution.py:27
  91.7 1.6 collective-permute-start.15
  93.2 2.2 collective-permute-start.18
  96.7 1.5 collective-permute-start.16
  98.2 2.2 collective-permute-start.17
  101.0 4.0 %collective-permute-start.24 = (bf16[512,1024]{1,0:T(8,128)(2,1)S(1)}, bf16[512,1024]{1,0:T(8,128)(2,1)S(1)}, u32[]{:S(2)}, u32[]{:S(2)}) collective-permute-start(bf16[512,1024]{1,0:T(8,128)(2,1)S(1)} %pad_maximum_fusion), channel_id=1, source_target_pairs={{4,1},{1,4},{6,3},{3,6},{12,9},{9,12},{14,11},{11,14},{20,17},{17,... | collective-permute-start | bytes 3145736 | tf_op jit(solution)/shard_map/ppermute | solution.py:178
  106.6 3.7 %collective-permute-start.19 = (bf16[1536,128]{1,0:T(8,128)(2,1)S(1)}, bf16[1536,128]{1,0:T(8,128)(2,1)S(1)}, u32[]{:S(2)}, u32[]{:S(2)}) collective-permute-start(bf16[1536,128]{1,0:T(8,128)(2,1)S(1)} %fusion.62), channel_id=1, source_target_pairs={{0,8},{24,16},{1,9},{25,17},{2,10},{26,18},{3,11},{27,19},{4,12},{... | collective-permute-start | bytes 1179656 | tf_op jit(solution)/shard_map/ppermute | solution.py:52
  110.3 2.7 %collective-permute-done.17 = bf16[512,384]{1,0:T(8,128)(2,1)S(1)} collective-permute-done((bf16[512,384]{1,0:T(8,128)(2,1)S(1)}, bf16[512,384]{1,0:T(8,128)(2,1)S(1)}, u32[]{:S(2)}, u32[]{:S(2)}) %collective-permute-start.17) | collective-permute-done | bytes 393248 | tf_op jit(solution)/shard_map/ppermute | solution.py:178
  114.6 3.5 %collective-permute-start.21 = (bf16[1536,128]{1,0:T(8,128)(2,1)S(1)}, bf16[1536,128]{1,0:T(8,128)(2,1)S(1)}, u32[]{:S(2)}, u32[]{:S(2)}) collective-permute-start(bf16[1536,128]{1,0:T(8,128)(2,1)S(1)} %fusion.63), channel_id=1, source_target_pairs={{0,8},{24,16},{1,9},{25,17},{2,10},{26,18},{3,11},{27,19},{4,12},{... | collective-permute-start | bytes 1179656 | tf_op jit(solution)/shard_map/ppermute | solution.py:52
  118.2 1.5 collective-permute-done.19
  120.5 2.2 fusion.30
  122.7 7.2 %collective-permute-start.26 = (bf16[1536,128]{1,0:T(8,128)(2,1)S(1)}, bf16[1536,128]{1,0:T(8,128)(2,1)S(1)}, u32[]{:S(2)}, u32[]{:S(2)}) collective-permute-start(bf16[1536,128]{1,0:T(8,128)(2,1)S(1)} %slice.480), channel_id=1, source_target_pairs={{0,8},{24,16},{1,9},{25,17},{2,10},{26,18},{3,11},{27,19},{4,12},{... | collective-permute-start | bytes 1179656 | tf_op jit(solution)/shard_map/ppermute | solution.py:52
  130.9 5.3 %collective-permute-start.22 = (bf16[1536,128]{1,0:T(8,128)(2,1)S(1)}, bf16[1536,128]{1,0:T(8,128)(2,1)S(1)}, u32[]{:S(2)}, u32[]{:S(2)}) collective-permute-start(bf16[1536,128]{1,0:T(8,128)(2,1)S(1)} %fusion.88), channel_id=1, source_target_pairs={{0,8},{24,16},{8,0},{16,24},{1,9},{25,17},{9,1},{17,25},{2,10},{26... | collective-permute-start | bytes 1179656 | tf_op jit(solution)/shard_map/ppermute | solution.py:52
  138.2 2.2 fusion.31
  140.4 2.2 fusion.32
  142.6 2.2 fusion.33
  144.8 2.2 fusion.34
  147.2 5.3 %collective-permute-start.28 = (bf16[1536,128]{1,0:T(8,128)(2,1)S(1)}, bf16[1536,128]{1,0:T(8,128)(2,1)S(1)}, u32[]{:S(2)}, u32[]{:S(2)}) collective-permute-start(bf16[1536,128]{1,0:T(8,128)(2,1)S(1)} %fusion.89), channel_id=1, source_target_pairs={{0,8},{24,16},{8,0},{16,24},{1,9},{25,17},{9,1},{17,25},{2,10},{26... | collective-permute-start | bytes 1179656 | tf_op jit(solution)/shard_map/ppermute | solution.py:52
  153.5 1.9 collective-permute-start.30
  155.8 6.4 %collective-permute-done.28 = bf16[1536,128]{1,0:T(8,128)(2,1)S(1)} collective-permute-done((bf16[1536,128]{1,0:T(8,128)(2,1)S(1)}, bf16[1536,128]{1,0:T(8,128)(2,1)S(1)}, u32[]{:S(2)}, u32[]{:S(2)}) %collective-permute-start.28) | collective-permute-done | bytes 393248 | tf_op jit(solution)/shard_map/ppermute | solution.py:52
  163.2 3.8 %collective-permute-start.32 = (bf16[1536,128]{1,0:T(8,128)(2,1)S(1)}, bf16[1536,128]{1,0:T(8,128)(2,1)S(1)}, u32[]{:S(2)}, u32[]{:S(2)}) collective-permute-start(bf16[1536,128]{1,0:T(8,128)(2,1)S(1)} %fusion.91), channel_id=1, source_target_pairs={{0,8},{24,16},{8,0},{16,24},{1,9},{25,17},{9,1},{17,25},{2,10},{26... | collective-permute-start | bytes 1179656 | tf_op jit(solution)/shard_map/ppermute | solution.py:52
  167.0 3.7 %collective-permute-done.30 = bf16[1536,128]{1,0:T(8,128)(2,1)S(1)} collective-permute-done((bf16[1536,128]{1,0:T(8,128)(2,1)S(1)}, bf16[1536,128]{1,0:T(8,128)(2,1)S(1)}, u32[]{:S(2)}, u32[]{:S(2)}) %collective-permute-start.30) | collective-permute-done | bytes 393248 | tf_op jit(solution)/shard_map/ppermute | solution.py:52
  172.1 5.8 %collective-permute-start.34 = (bf16[1536,128]{1,0:T(8,128)(2,1)S(1)}, bf16[1536,128]{1,0:T(8,128)(2,1)S(1)}, u32[]{:S(2)}, u32[]{:S(2)}) collective-permute-start(bf16[1536,128]{1,0:T(8,128)(2,1)S(1)} %fusion.92), channel_id=1, source_target_pairs={{0,8},{24,16},{8,0},{16,24},{1,9},{25,17},{9,1},{17,25},{2,10},{26... | collective-permute-start | bytes 1179656 | tf_op jit(solution)/shard_map/ppermute | solution.py:52
  180.3 6.1 %collective-permute-start.36 = (bf16[1536,128]{1,0:T(8,128)(2,1)S(1)}, bf16[1536,128]{1,0:T(8,128)(2,1)S(1)}, u32[]{:S(2)}, u32[]{:S(2)}) collective-permute-start(bf16[1536,128]{1,0:T(8,128)(2,1)S(1)} %fusion.93), channel_id=1, source_target_pairs={{0,8},{24,16},{8,0},{16,24},{1,9},{25,17},{9,1},{17,25},{2,10},{26... | collective-permute-start | bytes 1179656 | tf_op jit(solution)/shard_map/ppermute | solution.py:52
  189.0 6.1 %collective-permute-start.38 = (bf16[1536,128]{1,0:T(8,128)(2,1)S(1)}, bf16[1536,128]{1,0:T(8,128)(2,1)S(1)}, u32[]{:S(2)}, u32[]{:S(2)}) collective-permute-start(bf16[1536,128]{1,0:T(8,128)(2,1)S(1)} %fusion.94), channel_id=1, source_target_pairs={{0,8},{24,16},{8,0},{16,24},{1,9},{25,17},{9,1},{17,25},{2,10},{26... | collective-permute-start | bytes 1179656 | tf_op jit(solution)/shard_map/ppermute | solution.py:52
  197.9 5.6 %collective-permute-start.40 = (bf16[1536,128]{1,0:T(8,128)(2,1)S(1)}, bf16[1536,128]{1,0:T(8,128)(2,1)S(1)}, u32[]{:S(2)}, u32[]{:S(2)}) collective-permute-start(bf16[1536,128]{1,0:T(8,128)(2,1)S(1)} %fusion.95), channel_id=1, source_target_pairs={{0,8},{24,16},{8,0},{16,24},{1,9},{25,17},{9,1},{17,25},{2,10},{26... | collective-permute-start | bytes 1179656 | tf_op jit(solution)/shard_map/ppermute | solution.py:52
  205.9 6.3 %collective-permute-start.42 = (bf16[1536,128]{1,0:T(8,128)(2,1)S(1)}, bf16[1536,128]{1,0:T(8,128)(2,1)S(1)}, u32[]{:S(2)}, u32[]{:S(2)}) collective-permute-start(bf16[1536,128]{1,0:T(8,128)(2,1)S(1)} %fusion.96), channel_id=1, source_target_pairs={{0,8},{24,16},{8,0},{16,24},{1,9},{25,17},{9,1},{17,25},{2,10},{26... | collective-permute-start | bytes 1179656 | tf_op jit(solution)/shard_map/ppermute | solution.py:52
  215.5 6.0 %collective-permute-done.42 = bf16[1536,128]{1,0:T(8,128)(2,1)S(1)} collective-permute-done((bf16[1536,128]{1,0:T(8,128)(2,1)S(1)}, bf16[1536,128]{1,0:T(8,128)(2,1)S(1)}, u32[]{:S(2)}, u32[]{:S(2)}) %collective-permute-start.42) | collective-permute-done | bytes 393248 | tf_op jit(solution)/shard_map/ppermute | solution.py:52
  224.2 5.7 %collective-permute-done.44 = bf16[1536,128]{1,0:T(8,128)(2,1)S(1)} collective-permute-done((bf16[1536,128]{1,0:T(8,128)(2,1)S(1)}, bf16[1536,128]{1,0:T(8,128)(2,1)S(1)}, u32[]{:S(2)}, u32[]{:S(2)}) %collective-permute-start.44) | collective-permute-done | bytes 393248 | tf_op jit(solution)/shard_map/ppermute | solution.py:52
  232.3 1.9 collective-permute-done.46
  234.1 5.6 %collective-permute-done.47 = bf16[1536,128]{1,0:T(8,128)(2,1)S(1)} collective-permute-done((bf16[1536,128]{1,0:T(8,128)(2,1)S(1)}, bf16[1536,128]{1,0:T(8,128)(2,1)S(1)}, u32[]{:S(2)}, u32[]{:S(2)}) %collective-permute-start.47) | collective-permute-done | bytes 393248 | tf_op jit(solution)/shard_map/ppermute | solution.py:52
  240.7 3.4 %copy-done.2 = f32[1536,1536]{1,0:T(8,128)} copy-done((f32[1536,1536]{1,0:T(8,128)}, f32[1536,1536]{1,0:T(8,128)S(1)}, u32[]{:S(2)}) %copy-start.2) | copy-done | bytes 9437208
  244.1 2.2 copy-done.3
  (184 shorter events, 42.7 us)
Async XLA Ops:
  0.6 19.7 %collective-permute-start = (bf16[256,1536]{1,0:T(8,128)(2,1)}, bf16[256,1536]{1,0:T(8,128)(2,1)}, u32[]{:S(2)}, u32[]{:S(2)}) collective-permute-start(bf16[256,1536]{1,0:T(8,128)(2,1)} %param.8), channel_id=1, source_target_pairs={{0,4},{2,6},{4,0},{6,2},{1,5},{3,7},{5,1},{7,3},{8,12},{10,14},{12... | collective-permute-start | bytes 2359304 | tf_op jit(solution)/shard_map/ppermute | solution.py:27
  2.2 18.1 %collective-permute-start.1 = (bf16[256,1536]{1,0:T(8,128)(2,1)}, bf16[256,1536]{1,0:T(8,128)(2,1)S(1)}, u32[]{:S(2)}, u32[]{:S(2)}) collective-permute-start(bf16[256,1536]{1,0:T(8,128)(2,1)} %param.8), channel_id=1, source_target_pairs={{0,2},{2,0},{4,6},{6,4},{1,3},{3,1},{5,7},{7,5},{8,10},{10,8},{12,... | collective-permute-start | bytes 2359304 | tf_op jit(solution)/shard_map/ppermute | solution.py:27
  4.7 15.6 %collective-permute-start.2 = (bf16[256,1536]{1,0:T(8,128)(2,1)}, bf16[256,1536]{1,0:T(8,128)(2,1)}, u32[]{:S(2)}, u32[]{:S(2)}) collective-permute-start(bf16[256,1536]{1,0:T(8,128)(2,1)} %get-tuple-element.300), channel_id=1, source_target_pairs={{0,2},{2,0},{4,6},{6,4},{1,3},{3,1},{5,7},{7,5},{8,10},{10,8},{12,... | collective-permute-start | bytes 2359304 | tf_op jit(solution)/shard_map/ppermute | solution.py:27
  6.2 14.1 %collective-permute-start.3 = (bf16[256,1536]{1,0:T(8,128)(2,1)}, bf16[256,1536]{1,0:T(8,128)(2,1)}, u32[]{:S(2)}, u32[]{:S(2)}) collective-permute-start(bf16[256,1536]{1,0:T(8,128)(2,1)} %get-tuple-element.298), channel_id=1, source_target_pairs={{0,2},{2,0},{4,6},{6,4},{1,3},{3,1},{5,7},{7,5},{8,10},{10,8},{12,... | collective-permute-start | bytes 2359304 | tf_op jit(solution)/shard_map/ppermute | solution.py:27
  20.3 6.3 %collective-permute-start.6 = (bf16[256,1536]{1,0:T(8,128)(2,1)}, bf16[256,1536]{1,0:T(8,128)(2,1)S(1)}, u32[]{:S(2)}, u32[]{:S(2)}) collective-permute-start(bf16[256,1536]{1,0:T(8,128)(2,1)} %collective-permute-done), channel_id=1, source_target_pairs={{0,2},{2,0},{4,6},{6,4},{1,3},{3,1},{5,7},{7,5},{8,10},{10,8},{12,... | collective-permute-start | bytes 2359304 | tf_op jit(solution)/shard_map/ppermute | solution.py:27
  24.5 21.3 %collective-permute-start.4 = (bf16[128,1536]{1,0:T(8,128)(2,1)S(1)}, bf16[128,1536]{1,0:T(8,128)(2,1)S(1)}, u32[]{:S(2)}, u32[]{:S(2)}) collective-permute-start(bf16[128,1536]{1,0:T(8,128)(2,1)S(1)} %get-tuple-element.318), channel_id=1, source_target_pairs={{0,4},{2,6},{4,0},{6,2},{1,5},{3,7},{5,1},{7,3},{8,12},{10,14},{12... | collective-permute-start | bytes 1179656 | tf_op jit(solution)/shard_map/ppermute | solution.py:27
  26.1 18.8 %collective-permute-start.5 = (bf16[128,1536]{1,0:T(8,128)(2,1)S(1)}, bf16[128,1536]{1,0:T(8,128)(2,1)S(1)}, u32[]{:S(2)}, u32[]{:S(2)}) collective-permute-start(bf16[128,1536]{1,0:T(8,128)(2,1)S(1)} %get-tuple-element.317), channel_id=1, source_target_pairs={{0,4},{2,6},{4,0},{6,2},{1,5},{3,7},{5,1},{7,3},{8,12},{10,14},{12... | collective-permute-start | bytes 1179656 | tf_op jit(solution)/shard_map/ppermute | solution.py:27
  28.7 33.4 %collective-permute-start.11 = (bf16[128,1536]{1,0:T(8,128)(2,1)S(1)}, bf16[128,1536]{1,0:T(8,128)(2,1)S(1)}, u32[]{:S(2)}, u32[]{:S(2)}) collective-permute-start(bf16[128,1536]{1,0:T(8,128)(2,1)S(1)} %get-tuple-element.303), channel_id=1, source_target_pairs={{0,4},{2,6},{4,0},{6,2},{1,5},{3,7},{5,1},{7,3},{8,12},{10,14},{12... | collective-permute-start | bytes 1179656 | tf_op jit(solution)/shard_map/ppermute | solution.py:27
  30.3 31.0 %collective-permute-start.9 = (bf16[128,1536]{1,0:T(8,128)(2,1)S(1)}, bf16[128,1536]{1,0:T(8,128)(2,1)S(1)}, u32[]{:S(2)}, u32[]{:S(2)}) collective-permute-start(bf16[128,1536]{1,0:T(8,128)(2,1)S(1)} %get-tuple-element.304), channel_id=1, source_target_pairs={{0,4},{2,6},{4,0},{6,2},{1,5},{3,7},{5,1},{7,3},{8,12},{10,14},{12... | collective-permute-start | bytes 1179656 | tf_op jit(solution)/shard_map/ppermute | solution.py:27
  46.6 19.9 %collective-permute-start.7 = (bf16[128,1536]{1,0:T(8,128)(2,1)S(1)}, bf16[128,1536]{1,0:T(8,128)(2,1)S(1)}, u32[]{:S(2)}, u32[]{:S(2)}) collective-permute-start(bf16[128,1536]{1,0:T(8,128)(2,1)S(1)} %get-tuple-element.313), channel_id=1, source_target_pairs={{0,1},{1,0},{2,3},{3,2},{4,5},{5,4},{6,7},{7,6},{8,9},{9,8},{10,11... | collective-permute-start | bytes 1179656 | tf_op jit(solution)/shard_map/ppermute | solution.py:27
  47.0 19.1 %collective-permute-start.8 = (bf16[128,1536]{1,0:T(8,128)(2,1)S(1)}, bf16[128,1536]{1,0:T(8,128)(2,1)S(1)}, u32[]{:S(2)}, u32[]{:S(2)}) collective-permute-start(bf16[128,1536]{1,0:T(8,128)(2,1)S(1)} %get-tuple-element.311), channel_id=1, source_target_pairs={{0,1},{1,0},{2,3},{3,2},{4,5},{5,4},{6,7},{7,6},{8,9},{9,8},{10,11... | collective-permute-start | bytes 1179656 | tf_op jit(solution)/shard_map/ppermute | solution.py:27
  62.2 21.5 %collective-permute-start.12 = (bf16[128,1536]{1,0:T(8,128)(2,1)S(1)}, bf16[128,1536]{1,0:T(8,128)(2,1)S(1)}, u32[]{:S(2)}, u32[]{:S(2)}) collective-permute-start(bf16[128,1536]{1,0:T(8,128)(2,1)S(1)} %broadcast_select_fusion.2), channel_id=1, source_target_pairs={{0,1},{1,0},{2,3},{3,2},{4,5},{5,4},{6,7},{7,6},{8,9},{9,8},{10,11... | collective-permute-start | bytes 1179656 | tf_op jit(solution)/shard_map/ppermute | solution.py:27
  62.6 19.6 %collective-permute-start.10 = (bf16[128,1536]{1,0:T(8,128)(2,1)S(1)}, bf16[128,1536]{1,0:T(8,128)(2,1)S(1)}, u32[]{:S(2)}, u32[]{:S(2)}) collective-permute-start(bf16[128,1536]{1,0:T(8,128)(2,1)S(1)} %get-tuple-element.315), channel_id=1, source_target_pairs={{0,1},{1,0},{2,3},{3,2},{4,5},{5,4},{6,7},{7,6},{8,9},{9,8},{10,11... | collective-permute-start | bytes 1179656 | tf_op jit(solution)/shard_map/ppermute | solution.py:27
  85.4 1.4 collective-permute-start.13
  86.9 3.7 %collective-permute-start.14 = (f32[2,512]{1,0:T(2,128)S(1)}, f32[2,512]{1,0:T(2,128)S(1)}, u32[]{:S(2)}, u32[]{:S(2)}) collective-permute-start(f32[2,512]{1,0:T(2,128)S(1)} %maximum_add_fusion), channel_id=1, source_target_pairs={{0,1},{1,0},{2,3},{3,2},{4,5},{5,4},{6,7},{7,6},{8,9},{9,8},{10,11... | collective-permute-start | bytes 12296 | tf_op jit(solution)/shard_map/ppermute | solution.py:27
  91.7 5.0 %collective-permute-start.15 = (bf16[512,128]{1,0:T(8,128)(2,1)S(1)}, bf16[512,128]{1,0:T(8,128)(2,1)S(1)}, u32[]{:S(2)}, u32[]{:S(2)}) collective-permute-start(bf16[512,128]{1,0:T(8,128)(2,1)S(1)} %pad_maximum_fusion.5), channel_id=1, source_target_pairs={{0,1},{5,4},{4,0},{1,5},{2,3},{7,6},{6,2},{3,7},{8,9},{13,12},{12,... | collective-permute-start | bytes 393224 | tf_op jit(solution)/shard_map/ppermute | solution.py:177
  93.2 7.7 %collective-permute-start.18 = (bf16[512,128]{1,0:T(8,128)(2,1)S(1)}, bf16[512,128]{1,0:T(8,128)(2,1)S(1)}, u32[]{:S(2)}, u32[]{:S(2)}) collective-permute-start(bf16[512,128]{1,0:T(8,128)(2,1)S(1)} %pad_maximum_fusion.5), channel_id=1, source_target_pairs={{4,1},{1,4},{6,3},{3,6},{12,9},{9,12},{14,11},{11,14},{20,17},{17,... | collective-permute-start | bytes 393224 | tf_op jit(solution)/shard_map/ppermute | solution.py:178
  96.7 13.6 %collective-permute-start.16 = (bf16[512,384]{1,0:T(8,128)(2,1)S(1)}, bf16[512,384]{1,0:T(8,128)(2,1)S(1)}, u32[]{:S(2)}, u32[]{:S(2)}) collective-permute-start(bf16[512,384]{1,0:T(8,128)(2,1)S(1)} %pad_maximum_fusion.2), channel_id=1, source_target_pairs={{0,1},{5,4},{4,0},{1,5},{2,3},{7,6},{6,2},{3,7},{8,9},{13,12},{12,... | collective-permute-start | bytes 1179656 | tf_op jit(solution)/shard_map/ppermute | solution.py:177
  98.2 14.8 %collective-permute-start.17 = (bf16[512,384]{1,0:T(8,128)(2,1)S(1)}, bf16[512,384]{1,0:T(8,128)(2,1)S(1)}, u32[]{:S(2)}, u32[]{:S(2)}) collective-permute-start(bf16[512,384]{1,0:T(8,128)(2,1)S(1)} %pad_maximum_fusion.2), channel_id=1, source_target_pairs={{4,1},{1,4},{6,3},{3,6},{12,9},{9,12},{14,11},{11,14},{20,17},{17,... | collective-permute-start | bytes 1179656 | tf_op jit(solution)/shard_map/ppermute | solution.py:178
  101.0 36.9 %collective-permute-start.23 = (bf16[512,1024]{1,0:T(8,128)(2,1)S(1)}, bf16[512,1024]{1,0:T(8,128)(2,1)S(1)}, u32[]{:S(2)}, u32[]{:S(2)}) collective-permute-start(bf16[512,1024]{1,0:T(8,128)(2,1)S(1)} %pad_maximum_fusion), channel_id=1, source_target_pairs={{0,1},{5,4},{4,0},{1,5},{2,3},{7,6},{6,2},{3,7},{8,9},{13,12},{12,... | collective-permute-start | bytes 3145736 | tf_op jit(solution)/shard_map/ppermute | solution.py:177
  101.0 36.9 %collective-permute-start.24 = (bf16[512,1024]{1,0:T(8,128)(2,1)S(1)}, bf16[512,1024]{1,0:T(8,128)(2,1)S(1)}, u32[]{:S(2)}, u32[]{:S(2)}) collective-permute-start(bf16[512,1024]{1,0:T(8,128)(2,1)S(1)} %pad_maximum_fusion), channel_id=1, source_target_pairs={{4,1},{1,4},{6,3},{3,6},{12,9},{9,12},{14,11},{11,14},{20,17},{17,... | collective-permute-start | bytes 3145736 | tf_op jit(solution)/shard_map/ppermute | solution.py:178
  106.6 13.0 %collective-permute-start.19 = (bf16[1536,128]{1,0:T(8,128)(2,1)S(1)}, bf16[1536,128]{1,0:T(8,128)(2,1)S(1)}, u32[]{:S(2)}, u32[]{:S(2)}) collective-permute-start(bf16[1536,128]{1,0:T(8,128)(2,1)S(1)} %fusion.62), channel_id=1, source_target_pairs={{0,8},{24,16},{1,9},{25,17},{2,10},{26,18},{3,11},{27,19},{4,12},{... | collective-permute-start | bytes 1179656 | tf_op jit(solution)/shard_map/ppermute | solution.py:52
  114.6 15.3 %collective-permute-start.21 = (bf16[1536,128]{1,0:T(8,128)(2,1)S(1)}, bf16[1536,128]{1,0:T(8,128)(2,1)S(1)}, u32[]{:S(2)}, u32[]{:S(2)}) collective-permute-start(bf16[1536,128]{1,0:T(8,128)(2,1)S(1)} %fusion.63), channel_id=1, source_target_pairs={{0,8},{24,16},{1,9},{25,17},{2,10},{26,18},{3,11},{27,19},{4,12},{... | collective-permute-start | bytes 1179656 | tf_op jit(solution)/shard_map/ppermute | solution.py:52
  119.8 11.0 %collective-permute-start.20 = (bf16[1536,128]{1,0:T(8,128)(2,1)S(1)}, bf16[1536,128]{1,0:T(8,128)(2,1)S(1)}, u32[]{:S(2)}, u32[]{:S(2)}) collective-permute-start(bf16[1536,128]{1,0:T(8,128)(2,1)S(1)} %add_convert_fusion.35), channel_id=1, source_target_pairs={{8,16},{16,8},{9,17},{17,9},{10,18},{18,10},{11,19},{19,11},{12,20... | collective-permute-start | bytes 1179656 | tf_op jit(solution)/shard_map/ppermute | solution.py:60
  122.7 14.3 %collective-permute-start.26 = (bf16[1536,128]{1,0:T(8,128)(2,1)S(1)}, bf16[1536,128]{1,0:T(8,128)(2,1)S(1)}, u32[]{:S(2)}, u32[]{:S(2)}) collective-permute-start(bf16[1536,128]{1,0:T(8,128)(2,1)S(1)} %slice.480), channel_id=1, source_target_pairs={{0,8},{24,16},{1,9},{25,17},{2,10},{26,18},{3,11},{27,19},{4,12},{... | collective-permute-start | bytes 1179656 | tf_op jit(solution)/shard_map/ppermute | solution.py:52
  130.1 17.0 %collective-permute-start.25 = (bf16[1536,128]{1,0:T(8,128)(2,1)S(1)}, bf16[1536,128]{1,0:T(8,128)(2,1)S(1)}, u32[]{:S(2)}, u32[]{:S(2)}) collective-permute-start(bf16[1536,128]{1,0:T(8,128)(2,1)S(1)} %add_convert_fusion.34), channel_id=1, source_target_pairs={{8,16},{16,8},{9,17},{17,9},{10,18},{18,10},{11,19},{19,11},{12,20... | collective-permute-start | bytes 1179656 | tf_op jit(solution)/shard_map/ppermute | solution.py:60
  130.9 21.6 %collective-permute-start.22 = (bf16[1536,128]{1,0:T(8,128)(2,1)S(1)}, bf16[1536,128]{1,0:T(8,128)(2,1)S(1)}, u32[]{:S(2)}, u32[]{:S(2)}) collective-permute-start(bf16[1536,128]{1,0:T(8,128)(2,1)S(1)} %fusion.88), channel_id=1, source_target_pairs={{0,8},{24,16},{8,0},{16,24},{1,9},{25,17},{9,1},{17,25},{2,10},{26... | collective-permute-start | bytes 1179656 | tf_op jit(solution)/shard_map/ppermute | solution.py:52
  137.2 16.2 %collective-permute-start.27 = (bf16[1536,128]{1,0:T(8,128)(2,1)S(1)}, bf16[1536,128]{1,0:T(8,128)(2,1)S(1)}, u32[]{:S(2)}, u32[]{:S(2)}) collective-permute-start(bf16[1536,128]{1,0:T(8,128)(2,1)S(1)} %add_convert_fusion.32), channel_id=1, source_target_pairs={{8,16},{16,8},{9,17},{17,9},{10,18},{18,10},{11,19},{19,11},{12,20... | collective-permute-start | bytes 1179656 | tf_op jit(solution)/shard_map/ppermute | solution.py:60
  147.2 15.0 %collective-permute-start.28 = (bf16[1536,128]{1,0:T(8,128)(2,1)S(1)}, bf16[1536,128]{1,0:T(8,128)(2,1)S(1)}, u32[]{:S(2)}, u32[]{:S(2)}) collective-permute-start(bf16[1536,128]{1,0:T(8,128)(2,1)S(1)} %fusion.89), channel_id=1, source_target_pairs={{0,8},{24,16},{8,0},{16,24},{1,9},{25,17},{9,1},{17,25},{2,10},{26... | collective-permute-start | bytes 1179656 | tf_op jit(solution)/shard_map/ppermute | solution.py:52
  152.6 10.4 %collective-permute-start.29 = (bf16[1536,128]{1,0:T(8,128)(2,1)S(1)}, bf16[1536,128]{1,0:T(8,128)(2,1)S(1)}, u32[]{:S(2)}, u32[]{:S(2)}) collective-permute-start(bf16[1536,128]{1,0:T(8,128)(2,1)S(1)} %add_convert_fusion.30), channel_id=1, source_target_pairs={{8,16},{16,8},{9,17},{17,9},{10,18},{18,10},{11,19},{19,11},{12,20... | collective-permute-start | bytes 1179656 | tf_op jit(solution)/shard_map/ppermute | solution.py:60
  153.5 17.1 %collective-permute-start.30 = (bf16[1536,128]{1,0:T(8,128)(2,1)S(1)}, bf16[1536,128]{1,0:T(8,128)(2,1)S(1)}, u32[]{:S(2)}, u32[]{:S(2)}) collective-permute-start(bf16[1536,128]{1,0:T(8,128)(2,1)S(1)} %fusion.90), channel_id=1, source_target_pairs={{0,8},{24,16},{8,0},{16,24},{1,9},{25,17},{9,1},{17,25},{2,10},{26... | collective-permute-start | bytes 1179656 | tf_op jit(solution)/shard_map/ppermute | solution.py:52
  162.3 9.6 %collective-permute-start.31 = (bf16[1536,128]{1,0:T(8,128)(2,1)S(1)}, bf16[1536,128]{1,0:T(8,128)(2,1)S(1)}, u32[]{:S(2)}, u32[]{:S(2)}) collective-permute-start(bf16[1536,128]{1,0:T(8,128)(2,1)S(1)} %add_convert_fusion.28), channel_id=1, source_target_pairs={{8,16},{16,8},{9,17},{17,9},{10,18},{18,10},{11,19},{19,11},{12,20... | collective-permute-start | bytes 1179656 | tf_op jit(solution)/shard_map/ppermute | solution.py:60
  163.2 15.9 %collective-permute-start.32 = (bf16[1536,128]{1,0:T(8,128)(2,1)S(1)}, bf16[1536,128]{1,0:T(8,128)(2,1)S(1)}, u32[]{:S(2)}, u32[]{:S(2)}) collective-permute-start(bf16[1536,128]{1,0:T(8,128)(2,1)S(1)} %fusion.91), channel_id=1, source_target_pairs={{0,8},{24,16},{8,0},{16,24},{1,9},{25,17},{9,1},{17,25},{2,10},{26... | collective-permute-start | bytes 1179656 | tf_op jit(solution)/shard_map/ppermute | solution.py:52
  170.8 9.3 %collective-permute-start.33 = (bf16[1536,128]{1,0:T(8,128)(2,1)S(1)}, bf16[1536,128]{1,0:T(8,128)(2,1)S(1)}, u32[]{:S(2)}, u32[]{:S(2)}) collective-permute-start(bf16[1536,128]{1,0:T(8,128)(2,1)S(1)} %add_convert_fusion.26), channel_id=1, source_target_pairs={{8,16},{16,8},{9,17},{17,9},{10,18},{18,10},{11,19},{19,11},{12,20... | collective-permute-start | bytes 1179656 | tf_op jit(solution)/shard_map/ppermute | solution.py:60
  172.1 15.9 %collective-permute-start.34 = (bf16[1536,128]{1,0:T(8,128)(2,1)S(1)}, bf16[1536,128]{1,0:T(8,128)(2,1)S(1)}, u32[]{:S(2)}, u32[]{:S(2)}) collective-permute-start(bf16[1536,128]{1,0:T(8,128)(2,1)S(1)} %fusion.92), channel_id=1, source_target_pairs={{0,8},{24,16},{8,0},{16,24},{1,9},{25,17},{9,1},{17,25},{2,10},{26... | collective-permute-start | bytes 1179656 | tf_op jit(solution)/shard_map/ppermute | solution.py:52
  179.2 9.6 %collective-permute-start.35 = (bf16[1536,128]{1,0:T(8,128)(2,1)S(1)}, bf16[1536,128]{1,0:T(8,128)(2,1)S(1)}, u32[]{:S(2)}, u32[]{:S(2)}) collective-permute-start(bf16[1536,128]{1,0:T(8,128)(2,1)S(1)} %add_convert_fusion.24), channel_id=1, source_target_pairs={{8,16},{16,8},{9,17},{17,9},{10,18},{18,10},{11,19},{19,11},{12,20... | collective-permute-start | bytes 1179656 | tf_op jit(solution)/shard_map/ppermute | solution.py:60
  180.3 16.1 %collective-permute-start.36 = (bf16[1536,128]{1,0:T(8,128)(2,1)S(1)}, bf16[1536,128]{1,0:T(8,128)(2,1)S(1)}, u32[]{:S(2)}, u32[]{:S(2)}) collective-permute-start(bf16[1536,128]{1,0:T(8,128)(2,1)S(1)} %fusion.93), channel_id=1, source_target_pairs={{0,8},{24,16},{8,0},{16,24},{1,9},{25,17},{9,1},{17,25},{2,10},{26... | collective-permute-start | bytes 1179656 | tf_op jit(solution)/shard_map/ppermute | solution.py:52
  188.1 9.6 %collective-permute-start.37 = (bf16[1536,128]{1,0:T(8,128)(2,1)S(1)}, bf16[1536,128]{1,0:T(8,128)(2,1)S(1)}, u32[]{:S(2)}, u32[]{:S(2)}) collective-permute-start(bf16[1536,128]{1,0:T(8,128)(2,1)S(1)} %add_convert_fusion.22), channel_id=1, source_target_pairs={{8,16},{16,8},{9,17},{17,9},{10,18},{18,10},{11,19},{19,11},{12,20... | collective-permute-start | bytes 1179656 | tf_op jit(solution)/shard_map/ppermute | solution.py:60
  189.0 15.9 %collective-permute-start.38 = (bf16[1536,128]{1,0:T(8,128)(2,1)S(1)}, bf16[1536,128]{1,0:T(8,128)(2,1)S(1)}, u32[]{:S(2)}, u32[]{:S(2)}) collective-permute-start(bf16[1536,128]{1,0:T(8,128)(2,1)S(1)} %fusion.94), channel_id=1, source_target_pairs={{0,8},{24,16},{8,0},{16,24},{1,9},{25,17},{9,1},{17,25},{2,10},{26... | collective-permute-start | bytes 1179656 | tf_op jit(solution)/shard_map/ppermute | solution.py:52
  196.6 9.1 %collective-permute-start.39 = (bf16[1536,128]{1,0:T(8,128)(2,1)S(1)}, bf16[1536,128]{1,0:T(8,128)(2,1)S(1)}, u32[]{:S(2)}, u32[]{:S(2)}) collective-permute-start(bf16[1536,128]{1,0:T(8,128)(2,1)S(1)} %add_convert_fusion.20), channel_id=1, source_target_pairs={{8,16},{16,8},{9,17},{17,9},{10,18},{18,10},{11,19},{19,11},{12,20... | collective-permute-start | bytes 1179656 | tf_op jit(solution)/shard_map/ppermute | solution.py:60
  197.9 15.4 %collective-permute-start.40 = (bf16[1536,128]{1,0:T(8,128)(2,1)S(1)}, bf16[1536,128]{1,0:T(8,128)(2,1)S(1)}, u32[]{:S(2)}, u32[]{:S(2)}) collective-permute-start(bf16[1536,128]{1,0:T(8,128)(2,1)S(1)} %fusion.95), channel_id=1, source_target_pairs={{0,8},{24,16},{8,0},{16,24},{1,9},{25,17},{9,1},{17,25},{2,10},{26... | collective-permute-start | bytes 1179656 | tf_op jit(solution)/shard_map/ppermute | solution.py:52
  205.0 9.1 %collective-permute-start.41 = (bf16[1536,128]{1,0:T(8,128)(2,1)S(1)}, bf16[1536,128]{1,0:T(8,128)(2,1)S(1)}, u32[]{:S(2)}, u32[]{:S(2)}) collective-permute-start(bf16[1536,128]{1,0:T(8,128)(2,1)S(1)} %add_convert_fusion.18), channel_id=1, source_target_pairs={{8,16},{16,8},{9,17},{17,9},{10,18},{18,10},{11,19},{19,11},{12,20... | collective-permute-start | bytes 1179656 | tf_op jit(solution)/shard_map/ppermute | solution.py:60
  205.9 15.6 %collective-permute-start.42 = (bf16[1536,128]{1,0:T(8,128)(2,1)S(1)}, bf16[1536,128]{1,0:T(8,128)(2,1)S(1)}, u32[]{:S(2)}, u32[]{:S(2)}) collective-permute-start(bf16[1536,128]{1,0:T(8,128)(2,1)S(1)} %fusion.96), channel_id=1, source_target_pairs={{0,8},{24,16},{8,0},{16,24},{1,9},{25,17},{9,1},{17,25},{2,10},{26... | collective-permute-start | bytes 1179656 | tf_op jit(solution)/shard_map/ppermute | solution.py:52
  213.4 9.4 %collective-permute-start.43 = (bf16[1536,128]{1,0:T(8,128)(2,1)S(1)}, bf16[1536,128]{1,0:T(8,128)(2,1)S(1)}, u32[]{:S(2)}, u32[]{:S(2)}) collective-permute-start(bf16[1536,128]{1,0:T(8,128)(2,1)S(1)} %add_convert_fusion.16), channel_id=1, source_target_pairs={{8,16},{16,8},{9,17},{17,9},{10,18},{18,10},{11,19},{19,11},{12,20... | collective-permute-start | bytes 1179656 | tf_op jit(solution)/shard_map/ppermute | solution.py:60
  214.2 15.7 %collective-permute-start.44 = (bf16[1536,128]{1,0:T(8,128)(2,1)S(1)}, bf16[1536,128]{1,0:T(8,128)(2,1)S(1)}, u32[]{:S(2)}, u32[]{:S(2)}) collective-permute-start(bf16[1536,128]{1,0:T(8,128)(2,1)S(1)} %add_convert_fusion.15), channel_id=1, source_target_pairs={{8,0},{16,24},{9,1},{17,25},{10,2},{18,26},{11,3},{19,27},{12,4},{... | collective-permute-start | bytes 1179656 | tf_op jit(solution)/shard_map/ppermute | solution.py:52
  221.6 8.3 %collective-permute-start.45 = (bf16[1536,128]{1,0:T(8,128)(2,1)S(1)}, bf16[1536,128]{1,0:T(8,128)(2,1)S(1)}, u32[]{:S(2)}, u32[]{:S(2)}) collective-permute-start(bf16[1536,128]{1,0:T(8,128)(2,1)S(1)} %add_convert_fusion.14), channel_id=1, source_target_pairs={{8,16},{16,8},{9,17},{17,9},{10,18},{18,10},{11,19},{19,11},{12,20... | collective-permute-start | bytes 1179656 | tf_op jit(solution)/shard_map/ppermute | solution.py:60
  222.9 11.2 %collective-permute-start.46 = (bf16[1536,128]{1,0:T(8,128)(2,1)S(1)}, bf16[1536,128]{1,0:T(8,128)(2,1)S(1)}, u32[]{:S(2)}, u32[]{:S(2)}) collective-permute-start(bf16[1536,128]{1,0:T(8,128)(2,1)S(1)} %add_convert_fusion.13), channel_id=1, source_target_pairs={{8,0},{16,24},{9,1},{17,25},{10,2},{18,26},{11,3},{19,27},{12,4},{... | collective-permute-start | bytes 1179656 | tf_op jit(solution)/shard_map/ppermute | solution.py:52
  230.0 9.7 %collective-permute-start.47 = (bf16[1536,128]{1,0:T(8,128)(2,1)S(1)}, bf16[1536,128]{1,0:T(8,128)(2,1)S(1)}, u32[]{:S(2)}, u32[]{:S(2)}) collective-permute-start(bf16[1536,128]{1,0:T(8,128)(2,1)S(1)} %add_convert_fusion.12), channel_id=1, source_target_pairs={{8,0},{16,24},{9,1},{17,25},{10,2},{18,26},{11,3},{19,27},{12,4},{... | collective-permute-start | bytes 1179656 | tf_op jit(solution)/shard_map/ppermute | solution.py:52
  (13 other events, 137.8 us)

commit v8 on v7

--- a/solution.py
+++ b/solution.py
@@ -89,41 +89,45 @@
             jnp.dot(block, weight, preferred_element_type=f32).astype(bf16)
         )
 
+    def at(h, q, x):
+        return (h * group + q) * 2 + x
+
+    ring_pairs, cross_pairs = [], []
+    for q in range(group):
+        ring_pairs += [(at(x, q, x), at(x, q, 1 - x)) for x in (0, 1)]
+        ring_pairs += [(at(1 - x, q, x), at(x, q, x)) for x in (0, 1)]
+        cross_pairs += [(at(1 - x, q, x), at(x, q, 1 - x)) for x in (0, 1)]
+    inward_pairs = [(at(1 - x, q, x), at(1 - x, q, 1 - x)) for q in range(group) for x in (0, 1)]
+    outward_pairs = [(at(x, q, x), at(x, q, 1 - x)) for q in range(group) for x in (0, 1)]
+
     near_blocks = [context] + [swap(context, "fsdp", r) for r in range(1, group)]
     slices = [
         [lax.dynamic_slice_in_dim(array, (low ^ r) * cols, cols, axis=1) for r in range(group)]
         for array in (residual, cotangent)
     ]
     moved = [[swap(parts[r], "fsdp", r) if r else parts[r] for r in range(group)] for parts in slices]
-    held = together(swap(context, "fsdp", group), *near_blocks[1:], *moved[0], *moved[1])
-    near_blocks = [context] + list(held[1:group])
-    residual_parts, cotangent_parts = held[group : 2 * group], held[2 * group :]
+    held = together(swap(context, "fsdp", group), *moved[0], *moved[1])
+    residual_parts, cotangent_parts = held[1 : 1 + group], held[1 + group :]
     far_blocks = [held[0]] + [swap(held[0], "fsdp", r) for r in range(1, group)]
-    far_outs, near_first = [], None
+    near_out = project(jnp.concatenate(near_blocks, axis=0))
+    near_came = lax.ppermute(near_out, ("fsdp", "tp"), inward_pairs)
+    far_outs = []
     for r in range(group):
-        blocks = [far_blocks[r]] + ([context[:rows]] if r == group - 1 else [])
-        out = project(jnp.concatenate(blocks, axis=0))
+        out = project(far_blocks[r])
         far_outs += [swap(out[p * rows : (p + 1) * rows], "fsdp", group) for p in range(pieces)]
-        near_first = out[tok_rows:]
+    passed = [lax.ppermute(out, ("fsdp", "tp"), outward_pairs) for out in far_outs]
 
     gain_part = lax.dynamic_slice_in_dim(gain, t * (width // 2) + low * cols, cols).astype(f32)
 
-    keeps, arrivals = [], []
-    for r in range(group):
-        for p in range(pieces):
-            far_out, own_out = far_outs[r * pieces + p], near_first
-            if keeps:
-                block, keeps[-1] = together(near_blocks[r], keeps[-1])
-                own_out = project(block[p * rows : (p + 1) * rows])
-            far_out, own_out = together(far_out, own_out)
-            keeps.append(jnp.where(near, own_out, far_out))
-            arrivals.append(swap(jnp.where(near, far_out, own_out), "tp", 1))
     hidden, weighted, sums = [], [], []
-    for k, (keep, came) in enumerate(zip(keeps, arrivals)):
-        span = slice(k % pieces * rows, (k % pieces + 1) * rows)
-        res, cot = residual_parts[k // pieces], cotangent_parts[k // pieces]
+    for k in range(group * pieces):
+        r, p = k // pieces, k % pieces
+        span, long_span = slice(p * rows, (p + 1) * rows), slice(k * rows, (k + 1) * rows)
+        res, cot, came = residual_parts[r], cotangent_parts[r], passed[k]
         if sums:
             came, sums[-1] = together(came, sums[-1])
+        keep = jnp.where(near, near_out[long_span], far_outs[k])
+        came = jnp.where(near, near_came[long_span], came)
         h = res[span].astype(f32) + keep.astype(f32) + came.astype(f32)
         w = gain_part[None, :] * cot[span].astype(f32)
         hidden.append(h)
@@ -145,16 +149,7 @@
     context_all = jnp.concatenate(near_blocks + far_blocks, axis=0)
     narrow = 128
     units = cols // narrow
-    widths = [1, 3, units - 4]
-    def at(h, q, x):
-        return (h * group + q) * 2 + x
-
-    ring_pairs, cross_pairs = [], []
-    for q in range(group):
-        ring_pairs += [(at(x, q, x), at(x, q, 1 - x)) for x in (0, 1)]
-        ring_pairs += [(at(1 - x, q, x), at(x, q, x)) for x in (0, 1)]
-        cross_pairs += [(at(1 - x, q, x), at(x, q, 1 - x)) for x in (0, 1)]
-
+    widths = [1, min(4, units - 2), units - 1 - min(4, units - 2)]
     islands = lax.axis_size("island")
     line = IslandLine(units)
     parts, locals_, rings, crosses = [], [], [], []
@@ -172,47 +167,61 @@
         if c == 1:
             d_local, rings[0] = together(d_local, rings[0])
         elif c == 2:
-            d_local, crosses[0] = together(d_local, crosses[0])
+            d_local, parts[1] = together(d_local, parts[1])
         locals_.append(d_local)
         rings.append(lax.ppermute(d_local, ("fsdp", "tp"), ring_pairs))
         crosses.append(lax.ppermute(d_local, ("fsdp", "tp"), cross_pairs))
 
-    def add_pseudo(c):
-        start = sum(widths[:c]) * narrow
+    def gathered(c):
         d_near = jnp.where(near, locals_[c], rings[c])
         d_far = jnp.where(near, rings[c], crosses[c])
-        d_all = jnp.concatenate([d_near, d_far], axis=0)
-        cuts = list(range(0, widths[c], 2)) if widths[c] % 2 == 0 else [0] + list(range(1, widths[c], 2))
-        for lo, hi in zip(cuts, cuts[1:] + [widths[c]]):
-            at_cols = slice(start + lo * narrow, start + hi * narrow)
-            piece, first, second, outer = together(
-                d_all[:, lo * narrow : hi * narrow], first_moment, second_moment, weight
-            )
-            grad = lax.dot_general(
-                context_all, piece, (((0,), (0,)), ((), ())), preferred_element_type=f32
-            ) / (tok_rows * fsdp_count)
-            first = first[0, :, at_cols].astype(f32)
-            second = second[0, :, at_cols].astype(f32)
-            m_new = beta_one * first + (1.0 - beta_one) * grad
-            v_new = beta_two * second + (1.0 - beta_two) * grad * grad
-            update = m_new / bias_one / (
-                jnp.sqrt(v_new / bias_two) + adam_eps
-            ) + decay_rate * outer[:, at_cols].astype(f32)
-            pseudo = lax.optimization_barrier(update.astype(bf16))
-            parts.extend(pseudo[:, u * narrow : (u + 1) * narrow] for u in range(hi - lo))
-
-    for c in range(len(widths)):
-        move(c)
-    for c in range(len(widths)):
-        add_pseudo(c)
+        return jnp.concatenate([d_near, d_far], axis=0)
+
+    def add_pseudo(d_all, lo, hi, after=None):
+        at_cols = slice(lo * narrow, hi * narrow)
+        piece = d_all[:, : (hi - lo) * narrow]
+        if after in line.sums:
+            piece, line.sums[after] = together(piece, line.sums[after])
+        piece, first, second, outer = together(piece, first_moment, second_moment, weight)
+        grad = lax.dot_general(
+            context_all, piece, (((0,), (0,)), ((), ())), preferred_element_type=f32
+        ) / (tok_rows * fsdp_count)
+        first = first[0, :, at_cols].astype(f32)
+        second = second[0, :, at_cols].astype(f32)
+        m_new = beta_one * first + (1.0 - beta_one) * grad
+        v_new = beta_two * second + (1.0 - beta_two) * grad * grad
+        update = m_new / bias_one / (
+            jnp.sqrt(v_new / bias_two) + adam_eps
+        ) + decay_rate * outer[:, at_cols].astype(f32)
+        pseudo = lax.optimization_barrier(update.astype(bf16))
+        for u in range(hi - lo):
+            line.part[len(parts)] = pseudo[:, u * narrow : (u + 1) * narrow]
+            parts.append(line.part[len(parts)])
+
+    move(0)
+    move(1)
+    add_pseudo(gathered(0), 0, 1)
+    early = sum(widths[:2])
+    middle = gathered(1)
+    for lo in range(1, early, 2):
+        add_pseudo(middle[:, (lo - 1) * narrow :], lo, min(lo + 2, early))
+        if lo == 1:
+            move(2)
+            line.part[1] = parts[1]
+    last = gathered(2)
+    todo = [(lo, min(lo + 2, units)) for lo in range(early, units, 2)]
     if islands == 4:
-        line.part.update(enumerate(parts))
         for s in range(2):
             line.send_outer(s)
         for s in range(units + 3):
+            while todo and todo[0][0] - 3 <= s:
+                lo, hi = todo.pop(0)
+                add_pseudo(last[:, (lo - early) * narrow :], lo, hi, s - 1)
             line.step(s)
         sums = [line.totals[k] for k in range(units)]
     else:
+        for lo, hi in todo:
+            add_pseudo(last[:, (lo - early) * narrow :], lo, hi)
         sums = [lax.psum(part, "island") for part in parts]
     momentum_out, step_out = [], []
     for k, total in enumerate(sums):

time: 247 us -> 241 us (0.976)
  waiting for transfers between devices: 101 us -> 81.5 us
  local copies, waits for them, and re-layouts: 10.9 us -> 14.9 us
  matrix products: 22.2 us -> 25.6 us
  other arithmetic: 15.5 us -> 18.1 us
    ppermute x15 -> x11, waiting for transfers between devices: 60.1 us -> 33.4 us  [swap(): return lax.ppermute(value, axis, [(i, i ^ bit) for i in range(count)])]
    ppermute x0 -> x5, waiting for transfers between devices: none -> 9.18 us  [the longest x4 5.43 us: body(): lax.ppermute(out, ('fsdp', 'tp'), outward_pairs)]
    ppermute x0 -> x5, starting transfers between devices: none -> 8.71 us  [the longest x4 5.12 us: body(): lax.ppermute(out, ('fsdp', 'tp'), outward_pairs)]
    unnamed x29 -> x41, local copies, waits for them, and re-layouts: 7.12 us -> 11.5 us
    ppermute x15, waiting for transfers between devices: 36.2 us -> 32 us  [send_outer(): self.edge[s] = lax.ppermute(payload, 'island', pairs)]
    ppermute x15 -> x11, starting transfers between devices: 11 us -> 7.32 us  [swap(): return lax.ppermute(value, axis, [(i, i ^ bit) for i in range(count)])]
    reduce_sum x4, other arithmetic: 4.06 us -> 7.18 us  [body(): sums.append(jnp.stack([jnp.sum(h * h, axis=-1), jnp.sum(h * w, axis=-1)]))]
    ppermute x3, starting transfers between devices: 3.09 us -> 0.12 us  [move(): rings.append(lax.ppermute(d_local, ('fsdp', 'tp'), ring_pairs))]
  transfers between devices with their start and end apart: 48 -> 49, of which waited for: 22 -> 19; matrix products, arithmetic and copies ran while one was open for 16% -> 20% of each run, Pallas kernels for 0% -> 0%
where the time goes in v8:
time: 241 us; the launch traced here: 240 us
  starting transfers between devices  97.7 us (41%)
  waiting for transfers between devices  81.5 us (34%)
  matrix products  25.6 us (11%)
  other arithmetic  18.1 us (8%)
  local copies, waits for them, and re-layouts  14.9 us (6%)
    ppermute x15, starting transfers between devices, send_outer(): self.edge[s] = lax.ppermute(payload, 'island', pairs)  62.6 us
    ppermute x11, waiting for transfers between devices, swap(): return lax.ppermute(value, axis, [(i, i ^ bit) for i in range(count)])  33.4 us
    ppermute x15, waiting for transfers between devices, send_outer(): self.edge[s] = lax.ppermute(payload, 'island', pairs)  32 us
    dot_general x7, matrix products, add_pseudo(): lax.dot_general(context_all, piece, (((0,), (0,)), ((), ())), preferred_e...  16 us
    unnamed x41, local copies, waits for them, and re-layouts  11.5 us
    ppermute x3, starting transfers between devices, move(): crosses.append(lax.ppermute(d_local, ('fsdp', 'tp'), cross_pairs))  10.2 us
    dot_general x3, matrix products, project(): jnp.dot(block, weight, preferred_element_type=f32).astype(bf16)  9.61 us
    ppermute x12, starting transfers between devices, step(): self.mid[s] = lax.ppermute(self.sums[s], 'island', [(1, 2), (2, 1)])  8.71 us
  transfers between devices with their start and end apart: 49, of which 19 were waited for; matrix products, arithmetic and copies ran while one was open for 20% of the time, Pallas kernels for 0%

profile of v8, /device:TPU:2, one launch (start us, length us, event | category | flops | bytes accessed | tf_op | source)
XLA Modules:
  0.0 239.6 jit_solution(15733493178658113526)
XLA Ops:
  4.8 15.5 %collective-permute-done = bf16[256,1536]{1,0:T(8,128)(2,1)} collective-permute-done((bf16[256,1536]{1,0:T(8,128)(2,1)}, bf16[256,1536]{1,0:T(8,128)(2,1)}, u32[]{:S(2)}, u32[]{:S(2)}) %collective-permute-start) | collective-permute-done | bytes 786464 | tf_op jit(solution)/shard_map/ppermute | solution.py:27
  21.2 4.1 %convolution_convert_fusion.2 = bf16[256,1536]{1,0:T(8,128)(2,1)S(1)} fusion(bf16[256,1536]{1,0:T(8,128)(2,1)} %collective-permute-done, bf16[1536,1536]{1,0:T(8,128)(2,1)} %param.12), kind=kOutput, calls=%fused_computation.2 | convolution fusion | flops 1208352768 | bytes 6291456 | tf_op jit(solution)/shard_map/dot_general | solution.py:89
  27.7 4.1 %convolution_convert_fusion = bf16[512,1536]{1,0:T(8,128)(2,1)} fusion(bf16[1536,1536]{1,0:T(8,128)(2,1)S(1)} %bitcast.206, bf16[256,1536]{1,0:T(8,128)(2,1)S(1)} %collective-permute-done.5, bf16[256,1536]{1,0:T(8,128)(2,1)S(1)} %copy-done.3), kind=kOutput, calls=%fused_computation | convolution fusion | flops 2419851264 | bytes 7864320 | tf_op jit(solution)/shard_map/dot_general | solution.py:89
  31.8 3.6 %collective-permute-start.7 = (bf16[512,1536]{1,0:T(8,128)(2,1)}, bf16[512,1536]{1,0:T(8,128)(2,1)}, u32[]{:S(2)}, u32[]{:S(2)}) collective-permute-start(bf16[512,1536]{1,0:T(8,128)(2,1)} %convolution_convert_fusion), channel_id=1, source_target_pairs={{4,5},{1,0},{6,7},{3,2},{12,13},{9,8},{14,15},{11,10},{20,21},{17,... | collective-permute-start | bytes 4718600 | tf_op jit(solution)/shard_map/ppermute | solution.py:113
  35.4 2.2 collective-permute-done.6
  41.2 3.4 %collective-permute-start.12 = (bf16[128,1536]{1,0:T(8,128)(2,1)}, bf16[128,1536]{1,0:T(8,128)(2,1)S(1)}, u32[]{:S(2)}, u32[]{:S(2)}) collective-permute-start(bf16[128,1536]{1,0:T(8,128)(2,1)} %get-tuple-element.300), channel_id=1, source_target_pairs={{0,4},{2,6},{4,0},{6,2},{1,5},{3,7},{5,1},{7,3},{8,12},{10,14},{12... | collective-permute-start | bytes 1179656 | tf_op jit(solution)/shard_map/ppermute | solution.py:27
  46.4 2.2 constant_dynamic-update-slice_fusion.2
  49.9 6.1 %collective-permute-done.12 = bf16[128,1536]{1,0:T(8,128)(2,1)S(1)} collective-permute-done((bf16[128,1536]{1,0:T(8,128)(2,1)}, bf16[128,1536]{1,0:T(8,128)(2,1)S(1)}, u32[]{:S(2)}, u32[]{:S(2)}) %collective-permute-start.12) | collective-permute-done | bytes 393248 | tf_op jit(solution)/shard_map/ppermute | solution.py:27
  57.3 6.1 %collective-permute-done.10 = bf16[128,1536]{1,0:T(8,128)(2,1)} collective-permute-done((bf16[128,1536]{1,0:T(8,128)(2,1)}, bf16[128,1536]{1,0:T(8,128)(2,1)}, u32[]{:S(2)}, u32[]{:S(2)}) %collective-permute-start.10) | collective-permute-done | bytes 393248 | tf_op jit(solution)/shard_map/ppermute | solution.py:27
  64.7 3.8 %collective-permute-done.7 = bf16[512,1536]{1,0:T(8,128)(2,1)} collective-permute-done((bf16[512,1536]{1,0:T(8,128)(2,1)}, bf16[512,1536]{1,0:T(8,128)(2,1)}, u32[]{:S(2)}, u32[]{:S(2)}) %collective-permute-start.7) | collective-permute-done | bytes 1572896 | tf_op jit(solution)/shard_map/ppermute | solution.py:113
  68.4 1.8 multiply_reduce_fusion.7
  70.3 1.8 multiply_reduce_fusion.5
  72.1 5.4 %collective-permute-done.11 = bf16[128,1536]{1,0:T(8,128)(2,1)S(1)} collective-permute-done((bf16[128,1536]{1,0:T(8,128)(2,1)}, bf16[128,1536]{1,0:T(8,128)(2,1)S(1)}, u32[]{:S(2)}, u32[]{:S(2)}) %collective-permute-start.11) | collective-permute-done | bytes 393248 | tf_op jit(solution)/shard_map/ppermute | solution.py:118
  79.3 1.8 multiply_reduce_fusion.1
  82.8 3.5 %collective-permute-done.15 = f32[2,512]{1,0:T(2,128)S(1)} collective-permute-done((f32[2,512]{1,0:T(2,128)S(1)}, f32[2,512]{1,0:T(2,128)S(1)}, u32[]{:S(2)}, u32[]{:S(2)}) %collective-permute-start.15) | collective-permute-done | bytes 4128 | tf_op jit(solution)/shard_map/ppermute | solution.py:27
  87.1 3.5 %collective-permute-start.19 = (bf16[512,128]{1,0:T(8,128)(2,1)S(1)}, bf16[512,128]{1,0:T(8,128)(2,1)S(1)}, u32[]{:S(2)}, u32[]{:S(2)}) collective-permute-start(bf16[512,128]{1,0:T(8,128)(2,1)S(1)} %pad_maximum_fusion.5), channel_id=1, source_target_pairs={{4,1},{1,4},{6,3},{3,6},{12,9},{9,12},{14,11},{11,14},{20,17},{17,... | collective-permute-start | bytes 393224 | tf_op jit(solution)/shard_map/ppermute | solution.py:173
  92.1 3.4 %collective-permute-start.18 = (bf16[512,512]{1,0:T(8,128)(2,1)S(1)}, bf16[512,512]{1,0:T(8,128)(2,1)S(1)}, u32[]{:S(2)}, u32[]{:S(2)}) collective-permute-start(bf16[512,512]{1,0:T(8,128)(2,1)S(1)} %pad_maximum_fusion.2), channel_id=1, source_target_pairs={{4,1},{1,4},{6,3},{3,6},{12,9},{9,12},{14,11},{11,14},{20,17},{17,... | collective-permute-start | bytes 1572872 | tf_op jit(solution)/shard_map/ppermute | solution.py:173
  97.1 3.7 %collective-permute-start.20 = (bf16[1536,128]{1,0:T(8,128)(2,1)S(1)}, bf16[1536,128]{1,0:T(8,128)(2,1)S(1)}, u32[]{:S(2)}, u32[]{:S(2)}) collective-permute-start(bf16[1536,128]{1,0:T(8,128)(2,1)S(1)} %fusion.62), channel_id=1, source_target_pairs={{0,8},{24,16},{1,9},{25,17},{2,10},{26,18},{3,11},{27,19},{4,12},{... | collective-permute-start | bytes 1179656 | tf_op jit(solution)/shard_map/ppermute | solution.py:52
  100.8 3.1 %collective-permute-done.17 = bf16[512,512]{1,0:T(8,128)(2,1)S(1)} collective-permute-done((bf16[512,512]{1,0:T(8,128)(2,1)S(1)}, bf16[512,512]{1,0:T(8,128)(2,1)S(1)}, u32[]{:S(2)}, u32[]{:S(2)}) %collective-permute-start.17) | collective-permute-done | bytes 524320 | tf_op jit(solution)/shard_map/ppermute | solution.py:172
  103.9 2.8 %collective-permute-done.18 = bf16[512,512]{1,0:T(8,128)(2,1)S(1)} collective-permute-done((bf16[512,512]{1,0:T(8,128)(2,1)S(1)}, bf16[512,512]{1,0:T(8,128)(2,1)S(1)}, u32[]{:S(2)}, u32[]{:S(2)}) %collective-permute-start.18) | collective-permute-done | bytes 524320 | tf_op jit(solution)/shard_map/ppermute | solution.py:173
  106.8 2.2 fusion.34
  109.2 3.4 %collective-permute-start.25 = (bf16[512,896]{1,0:T(8,128)(2,1)S(1)}, bf16[512,896]{1,0:T(8,128)(2,1)S(1)}, u32[]{:S(2)}, u32[]{:S(2)}) collective-permute-start(bf16[512,896]{1,0:T(8,128)(2,1)S(1)} %pad_maximum_fusion), channel_id=1, source_target_pairs={{4,1},{1,4},{6,3},{3,6},{12,9},{9,12},{14,11},{11,14},{20,17},{17,... | collective-permute-start | bytes 2752520 | tf_op jit(solution)/shard_map/ppermute | solution.py:173
  112.5 3.5 %collective-permute-start.22 = (bf16[1536,128]{1,0:T(8,128)(2,1)S(1)}, bf16[1536,128]{1,0:T(8,128)(2,1)S(1)}, u32[]{:S(2)}, u32[]{:S(2)}) collective-permute-start(bf16[1536,128]{1,0:T(8,128)(2,1)S(1)} %get-tuple-element.160), channel_id=1, source_target_pairs={{0,8},{24,16},{1,9},{25,17},{2,10},{26,18},{3,11},{27,19},{4,12},{... | collective-permute-start | bytes 1179656 | tf_op jit(solution)/shard_map/ppermute | solution.py:52
  116.9 2.2 fusion.33
  119.1 4.1 %collective-permute-start.27 = (bf16[1536,128]{1,0:T(8,128)(2,1)S(1)}, bf16[1536,128]{1,0:T(8,128)(2,1)S(1)}, u32[]{:S(2)}, u32[]{:S(2)}) collective-permute-start(bf16[1536,128]{1,0:T(8,128)(2,1)S(1)} %get-tuple-element.295), channel_id=1, source_target_pairs={{0,8},{24,16},{1,9},{25,17},{2,10},{26,18},{3,11},{27,19},{4,12},{... | collective-permute-start | bytes 1179656 | tf_op jit(solution)/shard_map/ppermute | solution.py:52
  124.2 6.1 %collective-permute-start.23 = (bf16[1536,128]{1,0:T(8,128)(2,1)S(1)}, bf16[1536,128]{1,0:T(8,128)(2,1)S(1)}, u32[]{:S(2)}, u32[]{:S(2)}) collective-permute-start(bf16[1536,128]{1,0:T(8,128)(2,1)S(1)} %fusion.88), channel_id=1, source_target_pairs={{0,8},{24,16},{8,0},{16,24},{1,9},{25,17},{9,1},{17,25},{2,10},{26... | collective-permute-start | bytes 1179656 | tf_op jit(solution)/shard_map/ppermute | solution.py:52
  130.3 2.4 collective-permute-done.27
  134.0 5.1 %collective-permute-start.29 = (bf16[1536,128]{1,0:T(8,128)(2,1)S(1)}, bf16[1536,128]{1,0:T(8,128)(2,1)S(1)}, u32[]{:S(2)}, u32[]{:S(2)}) collective-permute-start(bf16[1536,128]{1,0:T(8,128)(2,1)S(1)} %fusion.89), channel_id=1, source_target_pairs={{0,8},{24,16},{8,0},{16,24},{1,9},{25,17},{9,1},{17,25},{2,10},{26... | collective-permute-start | bytes 1179656 | tf_op jit(solution)/shard_map/ppermute | solution.py:52
  139.1 2.1 collective-permute-done.23
  142.2 2.2 fusion.35
  144.6 5.1 %collective-permute-start.31 = (bf16[1536,128]{1,0:T(8,128)(2,1)S(1)}, bf16[1536,128]{1,0:T(8,128)(2,1)S(1)}, u32[]{:S(2)}, u32[]{:S(2)}) collective-permute-start(bf16[1536,128]{1,0:T(8,128)(2,1)S(1)} %fusion.90), channel_id=1, source_target_pairs={{0,8},{24,16},{8,0},{16,24},{1,9},{25,17},{9,1},{17,25},{2,10},{26... | collective-permute-start | bytes 1179656 | tf_op jit(solution)/shard_map/ppermute | solution.py:52
  149.7 2.2 fusion.36
  153.4 2.2 collective-permute-start.33
  155.6 4.1 %collective-permute-done.31 = bf16[1536,128]{1,0:T(8,128)(2,1)S(1)} collective-permute-done((bf16[1536,128]{1,0:T(8,128)(2,1)S(1)}, bf16[1536,128]{1,0:T(8,128)(2,1)S(1)}, u32[]{:S(2)}, u32[]{:S(2)}) %collective-permute-start.31) | collective-permute-done | bytes 393248 | tf_op jit(solution)/shard_map/ppermute | solution.py:52
  161.1 5.0 %collective-permute-start.35 = (bf16[1536,128]{1,0:T(8,128)(2,1)S(1)}, bf16[1536,128]{1,0:T(8,128)(2,1)S(1)}, u32[]{:S(2)}, u32[]{:S(2)}) collective-permute-start(bf16[1536,128]{1,0:T(8,128)(2,1)S(1)} %fusion.92), channel_id=1, source_target_pairs={{0,8},{24,16},{8,0},{16,24},{1,9},{25,17},{9,1},{17,25},{2,10},{26... | collective-permute-start | bytes 1179656 | tf_op jit(solution)/shard_map/ppermute | solution.py:52
  166.1 1.9 collective-permute-done.33
  169.0 6.7 %collective-permute-start.37 = (bf16[1536,128]{1,0:T(8,128)(2,1)S(1)}, bf16[1536,128]{1,0:T(8,128)(2,1)S(1)}, u32[]{:S(2)}, u32[]{:S(2)}) collective-permute-start(bf16[1536,128]{1,0:T(8,128)(2,1)S(1)} %fusion.93), channel_id=1, source_target_pairs={{0,8},{24,16},{8,0},{16,24},{1,9},{25,17},{9,1},{17,25},{2,10},{26... | collective-permute-start | bytes 1179656 | tf_op jit(solution)/shard_map/ppermute | solution.py:52
  175.7 3.3 %fusion.37 = bf16[1536,256]{1,0:T(8,128)(2,1)S(1)} fusion(bf16[1536,1536]{1,0:T(8,128)(2,1)S(1)} %bitcast.208, bf16[1,1536,1536]{2,1,0:T(8,128)(2,1)S(1)} %bitcast.210, bf16[1,1536,1536]{2,1,0:T(8,128)(2,1)} %param.13, bf16[1024,1536]{1,0:T(8,128)(2,1)S(1)} %constant_dynamic-update-slice_fusion, bf16[1024,256]{1,0:T(8,128)(2,1)S(1)} %get-tuple-element.213), kind=kOutput, calls=%fused_computation.56 | convolution fusion | flops 812384256 | bytes 6815744 | tf_op jit(solution)/shard_map/dot_general | solution.py:186
  181.2 3.1 %collective-permute-start.39 = (bf16[1536,128]{1,0:T(8,128)(2,1)S(1)}, bf16[1536,128]{1,0:T(8,128)(2,1)S(1)}, u32[]{:S(2)}, u32[]{:S(2)}) collective-permute-start(bf16[1536,128]{1,0:T(8,128)(2,1)S(1)} %fusion.94), channel_id=1, source_target_pairs={{0,8},{24,16},{8,0},{16,24},{1,9},{25,17},{9,1},{17,25},{2,10},{26... | collective-permute-start | bytes 1179656 | tf_op jit(solution)/shard_map/ppermute | solution.py:52
  184.9 2.5 %fusion.63 = bf16[1536,128]{1,0:T(8,128)(2,1)S(1)} fusion(bf16[1536,1536]{1,0:T(8,128)(2,1)S(1)} %bitcast.208, bf16[1,1536,1536]{2,1,0:T(8,128)(2,1)S(1)} %bitcast.210, bf16[1,1536,1536]{2,1,0:T(8,128)(2,1)} %param.13, bf16[1024,1536]{1,0:T(8,128)(2,1)S(1)} %constant_dynamic-update-slice_fusion, bf16[1024,128]{1,0:T(8,128)(2,1)S(1)} %pad_maximum_fusion.3), kind=kOutput, calls=%fused_computation.155 | convolution fusion | flops 406192128 | bytes 4980736 | tf_op jit(solution)/shard_map/dot_general | solution.py:186
  188.6 5.2 %collective-permute-start.41 = (bf16[1536,128]{1,0:T(8,128)(2,1)S(1)}, bf16[1536,128]{1,0:T(8,128)(2,1)S(1)}, u32[]{:S(2)}, u32[]{:S(2)}) collective-permute-start(bf16[1536,128]{1,0:T(8,128)(2,1)S(1)} %fusion.95), channel_id=1, source_target_pairs={{0,8},{24,16},{8,0},{16,24},{1,9},{25,17},{9,1},{17,25},{2,10},{26... | collective-permute-start | bytes 1179656 | tf_op jit(solution)/shard_map/ppermute | solution.py:52
  194.9 8.9 %collective-permute-start.43 = (bf16[1536,128]{1,0:T(8,128)(2,1)S(1)}, bf16[1536,128]{1,0:T(8,128)(2,1)S(1)}, u32[]{:S(2)}, u32[]{:S(2)}) collective-permute-start(bf16[1536,128]{1,0:T(8,128)(2,1)S(1)} %fusion.96), channel_id=1, source_target_pairs={{0,8},{24,16},{8,0},{16,24},{1,9},{25,17},{9,1},{17,25},{2,10},{26... | collective-permute-start | bytes 1179656 | tf_op jit(solution)/shard_map/ppermute | solution.py:52
  207.0 5.0 %collective-permute-done.43 = bf16[1536,128]{1,0:T(8,128)(2,1)S(1)} collective-permute-done((bf16[1536,128]{1,0:T(8,128)(2,1)S(1)}, bf16[1536,128]{1,0:T(8,128)(2,1)S(1)}, u32[]{:S(2)}, u32[]{:S(2)}) %collective-permute-start.43) | collective-permute-done | bytes 393248 | tf_op jit(solution)/shard_map/ppermute | solution.py:52
  214.7 5.7 %collective-permute-done.45 = bf16[1536,128]{1,0:T(8,128)(2,1)S(1)} collective-permute-done((bf16[1536,128]{1,0:T(8,128)(2,1)S(1)}, bf16[1536,128]{1,0:T(8,128)(2,1)S(1)}, u32[]{:S(2)}, u32[]{:S(2)}) %collective-permute-start.45) | collective-permute-done | bytes 393248 | tf_op jit(solution)/shard_map/ppermute | solution.py:52
  222.8 6.1 %collective-permute-done.47 = bf16[1536,128]{1,0:T(8,128)(2,1)S(1)} collective-permute-done((bf16[1536,128]{1,0:T(8,128)(2,1)S(1)}, bf16[1536,128]{1,0:T(8,128)(2,1)S(1)}, u32[]{:S(2)}, u32[]{:S(2)}) %collective-permute-start.47) | collective-permute-done | bytes 393248 | tf_op jit(solution)/shard_map/ppermute | solution.py:52
  228.9 4.2 %collective-permute-done.48 = bf16[1536,128]{1,0:T(8,128)(2,1)S(1)} collective-permute-done((bf16[1536,128]{1,0:T(8,128)(2,1)S(1)}, bf16[1536,128]{1,0:T(8,128)(2,1)S(1)}, u32[]{:S(2)}, u32[]{:S(2)}) %collective-permute-start.48) | collective-permute-done | bytes 393248 | tf_op jit(solution)/shard_map/ppermute | solution.py:52
  234.0 3.4 %copy-done.6 = f32[1536,1536]{1,0:T(8,128)} copy-done((f32[1536,1536]{1,0:T(8,128)}, f32[1536,1536]{1,0:T(8,128)S(1)}, u32[]{:S(2)}) %copy-start.6) | copy-done | bytes 9437208
  237.4 2.2 copy-done.7
  (192 shorter events, 45.9 us)
Async XLA Ops:
  0.6 19.7 %collective-permute-start = (bf16[256,1536]{1,0:T(8,128)(2,1)}, bf16[256,1536]{1,0:T(8,128)(2,1)}, u32[]{:S(2)}, u32[]{:S(2)}) collective-permute-start(bf16[256,1536]{1,0:T(8,128)(2,1)} %param.8), channel_id=1, source_target_pairs={{0,4},{2,6},{4,0},{6,2},{1,5},{3,7},{5,1},{7,3},{8,12},{10,14},{12... | collective-permute-start | bytes 2359304 | tf_op jit(solution)/shard_map/ppermute | solution.py:27
  3.7 16.6 %collective-permute-start.1 = (bf16[256,1536]{1,0:T(8,128)(2,1)S(1)}, bf16[256,1536]{1,0:T(8,128)(2,1)S(1)}, u32[]{:S(2)}, u32[]{:S(2)}) collective-permute-start(bf16[256,1536]{1,0:T(8,128)(2,1)S(1)} %get-tuple-element.285), channel_id=1, source_target_pairs={{0,2},{2,0},{4,6},{6,4},{1,3},{3,1},{5,7},{7,5},{8,10},{10,8},{12,... | collective-permute-start | bytes 2359304 | tf_op jit(solution)/shard_map/ppermute | solution.py:27
  3.9 16.4 %collective-permute-start.2 = (bf16[256,1536]{1,0:T(8,128)(2,1)S(1)}, bf16[256,1536]{1,0:T(8,128)(2,1)S(1)}, u32[]{:S(2)}, u32[]{:S(2)}) collective-permute-start(bf16[256,1536]{1,0:T(8,128)(2,1)S(1)} %get-tuple-element.283), channel_id=1, source_target_pairs={{0,2},{2,0},{4,6},{6,4},{1,3},{3,1},{5,7},{7,5},{8,10},{10,8},{12,... | collective-permute-start | bytes 2359304 | tf_op jit(solution)/shard_map/ppermute | solution.py:27
  4.8 22.8 %collective-permute-start.5 = (bf16[256,1536]{1,0:T(8,128)(2,1)S(1)}, bf16[256,1536]{1,0:T(8,128)(2,1)S(1)}, u32[]{:S(2)}, u32[]{:S(2)}) collective-permute-start(bf16[256,1536]{1,0:T(8,128)(2,1)S(1)} %copy-done.3), channel_id=1, source_target_pairs={{0,2},{2,0},{4,6},{6,4},{1,3},{3,1},{5,7},{7,5},{8,10},{10,8},{12,... | collective-permute-start | bytes 2359304 | tf_op jit(solution)/shard_map/ppermute | solution.py:27
  21.2 17.7 %collective-permute-start.9 = (bf16[256,1536]{1,0:T(8,128)(2,1)}, bf16[256,1536]{1,0:T(8,128)(2,1)S(1)}, u32[]{:S(2)}, u32[]{:S(2)}) collective-permute-start(bf16[256,1536]{1,0:T(8,128)(2,1)} %collective-permute-done), channel_id=1, source_target_pairs={{0,2},{2,0},{4,6},{6,4},{1,3},{3,1},{5,7},{7,5},{8,10},{10,8},{12,... | collective-permute-start | bytes 2359304 | tf_op jit(solution)/shard_map/ppermute | solution.py:27
  26.1 11.5 %collective-permute-start.6 = (bf16[128,1536]{1,0:T(8,128)(2,1)S(1)}, bf16[128,1536]{1,0:T(8,128)(2,1)}, u32[]{:S(2)}, u32[]{:S(2)}) collective-permute-start(bf16[128,1536]{1,0:T(8,128)(2,1)S(1)} %get-tuple-element.297), channel_id=1, source_target_pairs={{0,4},{2,6},{4,0},{6,2},{1,5},{3,7},{5,1},{7,3},{8,12},{10,14},{12... | collective-permute-start | bytes 1179656 | tf_op jit(solution)/shard_map/ppermute | solution.py:27
  31.8 36.6 %collective-permute-start.7 = (bf16[512,1536]{1,0:T(8,128)(2,1)}, bf16[512,1536]{1,0:T(8,128)(2,1)}, u32[]{:S(2)}, u32[]{:S(2)}) collective-permute-start(bf16[512,1536]{1,0:T(8,128)(2,1)} %convolution_convert_fusion), channel_id=1, source_target_pairs={{4,5},{1,0},{6,7},{3,2},{12,13},{9,8},{14,15},{11,10},{20,21},{17,... | collective-permute-start | bytes 4718600 | tf_op jit(solution)/shard_map/ppermute | solution.py:113
  35.4 13.2 %collective-permute-start.3 = (bf16[128,1536]{1,0:T(8,128)(2,1)}, bf16[128,1536]{1,0:T(8,128)(2,1)}, u32[]{:S(2)}, u32[]{:S(2)}) collective-permute-start(bf16[128,1536]{1,0:T(8,128)(2,1)} %get-tuple-element.298), channel_id=1, source_target_pairs={{0,4},{2,6},{4,0},{6,2},{1,5},{3,7},{5,1},{7,3},{8,12},{10,14},{12... | collective-permute-start | bytes 1179656 | tf_op jit(solution)/shard_map/ppermute | solution.py:27
  37.6 27.1 %collective-permute-start.8 = (bf16[128,1536]{1,0:T(8,128)(2,1)}, bf16[128,1536]{1,0:T(8,128)(2,1)}, u32[]{:S(2)}, u32[]{:S(2)}) collective-permute-start(bf16[128,1536]{1,0:T(8,128)(2,1)} %collective-permute-done.6), channel_id=1, source_target_pairs={{0,1},{5,4},{2,3},{7,6},{8,9},{13,12},{10,11},{15,14},{16,17},{21,... | collective-permute-start | bytes 1179656 | tf_op jit(solution)/shard_map/ppermute | solution.py:118
  41.2 14.8 %collective-permute-start.12 = (bf16[128,1536]{1,0:T(8,128)(2,1)}, bf16[128,1536]{1,0:T(8,128)(2,1)S(1)}, u32[]{:S(2)}, u32[]{:S(2)}) collective-permute-start(bf16[128,1536]{1,0:T(8,128)(2,1)} %get-tuple-element.300), channel_id=1, source_target_pairs={{0,4},{2,6},{4,0},{6,2},{1,5},{3,7},{5,1},{7,3},{8,12},{10,14},{12... | collective-permute-start | bytes 1179656 | tf_op jit(solution)/shard_map/ppermute | solution.py:27
  44.6 18.7 %collective-permute-start.10 = (bf16[128,1536]{1,0:T(8,128)(2,1)}, bf16[128,1536]{1,0:T(8,128)(2,1)}, u32[]{:S(2)}, u32[]{:S(2)}) collective-permute-start(bf16[128,1536]{1,0:T(8,128)(2,1)} %get-tuple-element.299), channel_id=1, source_target_pairs={{0,4},{2,6},{4,0},{6,2},{1,5},{3,7},{5,1},{7,3},{8,12},{10,14},{12... | collective-permute-start | bytes 1179656 | tf_op jit(solution)/shard_map/ppermute | solution.py:27
  48.6 21.7 %collective-permute-start.4 = (bf16[128,1536]{1,0:T(8,128)(2,1)}, bf16[128,1536]{1,0:T(8,128)(2,1)S(1)}, u32[]{:S(2)}, u32[]{:S(2)}) collective-permute-start(bf16[128,1536]{1,0:T(8,128)(2,1)} %collective-permute-done.3), channel_id=1, source_target_pairs={{0,1},{5,4},{2,3},{7,6},{8,9},{13,12},{10,11},{15,14},{16,17},{21,... | collective-permute-start | bytes 1179656 | tf_op jit(solution)/shard_map/ppermute | solution.py:118
  56.0 23.3 %collective-permute-start.13 = (bf16[128,1536]{1,0:T(8,128)(2,1)S(1)}, bf16[128,1536]{1,0:T(8,128)(2,1)S(1)}, u32[]{:S(2)}, u32[]{:S(2)}) collective-permute-start(bf16[128,1536]{1,0:T(8,128)(2,1)S(1)} %collective-permute-done.12), channel_id=1, source_target_pairs={{0,1},{5,4},{2,3},{7,6},{8,9},{13,12},{10,11},{15,14},{16,17},{21,... | collective-permute-start | bytes 1179656 | tf_op jit(solution)/shard_map/ppermute | solution.py:118
  63.4 14.2 %collective-permute-start.11 = (bf16[128,1536]{1,0:T(8,128)(2,1)}, bf16[128,1536]{1,0:T(8,128)(2,1)S(1)}, u32[]{:S(2)}, u32[]{:S(2)}) collective-permute-start(bf16[128,1536]{1,0:T(8,128)(2,1)} %collective-permute-done.10), channel_id=1, source_target_pairs={{0,1},{5,4},{2,3},{7,6},{8,9},{13,12},{10,11},{15,14},{16,17},{21,... | collective-permute-start | bytes 1179656 | tf_op jit(solution)/shard_map/ppermute | solution.py:118
  82.7 3.7 %collective-permute-start.15 = (f32[2,512]{1,0:T(2,128)S(1)}, f32[2,512]{1,0:T(2,128)S(1)}, u32[]{:S(2)}, u32[]{:S(2)}) collective-permute-start(f32[2,512]{1,0:T(2,128)S(1)} %maximum_add_fusion), channel_id=1, source_target_pairs={{0,1},{1,0},{2,3},{3,2},{4,5},{5,4},{6,7},{7,6},{8,9},{9,8},{10,11... | collective-permute-start | bytes 12296 | tf_op jit(solution)/shard_map/ppermute | solution.py:27
  87.0 5.0 %collective-permute-start.16 = (bf16[512,128]{1,0:T(8,128)(2,1)S(1)}, bf16[512,128]{1,0:T(8,128)(2,1)S(1)}, u32[]{:S(2)}, u32[]{:S(2)}) collective-permute-start(bf16[512,128]{1,0:T(8,128)(2,1)S(1)} %pad_maximum_fusion.5), channel_id=1, source_target_pairs={{0,1},{5,4},{4,0},{1,5},{2,3},{7,6},{6,2},{3,7},{8,9},{13,12},{12,... | collective-permute-start | bytes 393224 | tf_op jit(solution)/shard_map/ppermute | solution.py:172
  87.1 8.3 %collective-permute-start.19 = (bf16[512,128]{1,0:T(8,128)(2,1)S(1)}, bf16[512,128]{1,0:T(8,128)(2,1)S(1)}, u32[]{:S(2)}, u32[]{:S(2)}) collective-permute-start(bf16[512,128]{1,0:T(8,128)(2,1)S(1)} %pad_maximum_fusion.5), channel_id=1, source_target_pairs={{4,1},{1,4},{6,3},{3,6},{12,9},{9,12},{14,11},{11,14},{20,17},{17,... | collective-permute-start | bytes 393224 | tf_op jit(solution)/shard_map/ppermute | solution.py:173
  92.0 11.8 %collective-permute-start.17 = (bf16[512,512]{1,0:T(8,128)(2,1)S(1)}, bf16[512,512]{1,0:T(8,128)(2,1)S(1)}, u32[]{:S(2)}, u32[]{:S(2)}) collective-permute-start(bf16[512,512]{1,0:T(8,128)(2,1)S(1)} %pad_maximum_fusion.2), channel_id=1, source_target_pairs={{0,1},{5,4},{4,0},{1,5},{2,3},{7,6},{6,2},{3,7},{8,9},{13,12},{12,... | collective-permute-start | bytes 1572872 | tf_op jit(solution)/shard_map/ppermute | solution.py:172
  92.1 14.6 %collective-permute-start.18 = (bf16[512,512]{1,0:T(8,128)(2,1)S(1)}, bf16[512,512]{1,0:T(8,128)(2,1)S(1)}, u32[]{:S(2)}, u32[]{:S(2)}) collective-permute-start(bf16[512,512]{1,0:T(8,128)(2,1)S(1)} %pad_maximum_fusion.2), channel_id=1, source_target_pairs={{4,1},{1,4},{6,3},{3,6},{12,9},{9,12},{14,11},{11,14},{20,17},{17,... | collective-permute-start | bytes 1572872 | tf_op jit(solution)/shard_map/ppermute | solution.py:173
  97.1 19.0 %collective-permute-start.20 = (bf16[1536,128]{1,0:T(8,128)(2,1)S(1)}, bf16[1536,128]{1,0:T(8,128)(2,1)S(1)}, u32[]{:S(2)}, u32[]{:S(2)}) collective-permute-start(bf16[1536,128]{1,0:T(8,128)(2,1)S(1)} %fusion.62), channel_id=1, source_target_pairs={{0,8},{24,16},{1,9},{25,17},{2,10},{26,18},{3,11},{27,19},{4,12},{... | collective-permute-start | bytes 1179656 | tf_op jit(solution)/shard_map/ppermute | solution.py:52
  109.1 24.4 %collective-permute-start.24 = (bf16[512,896]{1,0:T(8,128)(2,1)S(1)}, bf16[512,896]{1,0:T(8,128)(2,1)S(1)}, u32[]{:S(2)}, u32[]{:S(2)}) collective-permute-start(bf16[512,896]{1,0:T(8,128)(2,1)S(1)} %pad_maximum_fusion), channel_id=1, source_target_pairs={{0,1},{5,4},{4,0},{1,5},{2,3},{7,6},{6,2},{3,7},{8,9},{13,12},{12,... | collective-permute-start | bytes 2752520 | tf_op jit(solution)/shard_map/ppermute | solution.py:172
  109.2 24.4 %collective-permute-start.25 = (bf16[512,896]{1,0:T(8,128)(2,1)S(1)}, bf16[512,896]{1,0:T(8,128)(2,1)S(1)}, u32[]{:S(2)}, u32[]{:S(2)}) collective-permute-start(bf16[512,896]{1,0:T(8,128)(2,1)S(1)} %pad_maximum_fusion), channel_id=1, source_target_pairs={{4,1},{1,4},{6,3},{3,6},{12,9},{9,12},{14,11},{11,14},{20,17},{17,... | collective-permute-start | bytes 2752520 | tf_op jit(solution)/shard_map/ppermute | solution.py:173
  112.5 10.6 %collective-permute-start.22 = (bf16[1536,128]{1,0:T(8,128)(2,1)S(1)}, bf16[1536,128]{1,0:T(8,128)(2,1)S(1)}, u32[]{:S(2)}, u32[]{:S(2)}) collective-permute-start(bf16[1536,128]{1,0:T(8,128)(2,1)S(1)} %get-tuple-element.160), channel_id=1, source_target_pairs={{0,8},{24,16},{1,9},{25,17},{2,10},{26,18},{3,11},{27,19},{4,12},{... | collective-permute-start | bytes 1179656 | tf_op jit(solution)/shard_map/ppermute | solution.py:52
  116.2 7.8 %collective-permute-start.21 = (bf16[1536,128]{1,0:T(8,128)(2,1)S(1)}, bf16[1536,128]{1,0:T(8,128)(2,1)S(1)}, u32[]{:S(2)}, u32[]{:S(2)}) collective-permute-start(bf16[1536,128]{1,0:T(8,128)(2,1)S(1)} %add_convert_fusion.35), channel_id=1, source_target_pairs={{8,16},{16,8},{9,17},{17,9},{10,18},{18,10},{11,19},{19,11},{12,20... | collective-permute-start | bytes 1179656 | tf_op jit(solution)/shard_map/ppermute | solution.py:60
  119.1 13.6 %collective-permute-start.27 = (bf16[1536,128]{1,0:T(8,128)(2,1)S(1)}, bf16[1536,128]{1,0:T(8,128)(2,1)S(1)}, u32[]{:S(2)}, u32[]{:S(2)}) collective-permute-start(bf16[1536,128]{1,0:T(8,128)(2,1)S(1)} %get-tuple-element.295), channel_id=1, source_target_pairs={{0,8},{24,16},{1,9},{25,17},{2,10},{26,18},{3,11},{27,19},{4,12},{... | collective-permute-start | bytes 1179656 | tf_op jit(solution)/shard_map/ppermute | solution.py:52
  123.3 10.2 %collective-permute-start.26 = (bf16[1536,128]{1,0:T(8,128)(2,1)S(1)}, bf16[1536,128]{1,0:T(8,128)(2,1)S(1)}, u32[]{:S(2)}, u32[]{:S(2)}) collective-permute-start(bf16[1536,128]{1,0:T(8,128)(2,1)S(1)} %add_convert_fusion.34), channel_id=1, source_target_pairs={{8,16},{16,8},{9,17},{17,9},{10,18},{18,10},{11,19},{19,11},{12,20... | collective-permute-start | bytes 1179656 | tf_op jit(solution)/shard_map/ppermute | solution.py:60
  124.2 17.0 %collective-permute-start.23 = (bf16[1536,128]{1,0:T(8,128)(2,1)S(1)}, bf16[1536,128]{1,0:T(8,128)(2,1)S(1)}, u32[]{:S(2)}, u32[]{:S(2)}) collective-permute-start(bf16[1536,128]{1,0:T(8,128)(2,1)S(1)} %fusion.88), channel_id=1, source_target_pairs={{0,8},{24,16},{8,0},{16,24},{1,9},{25,17},{9,1},{17,25},{2,10},{26... | collective-permute-start | bytes 1179656 | tf_op jit(solution)/shard_map/ppermute | solution.py:52
  132.8 9.4 %collective-permute-start.28 = (bf16[1536,128]{1,0:T(8,128)(2,1)S(1)}, bf16[1536,128]{1,0:T(8,128)(2,1)S(1)}, u32[]{:S(2)}, u32[]{:S(2)}) collective-permute-start(bf16[1536,128]{1,0:T(8,128)(2,1)S(1)} %add_convert_fusion.32), channel_id=1, source_target_pairs={{8,16},{16,8},{9,17},{17,9},{10,18},{18,10},{11,19},{19,11},{12,20... | collective-permute-start | bytes 1179656 | tf_op jit(solution)/shard_map/ppermute | solution.py:60
  134.0 18.4 %collective-permute-start.29 = (bf16[1536,128]{1,0:T(8,128)(2,1)S(1)}, bf16[1536,128]{1,0:T(8,128)(2,1)S(1)}, u32[]{:S(2)}, u32[]{:S(2)}) collective-permute-start(bf16[1536,128]{1,0:T(8,128)(2,1)S(1)} %fusion.89), channel_id=1, source_target_pairs={{0,8},{24,16},{8,0},{16,24},{1,9},{25,17},{9,1},{17,25},{2,10},{26... | collective-permute-start | bytes 1179656 | tf_op jit(solution)/shard_map/ppermute | solution.py:52
  141.2 11.9 %collective-permute-start.30 = (bf16[1536,128]{1,0:T(8,128)(2,1)S(1)}, bf16[1536,128]{1,0:T(8,128)(2,1)S(1)}, u32[]{:S(2)}, u32[]{:S(2)}) collective-permute-start(bf16[1536,128]{1,0:T(8,128)(2,1)S(1)} %add_convert_fusion.30), channel_id=1, source_target_pairs={{8,16},{16,8},{9,17},{17,9},{10,18},{18,10},{11,19},{19,11},{12,20... | collective-permute-start | bytes 1179656 | tf_op jit(solution)/shard_map/ppermute | solution.py:60
  144.6 15.1 %collective-permute-start.31 = (bf16[1536,128]{1,0:T(8,128)(2,1)S(1)}, bf16[1536,128]{1,0:T(8,128)(2,1)S(1)}, u32[]{:S(2)}, u32[]{:S(2)}) collective-permute-start(bf16[1536,128]{1,0:T(8,128)(2,1)S(1)} %fusion.90), channel_id=1, source_target_pairs={{0,8},{24,16},{8,0},{16,24},{1,9},{25,17},{9,1},{17,25},{2,10},{26... | collective-permute-start | bytes 1179656 | tf_op jit(solution)/shard_map/ppermute | solution.py:52
  152.5 8.5 %collective-permute-start.32 = (bf16[1536,128]{1,0:T(8,128)(2,1)S(1)}, bf16[1536,128]{1,0:T(8,128)(2,1)S(1)}, u32[]{:S(2)}, u32[]{:S(2)}) collective-permute-start(bf16[1536,128]{1,0:T(8,128)(2,1)S(1)} %add_convert_fusion.28), channel_id=1, source_target_pairs={{8,16},{16,8},{9,17},{17,9},{10,18},{18,10},{11,19},{19,11},{12,20... | collective-permute-start | bytes 1179656 | tf_op jit(solution)/shard_map/ppermute | solution.py:60
  153.4 14.7 %collective-permute-start.33 = (bf16[1536,128]{1,0:T(8,128)(2,1)S(1)}, bf16[1536,128]{1,0:T(8,128)(2,1)S(1)}, u32[]{:S(2)}, u32[]{:S(2)}) collective-permute-start(bf16[1536,128]{1,0:T(8,128)(2,1)S(1)} %fusion.91), channel_id=1, source_target_pairs={{0,8},{24,16},{8,0},{16,24},{1,9},{25,17},{9,1},{17,25},{2,10},{26... | collective-permute-start | bytes 1179656 | tf_op jit(solution)/shard_map/ppermute | solution.py:52
  159.8 9.0 %collective-permute-start.34 = (bf16[1536,128]{1,0:T(8,128)(2,1)S(1)}, bf16[1536,128]{1,0:T(8,128)(2,1)S(1)}, u32[]{:S(2)}, u32[]{:S(2)}) collective-permute-start(bf16[1536,128]{1,0:T(8,128)(2,1)S(1)} %add_convert_fusion.26), channel_id=1, source_target_pairs={{8,16},{16,8},{9,17},{17,9},{10,18},{18,10},{11,19},{19,11},{12,20... | collective-permute-start | bytes 1179656 | tf_op jit(solution)/shard_map/ppermute | solution.py:60
  161.1 18.8 %collective-permute-start.35 = (bf16[1536,128]{1,0:T(8,128)(2,1)S(1)}, bf16[1536,128]{1,0:T(8,128)(2,1)S(1)}, u32[]{:S(2)}, u32[]{:S(2)}) collective-permute-start(bf16[1536,128]{1,0:T(8,128)(2,1)S(1)} %fusion.92), channel_id=1, source_target_pairs={{0,8},{24,16},{8,0},{16,24},{1,9},{25,17},{9,1},{17,25},{2,10},{26... | collective-permute-start | bytes 1179656 | tf_op jit(solution)/shard_map/ppermute | solution.py:52
  168.1 12.9 %collective-permute-start.36 = (bf16[1536,128]{1,0:T(8,128)(2,1)S(1)}, bf16[1536,128]{1,0:T(8,128)(2,1)S(1)}, u32[]{:S(2)}, u32[]{:S(2)}) collective-permute-start(bf16[1536,128]{1,0:T(8,128)(2,1)S(1)} %add_convert_fusion.24), channel_id=1, source_target_pairs={{8,16},{16,8},{9,17},{17,9},{10,18},{18,10},{11,19},{19,11},{12,20... | collective-permute-start | bytes 1179656 | tf_op jit(solution)/shard_map/ppermute | solution.py:60
  169.0 15.7 %collective-permute-start.37 = (bf16[1536,128]{1,0:T(8,128)(2,1)S(1)}, bf16[1536,128]{1,0:T(8,128)(2,1)S(1)}, u32[]{:S(2)}, u32[]{:S(2)}) collective-permute-start(bf16[1536,128]{1,0:T(8,128)(2,1)S(1)} %fusion.93), channel_id=1, source_target_pairs={{0,8},{24,16},{8,0},{16,24},{1,9},{25,17},{9,1},{17,25},{2,10},{26... | collective-permute-start | bytes 1179656 | tf_op jit(solution)/shard_map/ppermute | solution.py:52
  180.1 8.4 %collective-permute-start.38 = (bf16[1536,128]{1,0:T(8,128)(2,1)S(1)}, bf16[1536,128]{1,0:T(8,128)(2,1)S(1)}, u32[]{:S(2)}, u32[]{:S(2)}) collective-permute-start(bf16[1536,128]{1,0:T(8,128)(2,1)S(1)} %add_convert_fusion.22), channel_id=1, source_target_pairs={{8,16},{16,8},{9,17},{17,9},{10,18},{18,10},{11,19},{19,11},{12,20... | collective-permute-start | bytes 1179656 | tf_op jit(solution)/shard_map/ppermute | solution.py:60
  181.2 12.7 %collective-permute-start.39 = (bf16[1536,128]{1,0:T(8,128)(2,1)S(1)}, bf16[1536,128]{1,0:T(8,128)(2,1)S(1)}, u32[]{:S(2)}, u32[]{:S(2)}) collective-permute-start(bf16[1536,128]{1,0:T(8,128)(2,1)S(1)} %fusion.94), channel_id=1, source_target_pairs={{0,8},{24,16},{8,0},{16,24},{1,9},{25,17},{9,1},{17,25},{2,10},{26... | collective-permute-start | bytes 1179656 | tf_op jit(solution)/shard_map/ppermute | solution.py:52
  187.3 7.4 %collective-permute-start.40 = (bf16[1536,128]{1,0:T(8,128)(2,1)S(1)}, bf16[1536,128]{1,0:T(8,128)(2,1)S(1)}, u32[]{:S(2)}, u32[]{:S(2)}) collective-permute-start(bf16[1536,128]{1,0:T(8,128)(2,1)S(1)} %add_convert_fusion.20), channel_id=1, source_target_pairs={{8,16},{16,8},{9,17},{17,9},{10,18},{18,10},{11,19},{19,11},{12,20... | collective-permute-start | bytes 1179656 | tf_op jit(solution)/shard_map/ppermute | solution.py:60
  188.6 16.1 %collective-permute-start.41 = (bf16[1536,128]{1,0:T(8,128)(2,1)S(1)}, bf16[1536,128]{1,0:T(8,128)(2,1)S(1)}, u32[]{:S(2)}, u32[]{:S(2)}) collective-permute-start(bf16[1536,128]{1,0:T(8,128)(2,1)S(1)} %fusion.95), channel_id=1, source_target_pairs={{0,8},{24,16},{8,0},{16,24},{1,9},{25,17},{9,1},{17,25},{2,10},{26... | collective-permute-start | bytes 1179656 | tf_op jit(solution)/shard_map/ppermute | solution.py:52
  194.0 11.5 %collective-permute-start.42 = (bf16[1536,128]{1,0:T(8,128)(2,1)S(1)}, bf16[1536,128]{1,0:T(8,128)(2,1)S(1)}, u32[]{:S(2)}, u32[]{:S(2)}) collective-permute-start(bf16[1536,128]{1,0:T(8,128)(2,1)S(1)} %add_convert_fusion.18), channel_id=1, source_target_pairs={{8,16},{16,8},{9,17},{17,9},{10,18},{18,10},{11,19},{19,11},{12,20... | collective-permute-start | bytes 1179656 | tf_op jit(solution)/shard_map/ppermute | solution.py:60
  194.9 17.1 %collective-permute-start.43 = (bf16[1536,128]{1,0:T(8,128)(2,1)S(1)}, bf16[1536,128]{1,0:T(8,128)(2,1)S(1)}, u32[]{:S(2)}, u32[]{:S(2)}) collective-permute-start(bf16[1536,128]{1,0:T(8,128)(2,1)S(1)} %fusion.96), channel_id=1, source_target_pairs={{0,8},{24,16},{8,0},{16,24},{1,9},{25,17},{9,1},{17,25},{2,10},{26... | collective-permute-start | bytes 1179656 | tf_op jit(solution)/shard_map/ppermute | solution.py:52
  204.8 8.5 %collective-permute-start.44 = (bf16[1536,128]{1,0:T(8,128)(2,1)S(1)}, bf16[1536,128]{1,0:T(8,128)(2,1)S(1)}, u32[]{:S(2)}, u32[]{:S(2)}) collective-permute-start(bf16[1536,128]{1,0:T(8,128)(2,1)S(1)} %add_convert_fusion.16), channel_id=1, source_target_pairs={{8,16},{16,8},{9,17},{17,9},{10,18},{18,10},{11,19},{19,11},{12,20... | collective-permute-start | bytes 1179656 | tf_op jit(solution)/shard_map/ppermute | solution.py:60
  205.7 14.8 %collective-permute-start.45 = (bf16[1536,128]{1,0:T(8,128)(2,1)S(1)}, bf16[1536,128]{1,0:T(8,128)(2,1)S(1)}, u32[]{:S(2)}, u32[]{:S(2)}) collective-permute-start(bf16[1536,128]{1,0:T(8,128)(2,1)S(1)} %add_convert_fusion.15), channel_id=1, source_target_pairs={{8,0},{16,24},{9,1},{17,25},{10,2},{18,26},{11,3},{19,27},{12,4},{... | collective-permute-start | bytes 1179656 | tf_op jit(solution)/shard_map/ppermute | solution.py:52
  212.1 8.3 %collective-permute-start.46 = (bf16[1536,128]{1,0:T(8,128)(2,1)S(1)}, bf16[1536,128]{1,0:T(8,128)(2,1)S(1)}, u32[]{:S(2)}, u32[]{:S(2)}) collective-permute-start(bf16[1536,128]{1,0:T(8,128)(2,1)S(1)} %add_convert_fusion.14), channel_id=1, source_target_pairs={{8,16},{16,8},{9,17},{17,9},{10,18},{18,10},{11,19},{19,11},{12,20... | collective-permute-start | bytes 1179656 | tf_op jit(solution)/shard_map/ppermute | solution.py:60
  213.4 15.4 %collective-permute-start.47 = (bf16[1536,128]{1,0:T(8,128)(2,1)S(1)}, bf16[1536,128]{1,0:T(8,128)(2,1)S(1)}, u32[]{:S(2)}, u32[]{:S(2)}) collective-permute-start(bf16[1536,128]{1,0:T(8,128)(2,1)S(1)} %add_convert_fusion.13), channel_id=1, source_target_pairs={{8,0},{16,24},{9,1},{17,25},{10,2},{18,26},{11,3},{19,27},{12,4},{... | collective-permute-start | bytes 1179656 | tf_op jit(solution)/shard_map/ppermute | solution.py:52
  220.5 12.5 %collective-permute-start.48 = (bf16[1536,128]{1,0:T(8,128)(2,1)S(1)}, bf16[1536,128]{1,0:T(8,128)(2,1)S(1)}, u32[]{:S(2)}, u32[]{:S(2)}) collective-permute-start(bf16[1536,128]{1,0:T(8,128)(2,1)S(1)} %add_convert_fusion.12), channel_id=1, source_target_pairs={{8,0},{16,24},{9,1},{17,25},{10,2},{18,26},{11,3},{19,27},{12,4},{... | collective-permute-start | bytes 1179656 | tf_op jit(solution)/shard_map/ppermute | solution.py:52
  (20 other events, 168.9 us)

commit v9 on v8

--- a/solution.py
+++ b/solution.py
@@ -111,10 +111,12 @@
     far_blocks = [held[0]] + [swap(held[0], "fsdp", r) for r in range(1, group)]
     near_out = project(jnp.concatenate(near_blocks, axis=0))
     near_came = lax.ppermute(near_out, ("fsdp", "tp"), inward_pairs)
-    far_outs = []
-    for r in range(group):
-        out = project(far_blocks[r])
-        far_outs += [swap(out[p * rows : (p + 1) * rows], "fsdp", group) for p in range(pieces)]
+    far_blocks[0], near_out = together(far_blocks[0], near_out)
+    far_outs = [
+        swap(project(far_blocks[r][p * rows : (p + 1) * rows]), "fsdp", group)
+        for r in range(group)
+        for p in range(pieces)
+    ]
     passed = [lax.ppermute(out, ("fsdp", "tp"), outward_pairs) for out in far_outs]
 
     gain_part = lax.dynamic_slice_in_dim(gain, t * (width // 2) + low * cols, cols).astype(f32)
@@ -123,13 +125,17 @@
     for k in range(group * pieces):
         r, p = k // pieces, k % pieces
         span, long_span = slice(p * rows, (p + 1) * rows), slice(k * rows, (k + 1) * rows)
-        res, cot, came = residual_parts[r], cotangent_parts[r], passed[k]
+        keep = jnp.where(near, near_out[long_span], far_outs[k])
+        base, w = lax.optimization_barrier(
+            (
+                residual_parts[r][span].astype(f32) + keep.astype(f32),
+                gain_part[None, :] * cotangent_parts[r][span].astype(f32),
+            )
+        )
+        came = passed[k]
         if sums:
             came, sums[-1] = together(came, sums[-1])
-        keep = jnp.where(near, near_out[long_span], far_outs[k])
-        came = jnp.where(near, near_came[long_span], came)
-        h = res[span].astype(f32) + keep.astype(f32) + came.astype(f32)
-        w = gain_part[None, :] * cot[span].astype(f32)
+        h = base + jnp.where(near, near_came[long_span], came).astype(f32)
         hidden.append(h)
         weighted.append(w)
         sums.append(jnp.stack([jnp.sum(h * h, axis=-1), jnp.sum(h * w, axis=-1)]))
@@ -149,7 +155,7 @@
     context_all = jnp.concatenate(near_blocks + far_blocks, axis=0)
     narrow = 128
     units = cols // narrow
-    widths = [1, min(4, units - 2), units - 1 - min(4, units - 2)]
+    widths = [3, units - 3]
     islands = lax.axis_size("island")
     line = IslandLine(units)
     parts, locals_, rings, crosses = [], [], [], []
@@ -164,10 +170,6 @@
             ],
             axis=0,
         ).astype(bf16)
-        if c == 1:
-            d_local, rings[0] = together(d_local, rings[0])
-        elif c == 2:
-            d_local, parts[1] = together(d_local, parts[1])
         locals_.append(d_local)
         rings.append(lax.ppermute(d_local, ("fsdp", "tp"), ring_pairs))
         crosses.append(lax.ppermute(d_local, ("fsdp", "tp"), cross_pairs))
@@ -198,17 +200,13 @@
             line.part[len(parts)] = pseudo[:, u * narrow : (u + 1) * narrow]
             parts.append(line.part[len(parts)])
 
-    move(0)
-    move(1)
-    add_pseudo(gathered(0), 0, 1)
-    early = sum(widths[:2])
-    middle = gathered(1)
-    for lo in range(1, early, 2):
-        add_pseudo(middle[:, (lo - 1) * narrow :], lo, min(lo + 2, early))
-        if lo == 1:
-            move(2)
-            line.part[1] = parts[1]
-    last = gathered(2)
+    for c in range(len(widths)):
+        move(c)
+    early = widths[0]
+    found = gathered(0)
+    add_pseudo(found, 0, 1)
+    add_pseudo(found[:, narrow:], 1, early)
+    last = gathered(1)
     todo = [(lo, min(lo + 2, units)) for lo in range(early, units, 2)]
     if islands == 4:
         for s in range(2):

time: 241 us -> 248 us (1.029)
  waiting for transfers between devices: 81.5 us -> 105 us
  starting transfers between devices: 97.7 us -> 89.1 us
  other arithmetic: 18.1 us -> 14.5 us
  local copies, waits for them, and re-layouts: 14.9 us -> 12.1 us
    ppermute x4, waiting for transfers between devices: 5.43 us -> 17.4 us  [body(): lax.ppermute(out, ('fsdp', 'tp'), outward_pairs)]
    ppermute x11, waiting for transfers between devices: 33.4 us -> 42.3 us  [swap(): return lax.ppermute(value, axis, [(i, i ^ bit) for i in range(count)])]
    reduce_sum x4, other arithmetic: 7.18 us -> 1.22 us  [body(): sums.append(jnp.stack([jnp.sum(h * h, axis=-1), jnp.sum(h * w, axis=-1)]))]
    ppermute x15, waiting for transfers between devices: 32 us -> 37.9 us  [send_outer(): self.edge[s] = lax.ppermute(payload, 'island', pairs)]
    ppermute x15, starting transfers between devices: 62.6 us -> 58.3 us  [send_outer(): self.edge[s] = lax.ppermute(payload, 'island', pairs)]
    ppermute x1, waiting for transfers between devices: 3.75 us -> 0.01 us  [body(): near_came = lax.ppermute(near_out, ('fsdp', 'tp'), inward_pairs)]
    ppermute x3 -> x2, starting transfers between devices: 10.2 us -> 6.99 us  [move(): crosses.append(lax.ppermute(d_local, ('fsdp', 'tp'), cross_pairs))]
    unnamed x41 -> x27, local copies, waits for them, and re-layouts: 11.5 us -> 8.53 us
  transfers between devices with their start and end apart: 49 -> 47, of which waited for: 19 -> 19; matrix products, arithmetic and copies ran while one was open for 20% -> 18% of each run, Pallas kernels for 0% -> 0%
where the time goes in v9:
time: 248 us; the launch traced here: 247 us
  waiting for transfers between devices  105 us (42%)
  starting transfers between devices  89.1 us (36%)
  matrix products  24.6 us (10%)
  other arithmetic  14.5 us (6%)
  local copies, waits for them, and re-layouts  12.1 us (5%)
    ppermute x15, starting transfers between devices, send_outer(): self.edge[s] = lax.ppermute(payload, 'island', pairs)  58.3 us
    ppermute x11, waiting for transfers between devices, swap(): return lax.ppermute(value, axis, [(i, i ^ bit) for i in range(count)])  42.3 us
    ppermute x15, waiting for transfers between devices, send_outer(): self.edge[s] = lax.ppermute(payload, 'island', pairs)  37.9 us
    ppermute x4, waiting for transfers between devices, body(): lax.ppermute(out, ('fsdp', 'tp'), outward_pairs)  17.4 us
    dot_general x7, matrix products, add_pseudo(): lax.dot_general(context_all, piece, (((0,), (0,)), ((), ())), preferred_e...  15.9 us
    dot_general x5, matrix products, project(): jnp.dot(block, weight, preferred_element_type=f32).astype(bf16)  8.7 us
    ppermute x12, starting transfers between devices, step(): self.mid[s] = lax.ppermute(self.sums[s], 'island', [(1, 2), (2, 1)])  8.58 us
    unnamed x27, local copies, waits for them, and re-layouts  8.53 us
  transfers between devices with their start and end apart: 47, of which 19 were waited for; matrix products, arithmetic and copies ran while one was open for 18% of the time, Pallas kernels for 0%

profile of v9, /device:TPU:2, one launch (start us, length us, event | category | flops | bytes accessed | tf_op | source)
XLA Modules:
  0.0 247.0 jit_solution(4937534306660702601)
XLA Ops:
  0.6 1.6 collective-permute-start
  2.2 2.5 constant_dynamic-slice_fusion.2
  8.1 12.0 %collective-permute-done = bf16[256,1536]{1,0:T(8,128)(2,1)S(1)} collective-permute-done((bf16[256,1536]{1,0:T(8,128)(2,1)}, bf16[256,1536]{1,0:T(8,128)(2,1)S(1)}, u32[]{:S(2)}, u32[]{:S(2)}) %collective-permute-start) | collective-permute-done | bytes 786464 | tf_op jit(solution)/shard_map/ppermute | solution.py:27
  20.3 5.6 %convolution_convert_fusion = bf16[512,1536]{1,0:T(8,128)(2,1)S(1)} fusion(bf16[1536,1536]{1,0:T(8,128)(2,1)} %param.12, bf16[256,1536]{1,0:T(8,128)(2,1)} %collective-permute-done.3, bf16[256,1536]{1,0:T(8,128)(2,1)} %param.8), kind=kOutput, calls=%fused_computation.8 | convolution fusion | flops 2419851264 | bytes 7864320 | tf_op jit(solution)/shard_map/dot_general | solution.py:89
  25.9 2.3 collective-permute-start.7
  30.4 1.6 collective-permute-start.5
  34.1 1.6 collective-permute-start.10
  37.3 12.1 %collective-permute-done.5 = bf16[128,1536]{1,0:T(8,128)(2,1)S(1)} collective-permute-done((bf16[128,1536]{1,0:T(8,128)(2,1)S(1)}, bf16[128,1536]{1,0:T(8,128)(2,1)S(1)}, u32[]{:S(2)}, u32[]{:S(2)}) %collective-permute-start.5) | collective-permute-done | bytes 393248 | tf_op jit(solution)/shard_map/ppermute | solution.py:27
  50.8 1.3 collective-permute-start.8
  52.1 5.8 %collective-permute-done.12 = bf16[128,1536]{1,0:T(8,128)(2,1)S(1)} collective-permute-done((bf16[128,1536]{1,0:T(8,128)(2,1)S(1)}, bf16[128,1536]{1,0:T(8,128)(2,1)S(1)}, u32[]{:S(2)}, u32[]{:S(2)}) %collective-permute-start.12) | collective-permute-done | bytes 393248 | tf_op jit(solution)/shard_map/ppermute | solution.py:27
  57.9 7.7 %collective-permute-done.10 = bf16[128,1536]{1,0:T(8,128)(2,1)S(1)} collective-permute-done((bf16[128,1536]{1,0:T(8,128)(2,1)S(1)}, bf16[128,1536]{1,0:T(8,128)(2,1)S(1)}, u32[]{:S(2)}, u32[]{:S(2)}) %collective-permute-start.10) | collective-permute-done | bytes 393248 | tf_op jit(solution)/shard_map/ppermute | solution.py:27
  65.5 1.7 convert_add_fusion.7
  70.5 17.4 %collective-permute-done.11 = bf16[128,1536]{1,0:T(8,128)(2,1)S(1)} collective-permute-done((bf16[128,1536]{1,0:T(8,128)(2,1)S(1)}, bf16[128,1536]{1,0:T(8,128)(2,1)S(1)}, u32[]{:S(2)}, u32[]{:S(2)}) %collective-permute-start.11) | collective-permute-done | bytes 393248 | tf_op jit(solution)/shard_map/ppermute | solution.py:120
  90.0 3.5 %collective-permute-done.15 = f32[2,512]{1,0:T(2,128)S(1)} collective-permute-done((f32[2,512]{1,0:T(2,128)S(1)}, f32[2,512]{1,0:T(2,128)S(1)}, u32[]{:S(2)}, u32[]{:S(2)}) %collective-permute-start.15) | collective-permute-done | bytes 4128 | tf_op jit(solution)/shard_map/ppermute | solution.py:27
  95.0 3.6 %collective-permute-start.19 = (bf16[512,384]{1,0:T(8,128)(2,1)S(1)}, bf16[512,384]{1,0:T(8,128)(2,1)S(1)}, u32[]{:S(2)}, u32[]{:S(2)}) collective-permute-start(bf16[512,384]{1,0:T(8,128)(2,1)S(1)} %pad_maximum_fusion.2), channel_id=1, source_target_pairs={{4,1},{1,4},{6,3},{3,6},{12,9},{9,12},{14,11},{11,14},{20,17},{17,... | collective-permute-start | bytes 1179656 | tf_op jit(solution)/shard_map/ppermute | solution.py:175
  99.3 3.4 %collective-permute-start.17 = (bf16[512,1152]{1,0:T(8,128)(2,1)S(1)}, bf16[512,1152]{1,0:T(8,128)(2,1)S(1)}, u32[]{:S(2)}, u32[]{:S(2)}) collective-permute-start(bf16[512,1152]{1,0:T(8,128)(2,1)S(1)} %pad_maximum_fusion), channel_id=1, source_target_pairs={{4,1},{1,4},{6,3},{3,6},{12,9},{9,12},{14,11},{11,14},{20,17},{17,... | collective-permute-start | bytes 3538952 | tf_op jit(solution)/shard_map/ppermute | solution.py:175
  102.7 3.4 %collective-permute-done.18 = bf16[512,384]{1,0:T(8,128)(2,1)S(1)} collective-permute-done((bf16[512,384]{1,0:T(8,128)(2,1)S(1)}, bf16[512,384]{1,0:T(8,128)(2,1)S(1)}, u32[]{:S(2)}, u32[]{:S(2)}) %collective-permute-start.18) | collective-permute-done | bytes 393248 | tf_op jit(solution)/shard_map/ppermute | solution.py:174
  106.0 4.1 %collective-permute-done.19 = bf16[512,384]{1,0:T(8,128)(2,1)S(1)} collective-permute-done((bf16[512,384]{1,0:T(8,128)(2,1)S(1)}, bf16[512,384]{1,0:T(8,128)(2,1)S(1)}, u32[]{:S(2)}, u32[]{:S(2)}) %collective-permute-start.19) | collective-permute-done | bytes 393248 | tf_op jit(solution)/shard_map/ppermute | solution.py:175
  110.4 1.4 fusion.62
  111.8 3.7 %collective-permute-start.20 = (bf16[1536,128]{1,0:T(8,128)(2,1)S(1)}, bf16[1536,128]{1,0:T(8,128)(2,1)S(1)}, u32[]{:S(2)}, u32[]{:S(2)}) collective-permute-start(bf16[1536,128]{1,0:T(8,128)(2,1)S(1)} %fusion.62), channel_id=1, source_target_pairs={{0,8},{24,16},{1,9},{25,17},{2,10},{26,18},{3,11},{27,19},{4,12},{... | collective-permute-start | bytes 1179656 | tf_op jit(solution)/shard_map/ppermute | solution.py:52
  115.5 2.2 fusion.34
  117.8 1.3 collective-permute-start.22
  119.1 1.3 collective-permute-start.25
  120.4 4.5 %collective-permute-done.20 = bf16[1536,128]{1,0:T(8,128)(2,1)S(1)} collective-permute-done((bf16[1536,128]{1,0:T(8,128)(2,1)S(1)}, bf16[1536,128]{1,0:T(8,128)(2,1)S(1)}, u32[]{:S(2)}, u32[]{:S(2)}) %collective-permute-start.20) | collective-permute-done | bytes 393248 | tf_op jit(solution)/shard_map/ppermute | solution.py:52
  125.7 6.9 %collective-permute-done.22 = bf16[1536,128]{1,0:T(8,128)(2,1)S(1)} collective-permute-done((bf16[1536,128]{1,0:T(8,128)(2,1)S(1)}, bf16[1536,128]{1,0:T(8,128)(2,1)S(1)}, u32[]{:S(2)}, u32[]{:S(2)}) %collective-permute-start.22) | collective-permute-done | bytes 393248 | tf_op jit(solution)/shard_map/ppermute | solution.py:52
  134.0 2.2 fusion.33
  136.4 5.7 %collective-permute-start.23 = (bf16[1536,128]{1,0:T(8,128)(2,1)S(1)}, bf16[1536,128]{1,0:T(8,128)(2,1)S(1)}, u32[]{:S(2)}, u32[]{:S(2)}) collective-permute-start(bf16[1536,128]{1,0:T(8,128)(2,1)S(1)} %fusion.88), channel_id=1, source_target_pairs={{0,8},{24,16},{8,0},{16,24},{1,9},{25,17},{9,1},{17,25},{2,10},{26... | collective-permute-start | bytes 1179656 | tf_op jit(solution)/shard_map/ppermute | solution.py:52
  142.9 2.2 fusion.35
  145.2 5.0 %collective-permute-start.27 = (bf16[1536,128]{1,0:T(8,128)(2,1)S(1)}, bf16[1536,128]{1,0:T(8,128)(2,1)S(1)}, u32[]{:S(2)}, u32[]{:S(2)}) collective-permute-start(bf16[1536,128]{1,0:T(8,128)(2,1)S(1)} %fusion.89), channel_id=1, source_target_pairs={{0,8},{24,16},{8,0},{16,24},{1,9},{25,17},{9,1},{17,25},{2,10},{26... | collective-permute-start | bytes 1179656 | tf_op jit(solution)/shard_map/ppermute | solution.py:52
  150.3 1.5 collective-permute-done.23
  152.8 3.9 %collective-permute-start.29 = (bf16[1536,128]{1,0:T(8,128)(2,1)S(1)}, bf16[1536,128]{1,0:T(8,128)(2,1)S(1)}, u32[]{:S(2)}, u32[]{:S(2)}) collective-permute-start(bf16[1536,128]{1,0:T(8,128)(2,1)S(1)} %fusion.90), channel_id=1, source_target_pairs={{0,8},{24,16},{8,0},{16,24},{1,9},{25,17},{9,1},{17,25},{2,10},{26... | collective-permute-start | bytes 1179656 | tf_op jit(solution)/shard_map/ppermute | solution.py:52
  156.7 3.5 %collective-permute-done.27 = bf16[1536,128]{1,0:T(8,128)(2,1)S(1)} collective-permute-done((bf16[1536,128]{1,0:T(8,128)(2,1)S(1)}, bf16[1536,128]{1,0:T(8,128)(2,1)S(1)}, u32[]{:S(2)}, u32[]{:S(2)}) %collective-permute-start.27) | collective-permute-done | bytes 393248 | tf_op jit(solution)/shard_map/ppermute | solution.py:52
  161.4 2.2 fusion.36
  164.6 4.2 %collective-permute-start.31 = (bf16[1536,128]{1,0:T(8,128)(2,1)S(1)}, bf16[1536,128]{1,0:T(8,128)(2,1)S(1)}, u32[]{:S(2)}, u32[]{:S(2)}) collective-permute-start(bf16[1536,128]{1,0:T(8,128)(2,1)S(1)} %fusion.91), channel_id=1, source_target_pairs={{0,8},{24,16},{8,0},{16,24},{1,9},{25,17},{9,1},{17,25},{2,10},{26... | collective-permute-start | bytes 1179656 | tf_op jit(solution)/shard_map/ppermute | solution.py:52
  169.8 6.4 %collective-permute-start.33 = (bf16[1536,128]{1,0:T(8,128)(2,1)S(1)}, bf16[1536,128]{1,0:T(8,128)(2,1)S(1)}, u32[]{:S(2)}, u32[]{:S(2)}) collective-permute-start(bf16[1536,128]{1,0:T(8,128)(2,1)S(1)} %fusion.92), channel_id=1, source_target_pairs={{0,8},{24,16},{8,0},{16,24},{1,9},{25,17},{9,1},{17,25},{2,10},{26... | collective-permute-start | bytes 1179656 | tf_op jit(solution)/shard_map/ppermute | solution.py:52
  176.2 3.3 %fusion.37 = bf16[1536,256]{1,0:T(8,128)(2,1)S(1)} fusion(bf16[1536,1536]{1,0:T(8,128)(2,1)S(1)} %bitcast.192, bf16[1,1536,1536]{2,1,0:T(8,128)(2,1)S(1)} %bitcast.208, bf16[1,1536,1536]{2,1,0:T(8,128)(2,1)} %param.13, bf16[1024,1536]{1,0:T(8,128)(2,1)S(1)} %constant_dynamic-update-slice_fusion, bf16[1024,256]{1,0:T(8,128)(2,1)S(1)} %get-tuple-element.225), kind=kOutput, calls=%fused_computation.60 | convolution fusion | flops 812384256 | bytes 6815744 | tf_op jit(solution)/shard_map/dot_general | solution.py:188
  181.5 3.5 %collective-permute-start.35 = (bf16[1536,128]{1,0:T(8,128)(2,1)S(1)}, bf16[1536,128]{1,0:T(8,128)(2,1)S(1)}, u32[]{:S(2)}, u32[]{:S(2)}) collective-permute-start(bf16[1536,128]{1,0:T(8,128)(2,1)S(1)} %fusion.93), channel_id=1, source_target_pairs={{0,8},{24,16},{8,0},{16,24},{1,9},{25,17},{9,1},{17,25},{2,10},{26... | collective-permute-start | bytes 1179656 | tf_op jit(solution)/shard_map/ppermute | solution.py:52
  187.2 7.6 %collective-permute-start.37 = (bf16[1536,128]{1,0:T(8,128)(2,1)S(1)}, bf16[1536,128]{1,0:T(8,128)(2,1)S(1)}, u32[]{:S(2)}, u32[]{:S(2)}) collective-permute-start(bf16[1536,128]{1,0:T(8,128)(2,1)S(1)} %fusion.94), channel_id=1, source_target_pairs={{0,8},{24,16},{8,0},{16,24},{1,9},{25,17},{9,1},{17,25},{2,10},{26... | collective-permute-start | bytes 1179656 | tf_op jit(solution)/shard_map/ppermute | solution.py:52
  195.9 7.4 %collective-permute-start.39 = (bf16[1536,128]{1,0:T(8,128)(2,1)S(1)}, bf16[1536,128]{1,0:T(8,128)(2,1)S(1)}, u32[]{:S(2)}, u32[]{:S(2)}) collective-permute-start(bf16[1536,128]{1,0:T(8,128)(2,1)S(1)} %fusion.95), channel_id=1, source_target_pairs={{0,8},{24,16},{8,0},{16,24},{1,9},{25,17},{9,1},{17,25},{2,10},{26... | collective-permute-start | bytes 1179656 | tf_op jit(solution)/shard_map/ppermute | solution.py:52
  203.2 2.4 fusion.63
  207.6 4.1 %collective-permute-start.41 = (bf16[1536,128]{1,0:T(8,128)(2,1)S(1)}, bf16[1536,128]{1,0:T(8,128)(2,1)S(1)}, u32[]{:S(2)}, u32[]{:S(2)}) collective-permute-start(bf16[1536,128]{1,0:T(8,128)(2,1)S(1)} %fusion.96), channel_id=1, source_target_pairs={{0,8},{24,16},{8,0},{16,24},{1,9},{25,17},{9,1},{17,25},{2,10},{26... | collective-permute-start | bytes 1179656 | tf_op jit(solution)/shard_map/ppermute | solution.py:52
  213.1 1.6 collective-permute-start.43
  214.6 6.2 %collective-permute-done.41 = bf16[1536,128]{1,0:T(8,128)(2,1)S(1)} collective-permute-done((bf16[1536,128]{1,0:T(8,128)(2,1)S(1)}, bf16[1536,128]{1,0:T(8,128)(2,1)S(1)}, u32[]{:S(2)}, u32[]{:S(2)}) %collective-permute-start.41) | collective-permute-done | bytes 393248 | tf_op jit(solution)/shard_map/ppermute | solution.py:52
  224.0 5.3 %collective-permute-done.43 = bf16[1536,128]{1,0:T(8,128)(2,1)S(1)} collective-permute-done((bf16[1536,128]{1,0:T(8,128)(2,1)S(1)}, bf16[1536,128]{1,0:T(8,128)(2,1)S(1)}, u32[]{:S(2)}, u32[]{:S(2)}) %collective-permute-start.43) | collective-permute-done | bytes 393248 | tf_op jit(solution)/shard_map/ppermute | solution.py:52
  230.7 6.0 %collective-permute-done.45 = bf16[1536,128]{1,0:T(8,128)(2,1)S(1)} collective-permute-done((bf16[1536,128]{1,0:T(8,128)(2,1)S(1)}, bf16[1536,128]{1,0:T(8,128)(2,1)S(1)}, u32[]{:S(2)}, u32[]{:S(2)}) %collective-permute-start.45) | collective-permute-done | bytes 393248 | tf_op jit(solution)/shard_map/ppermute | solution.py:52
  237.6 3.3 %collective-permute-done.46 = bf16[1536,128]{1,0:T(8,128)(2,1)S(1)} collective-permute-done((bf16[1536,128]{1,0:T(8,128)(2,1)S(1)}, bf16[1536,128]{1,0:T(8,128)(2,1)S(1)}, u32[]{:S(2)}, u32[]{:S(2)}) %collective-permute-start.46) | collective-permute-done | bytes 393248 | tf_op jit(solution)/shard_map/ppermute | solution.py:52
  241.3 3.4 %copy-done.1 = f32[1536,1536]{1,0:T(8,128)} copy-done((f32[1536,1536]{1,0:T(8,128)}, f32[1536,1536]{1,0:T(8,128)S(1)}, u32[]{:S(2)}) %copy-start.1) | copy-done | bytes 9437208
  244.8 2.2 copy-done.2
  (171 shorter events, 39.9 us)
Async XLA Ops:
  0.6 19.6 %collective-permute-start = (bf16[256,1536]{1,0:T(8,128)(2,1)}, bf16[256,1536]{1,0:T(8,128)(2,1)S(1)}, u32[]{:S(2)}, u32[]{:S(2)}) collective-permute-start(bf16[256,1536]{1,0:T(8,128)(2,1)} %param.8), channel_id=1, source_target_pairs={{0,4},{2,6},{4,0},{6,2},{1,5},{3,7},{5,1},{7,3},{8,12},{10,14},{12... | collective-permute-start | bytes 2359304 | tf_op jit(solution)/shard_map/ppermute | solution.py:27
  4.7 15.5 %collective-permute-start.1 = (bf16[256,1536]{1,0:T(8,128)(2,1)}, bf16[256,1536]{1,0:T(8,128)(2,1)}, u32[]{:S(2)}, u32[]{:S(2)}) collective-permute-start(bf16[256,1536]{1,0:T(8,128)(2,1)} %get-tuple-element.304), channel_id=1, source_target_pairs={{0,2},{2,0},{4,6},{6,4},{1,3},{3,1},{5,7},{7,5},{8,10},{10,8},{12,... | collective-permute-start | bytes 2359304 | tf_op jit(solution)/shard_map/ppermute | solution.py:27
  5.7 14.5 %collective-permute-start.2 = (bf16[256,1536]{1,0:T(8,128)(2,1)}, bf16[256,1536]{1,0:T(8,128)(2,1)S(1)}, u32[]{:S(2)}, u32[]{:S(2)}) collective-permute-start(bf16[256,1536]{1,0:T(8,128)(2,1)} %get-tuple-element.302), channel_id=1, source_target_pairs={{0,2},{2,0},{4,6},{6,4},{1,3},{3,1},{5,7},{7,5},{8,10},{10,8},{12,... | collective-permute-start | bytes 2359304 | tf_op jit(solution)/shard_map/ppermute | solution.py:27
  6.2 14.1 %collective-permute-start.3 = (bf16[256,1536]{1,0:T(8,128)(2,1)}, bf16[256,1536]{1,0:T(8,128)(2,1)}, u32[]{:S(2)}, u32[]{:S(2)}) collective-permute-start(bf16[256,1536]{1,0:T(8,128)(2,1)} %param.8), channel_id=1, source_target_pairs={{0,2},{2,0},{4,6},{6,4},{1,3},{3,1},{5,7},{7,5},{8,10},{10,8},{12,... | collective-permute-start | bytes 2359304 | tf_op jit(solution)/shard_map/ppermute | solution.py:27
  20.2 11.8 %collective-permute-start.9 = (bf16[256,1536]{1,0:T(8,128)(2,1)S(1)}, bf16[256,1536]{1,0:T(8,128)(2,1)S(1)}, u32[]{:S(2)}, u32[]{:S(2)}) collective-permute-start(bf16[256,1536]{1,0:T(8,128)(2,1)S(1)} %collective-permute-done), channel_id=1, source_target_pairs={{0,2},{2,0},{4,6},{6,4},{1,3},{3,1},{5,7},{7,5},{8,10},{10,8},{12,... | collective-permute-start | bytes 2359304 | tf_op jit(solution)/shard_map/ppermute | solution.py:27
  25.9 44.0 %collective-permute-start.7 = (bf16[512,1536]{1,0:T(8,128)(2,1)S(1)}, bf16[512,1536]{1,0:T(8,128)(2,1)S(1)}, u32[]{:S(2)}, u32[]{:S(2)}) collective-permute-start(bf16[512,1536]{1,0:T(8,128)(2,1)S(1)} %convolution_convert_fusion), channel_id=1, source_target_pairs={{4,5},{1,0},{6,7},{3,2},{12,13},{9,8},{14,15},{11,10},{20,21},{17,... | collective-permute-start | bytes 4718600 | tf_op jit(solution)/shard_map/ppermute | solution.py:113
  29.0 21.7 %collective-permute-start.4 = (bf16[128,1536]{1,0:T(8,128)(2,1)S(1)}, bf16[128,1536]{1,0:T(8,128)(2,1)S(1)}, u32[]{:S(2)}, u32[]{:S(2)}) collective-permute-start(bf16[128,1536]{1,0:T(8,128)(2,1)S(1)} %convolution_convert_fusion.4), channel_id=1, source_target_pairs={{0,4},{2,6},{4,0},{6,2},{1,5},{3,7},{5,1},{7,3},{8,12},{10,14},{12... | collective-permute-start | bytes 1179656 | tf_op jit(solution)/shard_map/ppermute | solution.py:27
  30.4 19.1 %collective-permute-start.5 = (bf16[128,1536]{1,0:T(8,128)(2,1)S(1)}, bf16[128,1536]{1,0:T(8,128)(2,1)S(1)}, u32[]{:S(2)}, u32[]{:S(2)}) collective-permute-start(bf16[128,1536]{1,0:T(8,128)(2,1)S(1)} %convolution_convert_fusion.3), channel_id=1, source_target_pairs={{0,4},{2,6},{4,0},{6,2},{1,5},{3,7},{5,1},{7,3},{8,12},{10,14},{12... | collective-permute-start | bytes 1179656 | tf_op jit(solution)/shard_map/ppermute | solution.py:27
  32.8 25.1 %collective-permute-start.12 = (bf16[128,1536]{1,0:T(8,128)(2,1)S(1)}, bf16[128,1536]{1,0:T(8,128)(2,1)S(1)}, u32[]{:S(2)}, u32[]{:S(2)}) collective-permute-start(bf16[128,1536]{1,0:T(8,128)(2,1)S(1)} %convolution_convert_fusion.1), channel_id=1, source_target_pairs={{0,4},{2,6},{4,0},{6,2},{1,5},{3,7},{5,1},{7,3},{8,12},{10,14},{12... | collective-permute-start | bytes 1179656 | tf_op jit(solution)/shard_map/ppermute | solution.py:27
  34.1 31.4 %collective-permute-start.10 = (bf16[128,1536]{1,0:T(8,128)(2,1)S(1)}, bf16[128,1536]{1,0:T(8,128)(2,1)S(1)}, u32[]{:S(2)}, u32[]{:S(2)}) collective-permute-start(bf16[128,1536]{1,0:T(8,128)(2,1)S(1)} %convolution_convert_fusion.2), channel_id=1, source_target_pairs={{0,4},{2,6},{4,0},{6,2},{1,5},{3,7},{5,1},{7,3},{8,12},{10,14},{12... | collective-permute-start | bytes 1179656 | tf_op jit(solution)/shard_map/ppermute | solution.py:27
  49.5 20.7 %collective-permute-start.6 = (bf16[128,1536]{1,0:T(8,128)(2,1)S(1)}, bf16[128,1536]{1,0:T(8,128)(2,1)S(1)}, u32[]{:S(2)}, u32[]{:S(2)}) collective-permute-start(bf16[128,1536]{1,0:T(8,128)(2,1)S(1)} %collective-permute-done.5), channel_id=1, source_target_pairs={{0,1},{5,4},{2,3},{7,6},{8,9},{13,12},{10,11},{15,14},{16,17},{21,... | collective-permute-start | bytes 1179656 | tf_op jit(solution)/shard_map/ppermute | solution.py:120
  50.8 19.1 %collective-permute-start.8 = (bf16[128,1536]{1,0:T(8,128)(2,1)S(1)}, bf16[128,1536]{1,0:T(8,128)(2,1)S(1)}, u32[]{:S(2)}, u32[]{:S(2)}) collective-permute-start(bf16[128,1536]{1,0:T(8,128)(2,1)S(1)} %collective-permute-done.4), channel_id=1, source_target_pairs={{0,1},{5,4},{2,3},{7,6},{8,9},{13,12},{10,11},{15,14},{16,17},{21,... | collective-permute-start | bytes 1179656 | tf_op jit(solution)/shard_map/ppermute | solution.py:120
  67.2 21.0 %collective-permute-start.13 = (bf16[128,1536]{1,0:T(8,128)(2,1)S(1)}, bf16[128,1536]{1,0:T(8,128)(2,1)S(1)}, u32[]{:S(2)}, u32[]{:S(2)}) collective-permute-start(bf16[128,1536]{1,0:T(8,128)(2,1)S(1)} %collective-permute-done.12), channel_id=1, source_target_pairs={{0,1},{5,4},{2,3},{7,6},{8,9},{13,12},{10,11},{15,14},{16,17},{21,... | collective-permute-start | bytes 1179656 | tf_op jit(solution)/shard_map/ppermute | solution.py:120
  68.5 19.4 %collective-permute-start.11 = (bf16[128,1536]{1,0:T(8,128)(2,1)S(1)}, bf16[128,1536]{1,0:T(8,128)(2,1)S(1)}, u32[]{:S(2)}, u32[]{:S(2)}) collective-permute-start(bf16[128,1536]{1,0:T(8,128)(2,1)S(1)} %collective-permute-done.10), channel_id=1, source_target_pairs={{0,1},{5,4},{2,3},{7,6},{8,9},{13,12},{10,11},{15,14},{16,17},{21,... | collective-permute-start | bytes 1179656 | tf_op jit(solution)/shard_map/ppermute | solution.py:120
  88.6 1.2 collective-permute-start.14
  89.8 3.7 %collective-permute-start.15 = (f32[2,512]{1,0:T(2,128)S(1)}, f32[2,512]{1,0:T(2,128)S(1)}, u32[]{:S(2)}, u32[]{:S(2)}) collective-permute-start(f32[2,512]{1,0:T(2,128)S(1)} %maximum_add_fusion), channel_id=1, source_target_pairs={{0,1},{1,0},{2,3},{3,2},{4,5},{5,4},{6,7},{7,6},{8,9},{9,8},{10,11... | collective-permute-start | bytes 12296 | tf_op jit(solution)/shard_map/ppermute | solution.py:27
  93.7 16.6 %slice-start.5 = ((s8[4718592]{0:T(1024)(128)(4,1)}), s8[4194304]{0:T(1024)(128)(4,1)S(1)}, s32[]{:S(2)}) async-start(s8[4718592]{0:T(1024)(128)(4,1)} %bitcast.207), calls=%async_computation.5 | async-start | bytes 8388608
  93.9 12.1 %collective-permute-start.18 = (bf16[512,384]{1,0:T(8,128)(2,1)S(1)}, bf16[512,384]{1,0:T(8,128)(2,1)S(1)}, u32[]{:S(2)}, u32[]{:S(2)}) collective-permute-start(bf16[512,384]{1,0:T(8,128)(2,1)S(1)} %pad_maximum_fusion.2), channel_id=1, source_target_pairs={{0,1},{5,4},{4,0},{1,5},{2,3},{7,6},{6,2},{3,7},{8,9},{13,12},{12,... | collective-permute-start | bytes 1179656 | tf_op jit(solution)/shard_map/ppermute | solution.py:174
  95.0 15.1 %collective-permute-start.19 = (bf16[512,384]{1,0:T(8,128)(2,1)S(1)}, bf16[512,384]{1,0:T(8,128)(2,1)S(1)}, u32[]{:S(2)}, u32[]{:S(2)}) collective-permute-start(bf16[512,384]{1,0:T(8,128)(2,1)S(1)} %pad_maximum_fusion.2), channel_id=1, source_target_pairs={{4,1},{1,4},{6,3},{3,6},{12,9},{9,12},{14,11},{11,14},{20,17},{17,... | collective-permute-start | bytes 1179656 | tf_op jit(solution)/shard_map/ppermute | solution.py:175
  99.2 34.1 %collective-permute-start.16 = (bf16[512,1152]{1,0:T(8,128)(2,1)S(1)}, bf16[512,1152]{1,0:T(8,128)(2,1)S(1)}, u32[]{:S(2)}, u32[]{:S(2)}) collective-permute-start(bf16[512,1152]{1,0:T(8,128)(2,1)S(1)} %pad_maximum_fusion), channel_id=1, source_target_pairs={{0,1},{5,4},{4,0},{1,5},{2,3},{7,6},{6,2},{3,7},{8,9},{13,12},{12,... | collective-permute-start | bytes 3538952 | tf_op jit(solution)/shard_map/ppermute | solution.py:174
  99.3 34.1 %collective-permute-start.17 = (bf16[512,1152]{1,0:T(8,128)(2,1)S(1)}, bf16[512,1152]{1,0:T(8,128)(2,1)S(1)}, u32[]{:S(2)}, u32[]{:S(2)}) collective-permute-start(bf16[512,1152]{1,0:T(8,128)(2,1)S(1)} %pad_maximum_fusion), channel_id=1, source_target_pairs={{4,1},{1,4},{6,3},{3,6},{12,9},{9,12},{14,11},{11,14},{20,17},{17,... | collective-permute-start | bytes 3538952 | tf_op jit(solution)/shard_map/ppermute | solution.py:175
  111.8 13.0 %collective-permute-start.20 = (bf16[1536,128]{1,0:T(8,128)(2,1)S(1)}, bf16[1536,128]{1,0:T(8,128)(2,1)S(1)}, u32[]{:S(2)}, u32[]{:S(2)}) collective-permute-start(bf16[1536,128]{1,0:T(8,128)(2,1)S(1)} %fusion.62), channel_id=1, source_target_pairs={{0,8},{24,16},{1,9},{25,17},{2,10},{26,18},{3,11},{27,19},{4,12},{... | collective-permute-start | bytes 1179656 | tf_op jit(solution)/shard_map/ppermute | solution.py:52
  117.8 14.8 %collective-permute-start.22 = (bf16[1536,128]{1,0:T(8,128)(2,1)S(1)}, bf16[1536,128]{1,0:T(8,128)(2,1)S(1)}, u32[]{:S(2)}, u32[]{:S(2)}) collective-permute-start(bf16[1536,128]{1,0:T(8,128)(2,1)S(1)} %get-tuple-element.313), channel_id=1, source_target_pairs={{0,8},{24,16},{1,9},{25,17},{2,10},{26,18},{3,11},{27,19},{4,12},{... | collective-permute-start | bytes 1179656 | tf_op jit(solution)/shard_map/ppermute | solution.py:52
  119.1 23.0 %collective-permute-start.25 = (bf16[1536,128]{1,0:T(8,128)(2,1)S(1)}, bf16[1536,128]{1,0:T(8,128)(2,1)S(1)}, u32[]{:S(2)}, u32[]{:S(2)}) collective-permute-start(bf16[1536,128]{1,0:T(8,128)(2,1)S(1)} %get-tuple-element.312), channel_id=1, source_target_pairs={{0,8},{24,16},{1,9},{25,17},{2,10},{26,18},{3,11},{27,19},{4,12},{... | collective-permute-start | bytes 1179656 | tf_op jit(solution)/shard_map/ppermute | solution.py:52
  125.0 8.4 %collective-permute-start.21 = (bf16[1536,128]{1,0:T(8,128)(2,1)S(1)}, bf16[1536,128]{1,0:T(8,128)(2,1)S(1)}, u32[]{:S(2)}, u32[]{:S(2)}) collective-permute-start(bf16[1536,128]{1,0:T(8,128)(2,1)S(1)} %add_convert_fusion.35), channel_id=1, source_target_pairs={{8,16},{16,8},{9,17},{17,9},{10,18},{18,10},{11,19},{19,11},{12,20... | collective-permute-start | bytes 1179656 | tf_op jit(solution)/shard_map/ppermute | solution.py:60
  132.7 10.2 %collective-permute-start.24 = (bf16[1536,128]{1,0:T(8,128)(2,1)S(1)}, bf16[1536,128]{1,0:T(8,128)(2,1)S(1)}, u32[]{:S(2)}, u32[]{:S(2)}) collective-permute-start(bf16[1536,128]{1,0:T(8,128)(2,1)S(1)} %add_convert_fusion.34), channel_id=1, source_target_pairs={{8,16},{16,8},{9,17},{17,9},{10,18},{18,10},{11,19},{19,11},{12,20... | collective-permute-start | bytes 1179656 | tf_op jit(solution)/shard_map/ppermute | solution.py:60
  136.4 15.4 %collective-permute-start.23 = (bf16[1536,128]{1,0:T(8,128)(2,1)S(1)}, bf16[1536,128]{1,0:T(8,128)(2,1)S(1)}, u32[]{:S(2)}, u32[]{:S(2)}) collective-permute-start(bf16[1536,128]{1,0:T(8,128)(2,1)S(1)} %fusion.88), channel_id=1, source_target_pairs={{0,8},{24,16},{8,0},{16,24},{1,9},{25,17},{9,1},{17,25},{2,10},{26... | collective-permute-start | bytes 1179656 | tf_op jit(solution)/shard_map/ppermute | solution.py:52
  142.2 10.4 %collective-permute-start.26 = (bf16[1536,128]{1,0:T(8,128)(2,1)S(1)}, bf16[1536,128]{1,0:T(8,128)(2,1)S(1)}, u32[]{:S(2)}, u32[]{:S(2)}) collective-permute-start(bf16[1536,128]{1,0:T(8,128)(2,1)S(1)} %add_convert_fusion.32), channel_id=1, source_target_pairs={{8,16},{16,8},{9,17},{17,9},{10,18},{18,10},{11,19},{19,11},{12,20... | collective-permute-start | bytes 1179656 | tf_op jit(solution)/shard_map/ppermute | solution.py:60
  145.2 15.0 %collective-permute-start.27 = (bf16[1536,128]{1,0:T(8,128)(2,1)S(1)}, bf16[1536,128]{1,0:T(8,128)(2,1)S(1)}, u32[]{:S(2)}, u32[]{:S(2)}) collective-permute-start(bf16[1536,128]{1,0:T(8,128)(2,1)S(1)} %fusion.89), channel_id=1, source_target_pairs={{0,8},{24,16},{8,0},{16,24},{1,9},{25,17},{9,1},{17,25},{2,10},{26... | collective-permute-start | bytes 1179656 | tf_op jit(solution)/shard_map/ppermute | solution.py:52
  151.9 12.5 %collective-permute-start.28 = (bf16[1536,128]{1,0:T(8,128)(2,1)S(1)}, bf16[1536,128]{1,0:T(8,128)(2,1)S(1)}, u32[]{:S(2)}, u32[]{:S(2)}) collective-permute-start(bf16[1536,128]{1,0:T(8,128)(2,1)S(1)} %add_convert_fusion.30), channel_id=1, source_target_pairs={{8,16},{16,8},{9,17},{17,9},{10,18},{18,10},{11,19},{19,11},{12,20... | collective-permute-start | bytes 1179656 | tf_op jit(solution)/shard_map/ppermute | solution.py:60
  152.8 16.1 %collective-permute-start.29 = (bf16[1536,128]{1,0:T(8,128)(2,1)S(1)}, bf16[1536,128]{1,0:T(8,128)(2,1)S(1)}, u32[]{:S(2)}, u32[]{:S(2)}) collective-permute-start(bf16[1536,128]{1,0:T(8,128)(2,1)S(1)} %fusion.90), channel_id=1, source_target_pairs={{0,8},{24,16},{8,0},{16,24},{1,9},{25,17},{9,1},{17,25},{2,10},{26... | collective-permute-start | bytes 1179656 | tf_op jit(solution)/shard_map/ppermute | solution.py:52
  160.3 9.3 %collective-permute-start.30 = (bf16[1536,128]{1,0:T(8,128)(2,1)S(1)}, bf16[1536,128]{1,0:T(8,128)(2,1)S(1)}, u32[]{:S(2)}, u32[]{:S(2)}) collective-permute-start(bf16[1536,128]{1,0:T(8,128)(2,1)S(1)} %add_convert_fusion.28), channel_id=1, source_target_pairs={{8,16},{16,8},{9,17},{17,9},{10,18},{18,10},{11,19},{19,11},{12,20... | collective-permute-start | bytes 1179656 | tf_op jit(solution)/shard_map/ppermute | solution.py:60
  164.6 15.9 %collective-permute-start.31 = (bf16[1536,128]{1,0:T(8,128)(2,1)S(1)}, bf16[1536,128]{1,0:T(8,128)(2,1)S(1)}, u32[]{:S(2)}, u32[]{:S(2)}) collective-permute-start(bf16[1536,128]{1,0:T(8,128)(2,1)S(1)} %fusion.91), channel_id=1, source_target_pairs={{0,8},{24,16},{8,0},{16,24},{1,9},{25,17},{9,1},{17,25},{2,10},{26... | collective-permute-start | bytes 1179656 | tf_op jit(solution)/shard_map/ppermute | solution.py:52
  169.0 12.4 %collective-permute-start.32 = (bf16[1536,128]{1,0:T(8,128)(2,1)S(1)}, bf16[1536,128]{1,0:T(8,128)(2,1)S(1)}, u32[]{:S(2)}, u32[]{:S(2)}) collective-permute-start(bf16[1536,128]{1,0:T(8,128)(2,1)S(1)} %add_convert_fusion.26), channel_id=1, source_target_pairs={{8,16},{16,8},{9,17},{17,9},{10,18},{18,10},{11,19},{19,11},{12,20... | collective-permute-start | bytes 1179656 | tf_op jit(solution)/shard_map/ppermute | solution.py:60
  169.8 15.9 %collective-permute-start.33 = (bf16[1536,128]{1,0:T(8,128)(2,1)S(1)}, bf16[1536,128]{1,0:T(8,128)(2,1)S(1)}, u32[]{:S(2)}, u32[]{:S(2)}) collective-permute-start(bf16[1536,128]{1,0:T(8,128)(2,1)S(1)} %fusion.92), channel_id=1, source_target_pairs={{0,8},{24,16},{8,0},{16,24},{1,9},{25,17},{9,1},{17,25},{2,10},{26... | collective-permute-start | bytes 1179656 | tf_op jit(solution)/shard_map/ppermute | solution.py:52
  180.6 6.4 %collective-permute-start.34 = (bf16[1536,128]{1,0:T(8,128)(2,1)S(1)}, bf16[1536,128]{1,0:T(8,128)(2,1)S(1)}, u32[]{:S(2)}, u32[]{:S(2)}) collective-permute-start(bf16[1536,128]{1,0:T(8,128)(2,1)S(1)} %add_convert_fusion.24), channel_id=1, source_target_pairs={{8,16},{16,8},{9,17},{17,9},{10,18},{18,10},{11,19},{19,11},{12,20... | collective-permute-start | bytes 1179656 | tf_op jit(solution)/shard_map/ppermute | solution.py:60
  181.5 13.4 %collective-permute-start.35 = (bf16[1536,128]{1,0:T(8,128)(2,1)S(1)}, bf16[1536,128]{1,0:T(8,128)(2,1)S(1)}, u32[]{:S(2)}, u32[]{:S(2)}) collective-permute-start(bf16[1536,128]{1,0:T(8,128)(2,1)S(1)} %fusion.93), channel_id=1, source_target_pairs={{0,8},{24,16},{8,0},{16,24},{1,9},{25,17},{9,1},{17,25},{2,10},{26... | collective-permute-start | bytes 1179656 | tf_op jit(solution)/shard_map/ppermute | solution.py:52
  185.9 9.8 %collective-permute-start.36 = (bf16[1536,128]{1,0:T(8,128)(2,1)S(1)}, bf16[1536,128]{1,0:T(8,128)(2,1)S(1)}, u32[]{:S(2)}, u32[]{:S(2)}) collective-permute-start(bf16[1536,128]{1,0:T(8,128)(2,1)S(1)} %add_convert_fusion.22), channel_id=1, source_target_pairs={{8,16},{16,8},{9,17},{17,9},{10,18},{18,10},{11,19},{19,11},{12,20... | collective-permute-start | bytes 1179656 | tf_op jit(solution)/shard_map/ppermute | solution.py:60
  187.2 19.4 %collective-permute-start.37 = (bf16[1536,128]{1,0:T(8,128)(2,1)S(1)}, bf16[1536,128]{1,0:T(8,128)(2,1)S(1)}, u32[]{:S(2)}, u32[]{:S(2)}) collective-permute-start(bf16[1536,128]{1,0:T(8,128)(2,1)S(1)} %fusion.94), channel_id=1, source_target_pairs={{0,8},{24,16},{8,0},{16,24},{1,9},{25,17},{9,1},{17,25},{2,10},{26... | collective-permute-start | bytes 1179656 | tf_op jit(solution)/shard_map/ppermute | solution.py:52
  195.0 12.5 %collective-permute-start.38 = (bf16[1536,128]{1,0:T(8,128)(2,1)S(1)}, bf16[1536,128]{1,0:T(8,128)(2,1)S(1)}, u32[]{:S(2)}, u32[]{:S(2)}) collective-permute-start(bf16[1536,128]{1,0:T(8,128)(2,1)S(1)} %add_convert_fusion.20), channel_id=1, source_target_pairs={{8,16},{16,8},{9,17},{17,9},{10,18},{18,10},{11,19},{19,11},{12,20... | collective-permute-start | bytes 1179656 | tf_op jit(solution)/shard_map/ppermute | solution.py:60
  195.9 15.8 %collective-permute-start.39 = (bf16[1536,128]{1,0:T(8,128)(2,1)S(1)}, bf16[1536,128]{1,0:T(8,128)(2,1)S(1)}, u32[]{:S(2)}, u32[]{:S(2)}) collective-permute-start(bf16[1536,128]{1,0:T(8,128)(2,1)S(1)} %fusion.95), channel_id=1, source_target_pairs={{0,8},{24,16},{8,0},{16,24},{1,9},{25,17},{9,1},{17,25},{2,10},{26... | collective-permute-start | bytes 1179656 | tf_op jit(solution)/shard_map/ppermute | solution.py:52
  206.7 6.2 %collective-permute-start.40 = (bf16[1536,128]{1,0:T(8,128)(2,1)S(1)}, bf16[1536,128]{1,0:T(8,128)(2,1)S(1)}, u32[]{:S(2)}, u32[]{:S(2)}) collective-permute-start(bf16[1536,128]{1,0:T(8,128)(2,1)S(1)} %add_convert_fusion.18), channel_id=1, source_target_pairs={{8,16},{16,8},{9,17},{17,9},{10,18},{18,10},{11,19},{19,11},{12,20... | collective-permute-start | bytes 1179656 | tf_op jit(solution)/shard_map/ppermute | solution.py:60
  207.6 13.2 %collective-permute-start.41 = (bf16[1536,128]{1,0:T(8,128)(2,1)S(1)}, bf16[1536,128]{1,0:T(8,128)(2,1)S(1)}, u32[]{:S(2)}, u32[]{:S(2)}) collective-permute-start(bf16[1536,128]{1,0:T(8,128)(2,1)S(1)} %fusion.96), channel_id=1, source_target_pairs={{0,8},{24,16},{8,0},{16,24},{1,9},{25,17},{9,1},{17,25},{2,10},{26... | collective-permute-start | bytes 1179656 | tf_op jit(solution)/shard_map/ppermute | solution.py:52
  211.8 9.9 %collective-permute-start.42 = (bf16[1536,128]{1,0:T(8,128)(2,1)S(1)}, bf16[1536,128]{1,0:T(8,128)(2,1)S(1)}, u32[]{:S(2)}, u32[]{:S(2)}) collective-permute-start(bf16[1536,128]{1,0:T(8,128)(2,1)S(1)} %add_convert_fusion.16), channel_id=1, source_target_pairs={{8,16},{16,8},{9,17},{17,9},{10,18},{18,10},{11,19},{19,11},{12,20... | collective-permute-start | bytes 1179656 | tf_op jit(solution)/shard_map/ppermute | solution.py:60
  213.1 16.2 %collective-permute-start.43 = (bf16[1536,128]{1,0:T(8,128)(2,1)S(1)}, bf16[1536,128]{1,0:T(8,128)(2,1)S(1)}, u32[]{:S(2)}, u32[]{:S(2)}) collective-permute-start(bf16[1536,128]{1,0:T(8,128)(2,1)S(1)} %add_convert_fusion.15), channel_id=1, source_target_pairs={{8,0},{16,24},{9,1},{17,25},{10,2},{18,26},{11,3},{19,27},{12,4},{... | collective-permute-start | bytes 1179656 | tf_op jit(solution)/shard_map/ppermute | solution.py:52
  220.9 8.3 %collective-permute-start.44 = (bf16[1536,128]{1,0:T(8,128)(2,1)S(1)}, bf16[1536,128]{1,0:T(8,128)(2,1)S(1)}, u32[]{:S(2)}, u32[]{:S(2)}) collective-permute-start(bf16[1536,128]{1,0:T(8,128)(2,1)S(1)} %add_convert_fusion.14), channel_id=1, source_target_pairs={{8,16},{16,8},{9,17},{17,9},{10,18},{18,10},{11,19},{19,11},{12,20... | collective-permute-start | bytes 1179656 | tf_op jit(solution)/shard_map/ppermute | solution.py:60
  221.8 14.9 %collective-permute-start.45 = (bf16[1536,128]{1,0:T(8,128)(2,1)S(1)}, bf16[1536,128]{1,0:T(8,128)(2,1)S(1)}, u32[]{:S(2)}, u32[]{:S(2)}) collective-permute-start(bf16[1536,128]{1,0:T(8,128)(2,1)S(1)} %add_convert_fusion.13), channel_id=1, source_target_pairs={{8,0},{16,24},{9,1},{17,25},{10,2},{18,26},{11,3},{19,27},{12,4},{... | collective-permute-start | bytes 1179656 | tf_op jit(solution)/shard_map/ppermute | solution.py:52
  229.4 11.5 %collective-permute-start.46 = (bf16[1536,128]{1,0:T(8,128)(2,1)S(1)}, bf16[1536,128]{1,0:T(8,128)(2,1)S(1)}, u32[]{:S(2)}, u32[]{:S(2)}) collective-permute-start(bf16[1536,128]{1,0:T(8,128)(2,1)S(1)} %add_convert_fusion.12), channel_id=1, source_target_pairs={{8,0},{16,24},{9,1},{17,25},{10,2},{18,26},{11,3},{19,27},{12,4},{... | collective-permute-start | bytes 1179656 | tf_op jit(solution)/shard_map/ppermute | solution.py:52
  (11 other events, 74.4 us)

commit v10 on v9

--- a/solution.py
+++ b/solution.py
@@ -109,14 +109,16 @@
     held = together(swap(context, "fsdp", group), *moved[0], *moved[1])
     residual_parts, cotangent_parts = held[1 : 1 + group], held[1 + group :]
     far_blocks = [held[0]] + [swap(held[0], "fsdp", r) for r in range(1, group)]
-    near_out = project(jnp.concatenate(near_blocks, axis=0))
+    far_outs = []
+    for k in range(group * pieces):
+        r, p = k // pieces, k % pieces
+        blocks = [far_blocks[r][p * rows : (p + 1) * rows]]
+        if k == group * pieces - 1:
+            blocks += near_blocks
+        out = project(jnp.concatenate(blocks, axis=0))
+        far_outs.append(swap(out[:rows], "fsdp", group))
+    near_out = out[rows:]
     near_came = lax.ppermute(near_out, ("fsdp", "tp"), inward_pairs)
-    far_blocks[0], near_out = together(far_blocks[0], near_out)
-    far_outs = [
-        swap(project(far_blocks[r][p * rows : (p + 1) * rows]), "fsdp", group)
-        for r in range(group)
-        for p in range(pieces)
-    ]
     passed = [lax.ppermute(out, ("fsdp", "tp"), outward_pairs) for out in far_outs]
 
     gain_part = lax.dynamic_slice_in_dim(gain, t * (width // 2) + low * cols, cols).astype(f32)
@@ -125,16 +127,16 @@
     for k in range(group * pieces):
         r, p = k // pieces, k % pieces
         span, long_span = slice(p * rows, (p + 1) * rows), slice(k * rows, (k + 1) * rows)
-        keep = jnp.where(near, near_out[long_span], far_outs[k])
+        far_out, came = far_outs[k], passed[k]
+        if sums:
+            far_out, sums[-1] = together(far_out, sums[-1])
+        keep = jnp.where(near, near_out[long_span], far_out)
         base, w = lax.optimization_barrier(
             (
                 residual_parts[r][span].astype(f32) + keep.astype(f32),
                 gain_part[None, :] * cotangent_parts[r][span].astype(f32),
             )
         )
-        came = passed[k]
-        if sums:
-            came, sums[-1] = together(came, sums[-1])
         h = base + jnp.where(near, near_came[long_span], came).astype(f32)
         hidden.append(h)
         weighted.append(w)
@@ -155,7 +157,7 @@
     context_all = jnp.concatenate(near_blocks + far_blocks, axis=0)
     narrow = 128
     units = cols // narrow
-    widths = [3, units - 3]
+    widths = [1, 3, units - 4]
     islands = lax.axis_size("island")
     line = IslandLine(units)
     parts, locals_, rings, crosses = [], [], [], []
@@ -170,6 +172,10 @@
             ],
             axis=0,
         ).astype(bf16)
+        if c == 1:
+            d_local, rings[0] = together(d_local, rings[0])
+        elif c == 2:
+            d_local, crosses[0] = together(d_local, crosses[0])
         locals_.append(d_local)
         rings.append(lax.ppermute(d_local, ("fsdp", "tp"), ring_pairs))
         crosses.append(lax.ppermute(d_local, ("fsdp", "tp"), cross_pairs))
@@ -202,11 +208,12 @@
 
     for c in range(len(widths)):
         move(c)
-    early = widths[0]
-    found = gathered(0)
-    add_pseudo(found, 0, 1)
-    add_pseudo(found[:, narrow:], 1, early)
-    last = gathered(1)
+    add_pseudo(gathered(0), 0, 1)
+    found = gathered(1)
+    early = sum(widths[:2])
+    add_pseudo(found, 1, 2)
+    add_pseudo(found[:, narrow:], 2, early)
+    last = gathered(2)
     todo = [(lo, min(lo + 2, units)) for lo in range(early, units, 2)]
     if islands == 4:
         for s in range(2):

time: 248 us -> 245 us (0.988)
  waiting for transfers between devices: 105 us -> 88.6 us
  starting transfers between devices: 89.1 us -> 101 us
    ppermute x15, waiting for transfers between devices: 37.9 us -> 26.7 us  [send_outer(): self.edge[s] = lax.ppermute(payload, 'island', pairs)]
    ppermute x15, starting transfers between devices: 58.3 us -> 67.3 us  [send_outer(): self.edge[s] = lax.ppermute(payload, 'island', pairs)]
    ppermute x4, waiting for transfers between devices: 17.4 us -> 14.2 us  [body(): lax.ppermute(out, ('fsdp', 'tp'), outward_pairs)]
    ppermute x2 -> x3, starting transfers between devices: 6.99 us -> 10.1 us  [move(): crosses.append(lax.ppermute(d_local, ('fsdp', 'tp'), cross_pairs))]
    dot_general x5 -> x4, matrix products: 8.7 us -> 9.4 us  [project(): jnp.dot(block, weight, preferred_element_type=f32).astype(bf16)]
    unnamed x27 -> x25, local copies, waits for them, and re-layouts: 8.53 us -> 8.12 us
    unnamed x26 -> x25, other arithmetic: 5.11 us -> 5.13 us
  transfers between devices with their start and end apart: 47 -> 49, of which waited for: 19 -> 19; matrix products, arithmetic and copies ran while one was open for 18% -> 18% of each run, Pallas kernels for 0% -> 0%
where the time goes in v10:
time: 245 us; the launch traced here: 244 us
  starting transfers between devices  101 us (41%)
  waiting for transfers between devices  88.6 us (36%)
  matrix products  25.4 us (10%)
  other arithmetic  15.3 us (6%)
  local copies, waits for them, and re-layouts  11.8 us (5%)
    ppermute x15, starting transfers between devices, send_outer(): self.edge[s] = lax.ppermute(payload, 'island', pairs)  67.3 us
    ppermute x11, waiting for transfers between devices, swap(): return lax.ppermute(value, axis, [(i, i ^ bit) for i in range(count)])  41.8 us
    ppermute x15, waiting for transfers between devices, send_outer(): self.edge[s] = lax.ppermute(payload, 'island', pairs)  26.7 us
    dot_general x7, matrix products, add_pseudo(): lax.dot_general(context_all, piece, (((0,), (0,)), ((), ())), preferred_e...  16 us
    ppermute x4, waiting for transfers between devices, body(): lax.ppermute(out, ('fsdp', 'tp'), outward_pairs)  14.2 us
    ppermute x3, starting transfers between devices, move(): crosses.append(lax.ppermute(d_local, ('fsdp', 'tp'), cross_pairs))  10.1 us
    dot_general x4, matrix products, project(): jnp.dot(block, weight, preferred_element_type=f32).astype(bf16)  9.4 us
    ppermute x12, starting transfers between devices, step(): self.mid[s] = lax.ppermute(self.sums[s], 'island', [(1, 2), (2, 1)])  8.45 us
  transfers between devices with their start and end apart: 49, of which 19 were waited for; matrix products, arithmetic and copies ran while one was open for 18% of the time, Pallas kernels for 0%

profile of v10, /device:TPU:2, one launch (start us, length us, event | category | flops | bytes accessed | tf_op | source)
XLA Modules:
  0.0 243.5 jit_solution(11464624067182282977)
XLA Ops:
  0.6 1.6 collective-permute-start
  2.2 2.5 %constant_dynamic-slice_fusion.2 = (bf16[256,1536]{1,0:T(8,128)(2,1)}, bf16[256,1536]{1,0:T(8,128)(2,1)S(1)}) fusion(bf16[256,3072]{1,0:T(8,128)(2,1)} %param.9, s32[]{:T(128)S(6)} %select_n.187, s32[]{:T(128)S(6)} %select_n.186), kind=kLoop, calls=%fused_computation.286 | loop fusion | bytes 3145736 | tf_op jit(solution)/shard_map/dynamic_slice | solution.py:105
  7.4 12.8 %collective-permute-done = bf16[256,1536]{1,0:T(8,128)(2,1)S(1)} collective-permute-done((bf16[256,1536]{1,0:T(8,128)(2,1)}, bf16[256,1536]{1,0:T(8,128)(2,1)S(1)}, u32[]{:S(2)}, u32[]{:S(2)}) %collective-permute-start) | collective-permute-done | bytes 786464 | tf_op jit(solution)/shard_map/ppermute | solution.py:27
  21.0 3.3 %convolution_convert_fusion.2 = bf16[128,1536]{1,0:T(8,128)(2,1)S(1)} fusion(bf16[1536,1536]{1,0:T(8,128)(2,1)} %param.12, bf16[256,1536]{1,0:T(8,128)(2,1)S(1)} %collective-permute-done), kind=kOutput, calls=%fused_computation.8 | convolution fusion | flops 604176384 | bytes 5505024 | tf_op jit(solution)/shard_map/dot_general | solution.py:89
  24.3 1.6 collective-permute-start.6
  27.3 4.6 %convolution_convert_fusion = bf16[640,1536]{1,0:T(8,128)(2,1)S(1)} fusion(bf16[1536,1536]{1,0:T(8,128)(2,1)S(1)} %copy-done, bf16[256,1536]{1,0:T(8,128)(2,1)} %collective-permute-done.4, bf16[256,1536]{1,0:T(8,128)(2,1)} %param.8, bf16[128,1536]{1,0:T(8,128)(2,1)S(1)} %slice.468), kind=kOutput, calls=%fused_computation | convolution fusion | flops 3026780160 | bytes 8650752 | tf_op jit(solution)/shard_map/dot_general | solution.py:89
  32.0 2.4 collective-permute-start.7
  36.0 8.3 %collective-permute-done.5 = bf16[128,1536]{1,0:T(8,128)(2,1)S(1)} collective-permute-done((bf16[128,1536]{1,0:T(8,128)(2,1)S(1)}, bf16[128,1536]{1,0:T(8,128)(2,1)S(1)}, u32[]{:S(2)}, u32[]{:S(2)}) %collective-permute-start.5) | collective-permute-done | bytes 393248 | tf_op jit(solution)/shard_map/ppermute | solution.py:27
  46.9 2.8 %collective-permute-start.11 = (bf16[128,1536]{1,0:T(8,128)(2,1)S(1)}, bf16[128,1536]{1,0:T(8,128)(2,1)S(1)}, u32[]{:S(2)}, u32[]{:S(2)}) collective-permute-start(bf16[128,1536]{1,0:T(8,128)(2,1)S(1)} %slice.475), channel_id=1, source_target_pairs={{0,4},{2,6},{4,0},{6,2},{1,5},{3,7},{5,1},{7,3},{8,12},{10,14},{12... | collective-permute-start | bytes 1179656 | tf_op jit(solution)/shard_map/ppermute | solution.py:27
  50.7 16.1 %collective-permute-done.9 = bf16[128,1536]{1,0:T(8,128)(2,1)S(1)} collective-permute-done((bf16[128,1536]{1,0:T(8,128)(2,1)S(1)}, bf16[128,1536]{1,0:T(8,128)(2,1)S(1)}, u32[]{:S(2)}, u32[]{:S(2)}) %collective-permute-start.9) | collective-permute-done | bytes 393248 | tf_op jit(solution)/shard_map/ppermute | solution.py:27
  71.3 9.4 %collective-permute-done.12 = bf16[128,1536]{1,0:T(8,128)(2,1)S(1)} collective-permute-done((bf16[128,1536]{1,0:T(8,128)(2,1)S(1)}, bf16[128,1536]{1,0:T(8,128)(2,1)S(1)}, u32[]{:S(2)}, u32[]{:S(2)}) %collective-permute-start.12) | collective-permute-done | bytes 393248 | tf_op jit(solution)/shard_map/ppermute | solution.py:122
  82.2 4.8 %collective-permute-done.13 = bf16[128,1536]{1,0:T(8,128)(2,1)S(1)} collective-permute-done((bf16[128,1536]{1,0:T(8,128)(2,1)S(1)}, bf16[128,1536]{1,0:T(8,128)(2,1)S(1)}, u32[]{:S(2)}, u32[]{:S(2)}) %collective-permute-start.13) | collective-permute-done | bytes 393248 | tf_op jit(solution)/shard_map/ppermute | solution.py:122
  88.7 3.5 %collective-permute-done.15 = f32[2,512]{1,0:T(2,128)S(1)} collective-permute-done((f32[2,512]{1,0:T(2,128)S(1)}, f32[2,512]{1,0:T(2,128)S(1)}, u32[]{:S(2)}, u32[]{:S(2)}) %collective-permute-start.15) | collective-permute-done | bytes 4128 | tf_op jit(solution)/shard_map/ppermute | solution.py:27
  93.3 3.4 %collective-permute-start.19 = (bf16[512,128]{1,0:T(8,128)(2,1)S(1)}, bf16[512,128]{1,0:T(8,128)(2,1)S(1)}, u32[]{:S(2)}, u32[]{:S(2)}) collective-permute-start(bf16[512,128]{1,0:T(8,128)(2,1)S(1)} %pad_maximum_fusion.5), channel_id=1, source_target_pairs={{4,1},{1,4},{6,3},{3,6},{12,9},{9,12},{14,11},{11,14},{20,17},{17,... | collective-permute-start | bytes 393224 | tf_op jit(solution)/shard_map/ppermute | solution.py:181
  96.8 1.5 collective-permute-done.16
  98.3 3.4 %collective-permute-start.18 = (bf16[512,384]{1,0:T(8,128)(2,1)S(1)}, bf16[512,384]{1,0:T(8,128)(2,1)S(1)}, u32[]{:S(2)}, u32[]{:S(2)}) collective-permute-start(bf16[512,384]{1,0:T(8,128)(2,1)S(1)} %pad_maximum_fusion.2), channel_id=1, source_target_pairs={{4,1},{1,4},{6,3},{3,6},{12,9},{9,12},{14,11},{11,14},{20,17},{17,... | collective-permute-start | bytes 1179656 | tf_op jit(solution)/shard_map/ppermute | solution.py:181
  101.7 3.4 %collective-permute-start.21 = (bf16[512,1024]{1,0:T(8,128)(2,1)S(1)}, bf16[512,1024]{1,0:T(8,128)(2,1)S(1)}, u32[]{:S(2)}, u32[]{:S(2)}) collective-permute-start(bf16[512,1024]{1,0:T(8,128)(2,1)S(1)} %pad_maximum_fusion), channel_id=1, source_target_pairs={{4,1},{1,4},{6,3},{3,6},{12,9},{9,12},{14,11},{11,14},{20,17},{17,... | collective-permute-start | bytes 3145736 | tf_op jit(solution)/shard_map/ppermute | solution.py:181
  105.3 1.4 fusion.64
  106.7 3.7 %collective-permute-start.22 = (bf16[1536,128]{1,0:T(8,128)(2,1)S(1)}, bf16[1536,128]{1,0:T(8,128)(2,1)S(1)}, u32[]{:S(2)}, u32[]{:S(2)}) collective-permute-start(bf16[1536,128]{1,0:T(8,128)(2,1)S(1)} %fusion.64), channel_id=1, source_target_pairs={{0,8},{24,16},{1,9},{25,17},{2,10},{26,18},{3,11},{27,19},{4,12},{... | collective-permute-start | bytes 1179656 | tf_op jit(solution)/shard_map/ppermute | solution.py:52
  110.4 2.7 %collective-permute-done.18 = bf16[512,384]{1,0:T(8,128)(2,1)S(1)} collective-permute-done((bf16[512,384]{1,0:T(8,128)(2,1)S(1)}, bf16[512,384]{1,0:T(8,128)(2,1)S(1)}, u32[]{:S(2)}, u32[]{:S(2)}) %collective-permute-start.18) | collective-permute-done | bytes 393248 | tf_op jit(solution)/shard_map/ppermute | solution.py:181
  113.2 1.4 fusion.65
  114.7 3.5 %collective-permute-start.24 = (bf16[1536,128]{1,0:T(8,128)(2,1)S(1)}, bf16[1536,128]{1,0:T(8,128)(2,1)S(1)}, u32[]{:S(2)}, u32[]{:S(2)}) collective-permute-start(bf16[1536,128]{1,0:T(8,128)(2,1)S(1)} %fusion.65), channel_id=1, source_target_pairs={{0,8},{24,16},{1,9},{25,17},{2,10},{26,18},{3,11},{27,19},{4,12},{... | collective-permute-start | bytes 1179656 | tf_op jit(solution)/shard_map/ppermute | solution.py:52
  118.2 1.5 collective-permute-done.22
  120.5 2.2 fusion.35
  122.8 7.2 %collective-permute-start.27 = (bf16[1536,128]{1,0:T(8,128)(2,1)S(1)}, bf16[1536,128]{1,0:T(8,128)(2,1)S(1)}, u32[]{:S(2)}, u32[]{:S(2)}) collective-permute-start(bf16[1536,128]{1,0:T(8,128)(2,1)S(1)} %slice.505), channel_id=1, source_target_pairs={{0,8},{24,16},{1,9},{25,17},{2,10},{26,18},{3,11},{27,19},{4,12},{... | collective-permute-start | bytes 1179656 | tf_op jit(solution)/shard_map/ppermute | solution.py:52
  130.8 1.6 collective-permute-done.21
  133.0 3.7 %collective-permute-start.25 = (bf16[1536,128]{1,0:T(8,128)(2,1)S(1)}, bf16[1536,128]{1,0:T(8,128)(2,1)S(1)}, u32[]{:S(2)}, u32[]{:S(2)}) collective-permute-start(bf16[1536,128]{1,0:T(8,128)(2,1)S(1)} %fusion.90), channel_id=1, source_target_pairs={{0,8},{24,16},{8,0},{16,24},{1,9},{25,17},{9,1},{17,25},{2,10},{26... | collective-permute-start | bytes 1179656 | tf_op jit(solution)/shard_map/ppermute | solution.py:52
  136.7 2.1 collective-permute-done.27
  138.8 2.2 fusion.36
  142.1 3.8 %collective-permute-start.29 = (bf16[1536,128]{1,0:T(8,128)(2,1)S(1)}, bf16[1536,128]{1,0:T(8,128)(2,1)S(1)}, u32[]{:S(2)}, u32[]{:S(2)}) collective-permute-start(bf16[1536,128]{1,0:T(8,128)(2,1)S(1)} %fusion.91), channel_id=1, source_target_pairs={{0,8},{24,16},{8,0},{16,24},{1,9},{25,17},{9,1},{17,25},{2,10},{26... | collective-permute-start | bytes 1179656 | tf_op jit(solution)/shard_map/ppermute | solution.py:52
  145.9 2.2 fusion.37
  149.0 6.9 %collective-permute-start.31 = (bf16[1536,128]{1,0:T(8,128)(2,1)S(1)}, bf16[1536,128]{1,0:T(8,128)(2,1)S(1)}, u32[]{:S(2)}, u32[]{:S(2)}) collective-permute-start(bf16[1536,128]{1,0:T(8,128)(2,1)S(1)} %fusion.92), channel_id=1, source_target_pairs={{0,8},{24,16},{8,0},{16,24},{1,9},{25,17},{9,1},{17,25},{2,10},{26... | collective-permute-start | bytes 1179656 | tf_op jit(solution)/shard_map/ppermute | solution.py:52
  157.4 6.9 %collective-permute-start.33 = (bf16[1536,128]{1,0:T(8,128)(2,1)S(1)}, bf16[1536,128]{1,0:T(8,128)(2,1)S(1)}, u32[]{:S(2)}, u32[]{:S(2)}) collective-permute-start(bf16[1536,128]{1,0:T(8,128)(2,1)S(1)} %fusion.93), channel_id=1, source_target_pairs={{0,8},{24,16},{8,0},{16,24},{1,9},{25,17},{9,1},{17,25},{2,10},{26... | collective-permute-start | bytes 1179656 | tf_op jit(solution)/shard_map/ppermute | solution.py:52
  165.8 3.3 %fusion.38 = bf16[1536,256]{1,0:T(8,128)(2,1)S(1)} fusion(bf16[1536,1536]{1,0:T(8,128)(2,1)S(1)} %copy-done, bf16[1,1536,1536]{2,1,0:T(8,128)(2,1)S(1)} %bitcast.205, bf16[1,1536,1536]{2,1,0:T(8,128)(2,1)} %param.13, bf16[1024,1536]{1,0:T(8,128)(2,1)S(1)} %constant_dynamic-update-slice_fusion, bf16[1024,256]{1,0:T(8,128)(2,1)S(1)} %get-tuple-element.222), kind=kOutput, calls=%fused_computation.58 | convolution fusion | flops 812384256 | bytes 6815744 | tf_op jit(solution)/shard_map/dot_general | solution.py:194
  169.7 4.2 %collective-permute-start.35 = (bf16[1536,128]{1,0:T(8,128)(2,1)S(1)}, bf16[1536,128]{1,0:T(8,128)(2,1)S(1)}, u32[]{:S(2)}, u32[]{:S(2)}) collective-permute-start(bf16[1536,128]{1,0:T(8,128)(2,1)S(1)} %fusion.94), channel_id=1, source_target_pairs={{0,8},{24,16},{8,0},{16,24},{1,9},{25,17},{9,1},{17,25},{2,10},{26... | collective-permute-start | bytes 1179656 | tf_op jit(solution)/shard_map/ppermute | solution.py:52
  175.4 5.8 %collective-permute-start.37 = (bf16[1536,128]{1,0:T(8,128)(2,1)S(1)}, bf16[1536,128]{1,0:T(8,128)(2,1)S(1)}, u32[]{:S(2)}, u32[]{:S(2)}) collective-permute-start(bf16[1536,128]{1,0:T(8,128)(2,1)S(1)} %fusion.95), channel_id=1, source_target_pairs={{0,8},{24,16},{8,0},{16,24},{1,9},{25,17},{9,1},{17,25},{2,10},{26... | collective-permute-start | bytes 1179656 | tf_op jit(solution)/shard_map/ppermute | solution.py:52
  181.2 3.3 %fusion.39 = bf16[1536,256]{1,0:T(8,128)(2,1)S(1)} fusion(bf16[1536,1536]{1,0:T(8,128)(2,1)S(1)} %copy-done, bf16[1,1536,1536]{2,1,0:T(8,128)(2,1)S(1)} %bitcast.205, bf16[1,1536,1536]{2,1,0:T(8,128)(2,1)} %param.13, bf16[1024,1536]{1,0:T(8,128)(2,1)S(1)} %constant_dynamic-update-slice_fusion, bf16[1024,256]{1,0:T(8,128)(2,1)S(1)} %get-tuple-element.242), kind=kOutput, calls=%fused_computation.59 | convolution fusion | flops 812384256 | bytes 6815744 | tf_op jit(solution)/shard_map/dot_general | solution.py:194
  186.0 4.4 %collective-permute-start.39 = (bf16[1536,128]{1,0:T(8,128)(2,1)S(1)}, bf16[1536,128]{1,0:T(8,128)(2,1)S(1)}, u32[]{:S(2)}, u32[]{:S(2)}) collective-permute-start(bf16[1536,128]{1,0:T(8,128)(2,1)S(1)} %fusion.96), channel_id=1, source_target_pairs={{0,8},{24,16},{8,0},{16,24},{1,9},{25,17},{9,1},{17,25},{2,10},{26... | collective-permute-start | bytes 1179656 | tf_op jit(solution)/shard_map/ppermute | solution.py:52
  193.1 6.7 %collective-permute-start.41 = (bf16[1536,128]{1,0:T(8,128)(2,1)S(1)}, bf16[1536,128]{1,0:T(8,128)(2,1)S(1)}, u32[]{:S(2)}, u32[]{:S(2)}) collective-permute-start(bf16[1536,128]{1,0:T(8,128)(2,1)S(1)} %fusion.97), channel_id=1, source_target_pairs={{0,8},{24,16},{8,0},{16,24},{1,9},{25,17},{9,1},{17,25},{2,10},{26... | collective-permute-start | bytes 1179656 | tf_op jit(solution)/shard_map/ppermute | solution.py:52
  201.4 6.7 %collective-permute-start.43 = (bf16[1536,128]{1,0:T(8,128)(2,1)S(1)}, bf16[1536,128]{1,0:T(8,128)(2,1)S(1)}, u32[]{:S(2)}, u32[]{:S(2)}) collective-permute-start(bf16[1536,128]{1,0:T(8,128)(2,1)S(1)} %fusion.98), channel_id=1, source_target_pairs={{0,8},{24,16},{8,0},{16,24},{1,9},{25,17},{9,1},{17,25},{2,10},{26... | collective-permute-start | bytes 1179656 | tf_op jit(solution)/shard_map/ppermute | solution.py:52
  209.5 1.3 collective-permute-start.45
  210.8 6.0 %collective-permute-done.43 = bf16[1536,128]{1,0:T(8,128)(2,1)S(1)} collective-permute-done((bf16[1536,128]{1,0:T(8,128)(2,1)S(1)}, bf16[1536,128]{1,0:T(8,128)(2,1)S(1)}, u32[]{:S(2)}, u32[]{:S(2)}) %collective-permute-start.43) | collective-permute-done | bytes 393248 | tf_op jit(solution)/shard_map/ppermute | solution.py:52
  218.2 1.3 collective-permute-start.47
  219.9 5.3 %collective-permute-done.45 = bf16[1536,128]{1,0:T(8,128)(2,1)S(1)} collective-permute-done((bf16[1536,128]{1,0:T(8,128)(2,1)S(1)}, bf16[1536,128]{1,0:T(8,128)(2,1)S(1)}, u32[]{:S(2)}, u32[]{:S(2)}) %collective-permute-start.45) | collective-permute-done | bytes 393248 | tf_op jit(solution)/shard_map/ppermute | solution.py:52
  227.1 6.1 %collective-permute-done.47 = bf16[1536,128]{1,0:T(8,128)(2,1)S(1)} collective-permute-done((bf16[1536,128]{1,0:T(8,128)(2,1)S(1)}, bf16[1536,128]{1,0:T(8,128)(2,1)S(1)}, u32[]{:S(2)}, u32[]{:S(2)}) %collective-permute-start.47) | collective-permute-done | bytes 393248 | tf_op jit(solution)/shard_map/ppermute | solution.py:52
  233.7 3.8 %collective-permute-done.48 = bf16[1536,128]{1,0:T(8,128)(2,1)S(1)} collective-permute-done((bf16[1536,128]{1,0:T(8,128)(2,1)S(1)}, bf16[1536,128]{1,0:T(8,128)(2,1)S(1)}, u32[]{:S(2)}, u32[]{:S(2)}) %collective-permute-start.48) | collective-permute-done | bytes 393248 | tf_op jit(solution)/shard_map/ppermute | solution.py:52
  237.9 3.4 %copy-done.2 = f32[1536,1536]{1,0:T(8,128)} copy-done((f32[1536,1536]{1,0:T(8,128)}, f32[1536,1536]{1,0:T(8,128)S(1)}, u32[]{:S(2)}) %copy-start.2) | copy-done | bytes 9437208
  241.3 2.2 copy-done.3
  (181 shorter events, 39.9 us)
Async XLA Ops:
  0.6 19.6 %collective-permute-start = (bf16[256,1536]{1,0:T(8,128)(2,1)}, bf16[256,1536]{1,0:T(8,128)(2,1)S(1)}, u32[]{:S(2)}, u32[]{:S(2)}) collective-permute-start(bf16[256,1536]{1,0:T(8,128)(2,1)} %param.8), channel_id=1, source_target_pairs={{0,4},{2,6},{4,0},{6,2},{1,5},{3,7},{5,1},{7,3},{8,12},{10,14},{12... | collective-permute-start | bytes 2359304 | tf_op jit(solution)/shard_map/ppermute | solution.py:27
  4.7 15.5 %collective-permute-start.1 = (bf16[256,1536]{1,0:T(8,128)(2,1)}, bf16[256,1536]{1,0:T(8,128)(2,1)}, u32[]{:S(2)}, u32[]{:S(2)}) collective-permute-start(bf16[256,1536]{1,0:T(8,128)(2,1)} %get-tuple-element.302), channel_id=1, source_target_pairs={{0,2},{2,0},{4,6},{6,4},{1,3},{3,1},{5,7},{7,5},{8,10},{10,8},{12,... | collective-permute-start | bytes 2359304 | tf_op jit(solution)/shard_map/ppermute | solution.py:27
  5.7 14.5 %collective-permute-start.2 = (bf16[256,1536]{1,0:T(8,128)(2,1)}, bf16[256,1536]{1,0:T(8,128)(2,1)S(1)}, u32[]{:S(2)}, u32[]{:S(2)}) collective-permute-start(bf16[256,1536]{1,0:T(8,128)(2,1)} %get-tuple-element.300), channel_id=1, source_target_pairs={{0,2},{2,0},{4,6},{6,4},{1,3},{3,1},{5,7},{7,5},{8,10},{10,8},{12,... | collective-permute-start | bytes 2359304 | tf_op jit(solution)/shard_map/ppermute | solution.py:27
  6.2 21.1 %collective-permute-start.4 = (bf16[256,1536]{1,0:T(8,128)(2,1)}, bf16[256,1536]{1,0:T(8,128)(2,1)}, u32[]{:S(2)}, u32[]{:S(2)}) collective-permute-start(bf16[256,1536]{1,0:T(8,128)(2,1)} %param.8), channel_id=1, source_target_pairs={{0,2},{2,0},{4,6},{6,4},{1,3},{3,1},{5,7},{7,5},{8,10},{10,8},{12,... | collective-permute-start | bytes 2359304 | tf_op jit(solution)/shard_map/ppermute | solution.py:27
  20.2 7.1 %collective-permute-start.3 = (bf16[256,1536]{1,0:T(8,128)(2,1)S(1)}, bf16[256,1536]{1,0:T(8,128)(2,1)S(1)}, u32[]{:S(2)}, u32[]{:S(2)}) collective-permute-start(bf16[256,1536]{1,0:T(8,128)(2,1)S(1)} %collective-permute-done), channel_id=1, source_target_pairs={{0,2},{2,0},{4,6},{6,4},{1,3},{3,1},{5,7},{7,5},{8,10},{10,8},{12,... | collective-permute-start | bytes 2359304 | tf_op jit(solution)/shard_map/ppermute | solution.py:27
  24.3 21.3 %collective-permute-start.6 = (bf16[128,1536]{1,0:T(8,128)(2,1)S(1)}, bf16[128,1536]{1,0:T(8,128)(2,1)S(1)}, u32[]{:S(2)}, u32[]{:S(2)}) collective-permute-start(bf16[128,1536]{1,0:T(8,128)(2,1)S(1)} %convolution_convert_fusion.2), channel_id=1, source_target_pairs={{0,4},{2,6},{4,0},{6,2},{1,5},{3,7},{5,1},{7,3},{8,12},{10,14},{12... | collective-permute-start | bytes 1179656 | tf_op jit(solution)/shard_map/ppermute | solution.py:27
  26.6 17.6 %collective-permute-start.5 = (bf16[128,1536]{1,0:T(8,128)(2,1)S(1)}, bf16[128,1536]{1,0:T(8,128)(2,1)S(1)}, u32[]{:S(2)}, u32[]{:S(2)}) collective-permute-start(bf16[128,1536]{1,0:T(8,128)(2,1)S(1)} %convolution_convert_fusion.3), channel_id=1, source_target_pairs={{0,4},{2,6},{4,0},{6,2},{1,5},{3,7},{5,1},{7,3},{8,12},{10,14},{12... | collective-permute-start | bytes 1179656 | tf_op jit(solution)/shard_map/ppermute | solution.py:27
  32.0 37.5 %collective-permute-start.7 = (bf16[512,1536]{1,0:T(8,128)(2,1)S(1)}, bf16[512,1536]{1,0:T(8,128)(2,1)S(1)}, u32[]{:S(2)}, u32[]{:S(2)}) collective-permute-start(bf16[512,1536]{1,0:T(8,128)(2,1)S(1)} %slice.470), channel_id=1, source_target_pairs={{4,5},{1,0},{6,7},{3,2},{12,13},{9,8},{14,15},{11,10},{20,21},{17,... | collective-permute-start | bytes 4718600 | tf_op jit(solution)/shard_map/ppermute | solution.py:121
  44.3 25.2 %collective-permute-start.8 = (bf16[128,1536]{1,0:T(8,128)(2,1)S(1)}, bf16[128,1536]{1,0:T(8,128)(2,1)S(1)}, u32[]{:S(2)}, u32[]{:S(2)}) collective-permute-start(bf16[128,1536]{1,0:T(8,128)(2,1)S(1)} %collective-permute-done.5), channel_id=1, source_target_pairs={{0,1},{5,4},{2,3},{7,6},{8,9},{13,12},{10,11},{15,14},{16,17},{21,... | collective-permute-start | bytes 1179656 | tf_op jit(solution)/shard_map/ppermute | solution.py:122
  45.6 24.3 %collective-permute-start.10 = (bf16[128,1536]{1,0:T(8,128)(2,1)S(1)}, bf16[128,1536]{1,0:T(8,128)(2,1)S(1)}, u32[]{:S(2)}, u32[]{:S(2)}) collective-permute-start(bf16[128,1536]{1,0:T(8,128)(2,1)S(1)} %collective-permute-done.6), channel_id=1, source_target_pairs={{0,1},{5,4},{2,3},{7,6},{8,9},{13,12},{10,11},{15,14},{16,17},{21,... | collective-permute-start | bytes 1179656 | tf_op jit(solution)/shard_map/ppermute | solution.py:122
  46.9 21.2 %collective-permute-start.11 = (bf16[128,1536]{1,0:T(8,128)(2,1)S(1)}, bf16[128,1536]{1,0:T(8,128)(2,1)S(1)}, u32[]{:S(2)}, u32[]{:S(2)}) collective-permute-start(bf16[128,1536]{1,0:T(8,128)(2,1)S(1)} %slice.475), channel_id=1, source_target_pairs={{0,4},{2,6},{4,0},{6,2},{1,5},{3,7},{5,1},{7,3},{8,12},{10,14},{12... | collective-permute-start | bytes 1179656 | tf_op jit(solution)/shard_map/ppermute | solution.py:27
  50.5 16.4 %collective-permute-start.9 = (bf16[128,1536]{1,0:T(8,128)(2,1)S(1)}, bf16[128,1536]{1,0:T(8,128)(2,1)S(1)}, u32[]{:S(2)}, u32[]{:S(2)}) collective-permute-start(bf16[128,1536]{1,0:T(8,128)(2,1)S(1)} %convolution_convert_fusion.1), channel_id=1, source_target_pairs={{0,4},{2,6},{4,0},{6,2},{1,5},{3,7},{5,1},{7,3},{8,12},{10,14},{12... | collective-permute-start | bytes 1179656 | tf_op jit(solution)/shard_map/ppermute | solution.py:27
  66.8 13.9 %collective-permute-start.12 = (bf16[128,1536]{1,0:T(8,128)(2,1)S(1)}, bf16[128,1536]{1,0:T(8,128)(2,1)S(1)}, u32[]{:S(2)}, u32[]{:S(2)}) collective-permute-start(bf16[128,1536]{1,0:T(8,128)(2,1)S(1)} %collective-permute-done.9), channel_id=1, source_target_pairs={{0,1},{5,4},{2,3},{7,6},{8,9},{13,12},{10,11},{15,14},{16,17},{21,... | collective-permute-start | bytes 1179656 | tf_op jit(solution)/shard_map/ppermute | solution.py:122
  68.1 18.9 %collective-permute-start.13 = (bf16[128,1536]{1,0:T(8,128)(2,1)S(1)}, bf16[128,1536]{1,0:T(8,128)(2,1)S(1)}, u32[]{:S(2)}, u32[]{:S(2)}) collective-permute-start(bf16[128,1536]{1,0:T(8,128)(2,1)S(1)} %collective-permute-done.11), channel_id=1, source_target_pairs={{0,1},{5,4},{2,3},{7,6},{8,9},{13,12},{10,11},{15,14},{16,17},{21,... | collective-permute-start | bytes 1179656 | tf_op jit(solution)/shard_map/ppermute | solution.py:122
  88.5 3.7 %collective-permute-start.15 = (f32[2,512]{1,0:T(2,128)S(1)}, f32[2,512]{1,0:T(2,128)S(1)}, u32[]{:S(2)}, u32[]{:S(2)}) collective-permute-start(f32[2,512]{1,0:T(2,128)S(1)} %maximum_add_fusion), channel_id=1, source_target_pairs={{0,1},{1,0},{2,3},{3,2},{4,5},{5,4},{6,7},{7,6},{8,9},{9,8},{10,11... | collective-permute-start | bytes 12296 | tf_op jit(solution)/shard_map/ppermute | solution.py:27
  93.3 5.0 %collective-permute-start.16 = (bf16[512,128]{1,0:T(8,128)(2,1)S(1)}, bf16[512,128]{1,0:T(8,128)(2,1)S(1)}, u32[]{:S(2)}, u32[]{:S(2)}) collective-permute-start(bf16[512,128]{1,0:T(8,128)(2,1)S(1)} %pad_maximum_fusion.5), channel_id=1, source_target_pairs={{0,1},{5,4},{4,0},{1,5},{2,3},{7,6},{6,2},{3,7},{8,9},{13,12},{12,... | collective-permute-start | bytes 393224 | tf_op jit(solution)/shard_map/ppermute | solution.py:180
  93.3 8.3 %collective-permute-start.19 = (bf16[512,128]{1,0:T(8,128)(2,1)S(1)}, bf16[512,128]{1,0:T(8,128)(2,1)S(1)}, u32[]{:S(2)}, u32[]{:S(2)}) collective-permute-start(bf16[512,128]{1,0:T(8,128)(2,1)S(1)} %pad_maximum_fusion.5), channel_id=1, source_target_pairs={{4,1},{1,4},{6,3},{3,6},{12,9},{9,12},{14,11},{11,14},{20,17},{17,... | collective-permute-start | bytes 393224 | tf_op jit(solution)/shard_map/ppermute | solution.py:181
  98.3 12.1 %collective-permute-start.17 = (bf16[512,384]{1,0:T(8,128)(2,1)S(1)}, bf16[512,384]{1,0:T(8,128)(2,1)S(1)}, u32[]{:S(2)}, u32[]{:S(2)}) collective-permute-start(bf16[512,384]{1,0:T(8,128)(2,1)S(1)} %pad_maximum_fusion.2), channel_id=1, source_target_pairs={{0,1},{5,4},{4,0},{1,5},{2,3},{7,6},{6,2},{3,7},{8,9},{13,12},{12,... | collective-permute-start | bytes 1179656 | tf_op jit(solution)/shard_map/ppermute | solution.py:180
  98.3 14.8 %collective-permute-start.18 = (bf16[512,384]{1,0:T(8,128)(2,1)S(1)}, bf16[512,384]{1,0:T(8,128)(2,1)S(1)}, u32[]{:S(2)}, u32[]{:S(2)}) collective-permute-start(bf16[512,384]{1,0:T(8,128)(2,1)S(1)} %pad_maximum_fusion.2), channel_id=1, source_target_pairs={{4,1},{1,4},{6,3},{3,6},{12,9},{9,12},{14,11},{11,14},{20,17},{17,... | collective-permute-start | bytes 1179656 | tf_op jit(solution)/shard_map/ppermute | solution.py:181
  101.7 29.1 %collective-permute-start.20 = (bf16[512,1024]{1,0:T(8,128)(2,1)S(1)}, bf16[512,1024]{1,0:T(8,128)(2,1)S(1)}, u32[]{:S(2)}, u32[]{:S(2)}) collective-permute-start(bf16[512,1024]{1,0:T(8,128)(2,1)S(1)} %pad_maximum_fusion), channel_id=1, source_target_pairs={{0,1},{5,4},{4,0},{1,5},{2,3},{7,6},{6,2},{3,7},{8,9},{13,12},{12,... | collective-permute-start | bytes 3145736 | tf_op jit(solution)/shard_map/ppermute | solution.py:180
  101.7 30.7 %collective-permute-start.21 = (bf16[512,1024]{1,0:T(8,128)(2,1)S(1)}, bf16[512,1024]{1,0:T(8,128)(2,1)S(1)}, u32[]{:S(2)}, u32[]{:S(2)}) collective-permute-start(bf16[512,1024]{1,0:T(8,128)(2,1)S(1)} %pad_maximum_fusion), channel_id=1, source_target_pairs={{4,1},{1,4},{6,3},{3,6},{12,9},{9,12},{14,11},{11,14},{20,17},{17,... | collective-permute-start | bytes 3145736 | tf_op jit(solution)/shard_map/ppermute | solution.py:181
  106.7 13.0 %collective-permute-start.22 = (bf16[1536,128]{1,0:T(8,128)(2,1)S(1)}, bf16[1536,128]{1,0:T(8,128)(2,1)S(1)}, u32[]{:S(2)}, u32[]{:S(2)}) collective-permute-start(bf16[1536,128]{1,0:T(8,128)(2,1)S(1)} %fusion.64), channel_id=1, source_target_pairs={{0,8},{24,16},{1,9},{25,17},{2,10},{26,18},{3,11},{27,19},{4,12},{... | collective-permute-start | bytes 1179656 | tf_op jit(solution)/shard_map/ppermute | solution.py:52
  114.7 15.3 %collective-permute-start.24 = (bf16[1536,128]{1,0:T(8,128)(2,1)S(1)}, bf16[1536,128]{1,0:T(8,128)(2,1)S(1)}, u32[]{:S(2)}, u32[]{:S(2)}) collective-permute-start(bf16[1536,128]{1,0:T(8,128)(2,1)S(1)} %fusion.65), channel_id=1, source_target_pairs={{0,8},{24,16},{1,9},{25,17},{2,10},{26,18},{3,11},{27,19},{4,12},{... | collective-permute-start | bytes 1179656 | tf_op jit(solution)/shard_map/ppermute | solution.py:52
  119.9 10.9 %collective-permute-start.23 = (bf16[1536,128]{1,0:T(8,128)(2,1)S(1)}, bf16[1536,128]{1,0:T(8,128)(2,1)S(1)}, u32[]{:S(2)}, u32[]{:S(2)}) collective-permute-start(bf16[1536,128]{1,0:T(8,128)(2,1)S(1)} %add_convert_fusion.35), channel_id=1, source_target_pairs={{8,16},{16,8},{9,17},{17,9},{10,18},{18,10},{11,19},{19,11},{12,20... | collective-permute-start | bytes 1179656 | tf_op jit(solution)/shard_map/ppermute | solution.py:60
  122.8 16.1 %collective-permute-start.27 = (bf16[1536,128]{1,0:T(8,128)(2,1)S(1)}, bf16[1536,128]{1,0:T(8,128)(2,1)S(1)}, u32[]{:S(2)}, u32[]{:S(2)}) collective-permute-start(bf16[1536,128]{1,0:T(8,128)(2,1)S(1)} %slice.505), channel_id=1, source_target_pairs={{0,8},{24,16},{1,9},{25,17},{2,10},{26,18},{3,11},{27,19},{4,12},{... | collective-permute-start | bytes 1179656 | tf_op jit(solution)/shard_map/ppermute | solution.py:52
  130.1 11.7 %collective-permute-start.26 = (bf16[1536,128]{1,0:T(8,128)(2,1)S(1)}, bf16[1536,128]{1,0:T(8,128)(2,1)S(1)}, u32[]{:S(2)}, u32[]{:S(2)}) collective-permute-start(bf16[1536,128]{1,0:T(8,128)(2,1)S(1)} %add_convert_fusion.34), channel_id=1, source_target_pairs={{8,16},{16,8},{9,17},{17,9},{10,18},{18,10},{11,19},{19,11},{12,20... | collective-permute-start | bytes 1179656 | tf_op jit(solution)/shard_map/ppermute | solution.py:60
  133.0 15.1 %collective-permute-start.25 = (bf16[1536,128]{1,0:T(8,128)(2,1)S(1)}, bf16[1536,128]{1,0:T(8,128)(2,1)S(1)}, u32[]{:S(2)}, u32[]{:S(2)}) collective-permute-start(bf16[1536,128]{1,0:T(8,128)(2,1)S(1)} %fusion.90), channel_id=1, source_target_pairs={{0,8},{24,16},{8,0},{16,24},{1,9},{25,17},{9,1},{17,25},{2,10},{26... | collective-permute-start | bytes 1179656 | tf_op jit(solution)/shard_map/ppermute | solution.py:52
  141.1 7.7 %collective-permute-start.28 = (bf16[1536,128]{1,0:T(8,128)(2,1)S(1)}, bf16[1536,128]{1,0:T(8,128)(2,1)S(1)}, u32[]{:S(2)}, u32[]{:S(2)}) collective-permute-start(bf16[1536,128]{1,0:T(8,128)(2,1)S(1)} %add_convert_fusion.32), channel_id=1, source_target_pairs={{8,16},{16,8},{9,17},{17,9},{10,18},{18,10},{11,19},{19,11},{12,20... | collective-permute-start | bytes 1179656 | tf_op jit(solution)/shard_map/ppermute | solution.py:60
  142.1 14.3 %collective-permute-start.29 = (bf16[1536,128]{1,0:T(8,128)(2,1)S(1)}, bf16[1536,128]{1,0:T(8,128)(2,1)S(1)}, u32[]{:S(2)}, u32[]{:S(2)}) collective-permute-start(bf16[1536,128]{1,0:T(8,128)(2,1)S(1)} %fusion.91), channel_id=1, source_target_pairs={{0,8},{24,16},{8,0},{16,24},{1,9},{25,17},{9,1},{17,25},{2,10},{26... | collective-permute-start | bytes 1179656 | tf_op jit(solution)/shard_map/ppermute | solution.py:52
  148.2 9.0 %collective-permute-start.30 = (bf16[1536,128]{1,0:T(8,128)(2,1)S(1)}, bf16[1536,128]{1,0:T(8,128)(2,1)S(1)}, u32[]{:S(2)}, u32[]{:S(2)}) collective-permute-start(bf16[1536,128]{1,0:T(8,128)(2,1)S(1)} %add_convert_fusion.30), channel_id=1, source_target_pairs={{8,16},{16,8},{9,17},{17,9},{10,18},{18,10},{11,19},{19,11},{12,20... | collective-permute-start | bytes 1179656 | tf_op jit(solution)/shard_map/ppermute | solution.py:60
  149.0 15.7 %collective-permute-start.31 = (bf16[1536,128]{1,0:T(8,128)(2,1)S(1)}, bf16[1536,128]{1,0:T(8,128)(2,1)S(1)}, u32[]{:S(2)}, u32[]{:S(2)}) collective-permute-start(bf16[1536,128]{1,0:T(8,128)(2,1)S(1)} %fusion.92), channel_id=1, source_target_pairs={{0,8},{24,16},{8,0},{16,24},{1,9},{25,17},{9,1},{17,25},{2,10},{26... | collective-permute-start | bytes 1179656 | tf_op jit(solution)/shard_map/ppermute | solution.py:52
  156.5 13.1 %collective-permute-start.32 = (bf16[1536,128]{1,0:T(8,128)(2,1)S(1)}, bf16[1536,128]{1,0:T(8,128)(2,1)S(1)}, u32[]{:S(2)}, u32[]{:S(2)}) collective-permute-start(bf16[1536,128]{1,0:T(8,128)(2,1)S(1)} %add_convert_fusion.28), channel_id=1, source_target_pairs={{8,16},{16,8},{9,17},{17,9},{10,18},{18,10},{11,19},{19,11},{12,20... | collective-permute-start | bytes 1179656 | tf_op jit(solution)/shard_map/ppermute | solution.py:60
  157.4 17.1 %collective-permute-start.33 = (bf16[1536,128]{1,0:T(8,128)(2,1)S(1)}, bf16[1536,128]{1,0:T(8,128)(2,1)S(1)}, u32[]{:S(2)}, u32[]{:S(2)}) collective-permute-start(bf16[1536,128]{1,0:T(8,128)(2,1)S(1)} %fusion.93), channel_id=1, source_target_pairs={{0,8},{24,16},{8,0},{16,24},{1,9},{25,17},{9,1},{17,25},{2,10},{26... | collective-permute-start | bytes 1179656 | tf_op jit(solution)/shard_map/ppermute | solution.py:52
  164.8 10.4 %collective-permute-start.34 = (bf16[1536,128]{1,0:T(8,128)(2,1)S(1)}, bf16[1536,128]{1,0:T(8,128)(2,1)S(1)}, u32[]{:S(2)}, u32[]{:S(2)}) collective-permute-start(bf16[1536,128]{1,0:T(8,128)(2,1)S(1)} %add_convert_fusion.26), channel_id=1, source_target_pairs={{8,16},{16,8},{9,17},{17,9},{10,18},{18,10},{11,19},{19,11},{12,20... | collective-permute-start | bytes 1179656 | tf_op jit(solution)/shard_map/ppermute | solution.py:60
  169.7 15.3 %collective-permute-start.35 = (bf16[1536,128]{1,0:T(8,128)(2,1)S(1)}, bf16[1536,128]{1,0:T(8,128)(2,1)S(1)}, u32[]{:S(2)}, u32[]{:S(2)}) collective-permute-start(bf16[1536,128]{1,0:T(8,128)(2,1)S(1)} %fusion.94), channel_id=1, source_target_pairs={{0,8},{24,16},{8,0},{16,24},{1,9},{25,17},{9,1},{17,25},{2,10},{26... | collective-permute-start | bytes 1179656 | tf_op jit(solution)/shard_map/ppermute | solution.py:52
  174.6 11.3 %collective-permute-start.36 = (bf16[1536,128]{1,0:T(8,128)(2,1)S(1)}, bf16[1536,128]{1,0:T(8,128)(2,1)S(1)}, u32[]{:S(2)}, u32[]{:S(2)}) collective-permute-start(bf16[1536,128]{1,0:T(8,128)(2,1)S(1)} %add_convert_fusion.24), channel_id=1, source_target_pairs={{8,16},{16,8},{9,17},{17,9},{10,18},{18,10},{11,19},{19,11},{12,20... | collective-permute-start | bytes 1179656 | tf_op jit(solution)/shard_map/ppermute | solution.py:60
  175.4 16.2 %collective-permute-start.37 = (bf16[1536,128]{1,0:T(8,128)(2,1)S(1)}, bf16[1536,128]{1,0:T(8,128)(2,1)S(1)}, u32[]{:S(2)}, u32[]{:S(2)}) collective-permute-start(bf16[1536,128]{1,0:T(8,128)(2,1)S(1)} %fusion.95), channel_id=1, source_target_pairs={{0,8},{24,16},{8,0},{16,24},{1,9},{25,17},{9,1},{17,25},{2,10},{26... | collective-permute-start | bytes 1179656 | tf_op jit(solution)/shard_map/ppermute | solution.py:52
  185.1 7.8 %collective-permute-start.38 = (bf16[1536,128]{1,0:T(8,128)(2,1)S(1)}, bf16[1536,128]{1,0:T(8,128)(2,1)S(1)}, u32[]{:S(2)}, u32[]{:S(2)}) collective-permute-start(bf16[1536,128]{1,0:T(8,128)(2,1)S(1)} %add_convert_fusion.22), channel_id=1, source_target_pairs={{8,16},{16,8},{9,17},{17,9},{10,18},{18,10},{11,19},{19,11},{12,20... | collective-permute-start | bytes 1179656 | tf_op jit(solution)/shard_map/ppermute | solution.py:60
  186.0 14.4 %collective-permute-start.39 = (bf16[1536,128]{1,0:T(8,128)(2,1)S(1)}, bf16[1536,128]{1,0:T(8,128)(2,1)S(1)}, u32[]{:S(2)}, u32[]{:S(2)}) collective-permute-start(bf16[1536,128]{1,0:T(8,128)(2,1)S(1)} %fusion.96), channel_id=1, source_target_pairs={{0,8},{24,16},{8,0},{16,24},{1,9},{25,17},{9,1},{17,25},{2,10},{26... | collective-permute-start | bytes 1179656 | tf_op jit(solution)/shard_map/ppermute | solution.py:52
  191.7 9.5 %collective-permute-start.40 = (bf16[1536,128]{1,0:T(8,128)(2,1)S(1)}, bf16[1536,128]{1,0:T(8,128)(2,1)S(1)}, u32[]{:S(2)}, u32[]{:S(2)}) collective-permute-start(bf16[1536,128]{1,0:T(8,128)(2,1)S(1)} %add_convert_fusion.20), channel_id=1, source_target_pairs={{8,16},{16,8},{9,17},{17,9},{10,18},{18,10},{11,19},{19,11},{12,20... | collective-permute-start | bytes 1179656 | tf_op jit(solution)/shard_map/ppermute | solution.py:60
  193.1 15.5 %collective-permute-start.41 = (bf16[1536,128]{1,0:T(8,128)(2,1)S(1)}, bf16[1536,128]{1,0:T(8,128)(2,1)S(1)}, u32[]{:S(2)}, u32[]{:S(2)}) collective-permute-start(bf16[1536,128]{1,0:T(8,128)(2,1)S(1)} %fusion.97), channel_id=1, source_target_pairs={{0,8},{24,16},{8,0},{16,24},{1,9},{25,17},{9,1},{17,25},{2,10},{26... | collective-permute-start | bytes 1179656 | tf_op jit(solution)/shard_map/ppermute | solution.py:52
  200.5 8.8 %collective-permute-start.42 = (bf16[1536,128]{1,0:T(8,128)(2,1)S(1)}, bf16[1536,128]{1,0:T(8,128)(2,1)S(1)}, u32[]{:S(2)}, u32[]{:S(2)}) collective-permute-start(bf16[1536,128]{1,0:T(8,128)(2,1)S(1)} %add_convert_fusion.18), channel_id=1, source_target_pairs={{8,16},{16,8},{9,17},{17,9},{10,18},{18,10},{11,19},{19,11},{12,20... | collective-permute-start | bytes 1179656 | tf_op jit(solution)/shard_map/ppermute | solution.py:60
  201.4 15.4 %collective-permute-start.43 = (bf16[1536,128]{1,0:T(8,128)(2,1)S(1)}, bf16[1536,128]{1,0:T(8,128)(2,1)S(1)}, u32[]{:S(2)}, u32[]{:S(2)}) collective-permute-start(bf16[1536,128]{1,0:T(8,128)(2,1)S(1)} %fusion.98), channel_id=1, source_target_pairs={{0,8},{24,16},{8,0},{16,24},{1,9},{25,17},{9,1},{17,25},{2,10},{26... | collective-permute-start | bytes 1179656 | tf_op jit(solution)/shard_map/ppermute | solution.py:52
  208.7 9.4 %collective-permute-start.44 = (bf16[1536,128]{1,0:T(8,128)(2,1)S(1)}, bf16[1536,128]{1,0:T(8,128)(2,1)S(1)}, u32[]{:S(2)}, u32[]{:S(2)}) collective-permute-start(bf16[1536,128]{1,0:T(8,128)(2,1)S(1)} %add_convert_fusion.16), channel_id=1, source_target_pairs={{8,16},{16,8},{9,17},{17,9},{10,18},{18,10},{11,19},{19,11},{12,20... | collective-permute-start | bytes 1179656 | tf_op jit(solution)/shard_map/ppermute | solution.py:60
  209.5 15.7 %collective-permute-start.45 = (bf16[1536,128]{1,0:T(8,128)(2,1)S(1)}, bf16[1536,128]{1,0:T(8,128)(2,1)S(1)}, u32[]{:S(2)}, u32[]{:S(2)}) collective-permute-start(bf16[1536,128]{1,0:T(8,128)(2,1)S(1)} %add_convert_fusion.15), channel_id=1, source_target_pairs={{8,0},{16,24},{9,1},{17,25},{10,2},{18,26},{11,3},{19,27},{12,4},{... | collective-permute-start | bytes 1179656 | tf_op jit(solution)/shard_map/ppermute | solution.py:52
  216.9 8.3 %collective-permute-start.46 = (bf16[1536,128]{1,0:T(8,128)(2,1)S(1)}, bf16[1536,128]{1,0:T(8,128)(2,1)S(1)}, u32[]{:S(2)}, u32[]{:S(2)}) collective-permute-start(bf16[1536,128]{1,0:T(8,128)(2,1)S(1)} %add_convert_fusion.14), channel_id=1, source_target_pairs={{8,16},{16,8},{9,17},{17,9},{10,18},{18,10},{11,19},{19,11},{12,20... | collective-permute-start | bytes 1179656 | tf_op jit(solution)/shard_map/ppermute | solution.py:60
  218.2 15.0 %collective-permute-start.47 = (bf16[1536,128]{1,0:T(8,128)(2,1)S(1)}, bf16[1536,128]{1,0:T(8,128)(2,1)S(1)}, u32[]{:S(2)}, u32[]{:S(2)}) collective-permute-start(bf16[1536,128]{1,0:T(8,128)(2,1)S(1)} %add_convert_fusion.13), channel_id=1, source_target_pairs={{8,0},{16,24},{9,1},{17,25},{10,2},{18,26},{11,3},{19,27},{12,4},{... | collective-permute-start | bytes 1179656 | tf_op jit(solution)/shard_map/ppermute | solution.py:52
  225.3 12.1 %collective-permute-start.48 = (bf16[1536,128]{1,0:T(8,128)(2,1)S(1)}, bf16[1536,128]{1,0:T(8,128)(2,1)S(1)}, u32[]{:S(2)}, u32[]{:S(2)}) collective-permute-start(bf16[1536,128]{1,0:T(8,128)(2,1)S(1)} %add_convert_fusion.12), channel_id=1, source_target_pairs={{8,0},{16,24},{9,1},{17,25},{10,2},{18,26},{11,3},{19,27},{12,4},{... | collective-permute-start | bytes 1179656 | tf_op jit(solution)/shard_map/ppermute | solution.py:52
  (12 other events, 116.9 us)

commit v11 on v10

--- a/solution.py
+++ b/solution.py
@@ -109,35 +109,39 @@
     held = together(swap(context, "fsdp", group), *moved[0], *moved[1])
     residual_parts, cotangent_parts = held[1 : 1 + group], held[1 + group :]
     far_blocks = [held[0]] + [swap(held[0], "fsdp", r) for r in range(1, group)]
-    far_outs = []
+    far_outs, near_out, passed, near_came = [], [], [], []
     for k in range(group * pieces):
         r, p = k // pieces, k % pieces
-        blocks = [far_blocks[r][p * rows : (p + 1) * rows]]
-        if k == group * pieces - 1:
-            blocks += near_blocks
+        far = far_blocks[r]
+        if 1 <= k <= group:
+            far, near_out[k - 1] = together(far, near_out[k - 1])
+        if k >= 2:
+            far, far_outs[k - 2] = together(far, far_outs[k - 2])
+        blocks = [far[p * rows : (p + 1) * rows]] + near_blocks[k : k + 1]
         out = project(jnp.concatenate(blocks, axis=0))
         far_outs.append(swap(out[:rows], "fsdp", group))
-    near_out = out[rows:]
-    near_came = lax.ppermute(near_out, ("fsdp", "tp"), inward_pairs)
-    passed = [lax.ppermute(out, ("fsdp", "tp"), outward_pairs) for out in far_outs]
+        passed.append(lax.ppermute(far_outs[k], ("fsdp", "tp"), outward_pairs))
+        if k < group:
+            near_out.append(out[rows:])
+            near_came.append(lax.ppermute(near_out[k], ("fsdp", "tp"), inward_pairs))
 
     gain_part = lax.dynamic_slice_in_dim(gain, t * (width // 2) + low * cols, cols).astype(f32)
 
     hidden, weighted, sums = [], [], []
     for k in range(group * pieces):
         r, p = k // pieces, k % pieces
-        span, long_span = slice(p * rows, (p + 1) * rows), slice(k * rows, (k + 1) * rows)
+        span = slice(p * rows, (p + 1) * rows)
         far_out, came = far_outs[k], passed[k]
         if sums:
             far_out, sums[-1] = together(far_out, sums[-1])
-        keep = jnp.where(near, near_out[long_span], far_out)
+        keep = jnp.where(near, near_out[r][span], far_out)
         base, w = lax.optimization_barrier(
             (
                 residual_parts[r][span].astype(f32) + keep.astype(f32),
                 gain_part[None, :] * cotangent_parts[r][span].astype(f32),
             )
         )
-        h = base + jnp.where(near, near_came[long_span], came).astype(f32)
+        h = base + jnp.where(near, near_came[r][span], came).astype(f32)
         hidden.append(h)
         weighted.append(w)
         sums.append(jnp.stack([jnp.sum(h * h, axis=-1), jnp.sum(h * w, axis=-1)]))

time: 245 us -> 251 us (1.024)
  starting transfers between devices: 101 us -> 106 us
  waiting for transfers between devices: 88.6 us -> 91.9 us
    ppermute x5 -> x6, waiting for transfers between devices: 14.2 us -> 25.6 us  [the longest x4 25.6 us: body(): passed.append(lax.ppermute(far_outs[k], ('fsdp', 'tp'), outward_pairs))]
    ppermute x11, waiting for transfers between devices: 41.8 us -> 32.6 us  [swap(): return lax.ppermute(value, axis, [(i, i ^ bit) for i in range(count)])]
    ppermute x5 -> x6, starting transfers between devices: 7.55 us -> 10.6 us  [the longest x2 5.49 us: body(): near_came.append(lax.ppermute(near_out[k], ('fsdp', 'tp'), inward_pairs))]
    unnamed x25 -> x26, other arithmetic: 5.13 us -> 5.07 us
    unnamed x25 -> x27, local copies, waits for them, and re-layouts: 8.12 us -> 8.12 us
  transfers between devices with their start and end apart: 49 -> 50, of which waited for: 19 -> 23; matrix products, arithmetic and copies ran while one was open for 18% -> 17% of each run, Pallas kernels for 0% -> 0%
where the time goes in v11:
time: 251 us; the launch traced here: 250 us
  starting transfers between devices  106 us (42%)
  waiting for transfers between devices  91.9 us (37%)
  matrix products  23.2 us (9%)
  other arithmetic  15.4 us (6%)
  local copies, waits for them, and re-layouts  11.9 us (5%)
    ppermute x15, starting transfers between devices, send_outer(): self.edge[s] = lax.ppermute(payload, 'island', pairs)  67.4 us
    ppermute x11, waiting for transfers between devices, swap(): return lax.ppermute(value, axis, [(i, i ^ bit) for i in range(count)])  32.6 us
    ppermute x15, waiting for transfers between devices, send_outer(): self.edge[s] = lax.ppermute(payload, 'island', pairs)  27.6 us
    ppermute x4, waiting for transfers between devices, body(): passed.append(lax.ppermute(far_outs[k], ('fsdp', 'tp'), outward_pairs))  25.6 us
    dot_general x7, matrix products, add_pseudo(): lax.dot_general(context_all, piece, (((0,), (0,)), ((), ())), preferred_e...  13.8 us
    ppermute x3, starting transfers between devices, move(): crosses.append(lax.ppermute(d_local, ('fsdp', 'tp'), cross_pairs))  10.2 us
    dot_general x4, matrix products, project(): jnp.dot(block, weight, preferred_element_type=f32).astype(bf16)  9.39 us
    ppermute x11, starting transfers between devices, swap(): return lax.ppermute(value, axis, [(i, i ^ bit) for i in range(count)])  9.03 us
  transfers between devices with their start and end apart: 50, of which 23 were waited for; matrix products, arithmetic and copies ran while one was open for 17% of the time, Pallas kernels for 0%

profile of v11, /device:TPU:2, one launch (start us, length us, event | category | flops | bytes accessed | tf_op | source)
XLA Modules:
  0.0 250.0 jit_solution(15015722405550234086)
XLA Ops:
  0.6 1.6 collective-permute-start
  2.2 2.5 constant_dynamic-slice_fusion.2
  8.1 12.0 %collective-permute-done = bf16[256,1536]{1,0:T(8,128)(2,1)S(1)} collective-permute-done((bf16[256,1536]{1,0:T(8,128)(2,1)}, bf16[256,1536]{1,0:T(8,128)(2,1)S(1)}, u32[]{:S(2)}, u32[]{:S(2)}) %collective-permute-start) | collective-permute-done | bytes 786464 | tf_op jit(solution)/shard_map/ppermute | solution.py:27
  20.3 4.7 %convolution_convert_fusion.1 = bf16[384,1536]{1,0:T(8,128)(2,1)S(1)} fusion(bf16[1536,1536]{1,0:T(8,128)(2,1)} %param.12, bf16[256,1536]{1,0:T(8,128)(2,1)} %param.8, bf16[128,1536]{1,0:T(8,128)(2,1)S(1)} %slice.361), kind=kOutput, calls=%fused_computation.1 | convolution fusion | flops 1814888448 | bytes 7077888 | tf_op jit(solution)/shard_map/dot_general | solution.py:89
  25.1 3.1 %convolution_convert_fusion = bf16[384,1536]{1,0:T(8,128)(2,1)S(1)} fusion(bf16[1536,1536]{1,0:T(8,128)(2,1)S(1)} %bitcast.193, bf16[256,1536]{1,0:T(8,128)(2,1)} %collective-permute-done.4, bf16[128,1536]{1,0:T(8,128)(2,1)S(1)} %slice.364), kind=kOutput, calls=%fused_computation | convolution fusion | flops 1814888448 | bytes 7077888 | tf_op jit(solution)/shard_map/dot_general | solution.py:89
  28.4 2.3 collective-permute-start.7
  31.3 1.5 collective-permute-start.5
  32.7 3.2 %collective-permute-start.12 = (bf16[256,1536]{1,0:T(8,128)(2,1)S(1)}, bf16[256,1536]{1,0:T(8,128)(2,1)S(1)}, u32[]{:S(2)}, u32[]{:S(2)}) collective-permute-start(bf16[256,1536]{1,0:T(8,128)(2,1)S(1)} %slice.473), channel_id=1, source_target_pairs={{4,5},{1,0},{6,7},{3,2},{12,13},{9,8},{14,15},{11,10},{20,21},{17,... | collective-permute-start | bytes 2359304 | tf_op jit(solution)/shard_map/ppermute | solution.py:126
  37.6 12.8 %collective-permute-done.5 = bf16[128,1536]{1,0:T(8,128)(2,1)S(1)} collective-permute-done((bf16[128,1536]{1,0:T(8,128)(2,1)S(1)}, bf16[128,1536]{1,0:T(8,128)(2,1)S(1)}, u32[]{:S(2)}, u32[]{:S(2)}) %collective-permute-start.5) | collective-permute-done | bytes 393248 | tf_op jit(solution)/shard_map/ppermute | solution.py:27
  53.8 4.0 %collective-permute-start.11 = (bf16[128,1536]{1,0:T(8,128)(2,1)S(1)}, bf16[128,1536]{1,0:T(8,128)(2,1)S(1)}, u32[]{:S(2)}, u32[]{:S(2)}) collective-permute-start(bf16[128,1536]{1,0:T(8,128)(2,1)S(1)} %convolution_convert_fusion.2), channel_id=1, source_target_pairs={{0,4},{2,6},{4,0},{6,2},{1,5},{3,7},{5,1},{7,3},{8,12},{10,14},{12... | collective-permute-start | bytes 1179656 | tf_op jit(solution)/shard_map/ppermute | solution.py:27
  58.7 5.6 %collective-permute-done.8 = bf16[128,1536]{1,0:T(8,128)(2,1)S(1)} collective-permute-done((bf16[128,1536]{1,0:T(8,128)(2,1)S(1)}, bf16[128,1536]{1,0:T(8,128)(2,1)S(1)}, u32[]{:S(2)}, u32[]{:S(2)}) %collective-permute-start.8) | collective-permute-done | bytes 393248 | tf_op jit(solution)/shard_map/ppermute | solution.py:123
  65.5 5.5 %collective-permute-done.10 = bf16[128,1536]{1,0:T(8,128)(2,1)S(1)} collective-permute-done((bf16[128,1536]{1,0:T(8,128)(2,1)S(1)}, bf16[128,1536]{1,0:T(8,128)(2,1)S(1)}, u32[]{:S(2)}, u32[]{:S(2)}) %collective-permute-start.10) | collective-permute-done | bytes 393248 | tf_op jit(solution)/shard_map/ppermute | solution.py:123
  71.4 3.1 %collective-permute-done.9 = bf16[128,1536]{1,0:T(8,128)(2,1)S(1)} collective-permute-done((bf16[128,1536]{1,0:T(8,128)(2,1)S(1)}, bf16[128,1536]{1,0:T(8,128)(2,1)S(1)}, u32[]{:S(2)}, u32[]{:S(2)}) %collective-permute-start.9) | collective-permute-done | bytes 393248 | tf_op jit(solution)/shard_map/ppermute | solution.py:27
  78.3 10.2 %collective-permute-done.13 = bf16[128,1536]{1,0:T(8,128)(2,1)S(1)} collective-permute-done((bf16[128,1536]{1,0:T(8,128)(2,1)S(1)}, bf16[128,1536]{1,0:T(8,128)(2,1)S(1)}, u32[]{:S(2)}, u32[]{:S(2)}) %collective-permute-start.13) | collective-permute-done | bytes 393248 | tf_op jit(solution)/shard_map/ppermute | solution.py:123
  89.9 4.2 %collective-permute-done.14 = bf16[128,1536]{1,0:T(8,128)(2,1)S(1)} collective-permute-done((bf16[128,1536]{1,0:T(8,128)(2,1)S(1)}, bf16[128,1536]{1,0:T(8,128)(2,1)S(1)}, u32[]{:S(2)}, u32[]{:S(2)}) %collective-permute-start.14) | collective-permute-done | bytes 393248 | tf_op jit(solution)/shard_map/ppermute | solution.py:123
  95.8 3.5 %collective-permute-done.16 = f32[2,512]{1,0:T(2,128)S(1)} collective-permute-done((f32[2,512]{1,0:T(2,128)S(1)}, f32[2,512]{1,0:T(2,128)S(1)}, u32[]{:S(2)}, u32[]{:S(2)}) %collective-permute-start.16) | collective-permute-done | bytes 4128 | tf_op jit(solution)/shard_map/ppermute | solution.py:27
  100.6 3.5 %collective-permute-start.20 = (bf16[512,128]{1,0:T(8,128)(2,1)S(1)}, bf16[512,128]{1,0:T(8,128)(2,1)S(1)}, u32[]{:S(2)}, u32[]{:S(2)}) collective-permute-start(bf16[512,128]{1,0:T(8,128)(2,1)S(1)} %pad_maximum_fusion.5), channel_id=1, source_target_pairs={{4,1},{1,4},{6,3},{3,6},{12,9},{9,12},{14,11},{11,14},{20,17},{17,... | collective-permute-start | bytes 393224 | tf_op jit(solution)/shard_map/ppermute | solution.py:185
  105.5 3.4 %collective-permute-start.19 = (bf16[512,384]{1,0:T(8,128)(2,1)S(1)}, bf16[512,384]{1,0:T(8,128)(2,1)S(1)}, u32[]{:S(2)}, u32[]{:S(2)}) collective-permute-start(bf16[512,384]{1,0:T(8,128)(2,1)S(1)} %pad_maximum_fusion.2), channel_id=1, source_target_pairs={{4,1},{1,4},{6,3},{3,6},{12,9},{9,12},{14,11},{11,14},{20,17},{17,... | collective-permute-start | bytes 1179656 | tf_op jit(solution)/shard_map/ppermute | solution.py:185
  109.0 3.4 %collective-permute-start.22 = (bf16[512,1024]{1,0:T(8,128)(2,1)S(1)}, bf16[512,1024]{1,0:T(8,128)(2,1)S(1)}, u32[]{:S(2)}, u32[]{:S(2)}) collective-permute-start(bf16[512,1024]{1,0:T(8,128)(2,1)S(1)} %pad_maximum_fusion), channel_id=1, source_target_pairs={{4,1},{1,4},{6,3},{3,6},{12,9},{9,12},{14,11},{11,14},{20,17},{17,... | collective-permute-start | bytes 3145736 | tf_op jit(solution)/shard_map/ppermute | solution.py:185
  112.5 1.4 fusion.65
  113.9 3.5 %collective-permute-start.23 = (bf16[1536,128]{1,0:T(8,128)(2,1)S(1)}, bf16[1536,128]{1,0:T(8,128)(2,1)S(1)}, u32[]{:S(2)}, u32[]{:S(2)}) collective-permute-start(bf16[1536,128]{1,0:T(8,128)(2,1)S(1)} %fusion.65), channel_id=1, source_target_pairs={{0,8},{24,16},{1,9},{25,17},{2,10},{26,18},{3,11},{27,19},{4,12},{... | collective-permute-start | bytes 1179656 | tf_op jit(solution)/shard_map/ppermute | solution.py:52
  117.6 2.8 %collective-permute-done.19 = bf16[512,384]{1,0:T(8,128)(2,1)S(1)} collective-permute-done((bf16[512,384]{1,0:T(8,128)(2,1)S(1)}, bf16[512,384]{1,0:T(8,128)(2,1)S(1)}, u32[]{:S(2)}, u32[]{:S(2)}) %collective-permute-start.19) | collective-permute-done | bytes 393248 | tf_op jit(solution)/shard_map/ppermute | solution.py:185
  120.5 1.4 fusion.66
  121.9 3.3 %collective-permute-start.25 = (bf16[1536,128]{1,0:T(8,128)(2,1)S(1)}, bf16[1536,128]{1,0:T(8,128)(2,1)S(1)}, u32[]{:S(2)}, u32[]{:S(2)}) collective-permute-start(bf16[1536,128]{1,0:T(8,128)(2,1)S(1)} %fusion.66), channel_id=1, source_target_pairs={{0,8},{24,16},{1,9},{25,17},{2,10},{26,18},{3,11},{27,19},{4,12},{... | collective-permute-start | bytes 1179656 | tf_op jit(solution)/shard_map/ppermute | solution.py:52
  125.2 1.5 collective-permute-done.23
  127.6 2.2 fusion.30
  129.8 7.2 %collective-permute-start.28 = (bf16[1536,128]{1,0:T(8,128)(2,1)S(1)}, bf16[1536,128]{1,0:T(8,128)(2,1)S(1)}, u32[]{:S(2)}, u32[]{:S(2)}) collective-permute-start(bf16[1536,128]{1,0:T(8,128)(2,1)S(1)} %slice.505), channel_id=1, source_target_pairs={{0,8},{24,16},{1,9},{25,17},{2,10},{26,18},{3,11},{27,19},{4,12},{... | collective-permute-start | bytes 1179656 | tf_op jit(solution)/shard_map/ppermute | solution.py:52
  137.9 1.8 collective-permute-done.22
  140.1 3.6 %collective-permute-start.26 = (bf16[1536,128]{1,0:T(8,128)(2,1)S(1)}, bf16[1536,128]{1,0:T(8,128)(2,1)S(1)}, u32[]{:S(2)}, u32[]{:S(2)}) collective-permute-start(bf16[1536,128]{1,0:T(8,128)(2,1)S(1)} %fusion.91), channel_id=1, source_target_pairs={{0,8},{24,16},{8,0},{16,24},{1,9},{25,17},{9,1},{17,25},{2,10},{26... | collective-permute-start | bytes 1179656 | tf_op jit(solution)/shard_map/ppermute | solution.py:52
  143.7 2.3 collective-permute-done.28
  146.0 2.2 fusion.31
  149.3 3.9 %collective-permute-start.30 = (bf16[1536,128]{1,0:T(8,128)(2,1)S(1)}, bf16[1536,128]{1,0:T(8,128)(2,1)S(1)}, u32[]{:S(2)}, u32[]{:S(2)}) collective-permute-start(bf16[1536,128]{1,0:T(8,128)(2,1)S(1)} %fusion.92), channel_id=1, source_target_pairs={{0,8},{24,16},{8,0},{16,24},{1,9},{25,17},{9,1},{17,25},{2,10},{26... | collective-permute-start | bytes 1179656 | tf_op jit(solution)/shard_map/ppermute | solution.py:52
  153.3 2.2 fusion.32
  156.4 6.4 %collective-permute-start.32 = (bf16[1536,128]{1,0:T(8,128)(2,1)S(1)}, bf16[1536,128]{1,0:T(8,128)(2,1)S(1)}, u32[]{:S(2)}, u32[]{:S(2)}) collective-permute-start(bf16[1536,128]{1,0:T(8,128)(2,1)S(1)} %fusion.93), channel_id=1, source_target_pairs={{0,8},{24,16},{8,0},{16,24},{1,9},{25,17},{9,1},{17,25},{2,10},{26... | collective-permute-start | bytes 1179656 | tf_op jit(solution)/shard_map/ppermute | solution.py:52
  164.3 6.9 %collective-permute-start.34 = (bf16[1536,128]{1,0:T(8,128)(2,1)S(1)}, bf16[1536,128]{1,0:T(8,128)(2,1)S(1)}, u32[]{:S(2)}, u32[]{:S(2)}) collective-permute-start(bf16[1536,128]{1,0:T(8,128)(2,1)S(1)} %fusion.94), channel_id=1, source_target_pairs={{0,8},{24,16},{8,0},{16,24},{1,9},{25,17},{9,1},{17,25},{2,10},{26... | collective-permute-start | bytes 1179656 | tf_op jit(solution)/shard_map/ppermute | solution.py:52
  173.0 2.2 fusion.33
  175.8 4.1 %collective-permute-start.36 = (bf16[1536,128]{1,0:T(8,128)(2,1)S(1)}, bf16[1536,128]{1,0:T(8,128)(2,1)S(1)}, u32[]{:S(2)}, u32[]{:S(2)}) collective-permute-start(bf16[1536,128]{1,0:T(8,128)(2,1)S(1)} %fusion.95), channel_id=1, source_target_pairs={{0,8},{24,16},{8,0},{16,24},{1,9},{25,17},{9,1},{17,25},{2,10},{26... | collective-permute-start | bytes 1179656 | tf_op jit(solution)/shard_map/ppermute | solution.py:52
  181.7 7.0 %collective-permute-start.38 = (bf16[1536,128]{1,0:T(8,128)(2,1)S(1)}, bf16[1536,128]{1,0:T(8,128)(2,1)S(1)}, u32[]{:S(2)}, u32[]{:S(2)}) collective-permute-start(bf16[1536,128]{1,0:T(8,128)(2,1)S(1)} %fusion.96), channel_id=1, source_target_pairs={{0,8},{24,16},{8,0},{16,24},{1,9},{25,17},{9,1},{17,25},{2,10},{26... | collective-permute-start | bytes 1179656 | tf_op jit(solution)/shard_map/ppermute | solution.py:52
  188.7 2.2 fusion.34
  192.3 4.8 %collective-permute-start.40 = (bf16[1536,128]{1,0:T(8,128)(2,1)S(1)}, bf16[1536,128]{1,0:T(8,128)(2,1)S(1)}, u32[]{:S(2)}, u32[]{:S(2)}) collective-permute-start(bf16[1536,128]{1,0:T(8,128)(2,1)S(1)} %fusion.97), channel_id=1, source_target_pairs={{0,8},{24,16},{8,0},{16,24},{1,9},{25,17},{9,1},{17,25},{2,10},{26... | collective-permute-start | bytes 1179656 | tf_op jit(solution)/shard_map/ppermute | solution.py:52
  199.6 6.5 %collective-permute-start.42 = (bf16[1536,128]{1,0:T(8,128)(2,1)S(1)}, bf16[1536,128]{1,0:T(8,128)(2,1)S(1)}, u32[]{:S(2)}, u32[]{:S(2)}) collective-permute-start(bf16[1536,128]{1,0:T(8,128)(2,1)S(1)} %fusion.98), channel_id=1, source_target_pairs={{0,8},{24,16},{8,0},{16,24},{1,9},{25,17},{9,1},{17,25},{2,10},{26... | collective-permute-start | bytes 1179656 | tf_op jit(solution)/shard_map/ppermute | solution.py:52
  208.1 6.4 %collective-permute-start.44 = (bf16[1536,128]{1,0:T(8,128)(2,1)S(1)}, bf16[1536,128]{1,0:T(8,128)(2,1)S(1)}, u32[]{:S(2)}, u32[]{:S(2)}) collective-permute-start(bf16[1536,128]{1,0:T(8,128)(2,1)S(1)} %fusion.99), channel_id=1, source_target_pairs={{0,8},{24,16},{8,0},{16,24},{1,9},{25,17},{9,1},{17,25},{2,10},{26... | collective-permute-start | bytes 1179656 | tf_op jit(solution)/shard_map/ppermute | solution.py:52
  217.3 6.1 %collective-permute-done.44 = bf16[1536,128]{1,0:T(8,128)(2,1)S(1)} collective-permute-done((bf16[1536,128]{1,0:T(8,128)(2,1)S(1)}, bf16[1536,128]{1,0:T(8,128)(2,1)S(1)}, u32[]{:S(2)}, u32[]{:S(2)}) %collective-permute-start.44) | collective-permute-done | bytes 393248 | tf_op jit(solution)/shard_map/ppermute | solution.py:52
  226.5 5.3 %collective-permute-done.46 = bf16[1536,128]{1,0:T(8,128)(2,1)S(1)} collective-permute-done((bf16[1536,128]{1,0:T(8,128)(2,1)S(1)}, bf16[1536,128]{1,0:T(8,128)(2,1)S(1)}, u32[]{:S(2)}, u32[]{:S(2)}) %collective-permute-start.46) | collective-permute-done | bytes 393248 | tf_op jit(solution)/shard_map/ppermute | solution.py:52
  233.6 6.0 %collective-permute-done.48 = bf16[1536,128]{1,0:T(8,128)(2,1)S(1)} collective-permute-done((bf16[1536,128]{1,0:T(8,128)(2,1)S(1)}, bf16[1536,128]{1,0:T(8,128)(2,1)S(1)}, u32[]{:S(2)}, u32[]{:S(2)}) %collective-permute-start.48) | collective-permute-done | bytes 393248 | tf_op jit(solution)/shard_map/ppermute | solution.py:52
  240.2 3.7 %collective-permute-done.49 = bf16[1536,128]{1,0:T(8,128)(2,1)S(1)} collective-permute-done((bf16[1536,128]{1,0:T(8,128)(2,1)S(1)}, bf16[1536,128]{1,0:T(8,128)(2,1)S(1)}, u32[]{:S(2)}, u32[]{:S(2)}) %collective-permute-start.49) | collective-permute-done | bytes 393248 | tf_op jit(solution)/shard_map/ppermute | solution.py:52
  244.4 3.4 %copy-done.1 = f32[1536,1536]{1,0:T(8,128)} copy-done((f32[1536,1536]{1,0:T(8,128)}, f32[1536,1536]{1,0:T(8,128)S(1)}, u32[]{:S(2)}) %copy-start.1) | copy-done | bytes 9437208
  247.8 2.2 copy-done.2
  (189 shorter events, 45.7 us)
Async XLA Ops:
  0.6 19.6 %collective-permute-start = (bf16[256,1536]{1,0:T(8,128)(2,1)}, bf16[256,1536]{1,0:T(8,128)(2,1)S(1)}, u32[]{:S(2)}, u32[]{:S(2)}) collective-permute-start(bf16[256,1536]{1,0:T(8,128)(2,1)} %param.8), channel_id=1, source_target_pairs={{0,4},{2,6},{4,0},{6,2},{1,5},{3,7},{5,1},{7,3},{8,12},{10,14},{12... | collective-permute-start | bytes 2359304 | tf_op jit(solution)/shard_map/ppermute | solution.py:27
  4.7 15.5 %collective-permute-start.1 = (bf16[256,1536]{1,0:T(8,128)(2,1)}, bf16[256,1536]{1,0:T(8,128)(2,1)}, u32[]{:S(2)}, u32[]{:S(2)}) collective-permute-start(bf16[256,1536]{1,0:T(8,128)(2,1)} %get-tuple-element.318), channel_id=1, source_target_pairs={{0,2},{2,0},{4,6},{6,4},{1,3},{3,1},{5,7},{7,5},{8,10},{10,8},{12,... | collective-permute-start | bytes 2359304 | tf_op jit(solution)/shard_map/ppermute | solution.py:27
  5.7 14.5 %collective-permute-start.2 = (bf16[256,1536]{1,0:T(8,128)(2,1)}, bf16[256,1536]{1,0:T(8,128)(2,1)S(1)}, u32[]{:S(2)}, u32[]{:S(2)}) collective-permute-start(bf16[256,1536]{1,0:T(8,128)(2,1)} %get-tuple-element.316), channel_id=1, source_target_pairs={{0,2},{2,0},{4,6},{6,4},{1,3},{3,1},{5,7},{7,5},{8,10},{10,8},{12,... | collective-permute-start | bytes 2359304 | tf_op jit(solution)/shard_map/ppermute | solution.py:27
  6.2 18.9 %collective-permute-start.4 = (bf16[256,1536]{1,0:T(8,128)(2,1)}, bf16[256,1536]{1,0:T(8,128)(2,1)}, u32[]{:S(2)}, u32[]{:S(2)}) collective-permute-start(bf16[256,1536]{1,0:T(8,128)(2,1)} %param.8), channel_id=1, source_target_pairs={{0,2},{2,0},{4,6},{6,4},{1,3},{3,1},{5,7},{7,5},{8,10},{10,8},{12,... | collective-permute-start | bytes 2359304 | tf_op jit(solution)/shard_map/ppermute | solution.py:27
  20.2 32.8 %collective-permute-start.3 = (bf16[256,1536]{1,0:T(8,128)(2,1)S(1)}, bf16[256,1536]{1,0:T(8,128)(2,1)S(1)}, u32[]{:S(2)}, u32[]{:S(2)}) collective-permute-start(bf16[256,1536]{1,0:T(8,128)(2,1)S(1)} %collective-permute-done), channel_id=1, source_target_pairs={{0,2},{2,0},{4,6},{6,4},{1,3},{3,1},{5,7},{7,5},{8,10},{10,8},{12,... | collective-permute-start | bytes 2359304 | tf_op jit(solution)/shard_map/ppermute | solution.py:27
  28.4 36.7 %collective-permute-start.7 = (bf16[256,1536]{1,0:T(8,128)(2,1)S(1)}, bf16[256,1536]{1,0:T(8,128)(2,1)S(1)}, u32[]{:S(2)}, u32[]{:S(2)}) collective-permute-start(bf16[256,1536]{1,0:T(8,128)(2,1)S(1)} %slice.472), channel_id=1, source_target_pairs={{4,5},{1,0},{6,7},{3,2},{12,13},{9,8},{14,15},{11,10},{20,21},{17,... | collective-permute-start | bytes 2359304 | tf_op jit(solution)/shard_map/ppermute | solution.py:126
  30.6 21.0 %collective-permute-start.6 = (bf16[128,1536]{1,0:T(8,128)(2,1)S(1)}, bf16[128,1536]{1,0:T(8,128)(2,1)S(1)}, u32[]{:S(2)}, u32[]{:S(2)}) collective-permute-start(bf16[128,1536]{1,0:T(8,128)(2,1)S(1)} %slice.475), channel_id=1, source_target_pairs={{0,4},{2,6},{4,0},{6,2},{1,5},{3,7},{5,1},{7,3},{8,12},{10,14},{12... | collective-permute-start | bytes 1179656 | tf_op jit(solution)/shard_map/ppermute | solution.py:27
  31.3 19.1 %collective-permute-start.5 = (bf16[128,1536]{1,0:T(8,128)(2,1)S(1)}, bf16[128,1536]{1,0:T(8,128)(2,1)S(1)}, u32[]{:S(2)}, u32[]{:S(2)}) collective-permute-start(bf16[128,1536]{1,0:T(8,128)(2,1)S(1)} %slice.474), channel_id=1, source_target_pairs={{0,4},{2,6},{4,0},{6,2},{1,5},{3,7},{5,1},{7,3},{8,12},{10,14},{12... | collective-permute-start | bytes 1179656 | tf_op jit(solution)/shard_map/ppermute | solution.py:27
  32.7 45.5 %collective-permute-start.12 = (bf16[256,1536]{1,0:T(8,128)(2,1)S(1)}, bf16[256,1536]{1,0:T(8,128)(2,1)S(1)}, u32[]{:S(2)}, u32[]{:S(2)}) collective-permute-start(bf16[256,1536]{1,0:T(8,128)(2,1)S(1)} %slice.473), channel_id=1, source_target_pairs={{4,5},{1,0},{6,7},{3,2},{12,13},{9,8},{14,15},{11,10},{20,21},{17,... | collective-permute-start | bytes 2359304 | tf_op jit(solution)/shard_map/ppermute | solution.py:126
  50.4 13.9 %collective-permute-start.8 = (bf16[128,1536]{1,0:T(8,128)(2,1)S(1)}, bf16[128,1536]{1,0:T(8,128)(2,1)S(1)}, u32[]{:S(2)}, u32[]{:S(2)}) collective-permute-start(bf16[128,1536]{1,0:T(8,128)(2,1)S(1)} %collective-permute-done.5), channel_id=1, source_target_pairs={{0,1},{5,4},{2,3},{7,6},{8,9},{13,12},{10,11},{15,14},{16,17},{21,... | collective-permute-start | bytes 1179656 | tf_op jit(solution)/shard_map/ppermute | solution.py:123
  51.7 19.4 %collective-permute-start.10 = (bf16[128,1536]{1,0:T(8,128)(2,1)S(1)}, bf16[128,1536]{1,0:T(8,128)(2,1)S(1)}, u32[]{:S(2)}, u32[]{:S(2)}) collective-permute-start(bf16[128,1536]{1,0:T(8,128)(2,1)S(1)} %collective-permute-done.6), channel_id=1, source_target_pairs={{0,1},{5,4},{2,3},{7,6},{8,9},{13,12},{10,11},{15,14},{16,17},{21,... | collective-permute-start | bytes 1179656 | tf_op jit(solution)/shard_map/ppermute | solution.py:123
  53.8 23.2 %collective-permute-start.11 = (bf16[128,1536]{1,0:T(8,128)(2,1)S(1)}, bf16[128,1536]{1,0:T(8,128)(2,1)S(1)}, u32[]{:S(2)}, u32[]{:S(2)}) collective-permute-start(bf16[128,1536]{1,0:T(8,128)(2,1)S(1)} %convolution_convert_fusion.2), channel_id=1, source_target_pairs={{0,4},{2,6},{4,0},{6,2},{1,5},{3,7},{5,1},{7,3},{8,12},{10,14},{12... | collective-permute-start | bytes 1179656 | tf_op jit(solution)/shard_map/ppermute | solution.py:27
  64.3 10.2 %collective-permute-start.9 = (bf16[128,1536]{1,0:T(8,128)(2,1)S(1)}, bf16[128,1536]{1,0:T(8,128)(2,1)S(1)}, u32[]{:S(2)}, u32[]{:S(2)}) collective-permute-start(bf16[128,1536]{1,0:T(8,128)(2,1)S(1)} %convolution_convert_fusion.3), channel_id=1, source_target_pairs={{0,4},{2,6},{4,0},{6,2},{1,5},{3,7},{5,1},{7,3},{8,12},{10,14},{12... | collective-permute-start | bytes 1179656 | tf_op jit(solution)/shard_map/ppermute | solution.py:27
  74.5 13.9 %collective-permute-start.13 = (bf16[128,1536]{1,0:T(8,128)(2,1)S(1)}, bf16[128,1536]{1,0:T(8,128)(2,1)S(1)}, u32[]{:S(2)}, u32[]{:S(2)}) collective-permute-start(bf16[128,1536]{1,0:T(8,128)(2,1)S(1)} %collective-permute-done.9), channel_id=1, source_target_pairs={{0,1},{5,4},{2,3},{7,6},{8,9},{13,12},{10,11},{15,14},{16,17},{21,... | collective-permute-start | bytes 1179656 | tf_op jit(solution)/shard_map/ppermute | solution.py:123
  77.0 17.2 %collective-permute-start.14 = (bf16[128,1536]{1,0:T(8,128)(2,1)S(1)}, bf16[128,1536]{1,0:T(8,128)(2,1)S(1)}, u32[]{:S(2)}, u32[]{:S(2)}) collective-permute-start(bf16[128,1536]{1,0:T(8,128)(2,1)S(1)} %collective-permute-done.11), channel_id=1, source_target_pairs={{0,1},{5,4},{2,3},{7,6},{8,9},{13,12},{10,11},{15,14},{16,17},{21,... | collective-permute-start | bytes 1179656 | tf_op jit(solution)/shard_map/ppermute | solution.py:123
  100.5 5.0 %collective-permute-start.17 = (bf16[512,128]{1,0:T(8,128)(2,1)S(1)}, bf16[512,128]{1,0:T(8,128)(2,1)S(1)}, u32[]{:S(2)}, u32[]{:S(2)}) collective-permute-start(bf16[512,128]{1,0:T(8,128)(2,1)S(1)} %pad_maximum_fusion.5), channel_id=1, source_target_pairs={{0,1},{5,4},{4,0},{1,5},{2,3},{7,6},{6,2},{3,7},{8,9},{13,12},{12,... | collective-permute-start | bytes 393224 | tf_op jit(solution)/shard_map/ppermute | solution.py:184
  100.6 8.3 %collective-permute-start.20 = (bf16[512,128]{1,0:T(8,128)(2,1)S(1)}, bf16[512,128]{1,0:T(8,128)(2,1)S(1)}, u32[]{:S(2)}, u32[]{:S(2)}) collective-permute-start(bf16[512,128]{1,0:T(8,128)(2,1)S(1)} %pad_maximum_fusion.5), channel_id=1, source_target_pairs={{4,1},{1,4},{6,3},{3,6},{12,9},{9,12},{14,11},{11,14},{20,17},{17,... | collective-permute-start | bytes 393224 | tf_op jit(solution)/shard_map/ppermute | solution.py:185
  105.5 12.1 %collective-permute-start.18 = (bf16[512,384]{1,0:T(8,128)(2,1)S(1)}, bf16[512,384]{1,0:T(8,128)(2,1)S(1)}, u32[]{:S(2)}, u32[]{:S(2)}) collective-permute-start(bf16[512,384]{1,0:T(8,128)(2,1)S(1)} %pad_maximum_fusion.2), channel_id=1, source_target_pairs={{0,1},{5,4},{4,0},{1,5},{2,3},{7,6},{6,2},{3,7},{8,9},{13,12},{12,... | collective-permute-start | bytes 1179656 | tf_op jit(solution)/shard_map/ppermute | solution.py:184
  105.5 14.8 %collective-permute-start.19 = (bf16[512,384]{1,0:T(8,128)(2,1)S(1)}, bf16[512,384]{1,0:T(8,128)(2,1)S(1)}, u32[]{:S(2)}, u32[]{:S(2)}) collective-permute-start(bf16[512,384]{1,0:T(8,128)(2,1)S(1)} %pad_maximum_fusion.2), channel_id=1, source_target_pairs={{4,1},{1,4},{6,3},{3,6},{12,9},{9,12},{14,11},{11,14},{20,17},{17,... | collective-permute-start | bytes 1179656 | tf_op jit(solution)/shard_map/ppermute | solution.py:185
  108.9 29.0 %collective-permute-start.21 = (bf16[512,1024]{1,0:T(8,128)(2,1)S(1)}, bf16[512,1024]{1,0:T(8,128)(2,1)S(1)}, u32[]{:S(2)}, u32[]{:S(2)}) collective-permute-start(bf16[512,1024]{1,0:T(8,128)(2,1)S(1)} %pad_maximum_fusion), channel_id=1, source_target_pairs={{0,1},{5,4},{4,0},{1,5},{2,3},{7,6},{6,2},{3,7},{8,9},{13,12},{12,... | collective-permute-start | bytes 3145736 | tf_op jit(solution)/shard_map/ppermute | solution.py:184
  109.0 30.7 %collective-permute-start.22 = (bf16[512,1024]{1,0:T(8,128)(2,1)S(1)}, bf16[512,1024]{1,0:T(8,128)(2,1)S(1)}, u32[]{:S(2)}, u32[]{:S(2)}) collective-permute-start(bf16[512,1024]{1,0:T(8,128)(2,1)S(1)} %pad_maximum_fusion), channel_id=1, source_target_pairs={{4,1},{1,4},{6,3},{3,6},{12,9},{9,12},{14,11},{11,14},{20,17},{17,... | collective-permute-start | bytes 3145736 | tf_op jit(solution)/shard_map/ppermute | solution.py:185
  113.9 12.8 %collective-permute-start.23 = (bf16[1536,128]{1,0:T(8,128)(2,1)S(1)}, bf16[1536,128]{1,0:T(8,128)(2,1)S(1)}, u32[]{:S(2)}, u32[]{:S(2)}) collective-permute-start(bf16[1536,128]{1,0:T(8,128)(2,1)S(1)} %fusion.65), channel_id=1, source_target_pairs={{0,8},{24,16},{1,9},{25,17},{2,10},{26,18},{3,11},{27,19},{4,12},{... | collective-permute-start | bytes 1179656 | tf_op jit(solution)/shard_map/ppermute | solution.py:52
  121.9 15.1 %collective-permute-start.25 = (bf16[1536,128]{1,0:T(8,128)(2,1)S(1)}, bf16[1536,128]{1,0:T(8,128)(2,1)S(1)}, u32[]{:S(2)}, u32[]{:S(2)}) collective-permute-start(bf16[1536,128]{1,0:T(8,128)(2,1)S(1)} %fusion.66), channel_id=1, source_target_pairs={{0,8},{24,16},{1,9},{25,17},{2,10},{26,18},{3,11},{27,19},{4,12},{... | collective-permute-start | bytes 1179656 | tf_op jit(solution)/shard_map/ppermute | solution.py:52
  126.9 11.0 %collective-permute-start.24 = (bf16[1536,128]{1,0:T(8,128)(2,1)S(1)}, bf16[1536,128]{1,0:T(8,128)(2,1)S(1)}, u32[]{:S(2)}, u32[]{:S(2)}) collective-permute-start(bf16[1536,128]{1,0:T(8,128)(2,1)S(1)} %add_convert_fusion.35), channel_id=1, source_target_pairs={{8,16},{16,8},{9,17},{17,9},{10,18},{18,10},{11,19},{19,11},{12,20... | collective-permute-start | bytes 1179656 | tf_op jit(solution)/shard_map/ppermute | solution.py:60
  129.8 16.2 %collective-permute-start.28 = (bf16[1536,128]{1,0:T(8,128)(2,1)S(1)}, bf16[1536,128]{1,0:T(8,128)(2,1)S(1)}, u32[]{:S(2)}, u32[]{:S(2)}) collective-permute-start(bf16[1536,128]{1,0:T(8,128)(2,1)S(1)} %slice.505), channel_id=1, source_target_pairs={{0,8},{24,16},{1,9},{25,17},{2,10},{26,18},{3,11},{27,19},{4,12},{... | collective-permute-start | bytes 1179656 | tf_op jit(solution)/shard_map/ppermute | solution.py:52
  137.1 12.0 %collective-permute-start.27 = (bf16[1536,128]{1,0:T(8,128)(2,1)S(1)}, bf16[1536,128]{1,0:T(8,128)(2,1)S(1)}, u32[]{:S(2)}, u32[]{:S(2)}) collective-permute-start(bf16[1536,128]{1,0:T(8,128)(2,1)S(1)} %add_convert_fusion.34), channel_id=1, source_target_pairs={{8,16},{16,8},{9,17},{17,9},{10,18},{18,10},{11,19},{19,11},{12,20... | collective-permute-start | bytes 1179656 | tf_op jit(solution)/shard_map/ppermute | solution.py:60
  140.1 15.3 %collective-permute-start.26 = (bf16[1536,128]{1,0:T(8,128)(2,1)S(1)}, bf16[1536,128]{1,0:T(8,128)(2,1)S(1)}, u32[]{:S(2)}, u32[]{:S(2)}) collective-permute-start(bf16[1536,128]{1,0:T(8,128)(2,1)S(1)} %fusion.91), channel_id=1, source_target_pairs={{0,8},{24,16},{8,0},{16,24},{1,9},{25,17},{9,1},{17,25},{2,10},{26... | collective-permute-start | bytes 1179656 | tf_op jit(solution)/shard_map/ppermute | solution.py:52
  148.3 8.0 %collective-permute-start.29 = (bf16[1536,128]{1,0:T(8,128)(2,1)S(1)}, bf16[1536,128]{1,0:T(8,128)(2,1)S(1)}, u32[]{:S(2)}, u32[]{:S(2)}) collective-permute-start(bf16[1536,128]{1,0:T(8,128)(2,1)S(1)} %add_convert_fusion.32), channel_id=1, source_target_pairs={{8,16},{16,8},{9,17},{17,9},{10,18},{18,10},{11,19},{19,11},{12,20... | collective-permute-start | bytes 1179656 | tf_op jit(solution)/shard_map/ppermute | solution.py:60
  149.3 13.9 %collective-permute-start.30 = (bf16[1536,128]{1,0:T(8,128)(2,1)S(1)}, bf16[1536,128]{1,0:T(8,128)(2,1)S(1)}, u32[]{:S(2)}, u32[]{:S(2)}) collective-permute-start(bf16[1536,128]{1,0:T(8,128)(2,1)S(1)} %fusion.92), channel_id=1, source_target_pairs={{0,8},{24,16},{8,0},{16,24},{1,9},{25,17},{9,1},{17,25},{2,10},{26... | collective-permute-start | bytes 1179656 | tf_op jit(solution)/shard_map/ppermute | solution.py:52
  155.6 8.5 %collective-permute-start.31 = (bf16[1536,128]{1,0:T(8,128)(2,1)S(1)}, bf16[1536,128]{1,0:T(8,128)(2,1)S(1)}, u32[]{:S(2)}, u32[]{:S(2)}) collective-permute-start(bf16[1536,128]{1,0:T(8,128)(2,1)S(1)} %add_convert_fusion.30), channel_id=1, source_target_pairs={{8,16},{16,8},{9,17},{17,9},{10,18},{18,10},{11,19},{19,11},{12,20... | collective-permute-start | bytes 1179656 | tf_op jit(solution)/shard_map/ppermute | solution.py:60
  156.4 15.5 %collective-permute-start.32 = (bf16[1536,128]{1,0:T(8,128)(2,1)S(1)}, bf16[1536,128]{1,0:T(8,128)(2,1)S(1)}, u32[]{:S(2)}, u32[]{:S(2)}) collective-permute-start(bf16[1536,128]{1,0:T(8,128)(2,1)S(1)} %fusion.93), channel_id=1, source_target_pairs={{0,8},{24,16},{8,0},{16,24},{1,9},{25,17},{9,1},{17,25},{2,10},{26... | collective-permute-start | bytes 1179656 | tf_op jit(solution)/shard_map/ppermute | solution.py:52
  163.4 12.2 %collective-permute-start.33 = (bf16[1536,128]{1,0:T(8,128)(2,1)S(1)}, bf16[1536,128]{1,0:T(8,128)(2,1)S(1)}, u32[]{:S(2)}, u32[]{:S(2)}) collective-permute-start(bf16[1536,128]{1,0:T(8,128)(2,1)S(1)} %add_convert_fusion.28), channel_id=1, source_target_pairs={{8,16},{16,8},{9,17},{17,9},{10,18},{18,10},{11,19},{19,11},{12,20... | collective-permute-start | bytes 1179656 | tf_op jit(solution)/shard_map/ppermute | solution.py:60
  164.3 16.4 %collective-permute-start.34 = (bf16[1536,128]{1,0:T(8,128)(2,1)S(1)}, bf16[1536,128]{1,0:T(8,128)(2,1)S(1)}, u32[]{:S(2)}, u32[]{:S(2)}) collective-permute-start(bf16[1536,128]{1,0:T(8,128)(2,1)S(1)} %fusion.94), channel_id=1, source_target_pairs={{0,8},{24,16},{8,0},{16,24},{1,9},{25,17},{9,1},{17,25},{2,10},{26... | collective-permute-start | bytes 1179656 | tf_op jit(solution)/shard_map/ppermute | solution.py:52
  172.0 9.5 %collective-permute-start.35 = (bf16[1536,128]{1,0:T(8,128)(2,1)S(1)}, bf16[1536,128]{1,0:T(8,128)(2,1)S(1)}, u32[]{:S(2)}, u32[]{:S(2)}) collective-permute-start(bf16[1536,128]{1,0:T(8,128)(2,1)S(1)} %add_convert_fusion.26), channel_id=1, source_target_pairs={{8,16},{16,8},{9,17},{17,9},{10,18},{18,10},{11,19},{19,11},{12,20... | collective-permute-start | bytes 1179656 | tf_op jit(solution)/shard_map/ppermute | solution.py:60
  175.8 15.5 %collective-permute-start.36 = (bf16[1536,128]{1,0:T(8,128)(2,1)S(1)}, bf16[1536,128]{1,0:T(8,128)(2,1)S(1)}, u32[]{:S(2)}, u32[]{:S(2)}) collective-permute-start(bf16[1536,128]{1,0:T(8,128)(2,1)S(1)} %fusion.95), channel_id=1, source_target_pairs={{0,8},{24,16},{8,0},{16,24},{1,9},{25,17},{9,1},{17,25},{2,10},{26... | collective-permute-start | bytes 1179656 | tf_op jit(solution)/shard_map/ppermute | solution.py:52
  180.8 11.3 %collective-permute-start.37 = (bf16[1536,128]{1,0:T(8,128)(2,1)S(1)}, bf16[1536,128]{1,0:T(8,128)(2,1)S(1)}, u32[]{:S(2)}, u32[]{:S(2)}) collective-permute-start(bf16[1536,128]{1,0:T(8,128)(2,1)S(1)} %add_convert_fusion.24), channel_id=1, source_target_pairs={{8,16},{16,8},{9,17},{17,9},{10,18},{18,10},{11,19},{19,11},{12,20... | collective-permute-start | bytes 1179656 | tf_op jit(solution)/shard_map/ppermute | solution.py:60
  181.7 16.4 %collective-permute-start.38 = (bf16[1536,128]{1,0:T(8,128)(2,1)S(1)}, bf16[1536,128]{1,0:T(8,128)(2,1)S(1)}, u32[]{:S(2)}, u32[]{:S(2)}) collective-permute-start(bf16[1536,128]{1,0:T(8,128)(2,1)S(1)} %fusion.96), channel_id=1, source_target_pairs={{0,8},{24,16},{8,0},{16,24},{1,9},{25,17},{9,1},{17,25},{2,10},{26... | collective-permute-start | bytes 1179656 | tf_op jit(solution)/shard_map/ppermute | solution.py:52
  191.5 7.9 %collective-permute-start.39 = (bf16[1536,128]{1,0:T(8,128)(2,1)S(1)}, bf16[1536,128]{1,0:T(8,128)(2,1)S(1)}, u32[]{:S(2)}, u32[]{:S(2)}) collective-permute-start(bf16[1536,128]{1,0:T(8,128)(2,1)S(1)} %add_convert_fusion.22), channel_id=1, source_target_pairs={{8,16},{16,8},{9,17},{17,9},{10,18},{18,10},{11,19},{19,11},{12,20... | collective-permute-start | bytes 1179656 | tf_op jit(solution)/shard_map/ppermute | solution.py:60
  192.3 14.8 %collective-permute-start.40 = (bf16[1536,128]{1,0:T(8,128)(2,1)S(1)}, bf16[1536,128]{1,0:T(8,128)(2,1)S(1)}, u32[]{:S(2)}, u32[]{:S(2)}) collective-permute-start(bf16[1536,128]{1,0:T(8,128)(2,1)S(1)} %fusion.97), channel_id=1, source_target_pairs={{0,8},{24,16},{8,0},{16,24},{1,9},{25,17},{9,1},{17,25},{2,10},{26... | collective-permute-start | bytes 1179656 | tf_op jit(solution)/shard_map/ppermute | solution.py:52
  198.2 9.7 %collective-permute-start.41 = (bf16[1536,128]{1,0:T(8,128)(2,1)S(1)}, bf16[1536,128]{1,0:T(8,128)(2,1)S(1)}, u32[]{:S(2)}, u32[]{:S(2)}) collective-permute-start(bf16[1536,128]{1,0:T(8,128)(2,1)S(1)} %add_convert_fusion.20), channel_id=1, source_target_pairs={{8,16},{16,8},{9,17},{17,9},{10,18},{18,10},{11,19},{19,11},{12,20... | collective-permute-start | bytes 1179656 | tf_op jit(solution)/shard_map/ppermute | solution.py:60
  199.6 15.4 %collective-permute-start.42 = (bf16[1536,128]{1,0:T(8,128)(2,1)S(1)}, bf16[1536,128]{1,0:T(8,128)(2,1)S(1)}, u32[]{:S(2)}, u32[]{:S(2)}) collective-permute-start(bf16[1536,128]{1,0:T(8,128)(2,1)S(1)} %fusion.98), channel_id=1, source_target_pairs={{0,8},{24,16},{8,0},{16,24},{1,9},{25,17},{9,1},{17,25},{2,10},{26... | collective-permute-start | bytes 1179656 | tf_op jit(solution)/shard_map/ppermute | solution.py:52
  207.3 8.6 %collective-permute-start.43 = (bf16[1536,128]{1,0:T(8,128)(2,1)S(1)}, bf16[1536,128]{1,0:T(8,128)(2,1)S(1)}, u32[]{:S(2)}, u32[]{:S(2)}) collective-permute-start(bf16[1536,128]{1,0:T(8,128)(2,1)S(1)} %add_convert_fusion.18), channel_id=1, source_target_pairs={{8,16},{16,8},{9,17},{17,9},{10,18},{18,10},{11,19},{19,11},{12,20... | collective-permute-start | bytes 1179656 | tf_op jit(solution)/shard_map/ppermute | solution.py:60
  208.1 15.2 %collective-permute-start.44 = (bf16[1536,128]{1,0:T(8,128)(2,1)S(1)}, bf16[1536,128]{1,0:T(8,128)(2,1)S(1)}, u32[]{:S(2)}, u32[]{:S(2)}) collective-permute-start(bf16[1536,128]{1,0:T(8,128)(2,1)S(1)} %fusion.99), channel_id=1, source_target_pairs={{0,8},{24,16},{8,0},{16,24},{1,9},{25,17},{9,1},{17,25},{2,10},{26... | collective-permute-start | bytes 1179656 | tf_op jit(solution)/shard_map/ppermute | solution.py:52
  215.1 9.5 %collective-permute-start.45 = (bf16[1536,128]{1,0:T(8,128)(2,1)S(1)}, bf16[1536,128]{1,0:T(8,128)(2,1)S(1)}, u32[]{:S(2)}, u32[]{:S(2)}) collective-permute-start(bf16[1536,128]{1,0:T(8,128)(2,1)S(1)} %add_convert_fusion.16), channel_id=1, source_target_pairs={{8,16},{16,8},{9,17},{17,9},{10,18},{18,10},{11,19},{19,11},{12,20... | collective-permute-start | bytes 1179656 | tf_op jit(solution)/shard_map/ppermute | solution.py:60
  216.0 15.8 %collective-permute-start.46 = (bf16[1536,128]{1,0:T(8,128)(2,1)S(1)}, bf16[1536,128]{1,0:T(8,128)(2,1)S(1)}, u32[]{:S(2)}, u32[]{:S(2)}) collective-permute-start(bf16[1536,128]{1,0:T(8,128)(2,1)S(1)} %add_convert_fusion.15), channel_id=1, source_target_pairs={{8,0},{16,24},{9,1},{17,25},{10,2},{18,26},{11,3},{19,27},{12,4},{... | collective-permute-start | bytes 1179656 | tf_op jit(solution)/shard_map/ppermute | solution.py:52
  223.4 8.3 %collective-permute-start.47 = (bf16[1536,128]{1,0:T(8,128)(2,1)S(1)}, bf16[1536,128]{1,0:T(8,128)(2,1)S(1)}, u32[]{:S(2)}, u32[]{:S(2)}) collective-permute-start(bf16[1536,128]{1,0:T(8,128)(2,1)S(1)} %add_convert_fusion.14), channel_id=1, source_target_pairs={{8,16},{16,8},{9,17},{17,9},{10,18},{18,10},{11,19},{19,11},{12,20... | collective-permute-start | bytes 1179656 | tf_op jit(solution)/shard_map/ppermute | solution.py:60
  224.7 15.0 %collective-permute-start.48 = (bf16[1536,128]{1,0:T(8,128)(2,1)S(1)}, bf16[1536,128]{1,0:T(8,128)(2,1)S(1)}, u32[]{:S(2)}, u32[]{:S(2)}) collective-permute-start(bf16[1536,128]{1,0:T(8,128)(2,1)S(1)} %add_convert_fusion.13), channel_id=1, source_target_pairs={{8,0},{16,24},{9,1},{17,25},{10,2},{18,26},{11,3},{19,27},{12,4},{... | collective-permute-start | bytes 1179656 | tf_op jit(solution)/shard_map/ppermute | solution.py:52
  231.9 12.0 %collective-permute-start.49 = (bf16[1536,128]{1,0:T(8,128)(2,1)S(1)}, bf16[1536,128]{1,0:T(8,128)(2,1)S(1)}, u32[]{:S(2)}, u32[]{:S(2)}) collective-permute-start(bf16[1536,128]{1,0:T(8,128)(2,1)S(1)} %add_convert_fusion.12), channel_id=1, source_target_pairs={{8,0},{16,24},{9,1},{17,25},{10,2},{18,26},{11,3},{19,27},{12,4},{... | collective-permute-start | bytes 1179656 | tf_op jit(solution)/shard_map/ppermute | solution.py:52
  (14 other events, 125.4 us)

commit v12 on v10

--- a/solution.py
+++ b/solution.py
@@ -109,16 +109,12 @@
     held = together(swap(context, "fsdp", group), *moved[0], *moved[1])
     residual_parts, cotangent_parts = held[1 : 1 + group], held[1 + group :]
     far_blocks = [held[0]] + [swap(held[0], "fsdp", r) for r in range(1, group)]
+    near_out = project(jnp.concatenate(near_blocks, axis=0))
+    near_came = lax.ppermute(near_out, ("fsdp", "tp"), inward_pairs)
     far_outs = []
-    for k in range(group * pieces):
-        r, p = k // pieces, k % pieces
-        blocks = [far_blocks[r][p * rows : (p + 1) * rows]]
-        if k == group * pieces - 1:
-            blocks += near_blocks
-        out = project(jnp.concatenate(blocks, axis=0))
-        far_outs.append(swap(out[:rows], "fsdp", group))
-    near_out = out[rows:]
-    near_came = lax.ppermute(near_out, ("fsdp", "tp"), inward_pairs)
+    for r in range(group):
+        out = project(far_blocks[r])
+        far_outs += [swap(out[p * rows : (p + 1) * rows], "fsdp", group) for p in range(pieces)]
     passed = [lax.ppermute(out, ("fsdp", "tp"), outward_pairs) for out in far_outs]
 
     gain_part = lax.dynamic_slice_in_dim(gain, t * (width // 2) + low * cols, cols).astype(f32)

time: 245 us -> 246 us (level)
    unnamed x25 -> x26, other arithmetic: 5.13 us -> 4.96 us
    dot_general x4 -> x3, matrix products: 9.4 us -> 9.23 us  [project(): jnp.dot(block, weight, preferred_element_type=f32).astype(bf16)]
    unnamed x25 -> x27, local copies, waits for them, and re-layouts: 8.12 us -> 8.26 us
where the time goes in v12:
time: 246 us; the launch traced here: 245 us
  starting transfers between devices  101 us (41%)
  waiting for transfers between devices  89.2 us (36%)
  matrix products  25.4 us (10%)
  other arithmetic  15.2 us (6%)
  local copies, waits for them, and re-layouts  11.8 us (5%)
    ppermute x15, starting transfers between devices, send_outer(): self.edge[s] = lax.ppermute(payload, 'island', pairs)  67.8 us
    ppermute x11, waiting for transfers between devices, swap(): return lax.ppermute(value, axis, [(i, i ^ bit) for i in range(count)])  42.5 us
    ppermute x15, waiting for transfers between devices, send_outer(): self.edge[s] = lax.ppermute(payload, 'island', pairs)  26.8 us
    dot_general x7, matrix products, add_pseudo(): lax.dot_general(context_all, piece, (((0,), (0,)), ((), ())), preferred_e...  16.2 us
    ppermute x4, waiting for transfers between devices, body(): lax.ppermute(out, ('fsdp', 'tp'), outward_pairs)  14 us
    ppermute x3, starting transfers between devices, move(): crosses.append(lax.ppermute(d_local, ('fsdp', 'tp'), cross_pairs))  10.1 us
    dot_general x3, matrix products, project(): jnp.dot(block, weight, preferred_element_type=f32).astype(bf16)  9.23 us
    ppermute x12, starting transfers between devices, step(): self.mid[s] = lax.ppermute(self.sums[s], 'island', [(1, 2), (2, 1)])  8.45 us
  transfers between devices with their start and end apart: 49, of which 19 were waited for; matrix products, arithmetic and copies ran while one was open for 18% of the time, Pallas kernels for 0%

profile of v12, /device:TPU:2, one launch (start us, length us, event | category | flops | bytes accessed | tf_op | source)
XLA Modules:
  0.0 244.5 jit_solution(10883393773488639946)
XLA Ops:
  0.6 1.6 collective-permute-start
  2.2 2.4 constant_dynamic-slice_fusion.2
  8.0 12.3 %collective-permute-done = bf16[256,1536]{1,0:T(8,128)(2,1)} collective-permute-done((bf16[256,1536]{1,0:T(8,128)(2,1)}, bf16[256,1536]{1,0:T(8,128)(2,1)}, u32[]{:S(2)}, u32[]{:S(2)}) %collective-permute-start) | collective-permute-done | bytes 786464 | tf_op jit(solution)/shard_map/ppermute | solution.py:27
  20.4 4.1 %convolution_convert_fusion.2 = bf16[256,1536]{1,0:T(8,128)(2,1)S(1)} fusion(bf16[256,1536]{1,0:T(8,128)(2,1)} %collective-permute-done, bf16[1536,1536]{1,0:T(8,128)(2,1)} %param.12), kind=kOutput, calls=%fused_computation.8 | convolution fusion | flops 1208352768 | bytes 6291456 | tf_op jit(solution)/shard_map/dot_general | solution.py:89
  24.6 1.6 collective-permute-start.5
  26.7 3.8 %convolution_convert_fusion = bf16[512,1536]{1,0:T(8,128)(2,1)S(1)} fusion(bf16[1536,1536]{1,0:T(8,128)(2,1)S(1)} %bitcast.206, bf16[256,1536]{1,0:T(8,128)(2,1)S(1)} %collective-permute-done.3, bf16[256,1536]{1,0:T(8,128)(2,1)} %param.8), kind=kOutput, calls=%fused_computation | convolution fusion | flops 2419851264 | bytes 7864320 | tf_op jit(solution)/shard_map/dot_general | solution.py:89
  30.5 2.3 collective-permute-start.6
  33.3 11.2 %collective-permute-done.4 = bf16[128,1536]{1,0:T(8,128)(2,1)S(1)} collective-permute-done((bf16[128,1536]{1,0:T(8,128)(2,1)S(1)}, bf16[128,1536]{1,0:T(8,128)(2,1)S(1)}, u32[]{:S(2)}, u32[]{:S(2)}) %collective-permute-start.4) | collective-permute-done | bytes 393248 | tf_op jit(solution)/shard_map/ppermute | solution.py:27
  45.7 1.4 convolution_convert_fusion.1
  47.2 2.8 %collective-permute-start.11 = (bf16[128,1536]{1,0:T(8,128)(2,1)S(1)}, bf16[128,1536]{1,0:T(8,128)(2,1)S(1)}, u32[]{:S(2)}, u32[]{:S(2)}) collective-permute-start(bf16[128,1536]{1,0:T(8,128)(2,1)S(1)} %get-tuple-element.313), channel_id=1, source_target_pairs={{0,4},{2,6},{4,0},{6,2},{1,5},{3,7},{5,1},{7,3},{8,12},{10,14},{12... | collective-permute-start | bytes 1179656 | tf_op jit(solution)/shard_map/ppermute | solution.py:27
  51.5 15.4 %collective-permute-done.9 = bf16[128,1536]{1,0:T(8,128)(2,1)S(1)} collective-permute-done((bf16[128,1536]{1,0:T(8,128)(2,1)S(1)}, bf16[128,1536]{1,0:T(8,128)(2,1)S(1)}, u32[]{:S(2)}, u32[]{:S(2)}) %collective-permute-start.9) | collective-permute-done | bytes 393248 | tf_op jit(solution)/shard_map/ppermute | solution.py:27
  71.4 9.4 %collective-permute-done.12 = bf16[128,1536]{1,0:T(8,128)(2,1)S(1)} collective-permute-done((bf16[128,1536]{1,0:T(8,128)(2,1)S(1)}, bf16[128,1536]{1,0:T(8,128)(2,1)S(1)}, u32[]{:S(2)}, u32[]{:S(2)}) %collective-permute-start.12) | collective-permute-done | bytes 393248 | tf_op jit(solution)/shard_map/ppermute | solution.py:118
  82.3 4.6 %collective-permute-done.13 = bf16[128,1536]{1,0:T(8,128)(2,1)S(1)} collective-permute-done((bf16[128,1536]{1,0:T(8,128)(2,1)S(1)}, bf16[128,1536]{1,0:T(8,128)(2,1)S(1)}, u32[]{:S(2)}, u32[]{:S(2)}) %collective-permute-start.13) | collective-permute-done | bytes 393248 | tf_op jit(solution)/shard_map/ppermute | solution.py:118
  87.3 1.3 constant_dynamic-update-slice_fusion.1
  88.8 3.5 %collective-permute-done.15 = f32[2,512]{1,0:T(2,128)S(1)} collective-permute-done((f32[2,512]{1,0:T(2,128)S(1)}, f32[2,512]{1,0:T(2,128)S(1)}, u32[]{:S(2)}, u32[]{:S(2)}) %collective-permute-start.15) | collective-permute-done | bytes 4128 | tf_op jit(solution)/shard_map/ppermute | solution.py:27
  93.5 3.4 %collective-permute-start.19 = (bf16[512,128]{1,0:T(8,128)(2,1)S(1)}, bf16[512,128]{1,0:T(8,128)(2,1)S(1)}, u32[]{:S(2)}, u32[]{:S(2)}) collective-permute-start(bf16[512,128]{1,0:T(8,128)(2,1)S(1)} %pad_maximum_fusion.5), channel_id=1, source_target_pairs={{4,1},{1,4},{6,3},{3,6},{12,9},{9,12},{14,11},{11,14},{20,17},{17,... | collective-permute-start | bytes 393224 | tf_op jit(solution)/shard_map/ppermute | solution.py:177
  97.0 1.5 collective-permute-done.16
  98.5 3.4 %collective-permute-start.18 = (bf16[512,384]{1,0:T(8,128)(2,1)S(1)}, bf16[512,384]{1,0:T(8,128)(2,1)S(1)}, u32[]{:S(2)}, u32[]{:S(2)}) collective-permute-start(bf16[512,384]{1,0:T(8,128)(2,1)S(1)} %pad_maximum_fusion.2), channel_id=1, source_target_pairs={{4,1},{1,4},{6,3},{3,6},{12,9},{9,12},{14,11},{11,14},{20,17},{17,... | collective-permute-start | bytes 1179656 | tf_op jit(solution)/shard_map/ppermute | solution.py:177
  101.9 3.4 %collective-permute-start.21 = (bf16[512,1024]{1,0:T(8,128)(2,1)S(1)}, bf16[512,1024]{1,0:T(8,128)(2,1)S(1)}, u32[]{:S(2)}, u32[]{:S(2)}) collective-permute-start(bf16[512,1024]{1,0:T(8,128)(2,1)S(1)} %pad_maximum_fusion), channel_id=1, source_target_pairs={{4,1},{1,4},{6,3},{3,6},{12,9},{9,12},{14,11},{11,14},{20,17},{17,... | collective-permute-start | bytes 3145736 | tf_op jit(solution)/shard_map/ppermute | solution.py:177
  105.4 1.5 fusion.62
  106.9 3.7 %collective-permute-start.22 = (bf16[1536,128]{1,0:T(8,128)(2,1)S(1)}, bf16[1536,128]{1,0:T(8,128)(2,1)S(1)}, u32[]{:S(2)}, u32[]{:S(2)}) collective-permute-start(bf16[1536,128]{1,0:T(8,128)(2,1)S(1)} %fusion.62), channel_id=1, source_target_pairs={{0,8},{24,16},{1,9},{25,17},{2,10},{26,18},{3,11},{27,19},{4,12},{... | collective-permute-start | bytes 1179656 | tf_op jit(solution)/shard_map/ppermute | solution.py:52
  110.6 2.7 %collective-permute-done.18 = bf16[512,384]{1,0:T(8,128)(2,1)S(1)} collective-permute-done((bf16[512,384]{1,0:T(8,128)(2,1)S(1)}, bf16[512,384]{1,0:T(8,128)(2,1)S(1)}, u32[]{:S(2)}, u32[]{:S(2)}) %collective-permute-start.18) | collective-permute-done | bytes 393248 | tf_op jit(solution)/shard_map/ppermute | solution.py:177
  113.5 1.5 fusion.63
  114.9 3.5 %collective-permute-start.24 = (bf16[1536,128]{1,0:T(8,128)(2,1)S(1)}, bf16[1536,128]{1,0:T(8,128)(2,1)S(1)}, u32[]{:S(2)}, u32[]{:S(2)}) collective-permute-start(bf16[1536,128]{1,0:T(8,128)(2,1)S(1)} %fusion.63), channel_id=1, source_target_pairs={{0,8},{24,16},{1,9},{25,17},{2,10},{26,18},{3,11},{27,19},{4,12},{... | collective-permute-start | bytes 1179656 | tf_op jit(solution)/shard_map/ppermute | solution.py:52
  118.5 1.5 collective-permute-done.22
  120.8 2.2 fusion.33
  123.0 7.2 %collective-permute-start.27 = (bf16[1536,128]{1,0:T(8,128)(2,1)S(1)}, bf16[1536,128]{1,0:T(8,128)(2,1)S(1)}, u32[]{:S(2)}, u32[]{:S(2)}) collective-permute-start(bf16[1536,128]{1,0:T(8,128)(2,1)S(1)} %slice.493), channel_id=1, source_target_pairs={{0,8},{24,16},{1,9},{25,17},{2,10},{26,18},{3,11},{27,19},{4,12},{... | collective-permute-start | bytes 1179656 | tf_op jit(solution)/shard_map/ppermute | solution.py:52
  131.1 1.8 collective-permute-done.21
  133.4 3.0 %collective-permute-start.25 = (bf16[1536,128]{1,0:T(8,128)(2,1)S(1)}, bf16[1536,128]{1,0:T(8,128)(2,1)S(1)}, u32[]{:S(2)}, u32[]{:S(2)}) collective-permute-start(bf16[1536,128]{1,0:T(8,128)(2,1)S(1)} %fusion.88), channel_id=1, source_target_pairs={{0,8},{24,16},{8,0},{16,24},{1,9},{25,17},{9,1},{17,25},{2,10},{26... | collective-permute-start | bytes 1179656 | tf_op jit(solution)/shard_map/ppermute | solution.py:52
  136.4 2.1 collective-permute-done.27
  138.6 2.2 fusion.34
  141.8 3.8 %collective-permute-start.29 = (bf16[1536,128]{1,0:T(8,128)(2,1)S(1)}, bf16[1536,128]{1,0:T(8,128)(2,1)S(1)}, u32[]{:S(2)}, u32[]{:S(2)}) collective-permute-start(bf16[1536,128]{1,0:T(8,128)(2,1)S(1)} %fusion.89), channel_id=1, source_target_pairs={{0,8},{24,16},{8,0},{16,24},{1,9},{25,17},{9,1},{17,25},{2,10},{26... | collective-permute-start | bytes 1179656 | tf_op jit(solution)/shard_map/ppermute | solution.py:52
  145.6 2.2 fusion.35
  148.8 7.9 %collective-permute-start.31 = (bf16[1536,128]{1,0:T(8,128)(2,1)S(1)}, bf16[1536,128]{1,0:T(8,128)(2,1)S(1)}, u32[]{:S(2)}, u32[]{:S(2)}) collective-permute-start(bf16[1536,128]{1,0:T(8,128)(2,1)S(1)} %fusion.90), channel_id=1, source_target_pairs={{0,8},{24,16},{8,0},{16,24},{1,9},{25,17},{9,1},{17,25},{2,10},{26... | collective-permute-start | bytes 1179656 | tf_op jit(solution)/shard_map/ppermute | solution.py:52
  158.1 7.0 %collective-permute-start.33 = (bf16[1536,128]{1,0:T(8,128)(2,1)S(1)}, bf16[1536,128]{1,0:T(8,128)(2,1)S(1)}, u32[]{:S(2)}, u32[]{:S(2)}) collective-permute-start(bf16[1536,128]{1,0:T(8,128)(2,1)S(1)} %fusion.91), channel_id=1, source_target_pairs={{0,8},{24,16},{8,0},{16,24},{1,9},{25,17},{9,1},{17,25},{2,10},{26... | collective-permute-start | bytes 1179656 | tf_op jit(solution)/shard_map/ppermute | solution.py:52
  166.3 3.3 %fusion.36 = bf16[1536,256]{1,0:T(8,128)(2,1)S(1)} fusion(bf16[1536,1536]{1,0:T(8,128)(2,1)S(1)} %bitcast.206, bf16[1,1536,1536]{2,1,0:T(8,128)(2,1)S(1)} %bitcast.208, bf16[1,1536,1536]{2,1,0:T(8,128)(2,1)} %param.13, bf16[1024,1536]{1,0:T(8,128)(2,1)S(1)} %constant_dynamic-update-slice_fusion, bf16[1024,256]{1,0:T(8,128)(2,1)S(1)} %get-tuple-element.222), kind=kOutput, calls=%fused_computation.55 | convolution fusion | flops 812384256 | bytes 6815744 | tf_op jit(solution)/shard_map/dot_general | solution.py:190
  170.3 3.9 %collective-permute-start.35 = (bf16[1536,128]{1,0:T(8,128)(2,1)S(1)}, bf16[1536,128]{1,0:T(8,128)(2,1)S(1)}, u32[]{:S(2)}, u32[]{:S(2)}) collective-permute-start(bf16[1536,128]{1,0:T(8,128)(2,1)S(1)} %fusion.92), channel_id=1, source_target_pairs={{0,8},{24,16},{8,0},{16,24},{1,9},{25,17},{9,1},{17,25},{2,10},{26... | collective-permute-start | bytes 1179656 | tf_op jit(solution)/shard_map/ppermute | solution.py:52
  175.9 6.0 %collective-permute-start.37 = (bf16[1536,128]{1,0:T(8,128)(2,1)S(1)}, bf16[1536,128]{1,0:T(8,128)(2,1)S(1)}, u32[]{:S(2)}, u32[]{:S(2)}) collective-permute-start(bf16[1536,128]{1,0:T(8,128)(2,1)S(1)} %fusion.93), channel_id=1, source_target_pairs={{0,8},{24,16},{8,0},{16,24},{1,9},{25,17},{9,1},{17,25},{2,10},{26... | collective-permute-start | bytes 1179656 | tf_op jit(solution)/shard_map/ppermute | solution.py:52
  181.9 3.3 %fusion.37 = bf16[1536,256]{1,0:T(8,128)(2,1)S(1)} fusion(bf16[1536,1536]{1,0:T(8,128)(2,1)S(1)} %bitcast.206, bf16[1,1536,1536]{2,1,0:T(8,128)(2,1)S(1)} %bitcast.208, bf16[1,1536,1536]{2,1,0:T(8,128)(2,1)} %param.13, bf16[1024,1536]{1,0:T(8,128)(2,1)S(1)} %constant_dynamic-update-slice_fusion, bf16[1024,256]{1,0:T(8,128)(2,1)S(1)} %get-tuple-element.242), kind=kOutput, calls=%fused_computation.56 | convolution fusion | flops 812384256 | bytes 6815744 | tf_op jit(solution)/shard_map/dot_general | solution.py:190
  186.6 4.2 %collective-permute-start.39 = (bf16[1536,128]{1,0:T(8,128)(2,1)S(1)}, bf16[1536,128]{1,0:T(8,128)(2,1)S(1)}, u32[]{:S(2)}, u32[]{:S(2)}) collective-permute-start(bf16[1536,128]{1,0:T(8,128)(2,1)S(1)} %fusion.94), channel_id=1, source_target_pairs={{0,8},{24,16},{8,0},{16,24},{1,9},{25,17},{9,1},{17,25},{2,10},{26... | collective-permute-start | bytes 1179656 | tf_op jit(solution)/shard_map/ppermute | solution.py:52
  193.0 7.0 %collective-permute-start.41 = (bf16[1536,128]{1,0:T(8,128)(2,1)S(1)}, bf16[1536,128]{1,0:T(8,128)(2,1)S(1)}, u32[]{:S(2)}, u32[]{:S(2)}) collective-permute-start(bf16[1536,128]{1,0:T(8,128)(2,1)S(1)} %fusion.95), channel_id=1, source_target_pairs={{0,8},{24,16},{8,0},{16,24},{1,9},{25,17},{9,1},{17,25},{2,10},{26... | collective-permute-start | bytes 1179656 | tf_op jit(solution)/shard_map/ppermute | solution.py:52
  201.6 6.8 %collective-permute-start.43 = (bf16[1536,128]{1,0:T(8,128)(2,1)S(1)}, bf16[1536,128]{1,0:T(8,128)(2,1)S(1)}, u32[]{:S(2)}, u32[]{:S(2)}) collective-permute-start(bf16[1536,128]{1,0:T(8,128)(2,1)S(1)} %fusion.96), channel_id=1, source_target_pairs={{0,8},{24,16},{8,0},{16,24},{1,9},{25,17},{9,1},{17,25},{2,10},{26... | collective-permute-start | bytes 1179656 | tf_op jit(solution)/shard_map/ppermute | solution.py:52
  211.1 6.2 %collective-permute-done.43 = bf16[1536,128]{1,0:T(8,128)(2,1)S(1)} collective-permute-done((bf16[1536,128]{1,0:T(8,128)(2,1)S(1)}, bf16[1536,128]{1,0:T(8,128)(2,1)S(1)}, u32[]{:S(2)}, u32[]{:S(2)}) %collective-permute-start.43) | collective-permute-done | bytes 393248 | tf_op jit(solution)/shard_map/ppermute | solution.py:52
  220.5 5.3 %collective-permute-done.45 = bf16[1536,128]{1,0:T(8,128)(2,1)S(1)} collective-permute-done((bf16[1536,128]{1,0:T(8,128)(2,1)S(1)}, bf16[1536,128]{1,0:T(8,128)(2,1)S(1)}, u32[]{:S(2)}, u32[]{:S(2)}) %collective-permute-start.45) | collective-permute-done | bytes 393248 | tf_op jit(solution)/shard_map/ppermute | solution.py:52
  227.7 6.5 %collective-permute-done.47 = bf16[1536,128]{1,0:T(8,128)(2,1)S(1)} collective-permute-done((bf16[1536,128]{1,0:T(8,128)(2,1)S(1)}, bf16[1536,128]{1,0:T(8,128)(2,1)S(1)}, u32[]{:S(2)}, u32[]{:S(2)}) %collective-permute-start.47) | collective-permute-done | bytes 393248 | tf_op jit(solution)/shard_map/ppermute | solution.py:52
  234.7 3.7 %collective-permute-done.48 = bf16[1536,128]{1,0:T(8,128)(2,1)S(1)} collective-permute-done((bf16[1536,128]{1,0:T(8,128)(2,1)S(1)}, bf16[1536,128]{1,0:T(8,128)(2,1)S(1)}, u32[]{:S(2)}, u32[]{:S(2)}) %collective-permute-start.48) | collective-permute-done | bytes 393248 | tf_op jit(solution)/shard_map/ppermute | solution.py:52
  238.9 3.4 %copy-done.1 = f32[1536,1536]{1,0:T(8,128)} copy-done((f32[1536,1536]{1,0:T(8,128)}, f32[1536,1536]{1,0:T(8,128)S(1)}, u32[]{:S(2)}) %copy-start.1) | copy-done | bytes 9437208
  242.3 2.2 copy-done.2
  (182 shorter events, 38.1 us)
Async XLA Ops:
  0.6 19.7 %collective-permute-start = (bf16[256,1536]{1,0:T(8,128)(2,1)}, bf16[256,1536]{1,0:T(8,128)(2,1)}, u32[]{:S(2)}, u32[]{:S(2)}) collective-permute-start(bf16[256,1536]{1,0:T(8,128)(2,1)} %param.8), channel_id=1, source_target_pairs={{0,4},{2,6},{4,0},{6,2},{1,5},{3,7},{5,1},{7,3},{8,12},{10,14},{12... | collective-permute-start | bytes 2359304 | tf_op jit(solution)/shard_map/ppermute | solution.py:27
  4.6 15.7 %collective-permute-start.1 = (bf16[256,1536]{1,0:T(8,128)(2,1)}, bf16[256,1536]{1,0:T(8,128)(2,1)}, u32[]{:S(2)}, u32[]{:S(2)}) collective-permute-start(bf16[256,1536]{1,0:T(8,128)(2,1)} %get-tuple-element.302), channel_id=1, source_target_pairs={{0,2},{2,0},{4,6},{6,4},{1,3},{3,1},{5,7},{7,5},{8,10},{10,8},{12,... | collective-permute-start | bytes 2359304 | tf_op jit(solution)/shard_map/ppermute | solution.py:27
  5.6 14.7 %collective-permute-start.2 = (bf16[256,1536]{1,0:T(8,128)(2,1)}, bf16[256,1536]{1,0:T(8,128)(2,1)S(1)}, u32[]{:S(2)}, u32[]{:S(2)}) collective-permute-start(bf16[256,1536]{1,0:T(8,128)(2,1)} %get-tuple-element.300), channel_id=1, source_target_pairs={{0,2},{2,0},{4,6},{6,4},{1,3},{3,1},{5,7},{7,5},{8,10},{10,8},{12,... | collective-permute-start | bytes 2359304 | tf_op jit(solution)/shard_map/ppermute | solution.py:27
  6.1 20.6 %collective-permute-start.3 = (bf16[256,1536]{1,0:T(8,128)(2,1)}, bf16[256,1536]{1,0:T(8,128)(2,1)S(1)}, u32[]{:S(2)}, u32[]{:S(2)}) collective-permute-start(bf16[256,1536]{1,0:T(8,128)(2,1)} %param.8), channel_id=1, source_target_pairs={{0,2},{2,0},{4,6},{6,4},{1,3},{3,1},{5,7},{7,5},{8,10},{10,8},{12,... | collective-permute-start | bytes 2359304 | tf_op jit(solution)/shard_map/ppermute | solution.py:27
  20.3 25.4 %collective-permute-start.8 = (bf16[256,1536]{1,0:T(8,128)(2,1)}, bf16[256,1536]{1,0:T(8,128)(2,1)S(1)}, u32[]{:S(2)}, u32[]{:S(2)}) collective-permute-start(bf16[256,1536]{1,0:T(8,128)(2,1)} %collective-permute-done), channel_id=1, source_target_pairs={{0,2},{2,0},{4,6},{6,4},{1,3},{3,1},{5,7},{7,5},{8,10},{10,8},{12,... | collective-permute-start | bytes 2359304 | tf_op jit(solution)/shard_map/ppermute | solution.py:27
  24.6 25.6 %collective-permute-start.5 = (bf16[128,1536]{1,0:T(8,128)(2,1)S(1)}, bf16[128,1536]{1,0:T(8,128)(2,1)S(1)}, u32[]{:S(2)}, u32[]{:S(2)}) collective-permute-start(bf16[128,1536]{1,0:T(8,128)(2,1)S(1)} %get-tuple-element.311), channel_id=1, source_target_pairs={{0,4},{2,6},{4,0},{6,2},{1,5},{3,7},{5,1},{7,3},{8,12},{10,14},{12... | collective-permute-start | bytes 1179656 | tf_op jit(solution)/shard_map/ppermute | solution.py:27
  26.2 18.3 %collective-permute-start.4 = (bf16[128,1536]{1,0:T(8,128)(2,1)S(1)}, bf16[128,1536]{1,0:T(8,128)(2,1)S(1)}, u32[]{:S(2)}, u32[]{:S(2)}) collective-permute-start(bf16[128,1536]{1,0:T(8,128)(2,1)S(1)} %get-tuple-element.310), channel_id=1, source_target_pairs={{0,4},{2,6},{4,0},{6,2},{1,5},{3,7},{5,1},{7,3},{8,12},{10,14},{12... | collective-permute-start | bytes 1179656 | tf_op jit(solution)/shard_map/ppermute | solution.py:27
  30.5 39.1 %collective-permute-start.6 = (bf16[512,1536]{1,0:T(8,128)(2,1)S(1)}, bf16[512,1536]{1,0:T(8,128)(2,1)S(1)}, u32[]{:S(2)}, u32[]{:S(2)}) collective-permute-start(bf16[512,1536]{1,0:T(8,128)(2,1)S(1)} %convolution_convert_fusion), channel_id=1, source_target_pairs={{4,5},{1,0},{6,7},{3,2},{12,13},{9,8},{14,15},{11,10},{20,21},{17,... | collective-permute-start | bytes 4718600 | tf_op jit(solution)/shard_map/ppermute | solution.py:113
  44.4 25.1 %collective-permute-start.7 = (bf16[128,1536]{1,0:T(8,128)(2,1)S(1)}, bf16[128,1536]{1,0:T(8,128)(2,1)S(1)}, u32[]{:S(2)}, u32[]{:S(2)}) collective-permute-start(bf16[128,1536]{1,0:T(8,128)(2,1)S(1)} %collective-permute-done.4), channel_id=1, source_target_pairs={{0,1},{5,4},{2,3},{7,6},{8,9},{13,12},{10,11},{15,14},{16,17},{21,... | collective-permute-start | bytes 1179656 | tf_op jit(solution)/shard_map/ppermute | solution.py:118
  47.2 21.0 %collective-permute-start.11 = (bf16[128,1536]{1,0:T(8,128)(2,1)S(1)}, bf16[128,1536]{1,0:T(8,128)(2,1)S(1)}, u32[]{:S(2)}, u32[]{:S(2)}) collective-permute-start(bf16[128,1536]{1,0:T(8,128)(2,1)S(1)} %get-tuple-element.313), channel_id=1, source_target_pairs={{0,4},{2,6},{4,0},{6,2},{1,5},{3,7},{5,1},{7,3},{8,12},{10,14},{12... | collective-permute-start | bytes 1179656 | tf_op jit(solution)/shard_map/ppermute | solution.py:27
  49.9 17.0 %collective-permute-start.9 = (bf16[128,1536]{1,0:T(8,128)(2,1)S(1)}, bf16[128,1536]{1,0:T(8,128)(2,1)S(1)}, u32[]{:S(2)}, u32[]{:S(2)}) collective-permute-start(bf16[128,1536]{1,0:T(8,128)(2,1)S(1)} %get-tuple-element.312), channel_id=1, source_target_pairs={{0,4},{2,6},{4,0},{6,2},{1,5},{3,7},{5,1},{7,3},{8,12},{10,14},{12... | collective-permute-start | bytes 1179656 | tf_op jit(solution)/shard_map/ppermute | solution.py:27
  50.2 19.8 %collective-permute-start.10 = (bf16[128,1536]{1,0:T(8,128)(2,1)S(1)}, bf16[128,1536]{1,0:T(8,128)(2,1)S(1)}, u32[]{:S(2)}, u32[]{:S(2)}) collective-permute-start(bf16[128,1536]{1,0:T(8,128)(2,1)S(1)} %collective-permute-done.5), channel_id=1, source_target_pairs={{0,1},{5,4},{2,3},{7,6},{8,9},{13,12},{10,11},{15,14},{16,17},{21,... | collective-permute-start | bytes 1179656 | tf_op jit(solution)/shard_map/ppermute | solution.py:118
  66.9 13.9 %collective-permute-start.12 = (bf16[128,1536]{1,0:T(8,128)(2,1)S(1)}, bf16[128,1536]{1,0:T(8,128)(2,1)S(1)}, u32[]{:S(2)}, u32[]{:S(2)}) collective-permute-start(bf16[128,1536]{1,0:T(8,128)(2,1)S(1)} %collective-permute-done.9), channel_id=1, source_target_pairs={{0,1},{5,4},{2,3},{7,6},{8,9},{13,12},{10,11},{15,14},{16,17},{21,... | collective-permute-start | bytes 1179656 | tf_op jit(solution)/shard_map/ppermute | solution.py:118
  68.2 18.7 %collective-permute-start.13 = (bf16[128,1536]{1,0:T(8,128)(2,1)S(1)}, bf16[128,1536]{1,0:T(8,128)(2,1)S(1)}, u32[]{:S(2)}, u32[]{:S(2)}) collective-permute-start(bf16[128,1536]{1,0:T(8,128)(2,1)S(1)} %collective-permute-done.11), channel_id=1, source_target_pairs={{0,1},{5,4},{2,3},{7,6},{8,9},{13,12},{10,11},{15,14},{16,17},{21,... | collective-permute-start | bytes 1179656 | tf_op jit(solution)/shard_map/ppermute | solution.py:118
  88.7 3.7 %collective-permute-start.15 = (f32[2,512]{1,0:T(2,128)S(1)}, f32[2,512]{1,0:T(2,128)S(1)}, u32[]{:S(2)}, u32[]{:S(2)}) collective-permute-start(f32[2,512]{1,0:T(2,128)S(1)} %maximum_add_fusion), channel_id=1, source_target_pairs={{0,1},{1,0},{2,3},{3,2},{4,5},{5,4},{6,7},{7,6},{8,9},{9,8},{10,11... | collective-permute-start | bytes 12296 | tf_op jit(solution)/shard_map/ppermute | solution.py:27
  93.4 5.0 %collective-permute-start.16 = (bf16[512,128]{1,0:T(8,128)(2,1)S(1)}, bf16[512,128]{1,0:T(8,128)(2,1)S(1)}, u32[]{:S(2)}, u32[]{:S(2)}) collective-permute-start(bf16[512,128]{1,0:T(8,128)(2,1)S(1)} %pad_maximum_fusion.5), channel_id=1, source_target_pairs={{0,1},{5,4},{4,0},{1,5},{2,3},{7,6},{6,2},{3,7},{8,9},{13,12},{12,... | collective-permute-start | bytes 393224 | tf_op jit(solution)/shard_map/ppermute | solution.py:176
  93.5 8.4 %collective-permute-start.19 = (bf16[512,128]{1,0:T(8,128)(2,1)S(1)}, bf16[512,128]{1,0:T(8,128)(2,1)S(1)}, u32[]{:S(2)}, u32[]{:S(2)}) collective-permute-start(bf16[512,128]{1,0:T(8,128)(2,1)S(1)} %pad_maximum_fusion.5), channel_id=1, source_target_pairs={{4,1},{1,4},{6,3},{3,6},{12,9},{9,12},{14,11},{11,14},{20,17},{17,... | collective-permute-start | bytes 393224 | tf_op jit(solution)/shard_map/ppermute | solution.py:177
  98.4 12.2 %collective-permute-start.17 = (bf16[512,384]{1,0:T(8,128)(2,1)S(1)}, bf16[512,384]{1,0:T(8,128)(2,1)S(1)}, u32[]{:S(2)}, u32[]{:S(2)}) collective-permute-start(bf16[512,384]{1,0:T(8,128)(2,1)S(1)} %pad_maximum_fusion.2), channel_id=1, source_target_pairs={{0,1},{5,4},{4,0},{1,5},{2,3},{7,6},{6,2},{3,7},{8,9},{13,12},{12,... | collective-permute-start | bytes 1179656 | tf_op jit(solution)/shard_map/ppermute | solution.py:176
  98.5 14.8 %collective-permute-start.18 = (bf16[512,384]{1,0:T(8,128)(2,1)S(1)}, bf16[512,384]{1,0:T(8,128)(2,1)S(1)}, u32[]{:S(2)}, u32[]{:S(2)}) collective-permute-start(bf16[512,384]{1,0:T(8,128)(2,1)S(1)} %pad_maximum_fusion.2), channel_id=1, source_target_pairs={{4,1},{1,4},{6,3},{3,6},{12,9},{9,12},{14,11},{11,14},{20,17},{17,... | collective-permute-start | bytes 1179656 | tf_op jit(solution)/shard_map/ppermute | solution.py:177
  101.8 29.2 %collective-permute-start.20 = (bf16[512,1024]{1,0:T(8,128)(2,1)S(1)}, bf16[512,1024]{1,0:T(8,128)(2,1)S(1)}, u32[]{:S(2)}, u32[]{:S(2)}) collective-permute-start(bf16[512,1024]{1,0:T(8,128)(2,1)S(1)} %pad_maximum_fusion), channel_id=1, source_target_pairs={{0,1},{5,4},{4,0},{1,5},{2,3},{7,6},{6,2},{3,7},{8,9},{13,12},{12,... | collective-permute-start | bytes 3145736 | tf_op jit(solution)/shard_map/ppermute | solution.py:176
  101.9 31.0 %collective-permute-start.21 = (bf16[512,1024]{1,0:T(8,128)(2,1)S(1)}, bf16[512,1024]{1,0:T(8,128)(2,1)S(1)}, u32[]{:S(2)}, u32[]{:S(2)}) collective-permute-start(bf16[512,1024]{1,0:T(8,128)(2,1)S(1)} %pad_maximum_fusion), channel_id=1, source_target_pairs={{4,1},{1,4},{6,3},{3,6},{12,9},{9,12},{14,11},{11,14},{20,17},{17,... | collective-permute-start | bytes 3145736 | tf_op jit(solution)/shard_map/ppermute | solution.py:177
  106.9 13.0 %collective-permute-start.22 = (bf16[1536,128]{1,0:T(8,128)(2,1)S(1)}, bf16[1536,128]{1,0:T(8,128)(2,1)S(1)}, u32[]{:S(2)}, u32[]{:S(2)}) collective-permute-start(bf16[1536,128]{1,0:T(8,128)(2,1)S(1)} %fusion.62), channel_id=1, source_target_pairs={{0,8},{24,16},{1,9},{25,17},{2,10},{26,18},{3,11},{27,19},{4,12},{... | collective-permute-start | bytes 1179656 | tf_op jit(solution)/shard_map/ppermute | solution.py:52
  114.9 15.3 %collective-permute-start.24 = (bf16[1536,128]{1,0:T(8,128)(2,1)S(1)}, bf16[1536,128]{1,0:T(8,128)(2,1)S(1)}, u32[]{:S(2)}, u32[]{:S(2)}) collective-permute-start(bf16[1536,128]{1,0:T(8,128)(2,1)S(1)} %fusion.63), channel_id=1, source_target_pairs={{0,8},{24,16},{1,9},{25,17},{2,10},{26,18},{3,11},{27,19},{4,12},{... | collective-permute-start | bytes 1179656 | tf_op jit(solution)/shard_map/ppermute | solution.py:52
  120.1 11.0 %collective-permute-start.23 = (bf16[1536,128]{1,0:T(8,128)(2,1)S(1)}, bf16[1536,128]{1,0:T(8,128)(2,1)S(1)}, u32[]{:S(2)}, u32[]{:S(2)}) collective-permute-start(bf16[1536,128]{1,0:T(8,128)(2,1)S(1)} %add_convert_fusion.35), channel_id=1, source_target_pairs={{8,16},{16,8},{9,17},{17,9},{10,18},{18,10},{11,19},{19,11},{12,20... | collective-permute-start | bytes 1179656 | tf_op jit(solution)/shard_map/ppermute | solution.py:60
  123.0 15.6 %collective-permute-start.27 = (bf16[1536,128]{1,0:T(8,128)(2,1)S(1)}, bf16[1536,128]{1,0:T(8,128)(2,1)S(1)}, u32[]{:S(2)}, u32[]{:S(2)}) collective-permute-start(bf16[1536,128]{1,0:T(8,128)(2,1)S(1)} %slice.493), channel_id=1, source_target_pairs={{0,8},{24,16},{1,9},{25,17},{2,10},{26,18},{3,11},{27,19},{4,12},{... | collective-permute-start | bytes 1179656 | tf_op jit(solution)/shard_map/ppermute | solution.py:52
  130.3 11.2 %collective-permute-start.26 = (bf16[1536,128]{1,0:T(8,128)(2,1)S(1)}, bf16[1536,128]{1,0:T(8,128)(2,1)S(1)}, u32[]{:S(2)}, u32[]{:S(2)}) collective-permute-start(bf16[1536,128]{1,0:T(8,128)(2,1)S(1)} %add_convert_fusion.34), channel_id=1, source_target_pairs={{8,16},{16,8},{9,17},{17,9},{10,18},{18,10},{11,19},{19,11},{12,20... | collective-permute-start | bytes 1179656 | tf_op jit(solution)/shard_map/ppermute | solution.py:60
  133.4 14.4 %collective-permute-start.25 = (bf16[1536,128]{1,0:T(8,128)(2,1)S(1)}, bf16[1536,128]{1,0:T(8,128)(2,1)S(1)}, u32[]{:S(2)}, u32[]{:S(2)}) collective-permute-start(bf16[1536,128]{1,0:T(8,128)(2,1)S(1)} %fusion.88), channel_id=1, source_target_pairs={{0,8},{24,16},{8,0},{16,24},{1,9},{25,17},{9,1},{17,25},{2,10},{26... | collective-permute-start | bytes 1179656 | tf_op jit(solution)/shard_map/ppermute | solution.py:52
  140.9 7.7 %collective-permute-start.28 = (bf16[1536,128]{1,0:T(8,128)(2,1)S(1)}, bf16[1536,128]{1,0:T(8,128)(2,1)S(1)}, u32[]{:S(2)}, u32[]{:S(2)}) collective-permute-start(bf16[1536,128]{1,0:T(8,128)(2,1)S(1)} %add_convert_fusion.32), channel_id=1, source_target_pairs={{8,16},{16,8},{9,17},{17,9},{10,18},{18,10},{11,19},{19,11},{12,20... | collective-permute-start | bytes 1179656 | tf_op jit(solution)/shard_map/ppermute | solution.py:60
  141.8 15.3 %collective-permute-start.29 = (bf16[1536,128]{1,0:T(8,128)(2,1)S(1)}, bf16[1536,128]{1,0:T(8,128)(2,1)S(1)}, u32[]{:S(2)}, u32[]{:S(2)}) collective-permute-start(bf16[1536,128]{1,0:T(8,128)(2,1)S(1)} %fusion.89), channel_id=1, source_target_pairs={{0,8},{24,16},{8,0},{16,24},{1,9},{25,17},{9,1},{17,25},{2,10},{26... | collective-permute-start | bytes 1179656 | tf_op jit(solution)/shard_map/ppermute | solution.py:52
  147.9 10.0 %collective-permute-start.30 = (bf16[1536,128]{1,0:T(8,128)(2,1)S(1)}, bf16[1536,128]{1,0:T(8,128)(2,1)S(1)}, u32[]{:S(2)}, u32[]{:S(2)}) collective-permute-start(bf16[1536,128]{1,0:T(8,128)(2,1)S(1)} %add_convert_fusion.30), channel_id=1, source_target_pairs={{8,16},{16,8},{9,17},{17,9},{10,18},{18,10},{11,19},{19,11},{12,20... | collective-permute-start | bytes 1179656 | tf_op jit(solution)/shard_map/ppermute | solution.py:60
  148.8 16.5 %collective-permute-start.31 = (bf16[1536,128]{1,0:T(8,128)(2,1)S(1)}, bf16[1536,128]{1,0:T(8,128)(2,1)S(1)}, u32[]{:S(2)}, u32[]{:S(2)}) collective-permute-start(bf16[1536,128]{1,0:T(8,128)(2,1)S(1)} %fusion.90), channel_id=1, source_target_pairs={{0,8},{24,16},{8,0},{16,24},{1,9},{25,17},{9,1},{17,25},{2,10},{26... | collective-permute-start | bytes 1179656 | tf_op jit(solution)/shard_map/ppermute | solution.py:52
  157.2 12.9 %collective-permute-start.32 = (bf16[1536,128]{1,0:T(8,128)(2,1)S(1)}, bf16[1536,128]{1,0:T(8,128)(2,1)S(1)}, u32[]{:S(2)}, u32[]{:S(2)}) collective-permute-start(bf16[1536,128]{1,0:T(8,128)(2,1)S(1)} %add_convert_fusion.28), channel_id=1, source_target_pairs={{8,16},{16,8},{9,17},{17,9},{10,18},{18,10},{11,19},{19,11},{12,20... | collective-permute-start | bytes 1179656 | tf_op jit(solution)/shard_map/ppermute | solution.py:60
  158.1 16.8 %collective-permute-start.33 = (bf16[1536,128]{1,0:T(8,128)(2,1)S(1)}, bf16[1536,128]{1,0:T(8,128)(2,1)S(1)}, u32[]{:S(2)}, u32[]{:S(2)}) collective-permute-start(bf16[1536,128]{1,0:T(8,128)(2,1)S(1)} %fusion.91), channel_id=1, source_target_pairs={{0,8},{24,16},{8,0},{16,24},{1,9},{25,17},{9,1},{17,25},{2,10},{26... | collective-permute-start | bytes 1179656 | tf_op jit(solution)/shard_map/ppermute | solution.py:52
  165.4 10.3 %collective-permute-start.34 = (bf16[1536,128]{1,0:T(8,128)(2,1)S(1)}, bf16[1536,128]{1,0:T(8,128)(2,1)S(1)}, u32[]{:S(2)}, u32[]{:S(2)}) collective-permute-start(bf16[1536,128]{1,0:T(8,128)(2,1)S(1)} %add_convert_fusion.26), channel_id=1, source_target_pairs={{8,16},{16,8},{9,17},{17,9},{10,18},{18,10},{11,19},{19,11},{12,20... | collective-permute-start | bytes 1179656 | tf_op jit(solution)/shard_map/ppermute | solution.py:60
  170.3 15.4 %collective-permute-start.35 = (bf16[1536,128]{1,0:T(8,128)(2,1)S(1)}, bf16[1536,128]{1,0:T(8,128)(2,1)S(1)}, u32[]{:S(2)}, u32[]{:S(2)}) collective-permute-start(bf16[1536,128]{1,0:T(8,128)(2,1)S(1)} %fusion.92), channel_id=1, source_target_pairs={{0,8},{24,16},{8,0},{16,24},{1,9},{25,17},{9,1},{17,25},{2,10},{26... | collective-permute-start | bytes 1179656 | tf_op jit(solution)/shard_map/ppermute | solution.py:52
  175.0 11.5 %collective-permute-start.36 = (bf16[1536,128]{1,0:T(8,128)(2,1)S(1)}, bf16[1536,128]{1,0:T(8,128)(2,1)S(1)}, u32[]{:S(2)}, u32[]{:S(2)}) collective-permute-start(bf16[1536,128]{1,0:T(8,128)(2,1)S(1)} %add_convert_fusion.24), channel_id=1, source_target_pairs={{8,16},{16,8},{9,17},{17,9},{10,18},{18,10},{11,19},{19,11},{12,20... | collective-permute-start | bytes 1179656 | tf_op jit(solution)/shard_map/ppermute | solution.py:60
  175.9 15.7 %collective-permute-start.37 = (bf16[1536,128]{1,0:T(8,128)(2,1)S(1)}, bf16[1536,128]{1,0:T(8,128)(2,1)S(1)}, u32[]{:S(2)}, u32[]{:S(2)}) collective-permute-start(bf16[1536,128]{1,0:T(8,128)(2,1)S(1)} %fusion.93), channel_id=1, source_target_pairs={{0,8},{24,16},{8,0},{16,24},{1,9},{25,17},{9,1},{17,25},{2,10},{26... | collective-permute-start | bytes 1179656 | tf_op jit(solution)/shard_map/ppermute | solution.py:52
  185.8 7.1 %collective-permute-start.38 = (bf16[1536,128]{1,0:T(8,128)(2,1)S(1)}, bf16[1536,128]{1,0:T(8,128)(2,1)S(1)}, u32[]{:S(2)}, u32[]{:S(2)}) collective-permute-start(bf16[1536,128]{1,0:T(8,128)(2,1)S(1)} %add_convert_fusion.22), channel_id=1, source_target_pairs={{8,16},{16,8},{9,17},{17,9},{10,18},{18,10},{11,19},{19,11},{12,20... | collective-permute-start | bytes 1179656 | tf_op jit(solution)/shard_map/ppermute | solution.py:60
  186.6 14.0 %collective-permute-start.39 = (bf16[1536,128]{1,0:T(8,128)(2,1)S(1)}, bf16[1536,128]{1,0:T(8,128)(2,1)S(1)}, u32[]{:S(2)}, u32[]{:S(2)}) collective-permute-start(bf16[1536,128]{1,0:T(8,128)(2,1)S(1)} %fusion.94), channel_id=1, source_target_pairs={{0,8},{24,16},{8,0},{16,24},{1,9},{25,17},{9,1},{17,25},{2,10},{26... | collective-permute-start | bytes 1179656 | tf_op jit(solution)/shard_map/ppermute | solution.py:52
  191.7 9.7 %collective-permute-start.40 = (bf16[1536,128]{1,0:T(8,128)(2,1)S(1)}, bf16[1536,128]{1,0:T(8,128)(2,1)S(1)}, u32[]{:S(2)}, u32[]{:S(2)}) collective-permute-start(bf16[1536,128]{1,0:T(8,128)(2,1)S(1)} %add_convert_fusion.20), channel_id=1, source_target_pairs={{8,16},{16,8},{9,17},{17,9},{10,18},{18,10},{11,19},{19,11},{12,20... | collective-permute-start | bytes 1179656 | tf_op jit(solution)/shard_map/ppermute | solution.py:60
  193.0 15.8 %collective-permute-start.41 = (bf16[1536,128]{1,0:T(8,128)(2,1)S(1)}, bf16[1536,128]{1,0:T(8,128)(2,1)S(1)}, u32[]{:S(2)}, u32[]{:S(2)}) collective-permute-start(bf16[1536,128]{1,0:T(8,128)(2,1)S(1)} %fusion.95), channel_id=1, source_target_pairs={{0,8},{24,16},{8,0},{16,24},{1,9},{25,17},{9,1},{17,25},{2,10},{26... | collective-permute-start | bytes 1179656 | tf_op jit(solution)/shard_map/ppermute | solution.py:52
  200.7 8.9 %collective-permute-start.42 = (bf16[1536,128]{1,0:T(8,128)(2,1)S(1)}, bf16[1536,128]{1,0:T(8,128)(2,1)S(1)}, u32[]{:S(2)}, u32[]{:S(2)}) collective-permute-start(bf16[1536,128]{1,0:T(8,128)(2,1)S(1)} %add_convert_fusion.18), channel_id=1, source_target_pairs={{8,16},{16,8},{9,17},{17,9},{10,18},{18,10},{11,19},{19,11},{12,20... | collective-permute-start | bytes 1179656 | tf_op jit(solution)/shard_map/ppermute | solution.py:60
  201.6 15.7 %collective-permute-start.43 = (bf16[1536,128]{1,0:T(8,128)(2,1)S(1)}, bf16[1536,128]{1,0:T(8,128)(2,1)S(1)}, u32[]{:S(2)}, u32[]{:S(2)}) collective-permute-start(bf16[1536,128]{1,0:T(8,128)(2,1)S(1)} %fusion.96), channel_id=1, source_target_pairs={{0,8},{24,16},{8,0},{16,24},{1,9},{25,17},{9,1},{17,25},{2,10},{26... | collective-permute-start | bytes 1179656 | tf_op jit(solution)/shard_map/ppermute | solution.py:52
  209.0 9.6 %collective-permute-start.44 = (bf16[1536,128]{1,0:T(8,128)(2,1)S(1)}, bf16[1536,128]{1,0:T(8,128)(2,1)S(1)}, u32[]{:S(2)}, u32[]{:S(2)}) collective-permute-start(bf16[1536,128]{1,0:T(8,128)(2,1)S(1)} %add_convert_fusion.16), channel_id=1, source_target_pairs={{8,16},{16,8},{9,17},{17,9},{10,18},{18,10},{11,19},{19,11},{12,20... | collective-permute-start | bytes 1179656 | tf_op jit(solution)/shard_map/ppermute | solution.py:60
  209.8 16.0 %collective-permute-start.45 = (bf16[1536,128]{1,0:T(8,128)(2,1)S(1)}, bf16[1536,128]{1,0:T(8,128)(2,1)S(1)}, u32[]{:S(2)}, u32[]{:S(2)}) collective-permute-start(bf16[1536,128]{1,0:T(8,128)(2,1)S(1)} %add_convert_fusion.15), channel_id=1, source_target_pairs={{8,0},{16,24},{9,1},{17,25},{10,2},{18,26},{11,3},{19,27},{12,4},{... | collective-permute-start | bytes 1179656 | tf_op jit(solution)/shard_map/ppermute | solution.py:52
  217.5 8.3 %collective-permute-start.46 = (bf16[1536,128]{1,0:T(8,128)(2,1)S(1)}, bf16[1536,128]{1,0:T(8,128)(2,1)S(1)}, u32[]{:S(2)}, u32[]{:S(2)}) collective-permute-start(bf16[1536,128]{1,0:T(8,128)(2,1)S(1)} %add_convert_fusion.14), channel_id=1, source_target_pairs={{8,16},{16,8},{9,17},{17,9},{10,18},{18,10},{11,19},{19,11},{12,20... | collective-permute-start | bytes 1179656 | tf_op jit(solution)/shard_map/ppermute | solution.py:60
  218.7 15.5 %collective-permute-start.47 = (bf16[1536,128]{1,0:T(8,128)(2,1)S(1)}, bf16[1536,128]{1,0:T(8,128)(2,1)S(1)}, u32[]{:S(2)}, u32[]{:S(2)}) collective-permute-start(bf16[1536,128]{1,0:T(8,128)(2,1)S(1)} %add_convert_fusion.13), channel_id=1, source_target_pairs={{8,0},{16,24},{9,1},{17,25},{10,2},{18,26},{11,3},{19,27},{12,4},{... | collective-permute-start | bytes 1179656 | tf_op jit(solution)/shard_map/ppermute | solution.py:52
  225.9 12.5 %collective-permute-start.48 = (bf16[1536,128]{1,0:T(8,128)(2,1)S(1)}, bf16[1536,128]{1,0:T(8,128)(2,1)S(1)}, u32[]{:S(2)}, u32[]{:S(2)}) collective-permute-start(bf16[1536,128]{1,0:T(8,128)(2,1)S(1)} %add_convert_fusion.12), channel_id=1, source_target_pairs={{8,0},{16,24},{9,1},{17,25},{10,2},{18,26},{11,3},{19,27},{12,4},{... | collective-permute-start | bytes 1179656 | tf_op jit(solution)/shard_map/ppermute | solution.py:52
  (13 other events, 130.1 us)

commit v13 on v12

--- a/solution.py
+++ b/solution.py
@@ -123,17 +123,13 @@
     for k in range(group * pieces):
         r, p = k // pieces, k % pieces
         span, long_span = slice(p * rows, (p + 1) * rows), slice(k * rows, (k + 1) * rows)
-        far_out, came = far_outs[k], passed[k]
+        res, cot, came = residual_parts[r], cotangent_parts[r], passed[k]
         if sums:
-            far_out, sums[-1] = together(far_out, sums[-1])
-        keep = jnp.where(near, near_out[long_span], far_out)
-        base, w = lax.optimization_barrier(
-            (
-                residual_parts[r][span].astype(f32) + keep.astype(f32),
-                gain_part[None, :] * cotangent_parts[r][span].astype(f32),
-            )
-        )
-        h = base + jnp.where(near, near_came[long_span], came).astype(f32)
+            came, sums[-1] = together(came, sums[-1])
+        keep = jnp.where(near, near_out[long_span], far_outs[k])
+        came = jnp.where(near, near_came[long_span], came)
+        h = res[span].astype(f32) + keep.astype(f32) + came.astype(f32)
+        w = gain_part[None, :] * cot[span].astype(f32)
         hidden.append(h)
         weighted.append(w)
         sums.append(jnp.stack([jnp.sum(h * h, axis=-1), jnp.sum(h * w, axis=-1)]))

time: 246 us -> 239 us (0.972)
  waiting for transfers between devices: 89.2 us -> 75.6 us
  local copies, waits for them, and re-layouts: 11.8 us -> 15 us
  other arithmetic: 15.2 us -> 18.2 us
    ppermute x11, waiting for transfers between devices: 42.5 us -> 33.4 us  [swap(): return lax.ppermute(value, axis, [(i, i ^ bit) for i in range(count)])]
    ppermute x4, waiting for transfers between devices: 14 us -> 5.41 us  [body(): lax.ppermute(out, ('fsdp', 'tp'), outward_pairs)]
    reduce_sum x4, other arithmetic: 1.2 us -> 7.19 us  [body(): sums.append(jnp.stack([jnp.sum(h * h, axis=-1), jnp.sum(h * w, axis=-1)]))]
    ppermute x1, waiting for transfers between devices: 0.01 us -> 3.73 us  [body(): near_came = lax.ppermute(near_out, ('fsdp', 'tp'), inward_pairs)]
    unnamed x27 -> x41, local copies, waits for them, and re-layouts: 8.26 us -> 11.6 us
    add x4 -> x0, other arithmetic: 2.54 us -> none  [body(): residual_parts[r][span].astype(f32) + keep.astype(f32)]
    unnamed x26 -> x27, other arithmetic: 4.96 us -> 5.01 us
  transfers between devices with their start and end apart: 49 -> 49, of which waited for: 19 -> 19; matrix products, arithmetic and copies ran while one was open for 18% -> 20% of each run, Pallas kernels for 0% -> 0%
where the time goes in v13:
time: 239 us; the launch traced here: 238 us
  starting transfers between devices  102 us (43%)
  waiting for transfers between devices  75.6 us (32%)
  matrix products  25.7 us (11%)
  other arithmetic  18.2 us (8%)
  local copies, waits for them, and re-layouts  15 us (6%)
    ppermute x15, starting transfers between devices, send_outer(): self.edge[s] = lax.ppermute(payload, 'island', pairs)  67.1 us
    ppermute x11, waiting for transfers between devices, swap(): return lax.ppermute(value, axis, [(i, i ^ bit) for i in range(count)])  33.4 us
    ppermute x15, waiting for transfers between devices, send_outer(): self.edge[s] = lax.ppermute(payload, 'island', pairs)  27.1 us
    dot_general x7, matrix products, add_pseudo(): lax.dot_general(context_all, piece, (((0,), (0,)), ((), ())), preferred_e...  16.1 us
    unnamed x41, local copies, waits for them, and re-layouts  11.6 us
    ppermute x3, starting transfers between devices, move(): crosses.append(lax.ppermute(d_local, ('fsdp', 'tp'), cross_pairs))  10.1 us
    dot_general x3, matrix products, project(): jnp.dot(block, weight, preferred_element_type=f32).astype(bf16)  9.61 us
    ppermute x12, starting transfers between devices, step(): self.mid[s] = lax.ppermute(self.sums[s], 'island', [(1, 2), (2, 1)])  8.45 us
  transfers between devices with their start and end apart: 49, of which 19 were waited for; matrix products, arithmetic and copies ran while one was open for 20% of the time, Pallas kernels for 0%

profile of v13, /device:TPU:2, one launch (start us, length us, event | category | flops | bytes accessed | tf_op | source)
XLA Modules:
  0.0 238.1 jit_solution(13688226879581582375)
XLA Ops:
  0.6 1.6 collective-permute-start
  4.8 15.5 %collective-permute-done = bf16[256,1536]{1,0:T(8,128)(2,1)} collective-permute-done((bf16[256,1536]{1,0:T(8,128)(2,1)}, bf16[256,1536]{1,0:T(8,128)(2,1)}, u32[]{:S(2)}, u32[]{:S(2)}) %collective-permute-start) | collective-permute-done | bytes 786464 | tf_op jit(solution)/shard_map/ppermute | solution.py:27
  21.2 4.1 %convolution_convert_fusion.2 = bf16[256,1536]{1,0:T(8,128)(2,1)S(1)} fusion(bf16[256,1536]{1,0:T(8,128)(2,1)} %collective-permute-done, bf16[1536,1536]{1,0:T(8,128)(2,1)} %param.12), kind=kOutput, calls=%fused_computation.8 | convolution fusion | flops 1208352768 | bytes 6291456 | tf_op jit(solution)/shard_map/dot_general | solution.py:89
  26.1 1.5 collective-permute-start.6
  27.7 4.1 %convolution_convert_fusion = bf16[512,1536]{1,0:T(8,128)(2,1)} fusion(bf16[1536,1536]{1,0:T(8,128)(2,1)S(1)} %bitcast.206, bf16[256,1536]{1,0:T(8,128)(2,1)S(1)} %collective-permute-done.5, bf16[256,1536]{1,0:T(8,128)(2,1)S(1)} %copy-done.3), kind=kOutput, calls=%fused_computation | convolution fusion | flops 2419851264 | bytes 7864320 | tf_op jit(solution)/shard_map/dot_general | solution.py:89
  31.8 3.6 %collective-permute-start.7 = (bf16[512,1536]{1,0:T(8,128)(2,1)}, bf16[512,1536]{1,0:T(8,128)(2,1)}, u32[]{:S(2)}, u32[]{:S(2)}) collective-permute-start(bf16[512,1536]{1,0:T(8,128)(2,1)} %convolution_convert_fusion), channel_id=1, source_target_pairs={{4,5},{1,0},{6,7},{3,2},{12,13},{9,8},{14,15},{11,10},{20,21},{17,... | collective-permute-start | bytes 4718600 | tf_op jit(solution)/shard_map/ppermute | solution.py:113
  35.4 2.2 collective-permute-done.6
  41.2 3.4 %collective-permute-start.12 = (bf16[128,1536]{1,0:T(8,128)(2,1)}, bf16[128,1536]{1,0:T(8,128)(2,1)S(1)}, u32[]{:S(2)}, u32[]{:S(2)}) collective-permute-start(bf16[128,1536]{1,0:T(8,128)(2,1)} %get-tuple-element.297), channel_id=1, source_target_pairs={{0,4},{2,6},{4,0},{6,2},{1,5},{3,7},{5,1},{7,3},{8,12},{10,14},{12... | collective-permute-start | bytes 1179656 | tf_op jit(solution)/shard_map/ppermute | solution.py:27
  46.4 2.2 constant_dynamic-update-slice_fusion.2
  49.9 6.2 %collective-permute-done.12 = bf16[128,1536]{1,0:T(8,128)(2,1)S(1)} collective-permute-done((bf16[128,1536]{1,0:T(8,128)(2,1)}, bf16[128,1536]{1,0:T(8,128)(2,1)S(1)}, u32[]{:S(2)}, u32[]{:S(2)}) %collective-permute-start.12) | collective-permute-done | bytes 393248 | tf_op jit(solution)/shard_map/ppermute | solution.py:27
  57.3 6.1 %collective-permute-done.10 = bf16[128,1536]{1,0:T(8,128)(2,1)} collective-permute-done((bf16[128,1536]{1,0:T(8,128)(2,1)}, bf16[128,1536]{1,0:T(8,128)(2,1)}, u32[]{:S(2)}, u32[]{:S(2)}) %collective-permute-start.10) | collective-permute-done | bytes 393248 | tf_op jit(solution)/shard_map/ppermute | solution.py:27
  64.7 3.7 %collective-permute-done.7 = bf16[512,1536]{1,0:T(8,128)(2,1)} collective-permute-done((bf16[512,1536]{1,0:T(8,128)(2,1)}, bf16[512,1536]{1,0:T(8,128)(2,1)}, u32[]{:S(2)}, u32[]{:S(2)}) %collective-permute-start.7) | collective-permute-done | bytes 1572896 | tf_op jit(solution)/shard_map/ppermute | solution.py:113
  68.4 1.8 multiply_reduce_fusion.7
  70.3 1.8 multiply_reduce_fusion.5
  72.1 5.4 %collective-permute-done.11 = bf16[128,1536]{1,0:T(8,128)(2,1)S(1)} collective-permute-done((bf16[128,1536]{1,0:T(8,128)(2,1)}, bf16[128,1536]{1,0:T(8,128)(2,1)S(1)}, u32[]{:S(2)}, u32[]{:S(2)}) %collective-permute-start.11) | collective-permute-done | bytes 393248 | tf_op jit(solution)/shard_map/ppermute | solution.py:118
  77.5 1.8 multiply_reduce_fusion.3
  79.3 1.8 multiply_reduce_fusion.1
  82.9 3.5 %collective-permute-done.15 = f32[2,512]{1,0:T(2,128)S(1)} collective-permute-done((f32[2,512]{1,0:T(2,128)S(1)}, f32[2,512]{1,0:T(2,128)S(1)}, u32[]{:S(2)}, u32[]{:S(2)}) %collective-permute-start.15) | collective-permute-done | bytes 4128 | tf_op jit(solution)/shard_map/ppermute | solution.py:27
  87.6 3.4 %collective-permute-start.19 = (bf16[512,128]{1,0:T(8,128)(2,1)S(1)}, bf16[512,128]{1,0:T(8,128)(2,1)S(1)}, u32[]{:S(2)}, u32[]{:S(2)}) collective-permute-start(bf16[512,128]{1,0:T(8,128)(2,1)S(1)} %pad_maximum_fusion.5), channel_id=1, source_target_pairs={{4,1},{1,4},{6,3},{3,6},{12,9},{9,12},{14,11},{11,14},{20,17},{17,... | collective-permute-start | bytes 393224 | tf_op jit(solution)/shard_map/ppermute | solution.py:173
  92.6 3.4 %collective-permute-start.18 = (bf16[512,384]{1,0:T(8,128)(2,1)S(1)}, bf16[512,384]{1,0:T(8,128)(2,1)S(1)}, u32[]{:S(2)}, u32[]{:S(2)}) collective-permute-start(bf16[512,384]{1,0:T(8,128)(2,1)S(1)} %pad_maximum_fusion.2), channel_id=1, source_target_pairs={{4,1},{1,4},{6,3},{3,6},{12,9},{9,12},{14,11},{11,14},{20,17},{17,... | collective-permute-start | bytes 1179656 | tf_op jit(solution)/shard_map/ppermute | solution.py:173
  96.0 3.4 %collective-permute-start.21 = (bf16[512,1024]{1,0:T(8,128)(2,1)S(1)}, bf16[512,1024]{1,0:T(8,128)(2,1)S(1)}, u32[]{:S(2)}, u32[]{:S(2)}) collective-permute-start(bf16[512,1024]{1,0:T(8,128)(2,1)S(1)} %pad_maximum_fusion), channel_id=1, source_target_pairs={{4,1},{1,4},{6,3},{3,6},{12,9},{9,12},{14,11},{11,14},{20,17},{17,... | collective-permute-start | bytes 3145736 | tf_op jit(solution)/shard_map/ppermute | solution.py:173
  101.0 3.7 %collective-permute-start.22 = (bf16[1536,128]{1,0:T(8,128)(2,1)S(1)}, bf16[1536,128]{1,0:T(8,128)(2,1)S(1)}, u32[]{:S(2)}, u32[]{:S(2)}) collective-permute-start(bf16[1536,128]{1,0:T(8,128)(2,1)S(1)} %fusion.62), channel_id=1, source_target_pairs={{0,8},{24,16},{1,9},{25,17},{2,10},{26,18},{3,11},{27,19},{4,12},{... | collective-permute-start | bytes 1179656 | tf_op jit(solution)/shard_map/ppermute | solution.py:52
  104.8 2.7 %collective-permute-done.18 = bf16[512,384]{1,0:T(8,128)(2,1)S(1)} collective-permute-done((bf16[512,384]{1,0:T(8,128)(2,1)S(1)}, bf16[512,384]{1,0:T(8,128)(2,1)S(1)}, u32[]{:S(2)}, u32[]{:S(2)}) %collective-permute-start.18) | collective-permute-done | bytes 393248 | tf_op jit(solution)/shard_map/ppermute | solution.py:173
  109.0 3.5 %collective-permute-start.24 = (bf16[1536,128]{1,0:T(8,128)(2,1)S(1)}, bf16[1536,128]{1,0:T(8,128)(2,1)S(1)}, u32[]{:S(2)}, u32[]{:S(2)}) collective-permute-start(bf16[1536,128]{1,0:T(8,128)(2,1)S(1)} %fusion.63), channel_id=1, source_target_pairs={{0,8},{24,16},{1,9},{25,17},{2,10},{26,18},{3,11},{27,19},{4,12},{... | collective-permute-start | bytes 1179656 | tf_op jit(solution)/shard_map/ppermute | solution.py:52
  112.5 1.5 collective-permute-done.22
  114.9 2.2 fusion.33
  117.1 7.2 %collective-permute-start.27 = (bf16[1536,128]{1,0:T(8,128)(2,1)S(1)}, bf16[1536,128]{1,0:T(8,128)(2,1)S(1)}, u32[]{:S(2)}, u32[]{:S(2)}) collective-permute-start(bf16[1536,128]{1,0:T(8,128)(2,1)S(1)} %slice.505), channel_id=1, source_target_pairs={{0,8},{24,16},{1,9},{25,17},{2,10},{26,18},{3,11},{27,19},{4,12},{... | collective-permute-start | bytes 1179656 | tf_op jit(solution)/shard_map/ppermute | solution.py:52
  125.2 1.7 collective-permute-done.21
  127.3 3.5 %collective-permute-start.25 = (bf16[1536,128]{1,0:T(8,128)(2,1)S(1)}, bf16[1536,128]{1,0:T(8,128)(2,1)S(1)}, u32[]{:S(2)}, u32[]{:S(2)}) collective-permute-start(bf16[1536,128]{1,0:T(8,128)(2,1)S(1)} %fusion.88), channel_id=1, source_target_pairs={{0,8},{24,16},{8,0},{16,24},{1,9},{25,17},{9,1},{17,25},{2,10},{26... | collective-permute-start | bytes 1179656 | tf_op jit(solution)/shard_map/ppermute | solution.py:52
  130.8 2.2 collective-permute-done.27
  133.0 2.2 fusion.34
  136.2 3.8 %collective-permute-start.29 = (bf16[1536,128]{1,0:T(8,128)(2,1)S(1)}, bf16[1536,128]{1,0:T(8,128)(2,1)S(1)}, u32[]{:S(2)}, u32[]{:S(2)}) collective-permute-start(bf16[1536,128]{1,0:T(8,128)(2,1)S(1)} %fusion.89), channel_id=1, source_target_pairs={{0,8},{24,16},{8,0},{16,24},{1,9},{25,17},{9,1},{17,25},{2,10},{26... | collective-permute-start | bytes 1179656 | tf_op jit(solution)/shard_map/ppermute | solution.py:52
  140.0 2.2 fusion.35
  143.2 7.2 %collective-permute-start.31 = (bf16[1536,128]{1,0:T(8,128)(2,1)S(1)}, bf16[1536,128]{1,0:T(8,128)(2,1)S(1)}, u32[]{:S(2)}, u32[]{:S(2)}) collective-permute-start(bf16[1536,128]{1,0:T(8,128)(2,1)S(1)} %fusion.90), channel_id=1, source_target_pairs={{0,8},{24,16},{8,0},{16,24},{1,9},{25,17},{9,1},{17,25},{2,10},{26... | collective-permute-start | bytes 1179656 | tf_op jit(solution)/shard_map/ppermute | solution.py:52
  151.8 6.9 %collective-permute-start.33 = (bf16[1536,128]{1,0:T(8,128)(2,1)S(1)}, bf16[1536,128]{1,0:T(8,128)(2,1)S(1)}, u32[]{:S(2)}, u32[]{:S(2)}) collective-permute-start(bf16[1536,128]{1,0:T(8,128)(2,1)S(1)} %fusion.91), channel_id=1, source_target_pairs={{0,8},{24,16},{8,0},{16,24},{1,9},{25,17},{9,1},{17,25},{2,10},{26... | collective-permute-start | bytes 1179656 | tf_op jit(solution)/shard_map/ppermute | solution.py:52
  160.1 3.3 %fusion.36 = bf16[1536,256]{1,0:T(8,128)(2,1)S(1)} fusion(bf16[1536,1536]{1,0:T(8,128)(2,1)S(1)} %bitcast.208, bf16[1,1536,1536]{2,1,0:T(8,128)(2,1)S(1)} %bitcast.210, bf16[1,1536,1536]{2,1,0:T(8,128)(2,1)} %param.13, bf16[1024,1536]{1,0:T(8,128)(2,1)S(1)} %constant_dynamic-update-slice_fusion, bf16[1024,256]{1,0:T(8,128)(2,1)S(1)} %get-tuple-element.206), kind=kOutput, calls=%fused_computation.55 | convolution fusion | flops 812384256 | bytes 6815744 | tf_op jit(solution)/shard_map/dot_general | solution.py:186
  164.1 4.2 %collective-permute-start.35 = (bf16[1536,128]{1,0:T(8,128)(2,1)S(1)}, bf16[1536,128]{1,0:T(8,128)(2,1)S(1)}, u32[]{:S(2)}, u32[]{:S(2)}) collective-permute-start(bf16[1536,128]{1,0:T(8,128)(2,1)S(1)} %fusion.92), channel_id=1, source_target_pairs={{0,8},{24,16},{8,0},{16,24},{1,9},{25,17},{9,1},{17,25},{2,10},{26... | collective-permute-start | bytes 1179656 | tf_op jit(solution)/shard_map/ppermute | solution.py:52
  169.8 5.9 %collective-permute-start.37 = (bf16[1536,128]{1,0:T(8,128)(2,1)S(1)}, bf16[1536,128]{1,0:T(8,128)(2,1)S(1)}, u32[]{:S(2)}, u32[]{:S(2)}) collective-permute-start(bf16[1536,128]{1,0:T(8,128)(2,1)S(1)} %fusion.93), channel_id=1, source_target_pairs={{0,8},{24,16},{8,0},{16,24},{1,9},{25,17},{9,1},{17,25},{2,10},{26... | collective-permute-start | bytes 1179656 | tf_op jit(solution)/shard_map/ppermute | solution.py:52
  175.7 3.3 %fusion.37 = bf16[1536,256]{1,0:T(8,128)(2,1)S(1)} fusion(bf16[1536,1536]{1,0:T(8,128)(2,1)S(1)} %bitcast.208, bf16[1,1536,1536]{2,1,0:T(8,128)(2,1)S(1)} %bitcast.210, bf16[1,1536,1536]{2,1,0:T(8,128)(2,1)} %param.13, bf16[1024,1536]{1,0:T(8,128)(2,1)S(1)} %constant_dynamic-update-slice_fusion, bf16[1024,256]{1,0:T(8,128)(2,1)S(1)} %get-tuple-element.226), kind=kOutput, calls=%fused_computation.56 | convolution fusion | flops 812384256 | bytes 6815744 | tf_op jit(solution)/shard_map/dot_general | solution.py:186
  180.5 4.4 %collective-permute-start.39 = (bf16[1536,128]{1,0:T(8,128)(2,1)S(1)}, bf16[1536,128]{1,0:T(8,128)(2,1)S(1)}, u32[]{:S(2)}, u32[]{:S(2)}) collective-permute-start(bf16[1536,128]{1,0:T(8,128)(2,1)S(1)} %fusion.94), channel_id=1, source_target_pairs={{0,8},{24,16},{8,0},{16,24},{1,9},{25,17},{9,1},{17,25},{2,10},{26... | collective-permute-start | bytes 1179656 | tf_op jit(solution)/shard_map/ppermute | solution.py:52
  187.7 6.3 %collective-permute-start.41 = (bf16[1536,128]{1,0:T(8,128)(2,1)S(1)}, bf16[1536,128]{1,0:T(8,128)(2,1)S(1)}, u32[]{:S(2)}, u32[]{:S(2)}) collective-permute-start(bf16[1536,128]{1,0:T(8,128)(2,1)S(1)} %fusion.95), channel_id=1, source_target_pairs={{0,8},{24,16},{8,0},{16,24},{1,9},{25,17},{9,1},{17,25},{2,10},{26... | collective-permute-start | bytes 1179656 | tf_op jit(solution)/shard_map/ppermute | solution.py:52
  196.0 6.4 %collective-permute-start.43 = (bf16[1536,128]{1,0:T(8,128)(2,1)S(1)}, bf16[1536,128]{1,0:T(8,128)(2,1)S(1)}, u32[]{:S(2)}, u32[]{:S(2)}) collective-permute-start(bf16[1536,128]{1,0:T(8,128)(2,1)S(1)} %fusion.96), channel_id=1, source_target_pairs={{0,8},{24,16},{8,0},{16,24},{1,9},{25,17},{9,1},{17,25},{2,10},{26... | collective-permute-start | bytes 1179656 | tf_op jit(solution)/shard_map/ppermute | solution.py:52
  205.1 6.3 %collective-permute-done.43 = bf16[1536,128]{1,0:T(8,128)(2,1)S(1)} collective-permute-done((bf16[1536,128]{1,0:T(8,128)(2,1)S(1)}, bf16[1536,128]{1,0:T(8,128)(2,1)S(1)}, u32[]{:S(2)}, u32[]{:S(2)}) %collective-permute-start.43) | collective-permute-done | bytes 393248 | tf_op jit(solution)/shard_map/ppermute | solution.py:52
  214.5 5.3 %collective-permute-done.45 = bf16[1536,128]{1,0:T(8,128)(2,1)S(1)} collective-permute-done((bf16[1536,128]{1,0:T(8,128)(2,1)S(1)}, bf16[1536,128]{1,0:T(8,128)(2,1)S(1)}, u32[]{:S(2)}, u32[]{:S(2)}) %collective-permute-start.45) | collective-permute-done | bytes 393248 | tf_op jit(solution)/shard_map/ppermute | solution.py:52
  221.7 6.0 %collective-permute-done.47 = bf16[1536,128]{1,0:T(8,128)(2,1)S(1)} collective-permute-done((bf16[1536,128]{1,0:T(8,128)(2,1)S(1)}, bf16[1536,128]{1,0:T(8,128)(2,1)S(1)}, u32[]{:S(2)}, u32[]{:S(2)}) %collective-permute-start.47) | collective-permute-done | bytes 393248 | tf_op jit(solution)/shard_map/ppermute | solution.py:52
  228.2 3.7 %collective-permute-done.48 = bf16[1536,128]{1,0:T(8,128)(2,1)S(1)} collective-permute-done((bf16[1536,128]{1,0:T(8,128)(2,1)S(1)}, bf16[1536,128]{1,0:T(8,128)(2,1)S(1)}, u32[]{:S(2)}, u32[]{:S(2)}) %collective-permute-start.48) | collective-permute-done | bytes 393248 | tf_op jit(solution)/shard_map/ppermute | solution.py:52
  232.4 3.4 %copy-done.6 = f32[1536,1536]{1,0:T(8,128)} copy-done((f32[1536,1536]{1,0:T(8,128)}, f32[1536,1536]{1,0:T(8,128)S(1)}, u32[]{:S(2)}) %copy-start.6) | copy-done | bytes 9437208
  235.9 2.2 copy-done.7
  (192 shorter events, 44.5 us)
Async XLA Ops:
  0.6 19.7 %collective-permute-start = (bf16[256,1536]{1,0:T(8,128)(2,1)}, bf16[256,1536]{1,0:T(8,128)(2,1)}, u32[]{:S(2)}, u32[]{:S(2)}) collective-permute-start(bf16[256,1536]{1,0:T(8,128)(2,1)} %param.8), channel_id=1, source_target_pairs={{0,4},{2,6},{4,0},{6,2},{1,5},{3,7},{5,1},{7,3},{8,12},{10,14},{12... | collective-permute-start | bytes 2359304 | tf_op jit(solution)/shard_map/ppermute | solution.py:27
  3.7 16.6 %collective-permute-start.1 = (bf16[256,1536]{1,0:T(8,128)(2,1)S(1)}, bf16[256,1536]{1,0:T(8,128)(2,1)S(1)}, u32[]{:S(2)}, u32[]{:S(2)}) collective-permute-start(bf16[256,1536]{1,0:T(8,128)(2,1)S(1)} %get-tuple-element.286), channel_id=1, source_target_pairs={{0,2},{2,0},{4,6},{6,4},{1,3},{3,1},{5,7},{7,5},{8,10},{10,8},{12,... | collective-permute-start | bytes 2359304 | tf_op jit(solution)/shard_map/ppermute | solution.py:27
  3.9 16.4 %collective-permute-start.2 = (bf16[256,1536]{1,0:T(8,128)(2,1)S(1)}, bf16[256,1536]{1,0:T(8,128)(2,1)S(1)}, u32[]{:S(2)}, u32[]{:S(2)}) collective-permute-start(bf16[256,1536]{1,0:T(8,128)(2,1)S(1)} %get-tuple-element.284), channel_id=1, source_target_pairs={{0,2},{2,0},{4,6},{6,4},{1,3},{3,1},{5,7},{7,5},{8,10},{10,8},{12,... | collective-permute-start | bytes 2359304 | tf_op jit(solution)/shard_map/ppermute | solution.py:27
  4.8 22.8 %collective-permute-start.5 = (bf16[256,1536]{1,0:T(8,128)(2,1)S(1)}, bf16[256,1536]{1,0:T(8,128)(2,1)S(1)}, u32[]{:S(2)}, u32[]{:S(2)}) collective-permute-start(bf16[256,1536]{1,0:T(8,128)(2,1)S(1)} %copy-done.3), channel_id=1, source_target_pairs={{0,2},{2,0},{4,6},{6,4},{1,3},{3,1},{5,7},{7,5},{8,10},{10,8},{12,... | collective-permute-start | bytes 2359304 | tf_op jit(solution)/shard_map/ppermute | solution.py:27
  21.2 17.7 %collective-permute-start.9 = (bf16[256,1536]{1,0:T(8,128)(2,1)}, bf16[256,1536]{1,0:T(8,128)(2,1)S(1)}, u32[]{:S(2)}, u32[]{:S(2)}) collective-permute-start(bf16[256,1536]{1,0:T(8,128)(2,1)} %collective-permute-done), channel_id=1, source_target_pairs={{0,2},{2,0},{4,6},{6,4},{1,3},{3,1},{5,7},{7,5},{8,10},{10,8},{12,... | collective-permute-start | bytes 2359304 | tf_op jit(solution)/shard_map/ppermute | solution.py:27
  26.1 11.5 %collective-permute-start.6 = (bf16[128,1536]{1,0:T(8,128)(2,1)S(1)}, bf16[128,1536]{1,0:T(8,128)(2,1)}, u32[]{:S(2)}, u32[]{:S(2)}) collective-permute-start(bf16[128,1536]{1,0:T(8,128)(2,1)S(1)} %get-tuple-element.294), channel_id=1, source_target_pairs={{0,4},{2,6},{4,0},{6,2},{1,5},{3,7},{5,1},{7,3},{8,12},{10,14},{12... | collective-permute-start | bytes 1179656 | tf_op jit(solution)/shard_map/ppermute | solution.py:27
  31.8 36.6 %collective-permute-start.7 = (bf16[512,1536]{1,0:T(8,128)(2,1)}, bf16[512,1536]{1,0:T(8,128)(2,1)}, u32[]{:S(2)}, u32[]{:S(2)}) collective-permute-start(bf16[512,1536]{1,0:T(8,128)(2,1)} %convolution_convert_fusion), channel_id=1, source_target_pairs={{4,5},{1,0},{6,7},{3,2},{12,13},{9,8},{14,15},{11,10},{20,21},{17,... | collective-permute-start | bytes 4718600 | tf_op jit(solution)/shard_map/ppermute | solution.py:113
  35.4 13.2 %collective-permute-start.3 = (bf16[128,1536]{1,0:T(8,128)(2,1)}, bf16[128,1536]{1,0:T(8,128)(2,1)}, u32[]{:S(2)}, u32[]{:S(2)}) collective-permute-start(bf16[128,1536]{1,0:T(8,128)(2,1)} %get-tuple-element.295), channel_id=1, source_target_pairs={{0,4},{2,6},{4,0},{6,2},{1,5},{3,7},{5,1},{7,3},{8,12},{10,14},{12... | collective-permute-start | bytes 1179656 | tf_op jit(solution)/shard_map/ppermute | solution.py:27
  37.6 27.1 %collective-permute-start.8 = (bf16[128,1536]{1,0:T(8,128)(2,1)}, bf16[128,1536]{1,0:T(8,128)(2,1)}, u32[]{:S(2)}, u32[]{:S(2)}) collective-permute-start(bf16[128,1536]{1,0:T(8,128)(2,1)} %collective-permute-done.6), channel_id=1, source_target_pairs={{0,1},{5,4},{2,3},{7,6},{8,9},{13,12},{10,11},{15,14},{16,17},{21,... | collective-permute-start | bytes 1179656 | tf_op jit(solution)/shard_map/ppermute | solution.py:118
  41.2 14.8 %collective-permute-start.12 = (bf16[128,1536]{1,0:T(8,128)(2,1)}, bf16[128,1536]{1,0:T(8,128)(2,1)S(1)}, u32[]{:S(2)}, u32[]{:S(2)}) collective-permute-start(bf16[128,1536]{1,0:T(8,128)(2,1)} %get-tuple-element.297), channel_id=1, source_target_pairs={{0,4},{2,6},{4,0},{6,2},{1,5},{3,7},{5,1},{7,3},{8,12},{10,14},{12... | collective-permute-start | bytes 1179656 | tf_op jit(solution)/shard_map/ppermute | solution.py:27
  44.6 18.8 %collective-permute-start.10 = (bf16[128,1536]{1,0:T(8,128)(2,1)}, bf16[128,1536]{1,0:T(8,128)(2,1)}, u32[]{:S(2)}, u32[]{:S(2)}) collective-permute-start(bf16[128,1536]{1,0:T(8,128)(2,1)} %get-tuple-element.296), channel_id=1, source_target_pairs={{0,4},{2,6},{4,0},{6,2},{1,5},{3,7},{5,1},{7,3},{8,12},{10,14},{12... | collective-permute-start | bytes 1179656 | tf_op jit(solution)/shard_map/ppermute | solution.py:27
  48.6 21.7 %collective-permute-start.4 = (bf16[128,1536]{1,0:T(8,128)(2,1)}, bf16[128,1536]{1,0:T(8,128)(2,1)S(1)}, u32[]{:S(2)}, u32[]{:S(2)}) collective-permute-start(bf16[128,1536]{1,0:T(8,128)(2,1)} %collective-permute-done.3), channel_id=1, source_target_pairs={{0,1},{5,4},{2,3},{7,6},{8,9},{13,12},{10,11},{15,14},{16,17},{21,... | collective-permute-start | bytes 1179656 | tf_op jit(solution)/shard_map/ppermute | solution.py:118
  56.0 23.3 %collective-permute-start.13 = (bf16[128,1536]{1,0:T(8,128)(2,1)S(1)}, bf16[128,1536]{1,0:T(8,128)(2,1)S(1)}, u32[]{:S(2)}, u32[]{:S(2)}) collective-permute-start(bf16[128,1536]{1,0:T(8,128)(2,1)S(1)} %collective-permute-done.12), channel_id=1, source_target_pairs={{0,1},{5,4},{2,3},{7,6},{8,9},{13,12},{10,11},{15,14},{16,17},{21,... | collective-permute-start | bytes 1179656 | tf_op jit(solution)/shard_map/ppermute | solution.py:118
  63.4 14.1 %collective-permute-start.11 = (bf16[128,1536]{1,0:T(8,128)(2,1)}, bf16[128,1536]{1,0:T(8,128)(2,1)S(1)}, u32[]{:S(2)}, u32[]{:S(2)}) collective-permute-start(bf16[128,1536]{1,0:T(8,128)(2,1)} %collective-permute-done.10), channel_id=1, source_target_pairs={{0,1},{5,4},{2,3},{7,6},{8,9},{13,12},{10,11},{15,14},{16,17},{21,... | collective-permute-start | bytes 1179656 | tf_op jit(solution)/shard_map/ppermute | solution.py:118
  82.8 3.7 %collective-permute-start.15 = (f32[2,512]{1,0:T(2,128)S(1)}, f32[2,512]{1,0:T(2,128)S(1)}, u32[]{:S(2)}, u32[]{:S(2)}) collective-permute-start(f32[2,512]{1,0:T(2,128)S(1)} %maximum_add_fusion), channel_id=1, source_target_pairs={{0,1},{1,0},{2,3},{3,2},{4,5},{5,4},{6,7},{7,6},{8,9},{9,8},{10,11... | collective-permute-start | bytes 12296 | tf_op jit(solution)/shard_map/ppermute | solution.py:27
  87.6 5.0 %collective-permute-start.16 = (bf16[512,128]{1,0:T(8,128)(2,1)S(1)}, bf16[512,128]{1,0:T(8,128)(2,1)S(1)}, u32[]{:S(2)}, u32[]{:S(2)}) collective-permute-start(bf16[512,128]{1,0:T(8,128)(2,1)S(1)} %pad_maximum_fusion.5), channel_id=1, source_target_pairs={{0,1},{5,4},{4,0},{1,5},{2,3},{7,6},{6,2},{3,7},{8,9},{13,12},{12,... | collective-permute-start | bytes 393224 | tf_op jit(solution)/shard_map/ppermute | solution.py:172
  87.6 8.3 %collective-permute-start.19 = (bf16[512,128]{1,0:T(8,128)(2,1)S(1)}, bf16[512,128]{1,0:T(8,128)(2,1)S(1)}, u32[]{:S(2)}, u32[]{:S(2)}) collective-permute-start(bf16[512,128]{1,0:T(8,128)(2,1)S(1)} %pad_maximum_fusion.5), channel_id=1, source_target_pairs={{4,1},{1,4},{6,3},{3,6},{12,9},{9,12},{14,11},{11,14},{20,17},{17,... | collective-permute-start | bytes 393224 | tf_op jit(solution)/shard_map/ppermute | solution.py:173
  92.6 12.2 %collective-permute-start.17 = (bf16[512,384]{1,0:T(8,128)(2,1)S(1)}, bf16[512,384]{1,0:T(8,128)(2,1)S(1)}, u32[]{:S(2)}, u32[]{:S(2)}) collective-permute-start(bf16[512,384]{1,0:T(8,128)(2,1)S(1)} %pad_maximum_fusion.2), channel_id=1, source_target_pairs={{0,1},{5,4},{4,0},{1,5},{2,3},{7,6},{6,2},{3,7},{8,9},{13,12},{12,... | collective-permute-start | bytes 1179656 | tf_op jit(solution)/shard_map/ppermute | solution.py:172
  92.6 14.8 %collective-permute-start.18 = (bf16[512,384]{1,0:T(8,128)(2,1)S(1)}, bf16[512,384]{1,0:T(8,128)(2,1)S(1)}, u32[]{:S(2)}, u32[]{:S(2)}) collective-permute-start(bf16[512,384]{1,0:T(8,128)(2,1)S(1)} %pad_maximum_fusion.2), channel_id=1, source_target_pairs={{4,1},{1,4},{6,3},{3,6},{12,9},{9,12},{14,11},{11,14},{20,17},{17,... | collective-permute-start | bytes 1179656 | tf_op jit(solution)/shard_map/ppermute | solution.py:173
  96.0 29.2 %collective-permute-start.20 = (bf16[512,1024]{1,0:T(8,128)(2,1)S(1)}, bf16[512,1024]{1,0:T(8,128)(2,1)S(1)}, u32[]{:S(2)}, u32[]{:S(2)}) collective-permute-start(bf16[512,1024]{1,0:T(8,128)(2,1)S(1)} %pad_maximum_fusion), channel_id=1, source_target_pairs={{0,1},{5,4},{4,0},{1,5},{2,3},{7,6},{6,2},{3,7},{8,9},{13,12},{12,... | collective-permute-start | bytes 3145736 | tf_op jit(solution)/shard_map/ppermute | solution.py:172
  96.0 30.8 %collective-permute-start.21 = (bf16[512,1024]{1,0:T(8,128)(2,1)S(1)}, bf16[512,1024]{1,0:T(8,128)(2,1)S(1)}, u32[]{:S(2)}, u32[]{:S(2)}) collective-permute-start(bf16[512,1024]{1,0:T(8,128)(2,1)S(1)} %pad_maximum_fusion), channel_id=1, source_target_pairs={{4,1},{1,4},{6,3},{3,6},{12,9},{9,12},{14,11},{11,14},{20,17},{17,... | collective-permute-start | bytes 3145736 | tf_op jit(solution)/shard_map/ppermute | solution.py:173
  101.0 13.0 %collective-permute-start.22 = (bf16[1536,128]{1,0:T(8,128)(2,1)S(1)}, bf16[1536,128]{1,0:T(8,128)(2,1)S(1)}, u32[]{:S(2)}, u32[]{:S(2)}) collective-permute-start(bf16[1536,128]{1,0:T(8,128)(2,1)S(1)} %fusion.62), channel_id=1, source_target_pairs={{0,8},{24,16},{1,9},{25,17},{2,10},{26,18},{3,11},{27,19},{4,12},{... | collective-permute-start | bytes 1179656 | tf_op jit(solution)/shard_map/ppermute | solution.py:52
  109.0 15.4 %collective-permute-start.24 = (bf16[1536,128]{1,0:T(8,128)(2,1)S(1)}, bf16[1536,128]{1,0:T(8,128)(2,1)S(1)}, u32[]{:S(2)}, u32[]{:S(2)}) collective-permute-start(bf16[1536,128]{1,0:T(8,128)(2,1)S(1)} %fusion.63), channel_id=1, source_target_pairs={{0,8},{24,16},{1,9},{25,17},{2,10},{26,18},{3,11},{27,19},{4,12},{... | collective-permute-start | bytes 1179656 | tf_op jit(solution)/shard_map/ppermute | solution.py:52
  114.2 11.0 %collective-permute-start.23 = (bf16[1536,128]{1,0:T(8,128)(2,1)S(1)}, bf16[1536,128]{1,0:T(8,128)(2,1)S(1)}, u32[]{:S(2)}, u32[]{:S(2)}) collective-permute-start(bf16[1536,128]{1,0:T(8,128)(2,1)S(1)} %add_convert_fusion.35), channel_id=1, source_target_pairs={{8,16},{16,8},{9,17},{17,9},{10,18},{18,10},{11,19},{19,11},{12,20... | collective-permute-start | bytes 1179656 | tf_op jit(solution)/shard_map/ppermute | solution.py:60
  117.1 15.9 %collective-permute-start.27 = (bf16[1536,128]{1,0:T(8,128)(2,1)S(1)}, bf16[1536,128]{1,0:T(8,128)(2,1)S(1)}, u32[]{:S(2)}, u32[]{:S(2)}) collective-permute-start(bf16[1536,128]{1,0:T(8,128)(2,1)S(1)} %slice.505), channel_id=1, source_target_pairs={{0,8},{24,16},{1,9},{25,17},{2,10},{26,18},{3,11},{27,19},{4,12},{... | collective-permute-start | bytes 1179656 | tf_op jit(solution)/shard_map/ppermute | solution.py:52
  124.5 11.6 %collective-permute-start.26 = (bf16[1536,128]{1,0:T(8,128)(2,1)S(1)}, bf16[1536,128]{1,0:T(8,128)(2,1)S(1)}, u32[]{:S(2)}, u32[]{:S(2)}) collective-permute-start(bf16[1536,128]{1,0:T(8,128)(2,1)S(1)} %add_convert_fusion.34), channel_id=1, source_target_pairs={{8,16},{16,8},{9,17},{17,9},{10,18},{18,10},{11,19},{19,11},{12,20... | collective-permute-start | bytes 1179656 | tf_op jit(solution)/shard_map/ppermute | solution.py:60
  127.3 14.9 %collective-permute-start.25 = (bf16[1536,128]{1,0:T(8,128)(2,1)S(1)}, bf16[1536,128]{1,0:T(8,128)(2,1)S(1)}, u32[]{:S(2)}, u32[]{:S(2)}) collective-permute-start(bf16[1536,128]{1,0:T(8,128)(2,1)S(1)} %fusion.88), channel_id=1, source_target_pairs={{0,8},{24,16},{8,0},{16,24},{1,9},{25,17},{9,1},{17,25},{2,10},{26... | collective-permute-start | bytes 1179656 | tf_op jit(solution)/shard_map/ppermute | solution.py:52
  135.3 7.7 %collective-permute-start.28 = (bf16[1536,128]{1,0:T(8,128)(2,1)S(1)}, bf16[1536,128]{1,0:T(8,128)(2,1)S(1)}, u32[]{:S(2)}, u32[]{:S(2)}) collective-permute-start(bf16[1536,128]{1,0:T(8,128)(2,1)S(1)} %add_convert_fusion.32), channel_id=1, source_target_pairs={{8,16},{16,8},{9,17},{17,9},{10,18},{18,10},{11,19},{19,11},{12,20... | collective-permute-start | bytes 1179656 | tf_op jit(solution)/shard_map/ppermute | solution.py:60
  136.2 14.6 %collective-permute-start.29 = (bf16[1536,128]{1,0:T(8,128)(2,1)S(1)}, bf16[1536,128]{1,0:T(8,128)(2,1)S(1)}, u32[]{:S(2)}, u32[]{:S(2)}) collective-permute-start(bf16[1536,128]{1,0:T(8,128)(2,1)S(1)} %fusion.89), channel_id=1, source_target_pairs={{0,8},{24,16},{8,0},{16,24},{1,9},{25,17},{9,1},{17,25},{2,10},{26... | collective-permute-start | bytes 1179656 | tf_op jit(solution)/shard_map/ppermute | solution.py:52
  142.3 9.3 %collective-permute-start.30 = (bf16[1536,128]{1,0:T(8,128)(2,1)S(1)}, bf16[1536,128]{1,0:T(8,128)(2,1)S(1)}, u32[]{:S(2)}, u32[]{:S(2)}) collective-permute-start(bf16[1536,128]{1,0:T(8,128)(2,1)S(1)} %add_convert_fusion.30), channel_id=1, source_target_pairs={{8,16},{16,8},{9,17},{17,9},{10,18},{18,10},{11,19},{19,11},{12,20... | collective-permute-start | bytes 1179656 | tf_op jit(solution)/shard_map/ppermute | solution.py:60
  143.2 15.9 %collective-permute-start.31 = (bf16[1536,128]{1,0:T(8,128)(2,1)S(1)}, bf16[1536,128]{1,0:T(8,128)(2,1)S(1)}, u32[]{:S(2)}, u32[]{:S(2)}) collective-permute-start(bf16[1536,128]{1,0:T(8,128)(2,1)S(1)} %fusion.90), channel_id=1, source_target_pairs={{0,8},{24,16},{8,0},{16,24},{1,9},{25,17},{9,1},{17,25},{2,10},{26... | collective-permute-start | bytes 1179656 | tf_op jit(solution)/shard_map/ppermute | solution.py:52
  151.0 13.0 %collective-permute-start.32 = (bf16[1536,128]{1,0:T(8,128)(2,1)S(1)}, bf16[1536,128]{1,0:T(8,128)(2,1)S(1)}, u32[]{:S(2)}, u32[]{:S(2)}) collective-permute-start(bf16[1536,128]{1,0:T(8,128)(2,1)S(1)} %add_convert_fusion.28), channel_id=1, source_target_pairs={{8,16},{16,8},{9,17},{17,9},{10,18},{18,10},{11,19},{19,11},{12,20... | collective-permute-start | bytes 1179656 | tf_op jit(solution)/shard_map/ppermute | solution.py:60
  151.8 16.9 %collective-permute-start.33 = (bf16[1536,128]{1,0:T(8,128)(2,1)S(1)}, bf16[1536,128]{1,0:T(8,128)(2,1)S(1)}, u32[]{:S(2)}, u32[]{:S(2)}) collective-permute-start(bf16[1536,128]{1,0:T(8,128)(2,1)S(1)} %fusion.91), channel_id=1, source_target_pairs={{0,8},{24,16},{8,0},{16,24},{1,9},{25,17},{9,1},{17,25},{2,10},{26... | collective-permute-start | bytes 1179656 | tf_op jit(solution)/shard_map/ppermute | solution.py:52
  159.2 10.4 %collective-permute-start.34 = (bf16[1536,128]{1,0:T(8,128)(2,1)S(1)}, bf16[1536,128]{1,0:T(8,128)(2,1)S(1)}, u32[]{:S(2)}, u32[]{:S(2)}) collective-permute-start(bf16[1536,128]{1,0:T(8,128)(2,1)S(1)} %add_convert_fusion.26), channel_id=1, source_target_pairs={{8,16},{16,8},{9,17},{17,9},{10,18},{18,10},{11,19},{19,11},{12,20... | collective-permute-start | bytes 1179656 | tf_op jit(solution)/shard_map/ppermute | solution.py:60
  164.1 15.4 %collective-permute-start.35 = (bf16[1536,128]{1,0:T(8,128)(2,1)S(1)}, bf16[1536,128]{1,0:T(8,128)(2,1)S(1)}, u32[]{:S(2)}, u32[]{:S(2)}) collective-permute-start(bf16[1536,128]{1,0:T(8,128)(2,1)S(1)} %fusion.92), channel_id=1, source_target_pairs={{0,8},{24,16},{8,0},{16,24},{1,9},{25,17},{9,1},{17,25},{2,10},{26... | collective-permute-start | bytes 1179656 | tf_op jit(solution)/shard_map/ppermute | solution.py:52
  168.9 11.4 %collective-permute-start.36 = (bf16[1536,128]{1,0:T(8,128)(2,1)S(1)}, bf16[1536,128]{1,0:T(8,128)(2,1)S(1)}, u32[]{:S(2)}, u32[]{:S(2)}) collective-permute-start(bf16[1536,128]{1,0:T(8,128)(2,1)S(1)} %add_convert_fusion.24), channel_id=1, source_target_pairs={{8,16},{16,8},{9,17},{17,9},{10,18},{18,10},{11,19},{19,11},{12,20... | collective-permute-start | bytes 1179656 | tf_op jit(solution)/shard_map/ppermute | solution.py:60
  169.8 16.4 %collective-permute-start.37 = (bf16[1536,128]{1,0:T(8,128)(2,1)S(1)}, bf16[1536,128]{1,0:T(8,128)(2,1)S(1)}, u32[]{:S(2)}, u32[]{:S(2)}) collective-permute-start(bf16[1536,128]{1,0:T(8,128)(2,1)S(1)} %fusion.93), channel_id=1, source_target_pairs={{0,8},{24,16},{8,0},{16,24},{1,9},{25,17},{9,1},{17,25},{2,10},{26... | collective-permute-start | bytes 1179656 | tf_op jit(solution)/shard_map/ppermute | solution.py:52
  179.6 7.9 %collective-permute-start.38 = (bf16[1536,128]{1,0:T(8,128)(2,1)S(1)}, bf16[1536,128]{1,0:T(8,128)(2,1)S(1)}, u32[]{:S(2)}, u32[]{:S(2)}) collective-permute-start(bf16[1536,128]{1,0:T(8,128)(2,1)S(1)} %add_convert_fusion.22), channel_id=1, source_target_pairs={{8,16},{16,8},{9,17},{17,9},{10,18},{18,10},{11,19},{19,11},{12,20... | collective-permute-start | bytes 1179656 | tf_op jit(solution)/shard_map/ppermute | solution.py:60
  180.5 14.5 %collective-permute-start.39 = (bf16[1536,128]{1,0:T(8,128)(2,1)S(1)}, bf16[1536,128]{1,0:T(8,128)(2,1)S(1)}, u32[]{:S(2)}, u32[]{:S(2)}) collective-permute-start(bf16[1536,128]{1,0:T(8,128)(2,1)S(1)} %fusion.94), channel_id=1, source_target_pairs={{0,8},{24,16},{8,0},{16,24},{1,9},{25,17},{9,1},{17,25},{2,10},{26... | collective-permute-start | bytes 1179656 | tf_op jit(solution)/shard_map/ppermute | solution.py:52
  186.3 9.5 %collective-permute-start.40 = (bf16[1536,128]{1,0:T(8,128)(2,1)S(1)}, bf16[1536,128]{1,0:T(8,128)(2,1)S(1)}, u32[]{:S(2)}, u32[]{:S(2)}) collective-permute-start(bf16[1536,128]{1,0:T(8,128)(2,1)S(1)} %add_convert_fusion.20), channel_id=1, source_target_pairs={{8,16},{16,8},{9,17},{17,9},{10,18},{18,10},{11,19},{19,11},{12,20... | collective-permute-start | bytes 1179656 | tf_op jit(solution)/shard_map/ppermute | solution.py:60
  187.7 15.2 %collective-permute-start.41 = (bf16[1536,128]{1,0:T(8,128)(2,1)S(1)}, bf16[1536,128]{1,0:T(8,128)(2,1)S(1)}, u32[]{:S(2)}, u32[]{:S(2)}) collective-permute-start(bf16[1536,128]{1,0:T(8,128)(2,1)S(1)} %fusion.95), channel_id=1, source_target_pairs={{0,8},{24,16},{8,0},{16,24},{1,9},{25,17},{9,1},{17,25},{2,10},{26... | collective-permute-start | bytes 1179656 | tf_op jit(solution)/shard_map/ppermute | solution.py:52
  195.1 8.6 %collective-permute-start.42 = (bf16[1536,128]{1,0:T(8,128)(2,1)S(1)}, bf16[1536,128]{1,0:T(8,128)(2,1)S(1)}, u32[]{:S(2)}, u32[]{:S(2)}) collective-permute-start(bf16[1536,128]{1,0:T(8,128)(2,1)S(1)} %add_convert_fusion.18), channel_id=1, source_target_pairs={{8,16},{16,8},{9,17},{17,9},{10,18},{18,10},{11,19},{19,11},{12,20... | collective-permute-start | bytes 1179656 | tf_op jit(solution)/shard_map/ppermute | solution.py:60
  196.0 15.4 %collective-permute-start.43 = (bf16[1536,128]{1,0:T(8,128)(2,1)S(1)}, bf16[1536,128]{1,0:T(8,128)(2,1)S(1)}, u32[]{:S(2)}, u32[]{:S(2)}) collective-permute-start(bf16[1536,128]{1,0:T(8,128)(2,1)S(1)} %fusion.96), channel_id=1, source_target_pairs={{0,8},{24,16},{8,0},{16,24},{1,9},{25,17},{9,1},{17,25},{2,10},{26... | collective-permute-start | bytes 1179656 | tf_op jit(solution)/shard_map/ppermute | solution.py:52
  203.0 9.7 %collective-permute-start.44 = (bf16[1536,128]{1,0:T(8,128)(2,1)S(1)}, bf16[1536,128]{1,0:T(8,128)(2,1)S(1)}, u32[]{:S(2)}, u32[]{:S(2)}) collective-permute-start(bf16[1536,128]{1,0:T(8,128)(2,1)S(1)} %add_convert_fusion.16), channel_id=1, source_target_pairs={{8,16},{16,8},{9,17},{17,9},{10,18},{18,10},{11,19},{19,11},{12,20... | collective-permute-start | bytes 1179656 | tf_op jit(solution)/shard_map/ppermute | solution.py:60
  203.8 16.0 %collective-permute-start.45 = (bf16[1536,128]{1,0:T(8,128)(2,1)S(1)}, bf16[1536,128]{1,0:T(8,128)(2,1)S(1)}, u32[]{:S(2)}, u32[]{:S(2)}) collective-permute-start(bf16[1536,128]{1,0:T(8,128)(2,1)S(1)} %add_convert_fusion.15), channel_id=1, source_target_pairs={{8,0},{16,24},{9,1},{17,25},{10,2},{18,26},{11,3},{19,27},{12,4},{... | collective-permute-start | bytes 1179656 | tf_op jit(solution)/shard_map/ppermute | solution.py:52
  211.5 8.3 %collective-permute-start.46 = (bf16[1536,128]{1,0:T(8,128)(2,1)S(1)}, bf16[1536,128]{1,0:T(8,128)(2,1)S(1)}, u32[]{:S(2)}, u32[]{:S(2)}) collective-permute-start(bf16[1536,128]{1,0:T(8,128)(2,1)S(1)} %add_convert_fusion.14), channel_id=1, source_target_pairs={{8,16},{16,8},{9,17},{17,9},{10,18},{18,10},{11,19},{19,11},{12,20... | collective-permute-start | bytes 1179656 | tf_op jit(solution)/shard_map/ppermute | solution.py:60
  212.8 15.0 %collective-permute-start.47 = (bf16[1536,128]{1,0:T(8,128)(2,1)S(1)}, bf16[1536,128]{1,0:T(8,128)(2,1)S(1)}, u32[]{:S(2)}, u32[]{:S(2)}) collective-permute-start(bf16[1536,128]{1,0:T(8,128)(2,1)S(1)} %add_convert_fusion.13), channel_id=1, source_target_pairs={{8,0},{16,24},{9,1},{17,25},{10,2},{18,26},{11,3},{19,27},{12,4},{... | collective-permute-start | bytes 1179656 | tf_op jit(solution)/shard_map/ppermute | solution.py:52
  219.9 12.0 %collective-permute-start.48 = (bf16[1536,128]{1,0:T(8,128)(2,1)S(1)}, bf16[1536,128]{1,0:T(8,128)(2,1)S(1)}, u32[]{:S(2)}, u32[]{:S(2)}) collective-permute-start(bf16[1536,128]{1,0:T(8,128)(2,1)S(1)} %add_convert_fusion.12), channel_id=1, source_target_pairs={{8,0},{16,24},{9,1},{17,25},{10,2},{18,26},{11,3},{19,27},{12,4},{... | collective-permute-start | bytes 1179656 | tf_op jit(solution)/shard_map/ppermute | solution.py:52
  (20 other events, 216.5 us)

commit v14 on v13

--- a/solution.py
+++ b/solution.py
@@ -119,17 +119,21 @@
 
     gain_part = lax.dynamic_slice_in_dim(gain, t * (width // 2) + low * cols, cols).astype(f32)
 
+    ready = [
+        lax.optimization_barrier((res.astype(f32), gain_part[None, :] * cot.astype(f32)))
+        for res, cot in zip(residual_parts, cotangent_parts)
+    ]
     hidden, weighted, sums = [], [], []
     for k in range(group * pieces):
         r, p = k // pieces, k % pieces
         span, long_span = slice(p * rows, (p + 1) * rows), slice(k * rows, (k + 1) * rows)
-        res, cot, came = residual_parts[r], cotangent_parts[r], passed[k]
+        came = passed[k]
         if sums:
             came, sums[-1] = together(came, sums[-1])
         keep = jnp.where(near, near_out[long_span], far_outs[k])
         came = jnp.where(near, near_came[long_span], came)
-        h = res[span].astype(f32) + keep.astype(f32) + came.astype(f32)
-        w = gain_part[None, :] * cot[span].astype(f32)
+        h = ready[r][0][span] + keep.astype(f32) + came.astype(f32)
+        w = ready[r][1][span]
         hidden.append(h)
         weighted.append(w)
         sums.append(jnp.stack([jnp.sum(h * h, axis=-1), jnp.sum(h * w, axis=-1)]))
@@ -180,8 +184,8 @@
     def add_pseudo(d_all, lo, hi, after=None):
         at_cols = slice(lo * narrow, hi * narrow)
         piece = d_all[:, : (hi - lo) * narrow]
-        if after in line.sums:
-            piece, line.sums[after] = together(piece, line.sums[after])
+        if after in line.paid:
+            piece, line.paid[after] = together(piece, line.paid[after])
         piece, first, second, outer = together(piece, first_moment, second_moment, weight)
         grad = lax.dot_general(
             context_all, piece, (((0,), (0,)), ((), ())), preferred_element_type=f32
@@ -213,7 +217,7 @@
         for s in range(units + 3):
             while todo and todo[0][0] - 3 <= s:
                 lo, hi = todo.pop(0)
-                add_pseudo(last[:, (lo - early) * narrow :], lo, hi, s - 1)
+                add_pseudo(last[:, (lo - early) * narrow :], lo, hi, s + 1)
             line.step(s)
         sums = [line.totals[k] for k in range(units)]
     else:

time: 239 us -> 247 us (1.033)
  waiting for transfers between devices: 75.6 us -> 87 us
  starting transfers between devices: 102 us -> 108 us
  other arithmetic: 18.2 us -> 14.2 us
  local copies, waits for them, and re-layouts: 15 us -> 11.7 us
  matrix products: 25.7 us -> 23 us
    ppermute x15, starting transfers between devices: 67.1 us -> 74.7 us  [send_outer(): self.edge[s] = lax.ppermute(payload, 'island', pairs)]
    ppermute x4, waiting for transfers between devices: 5.41 us -> 12.6 us  [body(): lax.ppermute(out, ('fsdp', 'tp'), outward_pairs)]
    ppermute x11, waiting for transfers between devices: 33.4 us -> 39.9 us  [swap(): return lax.ppermute(value, axis, [(i, i ^ bit) for i in range(count)])]
    reduce_sum x4, other arithmetic: 7.19 us -> 1.64 us  [body(): sums.append(jnp.stack([jnp.sum(h * h, axis=-1), jnp.sum(h * w, axis=-1)]))]
    ppermute x1, waiting for transfers between devices: 3.73 us -> 0.01 us  [body(): near_came = lax.ppermute(near_out, ('fsdp', 'tp'), inward_pairs)]
    unnamed x41 -> x29, local copies, waits for them, and re-layouts: 11.6 us -> 8.11 us
    ppermute x15, waiting for transfers between devices: 27.1 us -> 30.4 us  [send_outer(): self.edge[s] = lax.ppermute(payload, 'island', pairs)]
    unnamed x27 -> x26, other arithmetic: 5.01 us -> 4.91 us
  transfers between devices with their start and end apart: 49 -> 49, of which waited for: 19 -> 16; matrix products, arithmetic and copies ran while one was open for 20% -> 17% of each run, Pallas kernels for 0% -> 0%
where the time goes in v14:
time: 247 us; the launch traced here: 246 us
  starting transfers between devices  108 us (44%)
  waiting for transfers between devices  87 us (35%)
  matrix products  23 us (9%)
  other arithmetic  14.2 us (6%)
  local copies, waits for them, and re-layouts  11.7 us (5%)
    ppermute x15, starting transfers between devices, send_outer(): self.edge[s] = lax.ppermute(payload, 'island', pairs)  74.7 us
    ppermute x11, waiting for transfers between devices, swap(): return lax.ppermute(value, axis, [(i, i ^ bit) for i in range(count)])  39.9 us
    ppermute x15, waiting for transfers between devices, send_outer(): self.edge[s] = lax.ppermute(payload, 'island', pairs)  30.4 us
    dot_general x7, matrix products, add_pseudo(): lax.dot_general(context_all, piece, (((0,), (0,)), ((), ())), preferred_e...  13.9 us
    ppermute x4, waiting for transfers between devices, body(): lax.ppermute(out, ('fsdp', 'tp'), outward_pairs)  12.6 us
    ppermute x3, starting transfers between devices, move(): crosses.append(lax.ppermute(d_local, ('fsdp', 'tp'), cross_pairs))  10.2 us
    dot_general x3, matrix products, project(): jnp.dot(block, weight, preferred_element_type=f32).astype(bf16)  9.14 us
    ppermute x12, starting transfers between devices, step(): self.mid[s] = lax.ppermute(self.sums[s], 'island', [(1, 2), (2, 1)])  8.58 us
  transfers between devices with their start and end apart: 49, of which 16 were waited for; matrix products, arithmetic and copies ran while one was open for 17% of the time, Pallas kernels for 0%

profile of v14, /device:TPU:2, one launch (start us, length us, event | category | flops | bytes accessed | tf_op | source)
XLA Modules:
  0.0 246.1 jit_solution(14239224580280790884)
XLA Ops:
  0.6 1.6 collective-permute-start
  2.2 2.5 %constant_dynamic-slice_fusion.2 = (bf16[256,1536]{1,0:T(8,128)(2,1)}, bf16[256,1536]{1,0:T(8,128)(2,1)S(1)}) fusion(bf16[256,3072]{1,0:T(8,128)(2,1)} %param.9, s32[]{:T(128)S(6)} %select_n.187, s32[]{:T(128)S(6)} %select_n.186), kind=kLoop, calls=%fused_computation.274 | loop fusion | bytes 3145736 | tf_op jit(solution)/shard_map/dynamic_slice | solution.py:105
  7.0 13.3 %collective-permute-done = bf16[256,1536]{1,0:T(8,128)(2,1)} collective-permute-done((bf16[256,1536]{1,0:T(8,128)(2,1)}, bf16[256,1536]{1,0:T(8,128)(2,1)}, u32[]{:S(2)}, u32[]{:S(2)}) %collective-permute-start) | collective-permute-done | bytes 786464 | tf_op jit(solution)/shard_map/ppermute | solution.py:27
  20.4 4.0 %convolution_convert_fusion.2 = bf16[256,1536]{1,0:T(8,128)(2,1)S(1)} fusion(bf16[256,1536]{1,0:T(8,128)(2,1)} %collective-permute-done, bf16[1536,1536]{1,0:T(8,128)(2,1)} %param.12), kind=kOutput, calls=%fused_computation.8 | convolution fusion | flops 1208352768 | bytes 6291456 | tf_op jit(solution)/shard_map/dot_general | solution.py:89
  24.4 1.6 collective-permute-start.3
  26.6 3.8 %convolution_convert_fusion = bf16[512,1536]{1,0:T(8,128)(2,1)S(1)} fusion(bf16[1536,1536]{1,0:T(8,128)(2,1)S(1)} %bitcast.206, bf16[256,1536]{1,0:T(8,128)(2,1)} %collective-permute-done.5, bf16[256,1536]{1,0:T(8,128)(2,1)S(1)} %copy-done.1), kind=kOutput, calls=%fused_computation | convolution fusion | flops 2419851264 | bytes 7864320 | tf_op jit(solution)/shard_map/dot_general | solution.py:89
  30.3 2.3 collective-permute-start.7
  32.6 11.8 %collective-permute-done.6 = bf16[128,1536]{1,0:T(8,128)(2,1)S(1)} collective-permute-done((bf16[128,1536]{1,0:T(8,128)(2,1)S(1)}, bf16[128,1536]{1,0:T(8,128)(2,1)S(1)}, u32[]{:S(2)}, u32[]{:S(2)}) %collective-permute-start.6) | collective-permute-done | bytes 393248 | tf_op jit(solution)/shard_map/ppermute | solution.py:27
  45.7 1.4 convolution_convert_fusion.1
  47.2 2.8 %collective-permute-start.10 = (bf16[128,1536]{1,0:T(8,128)(2,1)S(1)}, bf16[128,1536]{1,0:T(8,128)(2,1)S(1)}, u32[]{:S(2)}, u32[]{:S(2)}) collective-permute-start(bf16[128,1536]{1,0:T(8,128)(2,1)S(1)} %get-tuple-element.310), channel_id=1, source_target_pairs={{0,4},{2,6},{4,0},{6,2},{1,5},{3,7},{5,1},{7,3},{8,12},{10,14},{12... | collective-permute-start | bytes 1179656 | tf_op jit(solution)/shard_map/ppermute | solution.py:27
  50.4 1.3 convert_element_type.447
  54.4 5.5 %collective-permute-done.10 = bf16[128,1536]{1,0:T(8,128)(2,1)S(1)} collective-permute-done((bf16[128,1536]{1,0:T(8,128)(2,1)S(1)}, bf16[128,1536]{1,0:T(8,128)(2,1)S(1)}, u32[]{:S(2)}, u32[]{:S(2)}) %collective-permute-start.10) | collective-permute-done | bytes 393248 | tf_op jit(solution)/shard_map/ppermute | solution.py:27
  61.2 5.8 %collective-permute-done.12 = bf16[128,1536]{1,0:T(8,128)(2,1)S(1)} collective-permute-done((bf16[128,1536]{1,0:T(8,128)(2,1)S(1)}, bf16[128,1536]{1,0:T(8,128)(2,1)S(1)}, u32[]{:S(2)}, u32[]{:S(2)}) %collective-permute-start.12) | collective-permute-done | bytes 393248 | tf_op jit(solution)/shard_map/ppermute | solution.py:27
  69.2 6.3 %collective-permute-done.11 = bf16[128,1536]{1,0:T(8,128)(2,1)S(1)} collective-permute-done((bf16[128,1536]{1,0:T(8,128)(2,1)S(1)}, bf16[128,1536]{1,0:T(8,128)(2,1)S(1)}, u32[]{:S(2)}, u32[]{:S(2)}) %collective-permute-start.11) | collective-permute-done | bytes 393248 | tf_op jit(solution)/shard_map/ppermute | solution.py:118
  75.9 6.3 %collective-permute-done.13 = bf16[128,1536]{1,0:T(8,128)(2,1)S(1)} collective-permute-done((bf16[128,1536]{1,0:T(8,128)(2,1)S(1)}, bf16[128,1536]{1,0:T(8,128)(2,1)S(1)}, u32[]{:S(2)}, u32[]{:S(2)}) %collective-permute-start.13) | collective-permute-done | bytes 393248 | tf_op jit(solution)/shard_map/ppermute | solution.py:118
  84.2 3.5 %collective-permute-done.15 = f32[2,512]{1,0:T(2,128)S(1)} collective-permute-done((f32[2,512]{1,0:T(2,128)S(1)}, f32[2,512]{1,0:T(2,128)S(1)}, u32[]{:S(2)}, u32[]{:S(2)}) %collective-permute-start.15) | collective-permute-done | bytes 4128 | tf_op jit(solution)/shard_map/ppermute | solution.py:27
  88.6 3.5 %collective-permute-start.19 = (bf16[512,128]{1,0:T(8,128)(2,1)S(1)}, bf16[512,128]{1,0:T(8,128)(2,1)S(1)}, u32[]{:S(2)}, u32[]{:S(2)}) collective-permute-start(bf16[512,128]{1,0:T(8,128)(2,1)S(1)} %pad_maximum_fusion.5), channel_id=1, source_target_pairs={{4,1},{1,4},{6,3},{3,6},{12,9},{9,12},{14,11},{11,14},{20,17},{17,... | collective-permute-start | bytes 393224 | tf_op jit(solution)/shard_map/ppermute | solution.py:177
  93.7 3.4 %collective-permute-start.18 = (bf16[512,384]{1,0:T(8,128)(2,1)S(1)}, bf16[512,384]{1,0:T(8,128)(2,1)S(1)}, u32[]{:S(2)}, u32[]{:S(2)}) collective-permute-start(bf16[512,384]{1,0:T(8,128)(2,1)S(1)} %pad_maximum_fusion.2), channel_id=1, source_target_pairs={{4,1},{1,4},{6,3},{3,6},{12,9},{9,12},{14,11},{11,14},{20,17},{17,... | collective-permute-start | bytes 1179656 | tf_op jit(solution)/shard_map/ppermute | solution.py:177
  97.1 3.4 %collective-permute-start.25 = (bf16[512,1024]{1,0:T(8,128)(2,1)S(1)}, bf16[512,1024]{1,0:T(8,128)(2,1)S(1)}, u32[]{:S(2)}, u32[]{:S(2)}) collective-permute-start(bf16[512,1024]{1,0:T(8,128)(2,1)S(1)} %pad_maximum_fusion), channel_id=1, source_target_pairs={{4,1},{1,4},{6,3},{3,6},{12,9},{9,12},{14,11},{11,14},{20,17},{17,... | collective-permute-start | bytes 3145736 | tf_op jit(solution)/shard_map/ppermute | solution.py:177
  100.6 1.5 fusion.62
  102.1 3.7 %collective-permute-start.20 = (bf16[1536,128]{1,0:T(8,128)(2,1)S(1)}, bf16[1536,128]{1,0:T(8,128)(2,1)S(1)}, u32[]{:S(2)}, u32[]{:S(2)}) collective-permute-start(bf16[1536,128]{1,0:T(8,128)(2,1)S(1)} %fusion.62), channel_id=1, source_target_pairs={{0,8},{24,16},{1,9},{25,17},{2,10},{26,18},{3,11},{27,19},{4,12},{... | collective-permute-start | bytes 1179656 | tf_op jit(solution)/shard_map/ppermute | solution.py:52
  105.8 2.7 %collective-permute-done.18 = bf16[512,384]{1,0:T(8,128)(2,1)S(1)} collective-permute-done((bf16[512,384]{1,0:T(8,128)(2,1)S(1)}, bf16[512,384]{1,0:T(8,128)(2,1)S(1)}, u32[]{:S(2)}, u32[]{:S(2)}) %collective-permute-start.18) | collective-permute-done | bytes 393248 | tf_op jit(solution)/shard_map/ppermute | solution.py:177
  108.7 1.5 fusion.63
  110.1 3.5 %collective-permute-start.22 = (bf16[1536,128]{1,0:T(8,128)(2,1)S(1)}, bf16[1536,128]{1,0:T(8,128)(2,1)S(1)}, u32[]{:S(2)}, u32[]{:S(2)}) collective-permute-start(bf16[1536,128]{1,0:T(8,128)(2,1)S(1)} %fusion.63), channel_id=1, source_target_pairs={{0,8},{24,16},{1,9},{25,17},{2,10},{26,18},{3,11},{27,19},{4,12},{... | collective-permute-start | bytes 1179656 | tf_op jit(solution)/shard_map/ppermute | solution.py:52
  113.6 1.5 collective-permute-done.20
  115.2 2.2 fusion.33
  118.2 2.3 collective-permute-done.22
  121.4 11.7 %collective-permute-start.23 = (bf16[1536,128]{1,0:T(8,128)(2,1)S(1)}, bf16[1536,128]{1,0:T(8,128)(2,1)S(1)}, u32[]{:S(2)}, u32[]{:S(2)}) collective-permute-start(bf16[1536,128]{1,0:T(8,128)(2,1)S(1)} %get-tuple-element.184), channel_id=1, source_target_pairs={{0,8},{24,16},{8,0},{16,24},{1,9},{25,17},{9,1},{17,25},{2,10},{26... | collective-permute-start | bytes 1179656 | tf_op jit(solution)/shard_map/ppermute | solution.py:52
  133.2 1.9 collective-permute-start.27
  135.5 2.2 fusion.34
  137.7 10.0 %collective-permute-done.27 = bf16[1536,128]{1,0:T(8,128)(2,1)S(1)} collective-permute-done((bf16[1536,128]{1,0:T(8,128)(2,1)S(1)}, bf16[1536,128]{1,0:T(8,128)(2,1)S(1)}, u32[]{:S(2)}, u32[]{:S(2)}) %collective-permute-start.27) | collective-permute-done | bytes 393248 | tf_op jit(solution)/shard_map/ppermute | solution.py:52
  148.6 5.8 %collective-permute-start.29 = (bf16[1536,128]{1,0:T(8,128)(2,1)S(1)}, bf16[1536,128]{1,0:T(8,128)(2,1)S(1)}, u32[]{:S(2)}, u32[]{:S(2)}) collective-permute-start(bf16[1536,128]{1,0:T(8,128)(2,1)S(1)} %fusion.89), channel_id=1, source_target_pairs={{0,8},{24,16},{8,0},{16,24},{1,9},{25,17},{9,1},{17,25},{2,10},{26... | collective-permute-start | bytes 1179656 | tf_op jit(solution)/shard_map/ppermute | solution.py:52
  155.4 2.2 fusion.35
  157.8 6.1 %collective-permute-start.31 = (bf16[1536,128]{1,0:T(8,128)(2,1)S(1)}, bf16[1536,128]{1,0:T(8,128)(2,1)S(1)}, u32[]{:S(2)}, u32[]{:S(2)}) collective-permute-start(bf16[1536,128]{1,0:T(8,128)(2,1)S(1)} %fusion.90), channel_id=1, source_target_pairs={{0,8},{24,16},{8,0},{16,24},{1,9},{25,17},{9,1},{17,25},{2,10},{26... | collective-permute-start | bytes 1179656 | tf_op jit(solution)/shard_map/ppermute | solution.py:52
  165.6 6.8 %collective-permute-start.33 = (bf16[1536,128]{1,0:T(8,128)(2,1)S(1)}, bf16[1536,128]{1,0:T(8,128)(2,1)S(1)}, u32[]{:S(2)}, u32[]{:S(2)}) collective-permute-start(bf16[1536,128]{1,0:T(8,128)(2,1)S(1)} %fusion.91), channel_id=1, source_target_pairs={{0,8},{24,16},{8,0},{16,24},{1,9},{25,17},{9,1},{17,25},{2,10},{26... | collective-permute-start | bytes 1179656 | tf_op jit(solution)/shard_map/ppermute | solution.py:52
  172.3 2.2 fusion.36
  176.0 4.8 %collective-permute-start.35 = (bf16[1536,128]{1,0:T(8,128)(2,1)S(1)}, bf16[1536,128]{1,0:T(8,128)(2,1)S(1)}, u32[]{:S(2)}, u32[]{:S(2)}) collective-permute-start(bf16[1536,128]{1,0:T(8,128)(2,1)S(1)} %fusion.92), channel_id=1, source_target_pairs={{0,8},{24,16},{8,0},{16,24},{1,9},{25,17},{9,1},{17,25},{2,10},{26... | collective-permute-start | bytes 1179656 | tf_op jit(solution)/shard_map/ppermute | solution.py:52
  182.2 7.1 %collective-permute-start.37 = (bf16[1536,128]{1,0:T(8,128)(2,1)S(1)}, bf16[1536,128]{1,0:T(8,128)(2,1)S(1)}, u32[]{:S(2)}, u32[]{:S(2)}) collective-permute-start(bf16[1536,128]{1,0:T(8,128)(2,1)S(1)} %fusion.93), channel_id=1, source_target_pairs={{0,8},{24,16},{8,0},{16,24},{1,9},{25,17},{9,1},{17,25},{2,10},{26... | collective-permute-start | bytes 1179656 | tf_op jit(solution)/shard_map/ppermute | solution.py:52
  190.3 7.4 %collective-permute-start.39 = (bf16[1536,128]{1,0:T(8,128)(2,1)S(1)}, bf16[1536,128]{1,0:T(8,128)(2,1)S(1)}, u32[]{:S(2)}, u32[]{:S(2)}) collective-permute-start(bf16[1536,128]{1,0:T(8,128)(2,1)S(1)} %fusion.94), channel_id=1, source_target_pairs={{0,8},{24,16},{8,0},{16,24},{1,9},{25,17},{9,1},{17,25},{2,10},{26... | collective-permute-start | bytes 1179656 | tf_op jit(solution)/shard_map/ppermute | solution.py:52
  197.8 2.2 fusion.37
  201.9 4.3 %collective-permute-start.41 = (bf16[1536,128]{1,0:T(8,128)(2,1)S(1)}, bf16[1536,128]{1,0:T(8,128)(2,1)S(1)}, u32[]{:S(2)}, u32[]{:S(2)}) collective-permute-start(bf16[1536,128]{1,0:T(8,128)(2,1)S(1)} %fusion.95), channel_id=1, source_target_pairs={{0,8},{24,16},{8,0},{16,24},{1,9},{25,17},{9,1},{17,25},{2,10},{26... | collective-permute-start | bytes 1179656 | tf_op jit(solution)/shard_map/ppermute | solution.py:52
  207.6 7.6 %collective-permute-start.43 = (bf16[1536,128]{1,0:T(8,128)(2,1)S(1)}, bf16[1536,128]{1,0:T(8,128)(2,1)S(1)}, u32[]{:S(2)}, u32[]{:S(2)}) collective-permute-start(bf16[1536,128]{1,0:T(8,128)(2,1)S(1)} %fusion.96), channel_id=1, source_target_pairs={{0,8},{24,16},{8,0},{16,24},{1,9},{25,17},{9,1},{17,25},{2,10},{26... | collective-permute-start | bytes 1179656 | tf_op jit(solution)/shard_map/ppermute | solution.py:52
  218.3 3.2 %collective-permute-done.43 = bf16[1536,128]{1,0:T(8,128)(2,1)S(1)} collective-permute-done((bf16[1536,128]{1,0:T(8,128)(2,1)S(1)}, bf16[1536,128]{1,0:T(8,128)(2,1)S(1)}, u32[]{:S(2)}, u32[]{:S(2)}) %collective-permute-start.43) | collective-permute-done | bytes 393248 | tf_op jit(solution)/shard_map/ppermute | solution.py:52
  223.8 5.7 %collective-permute-done.45 = bf16[1536,128]{1,0:T(8,128)(2,1)S(1)} collective-permute-done((bf16[1536,128]{1,0:T(8,128)(2,1)S(1)}, bf16[1536,128]{1,0:T(8,128)(2,1)S(1)}, u32[]{:S(2)}, u32[]{:S(2)}) %collective-permute-start.45) | collective-permute-done | bytes 393248 | tf_op jit(solution)/shard_map/ppermute | solution.py:52
  231.4 2.3 collective-permute-done.47
  234.6 5.4 %collective-permute-done.48 = bf16[1536,128]{1,0:T(8,128)(2,1)S(1)} collective-permute-done((bf16[1536,128]{1,0:T(8,128)(2,1)S(1)}, bf16[1536,128]{1,0:T(8,128)(2,1)S(1)}, u32[]{:S(2)}, u32[]{:S(2)}) %collective-permute-start.48) | collective-permute-done | bytes 393248 | tf_op jit(solution)/shard_map/ppermute | solution.py:52
  240.5 3.4 %copy-done.2 = f32[1536,1536]{1,0:T(8,128)} copy-done((f32[1536,1536]{1,0:T(8,128)}, f32[1536,1536]{1,0:T(8,128)S(1)}, u32[]{:S(2)}) %copy-start.2) | copy-done | bytes 9437208
  243.9 2.2 copy-done.3
  (178 shorter events, 37.1 us)
Async XLA Ops:
  0.6 19.7 %collective-permute-start = (bf16[256,1536]{1,0:T(8,128)(2,1)}, bf16[256,1536]{1,0:T(8,128)(2,1)}, u32[]{:S(2)}, u32[]{:S(2)}) collective-permute-start(bf16[256,1536]{1,0:T(8,128)(2,1)} %param.8), channel_id=1, source_target_pairs={{0,4},{2,6},{4,0},{6,2},{1,5},{3,7},{5,1},{7,3},{8,12},{10,14},{12... | collective-permute-start | bytes 2359304 | tf_op jit(solution)/shard_map/ppermute | solution.py:27
  4.7 15.6 %collective-permute-start.1 = (bf16[256,1536]{1,0:T(8,128)(2,1)}, bf16[256,1536]{1,0:T(8,128)(2,1)}, u32[]{:S(2)}, u32[]{:S(2)}) collective-permute-start(bf16[256,1536]{1,0:T(8,128)(2,1)} %get-tuple-element.302), channel_id=1, source_target_pairs={{0,2},{2,0},{4,6},{6,4},{1,3},{3,1},{5,7},{7,5},{8,10},{10,8},{12,... | collective-permute-start | bytes 2359304 | tf_op jit(solution)/shard_map/ppermute | solution.py:27
  5.7 14.6 %collective-permute-start.2 = (bf16[256,1536]{1,0:T(8,128)(2,1)}, bf16[256,1536]{1,0:T(8,128)(2,1)S(1)}, u32[]{:S(2)}, u32[]{:S(2)}) collective-permute-start(bf16[256,1536]{1,0:T(8,128)(2,1)} %get-tuple-element.300), channel_id=1, source_target_pairs={{0,2},{2,0},{4,6},{6,4},{1,3},{3,1},{5,7},{7,5},{8,10},{10,8},{12,... | collective-permute-start | bytes 2359304 | tf_op jit(solution)/shard_map/ppermute | solution.py:27
  6.2 20.4 %collective-permute-start.5 = (bf16[256,1536]{1,0:T(8,128)(2,1)S(1)}, bf16[256,1536]{1,0:T(8,128)(2,1)}, u32[]{:S(2)}, u32[]{:S(2)}) collective-permute-start(bf16[256,1536]{1,0:T(8,128)(2,1)S(1)} %copy-done.1), channel_id=1, source_target_pairs={{0,2},{2,0},{4,6},{6,4},{1,3},{3,1},{5,7},{7,5},{8,10},{10,8},{12,... | collective-permute-start | bytes 2359304 | tf_op jit(solution)/shard_map/ppermute | solution.py:27
  20.3 25.4 %collective-permute-start.9 = (bf16[256,1536]{1,0:T(8,128)(2,1)}, bf16[256,1536]{1,0:T(8,128)(2,1)S(1)}, u32[]{:S(2)}, u32[]{:S(2)}) collective-permute-start(bf16[256,1536]{1,0:T(8,128)(2,1)} %collective-permute-done), channel_id=1, source_target_pairs={{0,2},{2,0},{4,6},{6,4},{1,3},{3,1},{5,7},{7,5},{8,10},{10,8},{12,... | collective-permute-start | bytes 2359304 | tf_op jit(solution)/shard_map/ppermute | solution.py:27
  24.4 28.7 %collective-permute-start.3 = (bf16[128,1536]{1,0:T(8,128)(2,1)S(1)}, bf16[128,1536]{1,0:T(8,128)(2,1)S(1)}, u32[]{:S(2)}, u32[]{:S(2)}) collective-permute-start(bf16[128,1536]{1,0:T(8,128)(2,1)S(1)} %get-tuple-element.309), channel_id=1, source_target_pairs={{0,4},{2,6},{4,0},{6,2},{1,5},{3,7},{5,1},{7,3},{8,12},{10,14},{12... | collective-permute-start | bytes 1179656 | tf_op jit(solution)/shard_map/ppermute | solution.py:27
  26.0 18.4 %collective-permute-start.6 = (bf16[128,1536]{1,0:T(8,128)(2,1)S(1)}, bf16[128,1536]{1,0:T(8,128)(2,1)S(1)}, u32[]{:S(2)}, u32[]{:S(2)}) collective-permute-start(bf16[128,1536]{1,0:T(8,128)(2,1)S(1)} %get-tuple-element.308), channel_id=1, source_target_pairs={{0,4},{2,6},{4,0},{6,2},{1,5},{3,7},{5,1},{7,3},{8,12},{10,14},{12... | collective-permute-start | bytes 1179656 | tf_op jit(solution)/shard_map/ppermute | solution.py:27
  30.3 38.0 %collective-permute-start.7 = (bf16[512,1536]{1,0:T(8,128)(2,1)S(1)}, bf16[512,1536]{1,0:T(8,128)(2,1)S(1)}, u32[]{:S(2)}, u32[]{:S(2)}) collective-permute-start(bf16[512,1536]{1,0:T(8,128)(2,1)S(1)} %convolution_convert_fusion), channel_id=1, source_target_pairs={{4,5},{1,0},{6,7},{3,2},{12,13},{9,8},{14,15},{11,10},{20,21},{17,... | collective-permute-start | bytes 4718600 | tf_op jit(solution)/shard_map/ppermute | solution.py:113
  44.4 23.9 %collective-permute-start.8 = (bf16[128,1536]{1,0:T(8,128)(2,1)S(1)}, bf16[128,1536]{1,0:T(8,128)(2,1)S(1)}, u32[]{:S(2)}, u32[]{:S(2)}) collective-permute-start(bf16[128,1536]{1,0:T(8,128)(2,1)S(1)} %collective-permute-done.6), channel_id=1, source_target_pairs={{0,1},{5,4},{2,3},{7,6},{8,9},{13,12},{10,11},{15,14},{16,17},{21,... | collective-permute-start | bytes 1179656 | tf_op jit(solution)/shard_map/ppermute | solution.py:118
  47.2 12.8 %collective-permute-start.10 = (bf16[128,1536]{1,0:T(8,128)(2,1)S(1)}, bf16[128,1536]{1,0:T(8,128)(2,1)S(1)}, u32[]{:S(2)}, u32[]{:S(2)}) collective-permute-start(bf16[128,1536]{1,0:T(8,128)(2,1)S(1)} %get-tuple-element.310), channel_id=1, source_target_pairs={{0,4},{2,6},{4,0},{6,2},{1,5},{3,7},{5,1},{7,3},{8,12},{10,14},{12... | collective-permute-start | bytes 1179656 | tf_op jit(solution)/shard_map/ppermute | solution.py:27
  49.9 17.1 %collective-permute-start.12 = (bf16[128,1536]{1,0:T(8,128)(2,1)S(1)}, bf16[128,1536]{1,0:T(8,128)(2,1)S(1)}, u32[]{:S(2)}, u32[]{:S(2)}) collective-permute-start(bf16[128,1536]{1,0:T(8,128)(2,1)S(1)} %get-tuple-element.311), channel_id=1, source_target_pairs={{0,4},{2,6},{4,0},{6,2},{1,5},{3,7},{5,1},{7,3},{8,12},{10,14},{12... | collective-permute-start | bytes 1179656 | tf_op jit(solution)/shard_map/ppermute | solution.py:27
  53.1 15.6 %collective-permute-start.4 = (bf16[128,1536]{1,0:T(8,128)(2,1)S(1)}, bf16[128,1536]{1,0:T(8,128)(2,1)S(1)}, u32[]{:S(2)}, u32[]{:S(2)}) collective-permute-start(bf16[128,1536]{1,0:T(8,128)(2,1)S(1)} %collective-permute-done.3), channel_id=1, source_target_pairs={{0,1},{5,4},{2,3},{7,6},{8,9},{13,12},{10,11},{15,14},{16,17},{21,... | collective-permute-start | bytes 1179656 | tf_op jit(solution)/shard_map/ppermute | solution.py:118
  59.9 15.6 %collective-permute-start.11 = (bf16[128,1536]{1,0:T(8,128)(2,1)S(1)}, bf16[128,1536]{1,0:T(8,128)(2,1)S(1)}, u32[]{:S(2)}, u32[]{:S(2)}) collective-permute-start(bf16[128,1536]{1,0:T(8,128)(2,1)S(1)} %collective-permute-done.10), channel_id=1, source_target_pairs={{0,1},{5,4},{2,3},{7,6},{8,9},{13,12},{10,11},{15,14},{16,17},{21,... | collective-permute-start | bytes 1179656 | tf_op jit(solution)/shard_map/ppermute | solution.py:118
  67.0 15.2 %collective-permute-start.13 = (bf16[128,1536]{1,0:T(8,128)(2,1)S(1)}, bf16[128,1536]{1,0:T(8,128)(2,1)S(1)}, u32[]{:S(2)}, u32[]{:S(2)}) collective-permute-start(bf16[128,1536]{1,0:T(8,128)(2,1)S(1)} %collective-permute-done.12), channel_id=1, source_target_pairs={{0,1},{5,4},{2,3},{7,6},{8,9},{13,12},{10,11},{15,14},{16,17},{21,... | collective-permute-start | bytes 1179656 | tf_op jit(solution)/shard_map/ppermute | solution.py:118
  84.0 3.7 %collective-permute-start.15 = (f32[2,512]{1,0:T(2,128)S(1)}, f32[2,512]{1,0:T(2,128)S(1)}, u32[]{:S(2)}, u32[]{:S(2)}) collective-permute-start(f32[2,512]{1,0:T(2,128)S(1)} %maximum_add_fusion), channel_id=1, source_target_pairs={{0,1},{1,0},{2,3},{3,2},{4,5},{5,4},{6,7},{7,6},{8,9},{9,8},{10,11... | collective-permute-start | bytes 12296 | tf_op jit(solution)/shard_map/ppermute | solution.py:27
  88.6 5.0 %collective-permute-start.16 = (bf16[512,128]{1,0:T(8,128)(2,1)S(1)}, bf16[512,128]{1,0:T(8,128)(2,1)S(1)}, u32[]{:S(2)}, u32[]{:S(2)}) collective-permute-start(bf16[512,128]{1,0:T(8,128)(2,1)S(1)} %pad_maximum_fusion.5), channel_id=1, source_target_pairs={{0,1},{5,4},{4,0},{1,5},{2,3},{7,6},{6,2},{3,7},{8,9},{13,12},{12,... | collective-permute-start | bytes 393224 | tf_op jit(solution)/shard_map/ppermute | solution.py:176
  88.6 8.4 %collective-permute-start.19 = (bf16[512,128]{1,0:T(8,128)(2,1)S(1)}, bf16[512,128]{1,0:T(8,128)(2,1)S(1)}, u32[]{:S(2)}, u32[]{:S(2)}) collective-permute-start(bf16[512,128]{1,0:T(8,128)(2,1)S(1)} %pad_maximum_fusion.5), channel_id=1, source_target_pairs={{4,1},{1,4},{6,3},{3,6},{12,9},{9,12},{14,11},{11,14},{20,17},{17,... | collective-permute-start | bytes 393224 | tf_op jit(solution)/shard_map/ppermute | solution.py:177
  93.6 12.2 %collective-permute-start.17 = (bf16[512,384]{1,0:T(8,128)(2,1)S(1)}, bf16[512,384]{1,0:T(8,128)(2,1)S(1)}, u32[]{:S(2)}, u32[]{:S(2)}) collective-permute-start(bf16[512,384]{1,0:T(8,128)(2,1)S(1)} %pad_maximum_fusion.2), channel_id=1, source_target_pairs={{0,1},{5,4},{4,0},{1,5},{2,3},{7,6},{6,2},{3,7},{8,9},{13,12},{12,... | collective-permute-start | bytes 1179656 | tf_op jit(solution)/shard_map/ppermute | solution.py:176
  93.7 14.8 %collective-permute-start.18 = (bf16[512,384]{1,0:T(8,128)(2,1)S(1)}, bf16[512,384]{1,0:T(8,128)(2,1)S(1)}, u32[]{:S(2)}, u32[]{:S(2)}) collective-permute-start(bf16[512,384]{1,0:T(8,128)(2,1)S(1)} %pad_maximum_fusion.2), channel_id=1, source_target_pairs={{4,1},{1,4},{6,3},{3,6},{12,9},{9,12},{14,11},{11,14},{20,17},{17,... | collective-permute-start | bytes 1179656 | tf_op jit(solution)/shard_map/ppermute | solution.py:177
  97.0 38.1 %collective-permute-start.24 = (bf16[512,1024]{1,0:T(8,128)(2,1)S(1)}, bf16[512,1024]{1,0:T(8,128)(2,1)S(1)}, u32[]{:S(2)}, u32[]{:S(2)}) collective-permute-start(bf16[512,1024]{1,0:T(8,128)(2,1)S(1)} %pad_maximum_fusion), channel_id=1, source_target_pairs={{0,1},{5,4},{4,0},{1,5},{2,3},{7,6},{6,2},{3,7},{8,9},{13,12},{12,... | collective-permute-start | bytes 3145736 | tf_op jit(solution)/shard_map/ppermute | solution.py:176
  97.1 38.0 %collective-permute-start.25 = (bf16[512,1024]{1,0:T(8,128)(2,1)S(1)}, bf16[512,1024]{1,0:T(8,128)(2,1)S(1)}, u32[]{:S(2)}, u32[]{:S(2)}) collective-permute-start(bf16[512,1024]{1,0:T(8,128)(2,1)S(1)} %pad_maximum_fusion), channel_id=1, source_target_pairs={{4,1},{1,4},{6,3},{3,6},{12,9},{9,12},{14,11},{11,14},{20,17},{17,... | collective-permute-start | bytes 3145736 | tf_op jit(solution)/shard_map/ppermute | solution.py:177
  102.1 13.0 %collective-permute-start.20 = (bf16[1536,128]{1,0:T(8,128)(2,1)S(1)}, bf16[1536,128]{1,0:T(8,128)(2,1)S(1)}, u32[]{:S(2)}, u32[]{:S(2)}) collective-permute-start(bf16[1536,128]{1,0:T(8,128)(2,1)S(1)} %fusion.62), channel_id=1, source_target_pairs={{0,8},{24,16},{1,9},{25,17},{2,10},{26,18},{3,11},{27,19},{4,12},{... | collective-permute-start | bytes 1179656 | tf_op jit(solution)/shard_map/ppermute | solution.py:52
  110.1 10.3 %collective-permute-start.22 = (bf16[1536,128]{1,0:T(8,128)(2,1)S(1)}, bf16[1536,128]{1,0:T(8,128)(2,1)S(1)}, u32[]{:S(2)}, u32[]{:S(2)}) collective-permute-start(bf16[1536,128]{1,0:T(8,128)(2,1)S(1)} %fusion.63), channel_id=1, source_target_pairs={{0,8},{24,16},{1,9},{25,17},{2,10},{26,18},{3,11},{27,19},{4,12},{... | collective-permute-start | bytes 1179656 | tf_op jit(solution)/shard_map/ppermute | solution.py:52
  117.5 3.8 %collective-permute-start.21 = (bf16[1536,128]{1,0:T(8,128)(2,1)S(1)}, bf16[1536,128]{1,0:T(8,128)(2,1)S(1)}, u32[]{:S(2)}, u32[]{:S(2)}) collective-permute-start(bf16[1536,128]{1,0:T(8,128)(2,1)S(1)} %add_convert_fusion.35), channel_id=1, source_target_pairs={{8,16},{16,8},{9,17},{17,9},{10,18},{18,10},{11,19},{19,11},{12,20... | collective-permute-start | bytes 1179656 | tf_op jit(solution)/shard_map/ppermute | solution.py:60
  120.6 27.9 %collective-permute-start.26 = (bf16[1536,128]{1,0:T(8,128)(2,1)S(1)}, bf16[1536,128]{1,0:T(8,128)(2,1)S(1)}, u32[]{:S(2)}, u32[]{:S(2)}) collective-permute-start(bf16[1536,128]{1,0:T(8,128)(2,1)S(1)} %add_convert_fusion.34), channel_id=1, source_target_pairs={{8,16},{16,8},{9,17},{17,9},{10,18},{18,10},{11,19},{19,11},{12,20... | collective-permute-start | bytes 1179656 | tf_op jit(solution)/shard_map/ppermute | solution.py:60
  121.4 33.0 %collective-permute-start.23 = (bf16[1536,128]{1,0:T(8,128)(2,1)S(1)}, bf16[1536,128]{1,0:T(8,128)(2,1)S(1)}, u32[]{:S(2)}, u32[]{:S(2)}) collective-permute-start(bf16[1536,128]{1,0:T(8,128)(2,1)S(1)} %get-tuple-element.184), channel_id=1, source_target_pairs={{0,8},{24,16},{8,0},{16,24},{1,9},{25,17},{9,1},{17,25},{2,10},{26... | collective-permute-start | bytes 1179656 | tf_op jit(solution)/shard_map/ppermute | solution.py:52
  133.2 14.5 %collective-permute-start.27 = (bf16[1536,128]{1,0:T(8,128)(2,1)S(1)}, bf16[1536,128]{1,0:T(8,128)(2,1)S(1)}, u32[]{:S(2)}, u32[]{:S(2)}) collective-permute-start(bf16[1536,128]{1,0:T(8,128)(2,1)S(1)} %get-tuple-element.306), channel_id=1, source_target_pairs={{0,8},{24,16},{1,9},{25,17},{2,10},{26,18},{3,11},{27,19},{4,12},{... | collective-permute-start | bytes 1179656 | tf_op jit(solution)/shard_map/ppermute | solution.py:52
  147.7 9.9 %collective-permute-start.28 = (bf16[1536,128]{1,0:T(8,128)(2,1)S(1)}, bf16[1536,128]{1,0:T(8,128)(2,1)S(1)}, u32[]{:S(2)}, u32[]{:S(2)}) collective-permute-start(bf16[1536,128]{1,0:T(8,128)(2,1)S(1)} %add_convert_fusion.32), channel_id=1, source_target_pairs={{8,16},{16,8},{9,17},{17,9},{10,18},{18,10},{11,19},{19,11},{12,20... | collective-permute-start | bytes 1179656 | tf_op jit(solution)/shard_map/ppermute | solution.py:60
  148.6 15.3 %collective-permute-start.29 = (bf16[1536,128]{1,0:T(8,128)(2,1)S(1)}, bf16[1536,128]{1,0:T(8,128)(2,1)S(1)}, u32[]{:S(2)}, u32[]{:S(2)}) collective-permute-start(bf16[1536,128]{1,0:T(8,128)(2,1)S(1)} %fusion.89), channel_id=1, source_target_pairs={{0,8},{24,16},{8,0},{16,24},{1,9},{25,17},{9,1},{17,25},{2,10},{26... | collective-permute-start | bytes 1179656 | tf_op jit(solution)/shard_map/ppermute | solution.py:52
  154.6 10.8 %collective-permute-start.30 = (bf16[1536,128]{1,0:T(8,128)(2,1)S(1)}, bf16[1536,128]{1,0:T(8,128)(2,1)S(1)}, u32[]{:S(2)}, u32[]{:S(2)}) collective-permute-start(bf16[1536,128]{1,0:T(8,128)(2,1)S(1)} %add_convert_fusion.30), channel_id=1, source_target_pairs={{8,16},{16,8},{9,17},{17,9},{10,18},{18,10},{11,19},{19,11},{12,20... | collective-permute-start | bytes 1179656 | tf_op jit(solution)/shard_map/ppermute | solution.py:60
  157.8 17.2 %collective-permute-start.31 = (bf16[1536,128]{1,0:T(8,128)(2,1)S(1)}, bf16[1536,128]{1,0:T(8,128)(2,1)S(1)}, u32[]{:S(2)}, u32[]{:S(2)}) collective-permute-start(bf16[1536,128]{1,0:T(8,128)(2,1)S(1)} %fusion.90), channel_id=1, source_target_pairs={{0,8},{24,16},{8,0},{16,24},{1,9},{25,17},{9,1},{17,25},{2,10},{26... | collective-permute-start | bytes 1179656 | tf_op jit(solution)/shard_map/ppermute | solution.py:52
  164.0 11.8 %collective-permute-start.32 = (bf16[1536,128]{1,0:T(8,128)(2,1)S(1)}, bf16[1536,128]{1,0:T(8,128)(2,1)S(1)}, u32[]{:S(2)}, u32[]{:S(2)}) collective-permute-start(bf16[1536,128]{1,0:T(8,128)(2,1)S(1)} %add_convert_fusion.28), channel_id=1, source_target_pairs={{8,16},{16,8},{9,17},{17,9},{10,18},{18,10},{11,19},{19,11},{12,20... | collective-permute-start | bytes 1179656 | tf_op jit(solution)/shard_map/ppermute | solution.py:60
  165.6 15.2 %collective-permute-start.33 = (bf16[1536,128]{1,0:T(8,128)(2,1)S(1)}, bf16[1536,128]{1,0:T(8,128)(2,1)S(1)}, u32[]{:S(2)}, u32[]{:S(2)}) collective-permute-start(bf16[1536,128]{1,0:T(8,128)(2,1)S(1)} %fusion.91), channel_id=1, source_target_pairs={{0,8},{24,16},{8,0},{16,24},{1,9},{25,17},{9,1},{17,25},{2,10},{26... | collective-permute-start | bytes 1179656 | tf_op jit(solution)/shard_map/ppermute | solution.py:52
  175.1 6.9 %collective-permute-start.34 = (bf16[1536,128]{1,0:T(8,128)(2,1)S(1)}, bf16[1536,128]{1,0:T(8,128)(2,1)S(1)}, u32[]{:S(2)}, u32[]{:S(2)}) collective-permute-start(bf16[1536,128]{1,0:T(8,128)(2,1)S(1)} %add_convert_fusion.26), channel_id=1, source_target_pairs={{8,16},{16,8},{9,17},{17,9},{10,18},{18,10},{11,19},{19,11},{12,20... | collective-permute-start | bytes 1179656 | tf_op jit(solution)/shard_map/ppermute | solution.py:60
  176.0 13.3 %collective-permute-start.35 = (bf16[1536,128]{1,0:T(8,128)(2,1)S(1)}, bf16[1536,128]{1,0:T(8,128)(2,1)S(1)}, u32[]{:S(2)}, u32[]{:S(2)}) collective-permute-start(bf16[1536,128]{1,0:T(8,128)(2,1)S(1)} %fusion.92), channel_id=1, source_target_pairs={{0,8},{24,16},{8,0},{16,24},{1,9},{25,17},{9,1},{17,25},{2,10},{26... | collective-permute-start | bytes 1179656 | tf_op jit(solution)/shard_map/ppermute | solution.py:52
  180.9 9.2 %collective-permute-start.36 = (bf16[1536,128]{1,0:T(8,128)(2,1)S(1)}, bf16[1536,128]{1,0:T(8,128)(2,1)S(1)}, u32[]{:S(2)}, u32[]{:S(2)}) collective-permute-start(bf16[1536,128]{1,0:T(8,128)(2,1)S(1)} %add_convert_fusion.24), channel_id=1, source_target_pairs={{8,16},{16,8},{9,17},{17,9},{10,18},{18,10},{11,19},{19,11},{12,20... | collective-permute-start | bytes 1179656 | tf_op jit(solution)/shard_map/ppermute | solution.py:60
  182.2 18.7 %collective-permute-start.37 = (bf16[1536,128]{1,0:T(8,128)(2,1)S(1)}, bf16[1536,128]{1,0:T(8,128)(2,1)S(1)}, u32[]{:S(2)}, u32[]{:S(2)}) collective-permute-start(bf16[1536,128]{1,0:T(8,128)(2,1)S(1)} %fusion.93), channel_id=1, source_target_pairs={{0,8},{24,16},{8,0},{16,24},{1,9},{25,17},{9,1},{17,25},{2,10},{26... | collective-permute-start | bytes 1179656 | tf_op jit(solution)/shard_map/ppermute | solution.py:52
  189.4 12.3 %collective-permute-start.38 = (bf16[1536,128]{1,0:T(8,128)(2,1)S(1)}, bf16[1536,128]{1,0:T(8,128)(2,1)S(1)}, u32[]{:S(2)}, u32[]{:S(2)}) collective-permute-start(bf16[1536,128]{1,0:T(8,128)(2,1)S(1)} %add_convert_fusion.22), channel_id=1, source_target_pairs={{8,16},{16,8},{9,17},{17,9},{10,18},{18,10},{11,19},{19,11},{12,20... | collective-permute-start | bytes 1179656 | tf_op jit(solution)/shard_map/ppermute | solution.py:60
  190.3 15.9 %collective-permute-start.39 = (bf16[1536,128]{1,0:T(8,128)(2,1)S(1)}, bf16[1536,128]{1,0:T(8,128)(2,1)S(1)}, u32[]{:S(2)}, u32[]{:S(2)}) collective-permute-start(bf16[1536,128]{1,0:T(8,128)(2,1)S(1)} %fusion.94), channel_id=1, source_target_pairs={{0,8},{24,16},{8,0},{16,24},{1,9},{25,17},{9,1},{17,25},{2,10},{26... | collective-permute-start | bytes 1179656 | tf_op jit(solution)/shard_map/ppermute | solution.py:52
  201.0 6.4 %collective-permute-start.40 = (bf16[1536,128]{1,0:T(8,128)(2,1)S(1)}, bf16[1536,128]{1,0:T(8,128)(2,1)S(1)}, u32[]{:S(2)}, u32[]{:S(2)}) collective-permute-start(bf16[1536,128]{1,0:T(8,128)(2,1)S(1)} %add_convert_fusion.20), channel_id=1, source_target_pairs={{8,16},{16,8},{9,17},{17,9},{10,18},{18,10},{11,19},{19,11},{12,20... | collective-permute-start | bytes 1179656 | tf_op jit(solution)/shard_map/ppermute | solution.py:60
  201.9 13.3 %collective-permute-start.41 = (bf16[1536,128]{1,0:T(8,128)(2,1)S(1)}, bf16[1536,128]{1,0:T(8,128)(2,1)S(1)}, u32[]{:S(2)}, u32[]{:S(2)}) collective-permute-start(bf16[1536,128]{1,0:T(8,128)(2,1)S(1)} %fusion.95), channel_id=1, source_target_pairs={{0,8},{24,16},{8,0},{16,24},{1,9},{25,17},{9,1},{17,25},{2,10},{26... | collective-permute-start | bytes 1179656 | tf_op jit(solution)/shard_map/ppermute | solution.py:52
  206.3 9.7 %collective-permute-start.42 = (bf16[1536,128]{1,0:T(8,128)(2,1)S(1)}, bf16[1536,128]{1,0:T(8,128)(2,1)S(1)}, u32[]{:S(2)}, u32[]{:S(2)}) collective-permute-start(bf16[1536,128]{1,0:T(8,128)(2,1)S(1)} %add_convert_fusion.18), channel_id=1, source_target_pairs={{8,16},{16,8},{9,17},{17,9},{10,18},{18,10},{11,19},{19,11},{12,20... | collective-permute-start | bytes 1179656 | tf_op jit(solution)/shard_map/ppermute | solution.py:60
  207.6 13.9 %collective-permute-start.43 = (bf16[1536,128]{1,0:T(8,128)(2,1)S(1)}, bf16[1536,128]{1,0:T(8,128)(2,1)S(1)}, u32[]{:S(2)}, u32[]{:S(2)}) collective-permute-start(bf16[1536,128]{1,0:T(8,128)(2,1)S(1)} %fusion.96), channel_id=1, source_target_pairs={{0,8},{24,16},{8,0},{16,24},{1,9},{25,17},{9,1},{17,25},{2,10},{26... | collective-permute-start | bytes 1179656 | tf_op jit(solution)/shard_map/ppermute | solution.py:52
  215.3 7.1 %collective-permute-start.44 = (bf16[1536,128]{1,0:T(8,128)(2,1)S(1)}, bf16[1536,128]{1,0:T(8,128)(2,1)S(1)}, u32[]{:S(2)}, u32[]{:S(2)}) collective-permute-start(bf16[1536,128]{1,0:T(8,128)(2,1)S(1)} %add_convert_fusion.16), channel_id=1, source_target_pairs={{8,16},{16,8},{9,17},{17,9},{10,18},{18,10},{11,19},{19,11},{12,20... | collective-permute-start | bytes 1179656 | tf_op jit(solution)/shard_map/ppermute | solution.py:60
  216.1 13.3 %collective-permute-start.45 = (bf16[1536,128]{1,0:T(8,128)(2,1)S(1)}, bf16[1536,128]{1,0:T(8,128)(2,1)S(1)}, u32[]{:S(2)}, u32[]{:S(2)}) collective-permute-start(bf16[1536,128]{1,0:T(8,128)(2,1)S(1)} %add_convert_fusion.15), channel_id=1, source_target_pairs={{8,0},{16,24},{9,1},{17,25},{10,2},{18,26},{11,3},{19,27},{12,4},{... | collective-permute-start | bytes 1179656 | tf_op jit(solution)/shard_map/ppermute | solution.py:52
  221.7 8.3 %collective-permute-start.46 = (bf16[1536,128]{1,0:T(8,128)(2,1)S(1)}, bf16[1536,128]{1,0:T(8,128)(2,1)S(1)}, u32[]{:S(2)}, u32[]{:S(2)}) collective-permute-start(bf16[1536,128]{1,0:T(8,128)(2,1)S(1)} %add_convert_fusion.14), channel_id=1, source_target_pairs={{8,16},{16,8},{9,17},{17,9},{10,18},{18,10},{11,19},{19,11},{12,20... | collective-permute-start | bytes 1179656 | tf_op jit(solution)/shard_map/ppermute | solution.py:60
  222.5 11.2 %collective-permute-start.47 = (bf16[1536,128]{1,0:T(8,128)(2,1)S(1)}, bf16[1536,128]{1,0:T(8,128)(2,1)S(1)}, u32[]{:S(2)}, u32[]{:S(2)}) collective-permute-start(bf16[1536,128]{1,0:T(8,128)(2,1)S(1)} %add_convert_fusion.13), channel_id=1, source_target_pairs={{8,0},{16,24},{9,1},{17,25},{10,2},{18,26},{11,3},{19,27},{12,4},{... | collective-permute-start | bytes 1179656 | tf_op jit(solution)/shard_map/ppermute | solution.py:52
  230.1 10.0 %collective-permute-start.48 = (bf16[1536,128]{1,0:T(8,128)(2,1)S(1)}, bf16[1536,128]{1,0:T(8,128)(2,1)S(1)}, u32[]{:S(2)}, u32[]{:S(2)}) collective-permute-start(bf16[1536,128]{1,0:T(8,128)(2,1)S(1)} %add_convert_fusion.12), channel_id=1, source_target_pairs={{8,0},{16,24},{9,1},{17,25},{10,2},{18,26},{11,3},{19,27},{12,4},{... | collective-permute-start | bytes 1179656 | tf_op jit(solution)/shard_map/ppermute | solution.py:52
  (14 other events, 142.0 us)

commit v15 on v13

--- a/solution.py
+++ b/solution.py
@@ -1,6 +1,10 @@
+import functools
+
 import jax
 import jax.numpy as jnp
 from jax import lax
+from jax.experimental import pallas as pl
+from jax.experimental.pallas import tpu as pltpu
 from jax.sharding import PartitionSpec as P
 
 norm_eps = 1e-06
@@ -25,6 +29,55 @@
 def swap(value, axis, bit):
     count = lax.axis_size(axis)
     return lax.ppermute(value, axis, [(i, i ^ bit) for i in range(count)])
+
+
+def finish_kernel(count, start, narrow, islands, *refs):
+    totals, momentum = refs[:count], refs[count]
+    new_out, step_out, held, fresh, step, sems = refs[-6:]
+    columns = pl.ds(start, count * narrow)
+    load = pltpu.make_async_copy(momentum.at[:, columns], held, sems.at[0])
+    load.start()
+    load.wait()
+    for k in range(count):
+        at = slice(k * narrow, (k + 1) * narrow)
+        delta = totals[k][...].astype(f32) / islands
+        fresh[:, at], step[:, at] = outer_update(delta, held[:, at])
+    stores = [
+        pltpu.make_async_copy(fresh, new_out.at[:, columns], sems.at[1]),
+        pltpu.make_async_copy(step, step_out.at[:, columns], sems.at[2]),
+    ]
+    for store in stores:
+        store.start()
+    for store in stores:
+        store.wait()
+
+
+def finish(totals, start, islands, momentum, outputs):
+    rows, narrow = totals[0].shape
+    count = len(totals)
+    wide = count * narrow
+    in_hbm = pl.BlockSpec(memory_space=pltpu.HBM)
+    in_vmem = pl.BlockSpec(memory_space=pltpu.VMEM)
+    return pl.pallas_call(
+        functools.partial(finish_kernel, count, start, narrow, islands),
+        out_shape=(
+            jax.ShapeDtypeStruct(momentum.shape, f32),
+            jax.ShapeDtypeStruct(momentum.shape, bf16),
+        ),
+        in_specs=[in_vmem] * count + [in_hbm] * (1 + len(outputs)),
+        out_specs=(in_hbm, in_hbm),
+        scratch_shapes=[
+            pltpu.VMEM((rows, wide), f32),
+            pltpu.VMEM((rows, wide), f32),
+            pltpu.VMEM((rows, wide), bf16),
+            pltpu.SemaphoreType.DMA((3,)),
+        ],
+        input_output_aliases={count + 1 + k: k for k in range(len(outputs))},
+        compiler_params=pltpu.CompilerParams(vmem_limit_bytes=16 * 1024 * 1024),
+        cost_estimate=pl.CostEstimate(
+            flops=5 * rows * wide, bytes_accessed=12 * rows * wide, transcendentals=0
+        ),
+    )(*totals, momentum, *outputs)
 
 
 def together(*values):
@@ -220,14 +273,12 @@
         for lo, hi in todo:
             add_pseudo(last[:, (lo - early) * narrow :], lo, hi)
         sums = [lax.psum(part, "island") for part in parts]
-    momentum_out, step_out = [], []
-    for k, total in enumerate(sums):
-        cols_at = slice(k * narrow, (k + 1) * narrow)
-        delta = total.astype(f32) / islands
-        new_momentum, outer_step = outer_update(delta, momentum[:, cols_at])
-        momentum_out.append(new_momentum)
-        step_out.append(outer_step)
-    return (jnp.concatenate(momentum_out, axis=1), jnp.concatenate(step_out, axis=1))
+    ends = list(range(3, units - 3, 3)) + [units - 3, units - 1, units]
+    outputs, start = (), 0
+    for end in ends:
+        outputs = finish(sums[start:end], start * narrow, islands, momentum, outputs)
+        start = end
+    return outputs
 
 
 def solution(mesh):

time: 239 us -> 238 us (level); the launches traced: 238 us -> 234 us
  Pallas kernels: 0 us -> 11 us
  starting transfers between devices: 102 us -> 94.8 us
  local copies, waits for them, and re-layouts: 15 us -> 8.57 us
  other arithmetic: 18.2 us -> 13 us
  waiting for transfers between devices: 75.6 us -> 79.8 us
    pallas_call x0 -> x5, Pallas kernels: none -> 11 us  [finish(): pl.pallas_call(functools.partial(finish_kernel, count, start, narrow, isl...]
    ppermute x15, waiting for transfers between devices: 27.1 us -> 36 us  [send_outer(): self.edge[s] = lax.ppermute(payload, 'island', pairs)]
    ppermute x15, starting transfers between devices: 67.1 us -> 60 us  [send_outer(): self.edge[s] = lax.ppermute(payload, 'island', pairs)]
    unnamed x41 -> x37, local copies, waits for them, and re-layouts: 11.6 us -> 5.06 us
    unnamed x27 -> x5, other arithmetic: 5.01 us -> 0.01 us
    ppermute x3, waiting for transfers between devices: 4.35 us -> 1.48 us  [move(): crosses.append(lax.ppermute(d_local, ('fsdp', 'tp'), cross_pairs))]
  transfers between devices with their start and end apart: 49 -> 49, of which waited for: 19 -> 19; matrix products, arithmetic and copies ran while one was open for 20% -> 19% of each run, Pallas kernels for 0% -> 4%
where the time goes in v15:
time: 238 us; the launch traced here: 234 us
  starting transfers between devices  94.8 us (40%)
  waiting for transfers between devices  79.8 us (34%)
  matrix products  24.4 us (10%)
  other arithmetic  13 us (5%)
  Pallas kernels  11 us (5%)
  local copies, waits for them, and re-layouts  8.57 us (4%)
    ppermute x15, starting transfers between devices, send_outer(): self.edge[s] = lax.ppermute(payload, 'island', pairs)  60 us
    ppermute x15, waiting for transfers between devices, send_outer(): self.edge[s] = lax.ppermute(payload, 'island', pairs)  36 us
    ppermute x11, waiting for transfers between devices, swap(): return lax.ppermute(value, axis, [(i, i ^ bit) for i in range(count)])  33.4 us
    dot_general x7, matrix products, add_pseudo(): lax.dot_general(context_all, piece, (((0,), (0,)), ((), ())), preferred_e...  15 us
    pallas_call x5, Pallas kernels, finish(): pl.pallas_call(functools.partial(finish_kernel, count, start, narrow, isl...  11 us
    ppermute x3, starting transfers between devices, move(): crosses.append(lax.ppermute(d_local, ('fsdp', 'tp'), cross_pairs))  10.1 us
    dot_general x3, matrix products, project(): jnp.dot(block, weight, preferred_element_type=f32).astype(bf16)  9.49 us
    ppermute x12, starting transfers between devices, step(): self.mid[s] = lax.ppermute(self.sums[s], 'island', [(1, 2), (2, 1)])  8.58 us
  transfers between devices with their start and end apart: 49, of which 19 were waited for; matrix products, arithmetic and copies ran while one was open for 19% of the time, Pallas kernels for 4%

profile of v15, /device:TPU:2, one launch (start us, length us, event | category | flops | bytes accessed | tf_op | source)
XLA Modules:
  0.0 233.6 jit_solution(13319698569600055094)
XLA Ops:
  2.2 1.6 constant_dynamic-slice_fusion.2
  5.0 15.3 %collective-permute-done = bf16[256,1536]{1,0:T(8,128)(2,1)} collective-permute-done((bf16[256,1536]{1,0:T(8,128)(2,1)}, bf16[256,1536]{1,0:T(8,128)(2,1)}, u32[]{:S(2)}, u32[]{:S(2)}) %collective-permute-start) | collective-permute-done | bytes 786464 | tf_op jit(solution)/shard_map/ppermute | solution.py:31
  20.4 4.0 %convolution_convert_fusion.2 = bf16[256,1536]{1,0:T(8,128)(2,1)S(1)} fusion(bf16[256,1536]{1,0:T(8,128)(2,1)} %collective-permute-done, bf16[1536,1536]{1,0:T(8,128)(2,1)} %param.12), kind=kOutput, calls=%fused_computation.8 | convolution fusion | flops 1208352768 | bytes 6291456 | tf_op jit(solution)/shard_map/dot_general | solution.py:142
  26.7 4.1 %convolution_convert_fusion = bf16[512,1536]{1,0:T(8,128)(2,1)} fusion(bf16[1536,1536]{1,0:T(8,128)(2,1)S(1)} %bitcast.206, bf16[256,1536]{1,0:T(8,128)(2,1)S(1)} %collective-permute-done.5, bf16[256,1536]{1,0:T(8,128)(2,1)S(1)} %copy-done.1), kind=kOutput, calls=%fused_computation | convolution fusion | flops 2419851264 | bytes 7864320 | tf_op jit(solution)/shard_map/dot_general | solution.py:142
  30.8 3.6 %collective-permute-start.7 = (bf16[512,1536]{1,0:T(8,128)(2,1)}, bf16[512,1536]{1,0:T(8,128)(2,1)}, u32[]{:S(2)}, u32[]{:S(2)}) collective-permute-start(bf16[512,1536]{1,0:T(8,128)(2,1)} %convolution_convert_fusion), channel_id=1, source_target_pairs={{4,5},{1,0},{6,7},{3,2},{12,13},{9,8},{14,15},{11,10},{20,21},{17,... | collective-permute-start | bytes 4718600 | tf_op jit(solution)/shard_map/ppermute | solution.py:166
  34.4 2.3 collective-permute-done.6
  40.4 3.4 %collective-permute-start.10 = (bf16[128,1536]{1,0:T(8,128)(2,1)}, bf16[128,1536]{1,0:T(8,128)(2,1)}, u32[]{:S(2)}, u32[]{:S(2)}) collective-permute-start(bf16[128,1536]{1,0:T(8,128)(2,1)} %get-tuple-element.312), channel_id=1, source_target_pairs={{0,4},{2,6},{4,0},{6,2},{1,5},{3,7},{5,1},{7,3},{8,12},{10,14},{12... | collective-permute-start | bytes 1179656 | tf_op jit(solution)/shard_map/ppermute | solution.py:31
  45.5 2.1 constant_dynamic-update-slice_fusion.2
  48.9 6.3 %collective-permute-done.10 = bf16[128,1536]{1,0:T(8,128)(2,1)} collective-permute-done((bf16[128,1536]{1,0:T(8,128)(2,1)}, bf16[128,1536]{1,0:T(8,128)(2,1)}, u32[]{:S(2)}, u32[]{:S(2)}) %collective-permute-start.10) | collective-permute-done | bytes 393248 | tf_op jit(solution)/shard_map/ppermute | solution.py:31
  56.5 6.0 %collective-permute-done.12 = bf16[128,1536]{1,0:T(8,128)(2,1)S(1)} collective-permute-done((bf16[128,1536]{1,0:T(8,128)(2,1)}, bf16[128,1536]{1,0:T(8,128)(2,1)S(1)}, u32[]{:S(2)}, u32[]{:S(2)}) %collective-permute-start.12) | collective-permute-done | bytes 393248 | tf_op jit(solution)/shard_map/ppermute | solution.py:31
  63.7 3.9 %collective-permute-done.7 = bf16[512,1536]{1,0:T(8,128)(2,1)} collective-permute-done((bf16[512,1536]{1,0:T(8,128)(2,1)}, bf16[512,1536]{1,0:T(8,128)(2,1)}, u32[]{:S(2)}, u32[]{:S(2)}) %collective-permute-start.7) | collective-permute-done | bytes 1572896 | tf_op jit(solution)/shard_map/ppermute | solution.py:166
  67.6 1.8 multiply_reduce_fusion.7
  69.4 1.8 multiply_reduce_fusion.5
  71.2 1.7 multiply_reduce_fusion.3
  73.0 3.7 %collective-permute-done.13 = bf16[128,1536]{1,0:T(8,128)(2,1)S(1)} collective-permute-done((bf16[128,1536]{1,0:T(8,128)(2,1)S(1)}, bf16[128,1536]{1,0:T(8,128)(2,1)S(1)}, u32[]{:S(2)}, u32[]{:S(2)}) %collective-permute-start.13) | collective-permute-done | bytes 393248 | tf_op jit(solution)/shard_map/ppermute | solution.py:171
  76.7 1.6 multiply_reduce_fusion.1
  80.0 3.5 %collective-permute-done.15 = f32[2,512]{1,0:T(2,128)S(1)} collective-permute-done((f32[2,512]{1,0:T(2,128)S(1)}, f32[2,512]{1,0:T(2,128)S(1)}, u32[]{:S(2)}, u32[]{:S(2)}) %collective-permute-start.15) | collective-permute-done | bytes 4128 | tf_op jit(solution)/shard_map/ppermute | solution.py:31
  83.9 3.4 %collective-permute-start.16 = (bf16[512,128]{1,0:T(8,128)(2,1)S(1)}, bf16[512,128]{1,0:T(8,128)(2,1)S(1)}, u32[]{:S(2)}, u32[]{:S(2)}) collective-permute-start(bf16[512,128]{1,0:T(8,128)(2,1)S(1)} %pad_maximum_fusion.6), channel_id=1, source_target_pairs={{4,1},{1,4},{6,3},{3,6},{12,9},{9,12},{14,11},{11,14},{20,17},{17,... | collective-permute-start | bytes 393224 | tf_op jit(solution)/shard_map/ppermute | solution.py:226
  88.9 3.3 %collective-permute-start.22 = (bf16[512,384]{1,0:T(8,128)(2,1)S(1)}, bf16[512,384]{1,0:T(8,128)(2,1)S(1)}, u32[]{:S(2)}, u32[]{:S(2)}) collective-permute-start(bf16[512,384]{1,0:T(8,128)(2,1)S(1)} %pad_maximum_fusion.3), channel_id=1, source_target_pairs={{4,1},{1,4},{6,3},{3,6},{12,9},{9,12},{14,11},{11,14},{20,17},{17,... | collective-permute-start | bytes 1179656 | tf_op jit(solution)/shard_map/ppermute | solution.py:226
  92.3 3.4 %collective-permute-start.18 = (bf16[512,1024]{1,0:T(8,128)(2,1)S(1)}, bf16[512,1024]{1,0:T(8,128)(2,1)S(1)}, u32[]{:S(2)}, u32[]{:S(2)}) collective-permute-start(bf16[512,1024]{1,0:T(8,128)(2,1)S(1)} %pad_maximum_fusion), channel_id=1, source_target_pairs={{4,1},{1,4},{6,3},{3,6},{12,9},{9,12},{14,11},{11,14},{20,17},{17,... | collective-permute-start | bytes 3145736 | tf_op jit(solution)/shard_map/ppermute | solution.py:226
  95.9 2.6 %fusion.50 = bf16[1536,128]{1,0:T(8,128)(2,1)S(1)} fusion(bf16[1536,1536]{1,0:T(8,128)(2,1)S(1)} %bitcast.208, bf16[1,1536,1536]{2,1,0:T(8,128)(2,1)S(1)} %bitcast.210, bf16[1,1536,1536]{2,1,0:T(8,128)(2,1)} %param.13, bf16[1024,1536]{1,0:T(8,128)(2,1)S(1)} %constant_dynamic-update-slice_fusion, bf16[1024,128]{1,0:T(8,128)(2,1)S(1)} %pad_maximum_fusion.5), kind=kOutput, calls=%fused_computation.116 | convolution fusion | flops 406192128 | bytes 4980736 | tf_op jit(solution)/shard_map/dot_general | solution.py:239
  98.5 3.7 %collective-permute-start.20 = (bf16[1536,128]{1,0:T(8,128)(2,1)S(1)}, bf16[1536,128]{1,0:T(8,128)(2,1)S(1)}, u32[]{:S(2)}, u32[]{:S(2)}) collective-permute-start(bf16[1536,128]{1,0:T(8,128)(2,1)S(1)} %fusion.50), channel_id=1, source_target_pairs={{0,8},{24,16},{1,9},{25,17},{2,10},{26,18},{3,11},{27,19},{4,12},{... | collective-permute-start | bytes 1179656 | tf_op jit(solution)/shard_map/ppermute | solution.py:105
  104.5 2.2 fusion.34
  108.2 3.5 %collective-permute-start.25 = (bf16[1536,128]{1,0:T(8,128)(2,1)S(1)}, bf16[1536,128]{1,0:T(8,128)(2,1)S(1)}, u32[]{:S(2)}, u32[]{:S(2)}) collective-permute-start(bf16[1536,128]{1,0:T(8,128)(2,1)S(1)} %slice.459), channel_id=1, source_target_pairs={{0,8},{24,16},{1,9},{25,17},{2,10},{26,18},{3,11},{27,19},{4,12},{... | collective-permute-start | bytes 1179656 | tf_op jit(solution)/shard_map/ppermute | solution.py:105
  113.8 11.4 %collective-permute-done.23 = bf16[1536,128]{1,0:T(8,128)(2,1)S(1)} collective-permute-done((bf16[1536,128]{1,0:T(8,128)(2,1)S(1)}, bf16[1536,128]{1,0:T(8,128)(2,1)S(1)}, u32[]{:S(2)}, u32[]{:S(2)}) %collective-permute-start.23) | collective-permute-done | bytes 393248 | tf_op jit(solution)/shard_map/ppermute | solution.py:105
  126.3 2.2 fusion.33
  128.7 5.3 %collective-permute-start.28 = (bf16[1536,128]{1,0:T(8,128)(2,1)S(1)}, bf16[1536,128]{1,0:T(8,128)(2,1)S(1)}, u32[]{:S(2)}, u32[]{:S(2)}) collective-permute-start(bf16[1536,128]{1,0:T(8,128)(2,1)S(1)} %fusion.63), channel_id=1, source_target_pairs={{0,8},{24,16},{8,0},{16,24},{1,9},{25,17},{9,1},{17,25},{2,10},{26... | collective-permute-start | bytes 1179656 | tf_op jit(solution)/shard_map/ppermute | solution.py:105
  134.9 2.2 fusion.35
  137.2 6.1 %collective-permute-start.30 = (bf16[1536,128]{1,0:T(8,128)(2,1)S(1)}, bf16[1536,128]{1,0:T(8,128)(2,1)S(1)}, u32[]{:S(2)}, u32[]{:S(2)}) collective-permute-start(bf16[1536,128]{1,0:T(8,128)(2,1)S(1)} %fusion.64), channel_id=1, source_target_pairs={{0,8},{24,16},{8,0},{16,24},{1,9},{25,17},{9,1},{17,25},{2,10},{26... | collective-permute-start | bytes 1179656 | tf_op jit(solution)/shard_map/ppermute | solution.py:105
  144.6 4.9 %collective-permute-start.29 = (bf16[1536,128]{1,0:T(8,128)(2,1)S(1)}, bf16[1536,128]{1,0:T(8,128)(2,1)S(1)}, u32[]{:S(2)}, u32[]{:S(2)}) collective-permute-start(bf16[1536,128]{1,0:T(8,128)(2,1)S(1)} %fusion.65), channel_id=1, source_target_pairs={{0,8},{24,16},{8,0},{16,24},{1,9},{25,17},{9,1},{17,25},{2,10},{26... | collective-permute-start | bytes 1179656 | tf_op jit(solution)/shard_map/ppermute | solution.py:105
  149.6 3.3 %collective-permute-done.30 = bf16[1536,128]{1,0:T(8,128)(2,1)S(1)} collective-permute-done((bf16[1536,128]{1,0:T(8,128)(2,1)S(1)}, bf16[1536,128]{1,0:T(8,128)(2,1)S(1)}, u32[]{:S(2)}, u32[]{:S(2)}) %collective-permute-start.30) | collective-permute-done | bytes 393248 | tf_op jit(solution)/shard_map/ppermute | solution.py:105
  154.0 4.7 %collective-permute-start.33 = (bf16[1536,128]{1,0:T(8,128)(2,1)S(1)}, bf16[1536,128]{1,0:T(8,128)(2,1)S(1)}, u32[]{:S(2)}, u32[]{:S(2)}) collective-permute-start(bf16[1536,128]{1,0:T(8,128)(2,1)S(1)} %fusion.66), channel_id=1, source_target_pairs={{0,8},{24,16},{8,0},{16,24},{1,9},{25,17},{9,1},{17,25},{2,10},{26... | collective-permute-start | bytes 1179656 | tf_op jit(solution)/shard_map/ppermute | solution.py:105
  158.7 2.5 %collective-permute-done.29 = bf16[1536,128]{1,0:T(8,128)(2,1)S(1)} collective-permute-done((bf16[1536,128]{1,0:T(8,128)(2,1)S(1)}, bf16[1536,128]{1,0:T(8,128)(2,1)S(1)}, u32[]{:S(2)}, u32[]{:S(2)}) %collective-permute-start.29) | collective-permute-done | bytes 393248 | tf_op jit(solution)/shard_map/ppermute | solution.py:105
  161.4 2.2 fusion.37
  164.6 4.3 %collective-permute-start.36 = (bf16[1536,128]{1,0:T(8,128)(2,1)S(1)}, bf16[1536,128]{1,0:T(8,128)(2,1)S(1)}, u32[]{:S(2)}, u32[]{:S(2)}) collective-permute-start(bf16[1536,128]{1,0:T(8,128)(2,1)S(1)} %fusion.67), channel_id=1, source_target_pairs={{0,8},{24,16},{8,0},{16,24},{1,9},{25,17},{9,1},{17,25},{2,10},{26... | collective-permute-start | bytes 1179656 | tf_op jit(solution)/shard_map/ppermute | solution.py:105
  169.0 2.6 %shard_map.95 = (f32[1536,1536]{1,0:T(8,128)}, bf16[1536,1536]{1,0:T(8,128)(2,1)}) custom-call(bf16[1536,128]{1,0:T(8,128)(2,1)S(1)} %broadcast_select_fusion.6.refs_0_, bf16[1536,128]{1,0:T(8,128)(2,1)S(1)} %broadcast_select_fusion.5.refs_1_, bf16[1536,128]{1,0:T(8,128)(2,1)S(1)} %broadcast_select_fusion.4.refs_2_, f32[1536,1536]{1,0:T(8,128)S(1)} %bitcast.192), custom_call_target="tpu_custom_call" | custom-call | flops 2949120 | bytes 7077888 | tf_op jit(solution)/shard_map/pallas_call | solution.py:61
  172.6 5.4 %collective-permute-start.38 = (bf16[1536,128]{1,0:T(8,128)(2,1)S(1)}, bf16[1536,128]{1,0:T(8,128)(2,1)S(1)}, u32[]{:S(2)}, u32[]{:S(2)}) collective-permute-start(bf16[1536,128]{1,0:T(8,128)(2,1)S(1)} %fusion.68), channel_id=1, source_target_pairs={{0,8},{24,16},{8,0},{16,24},{1,9},{25,17},{9,1},{17,25},{2,10},{26... | collective-permute-start | bytes 1179656 | tf_op jit(solution)/shard_map/ppermute | solution.py:105
  178.0 2.2 fusion.36
  181.2 5.2 %collective-permute-start.40 = (bf16[1536,128]{1,0:T(8,128)(2,1)S(1)}, bf16[1536,128]{1,0:T(8,128)(2,1)S(1)}, u32[]{:S(2)}, u32[]{:S(2)}) collective-permute-start(bf16[1536,128]{1,0:T(8,128)(2,1)S(1)} %fusion.69), channel_id=1, source_target_pairs={{0,8},{24,16},{8,0},{16,24},{1,9},{25,17},{9,1},{17,25},{2,10},{26... | collective-permute-start | bytes 1179656 | tf_op jit(solution)/shard_map/ppermute | solution.py:105
  188.2 7.0 %collective-permute-start.39 = (bf16[1536,128]{1,0:T(8,128)(2,1)S(1)}, bf16[1536,128]{1,0:T(8,128)(2,1)S(1)}, u32[]{:S(2)}, u32[]{:S(2)}) collective-permute-start(bf16[1536,128]{1,0:T(8,128)(2,1)S(1)} %fusion.70), channel_id=1, source_target_pairs={{0,8},{24,16},{8,0},{16,24},{1,9},{25,17},{9,1},{17,25},{2,10},{26... | collective-permute-start | bytes 1179656 | tf_op jit(solution)/shard_map/ppermute | solution.py:105
  195.3 2.6 %shard_map.96 = (f32[1536,1536]{1,0:T(8,128)}, bf16[1536,1536]{1,0:T(8,128)(2,1)}) custom-call(bf16[1536,128]{1,0:T(8,128)(2,1)S(1)} %broadcast_select_fusion.9.refs_0_, bf16[1536,128]{1,0:T(8,128)(2,1)S(1)} %broadcast_select_fusion.8.refs_1_, bf16[1536,128]{1,0:T(8,128)(2,1)S(1)} %broadcast_select_fusion.7.refs_2_, ...), custom_call_target="tpu_custom_call", output_to_operand_aliasing={{0}: (4, {}), {1}: (5, {})} | custom-call | flops 2949120 | bytes 7077888 | tf_op jit(solution)/shard_map/pallas_call | solution.py:61
  198.9 4.8 %collective-permute-start.43 = (bf16[1536,128]{1,0:T(8,128)(2,1)S(1)}, bf16[1536,128]{1,0:T(8,128)(2,1)S(1)}, u32[]{:S(2)}, u32[]{:S(2)}) collective-permute-start(bf16[1536,128]{1,0:T(8,128)(2,1)S(1)} %fusion.71), channel_id=1, source_target_pairs={{0,8},{24,16},{8,0},{16,24},{1,9},{25,17},{9,1},{17,25},{2,10},{26... | collective-permute-start | bytes 1179656 | tf_op jit(solution)/shard_map/ppermute | solution.py:105
  205.9 5.9 %collective-permute-done.43 = bf16[1536,128]{1,0:T(8,128)(2,1)S(1)} collective-permute-done((bf16[1536,128]{1,0:T(8,128)(2,1)S(1)}, bf16[1536,128]{1,0:T(8,128)(2,1)S(1)}, u32[]{:S(2)}, u32[]{:S(2)}) %collective-permute-start.43) | collective-permute-done | bytes 393248 | tf_op jit(solution)/shard_map/ppermute | solution.py:105
  214.1 2.6 %shard_map.97 = (f32[1536,1536]{1,0:T(8,128)}, bf16[1536,1536]{1,0:T(8,128)(2,1)}) custom-call(bf16[1536,128]{1,0:T(8,128)(2,1)S(1)} %broadcast_select_fusion.12.refs_0_, bf16[1536,128]{1,0:T(8,128)(2,1)S(1)} %broadcast_select_fusion.11.refs_1_, bf16[1536,128]{1,0:T(8,128)(2,1)S(1)} %broadcast_select_fusion.10.refs_2_, ...), custom_call_target="tpu_custom_call", output_to_operand_aliasing={{0}: (4, {}), {1}: (5, {})} | custom-call | flops 2949120 | bytes 7077888 | tf_op jit(solution)/shard_map/pallas_call | solution.py:61
  216.7 3.5 %collective-permute-done.48 = bf16[1536,128]{1,0:T(8,128)(2,1)S(1)} collective-permute-done((bf16[1536,128]{1,0:T(8,128)(2,1)S(1)}, bf16[1536,128]{1,0:T(8,128)(2,1)S(1)}, u32[]{:S(2)}, u32[]{:S(2)}) %collective-permute-start.48) | collective-permute-done | bytes 393248 | tf_op jit(solution)/shard_map/ppermute | solution.py:105
  221.7 6.2 %collective-permute-done.47 = bf16[1536,128]{1,0:T(8,128)(2,1)S(1)} collective-permute-done((bf16[1536,128]{1,0:T(8,128)(2,1)S(1)}, bf16[1536,128]{1,0:T(8,128)(2,1)S(1)}, u32[]{:S(2)}, u32[]{:S(2)}) %collective-permute-start.47) | collective-permute-done | bytes 393248 | tf_op jit(solution)/shard_map/ppermute | solution.py:105
  228.0 1.9 shard_map.98
  229.9 2.2 collective-permute-done.46
  (181 shorter events, 42.0 us)
Async XLA Ops:
  0.6 19.7 %collective-permute-start = (bf16[256,1536]{1,0:T(8,128)(2,1)}, bf16[256,1536]{1,0:T(8,128)(2,1)}, u32[]{:S(2)}, u32[]{:S(2)}) collective-permute-start(bf16[256,1536]{1,0:T(8,128)(2,1)} %param.8), channel_id=1, source_target_pairs={{0,4},{2,6},{4,0},{6,2},{1,5},{3,7},{5,1},{7,3},{8,12},{10,14},{12... | collective-permute-start | bytes 2359304 | tf_op jit(solution)/shard_map/ppermute | solution.py:31
  3.8 16.5 %collective-permute-start.1 = (bf16[256,1536]{1,0:T(8,128)(2,1)S(1)}, bf16[256,1536]{1,0:T(8,128)(2,1)S(1)}, u32[]{:S(2)}, u32[]{:S(2)}) collective-permute-start(bf16[256,1536]{1,0:T(8,128)(2,1)S(1)} %get-tuple-element.302), channel_id=1, source_target_pairs={{0,2},{2,0},{4,6},{6,4},{1,3},{3,1},{5,7},{7,5},{8,10},{10,8},{12,... | collective-permute-start | bytes 2359304 | tf_op jit(solution)/shard_map/ppermute | solution.py:31
  4.2 16.1 %collective-permute-start.2 = (bf16[256,1536]{1,0:T(8,128)(2,1)S(1)}, bf16[256,1536]{1,0:T(8,128)(2,1)S(1)}, u32[]{:S(2)}, u32[]{:S(2)}) collective-permute-start(bf16[256,1536]{1,0:T(8,128)(2,1)S(1)} %get-tuple-element.300), channel_id=1, source_target_pairs={{0,2},{2,0},{4,6},{6,4},{1,3},{3,1},{5,7},{7,5},{8,10},{10,8},{12,... | collective-permute-start | bytes 2359304 | tf_op jit(solution)/shard_map/ppermute | solution.py:31
  5.0 21.7 %collective-permute-start.5 = (bf16[256,1536]{1,0:T(8,128)(2,1)S(1)}, bf16[256,1536]{1,0:T(8,128)(2,1)S(1)}, u32[]{:S(2)}, u32[]{:S(2)}) collective-permute-start(bf16[256,1536]{1,0:T(8,128)(2,1)S(1)} %copy-done.1), channel_id=1, source_target_pairs={{0,2},{2,0},{4,6},{6,4},{1,3},{3,1},{5,7},{7,5},{8,10},{10,8},{12,... | collective-permute-start | bytes 2359304 | tf_op jit(solution)/shard_map/ppermute | solution.py:31
  20.3 17.8 %collective-permute-start.9 = (bf16[256,1536]{1,0:T(8,128)(2,1)}, bf16[256,1536]{1,0:T(8,128)(2,1)S(1)}, u32[]{:S(2)}, u32[]{:S(2)}) collective-permute-start(bf16[256,1536]{1,0:T(8,128)(2,1)} %collective-permute-done), channel_id=1, source_target_pairs={{0,2},{2,0},{4,6},{6,4},{1,3},{3,1},{5,7},{7,5},{8,10},{10,8},{12,... | collective-permute-start | bytes 2359304 | tf_op jit(solution)/shard_map/ppermute | solution.py:31
  25.2 11.6 %collective-permute-start.6 = (bf16[128,1536]{1,0:T(8,128)(2,1)S(1)}, bf16[128,1536]{1,0:T(8,128)(2,1)}, u32[]{:S(2)}, u32[]{:S(2)}) collective-permute-start(bf16[128,1536]{1,0:T(8,128)(2,1)S(1)} %get-tuple-element.310), channel_id=1, source_target_pairs={{0,4},{2,6},{4,0},{6,2},{1,5},{3,7},{5,1},{7,3},{8,12},{10,14},{12... | collective-permute-start | bytes 1179656 | tf_op jit(solution)/shard_map/ppermute | solution.py:31
  30.8 36.7 %collective-permute-start.7 = (bf16[512,1536]{1,0:T(8,128)(2,1)}, bf16[512,1536]{1,0:T(8,128)(2,1)}, u32[]{:S(2)}, u32[]{:S(2)}) collective-permute-start(bf16[512,1536]{1,0:T(8,128)(2,1)} %convolution_convert_fusion), channel_id=1, source_target_pairs={{4,5},{1,0},{6,7},{3,2},{12,13},{9,8},{14,15},{11,10},{20,21},{17,... | collective-permute-start | bytes 4718600 | tf_op jit(solution)/shard_map/ppermute | solution.py:166
  34.4 13.2 %collective-permute-start.3 = (bf16[128,1536]{1,0:T(8,128)(2,1)}, bf16[128,1536]{1,0:T(8,128)(2,1)}, u32[]{:S(2)}, u32[]{:S(2)}) collective-permute-start(bf16[128,1536]{1,0:T(8,128)(2,1)} %get-tuple-element.311), channel_id=1, source_target_pairs={{0,4},{2,6},{4,0},{6,2},{1,5},{3,7},{5,1},{7,3},{8,12},{10,14},{12... | collective-permute-start | bytes 1179656 | tf_op jit(solution)/shard_map/ppermute | solution.py:31
  36.8 26.9 %collective-permute-start.8 = (bf16[128,1536]{1,0:T(8,128)(2,1)}, bf16[128,1536]{1,0:T(8,128)(2,1)}, u32[]{:S(2)}, u32[]{:S(2)}) collective-permute-start(bf16[128,1536]{1,0:T(8,128)(2,1)} %collective-permute-done.6), channel_id=1, source_target_pairs={{0,1},{5,4},{2,3},{7,6},{8,9},{13,12},{10,11},{15,14},{16,17},{21,... | collective-permute-start | bytes 1179656 | tf_op jit(solution)/shard_map/ppermute | solution.py:171
  40.4 14.8 %collective-permute-start.10 = (bf16[128,1536]{1,0:T(8,128)(2,1)}, bf16[128,1536]{1,0:T(8,128)(2,1)}, u32[]{:S(2)}, u32[]{:S(2)}) collective-permute-start(bf16[128,1536]{1,0:T(8,128)(2,1)} %get-tuple-element.312), channel_id=1, source_target_pairs={{0,4},{2,6},{4,0},{6,2},{1,5},{3,7},{5,1},{7,3},{8,12},{10,14},{12... | collective-permute-start | bytes 1179656 | tf_op jit(solution)/shard_map/ppermute | solution.py:31
  43.8 18.6 %collective-permute-start.12 = (bf16[128,1536]{1,0:T(8,128)(2,1)}, bf16[128,1536]{1,0:T(8,128)(2,1)S(1)}, u32[]{:S(2)}, u32[]{:S(2)}) collective-permute-start(bf16[128,1536]{1,0:T(8,128)(2,1)} %get-tuple-element.313), channel_id=1, source_target_pairs={{0,4},{2,6},{4,0},{6,2},{1,5},{3,7},{5,1},{7,3},{8,12},{10,14},{12... | collective-permute-start | bytes 1179656 | tf_op jit(solution)/shard_map/ppermute | solution.py:31
  47.6 21.8 %collective-permute-start.4 = (bf16[128,1536]{1,0:T(8,128)(2,1)}, bf16[128,1536]{1,0:T(8,128)(2,1)S(1)}, u32[]{:S(2)}, u32[]{:S(2)}) collective-permute-start(bf16[128,1536]{1,0:T(8,128)(2,1)} %collective-permute-done.3), channel_id=1, source_target_pairs={{0,1},{5,4},{2,3},{7,6},{8,9},{13,12},{10,11},{15,14},{16,17},{21,... | collective-permute-start | bytes 1179656 | tf_op jit(solution)/shard_map/ppermute | solution.py:171
  55.2 16.0 %collective-permute-start.11 = (bf16[128,1536]{1,0:T(8,128)(2,1)}, bf16[128,1536]{1,0:T(8,128)(2,1)S(1)}, u32[]{:S(2)}, u32[]{:S(2)}) collective-permute-start(bf16[128,1536]{1,0:T(8,128)(2,1)} %collective-permute-done.10), channel_id=1, source_target_pairs={{0,1},{5,4},{2,3},{7,6},{8,9},{13,12},{10,11},{15,14},{16,17},{21,... | collective-permute-start | bytes 1179656 | tf_op jit(solution)/shard_map/ppermute | solution.py:171
  62.4 14.3 %collective-permute-start.13 = (bf16[128,1536]{1,0:T(8,128)(2,1)S(1)}, bf16[128,1536]{1,0:T(8,128)(2,1)S(1)}, u32[]{:S(2)}, u32[]{:S(2)}) collective-permute-start(bf16[128,1536]{1,0:T(8,128)(2,1)S(1)} %collective-permute-done.12), channel_id=1, source_target_pairs={{0,1},{5,4},{2,3},{7,6},{8,9},{13,12},{10,11},{15,14},{16,17},{21,... | collective-permute-start | bytes 1179656 | tf_op jit(solution)/shard_map/ppermute | solution.py:171
  79.8 3.7 %collective-permute-start.15 = (f32[2,512]{1,0:T(2,128)S(1)}, f32[2,512]{1,0:T(2,128)S(1)}, u32[]{:S(2)}, u32[]{:S(2)}) collective-permute-start(f32[2,512]{1,0:T(2,128)S(1)} %maximum_add_fusion), channel_id=1, source_target_pairs={{0,1},{1,0},{2,3},{3,2},{4,5},{5,4},{6,7},{7,6},{8,9},{9,8},{10,11... | collective-permute-start | bytes 12296 | tf_op jit(solution)/shard_map/ppermute | solution.py:31
  83.8 5.0 %collective-permute-start.19 = (bf16[512,128]{1,0:T(8,128)(2,1)S(1)}, bf16[512,128]{1,0:T(8,128)(2,1)S(1)}, u32[]{:S(2)}, u32[]{:S(2)}) collective-permute-start(bf16[512,128]{1,0:T(8,128)(2,1)S(1)} %pad_maximum_fusion.6), channel_id=1, source_target_pairs={{0,1},{5,4},{4,0},{1,5},{2,3},{7,6},{6,2},{3,7},{8,9},{13,12},{12,... | collective-permute-start | bytes 393224 | tf_op jit(solution)/shard_map/ppermute | solution.py:225
  83.9 8.4 %collective-permute-start.16 = (bf16[512,128]{1,0:T(8,128)(2,1)S(1)}, bf16[512,128]{1,0:T(8,128)(2,1)S(1)}, u32[]{:S(2)}, u32[]{:S(2)}) collective-permute-start(bf16[512,128]{1,0:T(8,128)(2,1)S(1)} %pad_maximum_fusion.6), channel_id=1, source_target_pairs={{4,1},{1,4},{6,3},{3,6},{12,9},{9,12},{14,11},{11,14},{20,17},{17,... | collective-permute-start | bytes 393224 | tf_op jit(solution)/shard_map/ppermute | solution.py:226
  88.9 14.8 %collective-permute-start.22 = (bf16[512,384]{1,0:T(8,128)(2,1)S(1)}, bf16[512,384]{1,0:T(8,128)(2,1)S(1)}, u32[]{:S(2)}, u32[]{:S(2)}) collective-permute-start(bf16[512,384]{1,0:T(8,128)(2,1)S(1)} %pad_maximum_fusion.3), channel_id=1, source_target_pairs={{4,1},{1,4},{6,3},{3,6},{12,9},{9,12},{14,11},{11,14},{20,17},{17,... | collective-permute-start | bytes 1179656 | tf_op jit(solution)/shard_map/ppermute | solution.py:226
  92.2 12.1 %collective-permute-start.21 = (bf16[512,384]{1,0:T(8,128)(2,1)S(1)}, bf16[512,384]{1,0:T(8,128)(2,1)S(1)}, u32[]{:S(2)}, u32[]{:S(2)}) collective-permute-start(bf16[512,384]{1,0:T(8,128)(2,1)S(1)} %pad_maximum_fusion.3), channel_id=1, source_target_pairs={{0,1},{5,4},{4,0},{1,5},{2,3},{7,6},{6,2},{3,7},{8,9},{13,12},{12,... | collective-permute-start | bytes 1179656 | tf_op jit(solution)/shard_map/ppermute | solution.py:225
  92.3 33.7 %collective-permute-start.18 = (bf16[512,1024]{1,0:T(8,128)(2,1)S(1)}, bf16[512,1024]{1,0:T(8,128)(2,1)S(1)}, u32[]{:S(2)}, u32[]{:S(2)}) collective-permute-start(bf16[512,1024]{1,0:T(8,128)(2,1)S(1)} %pad_maximum_fusion), channel_id=1, source_target_pairs={{4,1},{1,4},{6,3},{3,6},{12,9},{9,12},{14,11},{11,14},{20,17},{17,... | collective-permute-start | bytes 3145736 | tf_op jit(solution)/shard_map/ppermute | solution.py:226
  95.7 30.3 %collective-permute-start.17 = (bf16[512,1024]{1,0:T(8,128)(2,1)S(1)}, bf16[512,1024]{1,0:T(8,128)(2,1)S(1)}, u32[]{:S(2)}, u32[]{:S(2)}) collective-permute-start(bf16[512,1024]{1,0:T(8,128)(2,1)S(1)} %pad_maximum_fusion), channel_id=1, source_target_pairs={{0,1},{5,4},{4,0},{1,5},{2,3},{7,6},{6,2},{3,7},{8,9},{13,12},{12,... | collective-permute-start | bytes 3145736 | tf_op jit(solution)/shard_map/ppermute | solution.py:225
  98.5 14.5 %collective-permute-start.20 = (bf16[1536,128]{1,0:T(8,128)(2,1)S(1)}, bf16[1536,128]{1,0:T(8,128)(2,1)S(1)}, u32[]{:S(2)}, u32[]{:S(2)}) collective-permute-start(bf16[1536,128]{1,0:T(8,128)(2,1)S(1)} %fusion.50), channel_id=1, source_target_pairs={{0,8},{24,16},{1,9},{25,17},{2,10},{26,18},{3,11},{27,19},{4,12},{... | collective-permute-start | bytes 1179656 | tf_op jit(solution)/shard_map/ppermute | solution.py:105
  108.2 25.9 %collective-permute-start.25 = (bf16[1536,128]{1,0:T(8,128)(2,1)S(1)}, bf16[1536,128]{1,0:T(8,128)(2,1)S(1)}, u32[]{:S(2)}, u32[]{:S(2)}) collective-permute-start(bf16[1536,128]{1,0:T(8,128)(2,1)S(1)} %slice.459), channel_id=1, source_target_pairs={{0,8},{24,16},{1,9},{25,17},{2,10},{26,18},{3,11},{27,19},{4,12},{... | collective-permute-start | bytes 1179656 | tf_op jit(solution)/shard_map/ppermute | solution.py:105
  111.7 13.5 %collective-permute-start.23 = (bf16[1536,128]{1,0:T(8,128)(2,1)S(1)}, bf16[1536,128]{1,0:T(8,128)(2,1)S(1)}, u32[]{:S(2)}, u32[]{:S(2)}) collective-permute-start(bf16[1536,128]{1,0:T(8,128)(2,1)S(1)} %fusion.51), channel_id=1, source_target_pairs={{0,8},{24,16},{1,9},{25,17},{2,10},{26,18},{3,11},{27,19},{4,12},{... | collective-permute-start | bytes 1179656 | tf_op jit(solution)/shard_map/ppermute | solution.py:105
  113.1 12.9 %collective-permute-start.26 = (bf16[1536,128]{1,0:T(8,128)(2,1)S(1)}, bf16[1536,128]{1,0:T(8,128)(2,1)S(1)}, u32[]{:S(2)}, u32[]{:S(2)}) collective-permute-start(bf16[1536,128]{1,0:T(8,128)(2,1)S(1)} %add_convert_fusion.23), channel_id=1, source_target_pairs={{8,16},{16,8},{9,17},{17,9},{10,18},{18,10},{11,19},{19,11},{12,20... | collective-permute-start | bytes 1179656 | tf_op jit(solution)/shard_map/ppermute | solution.py:113
  125.3 9.6 %collective-permute-start.24 = (bf16[1536,128]{1,0:T(8,128)(2,1)S(1)}, bf16[1536,128]{1,0:T(8,128)(2,1)S(1)}, u32[]{:S(2)}, u32[]{:S(2)}) collective-permute-start(bf16[1536,128]{1,0:T(8,128)(2,1)S(1)} %add_convert_fusion.22), channel_id=1, source_target_pairs={{8,16},{16,8},{9,17},{17,9},{10,18},{18,10},{11,19},{19,11},{12,20... | collective-permute-start | bytes 1179656 | tf_op jit(solution)/shard_map/ppermute | solution.py:113
  128.7 14.9 %collective-permute-start.28 = (bf16[1536,128]{1,0:T(8,128)(2,1)S(1)}, bf16[1536,128]{1,0:T(8,128)(2,1)S(1)}, u32[]{:S(2)}, u32[]{:S(2)}) collective-permute-start(bf16[1536,128]{1,0:T(8,128)(2,1)S(1)} %fusion.63), channel_id=1, source_target_pairs={{0,8},{24,16},{8,0},{16,24},{1,9},{25,17},{9,1},{17,25},{2,10},{26... | collective-permute-start | bytes 1179656 | tf_op jit(solution)/shard_map/ppermute | solution.py:105
  134.2 10.3 %collective-permute-start.27 = (bf16[1536,128]{1,0:T(8,128)(2,1)S(1)}, bf16[1536,128]{1,0:T(8,128)(2,1)S(1)}, u32[]{:S(2)}, u32[]{:S(2)}) collective-permute-start(bf16[1536,128]{1,0:T(8,128)(2,1)S(1)} %add_convert_fusion.20), channel_id=1, source_target_pairs={{8,16},{16,8},{9,17},{17,9},{10,18},{18,10},{11,19},{19,11},{12,20... | collective-permute-start | bytes 1179656 | tf_op jit(solution)/shard_map/ppermute | solution.py:113
  137.2 15.6 %collective-permute-start.30 = (bf16[1536,128]{1,0:T(8,128)(2,1)S(1)}, bf16[1536,128]{1,0:T(8,128)(2,1)S(1)}, u32[]{:S(2)}, u32[]{:S(2)}) collective-permute-start(bf16[1536,128]{1,0:T(8,128)(2,1)S(1)} %fusion.64), channel_id=1, source_target_pairs={{0,8},{24,16},{8,0},{16,24},{1,9},{25,17},{9,1},{17,25},{2,10},{26... | collective-permute-start | bytes 1179656 | tf_op jit(solution)/shard_map/ppermute | solution.py:105
  143.8 10.1 %collective-permute-start.31 = (bf16[1536,128]{1,0:T(8,128)(2,1)S(1)}, bf16[1536,128]{1,0:T(8,128)(2,1)S(1)}, u32[]{:S(2)}, u32[]{:S(2)}) collective-permute-start(bf16[1536,128]{1,0:T(8,128)(2,1)S(1)} %add_convert_fusion.18), channel_id=1, source_target_pairs={{8,16},{16,8},{9,17},{17,9},{10,18},{18,10},{11,19},{19,11},{12,20... | collective-permute-start | bytes 1179656 | tf_op jit(solution)/shard_map/ppermute | solution.py:113
  144.6 16.6 %collective-permute-start.29 = (bf16[1536,128]{1,0:T(8,128)(2,1)S(1)}, bf16[1536,128]{1,0:T(8,128)(2,1)S(1)}, u32[]{:S(2)}, u32[]{:S(2)}) collective-permute-start(bf16[1536,128]{1,0:T(8,128)(2,1)S(1)} %fusion.65), channel_id=1, source_target_pairs={{0,8},{24,16},{8,0},{16,24},{1,9},{25,17},{9,1},{17,25},{2,10},{26... | collective-permute-start | bytes 1179656 | tf_op jit(solution)/shard_map/ppermute | solution.py:105
  152.9 11.5 %collective-permute-start.34 = (bf16[1536,128]{1,0:T(8,128)(2,1)S(1)}, bf16[1536,128]{1,0:T(8,128)(2,1)S(1)}, u32[]{:S(2)}, u32[]{:S(2)}) collective-permute-start(bf16[1536,128]{1,0:T(8,128)(2,1)S(1)} %add_convert_fusion.16), channel_id=1, source_target_pairs={{8,16},{16,8},{9,17},{17,9},{10,18},{18,10},{11,19},{19,11},{12,20... | collective-permute-start | bytes 1179656 | tf_op jit(solution)/shard_map/ppermute | solution.py:113
  154.0 17.6 %collective-permute-start.33 = (bf16[1536,128]{1,0:T(8,128)(2,1)S(1)}, bf16[1536,128]{1,0:T(8,128)(2,1)S(1)}, u32[]{:S(2)}, u32[]{:S(2)}) collective-permute-start(bf16[1536,128]{1,0:T(8,128)(2,1)S(1)} %fusion.66), channel_id=1, source_target_pairs={{0,8},{24,16},{8,0},{16,24},{1,9},{25,17},{9,1},{17,25},{2,10},{26... | collective-permute-start | bytes 1179656 | tf_op jit(solution)/shard_map/ppermute | solution.py:105
  163.6 8.8 %collective-permute-start.32 = (bf16[1536,128]{1,0:T(8,128)(2,1)S(1)}, bf16[1536,128]{1,0:T(8,128)(2,1)S(1)}, u32[]{:S(2)}, u32[]{:S(2)}) collective-permute-start(bf16[1536,128]{1,0:T(8,128)(2,1)S(1)} %add_convert_fusion.14), channel_id=1, source_target_pairs={{8,16},{16,8},{9,17},{17,9},{10,18},{18,10},{11,19},{19,11},{12,20... | collective-permute-start | bytes 1179656 | tf_op jit(solution)/shard_map/ppermute | solution.py:113
  164.6 15.6 %collective-permute-start.36 = (bf16[1536,128]{1,0:T(8,128)(2,1)S(1)}, bf16[1536,128]{1,0:T(8,128)(2,1)S(1)}, u32[]{:S(2)}, u32[]{:S(2)}) collective-permute-start(bf16[1536,128]{1,0:T(8,128)(2,1)S(1)} %fusion.67), channel_id=1, source_target_pairs={{0,8},{24,16},{8,0},{16,24},{1,9},{25,17},{9,1},{17,25},{2,10},{26... | collective-permute-start | bytes 1179656 | tf_op jit(solution)/shard_map/ppermute | solution.py:105
  171.7 9.3 %collective-permute-start.35 = (bf16[1536,128]{1,0:T(8,128)(2,1)S(1)}, bf16[1536,128]{1,0:T(8,128)(2,1)S(1)}, u32[]{:S(2)}, u32[]{:S(2)}) collective-permute-start(bf16[1536,128]{1,0:T(8,128)(2,1)S(1)} %add_convert_fusion.12), channel_id=1, source_target_pairs={{8,16},{16,8},{9,17},{17,9},{10,18},{18,10},{11,19},{19,11},{12,20... | collective-permute-start | bytes 1179656 | tf_op jit(solution)/shard_map/ppermute | solution.py:113
  172.6 14.6 %collective-permute-start.38 = (bf16[1536,128]{1,0:T(8,128)(2,1)S(1)}, bf16[1536,128]{1,0:T(8,128)(2,1)S(1)}, u32[]{:S(2)}, u32[]{:S(2)}) collective-permute-start(bf16[1536,128]{1,0:T(8,128)(2,1)S(1)} %fusion.68), channel_id=1, source_target_pairs={{0,8},{24,16},{8,0},{16,24},{1,9},{25,17},{9,1},{17,25},{2,10},{26... | collective-permute-start | bytes 1179656 | tf_op jit(solution)/shard_map/ppermute | solution.py:105
  180.3 7.7 %collective-permute-start.37 = (bf16[1536,128]{1,0:T(8,128)(2,1)S(1)}, bf16[1536,128]{1,0:T(8,128)(2,1)S(1)}, u32[]{:S(2)}, u32[]{:S(2)}) collective-permute-start(bf16[1536,128]{1,0:T(8,128)(2,1)S(1)} %add_convert_fusion.10), channel_id=1, source_target_pairs={{8,16},{16,8},{9,17},{17,9},{10,18},{18,10},{11,19},{19,11},{12,20... | collective-permute-start | bytes 1179656 | tf_op jit(solution)/shard_map/ppermute | solution.py:113
  181.2 16.7 %collective-permute-start.40 = (bf16[1536,128]{1,0:T(8,128)(2,1)S(1)}, bf16[1536,128]{1,0:T(8,128)(2,1)S(1)}, u32[]{:S(2)}, u32[]{:S(2)}) collective-permute-start(bf16[1536,128]{1,0:T(8,128)(2,1)S(1)} %fusion.69), channel_id=1, source_target_pairs={{0,8},{24,16},{8,0},{16,24},{1,9},{25,17},{9,1},{17,25},{2,10},{26... | collective-permute-start | bytes 1179656 | tf_op jit(solution)/shard_map/ppermute | solution.py:105
  187.3 11.4 %collective-permute-start.41 = (bf16[1536,128]{1,0:T(8,128)(2,1)S(1)}, bf16[1536,128]{1,0:T(8,128)(2,1)S(1)}, u32[]{:S(2)}, u32[]{:S(2)}) collective-permute-start(bf16[1536,128]{1,0:T(8,128)(2,1)S(1)} %add_convert_fusion.8), channel_id=1, source_target_pairs={{8,16},{16,8},{9,17},{17,9},{10,18},{18,10},{11,19},{19,11},{12,20... | collective-permute-start | bytes 1179656 | tf_op jit(solution)/shard_map/ppermute | solution.py:113
  188.2 15.5 %collective-permute-start.39 = (bf16[1536,128]{1,0:T(8,128)(2,1)S(1)}, bf16[1536,128]{1,0:T(8,128)(2,1)S(1)}, u32[]{:S(2)}, u32[]{:S(2)}) collective-permute-start(bf16[1536,128]{1,0:T(8,128)(2,1)S(1)} %fusion.70), channel_id=1, source_target_pairs={{0,8},{24,16},{8,0},{16,24},{1,9},{25,17},{9,1},{17,25},{2,10},{26... | collective-permute-start | bytes 1179656 | tf_op jit(solution)/shard_map/ppermute | solution.py:105
  198.0 6.5 %collective-permute-start.44 = (bf16[1536,128]{1,0:T(8,128)(2,1)S(1)}, bf16[1536,128]{1,0:T(8,128)(2,1)S(1)}, u32[]{:S(2)}, u32[]{:S(2)}) collective-permute-start(bf16[1536,128]{1,0:T(8,128)(2,1)S(1)} %add_convert_fusion.6), channel_id=1, source_target_pairs={{8,16},{16,8},{9,17},{17,9},{10,18},{18,10},{11,19},{19,11},{12,20... | collective-permute-start | bytes 1179656 | tf_op jit(solution)/shard_map/ppermute | solution.py:113
  198.9 12.9 %collective-permute-start.43 = (bf16[1536,128]{1,0:T(8,128)(2,1)S(1)}, bf16[1536,128]{1,0:T(8,128)(2,1)S(1)}, u32[]{:S(2)}, u32[]{:S(2)}) collective-permute-start(bf16[1536,128]{1,0:T(8,128)(2,1)S(1)} %fusion.71), channel_id=1, source_target_pairs={{0,8},{24,16},{8,0},{16,24},{1,9},{25,17},{9,1},{17,25},{2,10},{26... | collective-permute-start | bytes 1179656 | tf_op jit(solution)/shard_map/ppermute | solution.py:105
  203.8 8.8 %collective-permute-start.42 = (bf16[1536,128]{1,0:T(8,128)(2,1)S(1)}, bf16[1536,128]{1,0:T(8,128)(2,1)S(1)}, u32[]{:S(2)}, u32[]{:S(2)}) collective-permute-start(bf16[1536,128]{1,0:T(8,128)(2,1)S(1)} %add_convert_fusion.4), channel_id=1, source_target_pairs={{8,16},{16,8},{9,17},{17,9},{10,18},{18,10},{11,19},{19,11},{12,20... | collective-permute-start | bytes 1179656 | tf_op jit(solution)/shard_map/ppermute | solution.py:113
  204.6 15.6 %collective-permute-start.48 = (bf16[1536,128]{1,0:T(8,128)(2,1)S(1)}, bf16[1536,128]{1,0:T(8,128)(2,1)S(1)}, u32[]{:S(2)}, u32[]{:S(2)}) collective-permute-start(bf16[1536,128]{1,0:T(8,128)(2,1)S(1)} %add_convert_fusion.3), channel_id=1, source_target_pairs={{8,0},{16,24},{9,1},{17,25},{10,2},{18,26},{11,3},{19,27},{12,4},{... | collective-permute-start | bytes 1179656 | tf_op jit(solution)/shard_map/ppermute | solution.py:105
  211.9 8.3 %collective-permute-start.45 = (bf16[1536,128]{1,0:T(8,128)(2,1)S(1)}, bf16[1536,128]{1,0:T(8,128)(2,1)S(1)}, u32[]{:S(2)}, u32[]{:S(2)}) collective-permute-start(bf16[1536,128]{1,0:T(8,128)(2,1)S(1)} %add_convert_fusion.2), channel_id=1, source_target_pairs={{8,16},{16,8},{9,17},{17,9},{10,18},{18,10},{11,19},{19,11},{12,20... | collective-permute-start | bytes 1179656 | tf_op jit(solution)/shard_map/ppermute | solution.py:113
  212.8 15.1 %collective-permute-start.47 = (bf16[1536,128]{1,0:T(8,128)(2,1)S(1)}, bf16[1536,128]{1,0:T(8,128)(2,1)S(1)}, u32[]{:S(2)}, u32[]{:S(2)}) collective-permute-start(bf16[1536,128]{1,0:T(8,128)(2,1)S(1)} %add_convert_fusion), channel_id=1, source_target_pairs={{8,0},{16,24},{9,1},{17,25},{10,2},{18,26},{11,3},{19,27},{12,4},{... | collective-permute-start | bytes 1179656 | tf_op jit(solution)/shard_map/ppermute | solution.py:105
  220.3 11.8 %collective-permute-start.46 = (bf16[1536,128]{1,0:T(8,128)(2,1)S(1)}, bf16[1536,128]{1,0:T(8,128)(2,1)S(1)}, u32[]{:S(2)}, u32[]{:S(2)}) collective-permute-start(bf16[1536,128]{1,0:T(8,128)(2,1)S(1)} %add_convert_fusion.1), channel_id=1, source_target_pairs={{8,0},{16,24},{9,1},{17,25},{10,2},{18,26},{11,3},{19,27},{12,4},{... | collective-permute-start | bytes 1179656 | tf_op jit(solution)/shard_map/ppermute | solution.py:105
  (18 other events, 136.3 us)

commit v16 on v15

--- a/solution.py
+++ b/solution.py
@@ -101,6 +101,8 @@
             payload = jnp.where(self.outer, self.part[s], total) if s < self.chunks else total
         else:
             payload = self.part[s]
+            if s == 2:
+                payload, self.sums[0] = together(payload, self.sums[0])
         self.paid[s] = payload
         self.edge[s] = lax.ppermute(payload, "island", pairs)
 
@@ -205,7 +207,7 @@
     widths = [1, 3, units - 4]
     islands = lax.axis_size("island")
     line = IslandLine(units)
-    parts, locals_, rings, crosses = [], [], [], []
+    locals_, rings, crosses = [], [], []
 
     def move(c):
         cols_at = slice(sum(widths[:c]) * narrow, sum(widths[: c + 1]) * narrow)
@@ -223,18 +225,23 @@
             d_local, crosses[0] = together(d_local, crosses[0])
         locals_.append(d_local)
         rings.append(lax.ppermute(d_local, ("fsdp", "tp"), ring_pairs))
-        crosses.append(lax.ppermute(d_local, ("fsdp", "tp"), cross_pairs))
+        d_cross = d_local
+        if c == 1:
+            d_cross, crosses[0] = together(d_local, crosses[0])
+        crosses.append(lax.ppermute(d_cross, ("fsdp", "tp"), cross_pairs))
 
     def gathered(c):
         d_near = jnp.where(near, locals_[c], rings[c])
         d_far = jnp.where(near, rings[c], crosses[c])
         return jnp.concatenate([d_near, d_far], axis=0)
 
-    def add_pseudo(d_all, lo, hi, after=None):
+    def add_pseudo(d_all, lo, hi, after=None, behind=None):
         at_cols = slice(lo * narrow, hi * narrow)
         piece = d_all[:, : (hi - lo) * narrow]
         if after in line.sums:
             piece, line.sums[after] = together(piece, line.sums[after])
+        if behind is not None:
+            piece, line.part[behind] = together(piece, line.part[behind])
         piece, first, second, outer = together(piece, first_moment, second_moment, weight)
         grad = lax.dot_general(
             context_all, piece, (((0,), (0,)), ((), ())), preferred_element_type=f32
@@ -248,8 +255,7 @@
         ) + decay_rate * outer[:, at_cols].astype(f32)
         pseudo = lax.optimization_barrier(update.astype(bf16))
         for u in range(hi - lo):
-            line.part[len(parts)] = pseudo[:, u * narrow : (u + 1) * narrow]
-            parts.append(line.part[len(parts)])
+            line.part[lo + u] = pseudo[:, u * narrow : (u + 1) * narrow]
 
     for c in range(len(widths)):
         move(c)
@@ -257,7 +263,7 @@
     found = gathered(1)
     early = sum(widths[:2])
     add_pseudo(found, 1, 2)
-    add_pseudo(found[:, narrow:], 2, early)
+    add_pseudo(found[:, narrow:], 2, early, behind=1)
     last = gathered(2)
     todo = [(lo, min(lo + 2, units)) for lo in range(early, units, 2)]
     if islands == 4:
@@ -272,7 +278,7 @@
     else:
         for lo, hi in todo:
             add_pseudo(last[:, (lo - early) * narrow :], lo, hi)
-        sums = [lax.psum(part, "island") for part in parts]
+        sums = [lax.psum(line.part[k], "island") for k in range(units)]
     ends = list(range(3, units - 3, 3)) + [units - 3, units - 1, units]
     outputs, start = (), 0
     for end in ends:

time: 238 us -> 253 us (1.063); the launches traced: 234 us -> 252 us
  waiting for transfers between devices: 79.8 us -> 95.7 us
  starting transfers between devices: 94.8 us -> 97.5 us
    ppermute x3, waiting for transfers between devices: 1.48 us -> 21.1 us  [move(): crosses.append(lax.ppermute(d_cross, ('fsdp', 'tp'), cross_pairs))]
    ppermute x15, waiting for transfers between devices: 36 us -> 29.6 us  [send_outer(): self.edge[s] = lax.ppermute(payload, 'island', pairs)]
    ppermute x3, waiting for transfers between devices: 1.34 us -> 4.09 us  [move(): rings.append(lax.ppermute(d_local, ('fsdp', 'tp'), ring_pairs))]
  transfers between devices with their start and end apart: 49 -> 49, of which waited for: 19 -> 18; matrix products, arithmetic and copies ran while one was open for 19% -> 17% of each run, Pallas kernels for 4% -> 4%
where the time goes in v16:
time: 253 us; the launch traced here: 252 us
  starting transfers between devices  97.5 us (39%)
  waiting for transfers between devices  95.7 us (38%)
  matrix products  24.3 us (10%)
  other arithmetic  13 us (5%)
  Pallas kernels  11 us (4%)
  local copies, waits for them, and re-layouts  8.57 us (3%)
    ppermute x15, starting transfers between devices, send_outer(): self.edge[s] = lax.ppermute(payload, 'island', pairs)  62.6 us
    ppermute x11, waiting for transfers between devices, swap(): return lax.ppermute(value, axis, [(i, i ^ bit) for i in range(count)])  33.4 us
    ppermute x15, waiting for transfers between devices, send_outer(): self.edge[s] = lax.ppermute(payload, 'island', pairs)  29.6 us
    ppermute x3, waiting for transfers between devices, move(): crosses.append(lax.ppermute(d_cross, ('fsdp', 'tp'), cross_pairs))  21.1 us
    dot_general x7, matrix products, add_pseudo(): lax.dot_general(context_all, piece, (((0,), (0,)), ((), ())), preferred_e...  14.8 us
    pallas_call x5, Pallas kernels, finish(): pl.pallas_call(functools.partial(finish_kernel, count, start, narrow, isl...  11 us
    ppermute x3, starting transfers between devices, move(): crosses.append(lax.ppermute(d_cross, ('fsdp', 'tp'), cross_pairs))  10.3 us
    dot_general x3, matrix products, project(): jnp.dot(block, weight, preferred_element_type=f32).astype(bf16)  9.49 us
  transfers between devices with their start and end apart: 49, of which 18 were waited for; matrix products, arithmetic and copies ran while one was open for 17% of the time, Pallas kernels for 4%

profile of v16, /device:TPU:2, one launch (start us, length us, event | category | flops | bytes accessed | tf_op | source)
XLA Modules:
  0.0 252.1 jit_solution(6985164589470957040)
XLA Ops:
  5.0 15.3 %collective-permute-done = bf16[256,1536]{1,0:T(8,128)(2,1)} collective-permute-done((bf16[256,1536]{1,0:T(8,128)(2,1)}, bf16[256,1536]{1,0:T(8,128)(2,1)}, u32[]{:S(2)}, u32[]{:S(2)}) %collective-permute-start) | collective-permute-done | bytes 786464 | tf_op jit(solution)/shard_map/ppermute | solution.py:31
  20.4 4.0 %convolution_convert_fusion.2 = bf16[256,1536]{1,0:T(8,128)(2,1)S(1)} fusion(bf16[256,1536]{1,0:T(8,128)(2,1)} %collective-permute-done, bf16[1536,1536]{1,0:T(8,128)(2,1)} %param.12), kind=kOutput, calls=%fused_computation.8 | convolution fusion | flops 1208352768 | bytes 6291456 | tf_op jit(solution)/shard_map/dot_general | solution.py:144
  26.7 4.1 %convolution_convert_fusion = bf16[512,1536]{1,0:T(8,128)(2,1)} fusion(bf16[1536,1536]{1,0:T(8,128)(2,1)S(1)} %bitcast.206, bf16[256,1536]{1,0:T(8,128)(2,1)S(1)} %collective-permute-done.5, bf16[256,1536]{1,0:T(8,128)(2,1)S(1)} %copy-done.1), kind=kOutput, calls=%fused_computation | convolution fusion | flops 2419851264 | bytes 7864320 | tf_op jit(solution)/shard_map/dot_general | solution.py:144
  30.8 3.6 %collective-permute-start.7 = (bf16[512,1536]{1,0:T(8,128)(2,1)}, bf16[512,1536]{1,0:T(8,128)(2,1)}, u32[]{:S(2)}, u32[]{:S(2)}) collective-permute-start(bf16[512,1536]{1,0:T(8,128)(2,1)} %convolution_convert_fusion), channel_id=1, source_target_pairs={{4,5},{1,0},{6,7},{3,2},{12,13},{9,8},{14,15},{11,10},{20,21},{17,... | collective-permute-start | bytes 4718600 | tf_op jit(solution)/shard_map/ppermute | solution.py:168
  34.4 2.3 collective-permute-done.6
  40.4 3.4 %collective-permute-start.10 = (bf16[128,1536]{1,0:T(8,128)(2,1)}, bf16[128,1536]{1,0:T(8,128)(2,1)}, u32[]{:S(2)}, u32[]{:S(2)}) collective-permute-start(bf16[128,1536]{1,0:T(8,128)(2,1)} %get-tuple-element.324), channel_id=1, source_target_pairs={{0,4},{2,6},{4,0},{6,2},{1,5},{3,7},{5,1},{7,3},{8,12},{10,14},{12... | collective-permute-start | bytes 1179656 | tf_op jit(solution)/shard_map/ppermute | solution.py:31
  45.5 2.1 constant_dynamic-update-slice_fusion.2
  48.9 6.3 %collective-permute-done.10 = bf16[128,1536]{1,0:T(8,128)(2,1)} collective-permute-done((bf16[128,1536]{1,0:T(8,128)(2,1)}, bf16[128,1536]{1,0:T(8,128)(2,1)}, u32[]{:S(2)}, u32[]{:S(2)}) %collective-permute-start.10) | collective-permute-done | bytes 393248 | tf_op jit(solution)/shard_map/ppermute | solution.py:31
  56.5 6.0 %collective-permute-done.12 = bf16[128,1536]{1,0:T(8,128)(2,1)S(1)} collective-permute-done((bf16[128,1536]{1,0:T(8,128)(2,1)}, bf16[128,1536]{1,0:T(8,128)(2,1)S(1)}, u32[]{:S(2)}, u32[]{:S(2)}) %collective-permute-start.12) | collective-permute-done | bytes 393248 | tf_op jit(solution)/shard_map/ppermute | solution.py:31
  63.7 3.9 %collective-permute-done.7 = bf16[512,1536]{1,0:T(8,128)(2,1)} collective-permute-done((bf16[512,1536]{1,0:T(8,128)(2,1)}, bf16[512,1536]{1,0:T(8,128)(2,1)}, u32[]{:S(2)}, u32[]{:S(2)}) %collective-permute-start.7) | collective-permute-done | bytes 1572896 | tf_op jit(solution)/shard_map/ppermute | solution.py:168
  67.6 1.8 multiply_reduce_fusion.7
  69.4 1.8 multiply_reduce_fusion.5
  71.2 1.7 multiply_reduce_fusion.3
  73.0 3.7 %collective-permute-done.13 = bf16[128,1536]{1,0:T(8,128)(2,1)S(1)} collective-permute-done((bf16[128,1536]{1,0:T(8,128)(2,1)S(1)}, bf16[128,1536]{1,0:T(8,128)(2,1)S(1)}, u32[]{:S(2)}, u32[]{:S(2)}) %collective-permute-start.13) | collective-permute-done | bytes 393248 | tf_op jit(solution)/shard_map/ppermute | solution.py:173
  80.0 3.5 %collective-permute-done.15 = f32[2,512]{1,0:T(2,128)S(1)} collective-permute-done((f32[2,512]{1,0:T(2,128)S(1)}, f32[2,512]{1,0:T(2,128)S(1)}, u32[]{:S(2)}, u32[]{:S(2)}) %collective-permute-start.15) | collective-permute-done | bytes 4128 | tf_op jit(solution)/shard_map/ppermute | solution.py:31
  83.8 3.3 %collective-permute-start.17 = (bf16[512,128]{1,0:T(8,128)(2,1)S(1)}, bf16[512,128]{1,0:T(8,128)(2,1)S(1)}, u32[]{:S(2)}, u32[]{:S(2)}) collective-permute-start(bf16[512,128]{1,0:T(8,128)(2,1)S(1)} %pad_maximum_fusion.5), channel_id=1, source_target_pairs={{4,1},{1,4},{6,3},{3,6},{12,9},{9,12},{14,11},{11,14},{20,17},{17,... | collective-permute-start | bytes 393224 | tf_op jit(solution)/shard_map/ppermute | solution.py:231
  88.1 4.1 %collective-permute-done.16 = bf16[512,128]{1,0:T(8,128)(2,1)S(1)} collective-permute-done((bf16[512,128]{1,0:T(8,128)(2,1)S(1)}, bf16[512,128]{1,0:T(8,128)(2,1)S(1)}, u32[]{:S(2)}, u32[]{:S(2)}) %collective-permute-start.16) | collective-permute-done | bytes 131104 | tf_op jit(solution)/shard_map/ppermute | solution.py:227
  92.2 3.4 %collective-permute-start.19 = (bf16[512,1024]{1,0:T(8,128)(2,1)S(1)}, bf16[512,1024]{1,0:T(8,128)(2,1)S(1)}, u32[]{:S(2)}, u32[]{:S(2)}) collective-permute-start(bf16[512,1024]{1,0:T(8,128)(2,1)S(1)} %pad_maximum_fusion), channel_id=1, source_target_pairs={{4,1},{1,4},{6,3},{3,6},{12,9},{9,12},{14,11},{11,14},{20,17},{17,... | collective-permute-start | bytes 3145736 | tf_op jit(solution)/shard_map/ppermute | solution.py:231
  95.8 3.6 %collective-permute-start.21 = (bf16[512,384]{1,0:T(8,128)(2,1)S(1)}, bf16[512,384]{1,0:T(8,128)(2,1)S(1)}, u32[]{:S(2)}, u32[]{:S(2)}) collective-permute-start(bf16[512,384]{1,0:T(8,128)(2,1)S(1)} %pad_maximum_fusion.2), channel_id=1, source_target_pairs={{4,1},{1,4},{6,3},{3,6},{12,9},{9,12},{14,11},{11,14},{20,17},{17,... | collective-permute-start | bytes 1179656 | tf_op jit(solution)/shard_map/ppermute | solution.py:231
  99.5 2.4 fusion.51
  101.9 3.7 %collective-permute-start.22 = (bf16[1536,128]{1,0:T(8,128)(2,1)S(1)}, bf16[1536,128]{1,0:T(8,128)(2,1)S(1)}, u32[]{:S(2)}, u32[]{:S(2)}) collective-permute-start(bf16[1536,128]{1,0:T(8,128)(2,1)S(1)} %fusion.51), channel_id=1, source_target_pairs={{0,8},{24,16},{1,9},{25,17},{2,10},{26,18},{3,11},{27,19},{4,12},{... | collective-permute-start | bytes 1179656 | tf_op jit(solution)/shard_map/ppermute | solution.py:107
  105.6 21.1 %collective-permute-done.21 = bf16[512,384]{1,0:T(8,128)(2,1)S(1)} collective-permute-done((bf16[512,384]{1,0:T(8,128)(2,1)S(1)}, bf16[512,384]{1,0:T(8,128)(2,1)S(1)}, u32[]{:S(2)}, u32[]{:S(2)}) %collective-permute-start.21) | collective-permute-done | bytes 393248 | tf_op jit(solution)/shard_map/ppermute | solution.py:231
  128.3 2.2 fusion.33
  130.5 3.5 %collective-permute-start.23 = (bf16[1536,128]{1,0:T(8,128)(2,1)S(1)}, bf16[1536,128]{1,0:T(8,128)(2,1)S(1)}, u32[]{:S(2)}, u32[]{:S(2)}) collective-permute-start(bf16[1536,128]{1,0:T(8,128)(2,1)S(1)} %fusion.50), channel_id=1, source_target_pairs={{0,8},{24,16},{1,9},{25,17},{2,10},{26,18},{3,11},{27,19},{4,12},{... | collective-permute-start | bytes 1179656 | tf_op jit(solution)/shard_map/ppermute | solution.py:107
  134.9 4.1 %collective-permute-start.25 = (bf16[1536,128]{1,0:T(8,128)(2,1)S(1)}, bf16[1536,128]{1,0:T(8,128)(2,1)S(1)}, u32[]{:S(2)}, u32[]{:S(2)}) collective-permute-start(bf16[1536,128]{1,0:T(8,128)(2,1)S(1)} %slice.458), channel_id=1, source_target_pairs={{0,8},{24,16},{1,9},{25,17},{2,10},{26,18},{3,11},{27,19},{4,12},{... | collective-permute-start | bytes 1179656 | tf_op jit(solution)/shard_map/ppermute | solution.py:107
  139.0 4.6 %collective-permute-done.23 = bf16[1536,128]{1,0:T(8,128)(2,1)S(1)} collective-permute-done((bf16[1536,128]{1,0:T(8,128)(2,1)S(1)}, bf16[1536,128]{1,0:T(8,128)(2,1)S(1)}, u32[]{:S(2)}, u32[]{:S(2)}) %collective-permute-start.23) | collective-permute-done | bytes 393248 | tf_op jit(solution)/shard_map/ppermute | solution.py:107
  144.7 2.2 fusion.34
  147.1 5.4 %collective-permute-start.28 = (bf16[1536,128]{1,0:T(8,128)(2,1)S(1)}, bf16[1536,128]{1,0:T(8,128)(2,1)S(1)}, u32[]{:S(2)}, u32[]{:S(2)}) collective-permute-start(bf16[1536,128]{1,0:T(8,128)(2,1)S(1)} %fusion.64), channel_id=1, source_target_pairs={{0,8},{24,16},{8,0},{16,24},{1,9},{25,17},{9,1},{17,25},{2,10},{26... | collective-permute-start | bytes 1179656 | tf_op jit(solution)/shard_map/ppermute | solution.py:107
  153.3 2.2 fusion.35
  155.6 6.8 %collective-permute-start.30 = (bf16[1536,128]{1,0:T(8,128)(2,1)S(1)}, bf16[1536,128]{1,0:T(8,128)(2,1)S(1)}, u32[]{:S(2)}, u32[]{:S(2)}) collective-permute-start(bf16[1536,128]{1,0:T(8,128)(2,1)S(1)} %fusion.65), channel_id=1, source_target_pairs={{0,8},{24,16},{8,0},{16,24},{1,9},{25,17},{9,1},{17,25},{2,10},{26... | collective-permute-start | bytes 1179656 | tf_op jit(solution)/shard_map/ppermute | solution.py:107
  163.4 5.2 %collective-permute-start.29 = (bf16[1536,128]{1,0:T(8,128)(2,1)S(1)}, bf16[1536,128]{1,0:T(8,128)(2,1)S(1)}, u32[]{:S(2)}, u32[]{:S(2)}) collective-permute-start(bf16[1536,128]{1,0:T(8,128)(2,1)S(1)} %fusion.66), channel_id=1, source_target_pairs={{0,8},{24,16},{8,0},{16,24},{1,9},{25,17},{9,1},{17,25},{2,10},{26... | collective-permute-start | bytes 1179656 | tf_op jit(solution)/shard_map/ppermute | solution.py:107
  168.7 2.6 %collective-permute-done.30 = bf16[1536,128]{1,0:T(8,128)(2,1)S(1)} collective-permute-done((bf16[1536,128]{1,0:T(8,128)(2,1)S(1)}, bf16[1536,128]{1,0:T(8,128)(2,1)S(1)}, u32[]{:S(2)}, u32[]{:S(2)}) %collective-permute-start.30) | collective-permute-done | bytes 393248 | tf_op jit(solution)/shard_map/ppermute | solution.py:107
  172.5 4.6 %collective-permute-start.33 = (bf16[1536,128]{1,0:T(8,128)(2,1)S(1)}, bf16[1536,128]{1,0:T(8,128)(2,1)S(1)}, u32[]{:S(2)}, u32[]{:S(2)}) collective-permute-start(bf16[1536,128]{1,0:T(8,128)(2,1)S(1)} %fusion.67), channel_id=1, source_target_pairs={{0,8},{24,16},{8,0},{16,24},{1,9},{25,17},{9,1},{17,25},{2,10},{26... | collective-permute-start | bytes 1179656 | tf_op jit(solution)/shard_map/ppermute | solution.py:107
  177.1 2.6 %collective-permute-done.29 = bf16[1536,128]{1,0:T(8,128)(2,1)S(1)} collective-permute-done((bf16[1536,128]{1,0:T(8,128)(2,1)S(1)}, bf16[1536,128]{1,0:T(8,128)(2,1)S(1)}, u32[]{:S(2)}, u32[]{:S(2)}) %collective-permute-start.29) | collective-permute-done | bytes 393248 | tf_op jit(solution)/shard_map/ppermute | solution.py:107
  179.9 2.2 fusion.37
  183.1 3.9 %collective-permute-start.36 = (bf16[1536,128]{1,0:T(8,128)(2,1)S(1)}, bf16[1536,128]{1,0:T(8,128)(2,1)S(1)}, u32[]{:S(2)}, u32[]{:S(2)}) collective-permute-start(bf16[1536,128]{1,0:T(8,128)(2,1)S(1)} %fusion.68), channel_id=1, source_target_pairs={{0,8},{24,16},{8,0},{16,24},{1,9},{25,17},{9,1},{17,25},{2,10},{26... | collective-permute-start | bytes 1179656 | tf_op jit(solution)/shard_map/ppermute | solution.py:107
  187.1 2.6 %shard_map.95 = (f32[1536,1536]{1,0:T(8,128)}, bf16[1536,1536]{1,0:T(8,128)(2,1)}) custom-call(bf16[1536,128]{1,0:T(8,128)(2,1)S(1)} %broadcast_select_fusion.6.refs_0_, bf16[1536,128]{1,0:T(8,128)(2,1)S(1)} %broadcast_select_fusion.5.refs_1_, bf16[1536,128]{1,0:T(8,128)(2,1)S(1)} %broadcast_select_fusion.4.refs_2_, f32[1536,1536]{1,0:T(8,128)S(1)} %bitcast.192), custom_call_target="tpu_custom_call" | custom-call | flops 2949120 | bytes 7077888 | tf_op jit(solution)/shard_map/pallas_call | solution.py:61
  190.7 4.4 %collective-permute-start.38 = (bf16[1536,128]{1,0:T(8,128)(2,1)S(1)}, bf16[1536,128]{1,0:T(8,128)(2,1)S(1)}, u32[]{:S(2)}, u32[]{:S(2)}) collective-permute-start(bf16[1536,128]{1,0:T(8,128)(2,1)S(1)} %fusion.69), channel_id=1, source_target_pairs={{0,8},{24,16},{8,0},{16,24},{1,9},{25,17},{9,1},{17,25},{2,10},{26... | collective-permute-start | bytes 1179656 | tf_op jit(solution)/shard_map/ppermute | solution.py:107
  195.1 2.2 fusion.36
  198.3 5.9 %collective-permute-start.40 = (bf16[1536,128]{1,0:T(8,128)(2,1)S(1)}, bf16[1536,128]{1,0:T(8,128)(2,1)S(1)}, u32[]{:S(2)}, u32[]{:S(2)}) collective-permute-start(bf16[1536,128]{1,0:T(8,128)(2,1)S(1)} %fusion.70), channel_id=1, source_target_pairs={{0,8},{24,16},{8,0},{16,24},{1,9},{25,17},{9,1},{17,25},{2,10},{26... | collective-permute-start | bytes 1179656 | tf_op jit(solution)/shard_map/ppermute | solution.py:107
  206.5 6.1 %collective-permute-start.39 = (bf16[1536,128]{1,0:T(8,128)(2,1)S(1)}, bf16[1536,128]{1,0:T(8,128)(2,1)S(1)}, u32[]{:S(2)}, u32[]{:S(2)}) collective-permute-start(bf16[1536,128]{1,0:T(8,128)(2,1)S(1)} %fusion.71), channel_id=1, source_target_pairs={{0,8},{24,16},{8,0},{16,24},{1,9},{25,17},{9,1},{17,25},{2,10},{26... | collective-permute-start | bytes 1179656 | tf_op jit(solution)/shard_map/ppermute | solution.py:107
  212.7 2.6 %shard_map.96 = (f32[1536,1536]{1,0:T(8,128)}, bf16[1536,1536]{1,0:T(8,128)(2,1)}) custom-call(bf16[1536,128]{1,0:T(8,128)(2,1)S(1)} %broadcast_select_fusion.9.refs_0_, bf16[1536,128]{1,0:T(8,128)(2,1)S(1)} %broadcast_select_fusion.8.refs_1_, bf16[1536,128]{1,0:T(8,128)(2,1)S(1)} %broadcast_select_fusion.7.refs_2_, ...), custom_call_target="tpu_custom_call", output_to_operand_aliasing={{0}: (4, {}), {1}: (5, {})} | custom-call | flops 2949120 | bytes 7077888 | tf_op jit(solution)/shard_map/pallas_call | solution.py:61
  216.3 5.1 %collective-permute-start.43 = (bf16[1536,128]{1,0:T(8,128)(2,1)S(1)}, bf16[1536,128]{1,0:T(8,128)(2,1)S(1)}, u32[]{:S(2)}, u32[]{:S(2)}) collective-permute-start(bf16[1536,128]{1,0:T(8,128)(2,1)S(1)} %fusion.72), channel_id=1, source_target_pairs={{0,8},{24,16},{8,0},{16,24},{1,9},{25,17},{9,1},{17,25},{2,10},{26... | collective-permute-start | bytes 1179656 | tf_op jit(solution)/shard_map/ppermute | solution.py:107
  224.9 6.5 %collective-permute-done.43 = bf16[1536,128]{1,0:T(8,128)(2,1)S(1)} collective-permute-done((bf16[1536,128]{1,0:T(8,128)(2,1)S(1)}, bf16[1536,128]{1,0:T(8,128)(2,1)S(1)}, u32[]{:S(2)}, u32[]{:S(2)}) %collective-permute-start.43) | collective-permute-done | bytes 393248 | tf_op jit(solution)/shard_map/ppermute | solution.py:107
  233.8 2.6 %shard_map.97 = (f32[1536,1536]{1,0:T(8,128)}, bf16[1536,1536]{1,0:T(8,128)(2,1)}) custom-call(bf16[1536,128]{1,0:T(8,128)(2,1)S(1)} %broadcast_select_fusion.12.refs_0_, bf16[1536,128]{1,0:T(8,128)(2,1)S(1)} %broadcast_select_fusion.11.refs_1_, bf16[1536,128]{1,0:T(8,128)(2,1)S(1)} %broadcast_select_fusion.10.refs_2_, ...), custom_call_target="tpu_custom_call", output_to_operand_aliasing={{0}: (4, {}), {1}: (5, {})} | custom-call | flops 2949120 | bytes 7077888 | tf_op jit(solution)/shard_map/pallas_call | solution.py:61
  239.4 7.0 %collective-permute-done.47 = bf16[1536,128]{1,0:T(8,128)(2,1)S(1)} collective-permute-done((bf16[1536,128]{1,0:T(8,128)(2,1)S(1)}, bf16[1536,128]{1,0:T(8,128)(2,1)S(1)}, u32[]{:S(2)}, u32[]{:S(2)}) %collective-permute-start.47) | collective-permute-done | bytes 393248 | tf_op jit(solution)/shard_map/ppermute | solution.py:107
  246.4 1.9 shard_map.98
  248.4 2.2 collective-permute-done.46
  (181 shorter events, 43.8 us)
Async XLA Ops:
  0.6 19.7 %collective-permute-start = (bf16[256,1536]{1,0:T(8,128)(2,1)}, bf16[256,1536]{1,0:T(8,128)(2,1)}, u32[]{:S(2)}, u32[]{:S(2)}) collective-permute-start(bf16[256,1536]{1,0:T(8,128)(2,1)} %param.8), channel_id=1, source_target_pairs={{0,4},{2,6},{4,0},{6,2},{1,5},{3,7},{5,1},{7,3},{8,12},{10,14},{12... | collective-permute-start | bytes 2359304 | tf_op jit(solution)/shard_map/ppermute | solution.py:31
  3.8 16.5 %collective-permute-start.1 = (bf16[256,1536]{1,0:T(8,128)(2,1)S(1)}, bf16[256,1536]{1,0:T(8,128)(2,1)S(1)}, u32[]{:S(2)}, u32[]{:S(2)}) collective-permute-start(bf16[256,1536]{1,0:T(8,128)(2,1)S(1)} %get-tuple-element.314), channel_id=1, source_target_pairs={{0,2},{2,0},{4,6},{6,4},{1,3},{3,1},{5,7},{7,5},{8,10},{10,8},{12,... | collective-permute-start | bytes 2359304 | tf_op jit(solution)/shard_map/ppermute | solution.py:31
  4.2 16.1 %collective-permute-start.2 = (bf16[256,1536]{1,0:T(8,128)(2,1)S(1)}, bf16[256,1536]{1,0:T(8,128)(2,1)S(1)}, u32[]{:S(2)}, u32[]{:S(2)}) collective-permute-start(bf16[256,1536]{1,0:T(8,128)(2,1)S(1)} %get-tuple-element.312), channel_id=1, source_target_pairs={{0,2},{2,0},{4,6},{6,4},{1,3},{3,1},{5,7},{7,5},{8,10},{10,8},{12,... | collective-permute-start | bytes 2359304 | tf_op jit(solution)/shard_map/ppermute | solution.py:31
  5.0 21.7 %collective-permute-start.5 = (bf16[256,1536]{1,0:T(8,128)(2,1)S(1)}, bf16[256,1536]{1,0:T(8,128)(2,1)S(1)}, u32[]{:S(2)}, u32[]{:S(2)}) collective-permute-start(bf16[256,1536]{1,0:T(8,128)(2,1)S(1)} %copy-done.1), channel_id=1, source_target_pairs={{0,2},{2,0},{4,6},{6,4},{1,3},{3,1},{5,7},{7,5},{8,10},{10,8},{12,... | collective-permute-start | bytes 2359304 | tf_op jit(solution)/shard_map/ppermute | solution.py:31
  20.3 17.8 %collective-permute-start.9 = (bf16[256,1536]{1,0:T(8,128)(2,1)}, bf16[256,1536]{1,0:T(8,128)(2,1)S(1)}, u32[]{:S(2)}, u32[]{:S(2)}) collective-permute-start(bf16[256,1536]{1,0:T(8,128)(2,1)} %collective-permute-done), channel_id=1, source_target_pairs={{0,2},{2,0},{4,6},{6,4},{1,3},{3,1},{5,7},{7,5},{8,10},{10,8},{12,... | collective-permute-start | bytes 2359304 | tf_op jit(solution)/shard_map/ppermute | solution.py:31
  25.2 11.6 %collective-permute-start.6 = (bf16[128,1536]{1,0:T(8,128)(2,1)S(1)}, bf16[128,1536]{1,0:T(8,128)(2,1)}, u32[]{:S(2)}, u32[]{:S(2)}) collective-permute-start(bf16[128,1536]{1,0:T(8,128)(2,1)S(1)} %get-tuple-element.322), channel_id=1, source_target_pairs={{0,4},{2,6},{4,0},{6,2},{1,5},{3,7},{5,1},{7,3},{8,12},{10,14},{12... | collective-permute-start | bytes 1179656 | tf_op jit(solution)/shard_map/ppermute | solution.py:31
  30.8 36.7 %collective-permute-start.7 = (bf16[512,1536]{1,0:T(8,128)(2,1)}, bf16[512,1536]{1,0:T(8,128)(2,1)}, u32[]{:S(2)}, u32[]{:S(2)}) collective-permute-start(bf16[512,1536]{1,0:T(8,128)(2,1)} %convolution_convert_fusion), channel_id=1, source_target_pairs={{4,5},{1,0},{6,7},{3,2},{12,13},{9,8},{14,15},{11,10},{20,21},{17,... | collective-permute-start | bytes 4718600 | tf_op jit(solution)/shard_map/ppermute | solution.py:168
  34.4 13.2 %collective-permute-start.3 = (bf16[128,1536]{1,0:T(8,128)(2,1)}, bf16[128,1536]{1,0:T(8,128)(2,1)}, u32[]{:S(2)}, u32[]{:S(2)}) collective-permute-start(bf16[128,1536]{1,0:T(8,128)(2,1)} %get-tuple-element.323), channel_id=1, source_target_pairs={{0,4},{2,6},{4,0},{6,2},{1,5},{3,7},{5,1},{7,3},{8,12},{10,14},{12... | collective-permute-start | bytes 1179656 | tf_op jit(solution)/shard_map/ppermute | solution.py:31
  36.8 26.9 %collective-permute-start.8 = (bf16[128,1536]{1,0:T(8,128)(2,1)}, bf16[128,1536]{1,0:T(8,128)(2,1)}, u32[]{:S(2)}, u32[]{:S(2)}) collective-permute-start(bf16[128,1536]{1,0:T(8,128)(2,1)} %collective-permute-done.6), channel_id=1, source_target_pairs={{0,1},{5,4},{2,3},{7,6},{8,9},{13,12},{10,11},{15,14},{16,17},{21,... | collective-permute-start | bytes 1179656 | tf_op jit(solution)/shard_map/ppermute | solution.py:173
  40.4 14.8 %collective-permute-start.10 = (bf16[128,1536]{1,0:T(8,128)(2,1)}, bf16[128,1536]{1,0:T(8,128)(2,1)}, u32[]{:S(2)}, u32[]{:S(2)}) collective-permute-start(bf16[128,1536]{1,0:T(8,128)(2,1)} %get-tuple-element.324), channel_id=1, source_target_pairs={{0,4},{2,6},{4,0},{6,2},{1,5},{3,7},{5,1},{7,3},{8,12},{10,14},{12... | collective-permute-start | bytes 1179656 | tf_op jit(solution)/shard_map/ppermute | solution.py:31
  43.8 18.6 %collective-permute-start.12 = (bf16[128,1536]{1,0:T(8,128)(2,1)}, bf16[128,1536]{1,0:T(8,128)(2,1)S(1)}, u32[]{:S(2)}, u32[]{:S(2)}) collective-permute-start(bf16[128,1536]{1,0:T(8,128)(2,1)} %get-tuple-element.325), channel_id=1, source_target_pairs={{0,4},{2,6},{4,0},{6,2},{1,5},{3,7},{5,1},{7,3},{8,12},{10,14},{12... | collective-permute-start | bytes 1179656 | tf_op jit(solution)/shard_map/ppermute | solution.py:31
  47.6 21.8 %collective-permute-start.4 = (bf16[128,1536]{1,0:T(8,128)(2,1)}, bf16[128,1536]{1,0:T(8,128)(2,1)S(1)}, u32[]{:S(2)}, u32[]{:S(2)}) collective-permute-start(bf16[128,1536]{1,0:T(8,128)(2,1)} %collective-permute-done.3), channel_id=1, source_target_pairs={{0,1},{5,4},{2,3},{7,6},{8,9},{13,12},{10,11},{15,14},{16,17},{21,... | collective-permute-start | bytes 1179656 | tf_op jit(solution)/shard_map/ppermute | solution.py:173
  55.2 16.0 %collective-permute-start.11 = (bf16[128,1536]{1,0:T(8,128)(2,1)}, bf16[128,1536]{1,0:T(8,128)(2,1)S(1)}, u32[]{:S(2)}, u32[]{:S(2)}) collective-permute-start(bf16[128,1536]{1,0:T(8,128)(2,1)} %collective-permute-done.10), channel_id=1, source_target_pairs={{0,1},{5,4},{2,3},{7,6},{8,9},{13,12},{10,11},{15,14},{16,17},{21,... | collective-permute-start | bytes 1179656 | tf_op jit(solution)/shard_map/ppermute | solution.py:173
  62.4 14.3 %collective-permute-start.13 = (bf16[128,1536]{1,0:T(8,128)(2,1)S(1)}, bf16[128,1536]{1,0:T(8,128)(2,1)S(1)}, u32[]{:S(2)}, u32[]{:S(2)}) collective-permute-start(bf16[128,1536]{1,0:T(8,128)(2,1)S(1)} %collective-permute-done.12), channel_id=1, source_target_pairs={{0,1},{5,4},{2,3},{7,6},{8,9},{13,12},{10,11},{15,14},{16,17},{21,... | collective-permute-start | bytes 1179656 | tf_op jit(solution)/shard_map/ppermute | solution.py:173
  79.8 3.7 %collective-permute-start.15 = (f32[2,512]{1,0:T(2,128)S(1)}, f32[2,512]{1,0:T(2,128)S(1)}, u32[]{:S(2)}, u32[]{:S(2)}) collective-permute-start(f32[2,512]{1,0:T(2,128)S(1)} %maximum_add_fusion), channel_id=1, source_target_pairs={{0,1},{1,0},{2,3},{3,2},{4,5},{5,4},{6,7},{7,6},{8,9},{9,8},{10,11... | collective-permute-start | bytes 12296 | tf_op jit(solution)/shard_map/ppermute | solution.py:31
  83.8 8.4 %collective-permute-start.17 = (bf16[512,128]{1,0:T(8,128)(2,1)S(1)}, bf16[512,128]{1,0:T(8,128)(2,1)S(1)}, u32[]{:S(2)}, u32[]{:S(2)}) collective-permute-start(bf16[512,128]{1,0:T(8,128)(2,1)S(1)} %pad_maximum_fusion.5), channel_id=1, source_target_pairs={{4,1},{1,4},{6,3},{3,6},{12,9},{9,12},{14,11},{11,14},{20,17},{17,... | collective-permute-start | bytes 393224 | tf_op jit(solution)/shard_map/ppermute | solution.py:231
  87.2 5.0 %collective-permute-start.16 = (bf16[512,128]{1,0:T(8,128)(2,1)S(1)}, bf16[512,128]{1,0:T(8,128)(2,1)S(1)}, u32[]{:S(2)}, u32[]{:S(2)}) collective-permute-start(bf16[512,128]{1,0:T(8,128)(2,1)S(1)} %pad_maximum_fusion.5), channel_id=1, source_target_pairs={{0,1},{5,4},{4,0},{1,5},{2,3},{7,6},{6,2},{3,7},{8,9},{13,12},{12,... | collective-permute-start | bytes 393224 | tf_op jit(solution)/shard_map/ppermute | solution.py:227
  92.2 34.5 %collective-permute-start.20 = (bf16[512,384]{1,0:T(8,128)(2,1)S(1)}, bf16[512,384]{1,0:T(8,128)(2,1)S(1)}, u32[]{:S(2)}, u32[]{:S(2)}) collective-permute-start(bf16[512,384]{1,0:T(8,128)(2,1)S(1)} %pad_maximum_fusion.2), channel_id=1, source_target_pairs={{0,1},{5,4},{4,0},{1,5},{2,3},{7,6},{6,2},{3,7},{8,9},{13,12},{12,... | collective-permute-start | bytes 1179656 | tf_op jit(solution)/shard_map/ppermute | solution.py:227
  92.2 52.2 %collective-permute-start.19 = (bf16[512,1024]{1,0:T(8,128)(2,1)S(1)}, bf16[512,1024]{1,0:T(8,128)(2,1)S(1)}, u32[]{:S(2)}, u32[]{:S(2)}) collective-permute-start(bf16[512,1024]{1,0:T(8,128)(2,1)S(1)} %pad_maximum_fusion), channel_id=1, source_target_pairs={{4,1},{1,4},{6,3},{3,6},{12,9},{9,12},{14,11},{11,14},{20,17},{17,... | collective-permute-start | bytes 3145736 | tf_op jit(solution)/shard_map/ppermute | solution.py:231
  95.6 48.8 %collective-permute-start.18 = (bf16[512,1024]{1,0:T(8,128)(2,1)S(1)}, bf16[512,1024]{1,0:T(8,128)(2,1)S(1)}, u32[]{:S(2)}, u32[]{:S(2)}) collective-permute-start(bf16[512,1024]{1,0:T(8,128)(2,1)S(1)} %pad_maximum_fusion), channel_id=1, source_target_pairs={{0,1},{5,4},{4,0},{1,5},{2,3},{7,6},{6,2},{3,7},{8,9},{13,12},{12,... | collective-permute-start | bytes 3145736 | tf_op jit(solution)/shard_map/ppermute | solution.py:227
  95.8 30.9 %collective-permute-start.21 = (bf16[512,384]{1,0:T(8,128)(2,1)S(1)}, bf16[512,384]{1,0:T(8,128)(2,1)S(1)}, u32[]{:S(2)}, u32[]{:S(2)}) collective-permute-start(bf16[512,384]{1,0:T(8,128)(2,1)S(1)} %pad_maximum_fusion.2), channel_id=1, source_target_pairs={{4,1},{1,4},{6,3},{3,6},{12,9},{9,12},{14,11},{11,14},{20,17},{17,... | collective-permute-start | bytes 1179656 | tf_op jit(solution)/shard_map/ppermute | solution.py:231
  101.9 32.1 %collective-permute-start.22 = (bf16[1536,128]{1,0:T(8,128)(2,1)S(1)}, bf16[1536,128]{1,0:T(8,128)(2,1)S(1)}, u32[]{:S(2)}, u32[]{:S(2)}) collective-permute-start(bf16[1536,128]{1,0:T(8,128)(2,1)S(1)} %fusion.51), channel_id=1, source_target_pairs={{0,8},{24,16},{1,9},{25,17},{2,10},{26,18},{3,11},{27,19},{4,12},{... | collective-permute-start | bytes 1179656 | tf_op jit(solution)/shard_map/ppermute | solution.py:107
  130.5 13.0 %collective-permute-start.23 = (bf16[1536,128]{1,0:T(8,128)(2,1)S(1)}, bf16[1536,128]{1,0:T(8,128)(2,1)S(1)}, u32[]{:S(2)}, u32[]{:S(2)}) collective-permute-start(bf16[1536,128]{1,0:T(8,128)(2,1)S(1)} %fusion.50), channel_id=1, source_target_pairs={{0,8},{24,16},{1,9},{25,17},{2,10},{26,18},{3,11},{27,19},{4,12},{... | collective-permute-start | bytes 1179656 | tf_op jit(solution)/shard_map/ppermute | solution.py:107
  134.2 10.2 %collective-permute-start.26 = (bf16[1536,128]{1,0:T(8,128)(2,1)S(1)}, bf16[1536,128]{1,0:T(8,128)(2,1)S(1)}, u32[]{:S(2)}, u32[]{:S(2)}) collective-permute-start(bf16[1536,128]{1,0:T(8,128)(2,1)S(1)} %add_convert_fusion.23), channel_id=1, source_target_pairs={{8,16},{16,8},{9,17},{17,9},{10,18},{18,10},{11,19},{19,11},{12,20... | collective-permute-start | bytes 1179656 | tf_op jit(solution)/shard_map/ppermute | solution.py:115
  134.9 17.6 %collective-permute-start.25 = (bf16[1536,128]{1,0:T(8,128)(2,1)S(1)}, bf16[1536,128]{1,0:T(8,128)(2,1)S(1)}, u32[]{:S(2)}, u32[]{:S(2)}) collective-permute-start(bf16[1536,128]{1,0:T(8,128)(2,1)S(1)} %slice.458), channel_id=1, source_target_pairs={{0,8},{24,16},{1,9},{25,17},{2,10},{26,18},{3,11},{27,19},{4,12},{... | collective-permute-start | bytes 1179656 | tf_op jit(solution)/shard_map/ppermute | solution.py:107
  143.7 9.6 %collective-permute-start.24 = (bf16[1536,128]{1,0:T(8,128)(2,1)S(1)}, bf16[1536,128]{1,0:T(8,128)(2,1)S(1)}, u32[]{:S(2)}, u32[]{:S(2)}) collective-permute-start(bf16[1536,128]{1,0:T(8,128)(2,1)S(1)} %add_convert_fusion.22), channel_id=1, source_target_pairs={{8,16},{16,8},{9,17},{17,9},{10,18},{18,10},{11,19},{19,11},{12,20... | collective-permute-start | bytes 1179656 | tf_op jit(solution)/shard_map/ppermute | solution.py:115
  147.1 15.3 %collective-permute-start.28 = (bf16[1536,128]{1,0:T(8,128)(2,1)S(1)}, bf16[1536,128]{1,0:T(8,128)(2,1)S(1)}, u32[]{:S(2)}, u32[]{:S(2)}) collective-permute-start(bf16[1536,128]{1,0:T(8,128)(2,1)S(1)} %fusion.64), channel_id=1, source_target_pairs={{0,8},{24,16},{8,0},{16,24},{1,9},{25,17},{9,1},{17,25},{2,10},{26... | collective-permute-start | bytes 1179656 | tf_op jit(solution)/shard_map/ppermute | solution.py:107
  152.6 10.7 %collective-permute-start.27 = (bf16[1536,128]{1,0:T(8,128)(2,1)S(1)}, bf16[1536,128]{1,0:T(8,128)(2,1)S(1)}, u32[]{:S(2)}, u32[]{:S(2)}) collective-permute-start(bf16[1536,128]{1,0:T(8,128)(2,1)S(1)} %add_convert_fusion.20), channel_id=1, source_target_pairs={{8,16},{16,8},{9,17},{17,9},{10,18},{18,10},{11,19},{19,11},{12,20... | collective-permute-start | bytes 1179656 | tf_op jit(solution)/shard_map/ppermute | solution.py:115
  155.6 15.7 %collective-permute-start.30 = (bf16[1536,128]{1,0:T(8,128)(2,1)S(1)}, bf16[1536,128]{1,0:T(8,128)(2,1)S(1)}, u32[]{:S(2)}, u32[]{:S(2)}) collective-permute-start(bf16[1536,128]{1,0:T(8,128)(2,1)S(1)} %fusion.65), channel_id=1, source_target_pairs={{0,8},{24,16},{8,0},{16,24},{1,9},{25,17},{9,1},{17,25},{2,10},{26... | collective-permute-start | bytes 1179656 | tf_op jit(solution)/shard_map/ppermute | solution.py:107
  162.6 9.8 %collective-permute-start.31 = (bf16[1536,128]{1,0:T(8,128)(2,1)S(1)}, bf16[1536,128]{1,0:T(8,128)(2,1)S(1)}, u32[]{:S(2)}, u32[]{:S(2)}) collective-permute-start(bf16[1536,128]{1,0:T(8,128)(2,1)S(1)} %add_convert_fusion.18), channel_id=1, source_target_pairs={{8,16},{16,8},{9,17},{17,9},{10,18},{18,10},{11,19},{19,11},{12,20... | collective-permute-start | bytes 1179656 | tf_op jit(solution)/shard_map/ppermute | solution.py:115
  163.4 16.3 %collective-permute-start.29 = (bf16[1536,128]{1,0:T(8,128)(2,1)S(1)}, bf16[1536,128]{1,0:T(8,128)(2,1)S(1)}, u32[]{:S(2)}, u32[]{:S(2)}) collective-permute-start(bf16[1536,128]{1,0:T(8,128)(2,1)S(1)} %fusion.66), channel_id=1, source_target_pairs={{0,8},{24,16},{8,0},{16,24},{1,9},{25,17},{9,1},{17,25},{2,10},{26... | collective-permute-start | bytes 1179656 | tf_op jit(solution)/shard_map/ppermute | solution.py:107
  171.4 11.5 %collective-permute-start.34 = (bf16[1536,128]{1,0:T(8,128)(2,1)S(1)}, bf16[1536,128]{1,0:T(8,128)(2,1)S(1)}, u32[]{:S(2)}, u32[]{:S(2)}) collective-permute-start(bf16[1536,128]{1,0:T(8,128)(2,1)S(1)} %add_convert_fusion.16), channel_id=1, source_target_pairs={{8,16},{16,8},{9,17},{17,9},{10,18},{18,10},{11,19},{19,11},{12,20... | collective-permute-start | bytes 1179656 | tf_op jit(solution)/shard_map/ppermute | solution.py:115
  172.5 17.2 %collective-permute-start.33 = (bf16[1536,128]{1,0:T(8,128)(2,1)S(1)}, bf16[1536,128]{1,0:T(8,128)(2,1)S(1)}, u32[]{:S(2)}, u32[]{:S(2)}) collective-permute-start(bf16[1536,128]{1,0:T(8,128)(2,1)S(1)} %fusion.67), channel_id=1, source_target_pairs={{0,8},{24,16},{8,0},{16,24},{1,9},{25,17},{9,1},{17,25},{2,10},{26... | collective-permute-start | bytes 1179656 | tf_op jit(solution)/shard_map/ppermute | solution.py:107
  182.1 8.4 %collective-permute-start.32 = (bf16[1536,128]{1,0:T(8,128)(2,1)S(1)}, bf16[1536,128]{1,0:T(8,128)(2,1)S(1)}, u32[]{:S(2)}, u32[]{:S(2)}) collective-permute-start(bf16[1536,128]{1,0:T(8,128)(2,1)S(1)} %add_convert_fusion.14), channel_id=1, source_target_pairs={{8,16},{16,8},{9,17},{17,9},{10,18},{18,10},{11,19},{19,11},{12,20... | collective-permute-start | bytes 1179656 | tf_op jit(solution)/shard_map/ppermute | solution.py:115
  183.1 14.2 %collective-permute-start.36 = (bf16[1536,128]{1,0:T(8,128)(2,1)S(1)}, bf16[1536,128]{1,0:T(8,128)(2,1)S(1)}, u32[]{:S(2)}, u32[]{:S(2)}) collective-permute-start(bf16[1536,128]{1,0:T(8,128)(2,1)S(1)} %fusion.68), channel_id=1, source_target_pairs={{0,8},{24,16},{8,0},{16,24},{1,9},{25,17},{9,1},{17,25},{2,10},{26... | collective-permute-start | bytes 1179656 | tf_op jit(solution)/shard_map/ppermute | solution.py:107
  189.8 8.3 %collective-permute-start.35 = (bf16[1536,128]{1,0:T(8,128)(2,1)S(1)}, bf16[1536,128]{1,0:T(8,128)(2,1)S(1)}, u32[]{:S(2)}, u32[]{:S(2)}) collective-permute-start(bf16[1536,128]{1,0:T(8,128)(2,1)S(1)} %add_convert_fusion.12), channel_id=1, source_target_pairs={{8,16},{16,8},{9,17},{17,9},{10,18},{18,10},{11,19},{19,11},{12,20... | collective-permute-start | bytes 1179656 | tf_op jit(solution)/shard_map/ppermute | solution.py:115
  190.7 14.8 %collective-permute-start.38 = (bf16[1536,128]{1,0:T(8,128)(2,1)S(1)}, bf16[1536,128]{1,0:T(8,128)(2,1)S(1)}, u32[]{:S(2)}, u32[]{:S(2)}) collective-permute-start(bf16[1536,128]{1,0:T(8,128)(2,1)S(1)} %fusion.69), channel_id=1, source_target_pairs={{0,8},{24,16},{8,0},{16,24},{1,9},{25,17},{9,1},{17,25},{2,10},{26... | collective-permute-start | bytes 1179656 | tf_op jit(solution)/shard_map/ppermute | solution.py:107
  197.4 8.9 %collective-permute-start.37 = (bf16[1536,128]{1,0:T(8,128)(2,1)S(1)}, bf16[1536,128]{1,0:T(8,128)(2,1)S(1)}, u32[]{:S(2)}, u32[]{:S(2)}) collective-permute-start(bf16[1536,128]{1,0:T(8,128)(2,1)S(1)} %add_convert_fusion.10), channel_id=1, source_target_pairs={{8,16},{16,8},{9,17},{17,9},{10,18},{18,10},{11,19},{19,11},{12,20... | collective-permute-start | bytes 1179656 | tf_op jit(solution)/shard_map/ppermute | solution.py:115
  198.3 17.0 %collective-permute-start.40 = (bf16[1536,128]{1,0:T(8,128)(2,1)S(1)}, bf16[1536,128]{1,0:T(8,128)(2,1)S(1)}, u32[]{:S(2)}, u32[]{:S(2)}) collective-permute-start(bf16[1536,128]{1,0:T(8,128)(2,1)S(1)} %fusion.70), channel_id=1, source_target_pairs={{0,8},{24,16},{8,0},{16,24},{1,9},{25,17},{9,1},{17,25},{2,10},{26... | collective-permute-start | bytes 1179656 | tf_op jit(solution)/shard_map/ppermute | solution.py:107
  205.6 10.5 %collective-permute-start.41 = (bf16[1536,128]{1,0:T(8,128)(2,1)S(1)}, bf16[1536,128]{1,0:T(8,128)(2,1)S(1)}, u32[]{:S(2)}, u32[]{:S(2)}) collective-permute-start(bf16[1536,128]{1,0:T(8,128)(2,1)S(1)} %add_convert_fusion.8), channel_id=1, source_target_pairs={{8,16},{16,8},{9,17},{17,9},{10,18},{18,10},{11,19},{19,11},{12,20... | collective-permute-start | bytes 1179656 | tf_op jit(solution)/shard_map/ppermute | solution.py:115
  206.5 16.2 %collective-permute-start.39 = (bf16[1536,128]{1,0:T(8,128)(2,1)S(1)}, bf16[1536,128]{1,0:T(8,128)(2,1)S(1)}, u32[]{:S(2)}, u32[]{:S(2)}) collective-permute-start(bf16[1536,128]{1,0:T(8,128)(2,1)S(1)} %fusion.71), channel_id=1, source_target_pairs={{0,8},{24,16},{8,0},{16,24},{1,9},{25,17},{9,1},{17,25},{2,10},{26... | collective-permute-start | bytes 1179656 | tf_op jit(solution)/shard_map/ppermute | solution.py:107
  215.4 8.1 %collective-permute-start.44 = (bf16[1536,128]{1,0:T(8,128)(2,1)S(1)}, bf16[1536,128]{1,0:T(8,128)(2,1)S(1)}, u32[]{:S(2)}, u32[]{:S(2)}) collective-permute-start(bf16[1536,128]{1,0:T(8,128)(2,1)S(1)} %add_convert_fusion.6), channel_id=1, source_target_pairs={{8,16},{16,8},{9,17},{17,9},{10,18},{18,10},{11,19},{19,11},{12,20... | collective-permute-start | bytes 1179656 | tf_op jit(solution)/shard_map/ppermute | solution.py:115
  216.3 15.2 %collective-permute-start.43 = (bf16[1536,128]{1,0:T(8,128)(2,1)S(1)}, bf16[1536,128]{1,0:T(8,128)(2,1)S(1)}, u32[]{:S(2)}, u32[]{:S(2)}) collective-permute-start(bf16[1536,128]{1,0:T(8,128)(2,1)S(1)} %fusion.72), channel_id=1, source_target_pairs={{0,8},{24,16},{8,0},{16,24},{1,9},{25,17},{9,1},{17,25},{2,10},{26... | collective-permute-start | bytes 1179656 | tf_op jit(solution)/shard_map/ppermute | solution.py:107
  222.8 9.5 %collective-permute-start.42 = (bf16[1536,128]{1,0:T(8,128)(2,1)S(1)}, bf16[1536,128]{1,0:T(8,128)(2,1)S(1)}, u32[]{:S(2)}, u32[]{:S(2)}) collective-permute-start(bf16[1536,128]{1,0:T(8,128)(2,1)S(1)} %add_convert_fusion.4), channel_id=1, source_target_pairs={{8,16},{16,8},{9,17},{17,9},{10,18},{18,10},{11,19},{19,11},{12,20... | collective-permute-start | bytes 1179656 | tf_op jit(solution)/shard_map/ppermute | solution.py:115
  223.6 15.7 %collective-permute-start.48 = (bf16[1536,128]{1,0:T(8,128)(2,1)S(1)}, bf16[1536,128]{1,0:T(8,128)(2,1)S(1)}, u32[]{:S(2)}, u32[]{:S(2)}) collective-permute-start(bf16[1536,128]{1,0:T(8,128)(2,1)S(1)} %add_convert_fusion.3), channel_id=1, source_target_pairs={{8,0},{16,24},{9,1},{17,25},{10,2},{18,26},{11,3},{19,27},{12,4},{... | collective-permute-start | bytes 1179656 | tf_op jit(solution)/shard_map/ppermute | solution.py:107
  231.6 4.8 %collective-permute-start.45 = (bf16[1536,128]{1,0:T(8,128)(2,1)S(1)}, bf16[1536,128]{1,0:T(8,128)(2,1)S(1)}, u32[]{:S(2)}, u32[]{:S(2)}) collective-permute-start(bf16[1536,128]{1,0:T(8,128)(2,1)S(1)} %add_convert_fusion.2), channel_id=1, source_target_pairs={{8,16},{16,8},{9,17},{17,9},{10,18},{18,10},{11,19},{19,11},{12,20... | collective-permute-start | bytes 1179656 | tf_op jit(solution)/shard_map/ppermute | solution.py:115
  232.4 13.9 %collective-permute-start.47 = (bf16[1536,128]{1,0:T(8,128)(2,1)S(1)}, bf16[1536,128]{1,0:T(8,128)(2,1)S(1)}, u32[]{:S(2)}, u32[]{:S(2)}) collective-permute-start(bf16[1536,128]{1,0:T(8,128)(2,1)S(1)} %add_convert_fusion), channel_id=1, source_target_pairs={{8,0},{16,24},{9,1},{17,25},{10,2},{18,26},{11,3},{19,27},{12,4},{... | collective-permute-start | bytes 1179656 | tf_op jit(solution)/shard_map/ppermute | solution.py:107
  236.5 14.1 %collective-permute-start.46 = (bf16[1536,128]{1,0:T(8,128)(2,1)S(1)}, bf16[1536,128]{1,0:T(8,128)(2,1)S(1)}, u32[]{:S(2)}, u32[]{:S(2)}) collective-permute-start(bf16[1536,128]{1,0:T(8,128)(2,1)S(1)} %add_convert_fusion.1), channel_id=1, source_target_pairs={{8,0},{16,24},{9,1},{17,25},{10,2},{18,26},{11,3},{19,27},{12,4},{... | collective-permute-start | bytes 1179656 | tf_op jit(solution)/shard_map/ppermute | solution.py:107
  (18 other events, 194.4 us)

commit v17 on v16

--- a/solution.py
+++ b/solution.py
@@ -225,10 +225,7 @@
             d_local, crosses[0] = together(d_local, crosses[0])
         locals_.append(d_local)
         rings.append(lax.ppermute(d_local, ("fsdp", "tp"), ring_pairs))
-        d_cross = d_local
-        if c == 1:
-            d_cross, crosses[0] = together(d_local, crosses[0])
-        crosses.append(lax.ppermute(d_cross, ("fsdp", "tp"), cross_pairs))
+        crosses.append(lax.ppermute(d_local, ("fsdp", "tp"), cross_pairs))
 
     def gathered(c):
         d_near = jnp.where(near, locals_[c], rings[c])

time: 253 us -> 232 us (0.917)
  waiting for transfers between devices: 95.7 us -> 75.7 us
    ppermute x3, waiting for transfers between devices: 21.1 us -> 3.3 us  [move(): crosses.append(lax.ppermute(d_local, ('fsdp', 'tp'), cross_pairs))]
  transfers between devices with their start and end apart: 49 -> 49, of which waited for: 18 -> 22; matrix products, arithmetic and copies ran while one was open for 17% -> 19% of each run, Pallas kernels for 4% -> 4%
where the time goes in v17:
time: 232 us; the launch traced here: 231 us
  starting transfers between devices  96.2 us (41%)
  waiting for transfers between devices  75.7 us (33%)
  matrix products  24.4 us (11%)
  other arithmetic  13 us (6%)
  Pallas kernels  11 us (5%)
  local copies, waits for them, and re-layouts  8.57 us (4%)
    ppermute x15, starting transfers between devices, send_outer(): self.edge[s] = lax.ppermute(payload, 'island', pairs)  61.5 us
    ppermute x11, waiting for transfers between devices, swap(): return lax.ppermute(value, axis, [(i, i ^ bit) for i in range(count)])  33.4 us
    ppermute x15, waiting for transfers between devices, send_outer(): self.edge[s] = lax.ppermute(payload, 'island', pairs)  29.8 us
    dot_general x7, matrix products, add_pseudo(): lax.dot_general(context_all, piece, (((0,), (0,)), ((), ())), preferred_e...  15 us
    pallas_call x5, Pallas kernels, finish(): pl.pallas_call(functools.partial(finish_kernel, count, start, narrow, isl...  11 us
    ppermute x3, starting transfers between devices, move(): crosses.append(lax.ppermute(d_local, ('fsdp', 'tp'), cross_pairs))  10.1 us
    dot_general x3, matrix products, project(): jnp.dot(block, weight, preferred_element_type=f32).astype(bf16)  9.49 us
    ppermute x12, starting transfers between devices, step(): self.mid[s] = lax.ppermute(self.sums[s], 'island', [(1, 2), (2, 1)])  8.58 us
  transfers between devices with their start and end apart: 49, of which 22 were waited for; matrix products, arithmetic and copies ran while one was open for 19% of the time, Pallas kernels for 4%

profile of v17, /device:TPU:2, one launch (start us, length us, event | category | flops | bytes accessed | tf_op | source)
XLA Modules:
  0.0 231.0 jit_solution(10345455403982463305)
XLA Ops:
  5.0 15.3 %collective-permute-done = bf16[256,1536]{1,0:T(8,128)(2,1)} collective-permute-done((bf16[256,1536]{1,0:T(8,128)(2,1)}, bf16[256,1536]{1,0:T(8,128)(2,1)}, u32[]{:S(2)}, u32[]{:S(2)}) %collective-permute-start) | collective-permute-done | bytes 786464 | tf_op jit(solution)/shard_map/ppermute | solution.py:31
  20.4 4.0 %convolution_convert_fusion.2 = bf16[256,1536]{1,0:T(8,128)(2,1)S(1)} fusion(bf16[256,1536]{1,0:T(8,128)(2,1)} %collective-permute-done, bf16[1536,1536]{1,0:T(8,128)(2,1)} %param.12), kind=kOutput, calls=%fused_computation.8 | convolution fusion | flops 1208352768 | bytes 6291456 | tf_op jit(solution)/shard_map/dot_general | solution.py:144
  26.7 4.1 %convolution_convert_fusion = bf16[512,1536]{1,0:T(8,128)(2,1)} fusion(bf16[1536,1536]{1,0:T(8,128)(2,1)S(1)} %bitcast.206, bf16[256,1536]{1,0:T(8,128)(2,1)S(1)} %collective-permute-done.5, bf16[256,1536]{1,0:T(8,128)(2,1)S(1)} %copy-done.1), kind=kOutput, calls=%fused_computation | convolution fusion | flops 2419851264 | bytes 7864320 | tf_op jit(solution)/shard_map/dot_general | solution.py:144
  30.8 3.6 %collective-permute-start.7 = (bf16[512,1536]{1,0:T(8,128)(2,1)}, bf16[512,1536]{1,0:T(8,128)(2,1)}, u32[]{:S(2)}, u32[]{:S(2)}) collective-permute-start(bf16[512,1536]{1,0:T(8,128)(2,1)} %convolution_convert_fusion), channel_id=1, source_target_pairs={{4,5},{1,0},{6,7},{3,2},{12,13},{9,8},{14,15},{11,10},{20,21},{17,... | collective-permute-start | bytes 4718600 | tf_op jit(solution)/shard_map/ppermute | solution.py:168
  34.4 2.3 %collective-permute-done.6 = bf16[128,1536]{1,0:T(8,128)(2,1)} collective-permute-done((bf16[128,1536]{1,0:T(8,128)(2,1)S(1)}, bf16[128,1536]{1,0:T(8,128)(2,1)}, u32[]{:S(2)}, u32[]{:S(2)}) %collective-permute-start.6) | collective-permute-done | bytes 393248 | tf_op jit(solution)/shard_map/ppermute | solution.py:31
  40.4 3.4 %collective-permute-start.10 = (bf16[128,1536]{1,0:T(8,128)(2,1)}, bf16[128,1536]{1,0:T(8,128)(2,1)}, u32[]{:S(2)}, u32[]{:S(2)}) collective-permute-start(bf16[128,1536]{1,0:T(8,128)(2,1)} %get-tuple-element.320), channel_id=1, source_target_pairs={{0,4},{2,6},{4,0},{6,2},{1,5},{3,7},{5,1},{7,3},{8,12},{10,14},{12... | collective-permute-start | bytes 1179656 | tf_op jit(solution)/shard_map/ppermute | solution.py:31
  45.5 2.1 constant_dynamic-update-slice_fusion.2
  48.9 6.3 %collective-permute-done.10 = bf16[128,1536]{1,0:T(8,128)(2,1)} collective-permute-done((bf16[128,1536]{1,0:T(8,128)(2,1)}, bf16[128,1536]{1,0:T(8,128)(2,1)}, u32[]{:S(2)}, u32[]{:S(2)}) %collective-permute-start.10) | collective-permute-done | bytes 393248 | tf_op jit(solution)/shard_map/ppermute | solution.py:31
  56.5 6.0 %collective-permute-done.12 = bf16[128,1536]{1,0:T(8,128)(2,1)S(1)} collective-permute-done((bf16[128,1536]{1,0:T(8,128)(2,1)}, bf16[128,1536]{1,0:T(8,128)(2,1)S(1)}, u32[]{:S(2)}, u32[]{:S(2)}) %collective-permute-start.12) | collective-permute-done | bytes 393248 | tf_op jit(solution)/shard_map/ppermute | solution.py:31
  63.7 3.9 %collective-permute-done.7 = bf16[512,1536]{1,0:T(8,128)(2,1)} collective-permute-done((bf16[512,1536]{1,0:T(8,128)(2,1)}, bf16[512,1536]{1,0:T(8,128)(2,1)}, u32[]{:S(2)}, u32[]{:S(2)}) %collective-permute-start.7) | collective-permute-done | bytes 1572896 | tf_op jit(solution)/shard_map/ppermute | solution.py:168
  67.6 1.8 multiply_reduce_fusion.7
  69.4 1.8 multiply_reduce_fusion.5
  71.2 1.7 multiply_reduce_fusion.3
  73.0 3.7 %collective-permute-done.13 = bf16[128,1536]{1,0:T(8,128)(2,1)S(1)} collective-permute-done((bf16[128,1536]{1,0:T(8,128)(2,1)S(1)}, bf16[128,1536]{1,0:T(8,128)(2,1)S(1)}, u32[]{:S(2)}, u32[]{:S(2)}) %collective-permute-start.13) | collective-permute-done | bytes 393248 | tf_op jit(solution)/shard_map/ppermute | solution.py:173
  80.0 3.5 %collective-permute-done.15 = f32[2,512]{1,0:T(2,128)S(1)} collective-permute-done((f32[2,512]{1,0:T(2,128)S(1)}, f32[2,512]{1,0:T(2,128)S(1)}, u32[]{:S(2)}, u32[]{:S(2)}) %collective-permute-start.15) | collective-permute-done | bytes 4128 | tf_op jit(solution)/shard_map/ppermute | solution.py:31
  83.9 3.4 %collective-permute-start.16 = (bf16[512,128]{1,0:T(8,128)(2,1)S(1)}, bf16[512,128]{1,0:T(8,128)(2,1)S(1)}, u32[]{:S(2)}, u32[]{:S(2)}) collective-permute-start(bf16[512,128]{1,0:T(8,128)(2,1)S(1)} %pad_maximum_fusion.5), channel_id=1, source_target_pairs={{4,1},{1,4},{6,3},{3,6},{12,9},{9,12},{14,11},{11,14},{20,17},{17,... | collective-permute-start | bytes 393224 | tf_op jit(solution)/shard_map/ppermute | solution.py:228
  88.9 3.3 %collective-permute-start.21 = (bf16[512,384]{1,0:T(8,128)(2,1)S(1)}, bf16[512,384]{1,0:T(8,128)(2,1)S(1)}, u32[]{:S(2)}, u32[]{:S(2)}) collective-permute-start(bf16[512,384]{1,0:T(8,128)(2,1)S(1)} %pad_maximum_fusion.2), channel_id=1, source_target_pairs={{4,1},{1,4},{6,3},{3,6},{12,9},{9,12},{14,11},{11,14},{20,17},{17,... | collective-permute-start | bytes 1179656 | tf_op jit(solution)/shard_map/ppermute | solution.py:228
  92.3 3.4 %collective-permute-start.18 = (bf16[512,1024]{1,0:T(8,128)(2,1)S(1)}, bf16[512,1024]{1,0:T(8,128)(2,1)S(1)}, u32[]{:S(2)}, u32[]{:S(2)}) collective-permute-start(bf16[512,1024]{1,0:T(8,128)(2,1)S(1)} %pad_maximum_fusion), channel_id=1, source_target_pairs={{4,1},{1,4},{6,3},{3,6},{12,9},{9,12},{14,11},{11,14},{20,17},{17,... | collective-permute-start | bytes 3145736 | tf_op jit(solution)/shard_map/ppermute | solution.py:228
  95.9 2.6 %fusion.51 = bf16[1536,128]{1,0:T(8,128)(2,1)S(1)} fusion(bf16[1536,1536]{1,0:T(8,128)(2,1)S(1)} %bitcast.208, bf16[1,1536,1536]{2,1,0:T(8,128)(2,1)S(1)} %bitcast.210, bf16[1,1536,1536]{2,1,0:T(8,128)(2,1)} %param.13, bf16[1024,1536]{1,0:T(8,128)(2,1)S(1)} %constant_dynamic-update-slice_fusion, bf16[1024,128]{1,0:T(8,128)(2,1)S(1)} %pad_maximum_fusion.4), kind=kOutput, calls=%fused_computation.119 | convolution fusion | flops 406192128 | bytes 4980736 | tf_op jit(solution)/shard_map/dot_general | solution.py:243
  98.5 3.7 %collective-permute-start.22 = (bf16[1536,128]{1,0:T(8,128)(2,1)S(1)}, bf16[1536,128]{1,0:T(8,128)(2,1)S(1)}, u32[]{:S(2)}, u32[]{:S(2)}) collective-permute-start(bf16[1536,128]{1,0:T(8,128)(2,1)S(1)} %fusion.51), channel_id=1, source_target_pairs={{0,8},{24,16},{1,9},{25,17},{2,10},{26,18},{3,11},{27,19},{4,12},{... | collective-permute-start | bytes 1179656 | tf_op jit(solution)/shard_map/ppermute | solution.py:107
  105.9 2.2 fusion.33
  108.2 3.5 %collective-permute-start.23 = (bf16[1536,128]{1,0:T(8,128)(2,1)S(1)}, bf16[1536,128]{1,0:T(8,128)(2,1)S(1)}, u32[]{:S(2)}, u32[]{:S(2)}) collective-permute-start(bf16[1536,128]{1,0:T(8,128)(2,1)S(1)} %fusion.50), channel_id=1, source_target_pairs={{0,8},{24,16},{1,9},{25,17},{2,10},{26,18},{3,11},{27,19},{4,12},{... | collective-permute-start | bytes 1179656 | tf_op jit(solution)/shard_map/ppermute | solution.py:107
  112.5 6.1 %collective-permute-start.25 = (bf16[1536,128]{1,0:T(8,128)(2,1)S(1)}, bf16[1536,128]{1,0:T(8,128)(2,1)S(1)}, u32[]{:S(2)}, u32[]{:S(2)}) collective-permute-start(bf16[1536,128]{1,0:T(8,128)(2,1)S(1)} %slice.458), channel_id=1, source_target_pairs={{0,8},{24,16},{1,9},{25,17},{2,10},{26,18},{3,11},{27,19},{4,12},{... | collective-permute-start | bytes 1179656 | tf_op jit(solution)/shard_map/ppermute | solution.py:107
  118.6 2.2 collective-permute-done.23
  121.7 1.8 collective-permute-done.18
  124.2 2.2 fusion.34
  126.5 3.3 %collective-permute-start.28 = (bf16[1536,128]{1,0:T(8,128)(2,1)S(1)}, bf16[1536,128]{1,0:T(8,128)(2,1)S(1)}, u32[]{:S(2)}, u32[]{:S(2)}) collective-permute-start(bf16[1536,128]{1,0:T(8,128)(2,1)S(1)} %fusion.64), channel_id=1, source_target_pairs={{0,8},{24,16},{8,0},{16,24},{1,9},{25,17},{9,1},{17,25},{2,10},{26... | collective-permute-start | bytes 1179656 | tf_op jit(solution)/shard_map/ppermute | solution.py:107
  130.7 2.2 fusion.35
  133.0 4.4 %collective-permute-start.30 = (bf16[1536,128]{1,0:T(8,128)(2,1)S(1)}, bf16[1536,128]{1,0:T(8,128)(2,1)S(1)}, u32[]{:S(2)}, u32[]{:S(2)}) collective-permute-start(bf16[1536,128]{1,0:T(8,128)(2,1)S(1)} %fusion.65), channel_id=1, source_target_pairs={{0,8},{24,16},{8,0},{16,24},{1,9},{25,17},{9,1},{17,25},{2,10},{26... | collective-permute-start | bytes 1179656 | tf_op jit(solution)/shard_map/ppermute | solution.py:107
  138.8 5.3 %collective-permute-start.29 = (bf16[1536,128]{1,0:T(8,128)(2,1)S(1)}, bf16[1536,128]{1,0:T(8,128)(2,1)S(1)}, u32[]{:S(2)}, u32[]{:S(2)}) collective-permute-start(bf16[1536,128]{1,0:T(8,128)(2,1)S(1)} %fusion.66), channel_id=1, source_target_pairs={{0,8},{24,16},{8,0},{16,24},{1,9},{25,17},{9,1},{17,25},{2,10},{26... | collective-permute-start | bytes 1179656 | tf_op jit(solution)/shard_map/ppermute | solution.py:107
  144.2 3.3 %collective-permute-done.30 = bf16[1536,128]{1,0:T(8,128)(2,1)S(1)} collective-permute-done((bf16[1536,128]{1,0:T(8,128)(2,1)S(1)}, bf16[1536,128]{1,0:T(8,128)(2,1)S(1)}, u32[]{:S(2)}, u32[]{:S(2)}) %collective-permute-start.30) | collective-permute-done | bytes 393248 | tf_op jit(solution)/shard_map/ppermute | solution.py:107
  148.7 4.1 %collective-permute-start.33 = (bf16[1536,128]{1,0:T(8,128)(2,1)S(1)}, bf16[1536,128]{1,0:T(8,128)(2,1)S(1)}, u32[]{:S(2)}, u32[]{:S(2)}) collective-permute-start(bf16[1536,128]{1,0:T(8,128)(2,1)S(1)} %fusion.67), channel_id=1, source_target_pairs={{0,8},{24,16},{8,0},{16,24},{1,9},{25,17},{9,1},{17,25},{2,10},{26... | collective-permute-start | bytes 1179656 | tf_op jit(solution)/shard_map/ppermute | solution.py:107
  152.8 3.1 %collective-permute-done.29 = bf16[1536,128]{1,0:T(8,128)(2,1)S(1)} collective-permute-done((bf16[1536,128]{1,0:T(8,128)(2,1)S(1)}, bf16[1536,128]{1,0:T(8,128)(2,1)S(1)}, u32[]{:S(2)}, u32[]{:S(2)}) %collective-permute-start.29) | collective-permute-done | bytes 393248 | tf_op jit(solution)/shard_map/ppermute | solution.py:107
  156.1 2.2 fusion.37
  159.3 3.6 %collective-permute-start.36 = (bf16[1536,128]{1,0:T(8,128)(2,1)S(1)}, bf16[1536,128]{1,0:T(8,128)(2,1)S(1)}, u32[]{:S(2)}, u32[]{:S(2)}) collective-permute-start(bf16[1536,128]{1,0:T(8,128)(2,1)S(1)} %fusion.68), channel_id=1, source_target_pairs={{0,8},{24,16},{8,0},{16,24},{1,9},{25,17},{9,1},{17,25},{2,10},{26... | collective-permute-start | bytes 1179656 | tf_op jit(solution)/shard_map/ppermute | solution.py:107
  163.0 2.6 %shard_map.95 = (f32[1536,1536]{1,0:T(8,128)}, bf16[1536,1536]{1,0:T(8,128)(2,1)}) custom-call(bf16[1536,128]{1,0:T(8,128)(2,1)S(1)} %broadcast_select_fusion.6.refs_0_, bf16[1536,128]{1,0:T(8,128)(2,1)S(1)} %broadcast_select_fusion.5.refs_1_, bf16[1536,128]{1,0:T(8,128)(2,1)S(1)} %broadcast_select_fusion.4.refs_2_, f32[1536,1536]{1,0:T(8,128)S(1)} %bitcast.192), custom_call_target="tpu_custom_call" | custom-call | flops 2949120 | bytes 7077888 | tf_op jit(solution)/shard_map/pallas_call | solution.py:61
  166.6 6.6 %collective-permute-start.38 = (bf16[1536,128]{1,0:T(8,128)(2,1)S(1)}, bf16[1536,128]{1,0:T(8,128)(2,1)S(1)}, u32[]{:S(2)}, u32[]{:S(2)}) collective-permute-start(bf16[1536,128]{1,0:T(8,128)(2,1)S(1)} %fusion.69), channel_id=1, source_target_pairs={{0,8},{24,16},{8,0},{16,24},{1,9},{25,17},{9,1},{17,25},{2,10},{26... | collective-permute-start | bytes 1179656 | tf_op jit(solution)/shard_map/ppermute | solution.py:107
  173.2 2.2 fusion.36
  176.4 5.2 %collective-permute-start.40 = (bf16[1536,128]{1,0:T(8,128)(2,1)S(1)}, bf16[1536,128]{1,0:T(8,128)(2,1)S(1)}, u32[]{:S(2)}, u32[]{:S(2)}) collective-permute-start(bf16[1536,128]{1,0:T(8,128)(2,1)S(1)} %fusion.70), channel_id=1, source_target_pairs={{0,8},{24,16},{8,0},{16,24},{1,9},{25,17},{9,1},{17,25},{2,10},{26... | collective-permute-start | bytes 1179656 | tf_op jit(solution)/shard_map/ppermute | solution.py:107
  183.0 7.0 %collective-permute-start.39 = (bf16[1536,128]{1,0:T(8,128)(2,1)S(1)}, bf16[1536,128]{1,0:T(8,128)(2,1)S(1)}, u32[]{:S(2)}, u32[]{:S(2)}) collective-permute-start(bf16[1536,128]{1,0:T(8,128)(2,1)S(1)} %fusion.71), channel_id=1, source_target_pairs={{0,8},{24,16},{8,0},{16,24},{1,9},{25,17},{9,1},{17,25},{2,10},{26... | collective-permute-start | bytes 1179656 | tf_op jit(solution)/shard_map/ppermute | solution.py:107
  190.1 2.6 %shard_map.96 = (f32[1536,1536]{1,0:T(8,128)}, bf16[1536,1536]{1,0:T(8,128)(2,1)}) custom-call(bf16[1536,128]{1,0:T(8,128)(2,1)S(1)} %broadcast_select_fusion.9.refs_0_, bf16[1536,128]{1,0:T(8,128)(2,1)S(1)} %broadcast_select_fusion.8.refs_1_, bf16[1536,128]{1,0:T(8,128)(2,1)S(1)} %broadcast_select_fusion.7.refs_2_, ...), custom_call_target="tpu_custom_call", output_to_operand_aliasing={{0}: (4, {}), {1}: (5, {})} | custom-call | flops 2949120 | bytes 7077888 | tf_op jit(solution)/shard_map/pallas_call | solution.py:61
  193.7 4.8 %collective-permute-start.43 = (bf16[1536,128]{1,0:T(8,128)(2,1)S(1)}, bf16[1536,128]{1,0:T(8,128)(2,1)S(1)}, u32[]{:S(2)}, u32[]{:S(2)}) collective-permute-start(bf16[1536,128]{1,0:T(8,128)(2,1)S(1)} %fusion.72), channel_id=1, source_target_pairs={{0,8},{24,16},{8,0},{16,24},{1,9},{25,17},{9,1},{17,25},{2,10},{26... | collective-permute-start | bytes 1179656 | tf_op jit(solution)/shard_map/ppermute | solution.py:107
  201.2 7.1 %collective-permute-done.43 = bf16[1536,128]{1,0:T(8,128)(2,1)S(1)} collective-permute-done((bf16[1536,128]{1,0:T(8,128)(2,1)S(1)}, bf16[1536,128]{1,0:T(8,128)(2,1)S(1)}, u32[]{:S(2)}, u32[]{:S(2)}) %collective-permute-start.43) | collective-permute-done | bytes 393248 | tf_op jit(solution)/shard_map/ppermute | solution.py:107
  210.6 2.6 %shard_map.97 = (f32[1536,1536]{1,0:T(8,128)}, bf16[1536,1536]{1,0:T(8,128)(2,1)}) custom-call(bf16[1536,128]{1,0:T(8,128)(2,1)S(1)} %broadcast_select_fusion.12.refs_0_, bf16[1536,128]{1,0:T(8,128)(2,1)S(1)} %broadcast_select_fusion.11.refs_1_, bf16[1536,128]{1,0:T(8,128)(2,1)S(1)} %broadcast_select_fusion.10.refs_2_, ...), custom_call_target="tpu_custom_call", output_to_operand_aliasing={{0}: (4, {}), {1}: (5, {})} | custom-call | flops 2949120 | bytes 7077888 | tf_op jit(solution)/shard_map/pallas_call | solution.py:61
  214.6 2.2 collective-permute-done.48
  216.9 8.4 %collective-permute-done.47 = bf16[1536,128]{1,0:T(8,128)(2,1)S(1)} collective-permute-done((bf16[1536,128]{1,0:T(8,128)(2,1)S(1)}, bf16[1536,128]{1,0:T(8,128)(2,1)S(1)}, u32[]{:S(2)}, u32[]{:S(2)}) %collective-permute-start.47) | collective-permute-done | bytes 393248 | tf_op jit(solution)/shard_map/ppermute | solution.py:107
  225.3 1.9 shard_map.98
  227.3 2.2 collective-permute-done.46
  (181 shorter events, 44.3 us)
Async XLA Ops:
  0.6 19.7 %collective-permute-start = (bf16[256,1536]{1,0:T(8,128)(2,1)}, bf16[256,1536]{1,0:T(8,128)(2,1)}, u32[]{:S(2)}, u32[]{:S(2)}) collective-permute-start(bf16[256,1536]{1,0:T(8,128)(2,1)} %param.8), channel_id=1, source_target_pairs={{0,4},{2,6},{4,0},{6,2},{1,5},{3,7},{5,1},{7,3},{8,12},{10,14},{12... | collective-permute-start | bytes 2359304 | tf_op jit(solution)/shard_map/ppermute | solution.py:31
  3.8 16.5 %collective-permute-start.1 = (bf16[256,1536]{1,0:T(8,128)(2,1)S(1)}, bf16[256,1536]{1,0:T(8,128)(2,1)S(1)}, u32[]{:S(2)}, u32[]{:S(2)}) collective-permute-start(bf16[256,1536]{1,0:T(8,128)(2,1)S(1)} %get-tuple-element.310), channel_id=1, source_target_pairs={{0,2},{2,0},{4,6},{6,4},{1,3},{3,1},{5,7},{7,5},{8,10},{10,8},{12,... | collective-permute-start | bytes 2359304 | tf_op jit(solution)/shard_map/ppermute | solution.py:31
  4.2 16.1 %collective-permute-start.2 = (bf16[256,1536]{1,0:T(8,128)(2,1)S(1)}, bf16[256,1536]{1,0:T(8,128)(2,1)S(1)}, u32[]{:S(2)}, u32[]{:S(2)}) collective-permute-start(bf16[256,1536]{1,0:T(8,128)(2,1)S(1)} %get-tuple-element.308), channel_id=1, source_target_pairs={{0,2},{2,0},{4,6},{6,4},{1,3},{3,1},{5,7},{7,5},{8,10},{10,8},{12,... | collective-permute-start | bytes 2359304 | tf_op jit(solution)/shard_map/ppermute | solution.py:31
  5.0 21.7 %collective-permute-start.5 = (bf16[256,1536]{1,0:T(8,128)(2,1)S(1)}, bf16[256,1536]{1,0:T(8,128)(2,1)S(1)}, u32[]{:S(2)}, u32[]{:S(2)}) collective-permute-start(bf16[256,1536]{1,0:T(8,128)(2,1)S(1)} %copy-done.1), channel_id=1, source_target_pairs={{0,2},{2,0},{4,6},{6,4},{1,3},{3,1},{5,7},{7,5},{8,10},{10,8},{12,... | collective-permute-start | bytes 2359304 | tf_op jit(solution)/shard_map/ppermute | solution.py:31
  20.3 17.8 %collective-permute-start.9 = (bf16[256,1536]{1,0:T(8,128)(2,1)}, bf16[256,1536]{1,0:T(8,128)(2,1)S(1)}, u32[]{:S(2)}, u32[]{:S(2)}) collective-permute-start(bf16[256,1536]{1,0:T(8,128)(2,1)} %collective-permute-done), channel_id=1, source_target_pairs={{0,2},{2,0},{4,6},{6,4},{1,3},{3,1},{5,7},{7,5},{8,10},{10,8},{12,... | collective-permute-start | bytes 2359304 | tf_op jit(solution)/shard_map/ppermute | solution.py:31
  25.2 11.6 %collective-permute-start.6 = (bf16[128,1536]{1,0:T(8,128)(2,1)S(1)}, bf16[128,1536]{1,0:T(8,128)(2,1)}, u32[]{:S(2)}, u32[]{:S(2)}) collective-permute-start(bf16[128,1536]{1,0:T(8,128)(2,1)S(1)} %get-tuple-element.318), channel_id=1, source_target_pairs={{0,4},{2,6},{4,0},{6,2},{1,5},{3,7},{5,1},{7,3},{8,12},{10,14},{12... | collective-permute-start | bytes 1179656 | tf_op jit(solution)/shard_map/ppermute | solution.py:31
  30.8 36.7 %collective-permute-start.7 = (bf16[512,1536]{1,0:T(8,128)(2,1)}, bf16[512,1536]{1,0:T(8,128)(2,1)}, u32[]{:S(2)}, u32[]{:S(2)}) collective-permute-start(bf16[512,1536]{1,0:T(8,128)(2,1)} %convolution_convert_fusion), channel_id=1, source_target_pairs={{4,5},{1,0},{6,7},{3,2},{12,13},{9,8},{14,15},{11,10},{20,21},{17,... | collective-permute-start | bytes 4718600 | tf_op jit(solution)/shard_map/ppermute | solution.py:168
  34.4 13.2 %collective-permute-start.3 = (bf16[128,1536]{1,0:T(8,128)(2,1)}, bf16[128,1536]{1,0:T(8,128)(2,1)}, u32[]{:S(2)}, u32[]{:S(2)}) collective-permute-start(bf16[128,1536]{1,0:T(8,128)(2,1)} %get-tuple-element.319), channel_id=1, source_target_pairs={{0,4},{2,6},{4,0},{6,2},{1,5},{3,7},{5,1},{7,3},{8,12},{10,14},{12... | collective-permute-start | bytes 1179656 | tf_op jit(solution)/shard_map/ppermute | solution.py:31
  36.8 26.9 %collective-permute-start.8 = (bf16[128,1536]{1,0:T(8,128)(2,1)}, bf16[128,1536]{1,0:T(8,128)(2,1)}, u32[]{:S(2)}, u32[]{:S(2)}) collective-permute-start(bf16[128,1536]{1,0:T(8,128)(2,1)} %collective-permute-done.6), channel_id=1, source_target_pairs={{0,1},{5,4},{2,3},{7,6},{8,9},{13,12},{10,11},{15,14},{16,17},{21,... | collective-permute-start | bytes 1179656 | tf_op jit(solution)/shard_map/ppermute | solution.py:173
  40.4 14.8 %collective-permute-start.10 = (bf16[128,1536]{1,0:T(8,128)(2,1)}, bf16[128,1536]{1,0:T(8,128)(2,1)}, u32[]{:S(2)}, u32[]{:S(2)}) collective-permute-start(bf16[128,1536]{1,0:T(8,128)(2,1)} %get-tuple-element.320), channel_id=1, source_target_pairs={{0,4},{2,6},{4,0},{6,2},{1,5},{3,7},{5,1},{7,3},{8,12},{10,14},{12... | collective-permute-start | bytes 1179656 | tf_op jit(solution)/shard_map/ppermute | solution.py:31
  43.8 18.6 %collective-permute-start.12 = (bf16[128,1536]{1,0:T(8,128)(2,1)}, bf16[128,1536]{1,0:T(8,128)(2,1)S(1)}, u32[]{:S(2)}, u32[]{:S(2)}) collective-permute-start(bf16[128,1536]{1,0:T(8,128)(2,1)} %get-tuple-element.321), channel_id=1, source_target_pairs={{0,4},{2,6},{4,0},{6,2},{1,5},{3,7},{5,1},{7,3},{8,12},{10,14},{12... | collective-permute-start | bytes 1179656 | tf_op jit(solution)/shard_map/ppermute | solution.py:31
  47.6 21.8 %collective-permute-start.4 = (bf16[128,1536]{1,0:T(8,128)(2,1)}, bf16[128,1536]{1,0:T(8,128)(2,1)S(1)}, u32[]{:S(2)}, u32[]{:S(2)}) collective-permute-start(bf16[128,1536]{1,0:T(8,128)(2,1)} %collective-permute-done.3), channel_id=1, source_target_pairs={{0,1},{5,4},{2,3},{7,6},{8,9},{13,12},{10,11},{15,14},{16,17},{21,... | collective-permute-start | bytes 1179656 | tf_op jit(solution)/shard_map/ppermute | solution.py:173
  55.2 16.0 %collective-permute-start.11 = (bf16[128,1536]{1,0:T(8,128)(2,1)}, bf16[128,1536]{1,0:T(8,128)(2,1)S(1)}, u32[]{:S(2)}, u32[]{:S(2)}) collective-permute-start(bf16[128,1536]{1,0:T(8,128)(2,1)} %collective-permute-done.10), channel_id=1, source_target_pairs={{0,1},{5,4},{2,3},{7,6},{8,9},{13,12},{10,11},{15,14},{16,17},{21,... | collective-permute-start | bytes 1179656 | tf_op jit(solution)/shard_map/ppermute | solution.py:173
  62.4 14.3 %collective-permute-start.13 = (bf16[128,1536]{1,0:T(8,128)(2,1)S(1)}, bf16[128,1536]{1,0:T(8,128)(2,1)S(1)}, u32[]{:S(2)}, u32[]{:S(2)}) collective-permute-start(bf16[128,1536]{1,0:T(8,128)(2,1)S(1)} %collective-permute-done.12), channel_id=1, source_target_pairs={{0,1},{5,4},{2,3},{7,6},{8,9},{13,12},{10,11},{15,14},{16,17},{21,... | collective-permute-start | bytes 1179656 | tf_op jit(solution)/shard_map/ppermute | solution.py:173
  79.8 3.7 %collective-permute-start.15 = (f32[2,512]{1,0:T(2,128)S(1)}, f32[2,512]{1,0:T(2,128)S(1)}, u32[]{:S(2)}, u32[]{:S(2)}) collective-permute-start(f32[2,512]{1,0:T(2,128)S(1)} %maximum_add_fusion), channel_id=1, source_target_pairs={{0,1},{1,0},{2,3},{3,2},{4,5},{5,4},{6,7},{7,6},{8,9},{9,8},{10,11... | collective-permute-start | bytes 12296 | tf_op jit(solution)/shard_map/ppermute | solution.py:31
  83.8 5.0 %collective-permute-start.19 = (bf16[512,128]{1,0:T(8,128)(2,1)S(1)}, bf16[512,128]{1,0:T(8,128)(2,1)S(1)}, u32[]{:S(2)}, u32[]{:S(2)}) collective-permute-start(bf16[512,128]{1,0:T(8,128)(2,1)S(1)} %pad_maximum_fusion.5), channel_id=1, source_target_pairs={{0,1},{5,4},{4,0},{1,5},{2,3},{7,6},{6,2},{3,7},{8,9},{13,12},{12,... | collective-permute-start | bytes 393224 | tf_op jit(solution)/shard_map/ppermute | solution.py:227
  83.9 8.4 %collective-permute-start.16 = (bf16[512,128]{1,0:T(8,128)(2,1)S(1)}, bf16[512,128]{1,0:T(8,128)(2,1)S(1)}, u32[]{:S(2)}, u32[]{:S(2)}) collective-permute-start(bf16[512,128]{1,0:T(8,128)(2,1)S(1)} %pad_maximum_fusion.5), channel_id=1, source_target_pairs={{4,1},{1,4},{6,3},{3,6},{12,9},{9,12},{14,11},{11,14},{20,17},{17,... | collective-permute-start | bytes 393224 | tf_op jit(solution)/shard_map/ppermute | solution.py:228
  88.9 14.8 %collective-permute-start.21 = (bf16[512,384]{1,0:T(8,128)(2,1)S(1)}, bf16[512,384]{1,0:T(8,128)(2,1)S(1)}, u32[]{:S(2)}, u32[]{:S(2)}) collective-permute-start(bf16[512,384]{1,0:T(8,128)(2,1)S(1)} %pad_maximum_fusion.2), channel_id=1, source_target_pairs={{4,1},{1,4},{6,3},{3,6},{12,9},{9,12},{14,11},{11,14},{20,17},{17,... | collective-permute-start | bytes 1179656 | tf_op jit(solution)/shard_map/ppermute | solution.py:228
  92.2 12.1 %collective-permute-start.20 = (bf16[512,384]{1,0:T(8,128)(2,1)S(1)}, bf16[512,384]{1,0:T(8,128)(2,1)S(1)}, u32[]{:S(2)}, u32[]{:S(2)}) collective-permute-start(bf16[512,384]{1,0:T(8,128)(2,1)S(1)} %pad_maximum_fusion.2), channel_id=1, source_target_pairs={{0,1},{5,4},{4,0},{1,5},{2,3},{7,6},{6,2},{3,7},{8,9},{13,12},{12,... | collective-permute-start | bytes 1179656 | tf_op jit(solution)/shard_map/ppermute | solution.py:227
  92.3 31.2 %collective-permute-start.18 = (bf16[512,1024]{1,0:T(8,128)(2,1)S(1)}, bf16[512,1024]{1,0:T(8,128)(2,1)S(1)}, u32[]{:S(2)}, u32[]{:S(2)}) collective-permute-start(bf16[512,1024]{1,0:T(8,128)(2,1)S(1)} %pad_maximum_fusion), channel_id=1, source_target_pairs={{4,1},{1,4},{6,3},{3,6},{12,9},{9,12},{14,11},{11,14},{20,17},{17,... | collective-permute-start | bytes 3145736 | tf_op jit(solution)/shard_map/ppermute | solution.py:228
  95.7 28.2 %collective-permute-start.17 = (bf16[512,1024]{1,0:T(8,128)(2,1)S(1)}, bf16[512,1024]{1,0:T(8,128)(2,1)S(1)}, u32[]{:S(2)}, u32[]{:S(2)}) collective-permute-start(bf16[512,1024]{1,0:T(8,128)(2,1)S(1)} %pad_maximum_fusion), channel_id=1, source_target_pairs={{0,1},{5,4},{4,0},{1,5},{2,3},{7,6},{6,2},{3,7},{8,9},{13,12},{12,... | collective-permute-start | bytes 3145736 | tf_op jit(solution)/shard_map/ppermute | solution.py:227
  98.5 13.1 %collective-permute-start.22 = (bf16[1536,128]{1,0:T(8,128)(2,1)S(1)}, bf16[1536,128]{1,0:T(8,128)(2,1)S(1)}, u32[]{:S(2)}, u32[]{:S(2)}) collective-permute-start(bf16[1536,128]{1,0:T(8,128)(2,1)S(1)} %fusion.51), channel_id=1, source_target_pairs={{0,8},{24,16},{1,9},{25,17},{2,10},{26,18},{3,11},{27,19},{4,12},{... | collective-permute-start | bytes 1179656 | tf_op jit(solution)/shard_map/ppermute | solution.py:107
  108.2 12.7 %collective-permute-start.23 = (bf16[1536,128]{1,0:T(8,128)(2,1)S(1)}, bf16[1536,128]{1,0:T(8,128)(2,1)S(1)}, u32[]{:S(2)}, u32[]{:S(2)}) collective-permute-start(bf16[1536,128]{1,0:T(8,128)(2,1)S(1)} %fusion.50), channel_id=1, source_target_pairs={{0,8},{24,16},{1,9},{25,17},{2,10},{26,18},{3,11},{27,19},{4,12},{... | collective-permute-start | bytes 1179656 | tf_op jit(solution)/shard_map/ppermute | solution.py:107
  111.8 9.9 %collective-permute-start.26 = (bf16[1536,128]{1,0:T(8,128)(2,1)S(1)}, bf16[1536,128]{1,0:T(8,128)(2,1)S(1)}, u32[]{:S(2)}, u32[]{:S(2)}) collective-permute-start(bf16[1536,128]{1,0:T(8,128)(2,1)S(1)} %add_convert_fusion.23), channel_id=1, source_target_pairs={{8,16},{16,8},{9,17},{17,9},{10,18},{18,10},{11,19},{19,11},{12,20... | collective-permute-start | bytes 1179656 | tf_op jit(solution)/shard_map/ppermute | solution.py:115
  112.5 17.4 %collective-permute-start.25 = (bf16[1536,128]{1,0:T(8,128)(2,1)S(1)}, bf16[1536,128]{1,0:T(8,128)(2,1)S(1)}, u32[]{:S(2)}, u32[]{:S(2)}) collective-permute-start(bf16[1536,128]{1,0:T(8,128)(2,1)S(1)} %slice.458), channel_id=1, source_target_pairs={{0,8},{24,16},{1,9},{25,17},{2,10},{26,18},{3,11},{27,19},{4,12},{... | collective-permute-start | bytes 1179656 | tf_op jit(solution)/shard_map/ppermute | solution.py:107
  121.0 9.7 %collective-permute-start.24 = (bf16[1536,128]{1,0:T(8,128)(2,1)S(1)}, bf16[1536,128]{1,0:T(8,128)(2,1)S(1)}, u32[]{:S(2)}, u32[]{:S(2)}) collective-permute-start(bf16[1536,128]{1,0:T(8,128)(2,1)S(1)} %add_convert_fusion.22), channel_id=1, source_target_pairs={{8,16},{16,8},{9,17},{17,9},{10,18},{18,10},{11,19},{19,11},{12,20... | collective-permute-start | bytes 1179656 | tf_op jit(solution)/shard_map/ppermute | solution.py:115
  126.5 11.3 %collective-permute-start.28 = (bf16[1536,128]{1,0:T(8,128)(2,1)S(1)}, bf16[1536,128]{1,0:T(8,128)(2,1)S(1)}, u32[]{:S(2)}, u32[]{:S(2)}) collective-permute-start(bf16[1536,128]{1,0:T(8,128)(2,1)S(1)} %fusion.64), channel_id=1, source_target_pairs={{0,8},{24,16},{8,0},{16,24},{1,9},{25,17},{9,1},{17,25},{2,10},{26... | collective-permute-start | bytes 1179656 | tf_op jit(solution)/shard_map/ppermute | solution.py:107
  129.9 8.7 %collective-permute-start.27 = (bf16[1536,128]{1,0:T(8,128)(2,1)S(1)}, bf16[1536,128]{1,0:T(8,128)(2,1)S(1)}, u32[]{:S(2)}, u32[]{:S(2)}) collective-permute-start(bf16[1536,128]{1,0:T(8,128)(2,1)S(1)} %add_convert_fusion.20), channel_id=1, source_target_pairs={{8,16},{16,8},{9,17},{17,9},{10,18},{18,10},{11,19},{19,11},{12,20... | collective-permute-start | bytes 1179656 | tf_op jit(solution)/shard_map/ppermute | solution.py:115
  133.0 14.5 %collective-permute-start.30 = (bf16[1536,128]{1,0:T(8,128)(2,1)S(1)}, bf16[1536,128]{1,0:T(8,128)(2,1)S(1)}, u32[]{:S(2)}, u32[]{:S(2)}) collective-permute-start(bf16[1536,128]{1,0:T(8,128)(2,1)S(1)} %fusion.65), channel_id=1, source_target_pairs={{0,8},{24,16},{8,0},{16,24},{1,9},{25,17},{9,1},{17,25},{2,10},{26... | collective-permute-start | bytes 1179656 | tf_op jit(solution)/shard_map/ppermute | solution.py:107
  138.0 10.6 %collective-permute-start.31 = (bf16[1536,128]{1,0:T(8,128)(2,1)S(1)}, bf16[1536,128]{1,0:T(8,128)(2,1)S(1)}, u32[]{:S(2)}, u32[]{:S(2)}) collective-permute-start(bf16[1536,128]{1,0:T(8,128)(2,1)S(1)} %add_convert_fusion.18), channel_id=1, source_target_pairs={{8,16},{16,8},{9,17},{17,9},{10,18},{18,10},{11,19},{19,11},{12,20... | collective-permute-start | bytes 1179656 | tf_op jit(solution)/shard_map/ppermute | solution.py:115
  138.8 17.1 %collective-permute-start.29 = (bf16[1536,128]{1,0:T(8,128)(2,1)S(1)}, bf16[1536,128]{1,0:T(8,128)(2,1)S(1)}, u32[]{:S(2)}, u32[]{:S(2)}) collective-permute-start(bf16[1536,128]{1,0:T(8,128)(2,1)S(1)} %fusion.66), channel_id=1, source_target_pairs={{0,8},{24,16},{8,0},{16,24},{1,9},{25,17},{9,1},{17,25},{2,10},{26... | collective-permute-start | bytes 1179656 | tf_op jit(solution)/shard_map/ppermute | solution.py:107
  147.6 11.5 %collective-permute-start.34 = (bf16[1536,128]{1,0:T(8,128)(2,1)S(1)}, bf16[1536,128]{1,0:T(8,128)(2,1)S(1)}, u32[]{:S(2)}, u32[]{:S(2)}) collective-permute-start(bf16[1536,128]{1,0:T(8,128)(2,1)S(1)} %add_convert_fusion.16), channel_id=1, source_target_pairs={{8,16},{16,8},{9,17},{17,9},{10,18},{18,10},{11,19},{19,11},{12,20... | collective-permute-start | bytes 1179656 | tf_op jit(solution)/shard_map/ppermute | solution.py:115
  148.7 16.9 %collective-permute-start.33 = (bf16[1536,128]{1,0:T(8,128)(2,1)S(1)}, bf16[1536,128]{1,0:T(8,128)(2,1)S(1)}, u32[]{:S(2)}, u32[]{:S(2)}) collective-permute-start(bf16[1536,128]{1,0:T(8,128)(2,1)S(1)} %fusion.67), channel_id=1, source_target_pairs={{0,8},{24,16},{8,0},{16,24},{1,9},{25,17},{9,1},{17,25},{2,10},{26... | collective-permute-start | bytes 1179656 | tf_op jit(solution)/shard_map/ppermute | solution.py:107
  158.3 8.1 %collective-permute-start.32 = (bf16[1536,128]{1,0:T(8,128)(2,1)S(1)}, bf16[1536,128]{1,0:T(8,128)(2,1)S(1)}, u32[]{:S(2)}, u32[]{:S(2)}) collective-permute-start(bf16[1536,128]{1,0:T(8,128)(2,1)S(1)} %add_convert_fusion.14), channel_id=1, source_target_pairs={{8,16},{16,8},{9,17},{17,9},{10,18},{18,10},{11,19},{19,11},{12,20... | collective-permute-start | bytes 1179656 | tf_op jit(solution)/shard_map/ppermute | solution.py:115
  159.3 16.1 %collective-permute-start.36 = (bf16[1536,128]{1,0:T(8,128)(2,1)S(1)}, bf16[1536,128]{1,0:T(8,128)(2,1)S(1)}, u32[]{:S(2)}, u32[]{:S(2)}) collective-permute-start(bf16[1536,128]{1,0:T(8,128)(2,1)S(1)} %fusion.68), channel_id=1, source_target_pairs={{0,8},{24,16},{8,0},{16,24},{1,9},{25,17},{9,1},{17,25},{2,10},{26... | collective-permute-start | bytes 1179656 | tf_op jit(solution)/shard_map/ppermute | solution.py:107
  165.7 10.5 %collective-permute-start.35 = (bf16[1536,128]{1,0:T(8,128)(2,1)S(1)}, bf16[1536,128]{1,0:T(8,128)(2,1)S(1)}, u32[]{:S(2)}, u32[]{:S(2)}) collective-permute-start(bf16[1536,128]{1,0:T(8,128)(2,1)S(1)} %add_convert_fusion.12), channel_id=1, source_target_pairs={{8,16},{16,8},{9,17},{17,9},{10,18},{18,10},{11,19},{19,11},{12,20... | collective-permute-start | bytes 1179656 | tf_op jit(solution)/shard_map/ppermute | solution.py:115
  166.6 15.4 %collective-permute-start.38 = (bf16[1536,128]{1,0:T(8,128)(2,1)S(1)}, bf16[1536,128]{1,0:T(8,128)(2,1)S(1)}, u32[]{:S(2)}, u32[]{:S(2)}) collective-permute-start(bf16[1536,128]{1,0:T(8,128)(2,1)S(1)} %fusion.69), channel_id=1, source_target_pairs={{0,8},{24,16},{8,0},{16,24},{1,9},{25,17},{9,1},{17,25},{2,10},{26... | collective-permute-start | bytes 1179656 | tf_op jit(solution)/shard_map/ppermute | solution.py:107
  175.5 7.3 %collective-permute-start.37 = (bf16[1536,128]{1,0:T(8,128)(2,1)S(1)}, bf16[1536,128]{1,0:T(8,128)(2,1)S(1)}, u32[]{:S(2)}, u32[]{:S(2)}) collective-permute-start(bf16[1536,128]{1,0:T(8,128)(2,1)S(1)} %add_convert_fusion.10), channel_id=1, source_target_pairs={{8,16},{16,8},{9,17},{17,9},{10,18},{18,10},{11,19},{19,11},{12,20... | collective-permute-start | bytes 1179656 | tf_op jit(solution)/shard_map/ppermute | solution.py:115
  176.4 16.3 %collective-permute-start.40 = (bf16[1536,128]{1,0:T(8,128)(2,1)S(1)}, bf16[1536,128]{1,0:T(8,128)(2,1)S(1)}, u32[]{:S(2)}, u32[]{:S(2)}) collective-permute-start(bf16[1536,128]{1,0:T(8,128)(2,1)S(1)} %fusion.70), channel_id=1, source_target_pairs={{0,8},{24,16},{8,0},{16,24},{1,9},{25,17},{9,1},{17,25},{2,10},{26... | collective-permute-start | bytes 1179656 | tf_op jit(solution)/shard_map/ppermute | solution.py:107
  182.1 11.4 %collective-permute-start.41 = (bf16[1536,128]{1,0:T(8,128)(2,1)S(1)}, bf16[1536,128]{1,0:T(8,128)(2,1)S(1)}, u32[]{:S(2)}, u32[]{:S(2)}) collective-permute-start(bf16[1536,128]{1,0:T(8,128)(2,1)S(1)} %add_convert_fusion.8), channel_id=1, source_target_pairs={{8,16},{16,8},{9,17},{17,9},{10,18},{18,10},{11,19},{19,11},{12,20... | collective-permute-start | bytes 1179656 | tf_op jit(solution)/shard_map/ppermute | solution.py:115
  183.0 16.0 %collective-permute-start.39 = (bf16[1536,128]{1,0:T(8,128)(2,1)S(1)}, bf16[1536,128]{1,0:T(8,128)(2,1)S(1)}, u32[]{:S(2)}, u32[]{:S(2)}) collective-permute-start(bf16[1536,128]{1,0:T(8,128)(2,1)S(1)} %fusion.71), channel_id=1, source_target_pairs={{0,8},{24,16},{8,0},{16,24},{1,9},{25,17},{9,1},{17,25},{2,10},{26... | collective-permute-start | bytes 1179656 | tf_op jit(solution)/shard_map/ppermute | solution.py:107
  192.8 7.0 %collective-permute-start.44 = (bf16[1536,128]{1,0:T(8,128)(2,1)S(1)}, bf16[1536,128]{1,0:T(8,128)(2,1)S(1)}, u32[]{:S(2)}, u32[]{:S(2)}) collective-permute-start(bf16[1536,128]{1,0:T(8,128)(2,1)S(1)} %add_convert_fusion.6), channel_id=1, source_target_pairs={{8,16},{16,8},{9,17},{17,9},{10,18},{18,10},{11,19},{19,11},{12,20... | collective-permute-start | bytes 1179656 | tf_op jit(solution)/shard_map/ppermute | solution.py:115
  193.7 14.6 %collective-permute-start.43 = (bf16[1536,128]{1,0:T(8,128)(2,1)S(1)}, bf16[1536,128]{1,0:T(8,128)(2,1)S(1)}, u32[]{:S(2)}, u32[]{:S(2)}) collective-permute-start(bf16[1536,128]{1,0:T(8,128)(2,1)S(1)} %fusion.72), channel_id=1, source_target_pairs={{0,8},{24,16},{8,0},{16,24},{1,9},{25,17},{9,1},{17,25},{2,10},{26... | collective-permute-start | bytes 1179656 | tf_op jit(solution)/shard_map/ppermute | solution.py:107
  199.1 10.0 %collective-permute-start.42 = (bf16[1536,128]{1,0:T(8,128)(2,1)S(1)}, bf16[1536,128]{1,0:T(8,128)(2,1)S(1)}, u32[]{:S(2)}, u32[]{:S(2)}) collective-permute-start(bf16[1536,128]{1,0:T(8,128)(2,1)S(1)} %add_convert_fusion.4), channel_id=1, source_target_pairs={{8,16},{16,8},{9,17},{17,9},{10,18},{18,10},{11,19},{19,11},{12,20... | collective-permute-start | bytes 1179656 | tf_op jit(solution)/shard_map/ppermute | solution.py:115
  199.9 16.9 %collective-permute-start.48 = (bf16[1536,128]{1,0:T(8,128)(2,1)S(1)}, bf16[1536,128]{1,0:T(8,128)(2,1)S(1)}, u32[]{:S(2)}, u32[]{:S(2)}) collective-permute-start(bf16[1536,128]{1,0:T(8,128)(2,1)S(1)} %add_convert_fusion.3), channel_id=1, source_target_pairs={{8,0},{16,24},{9,1},{17,25},{10,2},{18,26},{11,3},{19,27},{12,4},{... | collective-permute-start | bytes 1179656 | tf_op jit(solution)/shard_map/ppermute | solution.py:107
  208.4 4.8 %collective-permute-start.45 = (bf16[1536,128]{1,0:T(8,128)(2,1)S(1)}, bf16[1536,128]{1,0:T(8,128)(2,1)S(1)}, u32[]{:S(2)}, u32[]{:S(2)}) collective-permute-start(bf16[1536,128]{1,0:T(8,128)(2,1)S(1)} %add_convert_fusion.2), channel_id=1, source_target_pairs={{8,16},{16,8},{9,17},{17,9},{10,18},{18,10},{11,19},{19,11},{12,20... | collective-permute-start | bytes 1179656 | tf_op jit(solution)/shard_map/ppermute | solution.py:115
  209.3 16.0 %collective-permute-start.47 = (bf16[1536,128]{1,0:T(8,128)(2,1)S(1)}, bf16[1536,128]{1,0:T(8,128)(2,1)S(1)}, u32[]{:S(2)}, u32[]{:S(2)}) collective-permute-start(bf16[1536,128]{1,0:T(8,128)(2,1)S(1)} %add_convert_fusion), channel_id=1, source_target_pairs={{8,0},{16,24},{9,1},{17,25},{10,2},{18,26},{11,3},{19,27},{12,4},{... | collective-permute-start | bytes 1179656 | tf_op jit(solution)/shard_map/ppermute | solution.py:107
  213.3 16.2 %collective-permute-start.46 = (bf16[1536,128]{1,0:T(8,128)(2,1)S(1)}, bf16[1536,128]{1,0:T(8,128)(2,1)S(1)}, u32[]{:S(2)}, u32[]{:S(2)}) collective-permute-start(bf16[1536,128]{1,0:T(8,128)(2,1)S(1)} %add_convert_fusion.1), channel_id=1, source_target_pairs={{8,0},{16,24},{9,1},{17,25},{10,2},{18,26},{11,3},{19,27},{12,4},{... | collective-permute-start | bytes 1179656 | tf_op jit(solution)/shard_map/ppermute | solution.py:107
  (18 other events, 134.2 us)

commit v18 on v17

--- a/solution.py
+++ b/solution.py
@@ -271,6 +271,9 @@
                 lo, hi = todo.pop(0)
                 add_pseudo(last[:, (lo - early) * narrow :], lo, hi, s - 1)
             line.step(s)
+            first = 3 * (s - units + 2)
+            if first >= 0 and s + 2 in line.paid and first in line.totals:
+                line.totals[first], line.paid[s + 2] = together(line.totals[first], line.paid[s + 2])
         sums = [line.totals[k] for k in range(units)]
     else:
         for lo, hi in todo:

time: 232 us -> 233 us (level)
  transfers between devices with their start and end apart: 49 -> 49, of which waited for: 22 -> 23; matrix products, arithmetic and copies ran while one was open for 19% -> 19% of each run, Pallas kernels for 4% -> 4%
where the time goes in v18:
time: 233 us; the launch traced here: 231 us
  starting transfers between devices  98.3 us (42%)
  waiting for transfers between devices  73.4 us (32%)
  matrix products  24.4 us (10%)
  other arithmetic  13.2 us (6%)
  Pallas kernels  11.1 us (5%)
  local copies, waits for them, and re-layouts  8.57 us (4%)
    ppermute x15, starting transfers between devices, send_outer(): self.edge[s] = lax.ppermute(payload, 'island', pairs)  63.5 us
    ppermute x11, waiting for transfers between devices, swap(): return lax.ppermute(value, axis, [(i, i ^ bit) for i in range(count)])  33.4 us
    ppermute x15, waiting for transfers between devices, send_outer(): self.edge[s] = lax.ppermute(payload, 'island', pairs)  27.5 us
    dot_general x7, matrix products, add_pseudo(): lax.dot_general(context_all, piece, (((0,), (0,)), ((), ())), preferred_e...  15 us
    pallas_call x5, Pallas kernels, finish(): pl.pallas_call(functools.partial(finish_kernel, count, start, narrow, isl...  11.1 us
    ppermute x3, starting transfers between devices, move(): crosses.append(lax.ppermute(d_local, ('fsdp', 'tp'), cross_pairs))  10.1 us
    dot_general x3, matrix products, project(): jnp.dot(block, weight, preferred_element_type=f32).astype(bf16)  9.49 us
    ppermute x12, starting transfers between devices, step(): self.mid[s] = lax.ppermute(self.sums[s], 'island', [(1, 2), (2, 1)])  8.58 us
  transfers between devices with their start and end apart: 49, of which 23 were waited for; matrix products, arithmetic and copies ran while one was open for 19% of the time, Pallas kernels for 4%

profile of v18, /device:TPU:2, one launch (start us, length us, event | category | flops | bytes accessed | tf_op | source)
XLA Modules:
  0.0 230.9 jit_solution(14655454954735595726)
XLA Ops:
  5.0 15.3 %collective-permute-done = bf16[256,1536]{1,0:T(8,128)(2,1)} collective-permute-done((bf16[256,1536]{1,0:T(8,128)(2,1)}, bf16[256,1536]{1,0:T(8,128)(2,1)}, u32[]{:S(2)}, u32[]{:S(2)}) %collective-permute-start) | collective-permute-done | bytes 786464 | tf_op jit(solution)/shard_map/ppermute | solution.py:31
  20.4 4.0 %convolution_convert_fusion.2 = bf16[256,1536]{1,0:T(8,128)(2,1)S(1)} fusion(bf16[256,1536]{1,0:T(8,128)(2,1)} %collective-permute-done, bf16[1536,1536]{1,0:T(8,128)(2,1)} %param.12), kind=kOutput, calls=%fused_computation.8 | convolution fusion | flops 1208352768 | bytes 6291456 | tf_op jit(solution)/shard_map/dot_general | solution.py:144
  26.7 4.1 %convolution_convert_fusion = bf16[512,1536]{1,0:T(8,128)(2,1)} fusion(bf16[1536,1536]{1,0:T(8,128)(2,1)S(1)} %bitcast.206, bf16[256,1536]{1,0:T(8,128)(2,1)S(1)} %collective-permute-done.5, bf16[256,1536]{1,0:T(8,128)(2,1)S(1)} %copy-done.1), kind=kOutput, calls=%fused_computation | convolution fusion | flops 2419851264 | bytes 7864320 | tf_op jit(solution)/shard_map/dot_general | solution.py:144
  30.8 3.6 %collective-permute-start.7 = (bf16[512,1536]{1,0:T(8,128)(2,1)}, bf16[512,1536]{1,0:T(8,128)(2,1)}, u32[]{:S(2)}, u32[]{:S(2)}) collective-permute-start(bf16[512,1536]{1,0:T(8,128)(2,1)} %convolution_convert_fusion), channel_id=1, source_target_pairs={{4,5},{1,0},{6,7},{3,2},{12,13},{9,8},{14,15},{11,10},{20,21},{17,... | collective-permute-start | bytes 4718600 | tf_op jit(solution)/shard_map/ppermute | solution.py:168
  34.4 2.3 %collective-permute-done.6 = bf16[128,1536]{1,0:T(8,128)(2,1)} collective-permute-done((bf16[128,1536]{1,0:T(8,128)(2,1)S(1)}, bf16[128,1536]{1,0:T(8,128)(2,1)}, u32[]{:S(2)}, u32[]{:S(2)}) %collective-permute-start.6) | collective-permute-done | bytes 393248 | tf_op jit(solution)/shard_map/ppermute | solution.py:31
  40.4 3.4 %collective-permute-start.10 = (bf16[128,1536]{1,0:T(8,128)(2,1)}, bf16[128,1536]{1,0:T(8,128)(2,1)}, u32[]{:S(2)}, u32[]{:S(2)}) collective-permute-start(bf16[128,1536]{1,0:T(8,128)(2,1)} %get-tuple-element.332), channel_id=1, source_target_pairs={{0,4},{2,6},{4,0},{6,2},{1,5},{3,7},{5,1},{7,3},{8,12},{10,14},{12... | collective-permute-start | bytes 1179656 | tf_op jit(solution)/shard_map/ppermute | solution.py:31
  45.5 2.1 constant_dynamic-update-slice_fusion.2
  48.9 6.3 %collective-permute-done.10 = bf16[128,1536]{1,0:T(8,128)(2,1)} collective-permute-done((bf16[128,1536]{1,0:T(8,128)(2,1)}, bf16[128,1536]{1,0:T(8,128)(2,1)}, u32[]{:S(2)}, u32[]{:S(2)}) %collective-permute-start.10) | collective-permute-done | bytes 393248 | tf_op jit(solution)/shard_map/ppermute | solution.py:31
  56.5 6.0 %collective-permute-done.12 = bf16[128,1536]{1,0:T(8,128)(2,1)S(1)} collective-permute-done((bf16[128,1536]{1,0:T(8,128)(2,1)}, bf16[128,1536]{1,0:T(8,128)(2,1)S(1)}, u32[]{:S(2)}, u32[]{:S(2)}) %collective-permute-start.12) | collective-permute-done | bytes 393248 | tf_op jit(solution)/shard_map/ppermute | solution.py:31
  63.7 3.9 %collective-permute-done.7 = bf16[512,1536]{1,0:T(8,128)(2,1)} collective-permute-done((bf16[512,1536]{1,0:T(8,128)(2,1)}, bf16[512,1536]{1,0:T(8,128)(2,1)}, u32[]{:S(2)}, u32[]{:S(2)}) %collective-permute-start.7) | collective-permute-done | bytes 1572896 | tf_op jit(solution)/shard_map/ppermute | solution.py:168
  67.6 1.8 multiply_reduce_fusion.7
  69.4 1.8 multiply_reduce_fusion.5
  71.2 1.7 multiply_reduce_fusion.3
  73.0 3.7 %collective-permute-done.13 = bf16[128,1536]{1,0:T(8,128)(2,1)S(1)} collective-permute-done((bf16[128,1536]{1,0:T(8,128)(2,1)S(1)}, bf16[128,1536]{1,0:T(8,128)(2,1)S(1)}, u32[]{:S(2)}, u32[]{:S(2)}) %collective-permute-start.13) | collective-permute-done | bytes 393248 | tf_op jit(solution)/shard_map/ppermute | solution.py:173
  76.7 1.6 multiply_reduce_fusion.1
  80.0 3.5 %collective-permute-done.15 = f32[2,512]{1,0:T(2,128)S(1)} collective-permute-done((f32[2,512]{1,0:T(2,128)S(1)}, f32[2,512]{1,0:T(2,128)S(1)}, u32[]{:S(2)}, u32[]{:S(2)}) %collective-permute-start.15) | collective-permute-done | bytes 4128 | tf_op jit(solution)/shard_map/ppermute | solution.py:31
  83.9 3.4 %collective-permute-start.16 = (bf16[512,128]{1,0:T(8,128)(2,1)S(1)}, bf16[512,128]{1,0:T(8,128)(2,1)S(1)}, u32[]{:S(2)}, u32[]{:S(2)}) collective-permute-start(bf16[512,128]{1,0:T(8,128)(2,1)S(1)} %pad_maximum_fusion.5), channel_id=1, source_target_pairs={{4,1},{1,4},{6,3},{3,6},{12,9},{9,12},{14,11},{11,14},{20,17},{17,... | collective-permute-start | bytes 393224 | tf_op jit(solution)/shard_map/ppermute | solution.py:228
  88.9 3.3 %collective-permute-start.21 = (bf16[512,384]{1,0:T(8,128)(2,1)S(1)}, bf16[512,384]{1,0:T(8,128)(2,1)S(1)}, u32[]{:S(2)}, u32[]{:S(2)}) collective-permute-start(bf16[512,384]{1,0:T(8,128)(2,1)S(1)} %pad_maximum_fusion.2), channel_id=1, source_target_pairs={{4,1},{1,4},{6,3},{3,6},{12,9},{9,12},{14,11},{11,14},{20,17},{17,... | collective-permute-start | bytes 1179656 | tf_op jit(solution)/shard_map/ppermute | solution.py:228
  92.3 3.4 %collective-permute-start.18 = (bf16[512,1024]{1,0:T(8,128)(2,1)S(1)}, bf16[512,1024]{1,0:T(8,128)(2,1)S(1)}, u32[]{:S(2)}, u32[]{:S(2)}) collective-permute-start(bf16[512,1024]{1,0:T(8,128)(2,1)S(1)} %pad_maximum_fusion), channel_id=1, source_target_pairs={{4,1},{1,4},{6,3},{3,6},{12,9},{9,12},{14,11},{11,14},{20,17},{17,... | collective-permute-start | bytes 3145736 | tf_op jit(solution)/shard_map/ppermute | solution.py:228
  95.9 2.6 %fusion.51 = bf16[1536,128]{1,0:T(8,128)(2,1)S(1)} fusion(bf16[1536,1536]{1,0:T(8,128)(2,1)S(1)} %bitcast.208, bf16[1,1536,1536]{2,1,0:T(8,128)(2,1)S(1)} %bitcast.210, bf16[1,1536,1536]{2,1,0:T(8,128)(2,1)} %param.13, bf16[1024,1536]{1,0:T(8,128)(2,1)S(1)} %constant_dynamic-update-slice_fusion, bf16[1024,128]{1,0:T(8,128)(2,1)S(1)} %pad_maximum_fusion.4), kind=kOutput, calls=%fused_computation.119 | convolution fusion | flops 406192128 | bytes 4980736 | tf_op jit(solution)/shard_map/dot_general | solution.py:243
  98.5 3.7 %collective-permute-start.22 = (bf16[1536,128]{1,0:T(8,128)(2,1)S(1)}, bf16[1536,128]{1,0:T(8,128)(2,1)S(1)}, u32[]{:S(2)}, u32[]{:S(2)}) collective-permute-start(bf16[1536,128]{1,0:T(8,128)(2,1)S(1)} %fusion.51), channel_id=1, source_target_pairs={{0,8},{24,16},{1,9},{25,17},{2,10},{26,18},{3,11},{27,19},{4,12},{... | collective-permute-start | bytes 1179656 | tf_op jit(solution)/shard_map/ppermute | solution.py:107
  105.9 2.2 fusion.33
  108.2 3.5 %collective-permute-start.23 = (bf16[1536,128]{1,0:T(8,128)(2,1)S(1)}, bf16[1536,128]{1,0:T(8,128)(2,1)S(1)}, u32[]{:S(2)}, u32[]{:S(2)}) collective-permute-start(bf16[1536,128]{1,0:T(8,128)(2,1)S(1)} %fusion.50), channel_id=1, source_target_pairs={{0,8},{24,16},{1,9},{25,17},{2,10},{26,18},{3,11},{27,19},{4,12},{... | collective-permute-start | bytes 1179656 | tf_op jit(solution)/shard_map/ppermute | solution.py:107
  112.5 6.1 %collective-permute-start.25 = (bf16[1536,128]{1,0:T(8,128)(2,1)S(1)}, bf16[1536,128]{1,0:T(8,128)(2,1)S(1)}, u32[]{:S(2)}, u32[]{:S(2)}) collective-permute-start(bf16[1536,128]{1,0:T(8,128)(2,1)S(1)} %slice.458), channel_id=1, source_target_pairs={{0,8},{24,16},{1,9},{25,17},{2,10},{26,18},{3,11},{27,19},{4,12},{... | collective-permute-start | bytes 1179656 | tf_op jit(solution)/shard_map/ppermute | solution.py:107
  118.6 2.2 collective-permute-done.23
  121.7 1.8 collective-permute-done.18
  124.2 2.2 fusion.34
  126.5 3.3 %collective-permute-start.28 = (bf16[1536,128]{1,0:T(8,128)(2,1)S(1)}, bf16[1536,128]{1,0:T(8,128)(2,1)S(1)}, u32[]{:S(2)}, u32[]{:S(2)}) collective-permute-start(bf16[1536,128]{1,0:T(8,128)(2,1)S(1)} %fusion.64), channel_id=1, source_target_pairs={{0,8},{24,16},{8,0},{16,24},{1,9},{25,17},{9,1},{17,25},{2,10},{26... | collective-permute-start | bytes 1179656 | tf_op jit(solution)/shard_map/ppermute | solution.py:107
  130.7 2.2 fusion.35
  133.0 4.4 %collective-permute-start.30 = (bf16[1536,128]{1,0:T(8,128)(2,1)S(1)}, bf16[1536,128]{1,0:T(8,128)(2,1)S(1)}, u32[]{:S(2)}, u32[]{:S(2)}) collective-permute-start(bf16[1536,128]{1,0:T(8,128)(2,1)S(1)} %fusion.65), channel_id=1, source_target_pairs={{0,8},{24,16},{8,0},{16,24},{1,9},{25,17},{9,1},{17,25},{2,10},{26... | collective-permute-start | bytes 1179656 | tf_op jit(solution)/shard_map/ppermute | solution.py:107
  138.8 5.3 %collective-permute-start.29 = (bf16[1536,128]{1,0:T(8,128)(2,1)S(1)}, bf16[1536,128]{1,0:T(8,128)(2,1)S(1)}, u32[]{:S(2)}, u32[]{:S(2)}) collective-permute-start(bf16[1536,128]{1,0:T(8,128)(2,1)S(1)} %fusion.66), channel_id=1, source_target_pairs={{0,8},{24,16},{8,0},{16,24},{1,9},{25,17},{9,1},{17,25},{2,10},{26... | collective-permute-start | bytes 1179656 | tf_op jit(solution)/shard_map/ppermute | solution.py:107
  144.2 3.3 %collective-permute-done.30 = bf16[1536,128]{1,0:T(8,128)(2,1)S(1)} collective-permute-done((bf16[1536,128]{1,0:T(8,128)(2,1)S(1)}, bf16[1536,128]{1,0:T(8,128)(2,1)S(1)}, u32[]{:S(2)}, u32[]{:S(2)}) %collective-permute-start.30) | collective-permute-done | bytes 393248 | tf_op jit(solution)/shard_map/ppermute | solution.py:107
  148.7 4.1 %collective-permute-start.33 = (bf16[1536,128]{1,0:T(8,128)(2,1)S(1)}, bf16[1536,128]{1,0:T(8,128)(2,1)S(1)}, u32[]{:S(2)}, u32[]{:S(2)}) collective-permute-start(bf16[1536,128]{1,0:T(8,128)(2,1)S(1)} %fusion.67), channel_id=1, source_target_pairs={{0,8},{24,16},{8,0},{16,24},{1,9},{25,17},{9,1},{17,25},{2,10},{26... | collective-permute-start | bytes 1179656 | tf_op jit(solution)/shard_map/ppermute | solution.py:107
  152.8 3.1 %collective-permute-done.29 = bf16[1536,128]{1,0:T(8,128)(2,1)S(1)} collective-permute-done((bf16[1536,128]{1,0:T(8,128)(2,1)S(1)}, bf16[1536,128]{1,0:T(8,128)(2,1)S(1)}, u32[]{:S(2)}, u32[]{:S(2)}) %collective-permute-start.29) | collective-permute-done | bytes 393248 | tf_op jit(solution)/shard_map/ppermute | solution.py:107
  156.0 2.2 fusion.37
  159.2 3.6 %collective-permute-start.36 = (bf16[1536,128]{1,0:T(8,128)(2,1)S(1)}, bf16[1536,128]{1,0:T(8,128)(2,1)S(1)}, u32[]{:S(2)}, u32[]{:S(2)}) collective-permute-start(bf16[1536,128]{1,0:T(8,128)(2,1)S(1)} %fusion.68), channel_id=1, source_target_pairs={{0,8},{24,16},{8,0},{16,24},{1,9},{25,17},{9,1},{17,25},{2,10},{26... | collective-permute-start | bytes 1179656 | tf_op jit(solution)/shard_map/ppermute | solution.py:107
  165.0 7.8 %collective-permute-start.38 = (bf16[1536,128]{1,0:T(8,128)(2,1)S(1)}, bf16[1536,128]{1,0:T(8,128)(2,1)S(1)}, u32[]{:S(2)}, u32[]{:S(2)}) collective-permute-start(bf16[1536,128]{1,0:T(8,128)(2,1)S(1)} %fusion.69), channel_id=1, source_target_pairs={{0,8},{24,16},{8,0},{16,24},{1,9},{25,17},{9,1},{17,25},{2,10},{26... | collective-permute-start | bytes 1179656 | tf_op jit(solution)/shard_map/ppermute | solution.py:107
  172.8 2.2 fusion.36
  176.2 4.8 %collective-permute-start.40 = (bf16[1536,128]{1,0:T(8,128)(2,1)S(1)}, bf16[1536,128]{1,0:T(8,128)(2,1)S(1)}, u32[]{:S(2)}, u32[]{:S(2)}) collective-permute-start(bf16[1536,128]{1,0:T(8,128)(2,1)S(1)} %fusion.70), channel_id=1, source_target_pairs={{0,8},{24,16},{8,0},{16,24},{1,9},{25,17},{9,1},{17,25},{2,10},{26... | collective-permute-start | bytes 1179656 | tf_op jit(solution)/shard_map/ppermute | solution.py:107
  183.0 6.5 %collective-permute-start.39 = (bf16[1536,128]{1,0:T(8,128)(2,1)S(1)}, bf16[1536,128]{1,0:T(8,128)(2,1)S(1)}, u32[]{:S(2)}, u32[]{:S(2)}) collective-permute-start(bf16[1536,128]{1,0:T(8,128)(2,1)S(1)} %fusion.71), channel_id=1, source_target_pairs={{0,8},{24,16},{8,0},{16,24},{1,9},{25,17},{9,1},{17,25},{2,10},{26... | collective-permute-start | bytes 1179656 | tf_op jit(solution)/shard_map/ppermute | solution.py:107
  191.8 6.5 %collective-permute-start.43 = (bf16[1536,128]{1,0:T(8,128)(2,1)S(1)}, bf16[1536,128]{1,0:T(8,128)(2,1)S(1)}, u32[]{:S(2)}, u32[]{:S(2)}) collective-permute-start(bf16[1536,128]{1,0:T(8,128)(2,1)S(1)} %fusion.72), channel_id=1, source_target_pairs={{0,8},{24,16},{8,0},{16,24},{1,9},{25,17},{9,1},{17,25},{2,10},{26... | collective-permute-start | bytes 1179656 | tf_op jit(solution)/shard_map/ppermute | solution.py:107
  201.4 6.7 %collective-permute-done.43 = bf16[1536,128]{1,0:T(8,128)(2,1)S(1)} collective-permute-done((bf16[1536,128]{1,0:T(8,128)(2,1)S(1)}, bf16[1536,128]{1,0:T(8,128)(2,1)S(1)}, u32[]{:S(2)}, u32[]{:S(2)}) %collective-permute-start.43) | collective-permute-done | bytes 393248 | tf_op jit(solution)/shard_map/ppermute | solution.py:107
  208.9 2.6 %shard_map.95 = (f32[1536,1536]{1,0:T(8,128)}, bf16[1536,1536]{1,0:T(8,128)(2,1)}) custom-call(bf16[1536,128]{1,0:T(8,128)(2,1)S(1)} %broadcast_select_fusion.15.refs_0_, bf16[1536,128]{1,0:T(8,128)(2,1)S(1)} %broadcast_select_fusion.5.refs_1_, bf16[1536,128]{1,0:T(8,128)(2,1)S(1)} %broadcast_select_fusion.4.refs_2_, f32[1536,1536]{1,0:T(8,128)S(1)} %bitcast.192), custom_call_target="tpu_custom_call" | custom-call | flops 2949120 | bytes 7077888 | tf_op jit(solution)/shard_map/pallas_call | solution.py:61
  213.0 2.6 %shard_map.96 = (f32[1536,1536]{1,0:T(8,128)}, bf16[1536,1536]{1,0:T(8,128)(2,1)}) custom-call(bf16[1536,128]{1,0:T(8,128)(2,1)S(1)} %broadcast_select_fusion.13.refs_0_, bf16[1536,128]{1,0:T(8,128)(2,1)S(1)} %broadcast_select_fusion.7.refs_1_, bf16[1536,128]{1,0:T(8,128)(2,1)S(1)} %broadcast_select_fusion.6.refs_2_, ...), custom_call_target="tpu_custom_call", output_to_operand_aliasing={{0}: (4, {}), {1}: (5, {})} | custom-call | flops 2949120 | bytes 7077888 | tf_op jit(solution)/shard_map/pallas_call | solution.py:61
  217.1 2.6 %shard_map.97 = (f32[1536,1536]{1,0:T(8,128)}, bf16[1536,1536]{1,0:T(8,128)(2,1)}) custom-call(bf16[1536,128]{1,0:T(8,128)(2,1)S(1)} %broadcast_select_fusion.14.refs_0_, bf16[1536,128]{1,0:T(8,128)(2,1)S(1)} %broadcast_select_fusion.9.refs_1_, bf16[1536,128]{1,0:T(8,128)(2,1)S(1)} %broadcast_select_fusion.8.refs_2_, ...), custom_call_target="tpu_custom_call", output_to_operand_aliasing={{0}: (4, {}), {1}: (5, {})} | custom-call | flops 2949120 | bytes 7077888 | tf_op jit(solution)/shard_map/pallas_call | solution.py:61
  219.8 5.3 %collective-permute-done.47 = bf16[1536,128]{1,0:T(8,128)(2,1)S(1)} collective-permute-done((bf16[1536,128]{1,0:T(8,128)(2,1)S(1)}, bf16[1536,128]{1,0:T(8,128)(2,1)S(1)}, u32[]{:S(2)}, u32[]{:S(2)}) %collective-permute-start.47) | collective-permute-done | bytes 393248 | tf_op jit(solution)/shard_map/ppermute | solution.py:107
  225.2 1.9 shard_map.98
  227.1 2.2 collective-permute-done.46
  (181 shorter events, 46.2 us)
Async XLA Ops:
  0.6 19.7 %collective-permute-start = (bf16[256,1536]{1,0:T(8,128)(2,1)}, bf16[256,1536]{1,0:T(8,128)(2,1)}, u32[]{:S(2)}, u32[]{:S(2)}) collective-permute-start(bf16[256,1536]{1,0:T(8,128)(2,1)} %param.8), channel_id=1, source_target_pairs={{0,4},{2,6},{4,0},{6,2},{1,5},{3,7},{5,1},{7,3},{8,12},{10,14},{12... | collective-permute-start | bytes 2359304 | tf_op jit(solution)/shard_map/ppermute | solution.py:31
  3.8 16.5 %collective-permute-start.1 = (bf16[256,1536]{1,0:T(8,128)(2,1)S(1)}, bf16[256,1536]{1,0:T(8,128)(2,1)S(1)}, u32[]{:S(2)}, u32[]{:S(2)}) collective-permute-start(bf16[256,1536]{1,0:T(8,128)(2,1)S(1)} %get-tuple-element.322), channel_id=1, source_target_pairs={{0,2},{2,0},{4,6},{6,4},{1,3},{3,1},{5,7},{7,5},{8,10},{10,8},{12,... | collective-permute-start | bytes 2359304 | tf_op jit(solution)/shard_map/ppermute | solution.py:31
  4.2 16.1 %collective-permute-start.2 = (bf16[256,1536]{1,0:T(8,128)(2,1)S(1)}, bf16[256,1536]{1,0:T(8,128)(2,1)S(1)}, u32[]{:S(2)}, u32[]{:S(2)}) collective-permute-start(bf16[256,1536]{1,0:T(8,128)(2,1)S(1)} %get-tuple-element.320), channel_id=1, source_target_pairs={{0,2},{2,0},{4,6},{6,4},{1,3},{3,1},{5,7},{7,5},{8,10},{10,8},{12,... | collective-permute-start | bytes 2359304 | tf_op jit(solution)/shard_map/ppermute | solution.py:31
  5.0 21.7 %collective-permute-start.5 = (bf16[256,1536]{1,0:T(8,128)(2,1)S(1)}, bf16[256,1536]{1,0:T(8,128)(2,1)S(1)}, u32[]{:S(2)}, u32[]{:S(2)}) collective-permute-start(bf16[256,1536]{1,0:T(8,128)(2,1)S(1)} %copy-done.1), channel_id=1, source_target_pairs={{0,2},{2,0},{4,6},{6,4},{1,3},{3,1},{5,7},{7,5},{8,10},{10,8},{12,... | collective-permute-start | bytes 2359304 | tf_op jit(solution)/shard_map/ppermute | solution.py:31
  20.3 17.8 %collective-permute-start.9 = (bf16[256,1536]{1,0:T(8,128)(2,1)}, bf16[256,1536]{1,0:T(8,128)(2,1)S(1)}, u32[]{:S(2)}, u32[]{:S(2)}) collective-permute-start(bf16[256,1536]{1,0:T(8,128)(2,1)} %collective-permute-done), channel_id=1, source_target_pairs={{0,2},{2,0},{4,6},{6,4},{1,3},{3,1},{5,7},{7,5},{8,10},{10,8},{12,... | collective-permute-start | bytes 2359304 | tf_op jit(solution)/shard_map/ppermute | solution.py:31
  25.2 11.6 %collective-permute-start.6 = (bf16[128,1536]{1,0:T(8,128)(2,1)S(1)}, bf16[128,1536]{1,0:T(8,128)(2,1)}, u32[]{:S(2)}, u32[]{:S(2)}) collective-permute-start(bf16[128,1536]{1,0:T(8,128)(2,1)S(1)} %get-tuple-element.330), channel_id=1, source_target_pairs={{0,4},{2,6},{4,0},{6,2},{1,5},{3,7},{5,1},{7,3},{8,12},{10,14},{12... | collective-permute-start | bytes 1179656 | tf_op jit(solution)/shard_map/ppermute | solution.py:31
  30.8 36.7 %collective-permute-start.7 = (bf16[512,1536]{1,0:T(8,128)(2,1)}, bf16[512,1536]{1,0:T(8,128)(2,1)}, u32[]{:S(2)}, u32[]{:S(2)}) collective-permute-start(bf16[512,1536]{1,0:T(8,128)(2,1)} %convolution_convert_fusion), channel_id=1, source_target_pairs={{4,5},{1,0},{6,7},{3,2},{12,13},{9,8},{14,15},{11,10},{20,21},{17,... | collective-permute-start | bytes 4718600 | tf_op jit(solution)/shard_map/ppermute | solution.py:168
  34.4 13.2 %collective-permute-start.3 = (bf16[128,1536]{1,0:T(8,128)(2,1)}, bf16[128,1536]{1,0:T(8,128)(2,1)}, u32[]{:S(2)}, u32[]{:S(2)}) collective-permute-start(bf16[128,1536]{1,0:T(8,128)(2,1)} %get-tuple-element.331), channel_id=1, source_target_pairs={{0,4},{2,6},{4,0},{6,2},{1,5},{3,7},{5,1},{7,3},{8,12},{10,14},{12... | collective-permute-start | bytes 1179656 | tf_op jit(solution)/shard_map/ppermute | solution.py:31
  36.8 26.9 %collective-permute-start.8 = (bf16[128,1536]{1,0:T(8,128)(2,1)}, bf16[128,1536]{1,0:T(8,128)(2,1)}, u32[]{:S(2)}, u32[]{:S(2)}) collective-permute-start(bf16[128,1536]{1,0:T(8,128)(2,1)} %collective-permute-done.6), channel_id=1, source_target_pairs={{0,1},{5,4},{2,3},{7,6},{8,9},{13,12},{10,11},{15,14},{16,17},{21,... | collective-permute-start | bytes 1179656 | tf_op jit(solution)/shard_map/ppermute | solution.py:173
  40.4 14.8 %collective-permute-start.10 = (bf16[128,1536]{1,0:T(8,128)(2,1)}, bf16[128,1536]{1,0:T(8,128)(2,1)}, u32[]{:S(2)}, u32[]{:S(2)}) collective-permute-start(bf16[128,1536]{1,0:T(8,128)(2,1)} %get-tuple-element.332), channel_id=1, source_target_pairs={{0,4},{2,6},{4,0},{6,2},{1,5},{3,7},{5,1},{7,3},{8,12},{10,14},{12... | collective-permute-start | bytes 1179656 | tf_op jit(solution)/shard_map/ppermute | solution.py:31
  43.8 18.6 %collective-permute-start.12 = (bf16[128,1536]{1,0:T(8,128)(2,1)}, bf16[128,1536]{1,0:T(8,128)(2,1)S(1)}, u32[]{:S(2)}, u32[]{:S(2)}) collective-permute-start(bf16[128,1536]{1,0:T(8,128)(2,1)} %get-tuple-element.333), channel_id=1, source_target_pairs={{0,4},{2,6},{4,0},{6,2},{1,5},{3,7},{5,1},{7,3},{8,12},{10,14},{12... | collective-permute-start | bytes 1179656 | tf_op jit(solution)/shard_map/ppermute | solution.py:31
  47.6 21.8 %collective-permute-start.4 = (bf16[128,1536]{1,0:T(8,128)(2,1)}, bf16[128,1536]{1,0:T(8,128)(2,1)S(1)}, u32[]{:S(2)}, u32[]{:S(2)}) collective-permute-start(bf16[128,1536]{1,0:T(8,128)(2,1)} %collective-permute-done.3), channel_id=1, source_target_pairs={{0,1},{5,4},{2,3},{7,6},{8,9},{13,12},{10,11},{15,14},{16,17},{21,... | collective-permute-start | bytes 1179656 | tf_op jit(solution)/shard_map/ppermute | solution.py:173
  55.2 16.0 %collective-permute-start.11 = (bf16[128,1536]{1,0:T(8,128)(2,1)}, bf16[128,1536]{1,0:T(8,128)(2,1)S(1)}, u32[]{:S(2)}, u32[]{:S(2)}) collective-permute-start(bf16[128,1536]{1,0:T(8,128)(2,1)} %collective-permute-done.10), channel_id=1, source_target_pairs={{0,1},{5,4},{2,3},{7,6},{8,9},{13,12},{10,11},{15,14},{16,17},{21,... | collective-permute-start | bytes 1179656 | tf_op jit(solution)/shard_map/ppermute | solution.py:173
  62.4 14.3 %collective-permute-start.13 = (bf16[128,1536]{1,0:T(8,128)(2,1)S(1)}, bf16[128,1536]{1,0:T(8,128)(2,1)S(1)}, u32[]{:S(2)}, u32[]{:S(2)}) collective-permute-start(bf16[128,1536]{1,0:T(8,128)(2,1)S(1)} %collective-permute-done.12), channel_id=1, source_target_pairs={{0,1},{5,4},{2,3},{7,6},{8,9},{13,12},{10,11},{15,14},{16,17},{21,... | collective-permute-start | bytes 1179656 | tf_op jit(solution)/shard_map/ppermute | solution.py:173
  79.8 3.7 %collective-permute-start.15 = (f32[2,512]{1,0:T(2,128)S(1)}, f32[2,512]{1,0:T(2,128)S(1)}, u32[]{:S(2)}, u32[]{:S(2)}) collective-permute-start(f32[2,512]{1,0:T(2,128)S(1)} %maximum_add_fusion), channel_id=1, source_target_pairs={{0,1},{1,0},{2,3},{3,2},{4,5},{5,4},{6,7},{7,6},{8,9},{9,8},{10,11... | collective-permute-start | bytes 12296 | tf_op jit(solution)/shard_map/ppermute | solution.py:31
  83.8 5.0 %collective-permute-start.19 = (bf16[512,128]{1,0:T(8,128)(2,1)S(1)}, bf16[512,128]{1,0:T(8,128)(2,1)S(1)}, u32[]{:S(2)}, u32[]{:S(2)}) collective-permute-start(bf16[512,128]{1,0:T(8,128)(2,1)S(1)} %pad_maximum_fusion.5), channel_id=1, source_target_pairs={{0,1},{5,4},{4,0},{1,5},{2,3},{7,6},{6,2},{3,7},{8,9},{13,12},{12,... | collective-permute-start | bytes 393224 | tf_op jit(solution)/shard_map/ppermute | solution.py:227
  83.9 8.4 %collective-permute-start.16 = (bf16[512,128]{1,0:T(8,128)(2,1)S(1)}, bf16[512,128]{1,0:T(8,128)(2,1)S(1)}, u32[]{:S(2)}, u32[]{:S(2)}) collective-permute-start(bf16[512,128]{1,0:T(8,128)(2,1)S(1)} %pad_maximum_fusion.5), channel_id=1, source_target_pairs={{4,1},{1,4},{6,3},{3,6},{12,9},{9,12},{14,11},{11,14},{20,17},{17,... | collective-permute-start | bytes 393224 | tf_op jit(solution)/shard_map/ppermute | solution.py:228
  88.9 14.8 %collective-permute-start.21 = (bf16[512,384]{1,0:T(8,128)(2,1)S(1)}, bf16[512,384]{1,0:T(8,128)(2,1)S(1)}, u32[]{:S(2)}, u32[]{:S(2)}) collective-permute-start(bf16[512,384]{1,0:T(8,128)(2,1)S(1)} %pad_maximum_fusion.2), channel_id=1, source_target_pairs={{4,1},{1,4},{6,3},{3,6},{12,9},{9,12},{14,11},{11,14},{20,17},{17,... | collective-permute-start | bytes 1179656 | tf_op jit(solution)/shard_map/ppermute | solution.py:228
  92.2 12.1 %collective-permute-start.20 = (bf16[512,384]{1,0:T(8,128)(2,1)S(1)}, bf16[512,384]{1,0:T(8,128)(2,1)S(1)}, u32[]{:S(2)}, u32[]{:S(2)}) collective-permute-start(bf16[512,384]{1,0:T(8,128)(2,1)S(1)} %pad_maximum_fusion.2), channel_id=1, source_target_pairs={{0,1},{5,4},{4,0},{1,5},{2,3},{7,6},{6,2},{3,7},{8,9},{13,12},{12,... | collective-permute-start | bytes 1179656 | tf_op jit(solution)/shard_map/ppermute | solution.py:227
  92.3 31.2 %collective-permute-start.18 = (bf16[512,1024]{1,0:T(8,128)(2,1)S(1)}, bf16[512,1024]{1,0:T(8,128)(2,1)S(1)}, u32[]{:S(2)}, u32[]{:S(2)}) collective-permute-start(bf16[512,1024]{1,0:T(8,128)(2,1)S(1)} %pad_maximum_fusion), channel_id=1, source_target_pairs={{4,1},{1,4},{6,3},{3,6},{12,9},{9,12},{14,11},{11,14},{20,17},{17,... | collective-permute-start | bytes 3145736 | tf_op jit(solution)/shard_map/ppermute | solution.py:228
  95.7 28.2 %collective-permute-start.17 = (bf16[512,1024]{1,0:T(8,128)(2,1)S(1)}, bf16[512,1024]{1,0:T(8,128)(2,1)S(1)}, u32[]{:S(2)}, u32[]{:S(2)}) collective-permute-start(bf16[512,1024]{1,0:T(8,128)(2,1)S(1)} %pad_maximum_fusion), channel_id=1, source_target_pairs={{0,1},{5,4},{4,0},{1,5},{2,3},{7,6},{6,2},{3,7},{8,9},{13,12},{12,... | collective-permute-start | bytes 3145736 | tf_op jit(solution)/shard_map/ppermute | solution.py:227
  98.5 13.1 %collective-permute-start.22 = (bf16[1536,128]{1,0:T(8,128)(2,1)S(1)}, bf16[1536,128]{1,0:T(8,128)(2,1)S(1)}, u32[]{:S(2)}, u32[]{:S(2)}) collective-permute-start(bf16[1536,128]{1,0:T(8,128)(2,1)S(1)} %fusion.51), channel_id=1, source_target_pairs={{0,8},{24,16},{1,9},{25,17},{2,10},{26,18},{3,11},{27,19},{4,12},{... | collective-permute-start | bytes 1179656 | tf_op jit(solution)/shard_map/ppermute | solution.py:107
  108.2 12.7 %collective-permute-start.23 = (bf16[1536,128]{1,0:T(8,128)(2,1)S(1)}, bf16[1536,128]{1,0:T(8,128)(2,1)S(1)}, u32[]{:S(2)}, u32[]{:S(2)}) collective-permute-start(bf16[1536,128]{1,0:T(8,128)(2,1)S(1)} %fusion.50), channel_id=1, source_target_pairs={{0,8},{24,16},{1,9},{25,17},{2,10},{26,18},{3,11},{27,19},{4,12},{... | collective-permute-start | bytes 1179656 | tf_op jit(solution)/shard_map/ppermute | solution.py:107
  111.8 9.9 %collective-permute-start.26 = (bf16[1536,128]{1,0:T(8,128)(2,1)S(1)}, bf16[1536,128]{1,0:T(8,128)(2,1)S(1)}, u32[]{:S(2)}, u32[]{:S(2)}) collective-permute-start(bf16[1536,128]{1,0:T(8,128)(2,1)S(1)} %add_convert_fusion.23), channel_id=1, source_target_pairs={{8,16},{16,8},{9,17},{17,9},{10,18},{18,10},{11,19},{19,11},{12,20... | collective-permute-start | bytes 1179656 | tf_op jit(solution)/shard_map/ppermute | solution.py:115
  112.5 17.4 %collective-permute-start.25 = (bf16[1536,128]{1,0:T(8,128)(2,1)S(1)}, bf16[1536,128]{1,0:T(8,128)(2,1)S(1)}, u32[]{:S(2)}, u32[]{:S(2)}) collective-permute-start(bf16[1536,128]{1,0:T(8,128)(2,1)S(1)} %slice.458), channel_id=1, source_target_pairs={{0,8},{24,16},{1,9},{25,17},{2,10},{26,18},{3,11},{27,19},{4,12},{... | collective-permute-start | bytes 1179656 | tf_op jit(solution)/shard_map/ppermute | solution.py:107
  121.0 9.7 %collective-permute-start.24 = (bf16[1536,128]{1,0:T(8,128)(2,1)S(1)}, bf16[1536,128]{1,0:T(8,128)(2,1)S(1)}, u32[]{:S(2)}, u32[]{:S(2)}) collective-permute-start(bf16[1536,128]{1,0:T(8,128)(2,1)S(1)} %add_convert_fusion.22), channel_id=1, source_target_pairs={{8,16},{16,8},{9,17},{17,9},{10,18},{18,10},{11,19},{19,11},{12,20... | collective-permute-start | bytes 1179656 | tf_op jit(solution)/shard_map/ppermute | solution.py:115
  126.5 11.3 %collective-permute-start.28 = (bf16[1536,128]{1,0:T(8,128)(2,1)S(1)}, bf16[1536,128]{1,0:T(8,128)(2,1)S(1)}, u32[]{:S(2)}, u32[]{:S(2)}) collective-permute-start(bf16[1536,128]{1,0:T(8,128)(2,1)S(1)} %fusion.64), channel_id=1, source_target_pairs={{0,8},{24,16},{8,0},{16,24},{1,9},{25,17},{9,1},{17,25},{2,10},{26... | collective-permute-start | bytes 1179656 | tf_op jit(solution)/shard_map/ppermute | solution.py:107
  129.9 8.7 %collective-permute-start.27 = (bf16[1536,128]{1,0:T(8,128)(2,1)S(1)}, bf16[1536,128]{1,0:T(8,128)(2,1)S(1)}, u32[]{:S(2)}, u32[]{:S(2)}) collective-permute-start(bf16[1536,128]{1,0:T(8,128)(2,1)S(1)} %add_convert_fusion.20), channel_id=1, source_target_pairs={{8,16},{16,8},{9,17},{17,9},{10,18},{18,10},{11,19},{19,11},{12,20... | collective-permute-start | bytes 1179656 | tf_op jit(solution)/shard_map/ppermute | solution.py:115
  133.0 14.5 %collective-permute-start.30 = (bf16[1536,128]{1,0:T(8,128)(2,1)S(1)}, bf16[1536,128]{1,0:T(8,128)(2,1)S(1)}, u32[]{:S(2)}, u32[]{:S(2)}) collective-permute-start(bf16[1536,128]{1,0:T(8,128)(2,1)S(1)} %fusion.65), channel_id=1, source_target_pairs={{0,8},{24,16},{8,0},{16,24},{1,9},{25,17},{9,1},{17,25},{2,10},{26... | collective-permute-start | bytes 1179656 | tf_op jit(solution)/shard_map/ppermute | solution.py:107
  137.9 10.6 %collective-permute-start.31 = (bf16[1536,128]{1,0:T(8,128)(2,1)S(1)}, bf16[1536,128]{1,0:T(8,128)(2,1)S(1)}, u32[]{:S(2)}, u32[]{:S(2)}) collective-permute-start(bf16[1536,128]{1,0:T(8,128)(2,1)S(1)} %add_convert_fusion.18), channel_id=1, source_target_pairs={{8,16},{16,8},{9,17},{17,9},{10,18},{18,10},{11,19},{19,11},{12,20... | collective-permute-start | bytes 1179656 | tf_op jit(solution)/shard_map/ppermute | solution.py:115
  138.8 17.1 %collective-permute-start.29 = (bf16[1536,128]{1,0:T(8,128)(2,1)S(1)}, bf16[1536,128]{1,0:T(8,128)(2,1)S(1)}, u32[]{:S(2)}, u32[]{:S(2)}) collective-permute-start(bf16[1536,128]{1,0:T(8,128)(2,1)S(1)} %fusion.66), channel_id=1, source_target_pairs={{0,8},{24,16},{8,0},{16,24},{1,9},{25,17},{9,1},{17,25},{2,10},{26... | collective-permute-start | bytes 1179656 | tf_op jit(solution)/shard_map/ppermute | solution.py:107
  147.6 11.4 %collective-permute-start.34 = (bf16[1536,128]{1,0:T(8,128)(2,1)S(1)}, bf16[1536,128]{1,0:T(8,128)(2,1)S(1)}, u32[]{:S(2)}, u32[]{:S(2)}) collective-permute-start(bf16[1536,128]{1,0:T(8,128)(2,1)S(1)} %add_convert_fusion.16), channel_id=1, source_target_pairs={{8,16},{16,8},{9,17},{17,9},{10,18},{18,10},{11,19},{19,11},{12,20... | collective-permute-start | bytes 1179656 | tf_op jit(solution)/shard_map/ppermute | solution.py:115
  148.7 15.3 %collective-permute-start.33 = (bf16[1536,128]{1,0:T(8,128)(2,1)S(1)}, bf16[1536,128]{1,0:T(8,128)(2,1)S(1)}, u32[]{:S(2)}, u32[]{:S(2)}) collective-permute-start(bf16[1536,128]{1,0:T(8,128)(2,1)S(1)} %fusion.67), channel_id=1, source_target_pairs={{0,8},{24,16},{8,0},{16,24},{1,9},{25,17},{9,1},{17,25},{2,10},{26... | collective-permute-start | bytes 1179656 | tf_op jit(solution)/shard_map/ppermute | solution.py:107
  158.2 6.6 %collective-permute-start.32 = (bf16[1536,128]{1,0:T(8,128)(2,1)S(1)}, bf16[1536,128]{1,0:T(8,128)(2,1)S(1)}, u32[]{:S(2)}, u32[]{:S(2)}) collective-permute-start(bf16[1536,128]{1,0:T(8,128)(2,1)S(1)} %add_convert_fusion.14), channel_id=1, source_target_pairs={{8,16},{16,8},{9,17},{17,9},{10,18},{18,10},{11,19},{19,11},{12,20... | collective-permute-start | bytes 1179656 | tf_op jit(solution)/shard_map/ppermute | solution.py:115
  159.2 15.9 %collective-permute-start.36 = (bf16[1536,128]{1,0:T(8,128)(2,1)S(1)}, bf16[1536,128]{1,0:T(8,128)(2,1)S(1)}, u32[]{:S(2)}, u32[]{:S(2)}) collective-permute-start(bf16[1536,128]{1,0:T(8,128)(2,1)S(1)} %fusion.68), channel_id=1, source_target_pairs={{0,8},{24,16},{8,0},{16,24},{1,9},{25,17},{9,1},{17,25},{2,10},{26... | collective-permute-start | bytes 1179656 | tf_op jit(solution)/shard_map/ppermute | solution.py:107
  164.1 11.9 %collective-permute-start.35 = (bf16[1536,128]{1,0:T(8,128)(2,1)S(1)}, bf16[1536,128]{1,0:T(8,128)(2,1)S(1)}, u32[]{:S(2)}, u32[]{:S(2)}) collective-permute-start(bf16[1536,128]{1,0:T(8,128)(2,1)S(1)} %add_convert_fusion.12), channel_id=1, source_target_pairs={{8,16},{16,8},{9,17},{17,9},{10,18},{18,10},{11,19},{19,11},{12,20... | collective-permute-start | bytes 1179656 | tf_op jit(solution)/shard_map/ppermute | solution.py:115
  165.0 16.9 %collective-permute-start.38 = (bf16[1536,128]{1,0:T(8,128)(2,1)S(1)}, bf16[1536,128]{1,0:T(8,128)(2,1)S(1)}, u32[]{:S(2)}, u32[]{:S(2)}) collective-permute-start(bf16[1536,128]{1,0:T(8,128)(2,1)S(1)} %fusion.69), channel_id=1, source_target_pairs={{0,8},{24,16},{8,0},{16,24},{1,9},{25,17},{9,1},{17,25},{2,10},{26... | collective-permute-start | bytes 1179656 | tf_op jit(solution)/shard_map/ppermute | solution.py:107
  175.2 7.6 %collective-permute-start.37 = (bf16[1536,128]{1,0:T(8,128)(2,1)S(1)}, bf16[1536,128]{1,0:T(8,128)(2,1)S(1)}, u32[]{:S(2)}, u32[]{:S(2)}) collective-permute-start(bf16[1536,128]{1,0:T(8,128)(2,1)S(1)} %add_convert_fusion.10), channel_id=1, source_target_pairs={{8,16},{16,8},{9,17},{17,9},{10,18},{18,10},{11,19},{19,11},{12,20... | collective-permute-start | bytes 1179656 | tf_op jit(solution)/shard_map/ppermute | solution.py:115
  176.2 14.6 %collective-permute-start.40 = (bf16[1536,128]{1,0:T(8,128)(2,1)S(1)}, bf16[1536,128]{1,0:T(8,128)(2,1)S(1)}, u32[]{:S(2)}, u32[]{:S(2)}) collective-permute-start(bf16[1536,128]{1,0:T(8,128)(2,1)S(1)} %fusion.70), channel_id=1, source_target_pairs={{0,8},{24,16},{8,0},{16,24},{1,9},{25,17},{9,1},{17,25},{2,10},{26... | collective-permute-start | bytes 1179656 | tf_op jit(solution)/shard_map/ppermute | solution.py:107
  182.1 9.5 %collective-permute-start.41 = (bf16[1536,128]{1,0:T(8,128)(2,1)S(1)}, bf16[1536,128]{1,0:T(8,128)(2,1)S(1)}, u32[]{:S(2)}, u32[]{:S(2)}) collective-permute-start(bf16[1536,128]{1,0:T(8,128)(2,1)S(1)} %add_convert_fusion.8), channel_id=1, source_target_pairs={{8,16},{16,8},{9,17},{17,9},{10,18},{18,10},{11,19},{19,11},{12,20... | collective-permute-start | bytes 1179656 | tf_op jit(solution)/shard_map/ppermute | solution.py:115
  183.0 16.2 %collective-permute-start.39 = (bf16[1536,128]{1,0:T(8,128)(2,1)S(1)}, bf16[1536,128]{1,0:T(8,128)(2,1)S(1)}, u32[]{:S(2)}, u32[]{:S(2)}) collective-permute-start(bf16[1536,128]{1,0:T(8,128)(2,1)S(1)} %fusion.71), channel_id=1, source_target_pairs={{0,8},{24,16},{8,0},{16,24},{1,9},{25,17},{9,1},{17,25},{2,10},{26... | collective-permute-start | bytes 1179656 | tf_op jit(solution)/shard_map/ppermute | solution.py:107
  190.9 9.1 %collective-permute-start.44 = (bf16[1536,128]{1,0:T(8,128)(2,1)S(1)}, bf16[1536,128]{1,0:T(8,128)(2,1)S(1)}, u32[]{:S(2)}, u32[]{:S(2)}) collective-permute-start(bf16[1536,128]{1,0:T(8,128)(2,1)S(1)} %add_convert_fusion.6), channel_id=1, source_target_pairs={{8,16},{16,8},{9,17},{17,9},{10,18},{18,10},{11,19},{19,11},{12,20... | collective-permute-start | bytes 1179656 | tf_op jit(solution)/shard_map/ppermute | solution.py:115
  191.8 16.3 %collective-permute-start.43 = (bf16[1536,128]{1,0:T(8,128)(2,1)S(1)}, bf16[1536,128]{1,0:T(8,128)(2,1)S(1)}, u32[]{:S(2)}, u32[]{:S(2)}) collective-permute-start(bf16[1536,128]{1,0:T(8,128)(2,1)S(1)} %fusion.72), channel_id=1, source_target_pairs={{0,8},{24,16},{8,0},{16,24},{1,9},{25,17},{9,1},{17,25},{2,10},{26... | collective-permute-start | bytes 1179656 | tf_op jit(solution)/shard_map/ppermute | solution.py:107
  199.3 12.3 %collective-permute-start.42 = (bf16[1536,128]{1,0:T(8,128)(2,1)S(1)}, bf16[1536,128]{1,0:T(8,128)(2,1)S(1)}, u32[]{:S(2)}, u32[]{:S(2)}) collective-permute-start(bf16[1536,128]{1,0:T(8,128)(2,1)S(1)} %add_convert_fusion.4), channel_id=1, source_target_pairs={{8,16},{16,8},{9,17},{17,9},{10,18},{18,10},{11,19},{19,11},{12,20... | collective-permute-start | bytes 1179656 | tf_op jit(solution)/shard_map/ppermute | solution.py:115
  200.1 17.0 %collective-permute-start.48 = (bf16[1536,128]{1,0:T(8,128)(2,1)S(1)}, bf16[1536,128]{1,0:T(8,128)(2,1)S(1)}, u32[]{:S(2)}, u32[]{:S(2)}) collective-permute-start(bf16[1536,128]{1,0:T(8,128)(2,1)S(1)} %add_convert_fusion.3), channel_id=1, source_target_pairs={{8,0},{16,24},{9,1},{17,25},{10,2},{18,26},{11,3},{19,27},{12,4},{... | collective-permute-start | bytes 1179656 | tf_op jit(solution)/shard_map/ppermute | solution.py:107
  208.2 7.5 %collective-permute-start.45 = (bf16[1536,128]{1,0:T(8,128)(2,1)S(1)}, bf16[1536,128]{1,0:T(8,128)(2,1)S(1)}, u32[]{:S(2)}, u32[]{:S(2)}) collective-permute-start(bf16[1536,128]{1,0:T(8,128)(2,1)S(1)} %add_convert_fusion.2), channel_id=1, source_target_pairs={{8,16},{16,8},{9,17},{17,9},{10,18},{18,10},{11,19},{19,11},{12,20... | collective-permute-start | bytes 1179656 | tf_op jit(solution)/shard_map/ppermute | solution.py:115
  211.7 13.4 %collective-permute-start.47 = (bf16[1536,128]{1,0:T(8,128)(2,1)S(1)}, bf16[1536,128]{1,0:T(8,128)(2,1)S(1)}, u32[]{:S(2)}, u32[]{:S(2)}) collective-permute-start(bf16[1536,128]{1,0:T(8,128)(2,1)S(1)} %add_convert_fusion), channel_id=1, source_target_pairs={{8,0},{16,24},{9,1},{17,25},{10,2},{18,26},{11,3},{19,27},{12,4},{... | collective-permute-start | bytes 1179656 | tf_op jit(solution)/shard_map/ppermute | solution.py:107
  215.8 13.5 %collective-permute-start.46 = (bf16[1536,128]{1,0:T(8,128)(2,1)S(1)}, bf16[1536,128]{1,0:T(8,128)(2,1)S(1)}, u32[]{:S(2)}, u32[]{:S(2)}) collective-permute-start(bf16[1536,128]{1,0:T(8,128)(2,1)S(1)} %add_convert_fusion.1), channel_id=1, source_target_pairs={{8,0},{16,24},{9,1},{17,25},{10,2},{18,26},{11,3},{19,27},{12,4},{... | collective-permute-start | bytes 1179656 | tf_op jit(solution)/shard_map/ppermute | solution.py:107
  (18 other events, 219.5 us)

commit v19 on v18

--- a/solution.py
+++ b/solution.py
@@ -204,7 +204,7 @@
     context_all = jnp.concatenate(near_blocks + far_blocks, axis=0)
     narrow = 128
     units = cols // narrow
-    widths = [1, 3, units - 4]
+    widths = [1, min(4, units - 2), units - 1 - min(4, units - 2)]
     islands = lax.axis_size("island")
     line = IslandLine(units)
     locals_, rings, crosses = [], [], []
@@ -221,8 +221,8 @@
         ).astype(bf16)
         if c == 1:
             d_local, rings[0] = together(d_local, rings[0])
-        elif c == 2:
-            d_local, crosses[0] = together(d_local, crosses[0])
+        elif c == 2 and 0 in line.sums:
+            d_local, line.sums[0] = together(d_local, line.sums[0])
         locals_.append(d_local)
         rings.append(lax.ppermute(d_local, ("fsdp", "tp"), ring_pairs))
         crosses.append(lax.ppermute(d_local, ("fsdp", "tp"), cross_pairs))
@@ -254,14 +254,14 @@
         for u in range(hi - lo):
             line.part[lo + u] = pseudo[:, u * narrow : (u + 1) * narrow]
 
-    for c in range(len(widths)):
-        move(c)
+    move(0)
+    move(1)
     add_pseudo(gathered(0), 0, 1)
     found = gathered(1)
     early = sum(widths[:2])
     add_pseudo(found, 1, 2)
-    add_pseudo(found[:, narrow:], 2, early, behind=1)
-    last = gathered(2)
+    for lo in range(2, early, 2):
+        add_pseudo(found[:, (lo - 1) * narrow :], lo, min(lo + 2, early), behind=1)
     todo = [(lo, min(lo + 2, units)) for lo in range(early, units, 2)]
     if islands == 4:
         for s in range(2):
@@ -271,11 +271,16 @@
                 lo, hi = todo.pop(0)
                 add_pseudo(last[:, (lo - early) * narrow :], lo, hi, s - 1)
             line.step(s)
+            if s == 0:
+                move(2)
+                last = gathered(2)
             first = 3 * (s - units + 2)
             if first >= 0 and s + 2 in line.paid and first in line.totals:
                 line.totals[first], line.paid[s + 2] = together(line.totals[first], line.paid[s + 2])
         sums = [line.totals[k] for k in range(units)]
     else:
+        move(2)
+        last = gathered(2)
         for lo, hi in todo:
             add_pseudo(last[:, (lo - early) * narrow :], lo, hi)
         sums = [lax.psum(line.part[k], "island") for k in range(units)]

time: 233 us -> 237 us (1.017)
  waiting for transfers between devices: 73.4 us -> 81.4 us
  starting transfers between devices: 98.3 us -> 92.7 us
    ppermute x15, starting transfers between devices: 63.5 us -> 57.9 us  [send_outer(): self.edge[s] = lax.ppermute(payload, 'island', pairs)]
    ppermute x3, waiting for transfers between devices: 3.3 us -> 7.7 us  [move(): crosses.append(lax.ppermute(d_local, ('fsdp', 'tp'), cross_pairs))]
    ppermute x3, waiting for transfers between devices: 1.71 us -> 4.83 us  [move(): rings.append(lax.ppermute(d_local, ('fsdp', 'tp'), ring_pairs))]
    dot_general x7 -> x8, matrix products: 15 us -> 15.7 us  [add_pseudo(): lax.dot_general(context_all, piece, (((0,), (0,)), ((), ())), preferred_e...]
  transfers between devices with their start and end apart: 49 -> 49, of which waited for: 23 -> 22; matrix products, arithmetic and copies ran while one was open for 19% -> 19% of each run, Pallas kernels for 4% -> 3%
where the time goes in v19:
time: 237 us; the launch traced here: 234 us
  starting transfers between devices  92.7 us (39%)
  waiting for transfers between devices  81.4 us (34%)
  matrix products  25.2 us (11%)
  other arithmetic  13 us (5%)
  Pallas kernels  11.1 us (5%)
  local copies, waits for them, and re-layouts  8.57 us (4%)
    ppermute x15, starting transfers between devices, send_outer(): self.edge[s] = lax.ppermute(payload, 'island', pairs)  57.9 us
    ppermute x11, waiting for transfers between devices, swap(): return lax.ppermute(value, axis, [(i, i ^ bit) for i in range(count)])  33.4 us
    ppermute x15, waiting for transfers between devices, send_outer(): self.edge[s] = lax.ppermute(payload, 'island', pairs)  27.9 us
    dot_general x8, matrix products, add_pseudo(): lax.dot_general(context_all, piece, (((0,), (0,)), ((), ())), preferred_e...  15.7 us
    pallas_call x5, Pallas kernels, finish(): pl.pallas_call(functools.partial(finish_kernel, count, start, narrow, isl...  11.1 us
    ppermute x3, starting transfers between devices, move(): crosses.append(lax.ppermute(d_local, ('fsdp', 'tp'), cross_pairs))  10.1 us
    dot_general x3, matrix products, project(): jnp.dot(block, weight, preferred_element_type=f32).astype(bf16)  9.49 us
    ppermute x12, starting transfers between devices, step(): self.mid[s] = lax.ppermute(self.sums[s], 'island', [(1, 2), (2, 1)])  8.58 us
  transfers between devices with their start and end apart: 49, of which 22 were waited for; matrix products, arithmetic and copies ran while one was open for 19% of the time, Pallas kernels for 3%

profile of v19, /device:TPU:2, one launch (start us, length us, event | category | flops | bytes accessed | tf_op | source)
XLA Modules:
  0.0 233.9 jit_solution(13372355798462497724)
XLA Ops:
  5.0 15.3 %collective-permute-done = bf16[256,1536]{1,0:T(8,128)(2,1)} collective-permute-done((bf16[256,1536]{1,0:T(8,128)(2,1)}, bf16[256,1536]{1,0:T(8,128)(2,1)}, u32[]{:S(2)}, u32[]{:S(2)}) %collective-permute-start) | collective-permute-done | bytes 786464 | tf_op jit(solution)/shard_map/ppermute | solution.py:31
  20.4 4.0 %convolution_convert_fusion.2 = bf16[256,1536]{1,0:T(8,128)(2,1)S(1)} fusion(bf16[256,1536]{1,0:T(8,128)(2,1)} %collective-permute-done, bf16[1536,1536]{1,0:T(8,128)(2,1)} %param.12), kind=kOutput, calls=%fused_computation.2 | convolution fusion | flops 1208352768 | bytes 6291456 | tf_op jit(solution)/shard_map/dot_general | solution.py:144
  26.7 4.1 %convolution_convert_fusion = bf16[512,1536]{1,0:T(8,128)(2,1)} fusion(bf16[1536,1536]{1,0:T(8,128)(2,1)S(1)} %bitcast.230, bf16[256,1536]{1,0:T(8,128)(2,1)S(1)} %collective-permute-done.5, bf16[256,1536]{1,0:T(8,128)(2,1)S(1)} %copy-done.1), kind=kOutput, calls=%fused_computation | convolution fusion | flops 2419851264 | bytes 7864320 | tf_op jit(solution)/shard_map/dot_general | solution.py:144
  30.8 3.6 %collective-permute-start.7 = (bf16[512,1536]{1,0:T(8,128)(2,1)}, bf16[512,1536]{1,0:T(8,128)(2,1)}, u32[]{:S(2)}, u32[]{:S(2)}) collective-permute-start(bf16[512,1536]{1,0:T(8,128)(2,1)} %convolution_convert_fusion), channel_id=1, source_target_pairs={{4,5},{1,0},{6,7},{3,2},{12,13},{9,8},{14,15},{11,10},{20,21},{17,... | collective-permute-start | bytes 4718600 | tf_op jit(solution)/shard_map/ppermute | solution.py:168
  34.5 2.3 collective-permute-done.6
  40.4 3.4 %collective-permute-start.10 = (bf16[128,1536]{1,0:T(8,128)(2,1)}, bf16[128,1536]{1,0:T(8,128)(2,1)}, u32[]{:S(2)}, u32[]{:S(2)}) collective-permute-start(bf16[128,1536]{1,0:T(8,128)(2,1)} %get-tuple-element.345), channel_id=1, source_target_pairs={{0,4},{2,6},{4,0},{6,2},{1,5},{3,7},{5,1},{7,3},{8,12},{10,14},{12... | collective-permute-start | bytes 1179656 | tf_op jit(solution)/shard_map/ppermute | solution.py:31
  45.5 2.1 constant_dynamic-update-slice_fusion.2
  48.9 6.3 %collective-permute-done.10 = bf16[128,1536]{1,0:T(8,128)(2,1)} collective-permute-done((bf16[128,1536]{1,0:T(8,128)(2,1)}, bf16[128,1536]{1,0:T(8,128)(2,1)}, u32[]{:S(2)}, u32[]{:S(2)}) %collective-permute-start.10) | collective-permute-done | bytes 393248 | tf_op jit(solution)/shard_map/ppermute | solution.py:31
  56.5 6.0 %collective-permute-done.12 = bf16[128,1536]{1,0:T(8,128)(2,1)S(1)} collective-permute-done((bf16[128,1536]{1,0:T(8,128)(2,1)}, bf16[128,1536]{1,0:T(8,128)(2,1)S(1)}, u32[]{:S(2)}, u32[]{:S(2)}) %collective-permute-start.12) | collective-permute-done | bytes 393248 | tf_op jit(solution)/shard_map/ppermute | solution.py:31
  63.7 3.8 %collective-permute-done.7 = bf16[512,1536]{1,0:T(8,128)(2,1)} collective-permute-done((bf16[512,1536]{1,0:T(8,128)(2,1)}, bf16[512,1536]{1,0:T(8,128)(2,1)}, u32[]{:S(2)}, u32[]{:S(2)}) %collective-permute-start.7) | collective-permute-done | bytes 1572896 | tf_op jit(solution)/shard_map/ppermute | solution.py:168
  67.6 1.8 multiply_reduce_fusion.7
  69.4 1.8 multiply_reduce_fusion.5
  71.2 1.7 multiply_reduce_fusion.3
  73.0 3.7 %collective-permute-done.13 = bf16[128,1536]{1,0:T(8,128)(2,1)S(1)} collective-permute-done((bf16[128,1536]{1,0:T(8,128)(2,1)S(1)}, bf16[128,1536]{1,0:T(8,128)(2,1)S(1)}, u32[]{:S(2)}, u32[]{:S(2)}) %collective-permute-start.13) | collective-permute-done | bytes 393248 | tf_op jit(solution)/shard_map/ppermute | solution.py:173
  80.0 3.5 %collective-permute-done.15 = f32[2,512]{1,0:T(2,128)S(1)} collective-permute-done((f32[2,512]{1,0:T(2,128)S(1)}, f32[2,512]{1,0:T(2,128)S(1)}, u32[]{:S(2)}, u32[]{:S(2)}) %collective-permute-start.15) | collective-permute-done | bytes 4128 | tf_op jit(solution)/shard_map/ppermute | solution.py:31
  83.8 3.3 %collective-permute-start.19 = (bf16[512,128]{1,0:T(8,128)(2,1)S(1)}, bf16[512,128]{1,0:T(8,128)(2,1)S(1)}, u32[]{:S(2)}, u32[]{:S(2)}) collective-permute-start(bf16[512,128]{1,0:T(8,128)(2,1)S(1)} %pad_maximum_fusion.5), channel_id=1, source_target_pairs={{4,1},{1,4},{6,3},{3,6},{12,9},{9,12},{14,11},{11,14},{20,17},{17,... | collective-permute-start | bytes 393224 | tf_op jit(solution)/shard_map/ppermute | solution.py:228
  88.1 4.1 %collective-permute-done.16 = bf16[512,128]{1,0:T(8,128)(2,1)S(1)} collective-permute-done((bf16[512,128]{1,0:T(8,128)(2,1)S(1)}, bf16[512,128]{1,0:T(8,128)(2,1)S(1)}, u32[]{:S(2)}, u32[]{:S(2)}) %collective-permute-start.16) | collective-permute-done | bytes 131104 | tf_op jit(solution)/shard_map/ppermute | solution.py:227
  92.2 3.4 %collective-permute-start.18 = (bf16[512,512]{1,0:T(8,128)(2,1)S(1)}, bf16[512,512]{1,0:T(8,128)(2,1)S(1)}, u32[]{:S(2)}, u32[]{:S(2)}) collective-permute-start(bf16[512,512]{1,0:T(8,128)(2,1)S(1)} %pad_maximum_fusion.1), channel_id=1, source_target_pairs={{4,1},{1,4},{6,3},{3,6},{12,9},{9,12},{14,11},{11,14},{20,17},{17,... | collective-permute-start | bytes 1572872 | tf_op jit(solution)/shard_map/ppermute | solution.py:228
  95.8 2.6 %fusion.56 = bf16[1536,128]{1,0:T(8,128)(2,1)S(1)} fusion(bf16[1536,1536]{1,0:T(8,128)(2,1)S(1)} %bitcast.232, bf16[1,1536,1536]{2,1,0:T(8,128)(2,1)S(1)} %bitcast.234, bf16[1,1536,1536]{2,1,0:T(8,128)(2,1)} %param.13, bf16[1024,1536]{1,0:T(8,128)(2,1)S(1)} %constant_dynamic-update-slice_fusion, bf16[1024,128]{1,0:T(8,128)(2,1)S(1)} %pad_maximum_fusion.4), kind=kOutput, calls=%fused_computation.128 | convolution fusion | flops 406192128 | bytes 4980736 | tf_op jit(solution)/shard_map/dot_general | solution.py:243
  98.4 3.7 %collective-permute-start.20 = (bf16[1536,128]{1,0:T(8,128)(2,1)S(1)}, bf16[1536,128]{1,0:T(8,128)(2,1)S(1)}, u32[]{:S(2)}, u32[]{:S(2)}) collective-permute-start(bf16[1536,128]{1,0:T(8,128)(2,1)S(1)} %fusion.56), channel_id=1, source_target_pairs={{0,8},{24,16},{1,9},{25,17},{2,10},{26,18},{3,11},{27,19},{4,12},{... | collective-permute-start | bytes 1179656 | tf_op jit(solution)/shard_map/ppermute | solution.py:107
  102.1 4.9 %collective-permute-done.18 = bf16[512,512]{1,0:T(8,128)(2,1)S(1)} collective-permute-done((bf16[512,512]{1,0:T(8,128)(2,1)S(1)}, bf16[512,512]{1,0:T(8,128)(2,1)S(1)}, u32[]{:S(2)}, u32[]{:S(2)}) %collective-permute-start.18) | collective-permute-done | bytes 524320 | tf_op jit(solution)/shard_map/ppermute | solution.py:228
  109.0 2.2 fusion.27
  111.3 3.5 %collective-permute-start.24 = (bf16[1536,128]{1,0:T(8,128)(2,1)S(1)}, bf16[1536,128]{1,0:T(8,128)(2,1)S(1)}, u32[]{:S(2)}, u32[]{:S(2)}) collective-permute-start(bf16[1536,128]{1,0:T(8,128)(2,1)S(1)} %fusion.55), channel_id=1, source_target_pairs={{0,8},{24,16},{1,9},{25,17},{2,10},{26,18},{3,11},{27,19},{4,12},{... | collective-permute-start | bytes 1179656 | tf_op jit(solution)/shard_map/ppermute | solution.py:107
  115.6 3.3 %collective-permute-start.22 = (bf16[512,896]{1,0:T(8,128)(2,1)S(1)}, bf16[512,896]{1,0:T(8,128)(2,1)S(1)}, u32[]{:S(2)}, u32[]{:S(2)}) collective-permute-start(bf16[512,896]{1,0:T(8,128)(2,1)S(1)} %pad_maximum_fusion), channel_id=1, source_target_pairs={{4,1},{1,4},{6,3},{3,6},{12,9},{9,12},{14,11},{11,14},{20,17},{17,... | collective-permute-start | bytes 2752520 | tf_op jit(solution)/shard_map/ppermute | solution.py:228
  120.4 4.1 %collective-permute-start.26 = (bf16[1536,128]{1,0:T(8,128)(2,1)S(1)}, bf16[1536,128]{1,0:T(8,128)(2,1)S(1)}, u32[]{:S(2)}, u32[]{:S(2)}) collective-permute-start(bf16[1536,128]{1,0:T(8,128)(2,1)S(1)} %slice.466), channel_id=1, source_target_pairs={{0,8},{24,16},{1,9},{25,17},{2,10},{26,18},{3,11},{27,19},{4,12},{... | collective-permute-start | bytes 1179656 | tf_op jit(solution)/shard_map/ppermute | solution.py:107
  126.9 6.8 %collective-permute-done.26 = bf16[1536,128]{1,0:T(8,128)(2,1)S(1)} collective-permute-done((bf16[1536,128]{1,0:T(8,128)(2,1)S(1)}, bf16[1536,128]{1,0:T(8,128)(2,1)S(1)}, u32[]{:S(2)}, u32[]{:S(2)}) %collective-permute-start.26) | collective-permute-done | bytes 393248 | tf_op jit(solution)/shard_map/ppermute | solution.py:107
  134.5 2.8 %collective-permute-done.22 = bf16[512,896]{1,0:T(8,128)(2,1)S(1)} collective-permute-done((bf16[512,896]{1,0:T(8,128)(2,1)S(1)}, bf16[512,896]{1,0:T(8,128)(2,1)S(1)}, u32[]{:S(2)}, u32[]{:S(2)}) %collective-permute-start.22) | collective-permute-done | bytes 917536 | tf_op jit(solution)/shard_map/ppermute | solution.py:228
  138.1 2.2 collective-permute-start.27
  141.4 2.2 fusion.28
  143.8 7.6 %collective-permute-start.31 = (bf16[1536,128]{1,0:T(8,128)(2,1)S(1)}, bf16[1536,128]{1,0:T(8,128)(2,1)S(1)}, u32[]{:S(2)}, u32[]{:S(2)}) collective-permute-start(bf16[1536,128]{1,0:T(8,128)(2,1)S(1)} %fusion.73), channel_id=1, source_target_pairs={{0,8},{24,16},{8,0},{16,24},{1,9},{25,17},{9,1},{17,25},{2,10},{26... | collective-permute-start | bytes 1179656 | tf_op jit(solution)/shard_map/ppermute | solution.py:107
  151.4 2.2 fusion.30
  154.6 2.4 %collective-permute-start.33 = (bf16[1536,128]{1,0:T(8,128)(2,1)S(1)}, bf16[1536,128]{1,0:T(8,128)(2,1)S(1)}, u32[]{:S(2)}, u32[]{:S(2)}) collective-permute-start(bf16[1536,128]{1,0:T(8,128)(2,1)S(1)} %fusion.74), channel_id=1, source_target_pairs={{0,8},{24,16},{8,0},{16,24},{1,9},{25,17},{9,1},{17,25},{2,10},{26... | collective-permute-start | bytes 1179656 | tf_op jit(solution)/shard_map/ppermute | solution.py:107
  157.1 3.0 %collective-permute-done.31 = bf16[1536,128]{1,0:T(8,128)(2,1)S(1)} collective-permute-done((bf16[1536,128]{1,0:T(8,128)(2,1)S(1)}, bf16[1536,128]{1,0:T(8,128)(2,1)S(1)}, u32[]{:S(2)}, u32[]{:S(2)}) %collective-permute-start.31) | collective-permute-done | bytes 393248 | tf_op jit(solution)/shard_map/ppermute | solution.py:107
  161.1 6.8 %collective-permute-start.35 = (bf16[1536,128]{1,0:T(8,128)(2,1)S(1)}, bf16[1536,128]{1,0:T(8,128)(2,1)S(1)}, u32[]{:S(2)}, u32[]{:S(2)}) collective-permute-start(bf16[1536,128]{1,0:T(8,128)(2,1)S(1)} %fusion.75), channel_id=1, source_target_pairs={{0,8},{24,16},{8,0},{16,24},{1,9},{25,17},{9,1},{17,25},{2,10},{26... | collective-permute-start | bytes 1179656 | tf_op jit(solution)/shard_map/ppermute | solution.py:107
  169.5 6.4 %collective-permute-start.38 = (bf16[1536,128]{1,0:T(8,128)(2,1)S(1)}, bf16[1536,128]{1,0:T(8,128)(2,1)S(1)}, u32[]{:S(2)}, u32[]{:S(2)}) collective-permute-start(bf16[1536,128]{1,0:T(8,128)(2,1)S(1)} %fusion.76), channel_id=1, source_target_pairs={{0,8},{24,16},{8,0},{16,24},{1,9},{25,17},{9,1},{17,25},{2,10},{26... | collective-permute-start | bytes 1179656 | tf_op jit(solution)/shard_map/ppermute | solution.py:107
  175.8 2.2 fusion.29
  179.1 4.2 %collective-permute-start.40 = (bf16[1536,128]{1,0:T(8,128)(2,1)S(1)}, bf16[1536,128]{1,0:T(8,128)(2,1)S(1)}, u32[]{:S(2)}, u32[]{:S(2)}) collective-permute-start(bf16[1536,128]{1,0:T(8,128)(2,1)S(1)} %fusion.77), channel_id=1, source_target_pairs={{0,8},{24,16},{8,0},{16,24},{1,9},{25,17},{9,1},{17,25},{2,10},{26... | collective-permute-start | bytes 1179656 | tf_op jit(solution)/shard_map/ppermute | solution.py:107
  183.4 2.5 %collective-permute-done.38 = bf16[1536,128]{1,0:T(8,128)(2,1)S(1)} collective-permute-done((bf16[1536,128]{1,0:T(8,128)(2,1)S(1)}, bf16[1536,128]{1,0:T(8,128)(2,1)S(1)}, u32[]{:S(2)}, u32[]{:S(2)}) %collective-permute-start.38) | collective-permute-done | bytes 393248 | tf_op jit(solution)/shard_map/ppermute | solution.py:107
  188.6 5.0 %collective-permute-start.39 = (bf16[1536,128]{1,0:T(8,128)(2,1)S(1)}, bf16[1536,128]{1,0:T(8,128)(2,1)S(1)}, u32[]{:S(2)}, u32[]{:S(2)}) collective-permute-start(bf16[1536,128]{1,0:T(8,128)(2,1)S(1)} %fusion.78), channel_id=1, source_target_pairs={{0,8},{24,16},{8,0},{16,24},{1,9},{25,17},{9,1},{17,25},{2,10},{26... | collective-permute-start | bytes 1179656 | tf_op jit(solution)/shard_map/ppermute | solution.py:107
  195.3 6.5 %collective-permute-start.43 = (bf16[1536,128]{1,0:T(8,128)(2,1)S(1)}, bf16[1536,128]{1,0:T(8,128)(2,1)S(1)}, u32[]{:S(2)}, u32[]{:S(2)}) collective-permute-start(bf16[1536,128]{1,0:T(8,128)(2,1)S(1)} %fusion.79), channel_id=1, source_target_pairs={{0,8},{24,16},{8,0},{16,24},{1,9},{25,17},{9,1},{17,25},{2,10},{26... | collective-permute-start | bytes 1179656 | tf_op jit(solution)/shard_map/ppermute | solution.py:107
  201.9 1.7 collective-permute-done.39
  206.2 3.4 %collective-permute-done.43 = bf16[1536,128]{1,0:T(8,128)(2,1)S(1)} collective-permute-done((bf16[1536,128]{1,0:T(8,128)(2,1)S(1)}, bf16[1536,128]{1,0:T(8,128)(2,1)S(1)}, u32[]{:S(2)}, u32[]{:S(2)}) %collective-permute-start.43) | collective-permute-done | bytes 393248 | tf_op jit(solution)/shard_map/ppermute | solution.py:107
  210.4 2.6 %shard_map.95 = (f32[1536,1536]{1,0:T(8,128)}, bf16[1536,1536]{1,0:T(8,128)(2,1)}) custom-call(bf16[1536,128]{1,0:T(8,128)(2,1)S(1)} %broadcast_select_fusion.15.refs_0_, bf16[1536,128]{1,0:T(8,128)(2,1)S(1)} %broadcast_select_fusion.5.refs_1_, bf16[1536,128]{1,0:T(8,128)(2,1)S(1)} %broadcast_select_fusion.4.refs_2_, f32[1536,1536]{1,0:T(8,128)S(1)} %bitcast.216), custom_call_target="tpu_custom_call" | custom-call | flops 2949120 | bytes 7077888 | tf_op jit(solution)/shard_map/pallas_call | solution.py:61
  214.5 3.9 %collective-permute-done.48 = bf16[1536,128]{1,0:T(8,128)(2,1)S(1)} collective-permute-done((bf16[1536,128]{1,0:T(8,128)(2,1)S(1)}, bf16[1536,128]{1,0:T(8,128)(2,1)S(1)}, u32[]{:S(2)}, u32[]{:S(2)}) %collective-permute-start.48) | collective-permute-done | bytes 393248 | tf_op jit(solution)/shard_map/ppermute | solution.py:107
  219.9 2.6 %shard_map.96 = (f32[1536,1536]{1,0:T(8,128)}, bf16[1536,1536]{1,0:T(8,128)(2,1)}) custom-call(bf16[1536,128]{1,0:T(8,128)(2,1)S(1)} %broadcast_select_fusion.13.refs_0_, bf16[1536,128]{1,0:T(8,128)(2,1)S(1)} %broadcast_select_fusion.7.refs_1_, bf16[1536,128]{1,0:T(8,128)(2,1)S(1)} %broadcast_select_fusion.6.refs_2_, ...), custom_call_target="tpu_custom_call", output_to_operand_aliasing={{0}: (4, {}), {1}: (5, {})} | custom-call | flops 2949120 | bytes 7077888 | tf_op jit(solution)/shard_map/pallas_call | solution.py:61
  222.5 2.6 %shard_map.97 = (f32[1536,1536]{1,0:T(8,128)}, bf16[1536,1536]{1,0:T(8,128)(2,1)}) custom-call(bf16[1536,128]{1,0:T(8,128)(2,1)S(1)} %broadcast_select_fusion.14.refs_0_, bf16[1536,128]{1,0:T(8,128)(2,1)S(1)} %broadcast_select_fusion.9.refs_1_, bf16[1536,128]{1,0:T(8,128)(2,1)S(1)} %broadcast_select_fusion.8.refs_2_, ...), custom_call_target="tpu_custom_call", output_to_operand_aliasing={{0}: (4, {}), {1}: (5, {})} | custom-call | flops 2949120 | bytes 7077888 | tf_op jit(solution)/shard_map/pallas_call | solution.py:61
  226.2 4.2 %collective-permute-done.46 = bf16[1536,128]{1,0:T(8,128)(2,1)S(1)} collective-permute-done((bf16[1536,128]{1,0:T(8,128)(2,1)S(1)}, bf16[1536,128]{1,0:T(8,128)(2,1)S(1)}, u32[]{:S(2)}, u32[]{:S(2)}) %collective-permute-start.46) | collective-permute-done | bytes 393248 | tf_op jit(solution)/shard_map/ppermute | solution.py:107
  230.5 1.9 shard_map.98
  (183 shorter events, 47.3 us)
Async XLA Ops:
  0.6 19.7 %collective-permute-start = (bf16[256,1536]{1,0:T(8,128)(2,1)}, bf16[256,1536]{1,0:T(8,128)(2,1)}, u32[]{:S(2)}, u32[]{:S(2)}) collective-permute-start(bf16[256,1536]{1,0:T(8,128)(2,1)} %param.8), channel_id=1, source_target_pairs={{0,4},{2,6},{4,0},{6,2},{1,5},{3,7},{5,1},{7,3},{8,12},{10,14},{12... | collective-permute-start | bytes 2359304 | tf_op jit(solution)/shard_map/ppermute | solution.py:31
  3.8 16.5 %collective-permute-start.1 = (bf16[256,1536]{1,0:T(8,128)(2,1)S(1)}, bf16[256,1536]{1,0:T(8,128)(2,1)S(1)}, u32[]{:S(2)}, u32[]{:S(2)}) collective-permute-start(bf16[256,1536]{1,0:T(8,128)(2,1)S(1)} %get-tuple-element.333), channel_id=1, source_target_pairs={{0,2},{2,0},{4,6},{6,4},{1,3},{3,1},{5,7},{7,5},{8,10},{10,8},{12,... | collective-permute-start | bytes 2359304 | tf_op jit(solution)/shard_map/ppermute | solution.py:31
  4.2 16.1 %collective-permute-start.2 = (bf16[256,1536]{1,0:T(8,128)(2,1)S(1)}, bf16[256,1536]{1,0:T(8,128)(2,1)S(1)}, u32[]{:S(2)}, u32[]{:S(2)}) collective-permute-start(bf16[256,1536]{1,0:T(8,128)(2,1)S(1)} %get-tuple-element.331), channel_id=1, source_target_pairs={{0,2},{2,0},{4,6},{6,4},{1,3},{3,1},{5,7},{7,5},{8,10},{10,8},{12,... | collective-permute-start | bytes 2359304 | tf_op jit(solution)/shard_map/ppermute | solution.py:31
  5.0 21.7 %collective-permute-start.5 = (bf16[256,1536]{1,0:T(8,128)(2,1)S(1)}, bf16[256,1536]{1,0:T(8,128)(2,1)S(1)}, u32[]{:S(2)}, u32[]{:S(2)}) collective-permute-start(bf16[256,1536]{1,0:T(8,128)(2,1)S(1)} %copy-done.1), channel_id=1, source_target_pairs={{0,2},{2,0},{4,6},{6,4},{1,3},{3,1},{5,7},{7,5},{8,10},{10,8},{12,... | collective-permute-start | bytes 2359304 | tf_op jit(solution)/shard_map/ppermute | solution.py:31
  20.3 17.8 %collective-permute-start.9 = (bf16[256,1536]{1,0:T(8,128)(2,1)}, bf16[256,1536]{1,0:T(8,128)(2,1)S(1)}, u32[]{:S(2)}, u32[]{:S(2)}) collective-permute-start(bf16[256,1536]{1,0:T(8,128)(2,1)} %collective-permute-done), channel_id=1, source_target_pairs={{0,2},{2,0},{4,6},{6,4},{1,3},{3,1},{5,7},{7,5},{8,10},{10,8},{12,... | collective-permute-start | bytes 2359304 | tf_op jit(solution)/shard_map/ppermute | solution.py:31
  25.2 11.6 %collective-permute-start.6 = (bf16[128,1536]{1,0:T(8,128)(2,1)S(1)}, bf16[128,1536]{1,0:T(8,128)(2,1)}, u32[]{:S(2)}, u32[]{:S(2)}) collective-permute-start(bf16[128,1536]{1,0:T(8,128)(2,1)S(1)} %get-tuple-element.343), channel_id=1, source_target_pairs={{0,4},{2,6},{4,0},{6,2},{1,5},{3,7},{5,1},{7,3},{8,12},{10,14},{12... | collective-permute-start | bytes 1179656 | tf_op jit(solution)/shard_map/ppermute | solution.py:31
  30.8 36.7 %collective-permute-start.7 = (bf16[512,1536]{1,0:T(8,128)(2,1)}, bf16[512,1536]{1,0:T(8,128)(2,1)}, u32[]{:S(2)}, u32[]{:S(2)}) collective-permute-start(bf16[512,1536]{1,0:T(8,128)(2,1)} %convolution_convert_fusion), channel_id=1, source_target_pairs={{4,5},{1,0},{6,7},{3,2},{12,13},{9,8},{14,15},{11,10},{20,21},{17,... | collective-permute-start | bytes 4718600 | tf_op jit(solution)/shard_map/ppermute | solution.py:168
  34.5 13.1 %collective-permute-start.3 = (bf16[128,1536]{1,0:T(8,128)(2,1)}, bf16[128,1536]{1,0:T(8,128)(2,1)}, u32[]{:S(2)}, u32[]{:S(2)}) collective-permute-start(bf16[128,1536]{1,0:T(8,128)(2,1)} %get-tuple-element.344), channel_id=1, source_target_pairs={{0,4},{2,6},{4,0},{6,2},{1,5},{3,7},{5,1},{7,3},{8,12},{10,14},{12... | collective-permute-start | bytes 1179656 | tf_op jit(solution)/shard_map/ppermute | solution.py:31
  36.8 27.0 %collective-permute-start.8 = (bf16[128,1536]{1,0:T(8,128)(2,1)}, bf16[128,1536]{1,0:T(8,128)(2,1)}, u32[]{:S(2)}, u32[]{:S(2)}) collective-permute-start(bf16[128,1536]{1,0:T(8,128)(2,1)} %collective-permute-done.6), channel_id=1, source_target_pairs={{0,1},{5,4},{2,3},{7,6},{8,9},{13,12},{10,11},{15,14},{16,17},{21,... | collective-permute-start | bytes 1179656 | tf_op jit(solution)/shard_map/ppermute | solution.py:173
  40.4 14.8 %collective-permute-start.10 = (bf16[128,1536]{1,0:T(8,128)(2,1)}, bf16[128,1536]{1,0:T(8,128)(2,1)}, u32[]{:S(2)}, u32[]{:S(2)}) collective-permute-start(bf16[128,1536]{1,0:T(8,128)(2,1)} %get-tuple-element.345), channel_id=1, source_target_pairs={{0,4},{2,6},{4,0},{6,2},{1,5},{3,7},{5,1},{7,3},{8,12},{10,14},{12... | collective-permute-start | bytes 1179656 | tf_op jit(solution)/shard_map/ppermute | solution.py:31
  43.8 18.6 %collective-permute-start.12 = (bf16[128,1536]{1,0:T(8,128)(2,1)}, bf16[128,1536]{1,0:T(8,128)(2,1)S(1)}, u32[]{:S(2)}, u32[]{:S(2)}) collective-permute-start(bf16[128,1536]{1,0:T(8,128)(2,1)} %get-tuple-element.346), channel_id=1, source_target_pairs={{0,4},{2,6},{4,0},{6,2},{1,5},{3,7},{5,1},{7,3},{8,12},{10,14},{12... | collective-permute-start | bytes 1179656 | tf_op jit(solution)/shard_map/ppermute | solution.py:31
  47.6 21.8 %collective-permute-start.4 = (bf16[128,1536]{1,0:T(8,128)(2,1)}, bf16[128,1536]{1,0:T(8,128)(2,1)S(1)}, u32[]{:S(2)}, u32[]{:S(2)}) collective-permute-start(bf16[128,1536]{1,0:T(8,128)(2,1)} %collective-permute-done.3), channel_id=1, source_target_pairs={{0,1},{5,4},{2,3},{7,6},{8,9},{13,12},{10,11},{15,14},{16,17},{21,... | collective-permute-start | bytes 1179656 | tf_op jit(solution)/shard_map/ppermute | solution.py:173
  55.2 16.0 %collective-permute-start.11 = (bf16[128,1536]{1,0:T(8,128)(2,1)}, bf16[128,1536]{1,0:T(8,128)(2,1)S(1)}, u32[]{:S(2)}, u32[]{:S(2)}) collective-permute-start(bf16[128,1536]{1,0:T(8,128)(2,1)} %collective-permute-done.10), channel_id=1, source_target_pairs={{0,1},{5,4},{2,3},{7,6},{8,9},{13,12},{10,11},{15,14},{16,17},{21,... | collective-permute-start | bytes 1179656 | tf_op jit(solution)/shard_map/ppermute | solution.py:173
  62.4 14.2 %collective-permute-start.13 = (bf16[128,1536]{1,0:T(8,128)(2,1)S(1)}, bf16[128,1536]{1,0:T(8,128)(2,1)S(1)}, u32[]{:S(2)}, u32[]{:S(2)}) collective-permute-start(bf16[128,1536]{1,0:T(8,128)(2,1)S(1)} %collective-permute-done.12), channel_id=1, source_target_pairs={{0,1},{5,4},{2,3},{7,6},{8,9},{13,12},{10,11},{15,14},{16,17},{21,... | collective-permute-start | bytes 1179656 | tf_op jit(solution)/shard_map/ppermute | solution.py:173
  79.8 3.7 %collective-permute-start.15 = (f32[2,512]{1,0:T(2,128)S(1)}, f32[2,512]{1,0:T(2,128)S(1)}, u32[]{:S(2)}, u32[]{:S(2)}) collective-permute-start(f32[2,512]{1,0:T(2,128)S(1)} %maximum_add_fusion), channel_id=1, source_target_pairs={{0,1},{1,0},{2,3},{3,2},{4,5},{5,4},{6,7},{7,6},{8,9},{9,8},{10,11... | collective-permute-start | bytes 12296 | tf_op jit(solution)/shard_map/ppermute | solution.py:31
  83.8 11.8 %collective-permute-start.19 = (bf16[512,128]{1,0:T(8,128)(2,1)S(1)}, bf16[512,128]{1,0:T(8,128)(2,1)S(1)}, u32[]{:S(2)}, u32[]{:S(2)}) collective-permute-start(bf16[512,128]{1,0:T(8,128)(2,1)S(1)} %pad_maximum_fusion.5), channel_id=1, source_target_pairs={{4,1},{1,4},{6,3},{3,6},{12,9},{9,12},{14,11},{11,14},{20,17},{17,... | collective-permute-start | bytes 393224 | tf_op jit(solution)/shard_map/ppermute | solution.py:228
  87.2 5.0 %collective-permute-start.16 = (bf16[512,128]{1,0:T(8,128)(2,1)S(1)}, bf16[512,128]{1,0:T(8,128)(2,1)S(1)}, u32[]{:S(2)}, u32[]{:S(2)}) collective-permute-start(bf16[512,128]{1,0:T(8,128)(2,1)S(1)} %pad_maximum_fusion.5), channel_id=1, source_target_pairs={{0,1},{5,4},{4,0},{1,5},{2,3},{7,6},{6,2},{3,7},{8,9},{13,12},{12,... | collective-permute-start | bytes 393224 | tf_op jit(solution)/shard_map/ppermute | solution.py:227
  92.2 14.8 %collective-permute-start.18 = (bf16[512,512]{1,0:T(8,128)(2,1)S(1)}, bf16[512,512]{1,0:T(8,128)(2,1)S(1)}, u32[]{:S(2)}, u32[]{:S(2)}) collective-permute-start(bf16[512,512]{1,0:T(8,128)(2,1)S(1)} %pad_maximum_fusion.1), channel_id=1, source_target_pairs={{4,1},{1,4},{6,3},{3,6},{12,9},{9,12},{14,11},{11,14},{20,17},{17,... | collective-permute-start | bytes 1572872 | tf_op jit(solution)/shard_map/ppermute | solution.py:228
  95.6 11.8 %collective-permute-start.17 = (bf16[512,512]{1,0:T(8,128)(2,1)S(1)}, bf16[512,512]{1,0:T(8,128)(2,1)S(1)}, u32[]{:S(2)}, u32[]{:S(2)}) collective-permute-start(bf16[512,512]{1,0:T(8,128)(2,1)S(1)} %pad_maximum_fusion.1), channel_id=1, source_target_pairs={{0,1},{5,4},{4,0},{1,5},{2,3},{7,6},{6,2},{3,7},{8,9},{13,12},{12,... | collective-permute-start | bytes 1572872 | tf_op jit(solution)/shard_map/ppermute | solution.py:227
  98.4 16.3 %collective-permute-start.20 = (bf16[1536,128]{1,0:T(8,128)(2,1)S(1)}, bf16[1536,128]{1,0:T(8,128)(2,1)S(1)}, u32[]{:S(2)}, u32[]{:S(2)}) collective-permute-start(bf16[1536,128]{1,0:T(8,128)(2,1)S(1)} %fusion.56), channel_id=1, source_target_pairs={{0,8},{24,16},{1,9},{25,17},{2,10},{26,18},{3,11},{27,19},{4,12},{... | collective-permute-start | bytes 1179656 | tf_op jit(solution)/shard_map/ppermute | solution.py:107
  111.3 13.3 %collective-permute-start.24 = (bf16[1536,128]{1,0:T(8,128)(2,1)S(1)}, bf16[1536,128]{1,0:T(8,128)(2,1)S(1)}, u32[]{:S(2)}, u32[]{:S(2)}) collective-permute-start(bf16[1536,128]{1,0:T(8,128)(2,1)S(1)} %fusion.55), channel_id=1, source_target_pairs={{0,8},{24,16},{1,9},{25,17},{2,10},{26,18},{3,11},{27,19},{4,12},{... | collective-permute-start | bytes 1179656 | tf_op jit(solution)/shard_map/ppermute | solution.py:107
  114.9 10.5 %collective-permute-start.23 = (bf16[1536,128]{1,0:T(8,128)(2,1)S(1)}, bf16[1536,128]{1,0:T(8,128)(2,1)S(1)}, u32[]{:S(2)}, u32[]{:S(2)}) collective-permute-start(bf16[1536,128]{1,0:T(8,128)(2,1)S(1)} %add_convert_fusion.23), channel_id=1, source_target_pairs={{8,16},{16,8},{9,17},{17,9},{10,18},{18,10},{11,19},{19,11},{12,20... | collective-permute-start | bytes 1179656 | tf_op jit(solution)/shard_map/ppermute | solution.py:115
  115.6 21.8 %collective-permute-start.22 = (bf16[512,896]{1,0:T(8,128)(2,1)S(1)}, bf16[512,896]{1,0:T(8,128)(2,1)S(1)}, u32[]{:S(2)}, u32[]{:S(2)}) collective-permute-start(bf16[512,896]{1,0:T(8,128)(2,1)S(1)} %pad_maximum_fusion), channel_id=1, source_target_pairs={{4,1},{1,4},{6,3},{3,6},{12,9},{9,12},{14,11},{11,14},{20,17},{17,... | collective-permute-start | bytes 2752520 | tf_op jit(solution)/shard_map/ppermute | solution.py:228
  118.9 18.7 %collective-permute-start.21 = (bf16[512,896]{1,0:T(8,128)(2,1)S(1)}, bf16[512,896]{1,0:T(8,128)(2,1)S(1)}, u32[]{:S(2)}, u32[]{:S(2)}) collective-permute-start(bf16[512,896]{1,0:T(8,128)(2,1)S(1)} %pad_maximum_fusion), channel_id=1, source_target_pairs={{0,1},{5,4},{4,0},{1,5},{2,3},{7,6},{6,2},{3,7},{8,9},{13,12},{12,... | collective-permute-start | bytes 2752520 | tf_op jit(solution)/shard_map/ppermute | solution.py:227
  120.4 13.2 %collective-permute-start.26 = (bf16[1536,128]{1,0:T(8,128)(2,1)S(1)}, bf16[1536,128]{1,0:T(8,128)(2,1)S(1)}, u32[]{:S(2)}, u32[]{:S(2)}) collective-permute-start(bf16[1536,128]{1,0:T(8,128)(2,1)S(1)} %slice.466), channel_id=1, source_target_pairs={{0,8},{24,16},{1,9},{25,17},{2,10},{26,18},{3,11},{27,19},{4,12},{... | collective-permute-start | bytes 1179656 | tf_op jit(solution)/shard_map/ppermute | solution.py:107
  124.7 9.8 %collective-permute-start.25 = (bf16[1536,128]{1,0:T(8,128)(2,1)S(1)}, bf16[1536,128]{1,0:T(8,128)(2,1)S(1)}, u32[]{:S(2)}, u32[]{:S(2)}) collective-permute-start(bf16[1536,128]{1,0:T(8,128)(2,1)S(1)} %add_convert_fusion.22), channel_id=1, source_target_pairs={{8,16},{16,8},{9,17},{17,9},{10,18},{18,10},{11,19},{19,11},{12,20... | collective-permute-start | bytes 1179656 | tf_op jit(solution)/shard_map/ppermute | solution.py:115
  125.6 14.8 %collective-permute-start.28 = (bf16[1536,128]{1,0:T(8,128)(2,1)S(1)}, bf16[1536,128]{1,0:T(8,128)(2,1)S(1)}, u32[]{:S(2)}, u32[]{:S(2)}) collective-permute-start(bf16[1536,128]{1,0:T(8,128)(2,1)S(1)} %fusion.71), channel_id=1, source_target_pairs={{0,8},{24,16},{8,0},{16,24},{1,9},{25,17},{9,1},{17,25},{2,10},{26... | collective-permute-start | bytes 1179656 | tf_op jit(solution)/shard_map/ppermute | solution.py:107
  133.8 7.6 %collective-permute-start.29 = (bf16[1536,128]{1,0:T(8,128)(2,1)S(1)}, bf16[1536,128]{1,0:T(8,128)(2,1)S(1)}, u32[]{:S(2)}, u32[]{:S(2)}) collective-permute-start(bf16[1536,128]{1,0:T(8,128)(2,1)S(1)} %add_convert_fusion.20), channel_id=1, source_target_pairs={{8,16},{16,8},{9,17},{17,9},{10,18},{18,10},{11,19},{19,11},{12,20... | collective-permute-start | bytes 1179656 | tf_op jit(solution)/shard_map/ppermute | solution.py:115
  138.1 15.5 %collective-permute-start.27 = (bf16[1536,128]{1,0:T(8,128)(2,1)S(1)}, bf16[1536,128]{1,0:T(8,128)(2,1)S(1)}, u32[]{:S(2)}, u32[]{:S(2)}) collective-permute-start(bf16[1536,128]{1,0:T(8,128)(2,1)S(1)} %fusion.72), channel_id=1, source_target_pairs={{0,8},{24,16},{8,0},{16,24},{1,9},{25,17},{9,1},{17,25},{2,10},{26... | collective-permute-start | bytes 1179656 | tf_op jit(solution)/shard_map/ppermute | solution.py:107
  140.5 14.0 %collective-permute-start.32 = (bf16[1536,128]{1,0:T(8,128)(2,1)S(1)}, bf16[1536,128]{1,0:T(8,128)(2,1)S(1)}, u32[]{:S(2)}, u32[]{:S(2)}) collective-permute-start(bf16[1536,128]{1,0:T(8,128)(2,1)S(1)} %add_convert_fusion.18), channel_id=1, source_target_pairs={{8,16},{16,8},{9,17},{17,9},{10,18},{18,10},{11,19},{19,11},{12,20... | collective-permute-start | bytes 1179656 | tf_op jit(solution)/shard_map/ppermute | solution.py:115
  143.8 16.3 %collective-permute-start.31 = (bf16[1536,128]{1,0:T(8,128)(2,1)S(1)}, bf16[1536,128]{1,0:T(8,128)(2,1)S(1)}, u32[]{:S(2)}, u32[]{:S(2)}) collective-permute-start(bf16[1536,128]{1,0:T(8,128)(2,1)S(1)} %fusion.73), channel_id=1, source_target_pairs={{0,8},{24,16},{8,0},{16,24},{1,9},{25,17},{9,1},{17,25},{2,10},{26... | collective-permute-start | bytes 1179656 | tf_op jit(solution)/shard_map/ppermute | solution.py:107
  153.7 7.2 %collective-permute-start.30 = (bf16[1536,128]{1,0:T(8,128)(2,1)S(1)}, bf16[1536,128]{1,0:T(8,128)(2,1)S(1)}, u32[]{:S(2)}, u32[]{:S(2)}) collective-permute-start(bf16[1536,128]{1,0:T(8,128)(2,1)S(1)} %add_convert_fusion.16), channel_id=1, source_target_pairs={{8,16},{16,8},{9,17},{17,9},{10,18},{18,10},{11,19},{19,11},{12,20... | collective-permute-start | bytes 1179656 | tf_op jit(solution)/shard_map/ppermute | solution.py:115
  154.6 13.9 %collective-permute-start.33 = (bf16[1536,128]{1,0:T(8,128)(2,1)S(1)}, bf16[1536,128]{1,0:T(8,128)(2,1)S(1)}, u32[]{:S(2)}, u32[]{:S(2)}) collective-permute-start(bf16[1536,128]{1,0:T(8,128)(2,1)S(1)} %fusion.74), channel_id=1, source_target_pairs={{0,8},{24,16},{8,0},{16,24},{1,9},{25,17},{9,1},{17,25},{2,10},{26... | collective-permute-start | bytes 1179656 | tf_op jit(solution)/shard_map/ppermute | solution.py:107
  160.2 9.1 %collective-permute-start.36 = (bf16[1536,128]{1,0:T(8,128)(2,1)S(1)}, bf16[1536,128]{1,0:T(8,128)(2,1)S(1)}, u32[]{:S(2)}, u32[]{:S(2)}) collective-permute-start(bf16[1536,128]{1,0:T(8,128)(2,1)S(1)} %add_convert_fusion.14), channel_id=1, source_target_pairs={{8,16},{16,8},{9,17},{17,9},{10,18},{18,10},{11,19},{19,11},{12,20... | collective-permute-start | bytes 1179656 | tf_op jit(solution)/shard_map/ppermute | solution.py:115
  161.1 17.1 %collective-permute-start.35 = (bf16[1536,128]{1,0:T(8,128)(2,1)S(1)}, bf16[1536,128]{1,0:T(8,128)(2,1)S(1)}, u32[]{:S(2)}, u32[]{:S(2)}) collective-permute-start(bf16[1536,128]{1,0:T(8,128)(2,1)S(1)} %fusion.75), channel_id=1, source_target_pairs={{0,8},{24,16},{8,0},{16,24},{1,9},{25,17},{9,1},{17,25},{2,10},{26... | collective-permute-start | bytes 1179656 | tf_op jit(solution)/shard_map/ppermute | solution.py:107
  168.6 10.4 %collective-permute-start.34 = (bf16[1536,128]{1,0:T(8,128)(2,1)S(1)}, bf16[1536,128]{1,0:T(8,128)(2,1)S(1)}, u32[]{:S(2)}, u32[]{:S(2)}) collective-permute-start(bf16[1536,128]{1,0:T(8,128)(2,1)S(1)} %add_convert_fusion.12), channel_id=1, source_target_pairs={{8,16},{16,8},{9,17},{17,9},{10,18},{18,10},{11,19},{19,11},{12,20... | collective-permute-start | bytes 1179656 | tf_op jit(solution)/shard_map/ppermute | solution.py:115
  169.5 16.5 %collective-permute-start.38 = (bf16[1536,128]{1,0:T(8,128)(2,1)S(1)}, bf16[1536,128]{1,0:T(8,128)(2,1)S(1)}, u32[]{:S(2)}, u32[]{:S(2)}) collective-permute-start(bf16[1536,128]{1,0:T(8,128)(2,1)S(1)} %fusion.76), channel_id=1, source_target_pairs={{0,8},{24,16},{8,0},{16,24},{1,9},{25,17},{9,1},{17,25},{2,10},{26... | collective-permute-start | bytes 1179656 | tf_op jit(solution)/shard_map/ppermute | solution.py:107
  178.3 10.1 %collective-permute-start.37 = (bf16[1536,128]{1,0:T(8,128)(2,1)S(1)}, bf16[1536,128]{1,0:T(8,128)(2,1)S(1)}, u32[]{:S(2)}, u32[]{:S(2)}) collective-permute-start(bf16[1536,128]{1,0:T(8,128)(2,1)S(1)} %add_convert_fusion.10), channel_id=1, source_target_pairs={{8,16},{16,8},{9,17},{17,9},{10,18},{18,10},{11,19},{19,11},{12,20... | collective-permute-start | bytes 1179656 | tf_op jit(solution)/shard_map/ppermute | solution.py:115
  179.1 15.2 %collective-permute-start.40 = (bf16[1536,128]{1,0:T(8,128)(2,1)S(1)}, bf16[1536,128]{1,0:T(8,128)(2,1)S(1)}, u32[]{:S(2)}, u32[]{:S(2)}) collective-permute-start(bf16[1536,128]{1,0:T(8,128)(2,1)S(1)} %fusion.77), channel_id=1, source_target_pairs={{0,8},{24,16},{8,0},{16,24},{1,9},{25,17},{9,1},{17,25},{2,10},{26... | collective-permute-start | bytes 1179656 | tf_op jit(solution)/shard_map/ppermute | solution.py:107
  187.5 7.6 %collective-permute-start.41 = (bf16[1536,128]{1,0:T(8,128)(2,1)S(1)}, bf16[1536,128]{1,0:T(8,128)(2,1)S(1)}, u32[]{:S(2)}, u32[]{:S(2)}) collective-permute-start(bf16[1536,128]{1,0:T(8,128)(2,1)S(1)} %add_convert_fusion.8), channel_id=1, source_target_pairs={{8,16},{16,8},{9,17},{17,9},{10,18},{18,10},{11,19},{19,11},{12,20... | collective-permute-start | bytes 1179656 | tf_op jit(solution)/shard_map/ppermute | solution.py:115
  188.6 15.1 %collective-permute-start.39 = (bf16[1536,128]{1,0:T(8,128)(2,1)S(1)}, bf16[1536,128]{1,0:T(8,128)(2,1)S(1)}, u32[]{:S(2)}, u32[]{:S(2)}) collective-permute-start(bf16[1536,128]{1,0:T(8,128)(2,1)S(1)} %fusion.78), channel_id=1, source_target_pairs={{0,8},{24,16},{8,0},{16,24},{1,9},{25,17},{9,1},{17,25},{2,10},{26... | collective-permute-start | bytes 1179656 | tf_op jit(solution)/shard_map/ppermute | solution.py:107
  194.5 10.0 %collective-permute-start.44 = (bf16[1536,128]{1,0:T(8,128)(2,1)S(1)}, bf16[1536,128]{1,0:T(8,128)(2,1)S(1)}, u32[]{:S(2)}, u32[]{:S(2)}) collective-permute-start(bf16[1536,128]{1,0:T(8,128)(2,1)S(1)} %add_convert_fusion.6), channel_id=1, source_target_pairs={{8,16},{16,8},{9,17},{17,9},{10,18},{18,10},{11,19},{19,11},{12,20... | collective-permute-start | bytes 1179656 | tf_op jit(solution)/shard_map/ppermute | solution.py:115
  195.3 14.2 %collective-permute-start.43 = (bf16[1536,128]{1,0:T(8,128)(2,1)S(1)}, bf16[1536,128]{1,0:T(8,128)(2,1)S(1)}, u32[]{:S(2)}, u32[]{:S(2)}) collective-permute-start(bf16[1536,128]{1,0:T(8,128)(2,1)S(1)} %fusion.79), channel_id=1, source_target_pairs={{0,8},{24,16},{8,0},{16,24},{1,9},{25,17},{9,1},{17,25},{2,10},{26... | collective-permute-start | bytes 1179656 | tf_op jit(solution)/shard_map/ppermute | solution.py:107
  203.8 9.3 %collective-permute-start.42 = (bf16[1536,128]{1,0:T(8,128)(2,1)S(1)}, bf16[1536,128]{1,0:T(8,128)(2,1)S(1)}, u32[]{:S(2)}, u32[]{:S(2)}) collective-permute-start(bf16[1536,128]{1,0:T(8,128)(2,1)S(1)} %add_convert_fusion.4), channel_id=1, source_target_pairs={{8,16},{16,8},{9,17},{17,9},{10,18},{18,10},{11,19},{19,11},{12,20... | collective-permute-start | bytes 1179656 | tf_op jit(solution)/shard_map/ppermute | solution.py:115
  204.6 13.8 %collective-permute-start.48 = (bf16[1536,128]{1,0:T(8,128)(2,1)S(1)}, bf16[1536,128]{1,0:T(8,128)(2,1)S(1)}, u32[]{:S(2)}, u32[]{:S(2)}) collective-permute-start(bf16[1536,128]{1,0:T(8,128)(2,1)S(1)} %add_convert_fusion.3), channel_id=1, source_target_pairs={{8,0},{16,24},{9,1},{17,25},{10,2},{18,26},{11,3},{19,27},{12,4},{... | collective-permute-start | bytes 1179656 | tf_op jit(solution)/shard_map/ppermute | solution.py:107
  209.7 8.7 %collective-permute-start.45 = (bf16[1536,128]{1,0:T(8,128)(2,1)S(1)}, bf16[1536,128]{1,0:T(8,128)(2,1)S(1)}, u32[]{:S(2)}, u32[]{:S(2)}) collective-permute-start(bf16[1536,128]{1,0:T(8,128)(2,1)S(1)} %add_convert_fusion.2), channel_id=1, source_target_pairs={{8,16},{16,8},{9,17},{17,9},{10,18},{18,10},{11,19},{19,11},{12,20... | collective-permute-start | bytes 1179656 | tf_op jit(solution)/shard_map/ppermute | solution.py:115
  213.2 12.9 %collective-permute-start.47 = (bf16[1536,128]{1,0:T(8,128)(2,1)S(1)}, bf16[1536,128]{1,0:T(8,128)(2,1)S(1)}, u32[]{:S(2)}, u32[]{:S(2)}) collective-permute-start(bf16[1536,128]{1,0:T(8,128)(2,1)S(1)} %add_convert_fusion), channel_id=1, source_target_pairs={{8,0},{16,24},{9,1},{17,25},{10,2},{18,26},{11,3},{19,27},{12,4},{... | collective-permute-start | bytes 1179656 | tf_op jit(solution)/shard_map/ppermute | solution.py:107
  218.5 11.9 %collective-permute-start.46 = (bf16[1536,128]{1,0:T(8,128)(2,1)S(1)}, bf16[1536,128]{1,0:T(8,128)(2,1)S(1)}, u32[]{:S(2)}, u32[]{:S(2)}) collective-permute-start(bf16[1536,128]{1,0:T(8,128)(2,1)S(1)} %add_convert_fusion.1), channel_id=1, source_target_pairs={{8,0},{16,24},{9,1},{17,25},{10,2},{18,26},{11,3},{19,27},{12,4},{... | collective-permute-start | bytes 1179656 | tf_op jit(solution)/shard_map/ppermute | solution.py:107
  (18 other events, 190.3 us)

commit v20 on v18

--- a/solution.py
+++ b/solution.py
@@ -224,8 +224,8 @@
         elif c == 2:
             d_local, crosses[0] = together(d_local, crosses[0])
         locals_.append(d_local)
+        crosses.append(lax.ppermute(d_local, ("fsdp", "tp"), cross_pairs))
         rings.append(lax.ppermute(d_local, ("fsdp", "tp"), ring_pairs))
-        crosses.append(lax.ppermute(d_local, ("fsdp", "tp"), cross_pairs))
 
     def gathered(c):
         d_near = jnp.where(near, locals_[c], rings[c])

time: 233 us -> 233 us (level)
  no operation moved by 1% of the time
where the time goes in v20:
time: 233 us; the launch traced here: 231 us
  starting transfers between devices  98.3 us (42%)
  waiting for transfers between devices  73.4 us (32%)
  matrix products  24.4 us (10%)
  other arithmetic  13.2 us (6%)
  Pallas kernels  11.1 us (5%)
  local copies, waits for them, and re-layouts  8.57 us (4%)
    ppermute x15, starting transfers between devices, send_outer(): self.edge[s] = lax.ppermute(payload, 'island', pairs)  63.5 us
    ppermute x11, waiting for transfers between devices, swap(): return lax.ppermute(value, axis, [(i, i ^ bit) for i in range(count)])  33.4 us
    ppermute x15, waiting for transfers between devices, send_outer(): self.edge[s] = lax.ppermute(payload, 'island', pairs)  27.5 us
    dot_general x7, matrix products, add_pseudo(): lax.dot_general(context_all, piece, (((0,), (0,)), ((), ())), preferred_e...  15 us
    pallas_call x5, Pallas kernels, finish(): pl.pallas_call(functools.partial(finish_kernel, count, start, narrow, isl...  11.1 us
    ppermute x3, starting transfers between devices, move(): crosses.append(lax.ppermute(d_local, ('fsdp', 'tp'), cross_pairs))  10.1 us
    dot_general x3, matrix products, project(): jnp.dot(block, weight, preferred_element_type=f32).astype(bf16)  9.49 us
    ppermute x12, starting transfers between devices, step(): self.mid[s] = lax.ppermute(self.sums[s], 'island', [(1, 2), (2, 1)])  8.58 us
  transfers between devices with their start and end apart: 49, of which 23 were waited for; matrix products, arithmetic and copies ran while one was open for 19% of the time, Pallas kernels for 4%

profile of v20, /device:TPU:2, one launch (start us, length us, event | category | flops | bytes accessed | tf_op | source)
XLA Modules:
  0.0 230.9 jit_solution(14655454954735595726)
XLA Ops:
  5.0 15.3 %collective-permute-done = bf16[256,1536]{1,0:T(8,128)(2,1)} collective-permute-done((bf16[256,1536]{1,0:T(8,128)(2,1)}, bf16[256,1536]{1,0:T(8,128)(2,1)}, u32[]{:S(2)}, u32[]{:S(2)}) %collective-permute-start) | collective-permute-done | bytes 786464 | tf_op jit(solution)/shard_map/ppermute | solution.py:31
  20.4 4.0 %convolution_convert_fusion.2 = bf16[256,1536]{1,0:T(8,128)(2,1)S(1)} fusion(bf16[256,1536]{1,0:T(8,128)(2,1)} %collective-permute-done, bf16[1536,1536]{1,0:T(8,128)(2,1)} %param.12), kind=kOutput, calls=%fused_computation.8 | convolution fusion | flops 1208352768 | bytes 6291456 | tf_op jit(solution)/shard_map/dot_general | solution.py:144
  26.7 4.1 %convolution_convert_fusion = bf16[512,1536]{1,0:T(8,128)(2,1)} fusion(bf16[1536,1536]{1,0:T(8,128)(2,1)S(1)} %bitcast.206, bf16[256,1536]{1,0:T(8,128)(2,1)S(1)} %collective-permute-done.5, bf16[256,1536]{1,0:T(8,128)(2,1)S(1)} %copy-done.1), kind=kOutput, calls=%fused_computation | convolution fusion | flops 2419851264 | bytes 7864320 | tf_op jit(solution)/shard_map/dot_general | solution.py:144
  30.8 3.6 %collective-permute-start.7 = (bf16[512,1536]{1,0:T(8,128)(2,1)}, bf16[512,1536]{1,0:T(8,128)(2,1)}, u32[]{:S(2)}, u32[]{:S(2)}) collective-permute-start(bf16[512,1536]{1,0:T(8,128)(2,1)} %convolution_convert_fusion), channel_id=1, source_target_pairs={{4,5},{1,0},{6,7},{3,2},{12,13},{9,8},{14,15},{11,10},{20,21},{17,... | collective-permute-start | bytes 4718600 | tf_op jit(solution)/shard_map/ppermute | solution.py:168
  34.4 2.3 %collective-permute-done.6 = bf16[128,1536]{1,0:T(8,128)(2,1)} collective-permute-done((bf16[128,1536]{1,0:T(8,128)(2,1)S(1)}, bf16[128,1536]{1,0:T(8,128)(2,1)}, u32[]{:S(2)}, u32[]{:S(2)}) %collective-permute-start.6) | collective-permute-done | bytes 393248 | tf_op jit(solution)/shard_map/ppermute | solution.py:31
  40.4 3.4 %collective-permute-start.10 = (bf16[128,1536]{1,0:T(8,128)(2,1)}, bf16[128,1536]{1,0:T(8,128)(2,1)}, u32[]{:S(2)}, u32[]{:S(2)}) collective-permute-start(bf16[128,1536]{1,0:T(8,128)(2,1)} %get-tuple-element.332), channel_id=1, source_target_pairs={{0,4},{2,6},{4,0},{6,2},{1,5},{3,7},{5,1},{7,3},{8,12},{10,14},{12... | collective-permute-start | bytes 1179656 | tf_op jit(solution)/shard_map/ppermute | solution.py:31
  45.5 2.1 constant_dynamic-update-slice_fusion.2
  48.9 6.3 %collective-permute-done.10 = bf16[128,1536]{1,0:T(8,128)(2,1)} collective-permute-done((bf16[128,1536]{1,0:T(8,128)(2,1)}, bf16[128,1536]{1,0:T(8,128)(2,1)}, u32[]{:S(2)}, u32[]{:S(2)}) %collective-permute-start.10) | collective-permute-done | bytes 393248 | tf_op jit(solution)/shard_map/ppermute | solution.py:31
  56.5 6.0 %collective-permute-done.12 = bf16[128,1536]{1,0:T(8,128)(2,1)S(1)} collective-permute-done((bf16[128,1536]{1,0:T(8,128)(2,1)}, bf16[128,1536]{1,0:T(8,128)(2,1)S(1)}, u32[]{:S(2)}, u32[]{:S(2)}) %collective-permute-start.12) | collective-permute-done | bytes 393248 | tf_op jit(solution)/shard_map/ppermute | solution.py:31
  63.7 3.9 %collective-permute-done.7 = bf16[512,1536]{1,0:T(8,128)(2,1)} collective-permute-done((bf16[512,1536]{1,0:T(8,128)(2,1)}, bf16[512,1536]{1,0:T(8,128)(2,1)}, u32[]{:S(2)}, u32[]{:S(2)}) %collective-permute-start.7) | collective-permute-done | bytes 1572896 | tf_op jit(solution)/shard_map/ppermute | solution.py:168
  67.6 1.8 multiply_reduce_fusion.7
  69.4 1.8 multiply_reduce_fusion.5
  71.2 1.7 multiply_reduce_fusion.3
  73.0 3.7 %collective-permute-done.13 = bf16[128,1536]{1,0:T(8,128)(2,1)S(1)} collective-permute-done((bf16[128,1536]{1,0:T(8,128)(2,1)S(1)}, bf16[128,1536]{1,0:T(8,128)(2,1)S(1)}, u32[]{:S(2)}, u32[]{:S(2)}) %collective-permute-start.13) | collective-permute-done | bytes 393248 | tf_op jit(solution)/shard_map/ppermute | solution.py:173
  76.7 1.6 multiply_reduce_fusion.1
  80.0 3.5 %collective-permute-done.15 = f32[2,512]{1,0:T(2,128)S(1)} collective-permute-done((f32[2,512]{1,0:T(2,128)S(1)}, f32[2,512]{1,0:T(2,128)S(1)}, u32[]{:S(2)}, u32[]{:S(2)}) %collective-permute-start.15) | collective-permute-done | bytes 4128 | tf_op jit(solution)/shard_map/ppermute | solution.py:31
  83.9 3.4 %collective-permute-start.16 = (bf16[512,128]{1,0:T(8,128)(2,1)S(1)}, bf16[512,128]{1,0:T(8,128)(2,1)S(1)}, u32[]{:S(2)}, u32[]{:S(2)}) collective-permute-start(bf16[512,128]{1,0:T(8,128)(2,1)S(1)} %pad_maximum_fusion.5), channel_id=1, source_target_pairs={{4,1},{1,4},{6,3},{3,6},{12,9},{9,12},{14,11},{11,14},{20,17},{17,... | collective-permute-start | bytes 393224 | tf_op jit(solution)/shard_map/ppermute | solution.py:227
  88.9 3.3 %collective-permute-start.21 = (bf16[512,384]{1,0:T(8,128)(2,1)S(1)}, bf16[512,384]{1,0:T(8,128)(2,1)S(1)}, u32[]{:S(2)}, u32[]{:S(2)}) collective-permute-start(bf16[512,384]{1,0:T(8,128)(2,1)S(1)} %pad_maximum_fusion.2), channel_id=1, source_target_pairs={{4,1},{1,4},{6,3},{3,6},{12,9},{9,12},{14,11},{11,14},{20,17},{17,... | collective-permute-start | bytes 1179656 | tf_op jit(solution)/shard_map/ppermute | solution.py:227
  92.3 3.4 %collective-permute-start.18 = (bf16[512,1024]{1,0:T(8,128)(2,1)S(1)}, bf16[512,1024]{1,0:T(8,128)(2,1)S(1)}, u32[]{:S(2)}, u32[]{:S(2)}) collective-permute-start(bf16[512,1024]{1,0:T(8,128)(2,1)S(1)} %pad_maximum_fusion), channel_id=1, source_target_pairs={{4,1},{1,4},{6,3},{3,6},{12,9},{9,12},{14,11},{11,14},{20,17},{17,... | collective-permute-start | bytes 3145736 | tf_op jit(solution)/shard_map/ppermute | solution.py:227
  95.9 2.6 %fusion.51 = bf16[1536,128]{1,0:T(8,128)(2,1)S(1)} fusion(bf16[1536,1536]{1,0:T(8,128)(2,1)S(1)} %bitcast.208, bf16[1,1536,1536]{2,1,0:T(8,128)(2,1)S(1)} %bitcast.210, bf16[1,1536,1536]{2,1,0:T(8,128)(2,1)} %param.13, bf16[1024,1536]{1,0:T(8,128)(2,1)S(1)} %constant_dynamic-update-slice_fusion, bf16[1024,128]{1,0:T(8,128)(2,1)S(1)} %pad_maximum_fusion.4), kind=kOutput, calls=%fused_computation.119 | convolution fusion | flops 406192128 | bytes 4980736 | tf_op jit(solution)/shard_map/dot_general | solution.py:243
  98.5 3.7 %collective-permute-start.22 = (bf16[1536,128]{1,0:T(8,128)(2,1)S(1)}, bf16[1536,128]{1,0:T(8,128)(2,1)S(1)}, u32[]{:S(2)}, u32[]{:S(2)}) collective-permute-start(bf16[1536,128]{1,0:T(8,128)(2,1)S(1)} %fusion.51), channel_id=1, source_target_pairs={{0,8},{24,16},{1,9},{25,17},{2,10},{26,18},{3,11},{27,19},{4,12},{... | collective-permute-start | bytes 1179656 | tf_op jit(solution)/shard_map/ppermute | solution.py:107
  105.9 2.2 fusion.33
  108.2 3.5 %collective-permute-start.23 = (bf16[1536,128]{1,0:T(8,128)(2,1)S(1)}, bf16[1536,128]{1,0:T(8,128)(2,1)S(1)}, u32[]{:S(2)}, u32[]{:S(2)}) collective-permute-start(bf16[1536,128]{1,0:T(8,128)(2,1)S(1)} %fusion.50), channel_id=1, source_target_pairs={{0,8},{24,16},{1,9},{25,17},{2,10},{26,18},{3,11},{27,19},{4,12},{... | collective-permute-start | bytes 1179656 | tf_op jit(solution)/shard_map/ppermute | solution.py:107
  112.5 6.1 %collective-permute-start.25 = (bf16[1536,128]{1,0:T(8,128)(2,1)S(1)}, bf16[1536,128]{1,0:T(8,128)(2,1)S(1)}, u32[]{:S(2)}, u32[]{:S(2)}) collective-permute-start(bf16[1536,128]{1,0:T(8,128)(2,1)S(1)} %slice.458), channel_id=1, source_target_pairs={{0,8},{24,16},{1,9},{25,17},{2,10},{26,18},{3,11},{27,19},{4,12},{... | collective-permute-start | bytes 1179656 | tf_op jit(solution)/shard_map/ppermute | solution.py:107
  118.6 2.2 collective-permute-done.23
  121.7 1.8 collective-permute-done.18
  124.2 2.2 fusion.34
  126.5 3.3 %collective-permute-start.28 = (bf16[1536,128]{1,0:T(8,128)(2,1)S(1)}, bf16[1536,128]{1,0:T(8,128)(2,1)S(1)}, u32[]{:S(2)}, u32[]{:S(2)}) collective-permute-start(bf16[1536,128]{1,0:T(8,128)(2,1)S(1)} %fusion.64), channel_id=1, source_target_pairs={{0,8},{24,16},{8,0},{16,24},{1,9},{25,17},{9,1},{17,25},{2,10},{26... | collective-permute-start | bytes 1179656 | tf_op jit(solution)/shard_map/ppermute | solution.py:107
  130.7 2.2 fusion.35
  133.0 4.4 %collective-permute-start.30 = (bf16[1536,128]{1,0:T(8,128)(2,1)S(1)}, bf16[1536,128]{1,0:T(8,128)(2,1)S(1)}, u32[]{:S(2)}, u32[]{:S(2)}) collective-permute-start(bf16[1536,128]{1,0:T(8,128)(2,1)S(1)} %fusion.65), channel_id=1, source_target_pairs={{0,8},{24,16},{8,0},{16,24},{1,9},{25,17},{9,1},{17,25},{2,10},{26... | collective-permute-start | bytes 1179656 | tf_op jit(solution)/shard_map/ppermute | solution.py:107
  138.8 5.3 %collective-permute-start.29 = (bf16[1536,128]{1,0:T(8,128)(2,1)S(1)}, bf16[1536,128]{1,0:T(8,128)(2,1)S(1)}, u32[]{:S(2)}, u32[]{:S(2)}) collective-permute-start(bf16[1536,128]{1,0:T(8,128)(2,1)S(1)} %fusion.66), channel_id=1, source_target_pairs={{0,8},{24,16},{8,0},{16,24},{1,9},{25,17},{9,1},{17,25},{2,10},{26... | collective-permute-start | bytes 1179656 | tf_op jit(solution)/shard_map/ppermute | solution.py:107
  144.2 3.3 %collective-permute-done.30 = bf16[1536,128]{1,0:T(8,128)(2,1)S(1)} collective-permute-done((bf16[1536,128]{1,0:T(8,128)(2,1)S(1)}, bf16[1536,128]{1,0:T(8,128)(2,1)S(1)}, u32[]{:S(2)}, u32[]{:S(2)}) %collective-permute-start.30) | collective-permute-done | bytes 393248 | tf_op jit(solution)/shard_map/ppermute | solution.py:107
  148.7 4.1 %collective-permute-start.33 = (bf16[1536,128]{1,0:T(8,128)(2,1)S(1)}, bf16[1536,128]{1,0:T(8,128)(2,1)S(1)}, u32[]{:S(2)}, u32[]{:S(2)}) collective-permute-start(bf16[1536,128]{1,0:T(8,128)(2,1)S(1)} %fusion.67), channel_id=1, source_target_pairs={{0,8},{24,16},{8,0},{16,24},{1,9},{25,17},{9,1},{17,25},{2,10},{26... | collective-permute-start | bytes 1179656 | tf_op jit(solution)/shard_map/ppermute | solution.py:107
  152.8 3.1 %collective-permute-done.29 = bf16[1536,128]{1,0:T(8,128)(2,1)S(1)} collective-permute-done((bf16[1536,128]{1,0:T(8,128)(2,1)S(1)}, bf16[1536,128]{1,0:T(8,128)(2,1)S(1)}, u32[]{:S(2)}, u32[]{:S(2)}) %collective-permute-start.29) | collective-permute-done | bytes 393248 | tf_op jit(solution)/shard_map/ppermute | solution.py:107
  156.0 2.2 fusion.37
  159.2 3.6 %collective-permute-start.36 = (bf16[1536,128]{1,0:T(8,128)(2,1)S(1)}, bf16[1536,128]{1,0:T(8,128)(2,1)S(1)}, u32[]{:S(2)}, u32[]{:S(2)}) collective-permute-start(bf16[1536,128]{1,0:T(8,128)(2,1)S(1)} %fusion.68), channel_id=1, source_target_pairs={{0,8},{24,16},{8,0},{16,24},{1,9},{25,17},{9,1},{17,25},{2,10},{26... | collective-permute-start | bytes 1179656 | tf_op jit(solution)/shard_map/ppermute | solution.py:107
  165.0 7.8 %collective-permute-start.38 = (bf16[1536,128]{1,0:T(8,128)(2,1)S(1)}, bf16[1536,128]{1,0:T(8,128)(2,1)S(1)}, u32[]{:S(2)}, u32[]{:S(2)}) collective-permute-start(bf16[1536,128]{1,0:T(8,128)(2,1)S(1)} %fusion.69), channel_id=1, source_target_pairs={{0,8},{24,16},{8,0},{16,24},{1,9},{25,17},{9,1},{17,25},{2,10},{26... | collective-permute-start | bytes 1179656 | tf_op jit(solution)/shard_map/ppermute | solution.py:107
  172.8 2.2 fusion.36
  176.2 4.8 %collective-permute-start.40 = (bf16[1536,128]{1,0:T(8,128)(2,1)S(1)}, bf16[1536,128]{1,0:T(8,128)(2,1)S(1)}, u32[]{:S(2)}, u32[]{:S(2)}) collective-permute-start(bf16[1536,128]{1,0:T(8,128)(2,1)S(1)} %fusion.70), channel_id=1, source_target_pairs={{0,8},{24,16},{8,0},{16,24},{1,9},{25,17},{9,1},{17,25},{2,10},{26... | collective-permute-start | bytes 1179656 | tf_op jit(solution)/shard_map/ppermute | solution.py:107
  183.0 6.5 %collective-permute-start.39 = (bf16[1536,128]{1,0:T(8,128)(2,1)S(1)}, bf16[1536,128]{1,0:T(8,128)(2,1)S(1)}, u32[]{:S(2)}, u32[]{:S(2)}) collective-permute-start(bf16[1536,128]{1,0:T(8,128)(2,1)S(1)} %fusion.71), channel_id=1, source_target_pairs={{0,8},{24,16},{8,0},{16,24},{1,9},{25,17},{9,1},{17,25},{2,10},{26... | collective-permute-start | bytes 1179656 | tf_op jit(solution)/shard_map/ppermute | solution.py:107
  191.8 6.5 %collective-permute-start.43 = (bf16[1536,128]{1,0:T(8,128)(2,1)S(1)}, bf16[1536,128]{1,0:T(8,128)(2,1)S(1)}, u32[]{:S(2)}, u32[]{:S(2)}) collective-permute-start(bf16[1536,128]{1,0:T(8,128)(2,1)S(1)} %fusion.72), channel_id=1, source_target_pairs={{0,8},{24,16},{8,0},{16,24},{1,9},{25,17},{9,1},{17,25},{2,10},{26... | collective-permute-start | bytes 1179656 | tf_op jit(solution)/shard_map/ppermute | solution.py:107
  201.4 6.7 %collective-permute-done.43 = bf16[1536,128]{1,0:T(8,128)(2,1)S(1)} collective-permute-done((bf16[1536,128]{1,0:T(8,128)(2,1)S(1)}, bf16[1536,128]{1,0:T(8,128)(2,1)S(1)}, u32[]{:S(2)}, u32[]{:S(2)}) %collective-permute-start.43) | collective-permute-done | bytes 393248 | tf_op jit(solution)/shard_map/ppermute | solution.py:107
  208.9 2.6 %shard_map.95 = (f32[1536,1536]{1,0:T(8,128)}, bf16[1536,1536]{1,0:T(8,128)(2,1)}) custom-call(bf16[1536,128]{1,0:T(8,128)(2,1)S(1)} %broadcast_select_fusion.15.refs_0_, bf16[1536,128]{1,0:T(8,128)(2,1)S(1)} %broadcast_select_fusion.5.refs_1_, bf16[1536,128]{1,0:T(8,128)(2,1)S(1)} %broadcast_select_fusion.4.refs_2_, f32[1536,1536]{1,0:T(8,128)S(1)} %bitcast.192), custom_call_target="tpu_custom_call" | custom-call | flops 2949120 | bytes 7077888 | tf_op jit(solution)/shard_map/pallas_call | solution.py:61
  213.0 2.6 %shard_map.96 = (f32[1536,1536]{1,0:T(8,128)}, bf16[1536,1536]{1,0:T(8,128)(2,1)}) custom-call(bf16[1536,128]{1,0:T(8,128)(2,1)S(1)} %broadcast_select_fusion.13.refs_0_, bf16[1536,128]{1,0:T(8,128)(2,1)S(1)} %broadcast_select_fusion.7.refs_1_, bf16[1536,128]{1,0:T(8,128)(2,1)S(1)} %broadcast_select_fusion.6.refs_2_, ...), custom_call_target="tpu_custom_call", output_to_operand_aliasing={{0}: (4, {}), {1}: (5, {})} | custom-call | flops 2949120 | bytes 7077888 | tf_op jit(solution)/shard_map/pallas_call | solution.py:61
  217.1 2.6 %shard_map.97 = (f32[1536,1536]{1,0:T(8,128)}, bf16[1536,1536]{1,0:T(8,128)(2,1)}) custom-call(bf16[1536,128]{1,0:T(8,128)(2,1)S(1)} %broadcast_select_fusion.14.refs_0_, bf16[1536,128]{1,0:T(8,128)(2,1)S(1)} %broadcast_select_fusion.9.refs_1_, bf16[1536,128]{1,0:T(8,128)(2,1)S(1)} %broadcast_select_fusion.8.refs_2_, ...), custom_call_target="tpu_custom_call", output_to_operand_aliasing={{0}: (4, {}), {1}: (5, {})} | custom-call | flops 2949120 | bytes 7077888 | tf_op jit(solution)/shard_map/pallas_call | solution.py:61
  219.8 5.3 %collective-permute-done.47 = bf16[1536,128]{1,0:T(8,128)(2,1)S(1)} collective-permute-done((bf16[1536,128]{1,0:T(8,128)(2,1)S(1)}, bf16[1536,128]{1,0:T(8,128)(2,1)S(1)}, u32[]{:S(2)}, u32[]{:S(2)}) %collective-permute-start.47) | collective-permute-done | bytes 393248 | tf_op jit(solution)/shard_map/ppermute | solution.py:107
  225.2 1.9 shard_map.98
  227.1 2.2 collective-permute-done.46
  (181 shorter events, 46.2 us)
Async XLA Ops:
  0.6 19.7 %collective-permute-start = (bf16[256,1536]{1,0:T(8,128)(2,1)}, bf16[256,1536]{1,0:T(8,128)(2,1)}, u32[]{:S(2)}, u32[]{:S(2)}) collective-permute-start(bf16[256,1536]{1,0:T(8,128)(2,1)} %param.8), channel_id=1, source_target_pairs={{0,4},{2,6},{4,0},{6,2},{1,5},{3,7},{5,1},{7,3},{8,12},{10,14},{12... | collective-permute-start | bytes 2359304 | tf_op jit(solution)/shard_map/ppermute | solution.py:31
  3.8 16.5 %collective-permute-start.1 = (bf16[256,1536]{1,0:T(8,128)(2,1)S(1)}, bf16[256,1536]{1,0:T(8,128)(2,1)S(1)}, u32[]{:S(2)}, u32[]{:S(2)}) collective-permute-start(bf16[256,1536]{1,0:T(8,128)(2,1)S(1)} %get-tuple-element.322), channel_id=1, source_target_pairs={{0,2},{2,0},{4,6},{6,4},{1,3},{3,1},{5,7},{7,5},{8,10},{10,8},{12,... | collective-permute-start | bytes 2359304 | tf_op jit(solution)/shard_map/ppermute | solution.py:31
  4.2 16.1 %collective-permute-start.2 = (bf16[256,1536]{1,0:T(8,128)(2,1)S(1)}, bf16[256,1536]{1,0:T(8,128)(2,1)S(1)}, u32[]{:S(2)}, u32[]{:S(2)}) collective-permute-start(bf16[256,1536]{1,0:T(8,128)(2,1)S(1)} %get-tuple-element.320), channel_id=1, source_target_pairs={{0,2},{2,0},{4,6},{6,4},{1,3},{3,1},{5,7},{7,5},{8,10},{10,8},{12,... | collective-permute-start | bytes 2359304 | tf_op jit(solution)/shard_map/ppermute | solution.py:31
  5.0 21.7 %collective-permute-start.5 = (bf16[256,1536]{1,0:T(8,128)(2,1)S(1)}, bf16[256,1536]{1,0:T(8,128)(2,1)S(1)}, u32[]{:S(2)}, u32[]{:S(2)}) collective-permute-start(bf16[256,1536]{1,0:T(8,128)(2,1)S(1)} %copy-done.1), channel_id=1, source_target_pairs={{0,2},{2,0},{4,6},{6,4},{1,3},{3,1},{5,7},{7,5},{8,10},{10,8},{12,... | collective-permute-start | bytes 2359304 | tf_op jit(solution)/shard_map/ppermute | solution.py:31
  20.3 17.8 %collective-permute-start.9 = (bf16[256,1536]{1,0:T(8,128)(2,1)}, bf16[256,1536]{1,0:T(8,128)(2,1)S(1)}, u32[]{:S(2)}, u32[]{:S(2)}) collective-permute-start(bf16[256,1536]{1,0:T(8,128)(2,1)} %collective-permute-done), channel_id=1, source_target_pairs={{0,2},{2,0},{4,6},{6,4},{1,3},{3,1},{5,7},{7,5},{8,10},{10,8},{12,... | collective-permute-start | bytes 2359304 | tf_op jit(solution)/shard_map/ppermute | solution.py:31
  25.2 11.6 %collective-permute-start.6 = (bf16[128,1536]{1,0:T(8,128)(2,1)S(1)}, bf16[128,1536]{1,0:T(8,128)(2,1)}, u32[]{:S(2)}, u32[]{:S(2)}) collective-permute-start(bf16[128,1536]{1,0:T(8,128)(2,1)S(1)} %get-tuple-element.330), channel_id=1, source_target_pairs={{0,4},{2,6},{4,0},{6,2},{1,5},{3,7},{5,1},{7,3},{8,12},{10,14},{12... | collective-permute-start | bytes 1179656 | tf_op jit(solution)/shard_map/ppermute | solution.py:31
  30.8 36.7 %collective-permute-start.7 = (bf16[512,1536]{1,0:T(8,128)(2,1)}, bf16[512,1536]{1,0:T(8,128)(2,1)}, u32[]{:S(2)}, u32[]{:S(2)}) collective-permute-start(bf16[512,1536]{1,0:T(8,128)(2,1)} %convolution_convert_fusion), channel_id=1, source_target_pairs={{4,5},{1,0},{6,7},{3,2},{12,13},{9,8},{14,15},{11,10},{20,21},{17,... | collective-permute-start | bytes 4718600 | tf_op jit(solution)/shard_map/ppermute | solution.py:168
  34.4 13.2 %collective-permute-start.3 = (bf16[128,1536]{1,0:T(8,128)(2,1)}, bf16[128,1536]{1,0:T(8,128)(2,1)}, u32[]{:S(2)}, u32[]{:S(2)}) collective-permute-start(bf16[128,1536]{1,0:T(8,128)(2,1)} %get-tuple-element.331), channel_id=1, source_target_pairs={{0,4},{2,6},{4,0},{6,2},{1,5},{3,7},{5,1},{7,3},{8,12},{10,14},{12... | collective-permute-start | bytes 1179656 | tf_op jit(solution)/shard_map/ppermute | solution.py:31
  36.8 26.9 %collective-permute-start.8 = (bf16[128,1536]{1,0:T(8,128)(2,1)}, bf16[128,1536]{1,0:T(8,128)(2,1)}, u32[]{:S(2)}, u32[]{:S(2)}) collective-permute-start(bf16[128,1536]{1,0:T(8,128)(2,1)} %collective-permute-done.6), channel_id=1, source_target_pairs={{0,1},{5,4},{2,3},{7,6},{8,9},{13,12},{10,11},{15,14},{16,17},{21,... | collective-permute-start | bytes 1179656 | tf_op jit(solution)/shard_map/ppermute | solution.py:173
  40.4 14.8 %collective-permute-start.10 = (bf16[128,1536]{1,0:T(8,128)(2,1)}, bf16[128,1536]{1,0:T(8,128)(2,1)}, u32[]{:S(2)}, u32[]{:S(2)}) collective-permute-start(bf16[128,1536]{1,0:T(8,128)(2,1)} %get-tuple-element.332), channel_id=1, source_target_pairs={{0,4},{2,6},{4,0},{6,2},{1,5},{3,7},{5,1},{7,3},{8,12},{10,14},{12... | collective-permute-start | bytes 1179656 | tf_op jit(solution)/shard_map/ppermute | solution.py:31
  43.8 18.6 %collective-permute-start.12 = (bf16[128,1536]{1,0:T(8,128)(2,1)}, bf16[128,1536]{1,0:T(8,128)(2,1)S(1)}, u32[]{:S(2)}, u32[]{:S(2)}) collective-permute-start(bf16[128,1536]{1,0:T(8,128)(2,1)} %get-tuple-element.333), channel_id=1, source_target_pairs={{0,4},{2,6},{4,0},{6,2},{1,5},{3,7},{5,1},{7,3},{8,12},{10,14},{12... | collective-permute-start | bytes 1179656 | tf_op jit(solution)/shard_map/ppermute | solution.py:31
  47.6 21.8 %collective-permute-start.4 = (bf16[128,1536]{1,0:T(8,128)(2,1)}, bf16[128,1536]{1,0:T(8,128)(2,1)S(1)}, u32[]{:S(2)}, u32[]{:S(2)}) collective-permute-start(bf16[128,1536]{1,0:T(8,128)(2,1)} %collective-permute-done.3), channel_id=1, source_target_pairs={{0,1},{5,4},{2,3},{7,6},{8,9},{13,12},{10,11},{15,14},{16,17},{21,... | collective-permute-start | bytes 1179656 | tf_op jit(solution)/shard_map/ppermute | solution.py:173
  55.2 16.0 %collective-permute-start.11 = (bf16[128,1536]{1,0:T(8,128)(2,1)}, bf16[128,1536]{1,0:T(8,128)(2,1)S(1)}, u32[]{:S(2)}, u32[]{:S(2)}) collective-permute-start(bf16[128,1536]{1,0:T(8,128)(2,1)} %collective-permute-done.10), channel_id=1, source_target_pairs={{0,1},{5,4},{2,3},{7,6},{8,9},{13,12},{10,11},{15,14},{16,17},{21,... | collective-permute-start | bytes 1179656 | tf_op jit(solution)/shard_map/ppermute | solution.py:173
  62.4 14.3 %collective-permute-start.13 = (bf16[128,1536]{1,0:T(8,128)(2,1)S(1)}, bf16[128,1536]{1,0:T(8,128)(2,1)S(1)}, u32[]{:S(2)}, u32[]{:S(2)}) collective-permute-start(bf16[128,1536]{1,0:T(8,128)(2,1)S(1)} %collective-permute-done.12), channel_id=1, source_target_pairs={{0,1},{5,4},{2,3},{7,6},{8,9},{13,12},{10,11},{15,14},{16,17},{21,... | collective-permute-start | bytes 1179656 | tf_op jit(solution)/shard_map/ppermute | solution.py:173
  79.8 3.7 %collective-permute-start.15 = (f32[2,512]{1,0:T(2,128)S(1)}, f32[2,512]{1,0:T(2,128)S(1)}, u32[]{:S(2)}, u32[]{:S(2)}) collective-permute-start(f32[2,512]{1,0:T(2,128)S(1)} %maximum_add_fusion), channel_id=1, source_target_pairs={{0,1},{1,0},{2,3},{3,2},{4,5},{5,4},{6,7},{7,6},{8,9},{9,8},{10,11... | collective-permute-start | bytes 12296 | tf_op jit(solution)/shard_map/ppermute | solution.py:31
  83.8 5.0 %collective-permute-start.19 = (bf16[512,128]{1,0:T(8,128)(2,1)S(1)}, bf16[512,128]{1,0:T(8,128)(2,1)S(1)}, u32[]{:S(2)}, u32[]{:S(2)}) collective-permute-start(bf16[512,128]{1,0:T(8,128)(2,1)S(1)} %pad_maximum_fusion.5), channel_id=1, source_target_pairs={{0,1},{5,4},{4,0},{1,5},{2,3},{7,6},{6,2},{3,7},{8,9},{13,12},{12,... | collective-permute-start | bytes 393224 | tf_op jit(solution)/shard_map/ppermute | solution.py:228
  83.9 8.4 %collective-permute-start.16 = (bf16[512,128]{1,0:T(8,128)(2,1)S(1)}, bf16[512,128]{1,0:T(8,128)(2,1)S(1)}, u32[]{:S(2)}, u32[]{:S(2)}) collective-permute-start(bf16[512,128]{1,0:T(8,128)(2,1)S(1)} %pad_maximum_fusion.5), channel_id=1, source_target_pairs={{4,1},{1,4},{6,3},{3,6},{12,9},{9,12},{14,11},{11,14},{20,17},{17,... | collective-permute-start | bytes 393224 | tf_op jit(solution)/shard_map/ppermute | solution.py:227
  88.9 14.8 %collective-permute-start.21 = (bf16[512,384]{1,0:T(8,128)(2,1)S(1)}, bf16[512,384]{1,0:T(8,128)(2,1)S(1)}, u32[]{:S(2)}, u32[]{:S(2)}) collective-permute-start(bf16[512,384]{1,0:T(8,128)(2,1)S(1)} %pad_maximum_fusion.2), channel_id=1, source_target_pairs={{4,1},{1,4},{6,3},{3,6},{12,9},{9,12},{14,11},{11,14},{20,17},{17,... | collective-permute-start | bytes 1179656 | tf_op jit(solution)/shard_map/ppermute | solution.py:227
  92.2 12.1 %collective-permute-start.20 = (bf16[512,384]{1,0:T(8,128)(2,1)S(1)}, bf16[512,384]{1,0:T(8,128)(2,1)S(1)}, u32[]{:S(2)}, u32[]{:S(2)}) collective-permute-start(bf16[512,384]{1,0:T(8,128)(2,1)S(1)} %pad_maximum_fusion.2), channel_id=1, source_target_pairs={{0,1},{5,4},{4,0},{1,5},{2,3},{7,6},{6,2},{3,7},{8,9},{13,12},{12,... | collective-permute-start | bytes 1179656 | tf_op jit(solution)/shard_map/ppermute | solution.py:228
  92.3 31.2 %collective-permute-start.18 = (bf16[512,1024]{1,0:T(8,128)(2,1)S(1)}, bf16[512,1024]{1,0:T(8,128)(2,1)S(1)}, u32[]{:S(2)}, u32[]{:S(2)}) collective-permute-start(bf16[512,1024]{1,0:T(8,128)(2,1)S(1)} %pad_maximum_fusion), channel_id=1, source_target_pairs={{4,1},{1,4},{6,3},{3,6},{12,9},{9,12},{14,11},{11,14},{20,17},{17,... | collective-permute-start | bytes 3145736 | tf_op jit(solution)/shard_map/ppermute | solution.py:227
  95.7 28.2 %collective-permute-start.17 = (bf16[512,1024]{1,0:T(8,128)(2,1)S(1)}, bf16[512,1024]{1,0:T(8,128)(2,1)S(1)}, u32[]{:S(2)}, u32[]{:S(2)}) collective-permute-start(bf16[512,1024]{1,0:T(8,128)(2,1)S(1)} %pad_maximum_fusion), channel_id=1, source_target_pairs={{0,1},{5,4},{4,0},{1,5},{2,3},{7,6},{6,2},{3,7},{8,9},{13,12},{12,... | collective-permute-start | bytes 3145736 | tf_op jit(solution)/shard_map/ppermute | solution.py:228
  98.5 13.1 %collective-permute-start.22 = (bf16[1536,128]{1,0:T(8,128)(2,1)S(1)}, bf16[1536,128]{1,0:T(8,128)(2,1)S(1)}, u32[]{:S(2)}, u32[]{:S(2)}) collective-permute-start(bf16[1536,128]{1,0:T(8,128)(2,1)S(1)} %fusion.51), channel_id=1, source_target_pairs={{0,8},{24,16},{1,9},{25,17},{2,10},{26,18},{3,11},{27,19},{4,12},{... | collective-permute-start | bytes 1179656 | tf_op jit(solution)/shard_map/ppermute | solution.py:107
  108.2 12.7 %collective-permute-start.23 = (bf16[1536,128]{1,0:T(8,128)(2,1)S(1)}, bf16[1536,128]{1,0:T(8,128)(2,1)S(1)}, u32[]{:S(2)}, u32[]{:S(2)}) collective-permute-start(bf16[1536,128]{1,0:T(8,128)(2,1)S(1)} %fusion.50), channel_id=1, source_target_pairs={{0,8},{24,16},{1,9},{25,17},{2,10},{26,18},{3,11},{27,19},{4,12},{... | collective-permute-start | bytes 1179656 | tf_op jit(solution)/shard_map/ppermute | solution.py:107
  111.8 9.9 %collective-permute-start.26 = (bf16[1536,128]{1,0:T(8,128)(2,1)S(1)}, bf16[1536,128]{1,0:T(8,128)(2,1)S(1)}, u32[]{:S(2)}, u32[]{:S(2)}) collective-permute-start(bf16[1536,128]{1,0:T(8,128)(2,1)S(1)} %add_convert_fusion.23), channel_id=1, source_target_pairs={{8,16},{16,8},{9,17},{17,9},{10,18},{18,10},{11,19},{19,11},{12,20... | collective-permute-start | bytes 1179656 | tf_op jit(solution)/shard_map/ppermute | solution.py:115
  112.5 17.4 %collective-permute-start.25 = (bf16[1536,128]{1,0:T(8,128)(2,1)S(1)}, bf16[1536,128]{1,0:T(8,128)(2,1)S(1)}, u32[]{:S(2)}, u32[]{:S(2)}) collective-permute-start(bf16[1536,128]{1,0:T(8,128)(2,1)S(1)} %slice.458), channel_id=1, source_target_pairs={{0,8},{24,16},{1,9},{25,17},{2,10},{26,18},{3,11},{27,19},{4,12},{... | collective-permute-start | bytes 1179656 | tf_op jit(solution)/shard_map/ppermute | solution.py:107
  121.0 9.7 %collective-permute-start.24 = (bf16[1536,128]{1,0:T(8,128)(2,1)S(1)}, bf16[1536,128]{1,0:T(8,128)(2,1)S(1)}, u32[]{:S(2)}, u32[]{:S(2)}) collective-permute-start(bf16[1536,128]{1,0:T(8,128)(2,1)S(1)} %add_convert_fusion.22), channel_id=1, source_target_pairs={{8,16},{16,8},{9,17},{17,9},{10,18},{18,10},{11,19},{19,11},{12,20... | collective-permute-start | bytes 1179656 | tf_op jit(solution)/shard_map/ppermute | solution.py:115
  126.5 11.3 %collective-permute-start.28 = (bf16[1536,128]{1,0:T(8,128)(2,1)S(1)}, bf16[1536,128]{1,0:T(8,128)(2,1)S(1)}, u32[]{:S(2)}, u32[]{:S(2)}) collective-permute-start(bf16[1536,128]{1,0:T(8,128)(2,1)S(1)} %fusion.64), channel_id=1, source_target_pairs={{0,8},{24,16},{8,0},{16,24},{1,9},{25,17},{9,1},{17,25},{2,10},{26... | collective-permute-start | bytes 1179656 | tf_op jit(solution)/shard_map/ppermute | solution.py:107
  129.9 8.7 %collective-permute-start.27 = (bf16[1536,128]{1,0:T(8,128)(2,1)S(1)}, bf16[1536,128]{1,0:T(8,128)(2,1)S(1)}, u32[]{:S(2)}, u32[]{:S(2)}) collective-permute-start(bf16[1536,128]{1,0:T(8,128)(2,1)S(1)} %add_convert_fusion.20), channel_id=1, source_target_pairs={{8,16},{16,8},{9,17},{17,9},{10,18},{18,10},{11,19},{19,11},{12,20... | collective-permute-start | bytes 1179656 | tf_op jit(solution)/shard_map/ppermute | solution.py:115
  133.0 14.5 %collective-permute-start.30 = (bf16[1536,128]{1,0:T(8,128)(2,1)S(1)}, bf16[1536,128]{1,0:T(8,128)(2,1)S(1)}, u32[]{:S(2)}, u32[]{:S(2)}) collective-permute-start(bf16[1536,128]{1,0:T(8,128)(2,1)S(1)} %fusion.65), channel_id=1, source_target_pairs={{0,8},{24,16},{8,0},{16,24},{1,9},{25,17},{9,1},{17,25},{2,10},{26... | collective-permute-start | bytes 1179656 | tf_op jit(solution)/shard_map/ppermute | solution.py:107
  137.9 10.6 %collective-permute-start.31 = (bf16[1536,128]{1,0:T(8,128)(2,1)S(1)}, bf16[1536,128]{1,0:T(8,128)(2,1)S(1)}, u32[]{:S(2)}, u32[]{:S(2)}) collective-permute-start(bf16[1536,128]{1,0:T(8,128)(2,1)S(1)} %add_convert_fusion.18), channel_id=1, source_target_pairs={{8,16},{16,8},{9,17},{17,9},{10,18},{18,10},{11,19},{19,11},{12,20... | collective-permute-start | bytes 1179656 | tf_op jit(solution)/shard_map/ppermute | solution.py:115
  138.8 17.1 %collective-permute-start.29 = (bf16[1536,128]{1,0:T(8,128)(2,1)S(1)}, bf16[1536,128]{1,0:T(8,128)(2,1)S(1)}, u32[]{:S(2)}, u32[]{:S(2)}) collective-permute-start(bf16[1536,128]{1,0:T(8,128)(2,1)S(1)} %fusion.66), channel_id=1, source_target_pairs={{0,8},{24,16},{8,0},{16,24},{1,9},{25,17},{9,1},{17,25},{2,10},{26... | collective-permute-start | bytes 1179656 | tf_op jit(solution)/shard_map/ppermute | solution.py:107
  147.6 11.4 %collective-permute-start.34 = (bf16[1536,128]{1,0:T(8,128)(2,1)S(1)}, bf16[1536,128]{1,0:T(8,128)(2,1)S(1)}, u32[]{:S(2)}, u32[]{:S(2)}) collective-permute-start(bf16[1536,128]{1,0:T(8,128)(2,1)S(1)} %add_convert_fusion.16), channel_id=1, source_target_pairs={{8,16},{16,8},{9,17},{17,9},{10,18},{18,10},{11,19},{19,11},{12,20... | collective-permute-start | bytes 1179656 | tf_op jit(solution)/shard_map/ppermute | solution.py:115
  148.7 15.3 %collective-permute-start.33 = (bf16[1536,128]{1,0:T(8,128)(2,1)S(1)}, bf16[1536,128]{1,0:T(8,128)(2,1)S(1)}, u32[]{:S(2)}, u32[]{:S(2)}) collective-permute-start(bf16[1536,128]{1,0:T(8,128)(2,1)S(1)} %fusion.67), channel_id=1, source_target_pairs={{0,8},{24,16},{8,0},{16,24},{1,9},{25,17},{9,1},{17,25},{2,10},{26... | collective-permute-start | bytes 1179656 | tf_op jit(solution)/shard_map/ppermute | solution.py:107
  158.2 6.6 %collective-permute-start.32 = (bf16[1536,128]{1,0:T(8,128)(2,1)S(1)}, bf16[1536,128]{1,0:T(8,128)(2,1)S(1)}, u32[]{:S(2)}, u32[]{:S(2)}) collective-permute-start(bf16[1536,128]{1,0:T(8,128)(2,1)S(1)} %add_convert_fusion.14), channel_id=1, source_target_pairs={{8,16},{16,8},{9,17},{17,9},{10,18},{18,10},{11,19},{19,11},{12,20... | collective-permute-start | bytes 1179656 | tf_op jit(solution)/shard_map/ppermute | solution.py:115
  159.2 15.9 %collective-permute-start.36 = (bf16[1536,128]{1,0:T(8,128)(2,1)S(1)}, bf16[1536,128]{1,0:T(8,128)(2,1)S(1)}, u32[]{:S(2)}, u32[]{:S(2)}) collective-permute-start(bf16[1536,128]{1,0:T(8,128)(2,1)S(1)} %fusion.68), channel_id=1, source_target_pairs={{0,8},{24,16},{8,0},{16,24},{1,9},{25,17},{9,1},{17,25},{2,10},{26... | collective-permute-start | bytes 1179656 | tf_op jit(solution)/shard_map/ppermute | solution.py:107
  164.1 11.9 %collective-permute-start.35 = (bf16[1536,128]{1,0:T(8,128)(2,1)S(1)}, bf16[1536,128]{1,0:T(8,128)(2,1)S(1)}, u32[]{:S(2)}, u32[]{:S(2)}) collective-permute-start(bf16[1536,128]{1,0:T(8,128)(2,1)S(1)} %add_convert_fusion.12), channel_id=1, source_target_pairs={{8,16},{16,8},{9,17},{17,9},{10,18},{18,10},{11,19},{19,11},{12,20... | collective-permute-start | bytes 1179656 | tf_op jit(solution)/shard_map/ppermute | solution.py:115
  165.0 16.9 %collective-permute-start.38 = (bf16[1536,128]{1,0:T(8,128)(2,1)S(1)}, bf16[1536,128]{1,0:T(8,128)(2,1)S(1)}, u32[]{:S(2)}, u32[]{:S(2)}) collective-permute-start(bf16[1536,128]{1,0:T(8,128)(2,1)S(1)} %fusion.69), channel_id=1, source_target_pairs={{0,8},{24,16},{8,0},{16,24},{1,9},{25,17},{9,1},{17,25},{2,10},{26... | collective-permute-start | bytes 1179656 | tf_op jit(solution)/shard_map/ppermute | solution.py:107
  175.2 7.6 %collective-permute-start.37 = (bf16[1536,128]{1,0:T(8,128)(2,1)S(1)}, bf16[1536,128]{1,0:T(8,128)(2,1)S(1)}, u32[]{:S(2)}, u32[]{:S(2)}) collective-permute-start(bf16[1536,128]{1,0:T(8,128)(2,1)S(1)} %add_convert_fusion.10), channel_id=1, source_target_pairs={{8,16},{16,8},{9,17},{17,9},{10,18},{18,10},{11,19},{19,11},{12,20... | collective-permute-start | bytes 1179656 | tf_op jit(solution)/shard_map/ppermute | solution.py:115
  176.2 14.6 %collective-permute-start.40 = (bf16[1536,128]{1,0:T(8,128)(2,1)S(1)}, bf16[1536,128]{1,0:T(8,128)(2,1)S(1)}, u32[]{:S(2)}, u32[]{:S(2)}) collective-permute-start(bf16[1536,128]{1,0:T(8,128)(2,1)S(1)} %fusion.70), channel_id=1, source_target_pairs={{0,8},{24,16},{8,0},{16,24},{1,9},{25,17},{9,1},{17,25},{2,10},{26... | collective-permute-start | bytes 1179656 | tf_op jit(solution)/shard_map/ppermute | solution.py:107
  182.1 9.5 %collective-permute-start.41 = (bf16[1536,128]{1,0:T(8,128)(2,1)S(1)}, bf16[1536,128]{1,0:T(8,128)(2,1)S(1)}, u32[]{:S(2)}, u32[]{:S(2)}) collective-permute-start(bf16[1536,128]{1,0:T(8,128)(2,1)S(1)} %add_convert_fusion.8), channel_id=1, source_target_pairs={{8,16},{16,8},{9,17},{17,9},{10,18},{18,10},{11,19},{19,11},{12,20... | collective-permute-start | bytes 1179656 | tf_op jit(solution)/shard_map/ppermute | solution.py:115
  183.0 16.2 %collective-permute-start.39 = (bf16[1536,128]{1,0:T(8,128)(2,1)S(1)}, bf16[1536,128]{1,0:T(8,128)(2,1)S(1)}, u32[]{:S(2)}, u32[]{:S(2)}) collective-permute-start(bf16[1536,128]{1,0:T(8,128)(2,1)S(1)} %fusion.71), channel_id=1, source_target_pairs={{0,8},{24,16},{8,0},{16,24},{1,9},{25,17},{9,1},{17,25},{2,10},{26... | collective-permute-start | bytes 1179656 | tf_op jit(solution)/shard_map/ppermute | solution.py:107
  190.9 9.1 %collective-permute-start.44 = (bf16[1536,128]{1,0:T(8,128)(2,1)S(1)}, bf16[1536,128]{1,0:T(8,128)(2,1)S(1)}, u32[]{:S(2)}, u32[]{:S(2)}) collective-permute-start(bf16[1536,128]{1,0:T(8,128)(2,1)S(1)} %add_convert_fusion.6), channel_id=1, source_target_pairs={{8,16},{16,8},{9,17},{17,9},{10,18},{18,10},{11,19},{19,11},{12,20... | collective-permute-start | bytes 1179656 | tf_op jit(solution)/shard_map/ppermute | solution.py:115
  191.8 16.3 %collective-permute-start.43 = (bf16[1536,128]{1,0:T(8,128)(2,1)S(1)}, bf16[1536,128]{1,0:T(8,128)(2,1)S(1)}, u32[]{:S(2)}, u32[]{:S(2)}) collective-permute-start(bf16[1536,128]{1,0:T(8,128)(2,1)S(1)} %fusion.72), channel_id=1, source_target_pairs={{0,8},{24,16},{8,0},{16,24},{1,9},{25,17},{9,1},{17,25},{2,10},{26... | collective-permute-start | bytes 1179656 | tf_op jit(solution)/shard_map/ppermute | solution.py:107
  199.3 12.3 %collective-permute-start.42 = (bf16[1536,128]{1,0:T(8,128)(2,1)S(1)}, bf16[1536,128]{1,0:T(8,128)(2,1)S(1)}, u32[]{:S(2)}, u32[]{:S(2)}) collective-permute-start(bf16[1536,128]{1,0:T(8,128)(2,1)S(1)} %add_convert_fusion.4), channel_id=1, source_target_pairs={{8,16},{16,8},{9,17},{17,9},{10,18},{18,10},{11,19},{19,11},{12,20... | collective-permute-start | bytes 1179656 | tf_op jit(solution)/shard_map/ppermute | solution.py:115
  200.1 17.0 %collective-permute-start.48 = (bf16[1536,128]{1,0:T(8,128)(2,1)S(1)}, bf16[1536,128]{1,0:T(8,128)(2,1)S(1)}, u32[]{:S(2)}, u32[]{:S(2)}) collective-permute-start(bf16[1536,128]{1,0:T(8,128)(2,1)S(1)} %add_convert_fusion.3), channel_id=1, source_target_pairs={{8,0},{16,24},{9,1},{17,25},{10,2},{18,26},{11,3},{19,27},{12,4},{... | collective-permute-start | bytes 1179656 | tf_op jit(solution)/shard_map/ppermute | solution.py:107
  208.2 7.5 %collective-permute-start.45 = (bf16[1536,128]{1,0:T(8,128)(2,1)S(1)}, bf16[1536,128]{1,0:T(8,128)(2,1)S(1)}, u32[]{:S(2)}, u32[]{:S(2)}) collective-permute-start(bf16[1536,128]{1,0:T(8,128)(2,1)S(1)} %add_convert_fusion.2), channel_id=1, source_target_pairs={{8,16},{16,8},{9,17},{17,9},{10,18},{18,10},{11,19},{19,11},{12,20... | collective-permute-start | bytes 1179656 | tf_op jit(solution)/shard_map/ppermute | solution.py:115
  211.7 13.4 %collective-permute-start.47 = (bf16[1536,128]{1,0:T(8,128)(2,1)S(1)}, bf16[1536,128]{1,0:T(8,128)(2,1)S(1)}, u32[]{:S(2)}, u32[]{:S(2)}) collective-permute-start(bf16[1536,128]{1,0:T(8,128)(2,1)S(1)} %add_convert_fusion), channel_id=1, source_target_pairs={{8,0},{16,24},{9,1},{17,25},{10,2},{18,26},{11,3},{19,27},{12,4},{... | collective-permute-start | bytes 1179656 | tf_op jit(solution)/shard_map/ppermute | solution.py:107
  215.8 13.5 %collective-permute-start.46 = (bf16[1536,128]{1,0:T(8,128)(2,1)S(1)}, bf16[1536,128]{1,0:T(8,128)(2,1)S(1)}, u32[]{:S(2)}, u32[]{:S(2)}) collective-permute-start(bf16[1536,128]{1,0:T(8,128)(2,1)S(1)} %add_convert_fusion.1), channel_id=1, source_target_pairs={{8,0},{16,24},{9,1},{17,25},{10,2},{18,26},{11,3},{19,27},{12,4},{... | collective-permute-start | bytes 1179656 | tf_op jit(solution)/shard_map/ppermute | solution.py:107
  (18 other events, 219.5 us)

commit v21 on v18

--- a/solution.py
+++ b/solution.py
@@ -33,7 +33,7 @@
 
 def finish_kernel(count, start, narrow, islands, *refs):
     totals, momentum = refs[:count], refs[count]
-    new_out, step_out, held, fresh, step, sems = refs[-6:]
+    new_out, step_out, held, step, sems = refs[-5:]
     columns = pl.ds(start, count * narrow)
     load = pltpu.make_async_copy(momentum.at[:, columns], held, sems.at[0])
     load.start()
@@ -41,9 +41,9 @@
     for k in range(count):
         at = slice(k * narrow, (k + 1) * narrow)
         delta = totals[k][...].astype(f32) / islands
-        fresh[:, at], step[:, at] = outer_update(delta, held[:, at])
+        held[:, at], step[:, at] = outer_update(delta, held[:, at])
     stores = [
-        pltpu.make_async_copy(fresh, new_out.at[:, columns], sems.at[1]),
+        pltpu.make_async_copy(held, new_out.at[:, columns], sems.at[1]),
         pltpu.make_async_copy(step, step_out.at[:, columns], sems.at[2]),
     ]
     for store in stores:
@@ -68,12 +68,11 @@
         out_specs=(in_hbm, in_hbm),
         scratch_shapes=[
             pltpu.VMEM((rows, wide), f32),
-            pltpu.VMEM((rows, wide), f32),
             pltpu.VMEM((rows, wide), bf16),
             pltpu.SemaphoreType.DMA((3,)),
         ],
         input_output_aliases={count + 1 + k: k for k in range(len(outputs))},
-        compiler_params=pltpu.CompilerParams(vmem_limit_bytes=16 * 1024 * 1024),
+        compiler_params=pltpu.CompilerParams(vmem_limit_bytes=8 * 1024 * 1024),
         cost_estimate=pl.CostEstimate(
             flops=5 * rows * wide, bytes_accessed=12 * rows * wide, transcendentals=0
         ),

time: 233 us -> 233 us (level)
  no operation moved by 1% of the time
where the time goes in v21:
time: 233 us; the launch traced here: 231 us
  starting transfers between devices  98.4 us (42%)
  waiting for transfers between devices  73.8 us (32%)
  matrix products  24.4 us (10%)
  other arithmetic  13.1 us (6%)
  Pallas kernels  10.7 us (5%)
  local copies, waits for them, and re-layouts  8.57 us (4%)
    ppermute x15, starting transfers between devices, send_outer(): self.edge[s] = lax.ppermute(payload, 'island', pairs)  63.7 us
    ppermute x11, waiting for transfers between devices, swap(): return lax.ppermute(value, axis, [(i, i ^ bit) for i in range(count)])  33.4 us
    ppermute x15, waiting for transfers between devices, send_outer(): self.edge[s] = lax.ppermute(payload, 'island', pairs)  27.8 us
    dot_general x7, matrix products, add_pseudo(): lax.dot_general(context_all, piece, (((0,), (0,)), ((), ())), preferred_e...  15 us
    pallas_call x5, Pallas kernels, finish(): pl.pallas_call(functools.partial(finish_kernel, count, start, narrow, isl...  10.7 us
    ppermute x3, starting transfers between devices, move(): crosses.append(lax.ppermute(d_local, ('fsdp', 'tp'), cross_pairs))  10.1 us
    dot_general x3, matrix products, project(): jnp.dot(block, weight, preferred_element_type=f32).astype(bf16)  9.49 us
    ppermute x12, starting transfers between devices, step(): self.mid[s] = lax.ppermute(self.sums[s], 'island', [(1, 2), (2, 1)])  8.58 us
  transfers between devices with their start and end apart: 49, of which 23 were waited for; matrix products, arithmetic and copies ran while one was open for 19% of the time, Pallas kernels for 4%

profile of v21, /device:TPU:2, one launch (start us, length us, event | category | flops | bytes accessed | tf_op | source)
XLA Modules:
  0.0 231.0 jit_solution(14759551550580373652)
XLA Ops:
  5.0 15.3 %collective-permute-done = bf16[256,1536]{1,0:T(8,128)(2,1)} collective-permute-done((bf16[256,1536]{1,0:T(8,128)(2,1)}, bf16[256,1536]{1,0:T(8,128)(2,1)}, u32[]{:S(2)}, u32[]{:S(2)}) %collective-permute-start) | collective-permute-done | bytes 786464 | tf_op jit(solution)/shard_map/ppermute | solution.py:31
  20.4 4.0 %convolution_convert_fusion.2 = bf16[256,1536]{1,0:T(8,128)(2,1)S(1)} fusion(bf16[256,1536]{1,0:T(8,128)(2,1)} %collective-permute-done, bf16[1536,1536]{1,0:T(8,128)(2,1)} %param.12), kind=kOutput, calls=%fused_computation.8 | convolution fusion | flops 1208352768 | bytes 6291456 | tf_op jit(solution)/shard_map/dot_general | solution.py:143
  26.7 4.1 %convolution_convert_fusion = bf16[512,1536]{1,0:T(8,128)(2,1)} fusion(bf16[1536,1536]{1,0:T(8,128)(2,1)S(1)} %bitcast.206, bf16[256,1536]{1,0:T(8,128)(2,1)S(1)} %collective-permute-done.5, bf16[256,1536]{1,0:T(8,128)(2,1)S(1)} %copy-done.1), kind=kOutput, calls=%fused_computation | convolution fusion | flops 2419851264 | bytes 7864320 | tf_op jit(solution)/shard_map/dot_general | solution.py:143
  30.8 3.6 %collective-permute-start.7 = (bf16[512,1536]{1,0:T(8,128)(2,1)}, bf16[512,1536]{1,0:T(8,128)(2,1)}, u32[]{:S(2)}, u32[]{:S(2)}) collective-permute-start(bf16[512,1536]{1,0:T(8,128)(2,1)} %convolution_convert_fusion), channel_id=1, source_target_pairs={{4,5},{1,0},{6,7},{3,2},{12,13},{9,8},{14,15},{11,10},{20,21},{17,... | collective-permute-start | bytes 4718600 | tf_op jit(solution)/shard_map/ppermute | solution.py:167
  34.4 2.3 %collective-permute-done.6 = bf16[128,1536]{1,0:T(8,128)(2,1)} collective-permute-done((bf16[128,1536]{1,0:T(8,128)(2,1)S(1)}, bf16[128,1536]{1,0:T(8,128)(2,1)}, u32[]{:S(2)}, u32[]{:S(2)}) %collective-permute-start.6) | collective-permute-done | bytes 393248 | tf_op jit(solution)/shard_map/ppermute | solution.py:31
  40.4 3.4 %collective-permute-start.10 = (bf16[128,1536]{1,0:T(8,128)(2,1)}, bf16[128,1536]{1,0:T(8,128)(2,1)}, u32[]{:S(2)}, u32[]{:S(2)}) collective-permute-start(bf16[128,1536]{1,0:T(8,128)(2,1)} %get-tuple-element.332), channel_id=1, source_target_pairs={{0,4},{2,6},{4,0},{6,2},{1,5},{3,7},{5,1},{7,3},{8,12},{10,14},{12... | collective-permute-start | bytes 1179656 | tf_op jit(solution)/shard_map/ppermute | solution.py:31
  45.5 2.1 constant_dynamic-update-slice_fusion.2
  48.9 6.3 %collective-permute-done.10 = bf16[128,1536]{1,0:T(8,128)(2,1)} collective-permute-done((bf16[128,1536]{1,0:T(8,128)(2,1)}, bf16[128,1536]{1,0:T(8,128)(2,1)}, u32[]{:S(2)}, u32[]{:S(2)}) %collective-permute-start.10) | collective-permute-done | bytes 393248 | tf_op jit(solution)/shard_map/ppermute | solution.py:31
  56.5 6.0 %collective-permute-done.12 = bf16[128,1536]{1,0:T(8,128)(2,1)S(1)} collective-permute-done((bf16[128,1536]{1,0:T(8,128)(2,1)}, bf16[128,1536]{1,0:T(8,128)(2,1)S(1)}, u32[]{:S(2)}, u32[]{:S(2)}) %collective-permute-start.12) | collective-permute-done | bytes 393248 | tf_op jit(solution)/shard_map/ppermute | solution.py:31
  63.7 3.9 %collective-permute-done.7 = bf16[512,1536]{1,0:T(8,128)(2,1)} collective-permute-done((bf16[512,1536]{1,0:T(8,128)(2,1)}, bf16[512,1536]{1,0:T(8,128)(2,1)}, u32[]{:S(2)}, u32[]{:S(2)}) %collective-permute-start.7) | collective-permute-done | bytes 1572896 | tf_op jit(solution)/shard_map/ppermute | solution.py:167
  67.6 1.8 multiply_reduce_fusion.7
  69.4 1.8 multiply_reduce_fusion.5
  71.2 1.7 multiply_reduce_fusion.3
  73.0 3.7 %collective-permute-done.13 = bf16[128,1536]{1,0:T(8,128)(2,1)S(1)} collective-permute-done((bf16[128,1536]{1,0:T(8,128)(2,1)S(1)}, bf16[128,1536]{1,0:T(8,128)(2,1)S(1)}, u32[]{:S(2)}, u32[]{:S(2)}) %collective-permute-start.13) | collective-permute-done | bytes 393248 | tf_op jit(solution)/shard_map/ppermute | solution.py:172
  76.7 1.6 multiply_reduce_fusion.1
  80.0 3.5 %collective-permute-done.15 = f32[2,512]{1,0:T(2,128)S(1)} collective-permute-done((f32[2,512]{1,0:T(2,128)S(1)}, f32[2,512]{1,0:T(2,128)S(1)}, u32[]{:S(2)}, u32[]{:S(2)}) %collective-permute-start.15) | collective-permute-done | bytes 4128 | tf_op jit(solution)/shard_map/ppermute | solution.py:31
  83.9 3.4 %collective-permute-start.16 = (bf16[512,128]{1,0:T(8,128)(2,1)S(1)}, bf16[512,128]{1,0:T(8,128)(2,1)S(1)}, u32[]{:S(2)}, u32[]{:S(2)}) collective-permute-start(bf16[512,128]{1,0:T(8,128)(2,1)S(1)} %pad_maximum_fusion.5), channel_id=1, source_target_pairs={{4,1},{1,4},{6,3},{3,6},{12,9},{9,12},{14,11},{11,14},{20,17},{17,... | collective-permute-start | bytes 393224 | tf_op jit(solution)/shard_map/ppermute | solution.py:227
  88.9 3.3 %collective-permute-start.21 = (bf16[512,384]{1,0:T(8,128)(2,1)S(1)}, bf16[512,384]{1,0:T(8,128)(2,1)S(1)}, u32[]{:S(2)}, u32[]{:S(2)}) collective-permute-start(bf16[512,384]{1,0:T(8,128)(2,1)S(1)} %pad_maximum_fusion.2), channel_id=1, source_target_pairs={{4,1},{1,4},{6,3},{3,6},{12,9},{9,12},{14,11},{11,14},{20,17},{17,... | collective-permute-start | bytes 1179656 | tf_op jit(solution)/shard_map/ppermute | solution.py:227
  92.3 3.4 %collective-permute-start.18 = (bf16[512,1024]{1,0:T(8,128)(2,1)S(1)}, bf16[512,1024]{1,0:T(8,128)(2,1)S(1)}, u32[]{:S(2)}, u32[]{:S(2)}) collective-permute-start(bf16[512,1024]{1,0:T(8,128)(2,1)S(1)} %pad_maximum_fusion), channel_id=1, source_target_pairs={{4,1},{1,4},{6,3},{3,6},{12,9},{9,12},{14,11},{11,14},{20,17},{17,... | collective-permute-start | bytes 3145736 | tf_op jit(solution)/shard_map/ppermute | solution.py:227
  95.9 2.6 %fusion.51 = bf16[1536,128]{1,0:T(8,128)(2,1)S(1)} fusion(bf16[1536,1536]{1,0:T(8,128)(2,1)S(1)} %bitcast.208, bf16[1,1536,1536]{2,1,0:T(8,128)(2,1)S(1)} %bitcast.210, bf16[1,1536,1536]{2,1,0:T(8,128)(2,1)} %param.13, bf16[1024,1536]{1,0:T(8,128)(2,1)S(1)} %constant_dynamic-update-slice_fusion, bf16[1024,128]{1,0:T(8,128)(2,1)S(1)} %pad_maximum_fusion.4), kind=kOutput, calls=%fused_computation.119 | convolution fusion | flops 406192128 | bytes 4980736 | tf_op jit(solution)/shard_map/dot_general | solution.py:242
  98.5 3.7 %collective-permute-start.22 = (bf16[1536,128]{1,0:T(8,128)(2,1)S(1)}, bf16[1536,128]{1,0:T(8,128)(2,1)S(1)}, u32[]{:S(2)}, u32[]{:S(2)}) collective-permute-start(bf16[1536,128]{1,0:T(8,128)(2,1)S(1)} %fusion.51), channel_id=1, source_target_pairs={{0,8},{24,16},{1,9},{25,17},{2,10},{26,18},{3,11},{27,19},{4,12},{... | collective-permute-start | bytes 1179656 | tf_op jit(solution)/shard_map/ppermute | solution.py:106
  105.9 2.2 fusion.33
  108.2 3.5 %collective-permute-start.23 = (bf16[1536,128]{1,0:T(8,128)(2,1)S(1)}, bf16[1536,128]{1,0:T(8,128)(2,1)S(1)}, u32[]{:S(2)}, u32[]{:S(2)}) collective-permute-start(bf16[1536,128]{1,0:T(8,128)(2,1)S(1)} %fusion.50), channel_id=1, source_target_pairs={{0,8},{24,16},{1,9},{25,17},{2,10},{26,18},{3,11},{27,19},{4,12},{... | collective-permute-start | bytes 1179656 | tf_op jit(solution)/shard_map/ppermute | solution.py:106
  112.5 6.1 %collective-permute-start.25 = (bf16[1536,128]{1,0:T(8,128)(2,1)S(1)}, bf16[1536,128]{1,0:T(8,128)(2,1)S(1)}, u32[]{:S(2)}, u32[]{:S(2)}) collective-permute-start(bf16[1536,128]{1,0:T(8,128)(2,1)S(1)} %slice.458), channel_id=1, source_target_pairs={{0,8},{24,16},{1,9},{25,17},{2,10},{26,18},{3,11},{27,19},{4,12},{... | collective-permute-start | bytes 1179656 | tf_op jit(solution)/shard_map/ppermute | solution.py:106
  118.6 2.2 collective-permute-done.23
  121.7 1.8 collective-permute-done.18
  124.2 2.2 fusion.34
  126.5 3.3 %collective-permute-start.28 = (bf16[1536,128]{1,0:T(8,128)(2,1)S(1)}, bf16[1536,128]{1,0:T(8,128)(2,1)S(1)}, u32[]{:S(2)}, u32[]{:S(2)}) collective-permute-start(bf16[1536,128]{1,0:T(8,128)(2,1)S(1)} %fusion.64), channel_id=1, source_target_pairs={{0,8},{24,16},{8,0},{16,24},{1,9},{25,17},{9,1},{17,25},{2,10},{26... | collective-permute-start | bytes 1179656 | tf_op jit(solution)/shard_map/ppermute | solution.py:106
  130.7 2.2 fusion.35
  133.0 4.4 %collective-permute-start.30 = (bf16[1536,128]{1,0:T(8,128)(2,1)S(1)}, bf16[1536,128]{1,0:T(8,128)(2,1)S(1)}, u32[]{:S(2)}, u32[]{:S(2)}) collective-permute-start(bf16[1536,128]{1,0:T(8,128)(2,1)S(1)} %fusion.65), channel_id=1, source_target_pairs={{0,8},{24,16},{8,0},{16,24},{1,9},{25,17},{9,1},{17,25},{2,10},{26... | collective-permute-start | bytes 1179656 | tf_op jit(solution)/shard_map/ppermute | solution.py:106
  138.8 5.3 %collective-permute-start.29 = (bf16[1536,128]{1,0:T(8,128)(2,1)S(1)}, bf16[1536,128]{1,0:T(8,128)(2,1)S(1)}, u32[]{:S(2)}, u32[]{:S(2)}) collective-permute-start(bf16[1536,128]{1,0:T(8,128)(2,1)S(1)} %fusion.66), channel_id=1, source_target_pairs={{0,8},{24,16},{8,0},{16,24},{1,9},{25,17},{9,1},{17,25},{2,10},{26... | collective-permute-start | bytes 1179656 | tf_op jit(solution)/shard_map/ppermute | solution.py:106
  144.2 3.3 %collective-permute-done.30 = bf16[1536,128]{1,0:T(8,128)(2,1)S(1)} collective-permute-done((bf16[1536,128]{1,0:T(8,128)(2,1)S(1)}, bf16[1536,128]{1,0:T(8,128)(2,1)S(1)}, u32[]{:S(2)}, u32[]{:S(2)}) %collective-permute-start.30) | collective-permute-done | bytes 393248 | tf_op jit(solution)/shard_map/ppermute | solution.py:106
  148.7 4.1 %collective-permute-start.33 = (bf16[1536,128]{1,0:T(8,128)(2,1)S(1)}, bf16[1536,128]{1,0:T(8,128)(2,1)S(1)}, u32[]{:S(2)}, u32[]{:S(2)}) collective-permute-start(bf16[1536,128]{1,0:T(8,128)(2,1)S(1)} %fusion.67), channel_id=1, source_target_pairs={{0,8},{24,16},{8,0},{16,24},{1,9},{25,17},{9,1},{17,25},{2,10},{26... | collective-permute-start | bytes 1179656 | tf_op jit(solution)/shard_map/ppermute | solution.py:106
  152.8 3.1 %collective-permute-done.29 = bf16[1536,128]{1,0:T(8,128)(2,1)S(1)} collective-permute-done((bf16[1536,128]{1,0:T(8,128)(2,1)S(1)}, bf16[1536,128]{1,0:T(8,128)(2,1)S(1)}, u32[]{:S(2)}, u32[]{:S(2)}) %collective-permute-start.29) | collective-permute-done | bytes 393248 | tf_op jit(solution)/shard_map/ppermute | solution.py:106
  156.0 2.2 fusion.37
  159.2 3.6 %collective-permute-start.36 = (bf16[1536,128]{1,0:T(8,128)(2,1)S(1)}, bf16[1536,128]{1,0:T(8,128)(2,1)S(1)}, u32[]{:S(2)}, u32[]{:S(2)}) collective-permute-start(bf16[1536,128]{1,0:T(8,128)(2,1)S(1)} %fusion.68), channel_id=1, source_target_pairs={{0,8},{24,16},{8,0},{16,24},{1,9},{25,17},{9,1},{17,25},{2,10},{26... | collective-permute-start | bytes 1179656 | tf_op jit(solution)/shard_map/ppermute | solution.py:106
  165.0 7.8 %collective-permute-start.38 = (bf16[1536,128]{1,0:T(8,128)(2,1)S(1)}, bf16[1536,128]{1,0:T(8,128)(2,1)S(1)}, u32[]{:S(2)}, u32[]{:S(2)}) collective-permute-start(bf16[1536,128]{1,0:T(8,128)(2,1)S(1)} %fusion.69), channel_id=1, source_target_pairs={{0,8},{24,16},{8,0},{16,24},{1,9},{25,17},{9,1},{17,25},{2,10},{26... | collective-permute-start | bytes 1179656 | tf_op jit(solution)/shard_map/ppermute | solution.py:106
  172.8 2.2 fusion.36
  176.2 4.7 %collective-permute-start.40 = (bf16[1536,128]{1,0:T(8,128)(2,1)S(1)}, bf16[1536,128]{1,0:T(8,128)(2,1)S(1)}, u32[]{:S(2)}, u32[]{:S(2)}) collective-permute-start(bf16[1536,128]{1,0:T(8,128)(2,1)S(1)} %fusion.70), channel_id=1, source_target_pairs={{0,8},{24,16},{8,0},{16,24},{1,9},{25,17},{9,1},{17,25},{2,10},{26... | collective-permute-start | bytes 1179656 | tf_op jit(solution)/shard_map/ppermute | solution.py:106
  183.0 6.7 %collective-permute-start.39 = (bf16[1536,128]{1,0:T(8,128)(2,1)S(1)}, bf16[1536,128]{1,0:T(8,128)(2,1)S(1)}, u32[]{:S(2)}, u32[]{:S(2)}) collective-permute-start(bf16[1536,128]{1,0:T(8,128)(2,1)S(1)} %fusion.71), channel_id=1, source_target_pairs={{0,8},{24,16},{8,0},{16,24},{1,9},{25,17},{9,1},{17,25},{2,10},{26... | collective-permute-start | bytes 1179656 | tf_op jit(solution)/shard_map/ppermute | solution.py:106
  191.6 6.6 %collective-permute-start.43 = (bf16[1536,128]{1,0:T(8,128)(2,1)S(1)}, bf16[1536,128]{1,0:T(8,128)(2,1)S(1)}, u32[]{:S(2)}, u32[]{:S(2)}) collective-permute-start(bf16[1536,128]{1,0:T(8,128)(2,1)S(1)} %fusion.72), channel_id=1, source_target_pairs={{0,8},{24,16},{8,0},{16,24},{1,9},{25,17},{9,1},{17,25},{2,10},{26... | collective-permute-start | bytes 1179656 | tf_op jit(solution)/shard_map/ppermute | solution.py:106
  201.3 6.8 %collective-permute-done.43 = bf16[1536,128]{1,0:T(8,128)(2,1)S(1)} collective-permute-done((bf16[1536,128]{1,0:T(8,128)(2,1)S(1)}, bf16[1536,128]{1,0:T(8,128)(2,1)S(1)}, u32[]{:S(2)}, u32[]{:S(2)}) %collective-permute-start.43) | collective-permute-done | bytes 393248 | tf_op jit(solution)/shard_map/ppermute | solution.py:106
  208.9 2.5 %shard_map.95 = (f32[1536,1536]{1,0:T(8,128)}, bf16[1536,1536]{1,0:T(8,128)(2,1)}) custom-call(bf16[1536,128]{1,0:T(8,128)(2,1)S(1)} %broadcast_select_fusion.15.refs_0_, bf16[1536,128]{1,0:T(8,128)(2,1)S(1)} %broadcast_select_fusion.5.refs_1_, bf16[1536,128]{1,0:T(8,128)(2,1)S(1)} %broadcast_select_fusion.4.refs_2_, f32[1536,1536]{1,0:T(8,128)S(1)} %bitcast.192), custom_call_target="tpu_custom_call" | custom-call | flops 2949120 | bytes 7077888 | tf_op jit(solution)/shard_map/pallas_call | solution.py:61
  212.9 2.5 %shard_map.96 = (f32[1536,1536]{1,0:T(8,128)}, bf16[1536,1536]{1,0:T(8,128)(2,1)}) custom-call(bf16[1536,128]{1,0:T(8,128)(2,1)S(1)} %broadcast_select_fusion.13.refs_0_, bf16[1536,128]{1,0:T(8,128)(2,1)S(1)} %broadcast_select_fusion.7.refs_1_, bf16[1536,128]{1,0:T(8,128)(2,1)S(1)} %broadcast_select_fusion.6.refs_2_, ...), custom_call_target="tpu_custom_call", output_to_operand_aliasing={{0}: (4, {}), {1}: (5, {})} | custom-call | flops 2949120 | bytes 7077888 | tf_op jit(solution)/shard_map/pallas_call | solution.py:61
  216.9 2.5 %shard_map.97 = (f32[1536,1536]{1,0:T(8,128)}, bf16[1536,1536]{1,0:T(8,128)(2,1)}) custom-call(bf16[1536,128]{1,0:T(8,128)(2,1)S(1)} %broadcast_select_fusion.14.refs_0_, bf16[1536,128]{1,0:T(8,128)(2,1)S(1)} %broadcast_select_fusion.9.refs_1_, bf16[1536,128]{1,0:T(8,128)(2,1)S(1)} %broadcast_select_fusion.8.refs_2_, ...), custom_call_target="tpu_custom_call", output_to_operand_aliasing={{0}: (4, {}), {1}: (5, {})} | custom-call | flops 2949120 | bytes 7077888 | tf_op jit(solution)/shard_map/pallas_call | solution.py:61
  219.5 5.8 %collective-permute-done.47 = bf16[1536,128]{1,0:T(8,128)(2,1)S(1)} collective-permute-done((bf16[1536,128]{1,0:T(8,128)(2,1)S(1)}, bf16[1536,128]{1,0:T(8,128)(2,1)S(1)}, u32[]{:S(2)}, u32[]{:S(2)}) %collective-permute-start.47) | collective-permute-done | bytes 393248 | tf_op jit(solution)/shard_map/ppermute | solution.py:106
  225.3 1.9 shard_map.98
  227.2 2.3 collective-permute-done.46
  (181 shorter events, 45.9 us)
Async XLA Ops:
  0.6 19.7 %collective-permute-start = (bf16[256,1536]{1,0:T(8,128)(2,1)}, bf16[256,1536]{1,0:T(8,128)(2,1)}, u32[]{:S(2)}, u32[]{:S(2)}) collective-permute-start(bf16[256,1536]{1,0:T(8,128)(2,1)} %param.8), channel_id=1, source_target_pairs={{0,4},{2,6},{4,0},{6,2},{1,5},{3,7},{5,1},{7,3},{8,12},{10,14},{12... | collective-permute-start | bytes 2359304 | tf_op jit(solution)/shard_map/ppermute | solution.py:31
  3.8 16.5 %collective-permute-start.1 = (bf16[256,1536]{1,0:T(8,128)(2,1)S(1)}, bf16[256,1536]{1,0:T(8,128)(2,1)S(1)}, u32[]{:S(2)}, u32[]{:S(2)}) collective-permute-start(bf16[256,1536]{1,0:T(8,128)(2,1)S(1)} %get-tuple-element.322), channel_id=1, source_target_pairs={{0,2},{2,0},{4,6},{6,4},{1,3},{3,1},{5,7},{7,5},{8,10},{10,8},{12,... | collective-permute-start | bytes 2359304 | tf_op jit(solution)/shard_map/ppermute | solution.py:31
  4.2 16.1 %collective-permute-start.2 = (bf16[256,1536]{1,0:T(8,128)(2,1)S(1)}, bf16[256,1536]{1,0:T(8,128)(2,1)S(1)}, u32[]{:S(2)}, u32[]{:S(2)}) collective-permute-start(bf16[256,1536]{1,0:T(8,128)(2,1)S(1)} %get-tuple-element.320), channel_id=1, source_target_pairs={{0,2},{2,0},{4,6},{6,4},{1,3},{3,1},{5,7},{7,5},{8,10},{10,8},{12,... | collective-permute-start | bytes 2359304 | tf_op jit(solution)/shard_map/ppermute | solution.py:31
  5.0 21.7 %collective-permute-start.5 = (bf16[256,1536]{1,0:T(8,128)(2,1)S(1)}, bf16[256,1536]{1,0:T(8,128)(2,1)S(1)}, u32[]{:S(2)}, u32[]{:S(2)}) collective-permute-start(bf16[256,1536]{1,0:T(8,128)(2,1)S(1)} %copy-done.1), channel_id=1, source_target_pairs={{0,2},{2,0},{4,6},{6,4},{1,3},{3,1},{5,7},{7,5},{8,10},{10,8},{12,... | collective-permute-start | bytes 2359304 | tf_op jit(solution)/shard_map/ppermute | solution.py:31
  20.3 17.8 %collective-permute-start.9 = (bf16[256,1536]{1,0:T(8,128)(2,1)}, bf16[256,1536]{1,0:T(8,128)(2,1)S(1)}, u32[]{:S(2)}, u32[]{:S(2)}) collective-permute-start(bf16[256,1536]{1,0:T(8,128)(2,1)} %collective-permute-done), channel_id=1, source_target_pairs={{0,2},{2,0},{4,6},{6,4},{1,3},{3,1},{5,7},{7,5},{8,10},{10,8},{12,... | collective-permute-start | bytes 2359304 | tf_op jit(solution)/shard_map/ppermute | solution.py:31
  25.2 11.6 %collective-permute-start.6 = (bf16[128,1536]{1,0:T(8,128)(2,1)S(1)}, bf16[128,1536]{1,0:T(8,128)(2,1)}, u32[]{:S(2)}, u32[]{:S(2)}) collective-permute-start(bf16[128,1536]{1,0:T(8,128)(2,1)S(1)} %get-tuple-element.330), channel_id=1, source_target_pairs={{0,4},{2,6},{4,0},{6,2},{1,5},{3,7},{5,1},{7,3},{8,12},{10,14},{12... | collective-permute-start | bytes 1179656 | tf_op jit(solution)/shard_map/ppermute | solution.py:31
  30.8 36.7 %collective-permute-start.7 = (bf16[512,1536]{1,0:T(8,128)(2,1)}, bf16[512,1536]{1,0:T(8,128)(2,1)}, u32[]{:S(2)}, u32[]{:S(2)}) collective-permute-start(bf16[512,1536]{1,0:T(8,128)(2,1)} %convolution_convert_fusion), channel_id=1, source_target_pairs={{4,5},{1,0},{6,7},{3,2},{12,13},{9,8},{14,15},{11,10},{20,21},{17,... | collective-permute-start | bytes 4718600 | tf_op jit(solution)/shard_map/ppermute | solution.py:167
  34.4 13.2 %collective-permute-start.3 = (bf16[128,1536]{1,0:T(8,128)(2,1)}, bf16[128,1536]{1,0:T(8,128)(2,1)}, u32[]{:S(2)}, u32[]{:S(2)}) collective-permute-start(bf16[128,1536]{1,0:T(8,128)(2,1)} %get-tuple-element.331), channel_id=1, source_target_pairs={{0,4},{2,6},{4,0},{6,2},{1,5},{3,7},{5,1},{7,3},{8,12},{10,14},{12... | collective-permute-start | bytes 1179656 | tf_op jit(solution)/shard_map/ppermute | solution.py:31
  36.8 26.9 %collective-permute-start.8 = (bf16[128,1536]{1,0:T(8,128)(2,1)}, bf16[128,1536]{1,0:T(8,128)(2,1)}, u32[]{:S(2)}, u32[]{:S(2)}) collective-permute-start(bf16[128,1536]{1,0:T(8,128)(2,1)} %collective-permute-done.6), channel_id=1, source_target_pairs={{0,1},{5,4},{2,3},{7,6},{8,9},{13,12},{10,11},{15,14},{16,17},{21,... | collective-permute-start | bytes 1179656 | tf_op jit(solution)/shard_map/ppermute | solution.py:172
  40.4 14.8 %collective-permute-start.10 = (bf16[128,1536]{1,0:T(8,128)(2,1)}, bf16[128,1536]{1,0:T(8,128)(2,1)}, u32[]{:S(2)}, u32[]{:S(2)}) collective-permute-start(bf16[128,1536]{1,0:T(8,128)(2,1)} %get-tuple-element.332), channel_id=1, source_target_pairs={{0,4},{2,6},{4,0},{6,2},{1,5},{3,7},{5,1},{7,3},{8,12},{10,14},{12... | collective-permute-start | bytes 1179656 | tf_op jit(solution)/shard_map/ppermute | solution.py:31
  43.8 18.6 %collective-permute-start.12 = (bf16[128,1536]{1,0:T(8,128)(2,1)}, bf16[128,1536]{1,0:T(8,128)(2,1)S(1)}, u32[]{:S(2)}, u32[]{:S(2)}) collective-permute-start(bf16[128,1536]{1,0:T(8,128)(2,1)} %get-tuple-element.333), channel_id=1, source_target_pairs={{0,4},{2,6},{4,0},{6,2},{1,5},{3,7},{5,1},{7,3},{8,12},{10,14},{12... | collective-permute-start | bytes 1179656 | tf_op jit(solution)/shard_map/ppermute | solution.py:31
  47.6 21.8 %collective-permute-start.4 = (bf16[128,1536]{1,0:T(8,128)(2,1)}, bf16[128,1536]{1,0:T(8,128)(2,1)S(1)}, u32[]{:S(2)}, u32[]{:S(2)}) collective-permute-start(bf16[128,1536]{1,0:T(8,128)(2,1)} %collective-permute-done.3), channel_id=1, source_target_pairs={{0,1},{5,4},{2,3},{7,6},{8,9},{13,12},{10,11},{15,14},{16,17},{21,... | collective-permute-start | bytes 1179656 | tf_op jit(solution)/shard_map/ppermute | solution.py:172
  55.2 16.0 %collective-permute-start.11 = (bf16[128,1536]{1,0:T(8,128)(2,1)}, bf16[128,1536]{1,0:T(8,128)(2,1)S(1)}, u32[]{:S(2)}, u32[]{:S(2)}) collective-permute-start(bf16[128,1536]{1,0:T(8,128)(2,1)} %collective-permute-done.10), channel_id=1, source_target_pairs={{0,1},{5,4},{2,3},{7,6},{8,9},{13,12},{10,11},{15,14},{16,17},{21,... | collective-permute-start | bytes 1179656 | tf_op jit(solution)/shard_map/ppermute | solution.py:172
  62.4 14.3 %collective-permute-start.13 = (bf16[128,1536]{1,0:T(8,128)(2,1)S(1)}, bf16[128,1536]{1,0:T(8,128)(2,1)S(1)}, u32[]{:S(2)}, u32[]{:S(2)}) collective-permute-start(bf16[128,1536]{1,0:T(8,128)(2,1)S(1)} %collective-permute-done.12), channel_id=1, source_target_pairs={{0,1},{5,4},{2,3},{7,6},{8,9},{13,12},{10,11},{15,14},{16,17},{21,... | collective-permute-start | bytes 1179656 | tf_op jit(solution)/shard_map/ppermute | solution.py:172
  79.8 3.7 %collective-permute-start.15 = (f32[2,512]{1,0:T(2,128)S(1)}, f32[2,512]{1,0:T(2,128)S(1)}, u32[]{:S(2)}, u32[]{:S(2)}) collective-permute-start(f32[2,512]{1,0:T(2,128)S(1)} %maximum_add_fusion), channel_id=1, source_target_pairs={{0,1},{1,0},{2,3},{3,2},{4,5},{5,4},{6,7},{7,6},{8,9},{9,8},{10,11... | collective-permute-start | bytes 12296 | tf_op jit(solution)/shard_map/ppermute | solution.py:31
  83.8 5.0 %collective-permute-start.19 = (bf16[512,128]{1,0:T(8,128)(2,1)S(1)}, bf16[512,128]{1,0:T(8,128)(2,1)S(1)}, u32[]{:S(2)}, u32[]{:S(2)}) collective-permute-start(bf16[512,128]{1,0:T(8,128)(2,1)S(1)} %pad_maximum_fusion.5), channel_id=1, source_target_pairs={{0,1},{5,4},{4,0},{1,5},{2,3},{7,6},{6,2},{3,7},{8,9},{13,12},{12,... | collective-permute-start | bytes 393224 | tf_op jit(solution)/shard_map/ppermute | solution.py:226
  83.9 8.4 %collective-permute-start.16 = (bf16[512,128]{1,0:T(8,128)(2,1)S(1)}, bf16[512,128]{1,0:T(8,128)(2,1)S(1)}, u32[]{:S(2)}, u32[]{:S(2)}) collective-permute-start(bf16[512,128]{1,0:T(8,128)(2,1)S(1)} %pad_maximum_fusion.5), channel_id=1, source_target_pairs={{4,1},{1,4},{6,3},{3,6},{12,9},{9,12},{14,11},{11,14},{20,17},{17,... | collective-permute-start | bytes 393224 | tf_op jit(solution)/shard_map/ppermute | solution.py:227
  88.9 14.8 %collective-permute-start.21 = (bf16[512,384]{1,0:T(8,128)(2,1)S(1)}, bf16[512,384]{1,0:T(8,128)(2,1)S(1)}, u32[]{:S(2)}, u32[]{:S(2)}) collective-permute-start(bf16[512,384]{1,0:T(8,128)(2,1)S(1)} %pad_maximum_fusion.2), channel_id=1, source_target_pairs={{4,1},{1,4},{6,3},{3,6},{12,9},{9,12},{14,11},{11,14},{20,17},{17,... | collective-permute-start | bytes 1179656 | tf_op jit(solution)/shard_map/ppermute | solution.py:227
  92.2 12.1 %collective-permute-start.20 = (bf16[512,384]{1,0:T(8,128)(2,1)S(1)}, bf16[512,384]{1,0:T(8,128)(2,1)S(1)}, u32[]{:S(2)}, u32[]{:S(2)}) collective-permute-start(bf16[512,384]{1,0:T(8,128)(2,1)S(1)} %pad_maximum_fusion.2), channel_id=1, source_target_pairs={{0,1},{5,4},{4,0},{1,5},{2,3},{7,6},{6,2},{3,7},{8,9},{13,12},{12,... | collective-permute-start | bytes 1179656 | tf_op jit(solution)/shard_map/ppermute | solution.py:226
  92.3 31.2 %collective-permute-start.18 = (bf16[512,1024]{1,0:T(8,128)(2,1)S(1)}, bf16[512,1024]{1,0:T(8,128)(2,1)S(1)}, u32[]{:S(2)}, u32[]{:S(2)}) collective-permute-start(bf16[512,1024]{1,0:T(8,128)(2,1)S(1)} %pad_maximum_fusion), channel_id=1, source_target_pairs={{4,1},{1,4},{6,3},{3,6},{12,9},{9,12},{14,11},{11,14},{20,17},{17,... | collective-permute-start | bytes 3145736 | tf_op jit(solution)/shard_map/ppermute | solution.py:227
  95.7 28.2 %collective-permute-start.17 = (bf16[512,1024]{1,0:T(8,128)(2,1)S(1)}, bf16[512,1024]{1,0:T(8,128)(2,1)S(1)}, u32[]{:S(2)}, u32[]{:S(2)}) collective-permute-start(bf16[512,1024]{1,0:T(8,128)(2,1)S(1)} %pad_maximum_fusion), channel_id=1, source_target_pairs={{0,1},{5,4},{4,0},{1,5},{2,3},{7,6},{6,2},{3,7},{8,9},{13,12},{12,... | collective-permute-start | bytes 3145736 | tf_op jit(solution)/shard_map/ppermute | solution.py:226
  98.5 13.1 %collective-permute-start.22 = (bf16[1536,128]{1,0:T(8,128)(2,1)S(1)}, bf16[1536,128]{1,0:T(8,128)(2,1)S(1)}, u32[]{:S(2)}, u32[]{:S(2)}) collective-permute-start(bf16[1536,128]{1,0:T(8,128)(2,1)S(1)} %fusion.51), channel_id=1, source_target_pairs={{0,8},{24,16},{1,9},{25,17},{2,10},{26,18},{3,11},{27,19},{4,12},{... | collective-permute-start | bytes 1179656 | tf_op jit(solution)/shard_map/ppermute | solution.py:106
  108.2 12.7 %collective-permute-start.23 = (bf16[1536,128]{1,0:T(8,128)(2,1)S(1)}, bf16[1536,128]{1,0:T(8,128)(2,1)S(1)}, u32[]{:S(2)}, u32[]{:S(2)}) collective-permute-start(bf16[1536,128]{1,0:T(8,128)(2,1)S(1)} %fusion.50), channel_id=1, source_target_pairs={{0,8},{24,16},{1,9},{25,17},{2,10},{26,18},{3,11},{27,19},{4,12},{... | collective-permute-start | bytes 1179656 | tf_op jit(solution)/shard_map/ppermute | solution.py:106
  111.8 9.9 %collective-permute-start.26 = (bf16[1536,128]{1,0:T(8,128)(2,1)S(1)}, bf16[1536,128]{1,0:T(8,128)(2,1)S(1)}, u32[]{:S(2)}, u32[]{:S(2)}) collective-permute-start(bf16[1536,128]{1,0:T(8,128)(2,1)S(1)} %add_convert_fusion.23), channel_id=1, source_target_pairs={{8,16},{16,8},{9,17},{17,9},{10,18},{18,10},{11,19},{19,11},{12,20... | collective-permute-start | bytes 1179656 | tf_op jit(solution)/shard_map/ppermute | solution.py:114
  112.5 17.4 %collective-permute-start.25 = (bf16[1536,128]{1,0:T(8,128)(2,1)S(1)}, bf16[1536,128]{1,0:T(8,128)(2,1)S(1)}, u32[]{:S(2)}, u32[]{:S(2)}) collective-permute-start(bf16[1536,128]{1,0:T(8,128)(2,1)S(1)} %slice.458), channel_id=1, source_target_pairs={{0,8},{24,16},{1,9},{25,17},{2,10},{26,18},{3,11},{27,19},{4,12},{... | collective-permute-start | bytes 1179656 | tf_op jit(solution)/shard_map/ppermute | solution.py:106
  121.0 9.7 %collective-permute-start.24 = (bf16[1536,128]{1,0:T(8,128)(2,1)S(1)}, bf16[1536,128]{1,0:T(8,128)(2,1)S(1)}, u32[]{:S(2)}, u32[]{:S(2)}) collective-permute-start(bf16[1536,128]{1,0:T(8,128)(2,1)S(1)} %add_convert_fusion.22), channel_id=1, source_target_pairs={{8,16},{16,8},{9,17},{17,9},{10,18},{18,10},{11,19},{19,11},{12,20... | collective-permute-start | bytes 1179656 | tf_op jit(solution)/shard_map/ppermute | solution.py:114
  126.5 11.3 %collective-permute-start.28 = (bf16[1536,128]{1,0:T(8,128)(2,1)S(1)}, bf16[1536,128]{1,0:T(8,128)(2,1)S(1)}, u32[]{:S(2)}, u32[]{:S(2)}) collective-permute-start(bf16[1536,128]{1,0:T(8,128)(2,1)S(1)} %fusion.64), channel_id=1, source_target_pairs={{0,8},{24,16},{8,0},{16,24},{1,9},{25,17},{9,1},{17,25},{2,10},{26... | collective-permute-start | bytes 1179656 | tf_op jit(solution)/shard_map/ppermute | solution.py:106
  129.9 8.7 %collective-permute-start.27 = (bf16[1536,128]{1,0:T(8,128)(2,1)S(1)}, bf16[1536,128]{1,0:T(8,128)(2,1)S(1)}, u32[]{:S(2)}, u32[]{:S(2)}) collective-permute-start(bf16[1536,128]{1,0:T(8,128)(2,1)S(1)} %add_convert_fusion.20), channel_id=1, source_target_pairs={{8,16},{16,8},{9,17},{17,9},{10,18},{18,10},{11,19},{19,11},{12,20... | collective-permute-start | bytes 1179656 | tf_op jit(solution)/shard_map/ppermute | solution.py:114
  133.0 14.5 %collective-permute-start.30 = (bf16[1536,128]{1,0:T(8,128)(2,1)S(1)}, bf16[1536,128]{1,0:T(8,128)(2,1)S(1)}, u32[]{:S(2)}, u32[]{:S(2)}) collective-permute-start(bf16[1536,128]{1,0:T(8,128)(2,1)S(1)} %fusion.65), channel_id=1, source_target_pairs={{0,8},{24,16},{8,0},{16,24},{1,9},{25,17},{9,1},{17,25},{2,10},{26... | collective-permute-start | bytes 1179656 | tf_op jit(solution)/shard_map/ppermute | solution.py:106
  137.9 10.6 %collective-permute-start.31 = (bf16[1536,128]{1,0:T(8,128)(2,1)S(1)}, bf16[1536,128]{1,0:T(8,128)(2,1)S(1)}, u32[]{:S(2)}, u32[]{:S(2)}) collective-permute-start(bf16[1536,128]{1,0:T(8,128)(2,1)S(1)} %add_convert_fusion.18), channel_id=1, source_target_pairs={{8,16},{16,8},{9,17},{17,9},{10,18},{18,10},{11,19},{19,11},{12,20... | collective-permute-start | bytes 1179656 | tf_op jit(solution)/shard_map/ppermute | solution.py:114
  138.8 17.1 %collective-permute-start.29 = (bf16[1536,128]{1,0:T(8,128)(2,1)S(1)}, bf16[1536,128]{1,0:T(8,128)(2,1)S(1)}, u32[]{:S(2)}, u32[]{:S(2)}) collective-permute-start(bf16[1536,128]{1,0:T(8,128)(2,1)S(1)} %fusion.66), channel_id=1, source_target_pairs={{0,8},{24,16},{8,0},{16,24},{1,9},{25,17},{9,1},{17,25},{2,10},{26... | collective-permute-start | bytes 1179656 | tf_op jit(solution)/shard_map/ppermute | solution.py:106
  147.6 11.4 %collective-permute-start.34 = (bf16[1536,128]{1,0:T(8,128)(2,1)S(1)}, bf16[1536,128]{1,0:T(8,128)(2,1)S(1)}, u32[]{:S(2)}, u32[]{:S(2)}) collective-permute-start(bf16[1536,128]{1,0:T(8,128)(2,1)S(1)} %add_convert_fusion.16), channel_id=1, source_target_pairs={{8,16},{16,8},{9,17},{17,9},{10,18},{18,10},{11,19},{19,11},{12,20... | collective-permute-start | bytes 1179656 | tf_op jit(solution)/shard_map/ppermute | solution.py:114
  148.7 15.3 %collective-permute-start.33 = (bf16[1536,128]{1,0:T(8,128)(2,1)S(1)}, bf16[1536,128]{1,0:T(8,128)(2,1)S(1)}, u32[]{:S(2)}, u32[]{:S(2)}) collective-permute-start(bf16[1536,128]{1,0:T(8,128)(2,1)S(1)} %fusion.67), channel_id=1, source_target_pairs={{0,8},{24,16},{8,0},{16,24},{1,9},{25,17},{9,1},{17,25},{2,10},{26... | collective-permute-start | bytes 1179656 | tf_op jit(solution)/shard_map/ppermute | solution.py:106
  158.2 6.6 %collective-permute-start.32 = (bf16[1536,128]{1,0:T(8,128)(2,1)S(1)}, bf16[1536,128]{1,0:T(8,128)(2,1)S(1)}, u32[]{:S(2)}, u32[]{:S(2)}) collective-permute-start(bf16[1536,128]{1,0:T(8,128)(2,1)S(1)} %add_convert_fusion.14), channel_id=1, source_target_pairs={{8,16},{16,8},{9,17},{17,9},{10,18},{18,10},{11,19},{19,11},{12,20... | collective-permute-start | bytes 1179656 | tf_op jit(solution)/shard_map/ppermute | solution.py:114
  159.2 15.9 %collective-permute-start.36 = (bf16[1536,128]{1,0:T(8,128)(2,1)S(1)}, bf16[1536,128]{1,0:T(8,128)(2,1)S(1)}, u32[]{:S(2)}, u32[]{:S(2)}) collective-permute-start(bf16[1536,128]{1,0:T(8,128)(2,1)S(1)} %fusion.68), channel_id=1, source_target_pairs={{0,8},{24,16},{8,0},{16,24},{1,9},{25,17},{9,1},{17,25},{2,10},{26... | collective-permute-start | bytes 1179656 | tf_op jit(solution)/shard_map/ppermute | solution.py:106
  164.1 11.9 %collective-permute-start.35 = (bf16[1536,128]{1,0:T(8,128)(2,1)S(1)}, bf16[1536,128]{1,0:T(8,128)(2,1)S(1)}, u32[]{:S(2)}, u32[]{:S(2)}) collective-permute-start(bf16[1536,128]{1,0:T(8,128)(2,1)S(1)} %add_convert_fusion.12), channel_id=1, source_target_pairs={{8,16},{16,8},{9,17},{17,9},{10,18},{18,10},{11,19},{19,11},{12,20... | collective-permute-start | bytes 1179656 | tf_op jit(solution)/shard_map/ppermute | solution.py:114
  165.0 16.9 %collective-permute-start.38 = (bf16[1536,128]{1,0:T(8,128)(2,1)S(1)}, bf16[1536,128]{1,0:T(8,128)(2,1)S(1)}, u32[]{:S(2)}, u32[]{:S(2)}) collective-permute-start(bf16[1536,128]{1,0:T(8,128)(2,1)S(1)} %fusion.69), channel_id=1, source_target_pairs={{0,8},{24,16},{8,0},{16,24},{1,9},{25,17},{9,1},{17,25},{2,10},{26... | collective-permute-start | bytes 1179656 | tf_op jit(solution)/shard_map/ppermute | solution.py:106
  175.2 7.6 %collective-permute-start.37 = (bf16[1536,128]{1,0:T(8,128)(2,1)S(1)}, bf16[1536,128]{1,0:T(8,128)(2,1)S(1)}, u32[]{:S(2)}, u32[]{:S(2)}) collective-permute-start(bf16[1536,128]{1,0:T(8,128)(2,1)S(1)} %add_convert_fusion.10), channel_id=1, source_target_pairs={{8,16},{16,8},{9,17},{17,9},{10,18},{18,10},{11,19},{19,11},{12,20... | collective-permute-start | bytes 1179656 | tf_op jit(solution)/shard_map/ppermute | solution.py:114
  176.2 14.4 %collective-permute-start.40 = (bf16[1536,128]{1,0:T(8,128)(2,1)S(1)}, bf16[1536,128]{1,0:T(8,128)(2,1)S(1)}, u32[]{:S(2)}, u32[]{:S(2)}) collective-permute-start(bf16[1536,128]{1,0:T(8,128)(2,1)S(1)} %fusion.70), channel_id=1, source_target_pairs={{0,8},{24,16},{8,0},{16,24},{1,9},{25,17},{9,1},{17,25},{2,10},{26... | collective-permute-start | bytes 1179656 | tf_op jit(solution)/shard_map/ppermute | solution.py:106
  182.1 9.4 %collective-permute-start.41 = (bf16[1536,128]{1,0:T(8,128)(2,1)S(1)}, bf16[1536,128]{1,0:T(8,128)(2,1)S(1)}, u32[]{:S(2)}, u32[]{:S(2)}) collective-permute-start(bf16[1536,128]{1,0:T(8,128)(2,1)S(1)} %add_convert_fusion.8), channel_id=1, source_target_pairs={{8,16},{16,8},{9,17},{17,9},{10,18},{18,10},{11,19},{19,11},{12,20... | collective-permute-start | bytes 1179656 | tf_op jit(solution)/shard_map/ppermute | solution.py:114
  183.0 16.0 %collective-permute-start.39 = (bf16[1536,128]{1,0:T(8,128)(2,1)S(1)}, bf16[1536,128]{1,0:T(8,128)(2,1)S(1)}, u32[]{:S(2)}, u32[]{:S(2)}) collective-permute-start(bf16[1536,128]{1,0:T(8,128)(2,1)S(1)} %fusion.71), channel_id=1, source_target_pairs={{0,8},{24,16},{8,0},{16,24},{1,9},{25,17},{9,1},{17,25},{2,10},{26... | collective-permute-start | bytes 1179656 | tf_op jit(solution)/shard_map/ppermute | solution.py:106
  190.7 9.1 %collective-permute-start.44 = (bf16[1536,128]{1,0:T(8,128)(2,1)S(1)}, bf16[1536,128]{1,0:T(8,128)(2,1)S(1)}, u32[]{:S(2)}, u32[]{:S(2)}) collective-permute-start(bf16[1536,128]{1,0:T(8,128)(2,1)S(1)} %add_convert_fusion.6), channel_id=1, source_target_pairs={{8,16},{16,8},{9,17},{17,9},{10,18},{18,10},{11,19},{19,11},{12,20... | collective-permute-start | bytes 1179656 | tf_op jit(solution)/shard_map/ppermute | solution.py:114
  191.6 16.4 %collective-permute-start.43 = (bf16[1536,128]{1,0:T(8,128)(2,1)S(1)}, bf16[1536,128]{1,0:T(8,128)(2,1)S(1)}, u32[]{:S(2)}, u32[]{:S(2)}) collective-permute-start(bf16[1536,128]{1,0:T(8,128)(2,1)S(1)} %fusion.72), channel_id=1, source_target_pairs={{0,8},{24,16},{8,0},{16,24},{1,9},{25,17},{9,1},{17,25},{2,10},{26... | collective-permute-start | bytes 1179656 | tf_op jit(solution)/shard_map/ppermute | solution.py:106
  199.2 12.3 %collective-permute-start.42 = (bf16[1536,128]{1,0:T(8,128)(2,1)S(1)}, bf16[1536,128]{1,0:T(8,128)(2,1)S(1)}, u32[]{:S(2)}, u32[]{:S(2)}) collective-permute-start(bf16[1536,128]{1,0:T(8,128)(2,1)S(1)} %add_convert_fusion.4), channel_id=1, source_target_pairs={{8,16},{16,8},{9,17},{17,9},{10,18},{18,10},{11,19},{19,11},{12,20... | collective-permute-start | bytes 1179656 | tf_op jit(solution)/shard_map/ppermute | solution.py:114
  200.0 16.9 %collective-permute-start.48 = (bf16[1536,128]{1,0:T(8,128)(2,1)S(1)}, bf16[1536,128]{1,0:T(8,128)(2,1)S(1)}, u32[]{:S(2)}, u32[]{:S(2)}) collective-permute-start(bf16[1536,128]{1,0:T(8,128)(2,1)S(1)} %add_convert_fusion.3), channel_id=1, source_target_pairs={{8,0},{16,24},{9,1},{17,25},{10,2},{18,26},{11,3},{19,27},{12,4},{... | collective-permute-start | bytes 1179656 | tf_op jit(solution)/shard_map/ppermute | solution.py:106
  208.2 7.3 %collective-permute-start.45 = (bf16[1536,128]{1,0:T(8,128)(2,1)S(1)}, bf16[1536,128]{1,0:T(8,128)(2,1)S(1)}, u32[]{:S(2)}, u32[]{:S(2)}) collective-permute-start(bf16[1536,128]{1,0:T(8,128)(2,1)S(1)} %add_convert_fusion.2), channel_id=1, source_target_pairs={{8,16},{16,8},{9,17},{17,9},{10,18},{18,10},{11,19},{19,11},{12,20... | collective-permute-start | bytes 1179656 | tf_op jit(solution)/shard_map/ppermute | solution.py:114
  211.6 13.6 %collective-permute-start.47 = (bf16[1536,128]{1,0:T(8,128)(2,1)S(1)}, bf16[1536,128]{1,0:T(8,128)(2,1)S(1)}, u32[]{:S(2)}, u32[]{:S(2)}) collective-permute-start(bf16[1536,128]{1,0:T(8,128)(2,1)S(1)} %add_convert_fusion), channel_id=1, source_target_pairs={{8,0},{16,24},{9,1},{17,25},{10,2},{18,26},{11,3},{19,27},{12,4},{... | collective-permute-start | bytes 1179656 | tf_op jit(solution)/shard_map/ppermute | solution.py:106
  215.6 13.9 %collective-permute-start.46 = (bf16[1536,128]{1,0:T(8,128)(2,1)S(1)}, bf16[1536,128]{1,0:T(8,128)(2,1)S(1)}, u32[]{:S(2)}, u32[]{:S(2)}) collective-permute-start(bf16[1536,128]{1,0:T(8,128)(2,1)S(1)} %add_convert_fusion.1), channel_id=1, source_target_pairs={{8,0},{16,24},{9,1},{17,25},{10,2},{18,26},{11,3},{19,27},{12,4},{... | collective-permute-start | bytes 1179656 | tf_op jit(solution)/shard_map/ppermute | solution.py:106
  (18 other events, 219.5 us)

commit v22 on v17

--- a/solution.py
+++ b/solution.py
@@ -174,17 +174,20 @@
 
     gain_part = lax.dynamic_slice_in_dim(gain, t * (width // 2) + low * cols, cols).astype(f32)
 
+    ready = [
+        lax.optimization_barrier(gain_part[None, :] * cot.astype(f32)) for cot in cotangent_parts
+    ]
     hidden, weighted, sums = [], [], []
     for k in range(group * pieces):
         r, p = k // pieces, k % pieces
         span, long_span = slice(p * rows, (p + 1) * rows), slice(k * rows, (k + 1) * rows)
-        res, cot, came = residual_parts[r], cotangent_parts[r], passed[k]
+        res, came = residual_parts[r], passed[k]
         if sums:
             came, sums[-1] = together(came, sums[-1])
         keep = jnp.where(near, near_out[long_span], far_outs[k])
         came = jnp.where(near, near_came[long_span], came)
         h = res[span].astype(f32) + keep.astype(f32) + came.astype(f32)
-        w = gain_part[None, :] * cot[span].astype(f32)
+        w = ready[r][span]
         hidden.append(h)
         weighted.append(w)
         sums.append(jnp.stack([jnp.sum(h * h, axis=-1), jnp.sum(h * w, axis=-1)]))

time: 232 us -> 230 us (level)
  waiting for transfers between devices: 75.7 us -> 79.6 us
  other arithmetic: 13 us -> 10.3 us
  local copies, waits for them, and re-layouts: 8.57 us -> 6.15 us
    reduce_sum x4, other arithmetic: 6.95 us -> 3.99 us  [body(): sums.append(jnp.stack([jnp.sum(h * h, axis=-1), jnp.sum(h * w, axis=-1)]))]
    unnamed x37 -> x25, local copies, waits for them, and re-layouts: 5.06 us -> 2.49 us
  transfers between devices with their start and end apart: 49 -> 49, of which waited for: 22 -> 20; matrix products, arithmetic and copies ran while one was open for 19% -> 17% of each run, Pallas kernels for 4% -> 4%
where the time goes in v22:
time: 230 us; the launch traced here: 227 us
  starting transfers between devices  95 us (41%)
  waiting for transfers between devices  79.6 us (35%)
  matrix products  22.9 us (10%)
  Pallas kernels  11 us (5%)
  other arithmetic  10.3 us (4%)
  local copies, waits for them, and re-layouts  6.15 us (3%)
    ppermute x15, starting transfers between devices, send_outer(): self.edge[s] = lax.ppermute(payload, 'island', pairs)  61.3 us
    ppermute x11, waiting for transfers between devices, swap(): return lax.ppermute(value, axis, [(i, i ^ bit) for i in range(count)])  35.6 us
    ppermute x15, waiting for transfers between devices, send_outer(): self.edge[s] = lax.ppermute(payload, 'island', pairs)  28.3 us
    dot_general x7, matrix products, add_pseudo(): lax.dot_general(context_all, piece, (((0,), (0,)), ((), ())), preferred_e...  13.7 us
    pallas_call x5, Pallas kernels, finish(): pl.pallas_call(functools.partial(finish_kernel, count, start, narrow, isl...  11 us
    ppermute x3, starting transfers between devices, move(): crosses.append(lax.ppermute(d_local, ('fsdp', 'tp'), cross_pairs))  10.1 us
    dot_general x3, matrix products, project(): jnp.dot(block, weight, preferred_element_type=f32).astype(bf16)  9.1 us
    ppermute x12, starting transfers between devices, step(): self.mid[s] = lax.ppermute(self.sums[s], 'island', [(1, 2), (2, 1)])  8.58 us
  transfers between devices with their start and end apart: 49, of which 20 were waited for; matrix products, arithmetic and copies ran while one was open for 17% of the time, Pallas kernels for 4%

profile of v22, /device:TPU:2, one launch (start us, length us, event | category | flops | bytes accessed | tf_op | source)
XLA Modules:
  0.0 226.7 jit_solution(731403166775526703)
XLA Ops:
  0.6 1.6 collective-permute-start
  2.2 2.5 %constant_dynamic-slice_fusion.2 = (bf16[256,1536]{1,0:T(8,128)(2,1)}, bf16[256,1536]{1,0:T(8,128)(2,1)S(1)}) fusion(bf16[256,3072]{1,0:T(8,128)(2,1)} %param.9, s32[]{:T(128)S(6)} %select_n.188, s32[]{:T(128)S(6)} %select_n.187), kind=kLoop, calls=%fused_computation.230 | loop fusion | bytes 3145736 | tf_op jit(solution)/shard_map/dynamic_slice | solution.py:160
  7.0 13.3 %collective-permute-done = bf16[256,1536]{1,0:T(8,128)(2,1)} collective-permute-done((bf16[256,1536]{1,0:T(8,128)(2,1)}, bf16[256,1536]{1,0:T(8,128)(2,1)}, u32[]{:S(2)}, u32[]{:S(2)}) %collective-permute-start) | collective-permute-done | bytes 786464 | tf_op jit(solution)/shard_map/ppermute | solution.py:31
  20.4 4.0 %convolution_convert_fusion.2 = bf16[256,1536]{1,0:T(8,128)(2,1)S(1)} fusion(bf16[256,1536]{1,0:T(8,128)(2,1)} %collective-permute-done, bf16[1536,1536]{1,0:T(8,128)(2,1)} %param.12), kind=kOutput, calls=%fused_computation.8 | convolution fusion | flops 1208352768 | bytes 6291456 | tf_op jit(solution)/shard_map/dot_general | solution.py:144
  24.4 1.6 collective-permute-start.6
  26.1 3.7 %convolution_convert_fusion = bf16[512,1536]{1,0:T(8,128)(2,1)S(1)} fusion(bf16[1536,1536]{1,0:T(8,128)(2,1)S(1)} %bitcast.206, bf16[256,1536]{1,0:T(8,128)(2,1)} %collective-permute-done.5, bf16[256,1536]{1,0:T(8,128)(2,1)S(1)} %copy-done.1), kind=kOutput, calls=%fused_computation | convolution fusion | flops 2419851264 | bytes 7864320 | tf_op jit(solution)/shard_map/dot_general | solution.py:144
  30.4 2.3 %collective-permute-start.7 = (bf16[512,1536]{1,0:T(8,128)(2,1)S(1)}, bf16[512,1536]{1,0:T(8,128)(2,1)S(1)}, u32[]{:S(2)}, u32[]{:S(2)}) collective-permute-start(bf16[512,1536]{1,0:T(8,128)(2,1)S(1)} %convolution_convert_fusion), channel_id=1, source_target_pairs={{4,5},{1,0},{6,7},{3,2},{12,13},{9,8},{14,15},{11,10},{20,21},{17,... | collective-permute-start | bytes 4718600 | tf_op jit(solution)/shard_map/ppermute | solution.py:168
  32.7 3.8 %collective-permute-done.6 = bf16[128,1536]{1,0:T(8,128)(2,1)S(1)} collective-permute-done((bf16[128,1536]{1,0:T(8,128)(2,1)S(1)}, bf16[128,1536]{1,0:T(8,128)(2,1)S(1)}, u32[]{:S(2)}, u32[]{:S(2)}) %collective-permute-start.6) | collective-permute-done | bytes 393248 | tf_op jit(solution)/shard_map/ppermute | solution.py:31
  39.2 2.8 %collective-permute-start.10 = (bf16[128,1536]{1,0:T(8,128)(2,1)S(1)}, bf16[128,1536]{1,0:T(8,128)(2,1)S(1)}, u32[]{:S(2)}, u32[]{:S(2)}) collective-permute-start(bf16[128,1536]{1,0:T(8,128)(2,1)S(1)} %get-tuple-element.328), channel_id=1, source_target_pairs={{0,4},{2,6},{4,0},{6,2},{1,5},{3,7},{5,1},{7,3},{8,12},{10,14},{12... | collective-permute-start | bytes 1179656 | tf_op jit(solution)/shard_map/ppermute | solution.py:31
  46.1 7.1 %collective-permute-done.10 = bf16[128,1536]{1,0:T(8,128)(2,1)S(1)} collective-permute-done((bf16[128,1536]{1,0:T(8,128)(2,1)S(1)}, bf16[128,1536]{1,0:T(8,128)(2,1)S(1)}, u32[]{:S(2)}, u32[]{:S(2)}) %collective-permute-start.10) | collective-permute-done | bytes 393248 | tf_op jit(solution)/shard_map/ppermute | solution.py:31
  54.6 6.7 %collective-permute-done.12 = bf16[128,1536]{1,0:T(8,128)(2,1)S(1)} collective-permute-done((bf16[128,1536]{1,0:T(8,128)(2,1)S(1)}, bf16[128,1536]{1,0:T(8,128)(2,1)S(1)}, u32[]{:S(2)}, u32[]{:S(2)}) %collective-permute-start.12) | collective-permute-done | bytes 393248 | tf_op jit(solution)/shard_map/ppermute | solution.py:31
  62.6 3.7 %collective-permute-done.7 = bf16[512,1536]{1,0:T(8,128)(2,1)S(1)} collective-permute-done((bf16[512,1536]{1,0:T(8,128)(2,1)S(1)}, bf16[512,1536]{1,0:T(8,128)(2,1)S(1)}, u32[]{:S(2)}, u32[]{:S(2)}) %collective-permute-start.7) | collective-permute-done | bytes 1572896 | tf_op jit(solution)/shard_map/ppermute | solution.py:168
  67.2 1.7 multiply_reduce_fusion.1
  68.9 4.9 %collective-permute-done.13 = bf16[128,1536]{1,0:T(8,128)(2,1)S(1)} collective-permute-done((bf16[128,1536]{1,0:T(8,128)(2,1)S(1)}, bf16[128,1536]{1,0:T(8,128)(2,1)S(1)}, u32[]{:S(2)}, u32[]{:S(2)}) %collective-permute-start.13) | collective-permute-done | bytes 393248 | tf_op jit(solution)/shard_map/ppermute | solution.py:173
  76.8 3.5 %collective-permute-done.15 = f32[2,512]{1,0:T(2,128)S(1)} collective-permute-done((f32[2,512]{1,0:T(2,128)S(1)}, f32[2,512]{1,0:T(2,128)S(1)}, u32[]{:S(2)}, u32[]{:S(2)}) %collective-permute-start.15) | collective-permute-done | bytes 4128 | tf_op jit(solution)/shard_map/ppermute | solution.py:31
  80.7 3.4 %collective-permute-start.16 = (bf16[512,128]{1,0:T(8,128)(2,1)S(1)}, bf16[512,128]{1,0:T(8,128)(2,1)S(1)}, u32[]{:S(2)}, u32[]{:S(2)}) collective-permute-start(bf16[512,128]{1,0:T(8,128)(2,1)S(1)} %pad_maximum_fusion.5), channel_id=1, source_target_pairs={{4,1},{1,4},{6,3},{3,6},{12,9},{9,12},{14,11},{11,14},{20,17},{17,... | collective-permute-start | bytes 393224 | tf_op jit(solution)/shard_map/ppermute | solution.py:231
  85.6 3.4 %collective-permute-start.21 = (bf16[512,384]{1,0:T(8,128)(2,1)S(1)}, bf16[512,384]{1,0:T(8,128)(2,1)S(1)}, u32[]{:S(2)}, u32[]{:S(2)}) collective-permute-start(bf16[512,384]{1,0:T(8,128)(2,1)S(1)} %pad_maximum_fusion.2), channel_id=1, source_target_pairs={{4,1},{1,4},{6,3},{3,6},{12,9},{9,12},{14,11},{11,14},{20,17},{17,... | collective-permute-start | bytes 1179656 | tf_op jit(solution)/shard_map/ppermute | solution.py:231
  89.1 3.3 %collective-permute-start.18 = (bf16[512,1024]{1,0:T(8,128)(2,1)S(1)}, bf16[512,1024]{1,0:T(8,128)(2,1)S(1)}, u32[]{:S(2)}, u32[]{:S(2)}) collective-permute-start(bf16[512,1024]{1,0:T(8,128)(2,1)S(1)} %pad_maximum_fusion), channel_id=1, source_target_pairs={{4,1},{1,4},{6,3},{3,6},{12,9},{9,12},{14,11},{11,14},{20,17},{17,... | collective-permute-start | bytes 3145736 | tf_op jit(solution)/shard_map/ppermute | solution.py:231
  94.1 3.7 %collective-permute-start.22 = (bf16[1536,128]{1,0:T(8,128)(2,1)S(1)}, bf16[1536,128]{1,0:T(8,128)(2,1)S(1)}, u32[]{:S(2)}, u32[]{:S(2)}) collective-permute-start(bf16[1536,128]{1,0:T(8,128)(2,1)S(1)} %fusion.55), channel_id=1, source_target_pairs={{0,8},{24,16},{1,9},{25,17},{2,10},{26,18},{3,11},{27,19},{4,12},{... | collective-permute-start | bytes 1179656 | tf_op jit(solution)/shard_map/ppermute | solution.py:107
  97.8 2.6 %collective-permute-done.21 = bf16[512,384]{1,0:T(8,128)(2,1)S(1)} collective-permute-done((bf16[512,384]{1,0:T(8,128)(2,1)S(1)}, bf16[512,384]{1,0:T(8,128)(2,1)S(1)}, u32[]{:S(2)}, u32[]{:S(2)}) %collective-permute-start.21) | collective-permute-done | bytes 393248 | tf_op jit(solution)/shard_map/ppermute | solution.py:231
  102.7 2.2 fusion.33
  104.9 3.5 %collective-permute-start.23 = (bf16[1536,128]{1,0:T(8,128)(2,1)S(1)}, bf16[1536,128]{1,0:T(8,128)(2,1)S(1)}, u32[]{:S(2)}, u32[]{:S(2)}) collective-permute-start(bf16[1536,128]{1,0:T(8,128)(2,1)S(1)} %fusion.54), channel_id=1, source_target_pairs={{0,8},{24,16},{1,9},{25,17},{2,10},{26,18},{3,11},{27,19},{4,12},{... | collective-permute-start | bytes 1179656 | tf_op jit(solution)/shard_map/ppermute | solution.py:107
  109.2 4.1 %collective-permute-start.25 = (bf16[1536,128]{1,0:T(8,128)(2,1)S(1)}, bf16[1536,128]{1,0:T(8,128)(2,1)S(1)}, u32[]{:S(2)}, u32[]{:S(2)}) collective-permute-start(bf16[1536,128]{1,0:T(8,128)(2,1)S(1)} %slice.474), channel_id=1, source_target_pairs={{0,8},{24,16},{1,9},{25,17},{2,10},{26,18},{3,11},{27,19},{4,12},{... | collective-permute-start | bytes 1179656 | tf_op jit(solution)/shard_map/ppermute | solution.py:107
  113.3 3.7 %collective-permute-done.23 = bf16[1536,128]{1,0:T(8,128)(2,1)S(1)} collective-permute-done((bf16[1536,128]{1,0:T(8,128)(2,1)S(1)}, bf16[1536,128]{1,0:T(8,128)(2,1)S(1)}, u32[]{:S(2)}, u32[]{:S(2)}) %collective-permute-start.23) | collective-permute-done | bytes 393248 | tf_op jit(solution)/shard_map/ppermute | solution.py:107
  117.9 2.4 %collective-permute-done.18 = bf16[512,1024]{1,0:T(8,128)(2,1)S(1)} collective-permute-done((bf16[512,1024]{1,0:T(8,128)(2,1)S(1)}, bf16[512,1024]{1,0:T(8,128)(2,1)S(1)}, u32[]{:S(2)}, u32[]{:S(2)}) %collective-permute-start.18) | collective-permute-done | bytes 1048608 | tf_op jit(solution)/shard_map/ppermute | solution.py:231
  120.9 2.2 fusion.34
  123.3 2.2 collective-permute-start.28
  126.2 2.2 fusion.35
  128.6 4.6 %collective-permute-start.30 = (bf16[1536,128]{1,0:T(8,128)(2,1)S(1)}, bf16[1536,128]{1,0:T(8,128)(2,1)S(1)}, u32[]{:S(2)}, u32[]{:S(2)}) collective-permute-start(bf16[1536,128]{1,0:T(8,128)(2,1)S(1)} %fusion.69), channel_id=1, source_target_pairs={{0,8},{24,16},{8,0},{16,24},{1,9},{25,17},{9,1},{17,25},{2,10},{26... | collective-permute-start | bytes 1179656 | tf_op jit(solution)/shard_map/ppermute | solution.py:107
  134.2 6.1 %collective-permute-start.29 = (bf16[1536,128]{1,0:T(8,128)(2,1)S(1)}, bf16[1536,128]{1,0:T(8,128)(2,1)S(1)}, u32[]{:S(2)}, u32[]{:S(2)}) collective-permute-start(bf16[1536,128]{1,0:T(8,128)(2,1)S(1)} %fusion.70), channel_id=1, source_target_pairs={{0,8},{24,16},{8,0},{16,24},{1,9},{25,17},{9,1},{17,25},{2,10},{26... | collective-permute-start | bytes 1179656 | tf_op jit(solution)/shard_map/ppermute | solution.py:107
  140.4 2.8 %collective-permute-done.30 = bf16[1536,128]{1,0:T(8,128)(2,1)S(1)} collective-permute-done((bf16[1536,128]{1,0:T(8,128)(2,1)S(1)}, bf16[1536,128]{1,0:T(8,128)(2,1)S(1)}, u32[]{:S(2)}, u32[]{:S(2)}) %collective-permute-start.30) | collective-permute-done | bytes 393248 | tf_op jit(solution)/shard_map/ppermute | solution.py:107
  144.4 4.8 %collective-permute-start.33 = (bf16[1536,128]{1,0:T(8,128)(2,1)S(1)}, bf16[1536,128]{1,0:T(8,128)(2,1)S(1)}, u32[]{:S(2)}, u32[]{:S(2)}) collective-permute-start(bf16[1536,128]{1,0:T(8,128)(2,1)S(1)} %fusion.71), channel_id=1, source_target_pairs={{0,8},{24,16},{8,0},{16,24},{1,9},{25,17},{9,1},{17,25},{2,10},{26... | collective-permute-start | bytes 1179656 | tf_op jit(solution)/shard_map/ppermute | solution.py:107
  149.1 2.5 %collective-permute-done.29 = bf16[1536,128]{1,0:T(8,128)(2,1)S(1)} collective-permute-done((bf16[1536,128]{1,0:T(8,128)(2,1)S(1)}, bf16[1536,128]{1,0:T(8,128)(2,1)S(1)}, u32[]{:S(2)}, u32[]{:S(2)}) %collective-permute-start.29) | collective-permute-done | bytes 393248 | tf_op jit(solution)/shard_map/ppermute | solution.py:107
  151.7 2.2 fusion.37
  155.0 4.2 %collective-permute-start.36 = (bf16[1536,128]{1,0:T(8,128)(2,1)S(1)}, bf16[1536,128]{1,0:T(8,128)(2,1)S(1)}, u32[]{:S(2)}, u32[]{:S(2)}) collective-permute-start(bf16[1536,128]{1,0:T(8,128)(2,1)S(1)} %fusion.72), channel_id=1, source_target_pairs={{0,8},{24,16},{8,0},{16,24},{1,9},{25,17},{9,1},{17,25},{2,10},{26... | collective-permute-start | bytes 1179656 | tf_op jit(solution)/shard_map/ppermute | solution.py:107
  159.2 2.6 %shard_map.95 = (f32[1536,1536]{1,0:T(8,128)}, bf16[1536,1536]{1,0:T(8,128)(2,1)}) custom-call(bf16[1536,128]{1,0:T(8,128)(2,1)S(1)} %broadcast_select_fusion.6.refs_0_, bf16[1536,128]{1,0:T(8,128)(2,1)S(1)} %broadcast_select_fusion.5.refs_1_, bf16[1536,128]{1,0:T(8,128)(2,1)S(1)} %broadcast_select_fusion.4.refs_2_, f32[1536,1536]{1,0:T(8,128)S(1)} %bitcast.192), custom_call_target="tpu_custom_call" | custom-call | flops 2949120 | bytes 7077888 | tf_op jit(solution)/shard_map/pallas_call | solution.py:61
  162.8 7.0 %collective-permute-start.38 = (bf16[1536,128]{1,0:T(8,128)(2,1)S(1)}, bf16[1536,128]{1,0:T(8,128)(2,1)S(1)}, u32[]{:S(2)}, u32[]{:S(2)}) collective-permute-start(bf16[1536,128]{1,0:T(8,128)(2,1)S(1)} %fusion.73), channel_id=1, source_target_pairs={{0,8},{24,16},{8,0},{16,24},{1,9},{25,17},{9,1},{17,25},{2,10},{26... | collective-permute-start | bytes 1179656 | tf_op jit(solution)/shard_map/ppermute | solution.py:107
  169.8 2.2 fusion.36
  173.1 5.2 %collective-permute-start.40 = (bf16[1536,128]{1,0:T(8,128)(2,1)S(1)}, bf16[1536,128]{1,0:T(8,128)(2,1)S(1)}, u32[]{:S(2)}, u32[]{:S(2)}) collective-permute-start(bf16[1536,128]{1,0:T(8,128)(2,1)S(1)} %fusion.74), channel_id=1, source_target_pairs={{0,8},{24,16},{8,0},{16,24},{1,9},{25,17},{9,1},{17,25},{2,10},{26... | collective-permute-start | bytes 1179656 | tf_op jit(solution)/shard_map/ppermute | solution.py:107
  179.3 7.4 %collective-permute-start.39 = (bf16[1536,128]{1,0:T(8,128)(2,1)S(1)}, bf16[1536,128]{1,0:T(8,128)(2,1)S(1)}, u32[]{:S(2)}, u32[]{:S(2)}) collective-permute-start(bf16[1536,128]{1,0:T(8,128)(2,1)S(1)} %fusion.75), channel_id=1, source_target_pairs={{0,8},{24,16},{8,0},{16,24},{1,9},{25,17},{9,1},{17,25},{2,10},{26... | collective-permute-start | bytes 1179656 | tf_op jit(solution)/shard_map/ppermute | solution.py:107
  186.7 2.6 %shard_map.96 = (f32[1536,1536]{1,0:T(8,128)}, bf16[1536,1536]{1,0:T(8,128)(2,1)}) custom-call(bf16[1536,128]{1,0:T(8,128)(2,1)S(1)} %broadcast_select_fusion.9.refs_0_, bf16[1536,128]{1,0:T(8,128)(2,1)S(1)} %broadcast_select_fusion.8.refs_1_, bf16[1536,128]{1,0:T(8,128)(2,1)S(1)} %broadcast_select_fusion.7.refs_2_, ...), custom_call_target="tpu_custom_call", output_to_operand_aliasing={{0}: (4, {}), {1}: (5, {})} | custom-call | flops 2949120 | bytes 7077888 | tf_op jit(solution)/shard_map/pallas_call | solution.py:61
  190.3 4.8 %collective-permute-start.43 = (bf16[1536,128]{1,0:T(8,128)(2,1)S(1)}, bf16[1536,128]{1,0:T(8,128)(2,1)S(1)}, u32[]{:S(2)}, u32[]{:S(2)}) collective-permute-start(bf16[1536,128]{1,0:T(8,128)(2,1)S(1)} %fusion.76), channel_id=1, source_target_pairs={{0,8},{24,16},{8,0},{16,24},{1,9},{25,17},{9,1},{17,25},{2,10},{26... | collective-permute-start | bytes 1179656 | tf_op jit(solution)/shard_map/ppermute | solution.py:107
  197.4 6.8 %collective-permute-done.43 = bf16[1536,128]{1,0:T(8,128)(2,1)S(1)} collective-permute-done((bf16[1536,128]{1,0:T(8,128)(2,1)S(1)}, bf16[1536,128]{1,0:T(8,128)(2,1)S(1)}, u32[]{:S(2)}, u32[]{:S(2)}) %collective-permute-start.43) | collective-permute-done | bytes 393248 | tf_op jit(solution)/shard_map/ppermute | solution.py:107
  206.5 2.6 %shard_map.97 = (f32[1536,1536]{1,0:T(8,128)}, bf16[1536,1536]{1,0:T(8,128)(2,1)}) custom-call(bf16[1536,128]{1,0:T(8,128)(2,1)S(1)} %broadcast_select_fusion.12.refs_0_, bf16[1536,128]{1,0:T(8,128)(2,1)S(1)} %broadcast_select_fusion.11.refs_1_, bf16[1536,128]{1,0:T(8,128)(2,1)S(1)} %broadcast_select_fusion.10.refs_2_, ...), custom_call_target="tpu_custom_call", output_to_operand_aliasing={{0}: (4, {}), {1}: (5, {})} | custom-call | flops 2949120 | bytes 7077888 | tf_op jit(solution)/shard_map/pallas_call | solution.py:61
  210.5 2.1 collective-permute-done.48
  212.7 8.3 %collective-permute-done.47 = bf16[1536,128]{1,0:T(8,128)(2,1)S(1)} collective-permute-done((bf16[1536,128]{1,0:T(8,128)(2,1)S(1)}, bf16[1536,128]{1,0:T(8,128)(2,1)S(1)}, u32[]{:S(2)}, u32[]{:S(2)}) %collective-permute-start.47) | collective-permute-done | bytes 393248 | tf_op jit(solution)/shard_map/ppermute | solution.py:107
  221.0 1.9 shard_map.98
  223.0 2.2 collective-permute-done.46
  (166 shorter events, 40.1 us)
Async XLA Ops:
  0.6 19.7 %collective-permute-start = (bf16[256,1536]{1,0:T(8,128)(2,1)}, bf16[256,1536]{1,0:T(8,128)(2,1)}, u32[]{:S(2)}, u32[]{:S(2)}) collective-permute-start(bf16[256,1536]{1,0:T(8,128)(2,1)} %param.8), channel_id=1, source_target_pairs={{0,4},{2,6},{4,0},{6,2},{1,5},{3,7},{5,1},{7,3},{8,12},{10,14},{12... | collective-permute-start | bytes 2359304 | tf_op jit(solution)/shard_map/ppermute | solution.py:31
  4.7 15.6 %collective-permute-start.1 = (bf16[256,1536]{1,0:T(8,128)(2,1)}, bf16[256,1536]{1,0:T(8,128)(2,1)}, u32[]{:S(2)}, u32[]{:S(2)}) collective-permute-start(bf16[256,1536]{1,0:T(8,128)(2,1)} %get-tuple-element.322), channel_id=1, source_target_pairs={{0,2},{2,0},{4,6},{6,4},{1,3},{3,1},{5,7},{7,5},{8,10},{10,8},{12,... | collective-permute-start | bytes 2359304 | tf_op jit(solution)/shard_map/ppermute | solution.py:31
  5.7 14.6 %collective-permute-start.2 = (bf16[256,1536]{1,0:T(8,128)(2,1)}, bf16[256,1536]{1,0:T(8,128)(2,1)S(1)}, u32[]{:S(2)}, u32[]{:S(2)}) collective-permute-start(bf16[256,1536]{1,0:T(8,128)(2,1)} %get-tuple-element.320), channel_id=1, source_target_pairs={{0,2},{2,0},{4,6},{6,4},{1,3},{3,1},{5,7},{7,5},{8,10},{10,8},{12,... | collective-permute-start | bytes 2359304 | tf_op jit(solution)/shard_map/ppermute | solution.py:31
  6.2 19.8 %collective-permute-start.5 = (bf16[256,1536]{1,0:T(8,128)(2,1)S(1)}, bf16[256,1536]{1,0:T(8,128)(2,1)}, u32[]{:S(2)}, u32[]{:S(2)}) collective-permute-start(bf16[256,1536]{1,0:T(8,128)(2,1)S(1)} %copy-done.1), channel_id=1, source_target_pairs={{0,2},{2,0},{4,6},{6,4},{1,3},{3,1},{5,7},{7,5},{8,10},{10,8},{12,... | collective-permute-start | bytes 2359304 | tf_op jit(solution)/shard_map/ppermute | solution.py:31
  20.3 17.4 %collective-permute-start.9 = (bf16[256,1536]{1,0:T(8,128)(2,1)}, bf16[256,1536]{1,0:T(8,128)(2,1)S(1)}, u32[]{:S(2)}, u32[]{:S(2)}) collective-permute-start(bf16[256,1536]{1,0:T(8,128)(2,1)} %collective-permute-done), channel_id=1, source_target_pairs={{0,2},{2,0},{4,6},{6,4},{1,3},{3,1},{5,7},{7,5},{8,10},{10,8},{12,... | collective-permute-start | bytes 2359304 | tf_op jit(solution)/shard_map/ppermute | solution.py:31
  24.4 12.0 %collective-permute-start.6 = (bf16[128,1536]{1,0:T(8,128)(2,1)S(1)}, bf16[128,1536]{1,0:T(8,128)(2,1)S(1)}, u32[]{:S(2)}, u32[]{:S(2)}) collective-permute-start(bf16[128,1536]{1,0:T(8,128)(2,1)S(1)} %get-tuple-element.326), channel_id=1, source_target_pairs={{0,4},{2,6},{4,0},{6,2},{1,5},{3,7},{5,1},{7,3},{8,12},{10,14},{12... | collective-permute-start | bytes 1179656 | tf_op jit(solution)/shard_map/ppermute | solution.py:31
  29.8 15.1 %collective-permute-start.3 = (bf16[128,1536]{1,0:T(8,128)(2,1)S(1)}, bf16[128,1536]{1,0:T(8,128)(2,1)S(1)}, u32[]{:S(2)}, u32[]{:S(2)}) collective-permute-start(bf16[128,1536]{1,0:T(8,128)(2,1)S(1)} %get-tuple-element.327), channel_id=1, source_target_pairs={{0,4},{2,6},{4,0},{6,2},{1,5},{3,7},{5,1},{7,3},{8,12},{10,14},{12... | collective-permute-start | bytes 1179656 | tf_op jit(solution)/shard_map/ppermute | solution.py:31
  30.4 35.9 %collective-permute-start.7 = (bf16[512,1536]{1,0:T(8,128)(2,1)S(1)}, bf16[512,1536]{1,0:T(8,128)(2,1)S(1)}, u32[]{:S(2)}, u32[]{:S(2)}) collective-permute-start(bf16[512,1536]{1,0:T(8,128)(2,1)S(1)} %convolution_convert_fusion), channel_id=1, source_target_pairs={{4,5},{1,0},{6,7},{3,2},{12,13},{9,8},{14,15},{11,10},{20,21},{17,... | collective-permute-start | bytes 4718600 | tf_op jit(solution)/shard_map/ppermute | solution.py:168
  36.4 26.1 %collective-permute-start.8 = (bf16[128,1536]{1,0:T(8,128)(2,1)S(1)}, bf16[128,1536]{1,0:T(8,128)(2,1)S(1)}, u32[]{:S(2)}, u32[]{:S(2)}) collective-permute-start(bf16[128,1536]{1,0:T(8,128)(2,1)S(1)} %collective-permute-done.6), channel_id=1, source_target_pairs={{0,1},{5,4},{2,3},{7,6},{8,9},{13,12},{10,11},{15,14},{16,17},{21,... | collective-permute-start | bytes 1179656 | tf_op jit(solution)/shard_map/ppermute | solution.py:173
  39.2 14.1 %collective-permute-start.10 = (bf16[128,1536]{1,0:T(8,128)(2,1)S(1)}, bf16[128,1536]{1,0:T(8,128)(2,1)S(1)}, u32[]{:S(2)}, u32[]{:S(2)}) collective-permute-start(bf16[128,1536]{1,0:T(8,128)(2,1)S(1)} %get-tuple-element.328), channel_id=1, source_target_pairs={{0,4},{2,6},{4,0},{6,2},{1,5},{3,7},{5,1},{7,3},{8,12},{10,14},{12... | collective-permute-start | bytes 1179656 | tf_op jit(solution)/shard_map/ppermute | solution.py:31
  41.9 19.3 %collective-permute-start.12 = (bf16[128,1536]{1,0:T(8,128)(2,1)S(1)}, bf16[128,1536]{1,0:T(8,128)(2,1)S(1)}, u32[]{:S(2)}, u32[]{:S(2)}) collective-permute-start(bf16[128,1536]{1,0:T(8,128)(2,1)S(1)} %get-tuple-element.329), channel_id=1, source_target_pairs={{0,4},{2,6},{4,0},{6,2},{1,5},{3,7},{5,1},{7,3},{8,12},{10,14},{12... | collective-permute-start | bytes 1179656 | tf_op jit(solution)/shard_map/ppermute | solution.py:31
  44.9 21.9 %collective-permute-start.4 = (bf16[128,1536]{1,0:T(8,128)(2,1)S(1)}, bf16[128,1536]{1,0:T(8,128)(2,1)S(1)}, u32[]{:S(2)}, u32[]{:S(2)}) collective-permute-start(bf16[128,1536]{1,0:T(8,128)(2,1)S(1)} %collective-permute-done.3), channel_id=1, source_target_pairs={{0,1},{5,4},{2,3},{7,6},{8,9},{13,12},{10,11},{15,14},{16,17},{21,... | collective-permute-start | bytes 1179656 | tf_op jit(solution)/shard_map/ppermute | solution.py:173
  53.3 13.9 %collective-permute-start.11 = (bf16[128,1536]{1,0:T(8,128)(2,1)S(1)}, bf16[128,1536]{1,0:T(8,128)(2,1)S(1)}, u32[]{:S(2)}, u32[]{:S(2)}) collective-permute-start(bf16[128,1536]{1,0:T(8,128)(2,1)S(1)} %collective-permute-done.10), channel_id=1, source_target_pairs={{0,1},{5,4},{2,3},{7,6},{8,9},{13,12},{10,11},{15,14},{16,17},{21,... | collective-permute-start | bytes 1179656 | tf_op jit(solution)/shard_map/ppermute | solution.py:173
  61.3 12.6 %collective-permute-start.13 = (bf16[128,1536]{1,0:T(8,128)(2,1)S(1)}, bf16[128,1536]{1,0:T(8,128)(2,1)S(1)}, u32[]{:S(2)}, u32[]{:S(2)}) collective-permute-start(bf16[128,1536]{1,0:T(8,128)(2,1)S(1)} %collective-permute-done.12), channel_id=1, source_target_pairs={{0,1},{5,4},{2,3},{7,6},{8,9},{13,12},{10,11},{15,14},{16,17},{21,... | collective-permute-start | bytes 1179656 | tf_op jit(solution)/shard_map/ppermute | solution.py:173
  76.6 3.7 %collective-permute-start.15 = (f32[2,512]{1,0:T(2,128)S(1)}, f32[2,512]{1,0:T(2,128)S(1)}, u32[]{:S(2)}, u32[]{:S(2)}) collective-permute-start(f32[2,512]{1,0:T(2,128)S(1)} %maximum_add_fusion), channel_id=1, source_target_pairs={{0,1},{1,0},{2,3},{3,2},{4,5},{5,4},{6,7},{7,6},{8,9},{9,8},{10,11... | collective-permute-start | bytes 12296 | tf_op jit(solution)/shard_map/ppermute | solution.py:31
  80.6 5.0 %collective-permute-start.19 = (bf16[512,128]{1,0:T(8,128)(2,1)S(1)}, bf16[512,128]{1,0:T(8,128)(2,1)S(1)}, u32[]{:S(2)}, u32[]{:S(2)}) collective-permute-start(bf16[512,128]{1,0:T(8,128)(2,1)S(1)} %pad_maximum_fusion.5), channel_id=1, source_target_pairs={{0,1},{5,4},{4,0},{1,5},{2,3},{7,6},{6,2},{3,7},{8,9},{13,12},{12,... | collective-permute-start | bytes 393224 | tf_op jit(solution)/shard_map/ppermute | solution.py:230
  80.7 8.4 %collective-permute-start.16 = (bf16[512,128]{1,0:T(8,128)(2,1)S(1)}, bf16[512,128]{1,0:T(8,128)(2,1)S(1)}, u32[]{:S(2)}, u32[]{:S(2)}) collective-permute-start(bf16[512,128]{1,0:T(8,128)(2,1)S(1)} %pad_maximum_fusion.5), channel_id=1, source_target_pairs={{4,1},{1,4},{6,3},{3,6},{12,9},{9,12},{14,11},{11,14},{20,17},{17,... | collective-permute-start | bytes 393224 | tf_op jit(solution)/shard_map/ppermute | solution.py:231
  85.6 14.8 %collective-permute-start.21 = (bf16[512,384]{1,0:T(8,128)(2,1)S(1)}, bf16[512,384]{1,0:T(8,128)(2,1)S(1)}, u32[]{:S(2)}, u32[]{:S(2)}) collective-permute-start(bf16[512,384]{1,0:T(8,128)(2,1)S(1)} %pad_maximum_fusion.2), channel_id=1, source_target_pairs={{4,1},{1,4},{6,3},{3,6},{12,9},{9,12},{14,11},{11,14},{20,17},{17,... | collective-permute-start | bytes 1179656 | tf_op jit(solution)/shard_map/ppermute | solution.py:231
  89.0 12.1 %collective-permute-start.20 = (bf16[512,384]{1,0:T(8,128)(2,1)S(1)}, bf16[512,384]{1,0:T(8,128)(2,1)S(1)}, u32[]{:S(2)}, u32[]{:S(2)}) collective-permute-start(bf16[512,384]{1,0:T(8,128)(2,1)S(1)} %pad_maximum_fusion.2), channel_id=1, source_target_pairs={{0,1},{5,4},{4,0},{1,5},{2,3},{7,6},{6,2},{3,7},{8,9},{13,12},{12,... | collective-permute-start | bytes 1179656 | tf_op jit(solution)/shard_map/ppermute | solution.py:230
  89.1 31.2 %collective-permute-start.18 = (bf16[512,1024]{1,0:T(8,128)(2,1)S(1)}, bf16[512,1024]{1,0:T(8,128)(2,1)S(1)}, u32[]{:S(2)}, u32[]{:S(2)}) collective-permute-start(bf16[512,1024]{1,0:T(8,128)(2,1)S(1)} %pad_maximum_fusion), channel_id=1, source_target_pairs={{4,1},{1,4},{6,3},{3,6},{12,9},{9,12},{14,11},{11,14},{20,17},{17,... | collective-permute-start | bytes 3145736 | tf_op jit(solution)/shard_map/ppermute | solution.py:231
  92.4 28.2 %collective-permute-start.17 = (bf16[512,1024]{1,0:T(8,128)(2,1)S(1)}, bf16[512,1024]{1,0:T(8,128)(2,1)S(1)}, u32[]{:S(2)}, u32[]{:S(2)}) collective-permute-start(bf16[512,1024]{1,0:T(8,128)(2,1)S(1)} %pad_maximum_fusion), channel_id=1, source_target_pairs={{0,1},{5,4},{4,0},{1,5},{2,3},{7,6},{6,2},{3,7},{8,9},{13,12},{12,... | collective-permute-start | bytes 3145736 | tf_op jit(solution)/shard_map/ppermute | solution.py:230
  94.1 14.3 %collective-permute-start.22 = (bf16[1536,128]{1,0:T(8,128)(2,1)S(1)}, bf16[1536,128]{1,0:T(8,128)(2,1)S(1)}, u32[]{:S(2)}, u32[]{:S(2)}) collective-permute-start(bf16[1536,128]{1,0:T(8,128)(2,1)S(1)} %fusion.55), channel_id=1, source_target_pairs={{0,8},{24,16},{1,9},{25,17},{2,10},{26,18},{3,11},{27,19},{4,12},{... | collective-permute-start | bytes 1179656 | tf_op jit(solution)/shard_map/ppermute | solution.py:107
  104.9 12.1 %collective-permute-start.23 = (bf16[1536,128]{1,0:T(8,128)(2,1)S(1)}, bf16[1536,128]{1,0:T(8,128)(2,1)S(1)}, u32[]{:S(2)}, u32[]{:S(2)}) collective-permute-start(bf16[1536,128]{1,0:T(8,128)(2,1)S(1)} %fusion.54), channel_id=1, source_target_pairs={{0,8},{24,16},{1,9},{25,17},{2,10},{26,18},{3,11},{27,19},{4,12},{... | collective-permute-start | bytes 1179656 | tf_op jit(solution)/shard_map/ppermute | solution.py:107
  108.6 9.3 %collective-permute-start.26 = (bf16[1536,128]{1,0:T(8,128)(2,1)S(1)}, bf16[1536,128]{1,0:T(8,128)(2,1)S(1)}, u32[]{:S(2)}, u32[]{:S(2)}) collective-permute-start(bf16[1536,128]{1,0:T(8,128)(2,1)S(1)} %add_convert_fusion.23), channel_id=1, source_target_pairs={{8,16},{16,8},{9,17},{17,9},{10,18},{18,10},{11,19},{19,11},{12,20... | collective-permute-start | bytes 1179656 | tf_op jit(solution)/shard_map/ppermute | solution.py:115
  109.2 16.2 %collective-permute-start.25 = (bf16[1536,128]{1,0:T(8,128)(2,1)S(1)}, bf16[1536,128]{1,0:T(8,128)(2,1)S(1)}, u32[]{:S(2)}, u32[]{:S(2)}) collective-permute-start(bf16[1536,128]{1,0:T(8,128)(2,1)S(1)} %slice.474), channel_id=1, source_target_pairs={{0,8},{24,16},{1,9},{25,17},{2,10},{26,18},{3,11},{27,19},{4,12},{... | collective-permute-start | bytes 1179656 | tf_op jit(solution)/shard_map/ppermute | solution.py:107
  117.2 9.1 %collective-permute-start.24 = (bf16[1536,128]{1,0:T(8,128)(2,1)S(1)}, bf16[1536,128]{1,0:T(8,128)(2,1)S(1)}, u32[]{:S(2)}, u32[]{:S(2)}) collective-permute-start(bf16[1536,128]{1,0:T(8,128)(2,1)S(1)} %add_convert_fusion.22), channel_id=1, source_target_pairs={{8,16},{16,8},{9,17},{17,9},{10,18},{18,10},{11,19},{19,11},{12,20... | collective-permute-start | bytes 1179656 | tf_op jit(solution)/shard_map/ppermute | solution.py:115
  123.3 9.9 %collective-permute-start.28 = (bf16[1536,128]{1,0:T(8,128)(2,1)S(1)}, bf16[1536,128]{1,0:T(8,128)(2,1)S(1)}, u32[]{:S(2)}, u32[]{:S(2)}) collective-permute-start(bf16[1536,128]{1,0:T(8,128)(2,1)S(1)} %fusion.68), channel_id=1, source_target_pairs={{0,8},{24,16},{8,0},{16,24},{1,9},{25,17},{9,1},{17,25},{2,10},{26... | collective-permute-start | bytes 1179656 | tf_op jit(solution)/shard_map/ppermute | solution.py:107
  125.5 8.5 %collective-permute-start.27 = (bf16[1536,128]{1,0:T(8,128)(2,1)S(1)}, bf16[1536,128]{1,0:T(8,128)(2,1)S(1)}, u32[]{:S(2)}, u32[]{:S(2)}) collective-permute-start(bf16[1536,128]{1,0:T(8,128)(2,1)S(1)} %add_convert_fusion.20), channel_id=1, source_target_pairs={{8,16},{16,8},{9,17},{17,9},{10,18},{18,10},{11,19},{19,11},{12,20... | collective-permute-start | bytes 1179656 | tf_op jit(solution)/shard_map/ppermute | solution.py:115
  128.6 14.6 %collective-permute-start.30 = (bf16[1536,128]{1,0:T(8,128)(2,1)S(1)}, bf16[1536,128]{1,0:T(8,128)(2,1)S(1)}, u32[]{:S(2)}, u32[]{:S(2)}) collective-permute-start(bf16[1536,128]{1,0:T(8,128)(2,1)S(1)} %fusion.69), channel_id=1, source_target_pairs={{0,8},{24,16},{8,0},{16,24},{1,9},{25,17},{9,1},{17,25},{2,10},{26... | collective-permute-start | bytes 1179656 | tf_op jit(solution)/shard_map/ppermute | solution.py:107
  133.3 10.9 %collective-permute-start.31 = (bf16[1536,128]{1,0:T(8,128)(2,1)S(1)}, bf16[1536,128]{1,0:T(8,128)(2,1)S(1)}, u32[]{:S(2)}, u32[]{:S(2)}) collective-permute-start(bf16[1536,128]{1,0:T(8,128)(2,1)S(1)} %add_convert_fusion.18), channel_id=1, source_target_pairs={{8,16},{16,8},{9,17},{17,9},{10,18},{18,10},{11,19},{19,11},{12,20... | collective-permute-start | bytes 1179656 | tf_op jit(solution)/shard_map/ppermute | solution.py:115
  134.2 17.4 %collective-permute-start.29 = (bf16[1536,128]{1,0:T(8,128)(2,1)S(1)}, bf16[1536,128]{1,0:T(8,128)(2,1)S(1)}, u32[]{:S(2)}, u32[]{:S(2)}) collective-permute-start(bf16[1536,128]{1,0:T(8,128)(2,1)S(1)} %fusion.70), channel_id=1, source_target_pairs={{0,8},{24,16},{8,0},{16,24},{1,9},{25,17},{9,1},{17,25},{2,10},{26... | collective-permute-start | bytes 1179656 | tf_op jit(solution)/shard_map/ppermute | solution.py:107
  143.3 11.5 %collective-permute-start.34 = (bf16[1536,128]{1,0:T(8,128)(2,1)S(1)}, bf16[1536,128]{1,0:T(8,128)(2,1)S(1)}, u32[]{:S(2)}, u32[]{:S(2)}) collective-permute-start(bf16[1536,128]{1,0:T(8,128)(2,1)S(1)} %add_convert_fusion.16), channel_id=1, source_target_pairs={{8,16},{16,8},{9,17},{17,9},{10,18},{18,10},{11,19},{19,11},{12,20... | collective-permute-start | bytes 1179656 | tf_op jit(solution)/shard_map/ppermute | solution.py:115
  144.4 17.5 %collective-permute-start.33 = (bf16[1536,128]{1,0:T(8,128)(2,1)S(1)}, bf16[1536,128]{1,0:T(8,128)(2,1)S(1)}, u32[]{:S(2)}, u32[]{:S(2)}) collective-permute-start(bf16[1536,128]{1,0:T(8,128)(2,1)S(1)} %fusion.71), channel_id=1, source_target_pairs={{0,8},{24,16},{8,0},{16,24},{1,9},{25,17},{9,1},{17,25},{2,10},{26... | collective-permute-start | bytes 1179656 | tf_op jit(solution)/shard_map/ppermute | solution.py:107
  153.9 8.8 %collective-permute-start.32 = (bf16[1536,128]{1,0:T(8,128)(2,1)S(1)}, bf16[1536,128]{1,0:T(8,128)(2,1)S(1)}, u32[]{:S(2)}, u32[]{:S(2)}) collective-permute-start(bf16[1536,128]{1,0:T(8,128)(2,1)S(1)} %add_convert_fusion.14), channel_id=1, source_target_pairs={{8,16},{16,8},{9,17},{17,9},{10,18},{18,10},{11,19},{19,11},{12,20... | collective-permute-start | bytes 1179656 | tf_op jit(solution)/shard_map/ppermute | solution.py:115
  155.0 17.1 %collective-permute-start.36 = (bf16[1536,128]{1,0:T(8,128)(2,1)S(1)}, bf16[1536,128]{1,0:T(8,128)(2,1)S(1)}, u32[]{:S(2)}, u32[]{:S(2)}) collective-permute-start(bf16[1536,128]{1,0:T(8,128)(2,1)S(1)} %fusion.72), channel_id=1, source_target_pairs={{0,8},{24,16},{8,0},{16,24},{1,9},{25,17},{9,1},{17,25},{2,10},{26... | collective-permute-start | bytes 1179656 | tf_op jit(solution)/shard_map/ppermute | solution.py:107
  162.0 10.9 %collective-permute-start.35 = (bf16[1536,128]{1,0:T(8,128)(2,1)S(1)}, bf16[1536,128]{1,0:T(8,128)(2,1)S(1)}, u32[]{:S(2)}, u32[]{:S(2)}) collective-permute-start(bf16[1536,128]{1,0:T(8,128)(2,1)S(1)} %add_convert_fusion.12), channel_id=1, source_target_pairs={{8,16},{16,8},{9,17},{17,9},{10,18},{18,10},{11,19},{19,11},{12,20... | collective-permute-start | bytes 1179656 | tf_op jit(solution)/shard_map/ppermute | solution.py:115
  162.8 15.4 %collective-permute-start.38 = (bf16[1536,128]{1,0:T(8,128)(2,1)S(1)}, bf16[1536,128]{1,0:T(8,128)(2,1)S(1)}, u32[]{:S(2)}, u32[]{:S(2)}) collective-permute-start(bf16[1536,128]{1,0:T(8,128)(2,1)S(1)} %fusion.73), channel_id=1, source_target_pairs={{0,8},{24,16},{8,0},{16,24},{1,9},{25,17},{9,1},{17,25},{2,10},{26... | collective-permute-start | bytes 1179656 | tf_op jit(solution)/shard_map/ppermute | solution.py:107
  172.2 6.9 %collective-permute-start.37 = (bf16[1536,128]{1,0:T(8,128)(2,1)S(1)}, bf16[1536,128]{1,0:T(8,128)(2,1)S(1)}, u32[]{:S(2)}, u32[]{:S(2)}) collective-permute-start(bf16[1536,128]{1,0:T(8,128)(2,1)S(1)} %add_convert_fusion.10), channel_id=1, source_target_pairs={{8,16},{16,8},{9,17},{17,9},{10,18},{18,10},{11,19},{19,11},{12,20... | collective-permute-start | bytes 1179656 | tf_op jit(solution)/shard_map/ppermute | solution.py:115
  173.1 16.3 %collective-permute-start.40 = (bf16[1536,128]{1,0:T(8,128)(2,1)S(1)}, bf16[1536,128]{1,0:T(8,128)(2,1)S(1)}, u32[]{:S(2)}, u32[]{:S(2)}) collective-permute-start(bf16[1536,128]{1,0:T(8,128)(2,1)S(1)} %fusion.74), channel_id=1, source_target_pairs={{0,8},{24,16},{8,0},{16,24},{1,9},{25,17},{9,1},{17,25},{2,10},{26... | collective-permute-start | bytes 1179656 | tf_op jit(solution)/shard_map/ppermute | solution.py:107
  178.4 11.8 %collective-permute-start.41 = (bf16[1536,128]{1,0:T(8,128)(2,1)S(1)}, bf16[1536,128]{1,0:T(8,128)(2,1)S(1)}, u32[]{:S(2)}, u32[]{:S(2)}) collective-permute-start(bf16[1536,128]{1,0:T(8,128)(2,1)S(1)} %add_convert_fusion.8), channel_id=1, source_target_pairs={{8,16},{16,8},{9,17},{17,9},{10,18},{18,10},{11,19},{19,11},{12,20... | collective-permute-start | bytes 1179656 | tf_op jit(solution)/shard_map/ppermute | solution.py:115
  179.3 15.9 %collective-permute-start.39 = (bf16[1536,128]{1,0:T(8,128)(2,1)S(1)}, bf16[1536,128]{1,0:T(8,128)(2,1)S(1)}, u32[]{:S(2)}, u32[]{:S(2)}) collective-permute-start(bf16[1536,128]{1,0:T(8,128)(2,1)S(1)} %fusion.75), channel_id=1, source_target_pairs={{0,8},{24,16},{8,0},{16,24},{1,9},{25,17},{9,1},{17,25},{2,10},{26... | collective-permute-start | bytes 1179656 | tf_op jit(solution)/shard_map/ppermute | solution.py:107
  189.5 6.5 %collective-permute-start.44 = (bf16[1536,128]{1,0:T(8,128)(2,1)S(1)}, bf16[1536,128]{1,0:T(8,128)(2,1)S(1)}, u32[]{:S(2)}, u32[]{:S(2)}) collective-permute-start(bf16[1536,128]{1,0:T(8,128)(2,1)S(1)} %add_convert_fusion.6), channel_id=1, source_target_pairs={{8,16},{16,8},{9,17},{17,9},{10,18},{18,10},{11,19},{19,11},{12,20... | collective-permute-start | bytes 1179656 | tf_op jit(solution)/shard_map/ppermute | solution.py:115
  190.3 13.8 %collective-permute-start.43 = (bf16[1536,128]{1,0:T(8,128)(2,1)S(1)}, bf16[1536,128]{1,0:T(8,128)(2,1)S(1)}, u32[]{:S(2)}, u32[]{:S(2)}) collective-permute-start(bf16[1536,128]{1,0:T(8,128)(2,1)S(1)} %fusion.76), channel_id=1, source_target_pairs={{0,8},{24,16},{8,0},{16,24},{1,9},{25,17},{9,1},{17,25},{2,10},{26... | collective-permute-start | bytes 1179656 | tf_op jit(solution)/shard_map/ppermute | solution.py:107
  195.3 9.8 %collective-permute-start.42 = (bf16[1536,128]{1,0:T(8,128)(2,1)S(1)}, bf16[1536,128]{1,0:T(8,128)(2,1)S(1)}, u32[]{:S(2)}, u32[]{:S(2)}) collective-permute-start(bf16[1536,128]{1,0:T(8,128)(2,1)S(1)} %add_convert_fusion.4), channel_id=1, source_target_pairs={{8,16},{16,8},{9,17},{17,9},{10,18},{18,10},{11,19},{19,11},{12,20... | collective-permute-start | bytes 1179656 | tf_op jit(solution)/shard_map/ppermute | solution.py:115
  196.1 16.5 %collective-permute-start.48 = (bf16[1536,128]{1,0:T(8,128)(2,1)S(1)}, bf16[1536,128]{1,0:T(8,128)(2,1)S(1)}, u32[]{:S(2)}, u32[]{:S(2)}) collective-permute-start(bf16[1536,128]{1,0:T(8,128)(2,1)S(1)} %add_convert_fusion.3), channel_id=1, source_target_pairs={{8,0},{16,24},{9,1},{17,25},{10,2},{18,26},{11,3},{19,27},{12,4},{... | collective-permute-start | bytes 1179656 | tf_op jit(solution)/shard_map/ppermute | solution.py:107
  204.3 4.8 %collective-permute-start.45 = (bf16[1536,128]{1,0:T(8,128)(2,1)S(1)}, bf16[1536,128]{1,0:T(8,128)(2,1)S(1)}, u32[]{:S(2)}, u32[]{:S(2)}) collective-permute-start(bf16[1536,128]{1,0:T(8,128)(2,1)S(1)} %add_convert_fusion.2), channel_id=1, source_target_pairs={{8,16},{16,8},{9,17},{17,9},{10,18},{18,10},{11,19},{19,11},{12,20... | collective-permute-start | bytes 1179656 | tf_op jit(solution)/shard_map/ppermute | solution.py:115
  205.2 15.8 %collective-permute-start.47 = (bf16[1536,128]{1,0:T(8,128)(2,1)S(1)}, bf16[1536,128]{1,0:T(8,128)(2,1)S(1)}, u32[]{:S(2)}, u32[]{:S(2)}) collective-permute-start(bf16[1536,128]{1,0:T(8,128)(2,1)S(1)} %add_convert_fusion), channel_id=1, source_target_pairs={{8,0},{16,24},{9,1},{17,25},{10,2},{18,26},{11,3},{19,27},{12,4},{... | collective-permute-start | bytes 1179656 | tf_op jit(solution)/shard_map/ppermute | solution.py:107
  209.2 16.0 %collective-permute-start.46 = (bf16[1536,128]{1,0:T(8,128)(2,1)S(1)}, bf16[1536,128]{1,0:T(8,128)(2,1)S(1)}, u32[]{:S(2)}, u32[]{:S(2)}) collective-permute-start(bf16[1536,128]{1,0:T(8,128)(2,1)S(1)} %add_convert_fusion.1), channel_id=1, source_target_pairs={{8,0},{16,24},{9,1},{17,25},{10,2},{18,26},{11,3},{19,27},{12,4},{... | collective-permute-start | bytes 1179656 | tf_op jit(solution)/shard_map/ppermute | solution.py:107
  (12 other events, 111.3 us)
